TPU v7x, 32 devices: a whole 2x2x4 slice. The times are simulated.
32 devices in a mesh: strip: 8 (over z, x), chan: 4 (over y, core).
Axes of the slice: x: 2, y: 2, z: 4, core: 2. Of those that a mesh axis runs over, the one named last changes fastest.
Arguments:
- section_input: bfloat16 [48, 1024, 256], P(None, 'strip'), may hold values from -6 to 6
- conv_weight: bfloat16 [3, 3, 256, 256], replicated, may hold values from -0.125 to 0.125
- conv_bias: float32 [256], replicated, may hold values from -3 to 3
- deep_weight: bfloat16 [3, 3, 256, 512], P(None, None, None, 'chan'), may hold values from -0.125 to 0.125
- deep_bias: float32 [512], P('chan'), may hold values from -3 to 3
- labels: int32 [24, 512], P(None, 'strip'), may hold values from 0 to 32, as said below
- slot_ids: int32 [256], P('strip'), may hold values from 0 to 511, as said below
- embed_grad: float32 [512, 512], P('strip', 'chan'), may hold values from -0.8 to 0.8
Outputs:
- embeddings: float32 [512, 512], P('strip', 'chan')
- weight_grad: float32 [3, 3, 256, 512], P(None, None, None, 'chan')
- bias_grad: float32 [512], P('chan')
Inputs may be any that keep to these rules, and one draw needn't show every extreme that they name: `labels`: the value 32 marks background; any other value v names entry v of the list of the strip that holds the pixel. `slot_ids`: A value s names slot s % 64 of owner s // 64 (an index of strip). The slots within one strip's list differ; a slot stands in the lists of at most two strips, which are neighbours (a crack across a strip border). Every owner holds at most 64 components and some owner holds exactly 64.
All inputs are finite; a program needn't handle non-finite values.
Results may differ from a plain program's by a relative error of at most 0.0035.
Values may be sent and summed in bfloat16 or wider, within the bound.
No kernel may reach another device: no remote copies, remote signals or barrier semaphores. Data moves between devices by JAX's collectives and lax.ppermute only.
A program may use at most 64 MiB of HBM per device.

v0:
```python
import jax
import jax.numpy as jnp
from jax import lax
from jax.sharding import PartitionSpec as P


def with_halo(cells, sides, width):
    for axis, dim in sides:
        count = lax.axis_size(axis)
        ends = count - 1
        head = lax.slice_in_dim(cells, 0, width, axis=dim)
        tail = lax.slice_in_dim(cells, cells.shape[dim] - width, cells.shape[dim], axis=dim)
        cells = jnp.concatenate(
            [
                lax.ppermute(tail, axis, [(i, (i + 1) % count) for i in range(ends)]),
                cells,
                lax.ppermute(head, axis, [((i + 1) % count, i) for i in range(ends)]),
            ],
            axis=dim,
        )
    return cells


def swish(value):
    return value * jax.nn.sigmoid(value)


def swish_slope(value):
    sigma = jax.nn.sigmoid(value)
    return sigma * (1.0 + value * (1.0 - sigma))


def convolve(padded, weight, row_count, col_count):
    channels = padded.shape[-1]
    running = None
    for shift_row in range(3):
        for shift_col in range(3):
            window = padded[
                shift_row : shift_row + row_count, shift_col : shift_col + col_count
            ].reshape(row_count * col_count, channels)
            partial_term = jnp.dot(
                window, weight[shift_row, shift_col], preferred_element_type=jnp.float32
            )
            running = partial_term if running is None else running + partial_term
    return running.reshape(row_count, col_count, weight.shape[-1])


def pool_pairs(hidden):
    row_count, col_count, channels = hidden.shape
    return (
        hidden.reshape(row_count // 2, 2, col_count // 2, 2, channels)
        .mean(axis=(1, 3))
        .astype(jnp.bfloat16)
    )


def body(
    section_input, conv_weight, conv_bias, deep_weight, deep_bias, labels, slot_ids, embed_grad
):
    chan_count = lax.axis_size("chan")
    chan_pos = lax.axis_index("chan")
    strip_count = lax.axis_size("strip")
    strip_pos = lax.axis_index("strip")
    row_total, col_local, channels = section_input.shape
    row_part = row_total // chan_count
    half_cols = col_local // 2
    padded_rows = jnp.pad(section_input, ((1, 1), (0, 0), (0, 0)))
    own_rows = lax.dynamic_slice_in_dim(padded_rows, chan_pos * row_part, row_part + 2, 0)
    extended = with_halo(own_rows, (("strip", 1),), 3)
    hidden = swish(convolve(extended, conv_weight, row_part, col_local + 4) + conv_bias)
    pooled = pool_pairs(hidden)
    column = jnp.arange(half_cols + 2)
    outside = (column == 0) & (strip_pos == 0) | (column == half_cols + 1) & (
        strip_pos == strip_count - 1
    )
    pooled = jnp.where(outside[None, :, None], jnp.zeros_like(pooled), pooled)
    gathered = lax.all_gather(pooled, "chan", axis=0, tiled=True)
    padded_deep = jnp.pad(gathered, ((1, 1), (0, 0), (0, 0)))
    half_rows = gathered.shape[0]
    deep_pre = convolve(padded_deep, deep_weight, half_rows, half_cols) + deep_bias
    width_deep = deep_weight.shape[-1]
    features = swish(deep_pre).astype(jnp.bfloat16).reshape(-1, width_deep)
    flat_labels = labels.reshape(-1)
    list_len = slot_ids.shape[0]
    member = flat_labels[None, :] == jnp.arange(list_len, dtype=jnp.int32)[:, None]
    part_sums = jnp.dot(member.astype(jnp.bfloat16), features, preferred_element_type=jnp.float32)
    part_counts = jnp.sum(member.astype(jnp.float32), axis=1)
    owned = embed_grad.shape[0]
    dense_sums = (
        jnp.zeros((owned * strip_count, width_deep), jnp.float32).at[slot_ids].set(part_sums)
    )
    dense_counts = jnp.zeros((owned * strip_count,), jnp.float32).at[slot_ids].set(part_counts)
    slot_sums, slot_counts = (
        lax.psum_scatter(dense_sums, "strip", scatter_dimension=0, tiled=True),
        lax.psum_scatter(dense_counts, "strip", scatter_dimension=0, tiled=True),
    )
    divisor = jnp.maximum(slot_counts, 1.0)[:, None]
    embeddings = slot_sums / divisor
    every_grad = lax.all_gather(embed_grad / divisor, "strip", axis=0, tiled=True)
    entry_grad = every_grad[slot_ids]
    pixel_grad = lax.dot_general(
        member.astype(jnp.float32),
        entry_grad,
        (((0,), (0,)), ((), ())),
        precision=lax.Precision.HIGHEST,
        preferred_element_type=jnp.float32,
    )
    deep_grad = (pixel_grad * swish_slope(deep_pre.reshape(-1, width_deep))).astype(jnp.bfloat16)
    pieces = []
    for shift_row in range(3):
        for shift_col in range(3):
            window = padded_deep[
                shift_row : shift_row + half_rows, shift_col : shift_col + half_cols
            ].reshape(-1, channels)
            pieces.append(
                lax.dot_general(
                    window, deep_grad, (((0,), (0,)), ((), ())), preferred_element_type=jnp.float32
                )
            )
    local_weight = jnp.stack(pieces).reshape(3, 3, channels, width_deep)
    local_bias = jnp.sum(deep_grad.astype(jnp.float32), axis=0)
    weight_grad, bias_grad = lax.psum((local_weight, local_bias), "strip")
    return (embeddings, weight_grad, bias_grad)


def solution(mesh):
    placed = (
        P(None, "strip", None),
        P(),
        P(),
        P(None, None, None, "chan"),
        P("chan"),
        P(None, "strip"),
        P("strip"),
        P("strip", "chan"),
    )
    return jax.shard_map(
        body,
        mesh=mesh,
        in_specs=placed,
        out_specs=(P("strip", "chan"), P(None, None, None, "chan"), P("chan")),
        check_vma=False,
    )
```

profile of v0, /device:TPU:0, one launch (start us, length us, event | category | flops | bytes accessed | tf_op | source)
XLA Modules:
  0.0 256.2 jit_solution(11558336940414655059)
XLA Ops:
  7.2 1.0 pad_dynamic-slice_fusion.1
  8.3 4.8 %collective-permute-start = (bf16[14,3,256]{2,1,0:T(4,128)(2,1)S(1)}, bf16[14,3,256]{2,1,0:T(4,128)(2,1)S(1)}, u32[]{:S(2)}, u32[]{:S(2)}) collective-permute-start(bf16[14,3,256]{2,1,0:T(4,128)(2,1)S(1)} %get-tuple-element.3), channel_id=1, source_target_pairs={{0,4},{4,8},{8,12},{12,16},{16,20},{20,24},{24,28},{1,5},{5,9},{9,... | collective-permute-start | bytes 64520 | tf_op jit(solution)/shard_map/ppermute | solution.py:15
  13.1 1.3 collective-permute-start.1
  14.4 1.0 pad_dynamic-slice_fusion.2
  15.5 3.3 %collective-permute-done.1 = bf16[14,3,256]{2,1,0:T(4,128)(2,1)S(1)} collective-permute-done((bf16[14,3,256]{2,1,0:T(4,128)(2,1)S(1)}, bf16[14,3,256]{2,1,0:T(4,128)(2,1)S(1)}, u32[]{:S(2)}, u32[]{:S(2)}) %collective-permute-start.1) | collective-permute-done | bytes 21536 | tf_op jit(solution)/shard_map/ppermute | solution.py:17
  18.9 1.6 pad_maximum_fusion
  20.5 2.8 %fusion.59 = (bf16[12,132,256]{2,1,0:T(8,128)(2,1)}, bf16[12,132,256]{2,1,0:T(8,128)(2,1)}, bf16[12,132,256]{2,1,0:T(8,128)(2,1)}, bf16[12,132,256]{2,1,0:T(8,12...) fusion(bf16[14,134,256]{2,1,0:T(8,128)(2,1)S(1)} %pad_maximum_f, ...), kind=kLoop, calls=%fused_computation.111 | loop fusion | bytes 14598144 | tf_op jit(solution)/shard_map/slice | solution.py:38
  23.3 2.1 reshape.101
  25.4 2.1 reshape.100
  27.4 2.1 reshape.99
  29.5 2.0 reshape.98
  31.5 2.1 reshape.97
  33.6 1.0 reshape.96
  35.1 1.4 fusion.21
  39.5 0.8 copy-done.14
  41.8 0.8 copy-done.12
  43.0 0.8 copy-done.11
  44.1 1.0 reshape.102
  45.1 2.7 %fusion.2 = f32[6,66,256]{2,1,0:T(8,128)S(1)} fusion(f32[6,2,66,2,256]{4,3,2,1,0:T(2,128)S(1)} %reshape.102, f32[256]{0:T(256)S(1)} %copy-done.23), kind=kLoop, calls=%fused_computation.26 | loop fusion | flops 2331648 | bytes 2028544 | tf_op jit(solution)/shard_map/reduce_sum | solution.py:52
  47.9 9.4 %all_gather.6 = bf16[24,66,256]{2,1,0:T(8,128)(2,1)S(1)} all-gather(bf16[6,66,256]{2,1,0:T(8,128)(2,1)S(1)} %fusion.13), channel_id=1, replica_groups=mesh['strip'=8,'chan'=4] {'chan'}, dimensions={0}, use_global_device_ids=true | all-gather | bytes 1013760 | tf_op jit(solution)/shard_map/all_gather | solution.py:77
  57.3 1.4 pad_slice_fusion
  63.0 0.9 copy-done.19
  64.2 1.3 scatter_custom_fusion
  67.7 19.9 %all-reduce.2 = f32[512]{0:T(512)S(1)} all-reduce(f32[512]{0:T(512)S(1)} %scatter_custom_fusion.1), channel_id=3, replica_groups=mesh['strip'=8,'chan'=4] {'strip'}, use_global_device_ids=true, to_apply=%region_5.6.clone | all-reduce | flops 512 | bytes 4096
  87.7 39.5 %reduce-scatter.2.cloned.1.call-done = f32[64,128]{1,0:T(8,128)} async-done(((f32[512,128]{1,0:T(8,128)}), f32[64,128]{1,0:T(8,128)}) %reduce-scatter.2.cloned.1.call-update) | async-done | bytes 32784 | tf_op jit(solution)/shard_map/reduce_scatter | solution.py:94
  127.2 1.5 broadcast_divide_fusion
  128.7 30.9 %all_gather.7 = f32[512,128]{1,0:T(8,128)S(1)} all-gather(f32[64,128]{1,0:T(8,128)S(1)} %get-tuple-element.23), channel_id=1, replica_groups=mesh['strip'=8,'chan'=4] {'strip'}, dimensions={0}, use_global_device_ids=true | all-gather | bytes 294912 | tf_op jit(solution)/shard_map/all_gather | solution.py:99
  160.1 2.1 convert_reduce_fusion
  166.6 1.0 copy-done.17
  167.7 20.7 %psum.15 = f32[128]{0:T(128)} all-reduce(f32[128]{0:T(128)S(1)} %get-tuple-element.25), channel_id=1, replica_groups=mesh['strip'=8,'chan'=4] {'strip'}, use_global_device_ids=true, to_apply=%region_8.9 | all-reduce | flops 128 | bytes 1024 | tf_op jit(solution)/shard_map/psum | solution.py:122
  188.3 58.6 %all-reduce.5.cloned.1.call-done = f32[3,3,256,128]{3,2,1,0:T(8,128)} async-done(((f32[3,3,256,128]{3,2,1,0:T(8,128)}), f32[3,3,256,128]{3,2,1,0:T(8,128)}) %all-reduce.5.cloned.1.call-update) | async-done | bytes 1179664 | tf_op jit(solution)/shard_map/psum | solution.py:122
  247.0 2.4 copy.20
  (94 shorter events, 17.0 us)
Async XLA Ops:
  7.2 7.3 %copy-start = (bf16[48,128,256]{2,1,0:T(8,128)(2,1)S(1)}, bf16[48,128,256]{2,1,0:T(8,128)(2,1)}, u32[]{:S(2)}) copy-start(bf16[48,128,256]{2,1,0:T(8,128)(2,1)} %param.8) | copy-start | bytes 9437188
  7.2 120.0 %reduce-scatter.2.cloned.1.call-start = ((), (), s32[]{:S(2)}) async-start(), calls=%async_computation.1 | async-start | bytes 294912 | tf_op jit(solution)/shard_map/reduce_scatter | solution.py:94
  8.3 7.3 %collective-permute-start = (bf16[14,3,256]{2,1,0:T(4,128)(2,1)S(1)}, bf16[14,3,256]{2,1,0:T(4,128)(2,1)S(1)}, u32[]{:S(2)}, u32[]{:S(2)}) collective-permute-start(bf16[14,3,256]{2,1,0:T(4,128)(2,1)S(1)} %get-tuple-element.3), channel_id=1, source_target_pairs={{0,4},{4,8},{8,12},{12,16},{16,20},{20,24},{24,28},{1,5},{5,9},{9,... | collective-permute-start | bytes 64520 | tf_op jit(solution)/shard_map/ppermute | solution.py:15
  13.1 2.3 copy-start.25
  13.1 2.3 copy-start.22
  13.1 5.8 %collective-permute-start.1 = (bf16[14,3,256]{2,1,0:T(4,128)(2,1)S(1)}, bf16[14,3,256]{2,1,0:T(4,128)(2,1)S(1)}, u32[]{:S(2)}, u32[]{:S(2)}) collective-permute-start(bf16[14,3,256]{2,1,0:T(4,128)(2,1)S(1)} %get-tuple-element.4), channel_id=1, source_target_pairs={{4,0},{8,4},{12,8},{16,12},{20,16},{24,20},{28,24},{5,1},{9,5},{13... | collective-permute-start | bytes 64520 | tf_op jit(solution)/shard_map/ppermute | solution.py:17
  35.1 1.4 copy-start.18
  36.9 1.1 copy-start.16
  38.0 1.1 copy-start.15
  39.2 1.1 copy-start.14
  40.3 1.1 copy-start.13
  41.4 1.1 copy-start.12
  42.6 1.1 copy-start.11
  44.1 1.0 copy-start.23
  57.3 1.4 copy-start.20
  58.7 0.9 copy-start.7
  58.7 1.1 copy-start.9
  58.7 1.4 copy-start.5
  58.7 1.8 copy-start.3
  58.7 2.1 copy-start.1
  62.0 0.7 copy-start.24
  63.0 0.9 copy-start.19
  63.9 2.6 %copy-start.26 = (u32[32]{0:T(128)S(1)}, u32[32]{0:T(128)}, u32[]{:S(2)}) copy-start(u32[32]{0:T(128)} %constant.44) | copy-start | bytes 388
  63.9 63.3 %copy-start.21 = (f32[64,128]{1,0:T(8,128)S(1)}, f32[64,128]{1,0:T(8,128)}, u32[]{:S(2)}) copy-start(f32[64,128]{1,0:T(8,128)} %param.15) | copy-start | bytes 98308
  65.6 181.4 %all-reduce.5.cloned.1.call-start = ((), (), s32[]{:S(2)}) async-start(), calls=%async_computation.2 | async-start | bytes 2359296 | tf_op jit(solution)/shard_map/psum | solution.py:122
  160.1 2.1 copy-start.10
  160.1 2.5 copy-start.8
  162.2 1.1 copy-start.6
  162.7 1.2 copy-start.4
  163.4 1.2 copy-start.2
  166.6 1.0 copy-start.17
Sparse Core Ops, SparseCore 0:
  65.7 61.4 reduce-scatter.1
  167.8 79.1 all-reduce.4
where the time goes:
time: 257 us; the launch traced here: 256 us
  waiting for transfers between devices  102 us (40%)
  blocking collectives  80.8 us (31%)
  local copies, waits for them, and re-layouts  32.6 us (13%)
  between operations  15.1 us (6%)
  matrix products  13.7 us (5%)
  starting transfers between devices  6.22 us (2%)
  other arithmetic  6.08 us (2%)
    psum x1, waiting for transfers between devices, body(): weight_grad, bias_grad = lax.psum((local_weight, local_bias), 'strip')  58.6 us
    reduce_scatter x1, waiting for transfers between devices, body(): lax.psum_scatter(dense_sums, 'strip', scatter_dimension=0, tiled=True)  39.5 us
    all_gather x1, blocking collectives, body(): lax.all_gather(embed_grad / divisor, 'strip', axis=0, tiled=True)  30.9 us
    psum x1, blocking collectives, body(): weight_grad, bias_grad = lax.psum((local_weight, local_bias), 'strip')  20.7 us
    unnamed x1, blocking collectives  19.9 us
    reshape x9, local copies, waits for them, and re-layouts, convolve(): window = padded[shift_row:shift_row + row_count, shift_col:shift_col + co...  11.8 us
    unnamed x56, local copies, waits for them, and re-layouts  11 us
    all_gather x1, blocking collectives, body(): gathered = lax.all_gather(pooled, 'chan', axis=0, tiled=True)  9.38 us
  transfers between devices with their start and end apart: 4, of which 3 were waited for; matrix products, arithmetic and copies ran while one was open for 1% of the time, Pallas kernels for 0%

commit v1 on v0

--- a/solution.py
+++ b/solution.py
@@ -54,6 +54,67 @@
     )
 
 
+def swap(value, axis, mask):
+    count = lax.axis_size(axis)
+    return lax.ppermute(value, axis, [(i, i ^ mask) for i in range(count)])
+
+
+def bit_groups(count, first, most):
+    bits = count.bit_length() - 1
+    groups, at = [], 0
+    while at < bits:
+        size = min(first if at == 0 else most, bits - at)
+        groups.append((at, size))
+        at += size
+    return groups
+
+
+def gather_relative(value, axis, groups):
+    held = value[None]
+    for shift, size in groups:
+        held = jnp.concatenate(
+            [held] + [swap(held, axis, m << shift) for m in range(1, 1 << size)], axis=0
+        )
+    return held
+
+
+def pack(block, extra):
+    lanes = block.shape[-1]
+    top = jnp.maximum(jnp.max(jnp.abs(block)), jnp.max(jnp.abs(extra)))
+    power = jnp.ceil(jnp.log2(jnp.maximum(top, 1e-30)))
+    up = jnp.exp2(12.0 - power)
+    lead = block.shape[:-2]
+    tail = jnp.concatenate(
+        [extra * up, jnp.broadcast_to(power, (15, lanes))], axis=0
+    )
+    tail = jnp.broadcast_to(tail, lead + tail.shape)
+    return jnp.concatenate([block * up, tail], axis=-2).astype(jnp.float16)
+
+
+def unpack(packed):
+    wide = packed.astype(jnp.float32)
+    down = jnp.exp2(wide[..., -1:, :1] - 12.0)
+    return wide[..., :-16, :] * down, wide[..., -16:-15, :] * down
+
+
+def reduce_chunks(chunks, extra, axis, groups):
+    me = lax.axis_index(axis)
+    for shift, size in groups:
+        ways = 1 << size
+        digit = (me >> shift) & (ways - 1)
+        packed = pack(chunks, extra)
+        packed = packed.reshape((-1, ways) + packed.shape[1:])
+        total, total_extra = unpack(lax.dynamic_index_in_dim(packed, digit, 1, False))
+        for m in range(1, ways):
+            part = swap(
+                lax.dynamic_index_in_dim(packed, digit ^ m, 1, False), axis, m << shift
+            )
+            more, more_extra = unpack(part)
+            total, total_extra = total + more, total_extra + more_extra
+        chunks, extra = total, total_extra[0]
+    return chunks[0], extra
+
+
 def body(
     section_input, conv_weight, conv_bias, deep_weight, deep_bias, labels, slot_ids, embed_grad
 ):
@@ -64,6 +125,28 @@
     row_total, col_local, channels = section_input.shape
     row_part = row_total // chan_count
     half_cols = col_local // 2
+    list_len = slot_ids.shape[0]
+    owned, width_deep = embed_grad.shape
+
+    flat_labels = labels.reshape(-1)
+    member = flat_labels[None, :] == jnp.arange(list_len, dtype=jnp.int32)[:, None]
+    part_counts = jnp.sum(member.astype(jnp.float32), axis=1)
+    side = jnp.stack([slot_ids.astype(jnp.float32), part_counts])
+    side = jnp.pad(side, ((0, 6), (0, width_deep - list_len)))
+    small_groups = bit_groups(strip_count, 1, 2)
+    shared = gather_relative(jnp.concatenate([embed_grad, side]), "strip", small_groups)
+    every_id = shared[:, owned, :list_len].reshape(-1).astype(jnp.int32)
+    every_count = shared[:, owned + 1, :list_len].reshape(-1)
+    entry_count = jnp.sum(
+        jnp.where(slot_ids[:, None] == every_id[None, :], every_count[None, :], 0.0), axis=1
+    )
+    own_slots = strip_pos * owned + jnp.arange(owned, dtype=jnp.int32)
+    owner_hot = own_slots[:, None] == every_id[None, :]
+    slot_counts = jnp.sum(jnp.where(owner_hot, every_count[None, :], 0.0), axis=1)
+    place = ((slot_ids // owned) ^ strip_pos) * owned + slot_ids % owned
+    entry_grad = shared[:, :owned].reshape(-1, width_deep)[place]
+    entry_grad = entry_grad / jnp.maximum(entry_count, 1.0)[:, None]
+
     padded_rows = jnp.pad(section_input, ((1, 1), (0, 0), (0, 0)))
     own_rows = lax.dynamic_slice_in_dim(padded_rows, chan_pos * row_part, row_part + 2, 0)
     extended = with_halo(own_rows, (("strip", 1),), 3)
@@ -78,26 +161,14 @@
     padded_deep = jnp.pad(gathered, ((1, 1), (0, 0), (0, 0)))
     half_rows = gathered.shape[0]
     deep_pre = convolve(padded_deep, deep_weight, half_rows, half_cols) + deep_bias
-    width_deep = deep_weight.shape[-1]
     features = swish(deep_pre).astype(jnp.bfloat16).reshape(-1, width_deep)
-    flat_labels = labels.reshape(-1)
-    list_len = slot_ids.shape[0]
-    member = flat_labels[None, :] == jnp.arange(list_len, dtype=jnp.int32)[:, None]
     part_sums = jnp.dot(member.astype(jnp.bfloat16), features, preferred_element_type=jnp.float32)
-    part_counts = jnp.sum(member.astype(jnp.float32), axis=1)
-    owned = embed_grad.shape[0]
-    dense_sums = (
-        jnp.zeros((owned * strip_count, width_deep), jnp.float32).at[slot_ids].set(part_sums)
-    )
-    dense_counts = jnp.zeros((owned * strip_count,), jnp.float32).at[slot_ids].set(part_counts)
-    slot_sums, slot_counts = (
-        lax.psum_scatter(dense_sums, "strip", scatter_dimension=0, tiled=True),
-        lax.psum_scatter(dense_counts, "strip", scatter_dimension=0, tiled=True),
-    )
-    divisor = jnp.maximum(slot_counts, 1.0)[:, None]
-    embeddings = slot_sums / divisor
-    every_grad = lax.all_gather(embed_grad / divisor, "strip", axis=0, tiled=True)
-    entry_grad = every_grad[slot_ids]
+    every_sum = gather_relative(part_sums, "strip", small_groups).reshape(-1, width_deep)
+    slot_sums = jnp.dot(
+        owner_hot.astype(jnp.float32), every_sum, precision=lax.Precision.HIGHEST
+    )
+    embeddings = slot_sums / jnp.maximum(slot_counts, 1.0)[:, None]
+
     pixel_grad = lax.dot_general(
         member.astype(jnp.float32),
         entry_grad,
@@ -117,9 +188,14 @@
                     window, deep_grad, (((0,), (0,)), ((), ())), preferred_element_type=jnp.float32
                 )
             )
-    local_weight = jnp.stack(pieces).reshape(3, 3, channels, width_deep)
-    local_bias = jnp.sum(deep_grad.astype(jnp.float32), axis=0)
-    weight_grad, bias_grad = lax.psum((local_weight, local_bias), "strip")
+    local_weight = jnp.stack(pieces).reshape(strip_count, -1, width_deep)
+    local_bias = jnp.sum(deep_grad.astype(jnp.float32), axis=0, keepdims=True)
+    groups = bit_groups(strip_count, 3, 3)
+    chunk, bias_sum = reduce_chunks(local_weight, local_bias, "strip", groups)
+    packed = gather_relative(pack(chunk, bias_sum), "strip", groups)
+    weight_rows, bias_rows = unpack(packed[jnp.arange(strip_count) ^ strip_pos])
+    weight_grad = weight_rows.reshape(3, 3, channels, width_deep)
+    bias_grad = bias_rows[0, 0]
     return (embeddings, weight_grad, bias_grad)
 
 

time: 257 us -> 145 us (0.56)
  waiting for transfers between devices: 102 us -> 21.4 us
  blocking collectives: 80.8 us -> 9.36 us
  starting transfers between devices: 6.22 us -> 37.2 us
  other arithmetic: 6.08 us -> 16.4 us
  between operations: 15.1 us -> 9.6 us
    psum x1 -> x0, waiting for transfers between devices: 58.6 us -> none  [body(): weight_grad, bias_grad = lax.psum((local_weight, local_bias), 'strip')]
    reduce_scatter x1 -> x0, waiting for transfers between devices: 39.5 us -> none  [body(): lax.psum_scatter(dense_sums, 'strip', scatter_dimension=0, tiled=True)]
    ppermute x0 -> x22, starting transfers between devices: none -> 34 us  [swap(): return lax.ppermute(value, axis, [(i, i ^ mask) for i in range(count)])]
    all_gather x1 -> x0, blocking collectives: 30.9 us -> none  [body(): lax.all_gather(embed_grad / divisor, 'strip', axis=0, tiled=True)]
    psum x1 -> x0, blocking collectives: 20.7 us -> none  [body(): weight_grad, bias_grad = lax.psum((local_weight, local_bias), 'strip')]
    unnamed x1 -> x0, blocking collectives: 19.9 us -> none
    ppermute x0 -> x22, waiting for transfers between devices: none -> 19.3 us  [swap(): return lax.ppermute(value, axis, [(i, i ^ mask) for i in range(count)])]
    slice x0 -> x11, local copies, waits for them, and re-layouts: none -> 4.15 us  [the longest x8 4.11 us: unpack(): down = jnp.exp2(wide[..., -1:, :1] - 12.0)]
  transfers between devices with their start and end apart: 4 -> 24, of which waited for: 3 -> 6; matrix products, arithmetic and copies ran while one was open for 1% -> 27% of each run, Pallas kernels for 0% -> 0%
where the time goes in v1:
time: 145 us; the launch traced here: 144 us
  starting transfers between devices  37.2 us (26%)
  local copies, waits for them, and re-layouts  35 us (24%)
  waiting for transfers between devices  21.4 us (15%)
  other arithmetic  16.4 us (11%)
  matrix products  14.6 us (10%)
  between operations  9.6 us (7%)
  blocking collectives  9.36 us (6%)
    ppermute x22, starting transfers between devices, swap(): return lax.ppermute(value, axis, [(i, i ^ mask) for i in range(count)])  34 us
    ppermute x22, waiting for transfers between devices, swap(): return lax.ppermute(value, axis, [(i, i ^ mask) for i in range(count)])  19.3 us
    reshape x9, local copies, waits for them, and re-layouts, convolve(): window = padded[shift_row:shift_row + row_count, shift_col:shift_col + co...  11.8 us
    all_gather x1, blocking collectives, body(): gathered = lax.all_gather(pooled, 'chan', axis=0, tiled=True)  9.36 us
    unnamed x66, local copies, waits for them, and re-layouts  8.02 us
    dot_general x18, matrix products, convolve(): jnp.dot(window, weight[shift_row, shift_col], preferred_element_type=jnp....  7.62 us
    slice x2, local copies, waits for them, and re-layouts, convolve(): padded[shift_row:shift_row + row_count, shift_col:shift_col + col_count]  4.19 us
    slice x8, local copies, waits for them, and re-layouts, unpack(): down = jnp.exp2(wide[..., -1:, :1] - 12.0)  4.11 us
  transfers between devices with their start and end apart: 24, of which 6 were waited for; matrix products, arithmetic and copies ran while one was open for 27% of the time, Pallas kernels for 0%

profile of v1, /device:TPU:0, one launch (start us, length us, event | category | flops | bytes accessed | tf_op | source)
XLA Modules:
  0.0 143.5 jit_solution(13961548964186269760)
XLA Ops:
  3.1 2.9 %collective-permute-start = (f32[1,72,128]{2,1,0:T(8,128)S(1)}, f32[1,72,128]{2,1,0:T(8,128)S(1)}, u32[]{:S(2)}, u32[]{:S(2)}) collective-permute-start(f32[1,72,128]{2,1,0:T(8,128)S(1)} %maximum_bitcast_fusion), channel_id=1, source_target_pairs={{0,4},{4,0},{8,12},{12,8},{16,20},{20,16},{24,28},{28,24},{1,5},{5... | collective-permute-start | bytes 110600 | tf_op jit(solution)/shard_map/ppermute | solution.py:59
  7.0 1.9 %collective-permute-start.4 = (bf16[14,3,256]{2,1,0:T(4,128)(2,1)S(1)}, bf16[14,3,256]{2,1,0:T(4,128)(2,1)S(1)}, u32[]{:S(2)}, u32[]{:S(2)}) collective-permute-start(bf16[14,3,256]{2,1,0:T(4,128)(2,1)S(1)} %get-tuple-element.7), channel_id=1, source_target_pairs={{0,4},{4,8},{8,12},{12,16},{16,20},{20,24},{24,28},{1,5},{5,9},{9,... | collective-permute-start | bytes 64520 | tf_op jit(solution)/shard_map/ppermute | solution.py:15
  13.6 2.1 %collective-permute-done.5 = bf16[14,3,256]{2,1,0:T(4,128)(2,1)S(1)} collective-permute-done((bf16[14,3,256]{2,1,0:T(4,128)(2,1)S(1)}, bf16[14,3,256]{2,1,0:T(4,128)(2,1)S(1)}, u32[]{:S(2)}, u32[]{:S(2)}) %collective-permute-start.5) | collective-permute-done | bytes 21536 | tf_op jit(solution)/shard_map/ppermute | solution.py:17
  15.7 1.6 %pad_maximum_fusion = bf16[14,134,256]{2,1,0:T(8,128)(2,1)S(1)} fusion(bf16[14,3,256]{2,1,0:T(4,128)(2,1)S(1)} %collective-permute-done.5, bf16[14,128,256]{2,1,0:T(8,128)(2,1)} %pad_dynamic-slice_fusion.2, bf16[14,3,256]{2,1,0:T(4,128)(2,1)S(1)} %collective-permute-done.4), kind=kLoop, calls=%fused_computation.57 | loop fusion | flops 2881536 | bytes 1921024 | tf_op jit(solution)/shard_map/concatenate | solution.py:13
  17.4 2.8 %fusion.92 = (bf16[12,132,256]{2,1,0:T(8,128)(2,1)}, bf16[12,132,256]{2,1,0:T(8,128)(2,1)}, bf16[12,132,256]{2,1,0:T(8,128)(2,1)}, bf16[12,132,256]{2,1,0:T(8,12...) fusion(bf16[14,134,256]{2,1,0:T(8,128)(2,1)S(1)} %pad_maximum_f, ...), kind=kLoop, calls=%fused_computation.224 | loop fusion | bytes 14598144 | tf_op jit(solution)/shard_map/slice | solution.py:38
  20.2 2.0 %reshape.259 = bf16[1584,256]{1,0:T(8,128)(2,1)} reshape(bf16[12,132,256]{2,1,0:T(8,128)(2,1)} %get-tuple-element.9) | data formatting | bytes 1622016 | tf_op jit(solution)/shard_map/reshape | solution.py:40
  22.2 2.0 %reshape.258 = bf16[1584,256]{1,0:T(8,128)(2,1)} reshape(bf16[12,132,256]{2,1,0:T(8,128)(2,1)} %get-tuple-element.10) | data formatting | bytes 1622016 | tf_op jit(solution)/shard_map/reshape | solution.py:40
  24.3 2.0 %reshape.257 = bf16[1584,256]{1,0:T(8,128)(2,1)} reshape(bf16[12,132,256]{2,1,0:T(8,128)(2,1)} %get-tuple-element.11) | data formatting | bytes 1622016 | tf_op jit(solution)/shard_map/reshape | solution.py:40
  26.3 2.1 %reshape.256 = bf16[1584,256]{1,0:T(8,128)(2,1)} reshape(bf16[12,132,256]{2,1,0:T(8,128)(2,1)} %get-tuple-element.12) | data formatting | bytes 1622016 | tf_op jit(solution)/shard_map/reshape | solution.py:40
  28.4 2.1 %reshape.255 = bf16[1584,256]{1,0:T(8,128)(2,1)} reshape(bf16[12,132,256]{2,1,0:T(8,128)(2,1)} %get-tuple-element.13) | data formatting | bytes 1622016 | tf_op jit(solution)/shard_map/reshape | solution.py:40
  32.0 1.4 fusion.27
  42.0 2.7 %fusion.2 = f32[6,66,256]{2,1,0:T(8,128)S(1)} fusion(f32[6,2,66,2,256]{4,3,2,1,0:T(2,128)S(1)} %reshape.260, f32[256]{0:T(256)S(1)} %copy-done.25), kind=kLoop, calls=%fused_computation.33 | loop fusion | flops 2331648 | bytes 2028544 | tf_op jit(solution)/shard_map/reduce_sum | solution.py:52
  44.8 9.4 %all_gather.3 = bf16[24,66,256]{2,1,0:T(8,128)(2,1)S(1)} all-gather(bf16[6,66,256]{2,1,0:T(8,128)(2,1)S(1)} %fusion.12), channel_id=1, replica_groups=mesh['strip'=8,'chan'=4] {'chan'}, dimensions={0}, use_global_device_ids=true | all-gather | bytes 1013760 | tf_op jit(solution)/shard_map/all_gather | solution.py:160
  54.1 1.4 pad_slice_fusion
  60.7 2.9 %collective-permute-start.6 = (f32[1,32,128]{2,1,0:T(8,128)S(1)}, f32[1,32,128]{2,1,0:T(8,128)S(1)}, u32[]{:S(2)}, u32[]{:S(2)}) collective-permute-start(f32[1,32,128]{2,1,0:T(8,128)S(1)} %get-tuple-element.40), channel_id=1, source_target_pairs={{0,4},{4,0},{8,12},{12,8},{16,20},{20,16},{24,28},{28,24},{1,5},{5... | collective-permute-start | bytes 49160 | tf_op jit(solution)/shard_map/ppermute | solution.py:59
  63.7 2.2 %collective-permute-start.3 = (f32[2,72,128]{2,1,0:T(8,128)S(1)}, f32[2,72,128]{2,1,0:T(8,128)S(1)}, u32[]{:S(2)}, u32[]{:S(2)}) collective-permute-start(f32[2,72,128]{2,1,0:T(8,128)S(1)} %pad_maximum_fusion.1), channel_id=1, source_target_pairs={{0,24},{4,28},{8,16},{12,20},{16,8},{20,12},{24,0},{28,4},{1,25},{... | collective-permute-start | bytes 221192 | tf_op jit(solution)/shard_map/ppermute | solution.py:59
  66.8 1.4 collective-permute-start.1
  68.1 2.2 %collective-permute-start.9 = (f32[2,32,128]{2,1,0:T(8,128)S(1)}, f32[2,32,128]{2,1,0:T(8,128)S(1)}, u32[]{:S(2)}, u32[]{:S(2)}) collective-permute-start(f32[2,32,128]{2,1,0:T(8,128)S(1)} %pad_maximum_fusion.2), channel_id=1, source_target_pairs={{0,24},{4,28},{8,16},{12,20},{16,8},{20,12},{24,0},{28,4},{1,25},{... | collective-permute-start | bytes 98312 | tf_op jit(solution)/shard_map/ppermute | solution.py:59
  70.4 4.5 %collective-permute-done.7 = f32[2,32,128]{2,1,0:T(8,128)S(1)} collective-permute-done((f32[2,32,128]{2,1,0:T(8,128)S(1)}, f32[2,32,128]{2,1,0:T(8,128)S(1)}, u32[]{:S(2)}, u32[]{:S(2)}) %collective-permute-start.7) | collective-permute-done | bytes 32800 | tf_op jit(solution)/shard_map/ppermute | solution.py:59
  75.0 4.8 %collective-permute-done.8 = f32[2,32,128]{2,1,0:T(8,128)S(1)} collective-permute-done((f32[2,32,128]{2,1,0:T(8,128)S(1)}, f32[2,32,128]{2,1,0:T(8,128)S(1)}, u32[]{:S(2)}, u32[]{:S(2)}) %collective-permute-start.8) | collective-permute-done | bytes 32800 | tf_op jit(solution)/shard_map/ppermute | solution.py:59
  83.4 2.1 %convert_reduce_fusion = (f32[128]{0:T(128)S(1)}, bf16[1536,128]{1,0:T(8,128)(2,1)S(1)}) fusion(f32[1536,128]{1,0:T(8,128)} %copy-done.19, f32[32,128]{1,0:T(8,128)} %gather_fusion, f32[32]{0:T(128)} %broadcast_maximum_fusion, s32[1536]{0:T(1024)S(1)} %eq.70), kind=kOutput, calls=%fused_computation.58 | convolution fusion | flops 77713280 | bytes 1202816 | tf_op jit(solution)/shard_map/dot_general | solution.py:172
  93.5 1.4 multiply_convert_fusion
  95.1 1.7 %collective-permute-start.15 = (f16[1,304,128]{2,1,0:T(8,128)(2,1)S(1)}, f16[1,304,128]{2,1,0:T(8,128)(2,1)S(1)}, u32[]{:S(2)}, u32[]{:S(2)}) collective-permute-start(f16[1,304,128]{2,1,0:T(8,128)(2,1)S(1)} %get-tuple-element.33), channel_id=1, source_target_pairs={{0,24},{4,28},{8,16},{12,20},{16,8},{20,12},{24,0},{28,4},{1,25},{... | collective-permute-start | bytes 233480 | tf_op jit(solution)/shard_map/ppermute | solution.py:59
  96.8 3.1 %collective-permute-start.16 = (f16[1,304,128]{2,1,0:T(8,128)(2,1)S(1)}, f16[1,304,128]{2,1,0:T(8,128)(2,1)S(1)}, u32[]{:S(2)}, u32[]{:S(2)}) collective-permute-start(f16[1,304,128]{2,1,0:T(8,128)(2,1)S(1)} %get-tuple-element.34), channel_id=1, source_target_pairs={{0,28},{4,24},{8,20},{12,16},{16,12},{20,8},{24,4},{28,0},{1,29},{... | collective-permute-start | bytes 233480 | tf_op jit(solution)/shard_map/ppermute | solution.py:59
  100.6 3.0 %collective-permute-start.12 = (f16[1,304,128]{2,1,0:T(8,128)(2,1)S(1)}, f16[1,304,128]{2,1,0:T(8,128)(2,1)S(1)}, u32[]{:S(2)}, u32[]{:S(2)}) collective-permute-start(f16[1,304,128]{2,1,0:T(8,128)(2,1)S(1)} %get-tuple-element.30), channel_id=1, source_target_pairs={{0,12},{4,8},{8,4},{12,0},{16,28},{20,24},{24,20},{28,16},{1,13},{... | collective-permute-start | bytes 233480 | tf_op jit(solution)/shard_map/ppermute | solution.py:59
  104.9 1.8 %collective-permute-start.14 = (f16[1,304,128]{2,1,0:T(8,128)(2,1)S(1)}, f16[1,304,128]{2,1,0:T(8,128)(2,1)S(1)}, u32[]{:S(2)}, u32[]{:S(2)}) collective-permute-start(f16[1,304,128]{2,1,0:T(8,128)(2,1)S(1)} %get-tuple-element.32), channel_id=1, source_target_pairs={{0,20},{4,16},{8,28},{12,24},{16,4},{20,0},{24,12},{28,8},{1,21},{... | collective-permute-start | bytes 233480 | tf_op jit(solution)/shard_map/ppermute | solution.py:59
  119.6 1.6 %collective-permute-start.17 = (f16[1,304,128]{2,1,0:T(8,128)(2,1)S(1)}, f16[1,304,128]{2,1,0:T(8,128)(2,1)S(1)}, u32[]{:S(2)}, u32[]{:S(2)}) collective-permute-start(f16[1,304,128]{2,1,0:T(8,128)(2,1)S(1)} %get-tuple-element.35), channel_id=1, source_target_pairs={{0,4},{4,0},{8,12},{12,8},{16,20},{20,16},{24,28},{28,24},{1,5},{5... | collective-permute-start | bytes 233480 | tf_op jit(solution)/shard_map/ppermute | solution.py:59
  123.2 1.9 %collective-permute-start.21 = (f16[1,304,128]{2,1,0:T(8,128)(2,1)S(1)}, f16[1,304,128]{2,1,0:T(8,128)(2,1)S(1)}, u32[]{:S(2)}, u32[]{:S(2)}) collective-permute-start(f16[1,304,128]{2,1,0:T(8,128)(2,1)S(1)} %get-tuple-element.35), channel_id=1, source_target_pairs={{0,20},{4,16},{8,28},{12,24},{16,4},{20,0},{24,12},{28,8},{1,21},{... | collective-permute-start | bytes 233480 | tf_op jit(solution)/shard_map/ppermute | solution.py:59
  127.4 1.7 %collective-permute-start.18 = (f16[1,304,128]{2,1,0:T(8,128)(2,1)S(1)}, f16[1,304,128]{2,1,0:T(8,128)(2,1)S(1)}, u32[]{:S(2)}, u32[]{:S(2)}) collective-permute-start(f16[1,304,128]{2,1,0:T(8,128)(2,1)S(1)} %get-tuple-element.35), channel_id=1, source_target_pairs={{0,8},{4,12},{8,0},{12,4},{16,24},{20,28},{24,16},{28,20},{1,9},{5... | collective-permute-start | bytes 233480 | tf_op jit(solution)/shard_map/ppermute | solution.py:59
  129.1 4.4 %collective-permute-done.18 = f16[1,304,128]{2,1,0:T(8,128)(2,1)S(1)} collective-permute-done((f16[1,304,128]{2,1,0:T(8,128)(2,1)S(1)}, f16[1,304,128]{2,1,0:T(8,128)(2,1)S(1)}, u32[]{:S(2)}, u32[]{:S(2)}) %collective-permute-start.18) | collective-permute-done | bytes 77856 | tf_op jit(solution)/shard_map/ppermute | solution.py:59
  133.5 2.4 %collective-permute-start.23 = (f16[1,304,128]{2,1,0:T(8,128)(2,1)S(1)}, f16[1,304,128]{2,1,0:T(8,128)(2,1)S(1)}, u32[]{:S(2)}, u32[]{:S(2)}) collective-permute-start(f16[1,304,128]{2,1,0:T(8,128)(2,1)S(1)} %get-tuple-element.35), channel_id=1, source_target_pairs={{0,28},{4,24},{8,20},{12,16},{16,12},{20,8},{24,4},{28,0},{1,29},{... | collective-permute-start | bytes 233480 | tf_op jit(solution)/shard_map/ppermute | solution.py:59
  136.1 4.5 %collective-permute-done.23 = f16[1,304,128]{2,1,0:T(8,128)(2,1)S(1)} collective-permute-done((f16[1,304,128]{2,1,0:T(8,128)(2,1)S(1)}, f16[1,304,128]{2,1,0:T(8,128)(2,1)S(1)}, u32[]{:S(2)}, u32[]{:S(2)}) %collective-permute-start.23) | collective-permute-done | bytes 77856 | tf_op jit(solution)/shard_map/ppermute | solution.py:59
  (192 shorter events, 49.8 us)
Async XLA Ops:
  3.1 60.6 %collective-permute-start = (f32[1,72,128]{2,1,0:T(8,128)S(1)}, f32[1,72,128]{2,1,0:T(8,128)S(1)}, u32[]{:S(2)}, u32[]{:S(2)}) collective-permute-start(f32[1,72,128]{2,1,0:T(8,128)S(1)} %maximum_bitcast_fusion), channel_id=1, source_target_pairs={{0,4},{4,0},{8,12},{12,8},{16,20},{20,16},{24,28},{28,24},{1,5},{5... | collective-permute-start | bytes 110600 | tf_op jit(solution)/shard_map/ppermute | solution.py:59
  6.0 4.3 %copy-start.22 = (f32[64,128]{1,0:T(8,128)S(1)}, f32[64,128]{1,0:T(8,128)}, u32[]{:S(2)}) copy-start(f32[64,128]{1,0:T(8,128)} %param.15) | copy-start | bytes 98308
  6.0 4.9 %copy-start = (bf16[48,128,256]{2,1,0:T(8,128)(2,1)S(1)}, bf16[48,128,256]{2,1,0:T(8,128)(2,1)}, u32[]{:S(2)}) copy-start(bf16[48,128,256]{2,1,0:T(8,128)(2,1)} %param.8) | copy-start | bytes 9437188
  7.0 6.6 %collective-permute-start.4 = (bf16[14,3,256]{2,1,0:T(4,128)(2,1)S(1)}, bf16[14,3,256]{2,1,0:T(4,128)(2,1)S(1)}, u32[]{:S(2)}, u32[]{:S(2)}) collective-permute-start(bf16[14,3,256]{2,1,0:T(4,128)(2,1)S(1)} %get-tuple-element.7), channel_id=1, source_target_pairs={{0,4},{4,8},{8,12},{12,16},{16,20},{20,24},{24,28},{1,5},{5,9},{9,... | collective-permute-start | bytes 64520 | tf_op jit(solution)/shard_map/ppermute | solution.py:15
  9.0 6.8 %collective-permute-start.5 = (bf16[14,3,256]{2,1,0:T(4,128)(2,1)S(1)}, bf16[14,3,256]{2,1,0:T(4,128)(2,1)S(1)}, u32[]{:S(2)}, u32[]{:S(2)}) collective-permute-start(bf16[14,3,256]{2,1,0:T(4,128)(2,1)S(1)} %get-tuple-element.8), channel_id=1, source_target_pairs={{4,0},{8,4},{12,8},{16,12},{20,16},{24,20},{28,24},{5,1},{9,5},{13... | collective-permute-start | bytes 64520 | tf_op jit(solution)/shard_map/ppermute | solution.py:17
  55.5 1.8 %copy-start.3 = (bf16[24,64,256]{2,1,0:T(8,128)(2,1)}, bf16[24,64,256]{2,1,0:T(8,128)(2,1)S(1)}, u32[]{:S(2)}) copy-start(bf16[24,64,256]{2,1,0:T(8,128)(2,1)S(1)} %get-tuple-element.25) | copy-start | bytes 2359300
  55.6 2.1 %copy-start.1 = (bf16[24,64,256]{2,1,0:T(8,128)(2,1)}, bf16[24,64,256]{2,1,0:T(8,128)(2,1)S(1)}, u32[]{:S(2)}) copy-start(bf16[24,64,256]{2,1,0:T(8,128)(2,1)S(1)} %get-tuple-element.24) | copy-start | bytes 2359300
  59.8 8.3 %copy-start.21 = (f32[8,72,128]{2,1,0:T(8,128)S(1)}, f32[8,72,128]{2,1,0:T(8,128)}, u32[]{:S(2)}) copy-start(f32[8,72,128]{2,1,0:T(8,128)} %constant_dynamic-update-slice_fusion.4) | copy-start | bytes 884740
  60.7 7.4 %collective-permute-start.6 = (f32[1,32,128]{2,1,0:T(8,128)S(1)}, f32[1,32,128]{2,1,0:T(8,128)S(1)}, u32[]{:S(2)}, u32[]{:S(2)}) collective-permute-start(f32[1,32,128]{2,1,0:T(8,128)S(1)} %get-tuple-element.40), channel_id=1, source_target_pairs={{0,4},{4,0},{8,12},{12,8},{16,20},{20,16},{24,28},{28,24},{1,5},{5... | collective-permute-start | bytes 49160 | tf_op jit(solution)/shard_map/ppermute | solution.py:59
  63.7 16.2 %collective-permute-start.3 = (f32[2,72,128]{2,1,0:T(8,128)S(1)}, f32[2,72,128]{2,1,0:T(8,128)S(1)}, u32[]{:S(2)}, u32[]{:S(2)}) collective-permute-start(f32[2,72,128]{2,1,0:T(8,128)S(1)} %pad_maximum_fusion.1), channel_id=1, source_target_pairs={{0,24},{4,28},{8,16},{12,20},{16,8},{20,12},{24,0},{28,4},{1,25},{... | collective-permute-start | bytes 221192 | tf_op jit(solution)/shard_map/ppermute | solution.py:59
  65.8 14.0 %collective-permute-start.2 = (f32[2,72,128]{2,1,0:T(8,128)S(1)}, f32[2,72,128]{2,1,0:T(8,128)S(1)}, u32[]{:S(2)}, u32[]{:S(2)}) collective-permute-start(f32[2,72,128]{2,1,0:T(8,128)S(1)} %pad_maximum_fusion.1), channel_id=1, source_target_pairs={{0,16},{4,20},{8,24},{12,28},{16,0},{20,4},{24,8},{28,12},{1,17},{... | collective-permute-start | bytes 221192 | tf_op jit(solution)/shard_map/ppermute | solution.py:59
  66.8 13.1 %collective-permute-start.1 = (f32[2,72,128]{2,1,0:T(8,128)S(1)}, f32[2,72,128]{2,1,0:T(8,128)S(1)}, u32[]{:S(2)}, u32[]{:S(2)}) collective-permute-start(f32[2,72,128]{2,1,0:T(8,128)S(1)} %pad_maximum_fusion.1), channel_id=1, source_target_pairs={{0,8},{4,12},{8,0},{12,4},{16,24},{20,28},{24,16},{28,20},{1,9},{5... | collective-permute-start | bytes 221192 | tf_op jit(solution)/shard_map/ppermute | solution.py:59
  68.1 11.7 %collective-permute-start.9 = (f32[2,32,128]{2,1,0:T(8,128)S(1)}, f32[2,32,128]{2,1,0:T(8,128)S(1)}, u32[]{:S(2)}, u32[]{:S(2)}) collective-permute-start(f32[2,32,128]{2,1,0:T(8,128)S(1)} %pad_maximum_fusion.2), channel_id=1, source_target_pairs={{0,24},{4,28},{8,16},{12,20},{16,8},{20,12},{24,0},{28,4},{1,25},{... | collective-permute-start | bytes 98312 | tf_op jit(solution)/shard_map/ppermute | solution.py:59
  70.3 4.7 %collective-permute-start.7 = (f32[2,32,128]{2,1,0:T(8,128)S(1)}, f32[2,32,128]{2,1,0:T(8,128)S(1)}, u32[]{:S(2)}, u32[]{:S(2)}) collective-permute-start(f32[2,32,128]{2,1,0:T(8,128)S(1)} %pad_maximum_fusion.2), channel_id=1, source_target_pairs={{0,8},{4,12},{8,0},{12,4},{16,24},{20,28},{24,16},{28,20},{1,9},{5... | collective-permute-start | bytes 98312 | tf_op jit(solution)/shard_map/ppermute | solution.py:59
  75.0 4.8 %collective-permute-start.8 = (f32[2,32,128]{2,1,0:T(8,128)S(1)}, f32[2,32,128]{2,1,0:T(8,128)S(1)}, u32[]{:S(2)}, u32[]{:S(2)}) collective-permute-start(f32[2,32,128]{2,1,0:T(8,128)S(1)} %pad_maximum_fusion.2), channel_id=1, source_target_pairs={{0,16},{4,20},{8,24},{12,28},{16,0},{20,4},{24,8},{28,12},{1,17},{... | collective-permute-start | bytes 98312 | tf_op jit(solution)/shard_map/ppermute | solution.py:59
  83.4 2.7 %copy-start.10 = (bf16[24,64,256]{2,1,0:T(8,128)(2,1)S(1)}, bf16[24,64,256]{2,1,0:T(8,128)(2,1)}, u32[]{:S(2)}) copy-start(bf16[24,64,256]{2,1,0:T(8,128)(2,1)} %copy-done.9) | copy-start | bytes 2359300
  94.9 8.6 %copy-start.23 = (f32[256]{0:T(256)S(1)}, f32[256]{0:T(256)}, u32[]{:S(2)}) copy-start(f32[256]{0:T(256)} %broadcast_in_dim.70) | copy-start | bytes 3076
  94.9 8.6 %copy-start.24 = (s32[64]{0:T(128)S(1)}, s32[64]{0:T(128)}, u32[]{:S(2)}) copy-start(s32[64]{0:T(128)} %iota_add_fusion) | copy-start | bytes 772
  95.1 8.7 %collective-permute-start.15 = (f16[1,304,128]{2,1,0:T(8,128)(2,1)S(1)}, f16[1,304,128]{2,1,0:T(8,128)(2,1)S(1)}, u32[]{:S(2)}, u32[]{:S(2)}) collective-permute-start(f16[1,304,128]{2,1,0:T(8,128)(2,1)S(1)} %get-tuple-element.33), channel_id=1, source_target_pairs={{0,24},{4,28},{8,16},{12,20},{16,8},{20,12},{24,0},{28,4},{1,25},{... | collective-permute-start | bytes 233480 | tf_op jit(solution)/shard_map/ppermute | solution.py:59
  96.8 8.1 %collective-permute-start.16 = (f16[1,304,128]{2,1,0:T(8,128)(2,1)S(1)}, f16[1,304,128]{2,1,0:T(8,128)(2,1)S(1)}, u32[]{:S(2)}, u32[]{:S(2)}) collective-permute-start(f16[1,304,128]{2,1,0:T(8,128)(2,1)S(1)} %get-tuple-element.34), channel_id=1, source_target_pairs={{0,28},{4,24},{8,20},{12,16},{16,12},{20,8},{24,4},{28,0},{1,29},{... | collective-permute-start | bytes 233480 | tf_op jit(solution)/shard_map/ppermute | solution.py:59
  100.0 10.4 %collective-permute-start.10 = (f16[1,304,128]{2,1,0:T(8,128)(2,1)S(1)}, f16[1,304,128]{2,1,0:T(8,128)(2,1)S(1)}, u32[]{:S(2)}, u32[]{:S(2)}) collective-permute-start(f16[1,304,128]{2,1,0:T(8,128)(2,1)S(1)} %get-tuple-element.28), channel_id=1, source_target_pairs={{0,4},{4,0},{8,12},{12,8},{16,20},{20,16},{24,28},{28,24},{1,5},{5... | collective-permute-start | bytes 233480 | tf_op jit(solution)/shard_map/ppermute | solution.py:59
  100.6 11.0 %collective-permute-start.11 = (f16[1,304,128]{2,1,0:T(8,128)(2,1)S(1)}, f16[1,304,128]{2,1,0:T(8,128)(2,1)S(1)}, u32[]{:S(2)}, u32[]{:S(2)}) collective-permute-start(f16[1,304,128]{2,1,0:T(8,128)(2,1)S(1)} %get-tuple-element.29), channel_id=1, source_target_pairs={{0,8},{4,12},{8,0},{12,4},{16,24},{20,28},{24,16},{28,20},{1,9},{5... | collective-permute-start | bytes 233480 | tf_op jit(solution)/shard_map/ppermute | solution.py:59
  100.6 12.3 %collective-permute-start.12 = (f16[1,304,128]{2,1,0:T(8,128)(2,1)S(1)}, f16[1,304,128]{2,1,0:T(8,128)(2,1)S(1)}, u32[]{:S(2)}, u32[]{:S(2)}) collective-permute-start(f16[1,304,128]{2,1,0:T(8,128)(2,1)S(1)} %get-tuple-element.30), channel_id=1, source_target_pairs={{0,12},{4,8},{8,4},{12,0},{16,28},{20,24},{24,20},{28,16},{1,13},{... | collective-permute-start | bytes 233480 | tf_op jit(solution)/shard_map/ppermute | solution.py:59
  103.8 10.3 %collective-permute-start.13 = (f16[1,304,128]{2,1,0:T(8,128)(2,1)S(1)}, f16[1,304,128]{2,1,0:T(8,128)(2,1)S(1)}, u32[]{:S(2)}, u32[]{:S(2)}) collective-permute-start(f16[1,304,128]{2,1,0:T(8,128)(2,1)S(1)} %get-tuple-element.31), channel_id=1, source_target_pairs={{0,16},{4,20},{8,24},{12,28},{16,0},{20,4},{24,8},{28,12},{1,17},{... | collective-permute-start | bytes 233480 | tf_op jit(solution)/shard_map/ppermute | solution.py:59
  104.9 10.5 %collective-permute-start.14 = (f16[1,304,128]{2,1,0:T(8,128)(2,1)S(1)}, f16[1,304,128]{2,1,0:T(8,128)(2,1)S(1)}, u32[]{:S(2)}, u32[]{:S(2)}) collective-permute-start(f16[1,304,128]{2,1,0:T(8,128)(2,1)S(1)} %get-tuple-element.32), channel_id=1, source_target_pairs={{0,20},{4,16},{8,28},{12,24},{16,4},{20,0},{24,12},{28,8},{1,21},{... | collective-permute-start | bytes 233480 | tf_op jit(solution)/shard_map/ppermute | solution.py:59
  119.6 7.8 %collective-permute-start.17 = (f16[1,304,128]{2,1,0:T(8,128)(2,1)S(1)}, f16[1,304,128]{2,1,0:T(8,128)(2,1)S(1)}, u32[]{:S(2)}, u32[]{:S(2)}) collective-permute-start(f16[1,304,128]{2,1,0:T(8,128)(2,1)S(1)} %get-tuple-element.35), channel_id=1, source_target_pairs={{0,4},{4,0},{8,12},{12,8},{16,20},{20,16},{24,28},{28,24},{1,5},{5... | collective-permute-start | bytes 233480 | tf_op jit(solution)/shard_map/ppermute | solution.py:59
  122.0 14.0 %collective-permute-start.22 = (f16[1,304,128]{2,1,0:T(8,128)(2,1)S(1)}, f16[1,304,128]{2,1,0:T(8,128)(2,1)S(1)}, u32[]{:S(2)}, u32[]{:S(2)}) collective-permute-start(f16[1,304,128]{2,1,0:T(8,128)(2,1)S(1)} %get-tuple-element.35), channel_id=1, source_target_pairs={{0,24},{4,28},{8,16},{12,20},{16,8},{20,12},{24,0},{28,4},{1,25},{... | collective-permute-start | bytes 233480 | tf_op jit(solution)/shard_map/ppermute | solution.py:59
  123.2 12.7 %collective-permute-start.21 = (f16[1,304,128]{2,1,0:T(8,128)(2,1)S(1)}, f16[1,304,128]{2,1,0:T(8,128)(2,1)S(1)}, u32[]{:S(2)}, u32[]{:S(2)}) collective-permute-start(f16[1,304,128]{2,1,0:T(8,128)(2,1)S(1)} %get-tuple-element.35), channel_id=1, source_target_pairs={{0,20},{4,16},{8,28},{12,24},{16,4},{20,0},{24,12},{28,8},{1,21},{... | collective-permute-start | bytes 233480 | tf_op jit(solution)/shard_map/ppermute | solution.py:59
  125.2 10.8 %collective-permute-start.20 = (f16[1,304,128]{2,1,0:T(8,128)(2,1)S(1)}, f16[1,304,128]{2,1,0:T(8,128)(2,1)S(1)}, u32[]{:S(2)}, u32[]{:S(2)}) collective-permute-start(f16[1,304,128]{2,1,0:T(8,128)(2,1)S(1)} %get-tuple-element.35), channel_id=1, source_target_pairs={{0,16},{4,20},{8,24},{12,28},{16,0},{20,4},{24,8},{28,12},{1,17},{... | collective-permute-start | bytes 233480 | tf_op jit(solution)/shard_map/ppermute | solution.py:59
  126.5 9.4 %collective-permute-start.19 = (f16[1,304,128]{2,1,0:T(8,128)(2,1)S(1)}, f16[1,304,128]{2,1,0:T(8,128)(2,1)S(1)}, u32[]{:S(2)}, u32[]{:S(2)}) collective-permute-start(f16[1,304,128]{2,1,0:T(8,128)(2,1)S(1)} %get-tuple-element.35), channel_id=1, source_target_pairs={{0,12},{4,8},{8,4},{12,0},{16,28},{20,24},{24,20},{28,16},{1,13},{... | collective-permute-start | bytes 233480 | tf_op jit(solution)/shard_map/ppermute | solution.py:59
  127.4 6.1 %collective-permute-start.18 = (f16[1,304,128]{2,1,0:T(8,128)(2,1)S(1)}, f16[1,304,128]{2,1,0:T(8,128)(2,1)S(1)}, u32[]{:S(2)}, u32[]{:S(2)}) collective-permute-start(f16[1,304,128]{2,1,0:T(8,128)(2,1)S(1)} %get-tuple-element.35), channel_id=1, source_target_pairs={{0,8},{4,12},{8,0},{12,4},{16,24},{20,28},{24,16},{28,20},{1,9},{5... | collective-permute-start | bytes 233480 | tf_op jit(solution)/shard_map/ppermute | solution.py:59
  133.5 7.1 %collective-permute-start.23 = (f16[1,304,128]{2,1,0:T(8,128)(2,1)S(1)}, f16[1,304,128]{2,1,0:T(8,128)(2,1)S(1)}, u32[]{:S(2)}, u32[]{:S(2)}) collective-permute-start(f16[1,304,128]{2,1,0:T(8,128)(2,1)S(1)} %get-tuple-element.35), channel_id=1, source_target_pairs={{0,28},{4,24},{8,20},{12,16},{16,12},{20,8},{24,4},{28,0},{1,29},{... | collective-permute-start | bytes 233480 | tf_op jit(solution)/shard_map/ppermute | solution.py:59
  (19 other events, 21.4 us)

commit v2 on v0

v2 whole, which is shorter than its diff:
```python
import functools

import jax
import jax.numpy as jnp
from jax import lax
from jax.experimental import pallas as pl
from jax.experimental.pallas import tpu as pltpu
from jax.sharding import PartitionSpec as P

F32, BF16, F16 = jnp.float32, jnp.bfloat16, jnp.float16
VMEM = pl.BlockSpec(memory_space=pltpu.VMEM)
SMEM = pl.BlockSpec(memory_space=pltpu.SMEM)
SIDE = 8
NOTE = 16


def params():
    return pltpu.CompilerParams(vmem_limit_bytes=48 << 20)


def swap(value, axis, mask):
    count = lax.axis_size(axis)
    return lax.ppermute(value, axis, [(i, i ^ mask) for i in range(count)])


def bit_groups(count, first, most):
    bits = count.bit_length() - 1
    groups, at = [], 0
    while at < bits:
        size = min(first if at == 0 else most, bits - at)
        groups.append((at, size))
        at += size
    return groups


def gather_relative(value, axis, groups):
    parts = [value[None]]
    for shift, size in groups:
        held = parts[0] if len(parts) == 1 else jnp.concatenate(parts, axis=0)
        parts = [held] + [swap(held, axis, m << shift) for m in range(1, 1 << size)]
    return parts


def conv_kernel(where_ref, x_ref, w_ref, b_ref, out_ref, wide, taps, *, block):
    rows, cols, chans = x_ref.shape
    half_cols = cols // 2
    out_rows = out_ref.shape[0]
    first = where_ref[0] * (2 * out_rows) - 1
    total = 2 * out_rows + 2
    lanes = chans // 128
    edge = jnp.zeros((8, 128), F32)
    for t in range(wide.shape[0]):
        wide[t, 0:8] = edge
        wide[t, cols + 8 : cols + 16] = edge

    def prepare(i, slot):
        r = first + i
        inside = (r >= 0) & (r < rows)
        x = x_ref[jnp.clip(r, 0, rows - 1)].astype(F32)
        x = jnp.where(inside, x, 0.0)
        for t in range(lanes):
            wide[slot * lanes + t, 8 : 8 + cols] = x[:, t * 128 : (t + 1) * 128]
        for tap in range(4):
            for t in range(lanes):
                piece = wide[slot * lanes + t, pl.ds(7 + tap, half_cols, stride=2), :]
                at = (tap * lanes + t) * 128
                taps[i, :, at : at + 128] = piece.astype(BF16)

    def prepare_two(k, carry):
        prepare(2 * k, 0)
        prepare(2 * k + 1, 1)
        return carry

    lax.fori_loop(0, total // 2, prepare_two, 0)
    bias = b_ref[...]

    def step(k, carry):
        r0 = k * 2 * block
        acc = None
        for phase in range(2):
            lhs = jnp.concatenate(
                [
                    taps[pl.ds(r0 + dr, 2 * block), :, phase * chans : (phase + 3) * chans]
                    for dr in range(3)
                ],
                axis=-1,
            ).reshape(2 * block * half_cols, 9 * chans)
            v = jnp.dot(lhs, w_ref[...], preferred_element_type=F32) + bias
            h = (v * jax.nn.sigmoid(v)).reshape(block, 2, half_cols, chans)
            h = h[:, 0] + h[:, 1]
            acc = h if acc is None else acc + h
        out_ref[pl.ds(k * block, block)] = (acc * 0.25).astype(BF16)
        return carry

    lax.fori_loop(0, out_rows // block, step, 0)


def conv_pool(where, x, w, b):
    rows, cols, chans = x.shape
    out_rows = rows // 4
    block = next(k for k in (6, 4, 3, 2, 1) if out_rows % k == 0)
    return pl.pallas_call(
        functools.partial(conv_kernel, block=block),
        out_shape=jax.ShapeDtypeStruct((out_rows, cols // 2, chans), BF16),
        in_specs=[SMEM, VMEM, VMEM, VMEM],
        out_specs=VMEM,
        scratch_shapes=[
            pltpu.VMEM((2 * (chans // 128), cols + 16, 128), F32),
            pltpu.VMEM((2 * out_rows + 2, cols // 2, 4 * chans), BF16),
        ],
        compiler_params=params(),
        cost_estimate=pl.CostEstimate(
            flops=4 * out_rows * cols * 9 * chans * chans * 2,
            bytes_accessed=rows * cols * chans * 2,
            transcendentals=0,
        ),
        name="conv_pool",
    )(where, x, w, b)


def edge_kernel(where_ref, left_ref, head_ref, tail_ref, right_ref, w_ref, b_ref, out_ref, wide, acc):
    rows, width, chans = head_ref.shape
    lanes = chans // 128
    count = 8 * rows
    for s, pair in enumerate(((left_ref, head_ref), (tail_ref, right_ref))):
        for k, ref in enumerate(pair):
            x = ref[...].astype(F32)
            for t in range(lanes):
                for r in range(rows):
                    at = r * 8 + k * width
                    wide[s * lanes + t, at : at + width] = x[r, :, t * 128 : (t + 1) * 128]
    column = [
        [
            jnp.concatenate(
                [wide[s * lanes + t, pl.ds(c, rows, stride=8), :] for t in range(lanes)], axis=-1
            ).astype(BF16)
            for c in range(2 * width)
        ]
        for s in range(2)
    ]
    lhs = jnp.concatenate(
        [
            jnp.concatenate(column[s][2 * j + phase : 2 * j + phase + 3], axis=-1)
            for s in range(2)
            for j in range(2)
            for phase in range(2)
        ],
        axis=0,
    )
    bias = b_ref[...]
    depth = 3 * chans
    pad = rows + 16
    for dr in range(3):
        part = jnp.dot(lhs, w_ref[dr * depth : (dr + 1) * depth], preferred_element_type=F32)
        for g in range(8):
            own = part[g * rows : (g + 1) * rows]
            for t in range(lanes):
                at = 9 - dr
                piece = own[:, t * 128 : (t + 1) * 128]
                if dr == 0:
                    acc[g * lanes + t, 0:8] = jnp.zeros((8, 128), F32)
                    acc[g * lanes + t, 8 + rows : pad] = jnp.zeros((8, 128), F32)
                    acc[g * lanes + t, 8:9] = jnp.zeros((1, 128), F32)
                    acc[g * lanes + t, at : at + rows] = piece
                else:
                    acc[g * lanes + t, at : at + rows] += piece
    for g in range(4):
        for t in range(lanes):
            total = None
            for phase in range(2):
                at = (2 * g + phase) * lanes + t
                v = acc[at, 8 : 8 + rows] + bias[:, t * 128 : (t + 1) * 128]
                acc[at, 8 : 8 + rows] = v * jax.nn.sigmoid(v)
                both = (
                    acc[at, pl.ds(8, rows // 2, stride=2), :]
                    + acc[at, pl.ds(9, rows // 2, stride=2), :]
                )
                total = both if total is None else total + both
            lost = jnp.where(g == 0, where_ref[1], jnp.where(g == 3, where_ref[2], 0))
            keep = jnp.where(lost > 0, 0.0, 0.25)
            out_ref[g, t] = (total * keep).astype(BF16).astype(F32)


def conv_edges(where, left, head, tail, right, w, b):
    rows, _, chans = head.shape
    lanes = chans // 128
    return pl.pallas_call(
        edge_kernel,
        out_shape=jax.ShapeDtypeStruct((4, lanes, rows // 2, 128), F32),
        in_specs=[SMEM] + [VMEM] * 6,
        out_specs=VMEM,
        scratch_shapes=[
            pltpu.VMEM((2 * lanes, 8 * rows, 128), F32),
            pltpu.VMEM((8 * lanes, rows + 16, 128), F32),
        ],
        compiler_params=params(),
        name="conv_edges",
    )(where, left, head, tail, right, w, b)


def scale_rows(block, note_rows, sums):
    def exponent(values):
        top = None
        for v in values:
            one = jnp.max(jnp.max(jnp.abs(v), axis=0, keepdims=True), axis=1, keepdims=True)
            top = one if top is None else jnp.maximum(top, one)
        return jnp.ceil(jnp.log2(jnp.maximum(top, 1e-30)))

    power = exponent([block, note_rows])
    power_sums = exponent([sums])
    return power, power_sums


def note_block(bias, power, power_sums, width):
    row = lax.broadcasted_iota(jnp.int32, (NOTE, width), 0)
    bias = jnp.broadcast_to(bias * jnp.exp2(12.0 - power), (NOTE, width))
    power = jnp.broadcast_to(power, (NOTE, width))
    power_sums = jnp.broadcast_to(power_sums, (NOTE, width))
    return jnp.where(row == 0, bias, jnp.where(row == 1, power, power_sums))


def read_note(part, at):
    note = part[at : at + NOTE]
    down = jnp.exp2(note[1:2] - 12.0)
    return note[0:1] * down, down, jnp.exp2(note[2:3] - 12.0)


def deep_kernel(
    where_ref, own_ref, other_ref, edge_ref, w_ref, b_ref, lab_ref, slots_ref, *refs, block, n_parts, chunk, ways
):
    part_refs = refs[:n_parts]
    out_refs = refs[n_parts : n_parts + ways]
    wide, taps, member, grad, weight = refs[n_parts + ways :]
    part, cols, chans = own_ref.shape
    rows = 2 * part
    lanes = chans // 128
    width = w_ref.shape[-1]
    half, me = where_ref[0], where_ref[3]
    entries = slots_ref.shape[0]
    owned = part_refs[0].shape[1] - SIDE
    taps[0] = jnp.zeros(taps.shape[1:], BF16)
    taps[rows + 1] = jnp.zeros(taps.shape[1:], BF16)

    def prepare(ref, base, i, slot):
        x = ref[i].astype(F32)
        r = base + i
        for t in range(lanes):
            s = slot * lanes + t
            at = t * 128
            wide[s, 8 : 8 + cols] = x[:, at : at + 128]
            for g, place in enumerate((7, 8, 7 + cols, 8 + cols)):
                wide[s, place : place + 1] = edge_ref[g, t, pl.ds(r, 1), :]
        for tap in range(3):
            for t in range(lanes):
                piece = wide[slot * lanes + t, 7 + tap : 7 + tap + cols, :]
                at = (tap * lanes + t) * 128
                taps[r + 1, :, at : at + 128] = piece.astype(BF16)

    def prepare_two(k, carry):
        prepare(own_ref, half * part, k, 0)
        prepare(other_ref, (1 - half) * part, k, 1)
        return carry

    lax.fori_loop(0, part, prepare_two, 0)
    ids = slots_ref[...]
    total = jnp.zeros((entries, 1), F32)
    entry_grad = jnp.zeros((entries, width), F32)
    owner, inner = ids // owned, ids % owned
    spot = lax.broadcasted_iota(jnp.int32, (entries, owned), 1)
    m = 0
    for ref in part_refs:
        for k in range(ref.shape[0]):
            there = ref[k, owned : owned + 1, :entries] == ids.astype(F32)
            counts = ref[k, owned + 1 : owned + 2, :entries]
            total += jnp.sum(jnp.where(there, counts, 0.0), axis=1, keepdims=True)
            hot = ((owner ^ me) == m) & (inner == spot)
            entry_grad += jnp.dot(
                hot.astype(F32), ref[k, :owned], precision=lax.Precision.HIGHEST, preferred_element_type=F32
            )
            m += 1
    entry_grad = entry_grad / jnp.maximum(total, 1.0)
    lab = jnp.transpose(lab_ref[...].astype(F32))
    lane = lax.broadcasted_iota(jnp.int32, (cols, 128), 1)
    want = jnp.where(lane < 3 * entries, lane % entries, -1).astype(F32)
    for r in range(rows):
        member[r] = (lab[:, r : r + 1] == want).astype(BF16)
    high = entry_grad.astype(BF16)
    rest = entry_grad - high.astype(F32)
    mid = rest.astype(BF16)
    low = (rest - mid.astype(F32)).astype(BF16)
    terms = jnp.concatenate([high, mid, low, jnp.zeros((128 - 3 * entries, width), BF16)], axis=0)
    bias = b_ref[...]
    size = block * cols

    def step(k, carry):
        sums, bias_sum = carry
        r0 = k * block
        lhs = jnp.concatenate([taps[pl.ds(r0 + dr, block)] for dr in range(3)], axis=-1)
        v = jnp.dot(lhs.reshape(size, 9 * chans), w_ref[...], preferred_element_type=F32) + bias
        sig = jax.nn.sigmoid(v)
        features = (v * sig).astype(BF16)
        mem = member[pl.ds(r0, block)].reshape(size, 128)
        pixel = jnp.dot(mem, terms, preferred_element_type=F32)
        dg = (pixel * (sig * (1.0 + v * (1.0 - sig)))).astype(BF16)
        grad[pl.ds(k * size, size)] = dg
        sums = sums + lax.dot_general(
            mem, features, (((0,), (0,)), ((), ())), preferred_element_type=F32
        )[:entries]
        bias_sum = bias_sum + jnp.sum(dg.astype(F32), axis=0, keepdims=True)
        return sums, bias_sum

    sums, bias_sum = lax.fori_loop(
        0, rows // block, step, (jnp.zeros((entries, width), F32), jnp.zeros((1, width), F32))
    )
    depth = 3 * chans
    for dr in range(3):
        window = taps[dr : dr + rows].reshape(rows * cols, depth)
        out = lax.dot_general(grad[...], window, (((0,), (0,)), ((), ())), preferred_element_type=F32)
        weight[dr * depth : (dr + 1) * depth] = jnp.transpose(out)
    if weight.shape[0] > 3 * depth:
        weight[3 * depth :] = jnp.zeros((weight.shape[0] - 3 * depth, width), F32)
    power, power_sums = scale_rows(weight[...], bias_sum, sums)
    up = jnp.exp2(12.0 - power)
    note = note_block(bias_sum, power, power_sums, width)
    sums = sums * jnp.exp2(12.0 - power_sums)
    digit = lax.rem(me, ways)
    heads = weight.shape[0] // chunk // ways
    for m in range(ways):
        for hi in range(heads):
            j = hi * ways + (digit ^ m)
            out_refs[m][hi * chunk : (hi + 1) * chunk] = (
                weight[pl.ds(pl.multiple_of(j * chunk, 8), chunk)] * up
            )
        out_refs[m][heads * chunk : heads * chunk + NOTE] = note
        out_refs[m][heads * chunk + NOTE :] = sums


def deep_part(where, own, other, edges, w, b, labels, slots, parts, chunk, count, ways):
    part, cols, chans = own.shape
    rows, width = 2 * part, w.shape[-1]
    entries = slots.shape[0]
    block = next(k for k in (8, 4, 2, 1) if rows % k == 0)
    out = jax.ShapeDtypeStruct((count // ways * chunk + NOTE + entries, width), F32)
    return pl.pallas_call(
        functools.partial(deep_kernel, block=block, n_parts=len(parts), chunk=chunk, ways=ways),
        out_shape=(out,) * ways,
        in_specs=[SMEM] + [VMEM] * (7 + len(parts)),
        out_specs=(VMEM,) * ways,
        scratch_shapes=[
            pltpu.VMEM((2 * (chans // 128), cols + 16, 128), F32),
            pltpu.VMEM((rows + 2, cols, 3 * chans), BF16),
            pltpu.VMEM((rows, cols, 128), BF16),
            pltpu.VMEM((rows * cols, width), BF16),
            pltpu.VMEM((count * chunk, width), F32),
        ],
        compiler_params=params(),
        cost_estimate=pl.CostEstimate(
            flops=8 * rows * cols * 9 * chans * width, bytes_accessed=4 << 20, transcendentals=0
        ),
        name="deep_part",
    )(where, own, other, edges, w, b, labels, slots, *parts)


def merge_kernel(where_ref, *refs, chunk, heads, held, entries, shift, next_ways):
    n_parts = len(refs) - next_ways - 1
    part_refs, out_refs, sums_ref = refs[:n_parts], refs[n_parts:-1], refs[-1]
    width = part_refs[0].shape[-1]
    size = heads * chunk
    total, bias = jnp.zeros((size, width), F32), jnp.zeros((1, width), F32)
    sums_rows = held * entries
    for m, ref in enumerate(part_refs):
        more, down, down_sums = read_note(ref, size)
        total, bias = total + ref[:size] * down, bias + more
        sums_ref[m * sums_rows : (m + 1) * sums_rows] = ref[size + NOTE :] * down_sums
    sums = sums_ref[...]
    power, power_sums = scale_rows(total, bias, sums)
    note = note_block(bias, power, power_sums, width)
    total = total * jnp.exp2(12.0 - power)
    if next_ways == 1:
        out_refs[0][:size] = total
        out_refs[0][size:] = note
        return
    sums = sums * jnp.exp2(12.0 - power_sums)
    digit = lax.rem(where_ref[3] >> shift, next_ways)
    for m in range(next_ways):
        for hi in range(heads // next_ways):
            piece = jnp.zeros((chunk, width), F32)
            for d in range(next_ways):
                at = (hi * next_ways + d) * chunk
                piece = jnp.where((digit ^ m) == d, total[at : at + chunk], piece)
            out_refs[m][hi * chunk : (hi + 1) * chunk] = piece
        at = heads // next_ways * chunk
        out_refs[m][at : at + NOTE] = note
        out_refs[m][at + NOTE :] = sums


def merge(where, parts, chunk, heads, held, entries, shift, next_ways):
    width = parts[0].shape[-1]
    sums_rows = len(parts) * held * entries
    if next_ways == 1:
        outs = (jax.ShapeDtypeStruct((heads * chunk + NOTE, width), F32),)
    else:
        rows = heads // next_ways * chunk + NOTE + sums_rows
        outs = (jax.ShapeDtypeStruct((rows, width), F32),) * next_ways
    outs = outs + (jax.ShapeDtypeStruct((sums_rows, width), F32),)
    out = pl.pallas_call(
        functools.partial(
            merge_kernel, chunk=chunk, heads=heads, held=held, entries=entries, shift=shift, next_ways=next_ways
        ),
        out_shape=outs,
        in_specs=[SMEM] + [VMEM] * len(parts),
        out_specs=(VMEM,) * len(outs),
        compiler_params=params(),
        name="merge",
    )(where, *parts)
    return out[:-1], out[-1]


def embed_kernel(where_ref, sums_ref, *refs, entries):
    part_refs, out_ref = refs[:-1], refs[-1]
    owned, width = out_ref.shape
    own = (where_ref[3] * owned + lax.broadcasted_iota(jnp.int32, (owned, entries), 0)).astype(F32)
    sums, counts = jnp.zeros((owned, width), F32), jnp.zeros((owned, 1), F32)
    m = 0
    for ref in part_refs:
        for k in range(ref.shape[0]):
            there = ref[k, owned : owned + 1, :entries] == own
            count = ref[k, owned + 1 : owned + 2, :entries]
            counts += jnp.sum(jnp.where(there, count, 0.0), axis=1, keepdims=True)
            sums += jnp.dot(
                there.astype(F32),
                sums_ref[m * entries : (m + 1) * entries],
                precision=lax.Precision.HIGHEST,
                preferred_element_type=F32,
            )
            m += 1
    out_ref[...] = sums / jnp.maximum(counts, 1.0)


def spread_kernel(where_ref, *refs, chunk, rows):
    part_refs, weight_ref, bias_ref, place = refs[:-3], refs[-3], refs[-2], refs[-1]
    me = where_ref[3]
    m = 0
    for ref in part_refs:
        for k in range(ref.shape[0]):
            bias, down, _ = read_note(ref[k], chunk)
            j = me ^ m
            place[pl.ds(pl.multiple_of(j * chunk, 8), chunk)] = ref[k, :chunk] * down

            @pl.when(j == 0)
            def _():
                bias_ref[...] = bias

            m += 1
    weight_ref[...] = place[:rows]


def spread(where, parts, chunk, count, rows):
    width = parts[0].shape[-1]
    return pl.pallas_call(
        functools.partial(spread_kernel, chunk=chunk, rows=rows),
        out_shape=(jax.ShapeDtypeStruct((rows, width), F32), jax.ShapeDtypeStruct((1, width), F32)),
        in_specs=[SMEM] + [VMEM] * len(parts),
        out_specs=(VMEM, VMEM),
        scratch_shapes=[pltpu.VMEM((count * chunk, width), F32)],
        compiler_params=params(),
        name="spread",
    )(where, *parts)


def body(
    section_input, conv_weight, conv_bias, deep_weight, deep_bias, labels, slot_ids, embed_grad
):
    chan_count = lax.axis_size("chan")
    strip_count = lax.axis_size("strip")
    chan_pos = lax.axis_index("chan")
    strip_pos = lax.axis_index("strip")
    half = chan_pos & 1
    channels = section_input.shape[-1]
    entries = slot_ids.shape[0]
    owned, width = embed_grad.shape
    where = jnp.stack(
        [half, (strip_pos == 0).astype(jnp.int32), (strip_pos == strip_count - 1).astype(jnp.int32), strip_pos]
    ).astype(jnp.int32)
    conv_w = conv_weight.reshape(9 * channels, -1)
    conv_b = conv_bias.reshape(1, -1)

    head, tail = section_input[:, :3], section_input[:, -3:]
    pairs = []
    for s in range(strip_count):
        for c in range(chan_count):
            to = s + 1 - 2 * (c & 1)
            if 0 <= to < strip_count:
                pairs.append((s * chan_count + c, to * chan_count + c))
    got = lax.ppermute(jnp.where(half == 0, tail, head), ("strip", "chan"), pairs)
    traded = swap(got, "chan", 1)
    left = jnp.where(half == 0, got, traded)
    right = jnp.where(half == 0, traded, got)

    member = labels.reshape(1, -1) == jnp.arange(entries, dtype=jnp.int32)[:, None]
    counts = jnp.sum(member.astype(F32), axis=1)
    side = jnp.pad(
        jnp.stack([slot_ids.astype(F32), counts]), ((0, SIDE - 2), (0, width - entries))
    )
    shared = gather_relative(
        jnp.concatenate([embed_grad, side]), "strip", bit_groups(strip_count, 1, 2)
    )

    pooled = conv_pool(where, section_input, conv_w, conv_b)
    other = swap(pooled, "chan", 1)
    edges = conv_edges(where, left, head, tail, right, conv_w, conv_b)

    groups = bit_groups(strip_count, 3, 3)
    chunk = -(-9 * channels // strip_count // 8) * 8
    send = deep_part(
        where,
        pooled,
        other,
        edges,
        deep_weight.reshape(9 * channels, width),
        deep_bias.reshape(1, width),
        labels,
        slot_ids.reshape(entries, 1),
        shared,
        chunk,
        strip_count,
        1 << groups[0][1],
    )
    heads, held = strip_count, 1
    for k, (shift, size) in enumerate(groups):
        ways = 1 << size
        heads //= ways
        parts = [send[0]] + [
            swap(send[m].astype(F16), "strip", m << shift).astype(F32) for m in range(1, ways)
        ]
        after, next_size = groups[k + 1] if k + 1 < len(groups) else (0, 0)
        send, sums = merge(where, parts, chunk, heads, held, entries, after, 1 << next_size)
        held *= ways
    embeddings = pl.pallas_call(
        functools.partial(embed_kernel, entries=entries),
        out_shape=jax.ShapeDtypeStruct((owned, width), F32),
        in_specs=[SMEM] + [VMEM] * (1 + len(shared)),
        out_specs=VMEM,
        compiler_params=params(),
        name="embed",
    )(where, sums, *shared)
    gathered = gather_relative(send[0].astype(F16), "strip", groups)
    weight_rows, bias_row = spread(
        where, [g.astype(F32) for g in gathered], chunk, strip_count, 9 * channels
    )
    return (embeddings, weight_rows.reshape(3, 3, channels, width), bias_row[0])


def solution(mesh):
    placed = (
        P(None, "strip", None),
        P(),
        P(),
        P(None, None, None, "chan"),
        P("chan"),
        P(None, "strip"),
        P("strip"),
        P("strip", "chan"),
    )
    return jax.shard_map(
        body,
        mesh=mesh,
        in_specs=placed,
        out_specs=(P("strip", "chan"), P(None, None, None, "chan"), P("chan")),
        check_vma=False,
    )
```

time: 257 us -> 76.3 us (0.30)
  waiting for transfers between devices: 102 us -> 16.3 us
  blocking collectives: 80.8 us -> 0 us
  starting transfers between devices: 6.22 us -> 35.7 us
  local copies, waits for them, and re-layouts: 32.6 us -> 4.03 us
  Pallas kernels: 0 us -> 17.2 us
  between operations: 15.1 us -> 1 us
  matrix products: 13.7 us -> 0 us
  other arithmetic: 6.08 us -> 1.78 us
    psum x1 -> x0, waiting for transfers between devices: 58.6 us -> none  [body(): weight_grad, bias_grad = lax.psum((local_weight, local_bias), 'strip')]
    all_gather x2 -> x0, blocking collectives: 40.2 us -> none  [the longest x1 30.9 us: body(): lax.all_gather(embed_grad / divisor, 'strip', axis=0, tiled=True)]
    reduce_scatter x1 -> x0, waiting for transfers between devices: 39.5 us -> none  [body(): lax.psum_scatter(dense_sums, 'strip', scatter_dimension=0, tiled=True)]
    ppermute x2 -> x21, starting transfers between devices: 6.14 us -> 35.7 us  [the longest x20 30.8 us: swap(): return lax.ppermute(value, axis, [(i, i ^ mask) for i in range(count)])]
    psum x1 -> x0, blocking collectives: 20.7 us -> none  [body(): weight_grad, bias_grad = lax.psum((local_weight, local_bias), 'strip')]
    unnamed x1 -> x0, blocking collectives: 19.9 us -> none
    pallas_call x0 -> x6, Pallas kernels: none -> 17.2 us  [the longest x1 6.11 us: deep_part(): pl.pallas_call(functools.partial(deep_kernel, block=block, n_parts=len(pa...]
    dot_general x29 -> x0, matrix products: 13.7 us -> none  [the longest x18 7.63 us: convolve(): jnp.dot(window, weight[shift_row, shift_col], preferred_element_type=jnp....]
  transfers between devices with their start and end apart: 4 -> 21, of which waited for: 3 -> 8; matrix products, arithmetic and copies ran while one was open for 1% -> 1% of each run, Pallas kernels for 0% -> 11%
where the time goes in v2:
time: 76.3 us; the launch traced here: 76 us
  starting transfers between devices  35.7 us (47%)
  Pallas kernels  17.2 us (23%)
  waiting for transfers between devices  16.3 us (21%)
  local copies, waits for them, and re-layouts  4.03 us (5%)
  other arithmetic  1.78 us (2%)
  between operations  1 us (1%)
    ppermute x20, starting transfers between devices, swap(): return lax.ppermute(value, axis, [(i, i ^ mask) for i in range(count)])  30.8 us
    ppermute x20, waiting for transfers between devices, swap(): return lax.ppermute(value, axis, [(i, i ^ mask) for i in range(count)])  16.3 us
    pallas_call x1, Pallas kernels, deep_part(): pl.pallas_call(functools.partial(deep_kernel, block=block, n_parts=len(pa...  6.11 us
    pallas_call x1, Pallas kernels, conv_pool(): pl.pallas_call(functools.partial(conv_kernel, block=block), out_shape=jax...  5.73 us
    ppermute x1, starting transfers between devices, body(): lax.ppermute(jnp.where(half == 0, tail, head), ('strip', 'chan'), pairs)  4.85 us
    unnamed x20, local copies, waits for them, and re-layouts  3.87 us
    pallas_call x1, Pallas kernels, spread(): pl.pallas_call(functools.partial(spread_kernel, chunk=chunk, rows=rows),...  1.79 us
  transfers between devices with their start and end apart: 21, of which 8 were waited for; matrix products, arithmetic and copies ran while one was open for 1% of the time, Pallas kernels for 11%

profile of v2, /device:TPU:0, one launch (start us, length us, event | category | flops | bytes accessed | tf_op | source)
XLA Modules:
  0.0 76.0 jit_solution(5339006523986988057)
XLA Ops:
  0.6 1.1 %fusion.1 = (bf16[48,3,256]{2,1,0:T(4,128)(2,1)S(1)}, bf16[48,3,256]{2,1,0:T(4,128)(2,1)S(1)}, bf16[48,3,256]{2,1,0:T(4,128)(2,1)S(1)}) fusion(bf16[48,128,256]{2,1,0:T(8,128)(2,1)} %x_ref.1, pred[]{:T(512)S(6)} %eq.28), kind=kLoop, calls=%fused_computation.14 | loop fusion | flops 36864 | bytes 368641 | tf_op jit(solution)/shard_map/slice | solution.py:488
  1.8 4.8 %collective-permute-start.1 = (bf16[48,3,256]{2,1,0:T(4,128)(2,1)S(1)}, bf16[48,3,256]{2,1,0:T(4,128)(2,1)S(1)}, u32[]{:S(2)}, u32[]{:S(2)}) collective-permute-start(bf16[48,3,256]{2,1,0:T(4,128)(2,1)S(1)} %get-tuple-element.30), channel_id=1, source_target_pairs={{0,4},{2,6},{4,8},{5,1},{6,10},{7,3},{8,12},{9,5},{10,14},{11,7},{... | collective-permute-start | bytes 221192 | tf_op jit(solution)/shard_map/ppermute | solution.py:495
  6.7 1.3 %copy-done = bf16[3,3,256,256]{3,2,1,0:T(8,128)(2,1)S(1)} copy-done((bf16[3,3,256,256]{3,2,1,0:T(8,128)(2,1)S(1)}, bf16[3,3,256,256]{3,2,1,0:T(8,128)(2,1)}, u32[]{:S(2)}) %copy-start) | copy-done | bytes 1179672
  8.0 1.9 %copy-done.2 = bf16[48,128,256]{2,1,0:T(8,128)(2,1)S(1)} copy-done((bf16[48,128,256]{2,1,0:T(8,128)(2,1)S(1)}, bf16[48,128,256]{2,1,0:T(8,128)(2,1)}, u32[]{:S(2)}) %copy-start.2) | copy-done | bytes 3145752
  10.6 5.7 %conv_pool.1.own_ref = bf16[12,64,256]{2,1,0:T(8,128)(2,1)S(1)} custom-call(s32[4]{0:T(128)S(1)} %pad_add_fusion.where_ref, bf16[48,128,256]{2,1,0:T(8,128)(2,1)S(1)} %copy-done.2, bf16[2304,256]{1,0:T(8,128)(2,1)S(1)} %bitcast.19, f32[1,256]{1,0:T(1,128)S(1)} %bitcast.21), custom_call_target="tpu_custom_call" | custom-call | flops 7247757312 | bytes 3145728 | tf_op jit(solution)/shard_map/conv_pool/pallas_call | solution.py:102
  16.7 1.6 %collective-permute-start.3 = (f32[1,72,128]{2,1,0:T(8,128)S(1)}, f32[1,72,128]{2,1,0:T(8,128)S(1)}, u32[]{:S(2)}, u32[]{:S(2)}) collective-permute-start(f32[1,72,128]{2,1,0:T(8,128)S(1)} %maximum_bitcast_fusion), channel_id=1, source_target_pairs={{0,4},{4,0},{8,12},{12,8},{16,20},{20,16},{24,28},{28,24},{1,5},{5... | collective-permute-start | bytes 110600 | tf_op jit(solution)/shard_map/ppermute | solution.py:23
  18.6 2.1 %collective-permute-done.3 = f32[1,72,128]{2,1,0:T(8,128)S(1)} collective-permute-done((f32[1,72,128]{2,1,0:T(8,128)S(1)}, f32[1,72,128]{2,1,0:T(8,128)S(1)}, u32[]{:S(2)}, u32[]{:S(2)}) %collective-permute-start.3) | collective-permute-done | bytes 36896 | tf_op jit(solution)/shard_map/ppermute | solution.py:23
  20.7 3.6 %collective-permute-start.6 = (f32[2,72,128]{2,1,0:T(8,128)S(1)}, f32[2,72,128]{2,1,0:T(8,128)S(1)}, u32[]{:S(2)}, u32[]{:S(2)}) collective-permute-start(f32[2,72,128]{2,1,0:T(8,128)S(1)} %pad_maximum_fusion.refs_0_), channel_id=1, source_target_pairs={{0,24},{4,28},{8,16},{12,20},{16,8},{20,12},{24,0},{28,4},{1,25},{... | collective-permute-start | bytes 221192 | tf_op jit(solution)/shard_map/ppermute | solution.py:23
  24.3 0.8 %collective-permute-start.4 = (f32[2,72,128]{2,1,0:T(8,128)S(1)}, f32[2,72,128]{2,1,0:T(8,128)S(1)}, u32[]{:S(2)}, u32[]{:S(2)}) collective-permute-start(f32[2,72,128]{2,1,0:T(8,128)S(1)} %pad_maximum_fusion.refs_0_), channel_id=1, source_target_pairs={{0,8},{4,12},{8,0},{12,4},{16,24},{20,28},{24,16},{28,20},{1,9},{5... | collective-permute-start | bytes 221192 | tf_op jit(solution)/shard_map/ppermute | solution.py:23
  25.2 1.3 %conv_edges.1.edge_ref = f32[4,2,24,128]{3,2,1,0:T(8,128)S(1)} custom-call(s32[4]{0:T(128)S(1)} %pad_add_fusion.where_ref, bf16[48,3,256]{2,1,0:T(4,128)(2,1)S(1)} %get-tuple-element.33.left_ref, bf16[48,3,256]{2,1,0:T(4,128)(2,1)S(1)} %get-tuple-element.31.head_ref, bf16[48,3,256]{2,1,0:T(4,128)(2,1)S(1)} %get-tuple-element.29.tail_ref, ...), custom_call_target="tpu_custom_call" | custom-call | tf_op jit(solution)/shard_map/conv_edges/pallas_call | solution.py:187
  26.6 1.0 %collective-permute-done.6.refs_3_ = f32[2,72,128]{2,1,0:T(8,128)S(1)} collective-permute-done((f32[2,72,128]{2,1,0:T(8,128)S(1)}, f32[2,72,128]{2,1,0:T(8,128)S(1)}, u32[]{:S(2)}, u32[]{:S(2)}) %collective-permute-start.6) | collective-permute-done | bytes 73760 | tf_op jit(solution)/shard_map/ppermute | solution.py:23
  27.6 2.6 %collective-permute-done.5.refs_2_ = f32[2,72,128]{2,1,0:T(8,128)S(1)} collective-permute-done((f32[2,72,128]{2,1,0:T(8,128)S(1)}, f32[2,72,128]{2,1,0:T(8,128)S(1)}, u32[]{:S(2)}, u32[]{:S(2)}) %collective-permute-start.5) | collective-permute-done | bytes 73760 | tf_op jit(solution)/shard_map/ppermute | solution.py:23
  30.2 6.1 %deep_part.1 = (f32[336,128]{1,0:T(8,128)S(1)}, f32[336,128]{1,0:T(8,128)S(1)}, f32[336,128]{1,0:T(8,128)S(1)}, f32[336,128]{1,0:T(8,128)S(1)}, f32[336,128]{1,0...) custom-call(s32[4]{0:T(128)S(1)} %pad_add_fusion.where_ref, ...), custom_call_target="tpu_custom_call" | custom-call | flops 3623878656 | bytes 4194304 | tf_op jit(solution)/shard_map/deep_part/pallas_call | solution.py:344
  36.3 3.5 %collective-permute-start.13 = (f16[336,128]{1,0:T(8,128)(2,1)S(1)}, f16[336,128]{1,0:T(8,128)(2,1)S(1)}, u32[]{:S(2)}, u32[]{:S(2)}) collective-permute-start(f16[336,128]{1,0:T(8,128)(2,1)S(1)} %convert_element_type.95), channel_id=1, source_target_pairs={{0,28},{4,24},{8,20},{12,16},{16,12},{20,8},{24,4},{28,0},{1,29},{... | collective-permute-start | bytes 258056 | tf_op jit(solution)/shard_map/ppermute | solution.py:23
  39.9 1.3 %collective-permute-start.12 = (f16[336,128]{1,0:T(8,128)(2,1)S(1)}, f16[336,128]{1,0:T(8,128)(2,1)S(1)}, u32[]{:S(2)}, u32[]{:S(2)}) collective-permute-start(f16[336,128]{1,0:T(8,128)(2,1)S(1)} %convert_element_type.93), channel_id=1, source_target_pairs={{0,24},{4,28},{8,16},{12,20},{16,8},{20,12},{24,0},{28,4},{1,25},{... | collective-permute-start | bytes 258056 | tf_op jit(solution)/shard_map/ppermute | solution.py:23
  41.3 2.9 %collective-permute-start.10 = (f16[336,128]{1,0:T(8,128)(2,1)S(1)}, f16[336,128]{1,0:T(8,128)(2,1)S(1)}, u32[]{:S(2)}, u32[]{:S(2)}) collective-permute-start(f16[336,128]{1,0:T(8,128)(2,1)S(1)} %convert_element_type.89), channel_id=1, source_target_pairs={{0,16},{4,20},{8,24},{12,28},{16,0},{20,4},{24,8},{28,12},{1,17},{... | collective-permute-start | bytes 258056 | tf_op jit(solution)/shard_map/ppermute | solution.py:23
  44.3 1.2 %collective-permute-start.9 = (f16[336,128]{1,0:T(8,128)(2,1)S(1)}, f16[336,128]{1,0:T(8,128)(2,1)S(1)}, u32[]{:S(2)}, u32[]{:S(2)}) collective-permute-start(f16[336,128]{1,0:T(8,128)(2,1)S(1)} %convert_element_type.87), channel_id=1, source_target_pairs={{0,12},{4,8},{8,4},{12,0},{16,28},{20,24},{24,20},{28,16},{1,13},{... | collective-permute-start | bytes 258056 | tf_op jit(solution)/shard_map/ppermute | solution.py:23
  45.5 4.5 %collective-permute-start.8 = (f16[336,128]{1,0:T(8,128)(2,1)S(1)}, f16[336,128]{1,0:T(8,128)(2,1)S(1)}, u32[]{:S(2)}, u32[]{:S(2)}) collective-permute-start(f16[336,128]{1,0:T(8,128)(2,1)S(1)} %convert_element_type.85), channel_id=1, source_target_pairs={{0,8},{4,12},{8,0},{12,4},{16,24},{20,28},{24,16},{28,20},{1,9},{5... | collective-permute-start | bytes 258056 | tf_op jit(solution)/shard_map/ppermute | solution.py:23
  50.0 3.1 %collective-permute-done.11 = f16[336,128]{1,0:T(8,128)(2,1)S(1)} collective-permute-done((f16[336,128]{1,0:T(8,128)(2,1)S(1)}, f16[336,128]{1,0:T(8,128)(2,1)S(1)}, u32[]{:S(2)}, u32[]{:S(2)}) %collective-permute-start.11) | collective-permute-done | bytes 86048 | tf_op jit(solution)/shard_map/ppermute | solution.py:23
  53.7 0.8 %collective-permute-done.8 = f16[336,128]{1,0:T(8,128)(2,1)S(1)} collective-permute-done((f16[336,128]{1,0:T(8,128)(2,1)S(1)}, f16[336,128]{1,0:T(8,128)(2,1)S(1)}, u32[]{:S(2)}, u32[]{:S(2)}) %collective-permute-start.8) | collective-permute-done | bytes 86048 | tf_op jit(solution)/shard_map/ppermute | solution.py:23
  54.6 0.8 merge.1
  55.3 2.0 %collective-permute-start.19 = (f16[1,304,128]{2,1,0:T(8,128)(2,1)S(1)}, f16[1,304,128]{2,1,0:T(8,128)(2,1)S(1)}, u32[]{:S(2)}, u32[]{:S(2)}) collective-permute-start(f16[1,304,128]{2,1,0:T(8,128)(2,1)S(1)} %get-tuple-element.28), channel_id=1, source_target_pairs={{0,24},{4,28},{8,16},{12,20},{16,8},{20,12},{24,0},{28,4},{1,25},{... | collective-permute-start | bytes 233480 | tf_op jit(solution)/shard_map/ppermute | solution.py:23
  57.3 2.0 %collective-permute-start.18 = (f16[1,304,128]{2,1,0:T(8,128)(2,1)S(1)}, f16[1,304,128]{2,1,0:T(8,128)(2,1)S(1)}, u32[]{:S(2)}, u32[]{:S(2)}) collective-permute-start(f16[1,304,128]{2,1,0:T(8,128)(2,1)S(1)} %get-tuple-element.28), channel_id=1, source_target_pairs={{0,20},{4,16},{8,28},{12,24},{16,4},{20,0},{24,12},{28,8},{1,21},{... | collective-permute-start | bytes 233480 | tf_op jit(solution)/shard_map/ppermute | solution.py:23
  59.3 1.2 %collective-permute-start.17 = (f16[1,304,128]{2,1,0:T(8,128)(2,1)S(1)}, f16[1,304,128]{2,1,0:T(8,128)(2,1)S(1)}, u32[]{:S(2)}, u32[]{:S(2)}) collective-permute-start(f16[1,304,128]{2,1,0:T(8,128)(2,1)S(1)} %get-tuple-element.28), channel_id=1, source_target_pairs={{0,16},{4,20},{8,24},{12,28},{16,0},{20,4},{24,8},{28,12},{1,17},{... | collective-permute-start | bytes 233480 | tf_op jit(solution)/shard_map/ppermute | solution.py:23
  60.5 1.0 %collective-permute-start.16 = (f16[1,304,128]{2,1,0:T(8,128)(2,1)S(1)}, f16[1,304,128]{2,1,0:T(8,128)(2,1)S(1)}, u32[]{:S(2)}, u32[]{:S(2)}) collective-permute-start(f16[1,304,128]{2,1,0:T(8,128)(2,1)S(1)} %get-tuple-element.28), channel_id=1, source_target_pairs={{0,12},{4,8},{8,4},{12,0},{16,28},{20,24},{24,20},{28,16},{1,13},{... | collective-permute-start | bytes 233480 | tf_op jit(solution)/shard_map/ppermute | solution.py:23
  61.5 1.7 %collective-permute-start.15 = (f16[1,304,128]{2,1,0:T(8,128)(2,1)S(1)}, f16[1,304,128]{2,1,0:T(8,128)(2,1)S(1)}, u32[]{:S(2)}, u32[]{:S(2)}) collective-permute-start(f16[1,304,128]{2,1,0:T(8,128)(2,1)S(1)} %get-tuple-element.28), channel_id=1, source_target_pairs={{0,8},{4,12},{8,0},{12,4},{16,24},{20,28},{24,16},{28,20},{1,9},{5... | collective-permute-start | bytes 233480 | tf_op jit(solution)/shard_map/ppermute | solution.py:23
  63.2 0.8 %collective-permute-start.14 = (f16[1,304,128]{2,1,0:T(8,128)(2,1)S(1)}, f16[1,304,128]{2,1,0:T(8,128)(2,1)S(1)}, u32[]{:S(2)}, u32[]{:S(2)}) collective-permute-start(f16[1,304,128]{2,1,0:T(8,128)(2,1)S(1)} %get-tuple-element.28), channel_id=1, source_target_pairs={{0,4},{4,0},{8,12},{12,8},{16,20},{20,16},{24,28},{28,24},{1,5},{5... | collective-permute-start | bytes 233480 | tf_op jit(solution)/shard_map/ppermute | solution.py:23
  64.0 3.1 %collective-permute-done.18 = f16[1,304,128]{2,1,0:T(8,128)(2,1)S(1)} collective-permute-done((f16[1,304,128]{2,1,0:T(8,128)(2,1)S(1)}, f16[1,304,128]{2,1,0:T(8,128)(2,1)S(1)}, u32[]{:S(2)}, u32[]{:S(2)}) %collective-permute-start.18) | collective-permute-done | bytes 77856 | tf_op jit(solution)/shard_map/ppermute | solution.py:23
  67.1 2.4 %collective-permute-start.20 = (f16[1,304,128]{2,1,0:T(8,128)(2,1)S(1)}, f16[1,304,128]{2,1,0:T(8,128)(2,1)S(1)}, u32[]{:S(2)}, u32[]{:S(2)}) collective-permute-start(f16[1,304,128]{2,1,0:T(8,128)(2,1)S(1)} %get-tuple-element.28), channel_id=1, source_target_pairs={{0,28},{4,24},{8,20},{12,16},{16,12},{20,8},{24,4},{28,0},{1,29},{... | collective-permute-start | bytes 233480 | tf_op jit(solution)/shard_map/ppermute | solution.py:23
  69.6 1.5 %embed.1 = f32[64,128]{1,0:T(8,128)} custom-call(s32[4]{0:T(128)S(1)} %pad_add_fusion.where_ref, f32[256,128]{1,0:T(8,128)S(1)} %get-tuple-element.23.sums_ref, f32[2,72,128]{2,1,0:T(8,128)S(1)} %pad_maximum_fusion.refs_0_, f32[2,72,128]{2,1,0:T(8,128)S(1)} %collective-permute-done.4.refs_1_, f32[2,72,128]{2,1,0:T(8,128)S(1)} %collective-permute-done.5.refs_2_, ...), custom_call_target="tpu_custom_call" | custom-call | tf_op jit(solution)/shard_map/embed/pallas_call | solution.py:539
  71.2 3.0 %collective-permute-done.20 = f16[1,304,128]{2,1,0:T(8,128)(2,1)S(1)} collective-permute-done((f16[1,304,128]{2,1,0:T(8,128)(2,1)S(1)}, f16[1,304,128]{2,1,0:T(8,128)(2,1)S(1)}, u32[]{:S(2)}, u32[]{:S(2)}) %collective-permute-start.20) | collective-permute-done | bytes 77856 | tf_op jit(solution)/shard_map/ppermute | solution.py:23
  74.3 1.8 %spread.1 = (f32[2304,128]{1,0:T(8,128)}, f32[1,128]{1,0:T(1,128)}) custom-call(s32[4]{0:T(128)S(1)} %pad_add_fusion.where_ref, f32[1,304,128]{2,1,0:T(8,128)S(1)} %get-tuple-element.27.refs_0_, f32[1,304,128]{2,1,0:T(8,128)S(1)} %convert_element_type.100.refs_1_, f32[1,304,128]{2,1,0:T(8,128)S(1)} %convert_element_type.101.refs_2_, ...), custom_call_target="tpu_custom_call" | custom-call | tf_op jit(solution)/shard_map/spread/pallas_call | solution.py:460
  (68 shorter events, 2.5 us)
Async XLA Ops:
  1.8 16.6 %collective-permute-start.1 = (bf16[48,3,256]{2,1,0:T(4,128)(2,1)S(1)}, bf16[48,3,256]{2,1,0:T(4,128)(2,1)S(1)}, u32[]{:S(2)}, u32[]{:S(2)}) collective-permute-start(bf16[48,3,256]{2,1,0:T(4,128)(2,1)S(1)} %get-tuple-element.30), channel_id=1, source_target_pairs={{0,4},{2,6},{4,8},{5,1},{6,10},{7,3},{8,12},{9,5},{10,14},{11,7},{... | collective-permute-start | bytes 221192 | tf_op jit(solution)/shard_map/ppermute | solution.py:495
  6.7 1.3 %copy-start = (bf16[3,3,256,256]{3,2,1,0:T(8,128)(2,1)S(1)}, bf16[3,3,256,256]{3,2,1,0:T(8,128)(2,1)}, u32[]{:S(2)}) copy-start(bf16[3,3,256,256]{3,2,1,0:T(8,128)(2,1)} %param.9) | copy-start | bytes 3538948
  8.0 1.9 %copy-start.2 = (bf16[48,128,256]{2,1,0:T(8,128)(2,1)S(1)}, bf16[48,128,256]{2,1,0:T(8,128)(2,1)}, u32[]{:S(2)}) copy-start(bf16[48,128,256]{2,1,0:T(8,128)(2,1)} %x_ref.1) | copy-start | bytes 9437188
  9.9 0.7 copy-start.4
  10.6 5.9 %copy-start.9 = (s32[32]{0:T(128)S(1)}, s32[32]{0:T(128)}, u32[]{:S(2)}) copy-start(s32[32]{0:T(128)} %param.14) | copy-start | bytes 388
  10.6 5.9 %copy-start.3 = (s32[24,64]{1,0:T(8,128)S(1)}, s32[24,64]{1,0:T(8,128)}, u32[]{:S(2)}) copy-start(s32[24,64]{1,0:T(8,128)} %lab_ref.1) | copy-start | bytes 18436
  10.6 6.1 %copy-start.8 = (f32[64,128]{1,0:T(8,128)S(1)}, f32[64,128]{1,0:T(8,128)}, u32[]{:S(2)}) copy-start(f32[64,128]{1,0:T(8,128)} %param.15) | copy-start | bytes 98308
  10.6 14.6 %copy-start.1 = (bf16[3,3,256,256]{3,2,1,0:T(8,128)(2,1)S(1)}, bf16[3,3,256,256]{3,2,1,0:T(8,128)(2,1)}, u32[]{:S(2)}) copy-start(bf16[3,3,256,256]{3,2,1,0:T(8,128)(2,1)} %param.9) | copy-start | bytes 3538948
  10.6 14.6 %copy-start.5 = (f32[256]{0:T(256)S(1)}, f32[256]{0:T(256)}, u32[]{:S(2)}) copy-start(f32[256]{0:T(256)} %param.10) | copy-start | bytes 3076
  10.6 19.6 %copy-start.6 = (bf16[3,3,256,128]{3,2,1,0:T(8,128)(2,1)S(1)}, bf16[3,3,256,128]{3,2,1,0:T(8,128)(2,1)}, u32[]{:S(2)}) copy-start(bf16[3,3,256,128]{3,2,1,0:T(8,128)(2,1)} %param.11) | copy-start | bytes 1769476
  10.6 19.6 %copy-start.7 = (f32[128]{0:T(128)S(1)}, f32[128]{0:T(128)}, u32[]{:S(2)}) copy-start(f32[128]{0:T(128)} %param.12) | copy-start | bytes 1540
  16.4 13.8 %collective-permute-start = (bf16[12,64,256]{2,1,0:T(8,128)(2,1)S(1)}, bf16[12,64,256]{2,1,0:T(8,128)(2,1)S(1)}, u32[]{:S(2)}, u32[]{:S(2)}) collective-permute-start(bf16[12,64,256]{2,1,0:T(8,128)(2,1)S(1)} %conv_pool.1.own_ref), channel_id=1, source_target_pairs={{0,1},{1,0},{2,3},{3,2},{4,5},{5,4},{6,7},{7,6},{8,9},{9,8},{10,11... | collective-permute-start | bytes 1179656 | tf_op jit(solution)/shard_map/ppermute | solution.py:23
  16.7 4.0 %collective-permute-start.3 = (f32[1,72,128]{2,1,0:T(8,128)S(1)}, f32[1,72,128]{2,1,0:T(8,128)S(1)}, u32[]{:S(2)}, u32[]{:S(2)}) collective-permute-start(f32[1,72,128]{2,1,0:T(8,128)S(1)} %maximum_bitcast_fusion), channel_id=1, source_target_pairs={{0,4},{4,0},{8,12},{12,8},{16,20},{20,16},{24,28},{28,24},{1,5},{5... | collective-permute-start | bytes 110600 | tf_op jit(solution)/shard_map/ppermute | solution.py:23
  18.4 6.7 %collective-permute-start.2 = (bf16[48,3,256]{2,1,0:T(4,128)(2,1)S(1)}, bf16[48,3,256]{2,1,0:T(4,128)(2,1)S(1)}, u32[]{:S(2)}, u32[]{:S(2)}) collective-permute-start(bf16[48,3,256]{2,1,0:T(4,128)(2,1)S(1)} %collective-permute-done.1), channel_id=1, source_target_pairs={{0,1},{1,0},{2,3},{3,2},{4,5},{5,4},{6,7},{7,6},{8,9},{9,8},{10,11... | collective-permute-start | bytes 221192 | tf_op jit(solution)/shard_map/ppermute | solution.py:23
  20.7 6.8 %collective-permute-start.6 = (f32[2,72,128]{2,1,0:T(8,128)S(1)}, f32[2,72,128]{2,1,0:T(8,128)S(1)}, u32[]{:S(2)}, u32[]{:S(2)}) collective-permute-start(f32[2,72,128]{2,1,0:T(8,128)S(1)} %pad_maximum_fusion.refs_0_), channel_id=1, source_target_pairs={{0,24},{4,28},{8,16},{12,20},{16,8},{20,12},{24,0},{28,4},{1,25},{... | collective-permute-start | bytes 221192 | tf_op jit(solution)/shard_map/ppermute | solution.py:23
  24.3 5.8 %collective-permute-start.5 = (f32[2,72,128]{2,1,0:T(8,128)S(1)}, f32[2,72,128]{2,1,0:T(8,128)S(1)}, u32[]{:S(2)}, u32[]{:S(2)}) collective-permute-start(f32[2,72,128]{2,1,0:T(8,128)S(1)} %pad_maximum_fusion.refs_0_), channel_id=1, source_target_pairs={{0,16},{4,20},{8,24},{12,28},{16,0},{20,4},{24,8},{28,12},{1,17},{... | collective-permute-start | bytes 221192 | tf_op jit(solution)/shard_map/ppermute | solution.py:23
  24.3 5.8 %collective-permute-start.4 = (f32[2,72,128]{2,1,0:T(8,128)S(1)}, f32[2,72,128]{2,1,0:T(8,128)S(1)}, u32[]{:S(2)}, u32[]{:S(2)}) collective-permute-start(f32[2,72,128]{2,1,0:T(8,128)S(1)} %pad_maximum_fusion.refs_0_), channel_id=1, source_target_pairs={{0,8},{4,12},{8,0},{12,4},{16,24},{20,28},{24,16},{28,20},{1,9},{5... | collective-permute-start | bytes 221192 | tf_op jit(solution)/shard_map/ppermute | solution.py:23
  36.3 9.1 %collective-permute-start.13 = (f16[336,128]{1,0:T(8,128)(2,1)S(1)}, f16[336,128]{1,0:T(8,128)(2,1)S(1)}, u32[]{:S(2)}, u32[]{:S(2)}) collective-permute-start(f16[336,128]{1,0:T(8,128)(2,1)S(1)} %convert_element_type.95), channel_id=1, source_target_pairs={{0,28},{4,24},{8,20},{12,16},{16,12},{20,8},{24,4},{28,0},{1,29},{... | collective-permute-start | bytes 258056 | tf_op jit(solution)/shard_map/ppermute | solution.py:23
  39.9 10.1 %collective-permute-start.12 = (f16[336,128]{1,0:T(8,128)(2,1)S(1)}, f16[336,128]{1,0:T(8,128)(2,1)S(1)}, u32[]{:S(2)}, u32[]{:S(2)}) collective-permute-start(f16[336,128]{1,0:T(8,128)(2,1)S(1)} %convert_element_type.93), channel_id=1, source_target_pairs={{0,24},{4,28},{8,16},{12,20},{16,8},{20,12},{24,0},{28,4},{1,25},{... | collective-permute-start | bytes 258056 | tf_op jit(solution)/shard_map/ppermute | solution.py:23
  41.3 11.9 %collective-permute-start.11 = (f16[336,128]{1,0:T(8,128)(2,1)S(1)}, f16[336,128]{1,0:T(8,128)(2,1)S(1)}, u32[]{:S(2)}, u32[]{:S(2)}) collective-permute-start(f16[336,128]{1,0:T(8,128)(2,1)S(1)} %convert_element_type.91), channel_id=1, source_target_pairs={{0,20},{4,16},{8,28},{12,24},{16,4},{20,0},{24,12},{28,8},{1,21},{... | collective-permute-start | bytes 258056 | tf_op jit(solution)/shard_map/ppermute | solution.py:23
  41.3 12.3 %collective-permute-start.10 = (f16[336,128]{1,0:T(8,128)(2,1)S(1)}, f16[336,128]{1,0:T(8,128)(2,1)S(1)}, u32[]{:S(2)}, u32[]{:S(2)}) collective-permute-start(f16[336,128]{1,0:T(8,128)(2,1)S(1)} %convert_element_type.89), channel_id=1, source_target_pairs={{0,16},{4,20},{8,24},{12,28},{16,0},{20,4},{24,8},{28,12},{1,17},{... | collective-permute-start | bytes 258056 | tf_op jit(solution)/shard_map/ppermute | solution.py:23
  44.3 9.4 %collective-permute-start.9 = (f16[336,128]{1,0:T(8,128)(2,1)S(1)}, f16[336,128]{1,0:T(8,128)(2,1)S(1)}, u32[]{:S(2)}, u32[]{:S(2)}) collective-permute-start(f16[336,128]{1,0:T(8,128)(2,1)S(1)} %convert_element_type.87), channel_id=1, source_target_pairs={{0,12},{4,8},{8,4},{12,0},{16,28},{20,24},{24,20},{28,16},{1,13},{... | collective-permute-start | bytes 258056 | tf_op jit(solution)/shard_map/ppermute | solution.py:23
  45.5 9.0 %collective-permute-start.8 = (f16[336,128]{1,0:T(8,128)(2,1)S(1)}, f16[336,128]{1,0:T(8,128)(2,1)S(1)}, u32[]{:S(2)}, u32[]{:S(2)}) collective-permute-start(f16[336,128]{1,0:T(8,128)(2,1)S(1)} %convert_element_type.85), channel_id=1, source_target_pairs={{0,8},{4,12},{8,0},{12,4},{16,24},{20,28},{24,16},{28,20},{1,9},{5... | collective-permute-start | bytes 258056 | tf_op jit(solution)/shard_map/ppermute | solution.py:23
  49.9 4.6 %collective-permute-start.7 = (f16[336,128]{1,0:T(8,128)(2,1)S(1)}, f16[336,128]{1,0:T(8,128)(2,1)S(1)}, u32[]{:S(2)}, u32[]{:S(2)}) collective-permute-start(f16[336,128]{1,0:T(8,128)(2,1)S(1)} %convert_element_type.83), channel_id=1, source_target_pairs={{0,4},{4,0},{8,12},{12,8},{16,20},{20,16},{24,28},{28,24},{1,5},{5... | collective-permute-start | bytes 258056 | tf_op jit(solution)/shard_map/ppermute | solution.py:23
  55.3 7.8 %collective-permute-start.19 = (f16[1,304,128]{2,1,0:T(8,128)(2,1)S(1)}, f16[1,304,128]{2,1,0:T(8,128)(2,1)S(1)}, u32[]{:S(2)}, u32[]{:S(2)}) collective-permute-start(f16[1,304,128]{2,1,0:T(8,128)(2,1)S(1)} %get-tuple-element.28), channel_id=1, source_target_pairs={{0,24},{4,28},{8,16},{12,20},{16,8},{20,12},{24,0},{28,4},{1,25},{... | collective-permute-start | bytes 233480 | tf_op jit(solution)/shard_map/ppermute | solution.py:23
  57.3 9.8 %collective-permute-start.18 = (f16[1,304,128]{2,1,0:T(8,128)(2,1)S(1)}, f16[1,304,128]{2,1,0:T(8,128)(2,1)S(1)}, u32[]{:S(2)}, u32[]{:S(2)}) collective-permute-start(f16[1,304,128]{2,1,0:T(8,128)(2,1)S(1)} %get-tuple-element.28), channel_id=1, source_target_pairs={{0,20},{4,16},{8,28},{12,24},{16,4},{20,0},{24,12},{28,8},{1,21},{... | collective-permute-start | bytes 233480 | tf_op jit(solution)/shard_map/ppermute | solution.py:23
  59.3 11.8 %collective-permute-start.17 = (f16[1,304,128]{2,1,0:T(8,128)(2,1)S(1)}, f16[1,304,128]{2,1,0:T(8,128)(2,1)S(1)}, u32[]{:S(2)}, u32[]{:S(2)}) collective-permute-start(f16[1,304,128]{2,1,0:T(8,128)(2,1)S(1)} %get-tuple-element.28), channel_id=1, source_target_pairs={{0,16},{4,20},{8,24},{12,28},{16,0},{20,4},{24,8},{28,12},{1,17},{... | collective-permute-start | bytes 233480 | tf_op jit(solution)/shard_map/ppermute | solution.py:23
  60.5 10.6 %collective-permute-start.16 = (f16[1,304,128]{2,1,0:T(8,128)(2,1)S(1)}, f16[1,304,128]{2,1,0:T(8,128)(2,1)S(1)}, u32[]{:S(2)}, u32[]{:S(2)}) collective-permute-start(f16[1,304,128]{2,1,0:T(8,128)(2,1)S(1)} %get-tuple-element.28), channel_id=1, source_target_pairs={{0,12},{4,8},{8,4},{12,0},{16,28},{20,24},{24,20},{28,16},{1,13},{... | collective-permute-start | bytes 233480 | tf_op jit(solution)/shard_map/ppermute | solution.py:23
  61.5 9.7 %collective-permute-start.15 = (f16[1,304,128]{2,1,0:T(8,128)(2,1)S(1)}, f16[1,304,128]{2,1,0:T(8,128)(2,1)S(1)}, u32[]{:S(2)}, u32[]{:S(2)}) collective-permute-start(f16[1,304,128]{2,1,0:T(8,128)(2,1)S(1)} %get-tuple-element.28), channel_id=1, source_target_pairs={{0,8},{4,12},{8,0},{12,4},{16,24},{20,28},{24,16},{28,20},{1,9},{5... | collective-permute-start | bytes 233480 | tf_op jit(solution)/shard_map/ppermute | solution.py:23
  63.2 8.0 %collective-permute-start.14 = (f16[1,304,128]{2,1,0:T(8,128)(2,1)S(1)}, f16[1,304,128]{2,1,0:T(8,128)(2,1)S(1)}, u32[]{:S(2)}, u32[]{:S(2)}) collective-permute-start(f16[1,304,128]{2,1,0:T(8,128)(2,1)S(1)} %get-tuple-element.28), channel_id=1, source_target_pairs={{0,4},{4,0},{8,12},{12,8},{16,20},{20,16},{24,28},{28,24},{1,5},{5... | collective-permute-start | bytes 233480 | tf_op jit(solution)/shard_map/ppermute | solution.py:23
  67.1 7.1 %collective-permute-start.20 = (f16[1,304,128]{2,1,0:T(8,128)(2,1)S(1)}, f16[1,304,128]{2,1,0:T(8,128)(2,1)S(1)}, u32[]{:S(2)}, u32[]{:S(2)}) collective-permute-start(f16[1,304,128]{2,1,0:T(8,128)(2,1)S(1)} %get-tuple-element.28), channel_id=1, source_target_pairs={{0,28},{4,24},{8,20},{12,16},{16,12},{20,8},{24,4},{28,0},{1,29},{... | collective-permute-start | bytes 233480 | tf_op jit(solution)/shard_map/ppermute | solution.py:23

commit v3 on v2

--- a/solution.py
+++ b/solution.py
@@ -10,6 +10,7 @@
 F32, BF16, F16 = jnp.float32, jnp.bfloat16, jnp.float16
 VMEM = pl.BlockSpec(memory_space=pltpu.VMEM)
 SMEM = pl.BlockSpec(memory_space=pltpu.SMEM)
+ANY = pl.BlockSpec(memory_space=pl.ANY)
 SIDE = 8
 NOTE = 16
 
@@ -33,20 +34,41 @@
     return groups
 
 
-def gather_relative(value, axis, groups):
-    parts = [value[None]]
+def gather_groups(value, axis, groups):
+    parts = [value]
     for shift, size in groups:
         held = parts[0] if len(parts) == 1 else jnp.concatenate(parts, axis=0)
         parts = [held] + [swap(held, axis, m << shift) for m in range(1, 1 << size)]
     return parts
 
 
-def conv_kernel(where_ref, x_ref, w_ref, b_ref, out_ref, wide, taps, *, block):
-    rows, cols, chans = x_ref.shape
+def high_groups(count):
+    return [(at + 1, size) for at, size in bit_groups(count // 2, 2, 2)]
+
+
+def conv_kernel(
+    where_ref, x_hbm, w_hbm, b_ref, *refs, part, parts, block
+):
+    out_ref, rows_ref, w_ref, wide, taps, sems = refs[-6:]
+    rows, cols, chans = x_hbm.shape
     half_cols = cols // 2
     out_rows = out_ref.shape[0]
-    first = where_ref[0] * (2 * out_rows) - 1
     total = 2 * out_rows + 2
+    first = (where_ref[0] * parts + part) * (2 * out_rows) - 1
+    start = jnp.clip(first, 0, rows - total)
+    offset = first - start
+    early = total // 2
+    copies = [
+        pltpu.make_async_copy(x_hbm.at[pl.ds(start, early)], rows_ref.at[pl.ds(0, early)], sems.at[0]),
+        pltpu.make_async_copy(
+            x_hbm.at[pl.ds(start + early, total - early)],
+            rows_ref.at[pl.ds(early, total - early)],
+            sems.at[1],
+        ),
+        pltpu.make_async_copy(w_hbm, w_ref, sems.at[2]),
+    ]
+    for copy in copies:
+        copy.start()
     lanes = chans // 128
     edge = jnp.zeros((8, 128), F32)
     for t in range(wide.shape[0]):
@@ -54,9 +76,9 @@
         wide[t, cols + 8 : cols + 16] = edge
 
     def prepare(i, slot):
-        r = first + i
-        inside = (r >= 0) & (r < rows)
-        x = x_ref[jnp.clip(r, 0, rows - 1)].astype(F32)
+        r = i + offset
+        inside = (r >= 0) & (r < total)
+        x = rows_ref[jnp.clip(r, 0, total - 1)].astype(F32)
         x = jnp.where(inside, x, 0.0)
         for t in range(lanes):
             wide[slot * lanes + t, 8 : 8 + cols] = x[:, t * 128 : (t + 1) * 128]
@@ -71,7 +93,12 @@
         prepare(2 * k + 1, 1)
         return carry
 
-    lax.fori_loop(0, total // 2, prepare_two, 0)
+    copies[0].wait()
+    ready = (early - 1) // 2
+    lax.fori_loop(0, ready, prepare_two, 0)
+    copies[1].wait()
+    lax.fori_loop(ready, total // 2, prepare_two, 0)
+    copies[2].wait()
     bias = b_ref[...]
 
     def step(k, carry):
@@ -95,30 +122,37 @@
     lax.fori_loop(0, out_rows // block, step, 0)
 
 
-def conv_pool(where, x, w, b):
+def conv_pool(where, x, w, b, part, parts, after=()):
     rows, cols, chans = x.shape
-    out_rows = rows // 4
+    out_rows = rows // 4 // parts
     block = next(k for k in (6, 4, 3, 2, 1) if out_rows % k == 0)
+    total = 2 * out_rows + 2
     return pl.pallas_call(
-        functools.partial(conv_kernel, block=block),
+        functools.partial(conv_kernel, part=part, parts=parts, block=block),
         out_shape=jax.ShapeDtypeStruct((out_rows, cols // 2, chans), BF16),
-        in_specs=[SMEM, VMEM, VMEM, VMEM],
+        in_specs=[SMEM, ANY, ANY, VMEM] + [ANY] * len(after),
         out_specs=VMEM,
         scratch_shapes=[
+            pltpu.VMEM((total, cols, chans), BF16),
+            pltpu.VMEM(w.shape, BF16),
             pltpu.VMEM((2 * (chans // 128), cols + 16, 128), F32),
-            pltpu.VMEM((2 * out_rows + 2, cols // 2, 4 * chans), BF16),
+            pltpu.VMEM((total, cols // 2, 4 * chans), BF16),
+            pltpu.SemaphoreType.DMA((3,)),
         ],
         compiler_params=params(),
         cost_estimate=pl.CostEstimate(
             flops=4 * out_rows * cols * 9 * chans * chans * 2,
-            bytes_accessed=rows * cols * chans * 2,
+            bytes_accessed=2 * total * cols * chans,
             transcendentals=0,
         ),
         name="conv_pool",
-    )(where, x, w, b)
-
-
-def edge_kernel(where_ref, left_ref, head_ref, tail_ref, right_ref, w_ref, b_ref, out_ref, wide, acc):
+    )(where, x, w, b, *after)
+
+
+def edge_kernel(where_ref, left_ref, head_ref, tail_ref, right_ref, w_hbm, b_ref, *refs):
+    out_ref, w_ref, wide, acc, sem = refs[-5:]
+    copy = pltpu.make_async_copy(w_hbm, w_ref, sem)
+    copy.start()
     rows, width, chans = head_ref.shape
     lanes = chans // 128
     count = 8 * rows
@@ -150,6 +184,7 @@
     bias = b_ref[...]
     depth = 3 * chans
     pad = rows + 16
+    copy.wait()
     for dr in range(3):
         part = jnp.dot(lhs, w_ref[dr * depth : (dr + 1) * depth], preferred_element_type=F32)
         for g in range(8):
@@ -181,21 +216,23 @@
             out_ref[g, t] = (total * keep).astype(BF16).astype(F32)
 
 
-def conv_edges(where, left, head, tail, right, w, b):
+def conv_edges(where, left, head, tail, right, w, b, after):
     rows, _, chans = head.shape
     lanes = chans // 128
     return pl.pallas_call(
         edge_kernel,
         out_shape=jax.ShapeDtypeStruct((4, lanes, rows // 2, 128), F32),
-        in_specs=[SMEM] + [VMEM] * 6,
+        in_specs=[SMEM] + [VMEM] * 4 + [ANY, VMEM] + [ANY] * len(after),
         out_specs=VMEM,
         scratch_shapes=[
+            pltpu.VMEM(w.shape, BF16),
             pltpu.VMEM((2 * lanes, 8 * rows, 128), F32),
             pltpu.VMEM((8 * lanes, rows + 16, 128), F32),
+            pltpu.SemaphoreType.DMA,
         ],
         compiler_params=params(),
         name="conv_edges",
-    )(where, left, head, tail, right, w, b)
+    )(where, left, head, tail, right, w, b, *after)
 
 
 def scale_rows(block, note_rows, sums):
@@ -226,13 +263,14 @@
 
 
 def deep_kernel(
-    where_ref, own_ref, other_ref, edge_ref, w_ref, b_ref, lab_ref, slots_ref, *refs, block, n_parts, chunk, ways
+    where_ref, edge_ref, w_ref, b_ref, lab_ref, slots_ref, *refs, block, n_maps, n_parts, chunk, ways
 ):
+    map_refs, refs = refs[: 2 * n_maps], refs[2 * n_maps :]
     part_refs = refs[:n_parts]
     out_refs = refs[n_parts : n_parts + ways]
     wide, taps, member, grad, weight = refs[n_parts + ways :]
-    part, cols, chans = own_ref.shape
-    rows = 2 * part
+    part, cols, chans = map_refs[0].shape
+    rows = 2 * n_maps * part
     lanes = chans // 128
     width = w_ref.shape[-1]
     half, me = where_ref[0], where_ref[3]
@@ -256,12 +294,13 @@
                 at = (tap * lanes + t) * 128
                 taps[r + 1, :, at : at + 128] = piece.astype(BF16)
 
-    def prepare_two(k, carry):
-        prepare(own_ref, half * part, k, 0)
-        prepare(other_ref, (1 - half) * part, k, 1)
+    def prepare_rows(k, carry):
+        for q in range(n_maps):
+            prepare(map_refs[q], (half * n_maps + q) * part, k, 2 * q)
+            prepare(map_refs[n_maps + q], ((1 - half) * n_maps + q) * part, k, 2 * q + 1)
         return carry
 
-    lax.fori_loop(0, part, prepare_two, 0)
+    lax.fori_loop(0, part, prepare_rows, 0)
     ids = slots_ref[...]
     total = jnp.zeros((entries, 1), F32)
     entry_grad = jnp.zeros((entries, width), F32)
@@ -336,18 +375,20 @@
 
 
 def deep_part(where, own, other, edges, w, b, labels, slots, parts, chunk, count, ways):
-    part, cols, chans = own.shape
-    rows, width = 2 * part, w.shape[-1]
+    part, cols, chans = own[0].shape
+    rows, width = 2 * len(own) * part, w.shape[-1]
     entries = slots.shape[0]
     block = next(k for k in (8, 4, 2, 1) if rows % k == 0)
     out = jax.ShapeDtypeStruct((count // ways * chunk + NOTE + entries, width), F32)
     return pl.pallas_call(
-        functools.partial(deep_kernel, block=block, n_parts=len(parts), chunk=chunk, ways=ways),
+        functools.partial(
+            deep_kernel, block=block, n_maps=len(own), n_parts=len(parts), chunk=chunk, ways=ways
+        ),
         out_shape=(out,) * ways,
-        in_specs=[SMEM] + [VMEM] * (7 + len(parts)),
+        in_specs=[SMEM] + [VMEM] * (5 + 2 * len(own) + len(parts)),
         out_specs=(VMEM,) * ways,
         scratch_shapes=[
-            pltpu.VMEM((2 * (chans // 128), cols + 16, 128), F32),
+            pltpu.VMEM((2 * len(own) * (chans // 128), cols + 16, 128), F32),
             pltpu.VMEM((rows + 2, cols, 3 * chans), BF16),
             pltpu.VMEM((rows, cols, 128), BF16),
             pltpu.VMEM((rows * cols, width), BF16),
@@ -358,7 +399,7 @@
             flops=8 * rows * cols * 9 * chans * width, bytes_accessed=4 << 20, transcendentals=0
         ),
         name="deep_part",
-    )(where, own, other, edges, w, b, labels, slots, *parts)
+    )(where, edges, w, b, labels, slots, *own, *other, *parts)
 
 
 def merge_kernel(where_ref, *refs, chunk, heads, held, entries, shift, next_ways):
@@ -441,7 +482,8 @@
     part_refs, weight_ref, bias_ref, place = refs[:-3], refs[-3], refs[-2], refs[-1]
     me = where_ref[3]
     m = 0
-    for ref in part_refs:
+    for p, ref in enumerate(part_refs):
+        m = 1 if p == len(part_refs) // 2 else m
         for k in range(ref.shape[0]):
             bias, down, _ = read_note(ref[k], chunk)
             j = me ^ m
@@ -451,7 +493,7 @@
             def _():
                 bias_ref[...] = bias
 
-            m += 1
+            m += 2
     weight_ref[...] = place[:rows]
 
 
@@ -502,13 +544,15 @@
     side = jnp.pad(
         jnp.stack([slot_ids.astype(F32), counts]), ((0, SIDE - 2), (0, width - entries))
     )
-    shared = gather_relative(
-        jnp.concatenate([embed_grad, side]), "strip", bit_groups(strip_count, 1, 2)
-    )
-
-    pooled = conv_pool(where, section_input, conv_w, conv_b)
-    other = swap(pooled, "chan", 1)
-    edges = conv_edges(where, left, head, tail, right, conv_w, conv_b)
+    packed = jnp.concatenate([embed_grad, side])
+    near = swap(packed, "strip", 1)
+    shared = gather_groups(jnp.stack([packed, near]), "strip", bit_groups(strip_count, 1, 2)[1:])
+
+    own_a = conv_pool(where, section_input, conv_w, conv_b, 0, 2)
+    own_b = conv_pool(where, section_input, conv_w, conv_b, 1, 2, (near,))
+    pooled = [own_a, own_b]
+    other = [swap(p, "chan", 1) for p in pooled]
+    edges = conv_edges(where, left, head, tail, right, conv_w, conv_b, shared[1:])
 
     groups = bit_groups(strip_count, 3, 3)
     chunk = -(-9 * channels // strip_count // 8) * 8
@@ -544,7 +588,8 @@
         compiler_params=params(),
         name="embed",
     )(where, sums, *shared)
-    gathered = gather_relative(send[0].astype(F16), "strip", groups)
+    gathered = gather_groups(send[0].astype(F16)[None], "strip", high_groups(strip_count))
+    gathered = gathered + [swap(g, "strip", 1) for g in gathered]
     weight_rows, bias_row = spread(
         where, [g.astype(F32) for g in gathered], chunk, strip_count, 9 * channels
     )

time: 76.3 us -> 77.7 us (1.018)
  waiting for transfers between devices: 16.3 us -> 7.38 us
  starting transfers between devices: 35.7 us -> 39.3 us
  Pallas kernels: 17.2 us -> 19.8 us
  local copies, waits for them, and re-layouts: 4.03 us -> 6.61 us
  other arithmetic: 1.78 us -> 3.2 us
    ppermute x20 -> x21, waiting for transfers between devices: 16.3 us -> 7.38 us  [swap(): return lax.ppermute(value, axis, [(i, i ^ mask) for i in range(count)])]
    ppermute x20 -> x21, starting transfers between devices: 30.8 us -> 37.4 us  [swap(): return lax.ppermute(value, axis, [(i, i ^ mask) for i in range(count)])]
    ppermute x1, starting transfers between devices: 4.85 us -> 1.91 us  [body(): lax.ppermute(jnp.where(half == 0, tail, head), ('strip', 'chan'), pairs)]
    pallas_call x2 -> x3, Pallas kernels: 11.8 us -> 14.1 us  [the longest x2 7.97 us: conv_pool(): pl.pallas_call(functools.partial(conv_kernel, part=part, parts=parts, blo...]
    unnamed x20, local copies, waits for them, and re-layouts: 3.87 us -> 5.75 us
  transfers between devices with their start and end apart: 21 -> 22, of which waited for: 8 -> 7; matrix products, arithmetic and copies ran while one was open for 1% -> 2% of each run, Pallas kernels for 11% -> 14%
where the time goes in v3:
time: 77.7 us; the launch traced here: 77.3 us
  starting transfers between devices  39.3 us (51%)
  Pallas kernels  19.8 us (25%)
  waiting for transfers between devices  7.38 us (9%)
  local copies, waits for them, and re-layouts  6.61 us (9%)
  other arithmetic  3.2 us (4%)
  between operations  0.99 us (1%)
    ppermute x21, starting transfers between devices, swap(): return lax.ppermute(value, axis, [(i, i ^ mask) for i in range(count)])  37.4 us
    pallas_call x2, Pallas kernels, conv_pool(): pl.pallas_call(functools.partial(conv_kernel, part=part, parts=parts, blo...  7.97 us
    ppermute x21, waiting for transfers between devices, swap(): return lax.ppermute(value, axis, [(i, i ^ mask) for i in range(count)])  7.38 us
    pallas_call x1, Pallas kernels, deep_part(): pl.pallas_call(functools.partial(deep_kernel, block=block, n_maps=len(own...  6.1 us
    unnamed x20, local copies, waits for them, and re-layouts  5.75 us
    ppermute x1, starting transfers between devices, body(): lax.ppermute(jnp.where(half == 0, tail, head), ('strip', 'chan'), pairs)  1.91 us
    pallas_call x1, Pallas kernels, spread(): pl.pallas_call(functools.partial(spread_kernel, chunk=chunk, rows=rows),...  1.79 us
    pallas_call x1, Pallas kernels, conv_edges(): pl.pallas_call(edge_kernel, out_shape=jax.ShapeDtypeStruct((4, lanes, row...  1.71 us
  transfers between devices with their start and end apart: 22, of which 7 were waited for; matrix products, arithmetic and copies ran while one was open for 2% of the time, Pallas kernels for 14%

profile of v3, /device:TPU:0, one launch (start us, length us, event | category | flops | bytes accessed | tf_op | source)
XLA Modules:
  0.0 77.3 jit_solution(13205417703803226227)
XLA Ops:
  0.6 0.7 convert_bitcast_fusion.1
  1.3 0.8 %eq.29 = s32[1536]{0:T(1024)S(1)} reshape(s32[24,64]{1,0:T(8,128)} %lab_ref.1) | data formatting | bytes 12288 | tf_op jit(solution)/shard_map/eq | solution.py:542
  2.2 0.8 fusion
  3.0 2.9 %collective-permute-start.2 = (f32[72,128]{1,0:T(8,128)S(1)}, f32[72,128]{1,0:T(8,128)S(1)}, u32[]{:S(2)}, u32[]{:S(2)}) collective-permute-start(f32[72,128]{1,0:T(8,128)S(1)} %get-tuple-element.35), channel_id=1, source_target_pairs={{0,4},{4,0},{8,12},{12,8},{16,20},{20,16},{24,28},{28,24},{1,5},{5... | collective-permute-start | bytes 110600 | tf_op jit(solution)/shard_map/ppermute | solution.py:24
  6.0 1.3 %copy-done = bf16[3,3,256,256]{3,2,1,0:T(8,128)(2,1)S(1)} copy-done((bf16[3,3,256,256]{3,2,1,0:T(8,128)(2,1)S(1)}, bf16[3,3,256,256]{3,2,1,0:T(8,128)(2,1)}, u32[]{:S(2)}) %copy-start) | copy-done | bytes 1179672
  7.3 1.9 %copy-done.2 = bf16[48,128,256]{2,1,0:T(8,128)(2,1)S(1)} copy-done((bf16[48,128,256]{2,1,0:T(8,128)(2,1)S(1)}, bf16[48,128,256]{2,1,0:T(8,128)(2,1)}, u32[]{:S(2)}) %copy-start.2) | copy-done | bytes 3145752
  9.2 0.7 copy-done.5
  9.8 4.0 %conv_pool.2.refs_0_ = bf16[6,64,256]{2,1,0:T(8,128)(2,1)S(1)} custom-call(s32[4]{0:T(128)S(1)} %pad_add_fusion.where_ref, bf16[48,128,256]{2,1,0:T(8,128)(2,1)S(1)} %copy-done.2, bf16[2304,256]{1,0:T(8,128)(2,1)S(1)} %bitcast.20, f32[1,256]{1,0:T(1,128)S(1)} %bitcast.24), custom_call_target="tpu_custom_call" | custom-call | flops 3623878656 | bytes 917504 | tf_op jit(solution)/shard_map/conv_pool/pallas_call | solution.py:130
  13.9 1.1 %fusion.2 = (bf16[48,3,256]{2,1,0:T(4,128)(2,1)S(1)}, bf16[48,3,256]{2,1,0:T(4,128)(2,1)S(1)}, bf16[48,3,256]{2,1,0:T(4,128)(2,1)S(1)}) fusion(bf16[48,128,256]{2,1,0:T(8,128)(2,1)} %x_hbm.3, pred[]{:T(512)S(6)} %eq.28), kind=kLoop, calls=%fused_computation.15 | loop fusion | flops 36864 | bytes 368641 | tf_op jit(solution)/shard_map/slice | solution.py:530
  15.1 1.9 %collective-permute-start = (bf16[48,3,256]{2,1,0:T(4,128)(2,1)S(1)}, bf16[48,3,256]{2,1,0:T(4,128)(2,1)S(1)}, u32[]{:S(2)}, u32[]{:S(2)}) collective-permute-start(bf16[48,3,256]{2,1,0:T(4,128)(2,1)S(1)} %get-tuple-element.30), channel_id=1, source_target_pairs={{0,4},{2,6},{4,8},{5,1},{6,10},{7,3},{8,12},{9,5},{10,14},{11,7},{... | collective-permute-start | bytes 221192 | tf_op jit(solution)/shard_map/ppermute | solution.py:537
  17.1 4.2 %collective-permute-start.5 = (f32[2,72,128]{2,1,0:T(8,128)S(1)}, f32[2,72,128]{2,1,0:T(8,128)S(1)}, u32[]{:S(2)}, u32[]{:S(2)}) collective-permute-start(f32[2,72,128]{2,1,0:T(8,128)S(1)} %pad_maximum_fusion.refs_4_.refs_0_), channel_id=1, source_target_pairs={{0,24},{4,28},{8,16},{12,20},{16,8},{20,12},{24,0},{28,4},{1,25},{... | collective-permute-start | bytes 221192 | tf_op jit(solution)/shard_map/ppermute | solution.py:24
  22.0 1.9 %copy-done.3 = bf16[48,128,256]{2,1,0:T(8,128)(2,1)S(1)} copy-done((bf16[48,128,256]{2,1,0:T(8,128)(2,1)S(1)}, bf16[48,128,256]{2,1,0:T(8,128)(2,1)}, u32[]{:S(2)}) %copy-start.3) | copy-done | bytes 3145752
  23.9 4.0 %conv_pool.3.refs_1_ = bf16[6,64,256]{2,1,0:T(8,128)(2,1)S(1)} custom-call(s32[4]{0:T(128)S(1)} %pad_add_fusion.where_ref, bf16[48,128,256]{2,1,0:T(8,128)(2,1)S(1)} %copy-done.3, bf16[2304,256]{1,0:T(8,128)(2,1)S(1)} %bitcast.21, f32[1,256]{1,0:T(1,128)S(1)} %bitcast.25, f32[72,128]{1,0:T(8,128)S(1)} %collective-permute-done.2.refs_0_), custom_call_target="tpu_custom_call" | custom-call | flops 3623878656 | bytes 917504 | tf_op jit(solution)/shard_map/conv_pool/pallas_call | solution.py:130
  28.6 1.7 %conv_edges.1.edge_ref = f32[4,2,24,128]{3,2,1,0:T(8,128)S(1)} custom-call(s32[4]{0:T(128)S(1)} %pad_add_fusion.where_ref, bf16[48,3,256]{2,1,0:T(4,128)(2,1)S(1)} %get-tuple-element.33.left_ref, bf16[48,3,256]{2,1,0:T(4,128)(2,1)S(1)} %get-tuple-element.31.head_ref, bf16[48,3,256]{2,1,0:T(4,128)(2,1)S(1)} %get-tuple-element.29.tail_ref, ...), custom_call_target="tpu_custom_call" | custom-call | tf_op jit(solution)/shard_map/conv_edges/pallas_call | solution.py:222
  30.3 6.1 %deep_part.1 = (f32[336,128]{1,0:T(8,128)S(1)}, f32[336,128]{1,0:T(8,128)S(1)}, f32[336,128]{1,0:T(8,128)S(1)}, f32[336,128]{1,0:T(8,128)S(1)}, f32[336,128]{1,0...) custom-call(s32[4]{0:T(128)S(1)} %pad_add_fusion.where_ref, ...), custom_call_target="tpu_custom_call" | custom-call | flops 3623878656 | bytes 4194304 | tf_op jit(solution)/shard_map/deep_part/pallas_call | solution.py:383
  36.5 3.8 %collective-permute-start.14 = (f16[336,128]{1,0:T(8,128)(2,1)S(1)}, f16[336,128]{1,0:T(8,128)(2,1)S(1)}, u32[]{:S(2)}, u32[]{:S(2)}) collective-permute-start(f16[336,128]{1,0:T(8,128)(2,1)S(1)} %convert_element_type.95), channel_id=1, source_target_pairs={{0,28},{4,24},{8,20},{12,16},{16,12},{20,8},{24,4},{28,0},{1,29},{... | collective-permute-start | bytes 258056 | tf_op jit(solution)/shard_map/ppermute | solution.py:24
  40.3 2.2 %collective-permute-start.13 = (f16[336,128]{1,0:T(8,128)(2,1)S(1)}, f16[336,128]{1,0:T(8,128)(2,1)S(1)}, u32[]{:S(2)}, u32[]{:S(2)}) collective-permute-start(f16[336,128]{1,0:T(8,128)(2,1)S(1)} %convert_element_type.93), channel_id=1, source_target_pairs={{0,24},{4,28},{8,16},{12,20},{16,8},{20,12},{24,0},{28,4},{1,25},{... | collective-permute-start | bytes 258056 | tf_op jit(solution)/shard_map/ppermute | solution.py:24
  42.6 4.4 %collective-permute-start.12 = (f16[336,128]{1,0:T(8,128)(2,1)S(1)}, f16[336,128]{1,0:T(8,128)(2,1)S(1)}, u32[]{:S(2)}, u32[]{:S(2)}) collective-permute-start(f16[336,128]{1,0:T(8,128)(2,1)S(1)} %convert_element_type.91), channel_id=1, source_target_pairs={{0,20},{4,16},{8,28},{12,24},{16,4},{20,0},{24,12},{28,8},{1,21},{... | collective-permute-start | bytes 258056 | tf_op jit(solution)/shard_map/ppermute | solution.py:24
  47.0 1.5 %collective-permute-start.10 = (f16[336,128]{1,0:T(8,128)(2,1)S(1)}, f16[336,128]{1,0:T(8,128)(2,1)S(1)}, u32[]{:S(2)}, u32[]{:S(2)}) collective-permute-start(f16[336,128]{1,0:T(8,128)(2,1)S(1)} %convert_element_type.87), channel_id=1, source_target_pairs={{0,12},{4,8},{8,4},{12,0},{16,28},{20,24},{24,20},{28,16},{1,13},{... | collective-permute-start | bytes 258056 | tf_op jit(solution)/shard_map/ppermute | solution.py:24
  49.2 5.4 %collective-permute-start.8 = (f16[336,128]{1,0:T(8,128)(2,1)S(1)}, f16[336,128]{1,0:T(8,128)(2,1)S(1)}, u32[]{:S(2)}, u32[]{:S(2)}) collective-permute-start(f16[336,128]{1,0:T(8,128)(2,1)S(1)} %convert_element_type.83), channel_id=1, source_target_pairs={{0,4},{4,0},{8,12},{12,8},{16,20},{20,16},{24,28},{28,24},{1,5},{5... | collective-permute-start | bytes 258056 | tf_op jit(solution)/shard_map/ppermute | solution.py:24
  54.6 2.1 %collective-permute-done.12 = f16[336,128]{1,0:T(8,128)(2,1)S(1)} collective-permute-done((f16[336,128]{1,0:T(8,128)(2,1)S(1)}, f16[336,128]{1,0:T(8,128)(2,1)S(1)}, u32[]{:S(2)}, u32[]{:S(2)}) %collective-permute-start.12) | collective-permute-done | bytes 86048 | tf_op jit(solution)/shard_map/ppermute | solution.py:24
  56.8 1.1 %collective-permute-done.11 = f16[336,128]{1,0:T(8,128)(2,1)S(1)} collective-permute-done((f16[336,128]{1,0:T(8,128)(2,1)S(1)}, f16[336,128]{1,0:T(8,128)(2,1)S(1)}, u32[]{:S(2)}, u32[]{:S(2)}) %collective-permute-start.11) | collective-permute-done | bytes 86048 | tf_op jit(solution)/shard_map/ppermute | solution.py:24
  58.3 0.8 merge.1
  59.1 4.1 %collective-permute-start.17 = (f16[1,304,128]{2,1,0:T(8,128)(2,1)S(1)}, f16[1,304,128]{2,1,0:T(8,128)(2,1)S(1)}, u32[]{:S(2)}, u32[]{:S(2)}) collective-permute-start(f16[1,304,128]{2,1,0:T(8,128)(2,1)S(1)} %get-tuple-element.28), channel_id=1, source_target_pairs={{0,24},{4,28},{8,16},{12,20},{16,8},{20,12},{24,0},{28,4},{1,25},{... | collective-permute-start | bytes 233480 | tf_op jit(solution)/shard_map/ppermute | solution.py:24
  63.8 2.0 %collective-permute-start.18 = (f16[1,304,128]{2,1,0:T(8,128)(2,1)S(1)}, f16[1,304,128]{2,1,0:T(8,128)(2,1)S(1)}, u32[]{:S(2)}, u32[]{:S(2)}) collective-permute-start(f16[1,304,128]{2,1,0:T(8,128)(2,1)S(1)} %get-tuple-element.28), channel_id=1, source_target_pairs={{0,4},{4,0},{8,12},{12,8},{16,20},{20,16},{24,28},{28,24},{1,5},{5... | collective-permute-start | bytes 233480 | tf_op jit(solution)/shard_map/ppermute | solution.py:24
  66.2 2.2 %collective-permute-start.21 = (f16[1,304,128]{2,1,0:T(8,128)(2,1)S(1)}, f16[1,304,128]{2,1,0:T(8,128)(2,1)S(1)}, u32[]{:S(2)}, u32[]{:S(2)}) collective-permute-start(f16[1,304,128]{2,1,0:T(8,128)(2,1)S(1)} %collective-permute-done.17), channel_id=1, source_target_pairs={{0,4},{4,0},{8,12},{12,8},{16,20},{20,16},{24,28},{28,24},{1,5},{5... | collective-permute-start | bytes 233480 | tf_op jit(solution)/shard_map/ppermute | solution.py:24
  68.4 0.8 %collective-permute-done.16 = f16[1,304,128]{2,1,0:T(8,128)(2,1)S(1)} collective-permute-done((f16[1,304,128]{2,1,0:T(8,128)(2,1)S(1)}, f16[1,304,128]{2,1,0:T(8,128)(2,1)S(1)}, u32[]{:S(2)}, u32[]{:S(2)}) %collective-permute-start.16) | collective-permute-done | bytes 77856 | tf_op jit(solution)/shard_map/ppermute | solution.py:24
  69.2 1.9 %collective-permute-start.20 = (f16[1,304,128]{2,1,0:T(8,128)(2,1)S(1)}, f16[1,304,128]{2,1,0:T(8,128)(2,1)S(1)}, u32[]{:S(2)}, u32[]{:S(2)}) collective-permute-start(f16[1,304,128]{2,1,0:T(8,128)(2,1)S(1)} %collective-permute-done.16), channel_id=1, source_target_pairs={{0,4},{4,0},{8,12},{12,8},{16,20},{20,16},{24,28},{28,24},{1,5},{5... | collective-permute-start | bytes 233480 | tf_op jit(solution)/shard_map/ppermute | solution.py:24
  71.3 1.5 %embed.1 = f32[64,128]{1,0:T(8,128)} custom-call(s32[4]{0:T(128)S(1)} %pad_add_fusion.where_ref, f32[256,128]{1,0:T(8,128)S(1)} %get-tuple-element.23.sums_ref, f32[2,72,128]{2,1,0:T(8,128)S(1)} %pad_maximum_fusion.refs_4_.refs_0_, f32[2,72,128]{2,1,0:T(8,128)S(1)} %collective-permute-done.3.refs_0_.refs_5_.refs_1_, ...), custom_call_target="tpu_custom_call" | custom-call | tf_op jit(solution)/shard_map/embed/pallas_call | solution.py:583
  72.9 1.0 %collective-permute-done.20 = f16[1,304,128]{2,1,0:T(8,128)(2,1)S(1)} collective-permute-done((f16[1,304,128]{2,1,0:T(8,128)(2,1)S(1)}, f16[1,304,128]{2,1,0:T(8,128)(2,1)S(1)}, u32[]{:S(2)}, u32[]{:S(2)}) %collective-permute-start.20) | collective-permute-done | bytes 77856 | tf_op jit(solution)/shard_map/ppermute | solution.py:24
  74.0 1.5 %collective-permute-done.19 = f16[1,304,128]{2,1,0:T(8,128)(2,1)S(1)} collective-permute-done((f16[1,304,128]{2,1,0:T(8,128)(2,1)S(1)}, f16[1,304,128]{2,1,0:T(8,128)(2,1)S(1)}, u32[]{:S(2)}, u32[]{:S(2)}) %collective-permute-start.19) | collective-permute-done | bytes 77856 | tf_op jit(solution)/shard_map/ppermute | solution.py:24
  75.5 1.8 %spread.1 = (f32[2304,128]{1,0:T(8,128)}, f32[1,128]{1,0:T(1,128)}) custom-call(s32[4]{0:T(128)S(1)} %pad_add_fusion.where_ref, f32[1,304,128]{2,1,0:T(8,128)S(1)} %get-tuple-element.27.refs_0_, f32[1,304,128]{2,1,0:T(8,128)S(1)} %convert_element_type.100.refs_1_, f32[1,304,128]{2,1,0:T(8,128)S(1)} %convert_element_type.101.refs_2_, ...), custom_call_target="tpu_custom_call" | custom-call | tf_op jit(solution)/shard_map/spread/pallas_call | solution.py:502
  (71 shorter events, 4.2 us)
Async XLA Ops:
  3.0 14.1 %collective-permute-start.2 = (f32[72,128]{1,0:T(8,128)S(1)}, f32[72,128]{1,0:T(8,128)S(1)}, u32[]{:S(2)}, u32[]{:S(2)}) collective-permute-start(f32[72,128]{1,0:T(8,128)S(1)} %get-tuple-element.35), channel_id=1, source_target_pairs={{0,4},{4,0},{8,12},{12,8},{16,20},{20,16},{24,28},{28,24},{1,5},{5... | collective-permute-start | bytes 110600 | tf_op jit(solution)/shard_map/ppermute | solution.py:24
  6.0 1.3 %copy-start = (bf16[3,3,256,256]{3,2,1,0:T(8,128)(2,1)S(1)}, bf16[3,3,256,256]{3,2,1,0:T(8,128)(2,1)}, u32[]{:S(2)}) copy-start(bf16[3,3,256,256]{3,2,1,0:T(8,128)(2,1)} %param.9) | copy-start | bytes 3538948
  7.3 1.9 %copy-start.2 = (bf16[48,128,256]{2,1,0:T(8,128)(2,1)S(1)}, bf16[48,128,256]{2,1,0:T(8,128)(2,1)}, u32[]{:S(2)}) copy-start(bf16[48,128,256]{2,1,0:T(8,128)(2,1)} %x_hbm.3) | copy-start | bytes 9437188
  9.2 0.7 copy-start.5
  9.8 7.2 %copy-start.9 = (s32[32]{0:T(128)S(1)}, s32[32]{0:T(128)}, u32[]{:S(2)}) copy-start(s32[32]{0:T(128)} %param.14) | copy-start | bytes 388
  9.8 12.1 %copy-start.1 = (bf16[3,3,256,256]{3,2,1,0:T(8,128)(2,1)S(1)}, bf16[3,3,256,256]{3,2,1,0:T(8,128)(2,1)}, u32[]{:S(2)}) copy-start(bf16[3,3,256,256]{3,2,1,0:T(8,128)(2,1)} %param.9) | copy-start | bytes 3538948
  9.8 12.1 %copy-start.6 = (f32[256]{0:T(256)S(1)}, f32[256]{0:T(256)}, u32[]{:S(2)}) copy-start(f32[256]{0:T(256)} %param.10) | copy-start | bytes 3076
  13.8 16.4 %collective-permute-start.6 = (bf16[6,64,256]{2,1,0:T(8,128)(2,1)S(1)}, bf16[6,64,256]{2,1,0:T(8,128)(2,1)S(1)}, u32[]{:S(2)}, u32[]{:S(2)}) collective-permute-start(bf16[6,64,256]{2,1,0:T(8,128)(2,1)S(1)} %conv_pool.2.refs_0_), channel_id=1, source_target_pairs={{0,1},{1,0},{2,3},{3,2},{4,5},{5,4},{6,7},{7,6},{8,9},{9,8},{10,11... | collective-permute-start | bytes 589832 | tf_op jit(solution)/shard_map/ppermute | solution.py:24
  15.1 6.9 %collective-permute-start = (bf16[48,3,256]{2,1,0:T(4,128)(2,1)S(1)}, bf16[48,3,256]{2,1,0:T(4,128)(2,1)S(1)}, u32[]{:S(2)}, u32[]{:S(2)}) collective-permute-start(bf16[48,3,256]{2,1,0:T(4,128)(2,1)S(1)} %get-tuple-element.30), channel_id=1, source_target_pairs={{0,4},{2,6},{4,8},{5,1},{6,10},{7,3},{8,12},{9,5},{10,14},{11,7},{... | collective-permute-start | bytes 221192 | tf_op jit(solution)/shard_map/ppermute | solution.py:537
  17.1 13.2 %copy-start.4 = (s32[24,64]{1,0:T(8,128)S(1)}, s32[24,64]{1,0:T(8,128)}, u32[]{:S(2)}) copy-start(s32[24,64]{1,0:T(8,128)} %lab_ref.1) | copy-start | bytes 18436
  17.1 13.2 %copy-start.8 = (f32[128]{0:T(128)S(1)}, f32[128]{0:T(128)}, u32[]{:S(2)}) copy-start(f32[128]{0:T(128)} %param.12) | copy-start | bytes 1540
  17.1 11.4 %collective-permute-start.5 = (f32[2,72,128]{2,1,0:T(8,128)S(1)}, f32[2,72,128]{2,1,0:T(8,128)S(1)}, u32[]{:S(2)}, u32[]{:S(2)}) collective-permute-start(f32[2,72,128]{2,1,0:T(8,128)S(1)} %pad_maximum_fusion.refs_4_.refs_0_), channel_id=1, source_target_pairs={{0,24},{4,28},{8,16},{12,20},{16,8},{20,12},{24,0},{28,4},{1,25},{... | collective-permute-start | bytes 221192 | tf_op jit(solution)/shard_map/ppermute | solution.py:24
  21.3 7.2 %collective-permute-start.4 = (f32[2,72,128]{2,1,0:T(8,128)S(1)}, f32[2,72,128]{2,1,0:T(8,128)S(1)}, u32[]{:S(2)}, u32[]{:S(2)}) collective-permute-start(f32[2,72,128]{2,1,0:T(8,128)S(1)} %pad_maximum_fusion.refs_4_.refs_0_), channel_id=1, source_target_pairs={{0,16},{4,20},{8,24},{12,28},{16,0},{20,4},{24,8},{28,12},{1,17},{... | collective-permute-start | bytes 221192 | tf_op jit(solution)/shard_map/ppermute | solution.py:24
  21.3 7.2 %collective-permute-start.3 = (f32[2,72,128]{2,1,0:T(8,128)S(1)}, f32[2,72,128]{2,1,0:T(8,128)S(1)}, u32[]{:S(2)}, u32[]{:S(2)}) collective-permute-start(f32[2,72,128]{2,1,0:T(8,128)S(1)} %pad_maximum_fusion.refs_4_.refs_0_), channel_id=1, source_target_pairs={{0,8},{4,12},{8,0},{12,4},{16,24},{20,28},{24,16},{28,20},{1,9},{5... | collective-permute-start | bytes 221192 | tf_op jit(solution)/shard_map/ppermute | solution.py:24
  22.0 5.9 %collective-permute-start.1 = (bf16[48,3,256]{2,1,0:T(4,128)(2,1)S(1)}, bf16[48,3,256]{2,1,0:T(4,128)(2,1)S(1)}, u32[]{:S(2)}, u32[]{:S(2)}) collective-permute-start(bf16[48,3,256]{2,1,0:T(4,128)(2,1)S(1)} %collective-permute-done), channel_id=1, source_target_pairs={{0,1},{1,0},{2,3},{3,2},{4,5},{5,4},{6,7},{7,6},{8,9},{9,8},{10,11... | collective-permute-start | bytes 221192 | tf_op jit(solution)/shard_map/ppermute | solution.py:24
  22.0 1.9 %copy-start.3 = (bf16[48,128,256]{2,1,0:T(8,128)(2,1)S(1)}, bf16[48,128,256]{2,1,0:T(8,128)(2,1)}, u32[]{:S(2)}) copy-start(bf16[48,128,256]{2,1,0:T(8,128)(2,1)} %x_hbm.3) | copy-start | bytes 9437188
  23.9 6.4 %copy-start.7 = (bf16[3,3,256,128]{3,2,1,0:T(8,128)(2,1)S(1)}, bf16[3,3,256,128]{3,2,1,0:T(8,128)(2,1)}, u32[]{:S(2)}) copy-start(bf16[3,3,256,128]{3,2,1,0:T(8,128)(2,1)} %param.11) | copy-start | bytes 1769476
  27.9 2.4 %collective-permute-start.7 = (bf16[6,64,256]{2,1,0:T(8,128)(2,1)S(1)}, bf16[6,64,256]{2,1,0:T(8,128)(2,1)S(1)}, u32[]{:S(2)}, u32[]{:S(2)}) collective-permute-start(bf16[6,64,256]{2,1,0:T(8,128)(2,1)S(1)} %conv_pool.3.refs_1_), channel_id=1, source_target_pairs={{0,1},{1,0},{2,3},{3,2},{4,5},{5,4},{6,7},{7,6},{8,9},{9,8},{10,11... | collective-permute-start | bytes 589832 | tf_op jit(solution)/shard_map/ppermute | solution.py:24
  36.5 12.1 %collective-permute-start.14 = (f16[336,128]{1,0:T(8,128)(2,1)S(1)}, f16[336,128]{1,0:T(8,128)(2,1)S(1)}, u32[]{:S(2)}, u32[]{:S(2)}) collective-permute-start(f16[336,128]{1,0:T(8,128)(2,1)S(1)} %convert_element_type.95), channel_id=1, source_target_pairs={{0,28},{4,24},{8,20},{12,16},{16,12},{20,8},{24,4},{28,0},{1,29},{... | collective-permute-start | bytes 258056 | tf_op jit(solution)/shard_map/ppermute | solution.py:24
  40.3 8.9 %collective-permute-start.13 = (f16[336,128]{1,0:T(8,128)(2,1)S(1)}, f16[336,128]{1,0:T(8,128)(2,1)S(1)}, u32[]{:S(2)}, u32[]{:S(2)}) collective-permute-start(f16[336,128]{1,0:T(8,128)(2,1)S(1)} %convert_element_type.93), channel_id=1, source_target_pairs={{0,24},{4,28},{8,16},{12,20},{16,8},{20,12},{24,0},{28,4},{1,25},{... | collective-permute-start | bytes 258056 | tf_op jit(solution)/shard_map/ppermute | solution.py:24
  42.6 14.1 %collective-permute-start.12 = (f16[336,128]{1,0:T(8,128)(2,1)S(1)}, f16[336,128]{1,0:T(8,128)(2,1)S(1)}, u32[]{:S(2)}, u32[]{:S(2)}) collective-permute-start(f16[336,128]{1,0:T(8,128)(2,1)S(1)} %convert_element_type.91), channel_id=1, source_target_pairs={{0,20},{4,16},{8,28},{12,24},{16,4},{20,0},{24,12},{28,8},{1,21},{... | collective-permute-start | bytes 258056 | tf_op jit(solution)/shard_map/ppermute | solution.py:24
  47.0 10.9 %collective-permute-start.11 = (f16[336,128]{1,0:T(8,128)(2,1)S(1)}, f16[336,128]{1,0:T(8,128)(2,1)S(1)}, u32[]{:S(2)}, u32[]{:S(2)}) collective-permute-start(f16[336,128]{1,0:T(8,128)(2,1)S(1)} %convert_element_type.89), channel_id=1, source_target_pairs={{0,16},{4,20},{8,24},{12,28},{16,0},{20,4},{24,8},{28,12},{1,17},{... | collective-permute-start | bytes 258056 | tf_op jit(solution)/shard_map/ppermute | solution.py:24
  47.0 10.9 %collective-permute-start.10 = (f16[336,128]{1,0:T(8,128)(2,1)S(1)}, f16[336,128]{1,0:T(8,128)(2,1)S(1)}, u32[]{:S(2)}, u32[]{:S(2)}) collective-permute-start(f16[336,128]{1,0:T(8,128)(2,1)S(1)} %convert_element_type.87), channel_id=1, source_target_pairs={{0,12},{4,8},{8,4},{12,0},{16,28},{20,24},{24,20},{28,16},{1,13},{... | collective-permute-start | bytes 258056 | tf_op jit(solution)/shard_map/ppermute | solution.py:24
  48.6 9.3 %collective-permute-start.9 = (f16[336,128]{1,0:T(8,128)(2,1)S(1)}, f16[336,128]{1,0:T(8,128)(2,1)S(1)}, u32[]{:S(2)}, u32[]{:S(2)}) collective-permute-start(f16[336,128]{1,0:T(8,128)(2,1)S(1)} %convert_element_type.85), channel_id=1, source_target_pairs={{0,8},{4,12},{8,0},{12,4},{16,24},{20,28},{24,16},{28,20},{1,9},{5... | collective-permute-start | bytes 258056 | tf_op jit(solution)/shard_map/ppermute | solution.py:24
  49.2 9.1 %collective-permute-start.8 = (f16[336,128]{1,0:T(8,128)(2,1)S(1)}, f16[336,128]{1,0:T(8,128)(2,1)S(1)}, u32[]{:S(2)}, u32[]{:S(2)}) collective-permute-start(f16[336,128]{1,0:T(8,128)(2,1)S(1)} %convert_element_type.83), channel_id=1, source_target_pairs={{0,4},{4,0},{8,12},{12,8},{16,20},{20,16},{24,28},{28,24},{1,5},{5... | collective-permute-start | bytes 258056 | tf_op jit(solution)/shard_map/ppermute | solution.py:24
  59.1 7.1 %collective-permute-start.17 = (f16[1,304,128]{2,1,0:T(8,128)(2,1)S(1)}, f16[1,304,128]{2,1,0:T(8,128)(2,1)S(1)}, u32[]{:S(2)}, u32[]{:S(2)}) collective-permute-start(f16[1,304,128]{2,1,0:T(8,128)(2,1)S(1)} %get-tuple-element.28), channel_id=1, source_target_pairs={{0,24},{4,28},{8,16},{12,20},{16,8},{20,12},{24,0},{28,4},{1,25},{... | collective-permute-start | bytes 233480 | tf_op jit(solution)/shard_map/ppermute | solution.py:24
  63.2 6.1 %collective-permute-start.16 = (f16[1,304,128]{2,1,0:T(8,128)(2,1)S(1)}, f16[1,304,128]{2,1,0:T(8,128)(2,1)S(1)}, u32[]{:S(2)}, u32[]{:S(2)}) collective-permute-start(f16[1,304,128]{2,1,0:T(8,128)(2,1)S(1)} %get-tuple-element.28), channel_id=1, source_target_pairs={{0,16},{4,20},{8,24},{12,28},{16,0},{20,4},{24,8},{28,12},{1,17},{... | collective-permute-start | bytes 233480 | tf_op jit(solution)/shard_map/ppermute | solution.py:24
  63.2 7.9 %collective-permute-start.15 = (f16[1,304,128]{2,1,0:T(8,128)(2,1)S(1)}, f16[1,304,128]{2,1,0:T(8,128)(2,1)S(1)}, u32[]{:S(2)}, u32[]{:S(2)}) collective-permute-start(f16[1,304,128]{2,1,0:T(8,128)(2,1)S(1)} %get-tuple-element.28), channel_id=1, source_target_pairs={{0,8},{4,12},{8,0},{12,4},{16,24},{20,28},{24,16},{28,20},{1,9},{5... | collective-permute-start | bytes 233480 | tf_op jit(solution)/shard_map/ppermute | solution.py:24
  63.8 9.0 %collective-permute-start.18 = (f16[1,304,128]{2,1,0:T(8,128)(2,1)S(1)}, f16[1,304,128]{2,1,0:T(8,128)(2,1)S(1)}, u32[]{:S(2)}, u32[]{:S(2)}) collective-permute-start(f16[1,304,128]{2,1,0:T(8,128)(2,1)S(1)} %get-tuple-element.28), channel_id=1, source_target_pairs={{0,4},{4,0},{8,12},{12,8},{16,20},{20,16},{24,28},{28,24},{1,5},{5... | collective-permute-start | bytes 233480 | tf_op jit(solution)/shard_map/ppermute | solution.py:24
  66.2 6.7 %collective-permute-start.21 = (f16[1,304,128]{2,1,0:T(8,128)(2,1)S(1)}, f16[1,304,128]{2,1,0:T(8,128)(2,1)S(1)}, u32[]{:S(2)}, u32[]{:S(2)}) collective-permute-start(f16[1,304,128]{2,1,0:T(8,128)(2,1)S(1)} %collective-permute-done.17), channel_id=1, source_target_pairs={{0,4},{4,0},{8,12},{12,8},{16,20},{20,16},{24,28},{28,24},{1,5},{5... | collective-permute-start | bytes 233480 | tf_op jit(solution)/shard_map/ppermute | solution.py:24
  69.2 4.7 %collective-permute-start.20 = (f16[1,304,128]{2,1,0:T(8,128)(2,1)S(1)}, f16[1,304,128]{2,1,0:T(8,128)(2,1)S(1)}, u32[]{:S(2)}, u32[]{:S(2)}) collective-permute-start(f16[1,304,128]{2,1,0:T(8,128)(2,1)S(1)} %collective-permute-done.16), channel_id=1, source_target_pairs={{0,4},{4,0},{8,12},{12,8},{16,20},{20,16},{24,28},{28,24},{1,5},{5... | collective-permute-start | bytes 233480 | tf_op jit(solution)/shard_map/ppermute | solution.py:24
  71.1 4.4 %collective-permute-start.19 = (f16[1,304,128]{2,1,0:T(8,128)(2,1)S(1)}, f16[1,304,128]{2,1,0:T(8,128)(2,1)S(1)}, u32[]{:S(2)}, u32[]{:S(2)}) collective-permute-start(f16[1,304,128]{2,1,0:T(8,128)(2,1)S(1)} %collective-permute-done.15), channel_id=1, source_target_pairs={{0,4},{4,0},{8,12},{12,8},{16,20},{20,16},{24,28},{28,24},{1,5},{5... | collective-permute-start | bytes 233480 | tf_op jit(solution)/shard_map/ppermute | solution.py:24

commit v4 on v3

v4 whole, which is shorter than its diff:
```python
import functools

import jax
import jax.numpy as jnp
from jax import lax
from jax.experimental import pallas as pl
from jax.experimental.pallas import tpu as pltpu
from jax.sharding import PartitionSpec as P

F32, BF16, F16 = jnp.float32, jnp.bfloat16, jnp.float16
VMEM = pl.BlockSpec(memory_space=pltpu.VMEM)
SMEM = pl.BlockSpec(memory_space=pltpu.SMEM)
HBM = pl.BlockSpec(memory_space=pltpu.HBM)
ANY = pl.BlockSpec(memory_space=pl.ANY)
SIDE = 8
NOTE = 16


def params(mib=8):
    return pltpu.CompilerParams(vmem_limit_bytes=mib << 20)


def swap(value, axis, mask):
    count = lax.axis_size(axis)
    return lax.ppermute(value, axis, [(i, i ^ mask) for i in range(count)])


def bit_groups(count, first, most):
    bits = count.bit_length() - 1
    groups, at = [], 0
    while at < bits:
        size = min(first if at == 0 else most, bits - at)
        groups.append((at, size))
        at += size
    return groups


def gather_groups(value, axis, groups):
    parts = [value]
    for shift, size in groups:
        held = parts[0] if len(parts) == 1 else jnp.concatenate(parts, axis=0)
        parts = [held] + [swap(held, axis, m << shift) for m in range(1, 1 << size)]
    return parts


def relative(refs):
    half = len(refs) // 2
    for low in range(2):
        m = low
        for ref in refs[low * half : (low + 1) * half]:
            for k in range(ref.shape[0]):
                yield m, ref, k
                m += 2


def high_groups(count):
    return [(at + 1, size) for at, size in bit_groups(count // 2, 2, 2)]


def window_kernel(where_ref, x_hbm, taps, rows_ref, wide, sems):
    rows, cols, chans = x_hbm.shape
    half_cols = cols // 2
    total = taps.shape[0]
    first = where_ref[0] * (total - 2) - 1
    start = jnp.clip(first, 0, rows - total)
    offset = first - start
    steps = sems.shape[0]
    cuts = [k * total // steps for k in range(steps + 1)]
    copies = []
    for k in range(steps):
        at, size = cuts[k], cuts[k + 1] - cuts[k]
        copies.append(
            pltpu.make_async_copy(
                x_hbm.at[pl.ds(start + at, size)], rows_ref.at[pl.ds(at, size)], sems.at[k]
            )
        )
        copies[k].start()
    lanes = chans // 128
    border = jnp.zeros((8, 128), F32)
    for t in range(wide.shape[0]):
        wide[t, 0:8] = border
        wide[t, cols + 8 : cols + 16] = border

    def prepare(i, slot):
        r = i + offset
        inside = (r >= 0) & (r < total)
        x = rows_ref[jnp.clip(r, 0, total - 1)].astype(F32)
        x = jnp.where(inside, x, 0.0)
        for t in range(lanes):
            wide[slot * lanes + t, 8 : 8 + cols] = x[:, t * 128 : (t + 1) * 128]
        for tap in range(4):
            for t in range(lanes):
                piece = wide[slot * lanes + t, pl.ds(7 + tap, half_cols, stride=2), :]
                at = (tap * lanes + t) * 128
                taps[i, :, at : at + 128] = piece.astype(BF16)

    def prepare_two(k, carry):
        prepare(2 * k, 0)
        prepare(2 * k + 1, 1)
        return carry

    done = 0
    for k in range(steps):
        copies[k].wait()
        ready = (cuts[k + 1] - 1) // 2 if k + 1 < steps else total // 2
        lax.fori_loop(done, ready, prepare_two, 0)
        done = ready


def windows(where, x):
    rows, cols, chans = x.shape
    total = rows // 2 + 2
    return pl.pallas_call(
        window_kernel,
        out_shape=jax.ShapeDtypeStruct((total, cols // 2, 4 * chans), BF16),
        in_specs=[SMEM, HBM],
        out_specs=VMEM,
        scratch_shapes=[
            pltpu.VMEM((total, cols, chans), BF16),
            pltpu.VMEM((2 * (chans // 128), cols + 16, 128), F32),
            pltpu.SemaphoreType.DMA((4,)),
        ],
        compiler_params=params(12),
        cost_estimate=pl.CostEstimate(flops=0, bytes_accessed=12 << 20, transcendentals=0),
        name="windows",
    )(where, pltpu.with_memory_space_constraint(x, pltpu.HBM))


def edge_part(where_ref, pairs, w_ref, bias, edge_ref, wide, acc):
    rows, width, chans = pairs[0][0].shape
    lanes = chans // 128
    for s, pair in enumerate(pairs):
        for k, ref in enumerate(pair):
            x = ref[...].astype(F32)
            for t in range(lanes):
                for r in range(rows):
                    at = r * 8 + k * width
                    wide[s * lanes + t, at : at + width] = x[r, :, t * 128 : (t + 1) * 128]
    column = [
        [
            jnp.concatenate(
                [wide[s * lanes + t, pl.ds(c, rows, stride=8), :] for t in range(lanes)], axis=-1
            ).astype(BF16)
            for c in range(2 * width)
        ]
        for s in range(2)
    ]
    lhs = jnp.concatenate(
        [
            jnp.concatenate(column[s][2 * j + phase : 2 * j + phase + 3], axis=-1)
            for s in range(2)
            for j in range(2)
            for phase in range(2)
        ],
        axis=0,
    )
    depth = 3 * chans
    pad = rows + 16
    for dr in range(3):
        part = jnp.dot(lhs, w_ref[dr * depth : (dr + 1) * depth], preferred_element_type=F32)
        for g in range(8):
            own = part[g * rows : (g + 1) * rows]
            for t in range(lanes):
                at = 9 - dr
                piece = own[:, t * 128 : (t + 1) * 128]
                if dr == 0:
                    acc[g * lanes + t, 0:8] = jnp.zeros((8, 128), F32)
                    acc[g * lanes + t, 8 + rows : pad] = jnp.zeros((8, 128), F32)
                    acc[g * lanes + t, 8:9] = jnp.zeros((1, 128), F32)
                    acc[g * lanes + t, at : at + rows] = piece
                else:
                    acc[g * lanes + t, at : at + rows] += piece
    for g in range(4):
        for t in range(lanes):
            total = None
            for phase in range(2):
                at = (2 * g + phase) * lanes + t
                v = acc[at, 8 : 8 + rows] + bias[:, t * 128 : (t + 1) * 128]
                acc[at, 8 : 8 + rows] = v * jax.nn.sigmoid(v)
                both = (
                    acc[at, pl.ds(8, rows // 2, stride=2), :]
                    + acc[at, pl.ds(9, rows // 2, stride=2), :]
                )
                total = both if total is None else total + both
            lost = jnp.where(g == 0, where_ref[1], jnp.where(g == 3, where_ref[2], 0))
            keep = jnp.where(lost > 0, 0.0, 0.25)
            edge_ref[g, t] = (total * keep).astype(BF16).astype(F32)


def conv_kernel(
    where_ref, taps, w_ref, b_ref, left_ref, head_ref, tail_ref, right_ref, *refs, block
):
    out_ref, edge_ref, wide, acc = refs[-4:]
    half_cols, chans = taps.shape[1], taps.shape[2] // 4
    out_rows = out_ref.shape[0]
    bias = b_ref[...]

    def step(k, carry):
        r0 = k * 2 * block
        total = None
        for phase in range(2):
            lhs = jnp.concatenate(
                [
                    taps[pl.ds(r0 + dr, 2 * block), :, phase * chans : (phase + 3) * chans]
                    for dr in range(3)
                ],
                axis=-1,
            ).reshape(2 * block * half_cols, 9 * chans)
            v = jnp.dot(lhs, w_ref[...], preferred_element_type=F32) + bias
            h = (v * jax.nn.sigmoid(v)).reshape(block, 2, half_cols, chans)
            h = h[:, 0] + h[:, 1]
            total = h if total is None else total + h
        out_ref[pl.ds(k * block, block)] = (total * 0.25).astype(BF16)
        return carry

    lax.fori_loop(0, out_rows // block, step, 0)
    pairs = ((left_ref, head_ref), (tail_ref, right_ref))
    edge_part(where_ref, pairs, w_ref, bias, edge_ref, wide, acc)


def conv_pool(where, taps, w, b, left, head, tail, right, after):
    total, half_cols, width = taps.shape
    chans, rows = width // 4, head.shape[0]
    out_rows, lanes = (total - 2) // 2, chans // 128
    block = next(k for k in (6, 4, 3, 2, 1) if out_rows % k == 0)
    return pl.pallas_call(
        functools.partial(conv_kernel, block=block),
        out_shape=(
            jax.ShapeDtypeStruct((out_rows, half_cols, chans), BF16),
            jax.ShapeDtypeStruct((4, lanes, rows // 2, 128), F32),
        ),
        in_specs=[SMEM] + [VMEM] * 7 + [ANY] * len(after),
        out_specs=(VMEM, VMEM),
        scratch_shapes=[
            pltpu.VMEM((2 * lanes, 8 * rows, 128), F32),
            pltpu.VMEM((8 * lanes, rows + 16, 128), F32),
        ],
        compiler_params=params(24),
        cost_estimate=pl.CostEstimate(
            flops=8 * out_rows * half_cols * 9 * chans * chans,
            bytes_accessed=8 << 20,
            transcendentals=0,
        ),
        name="conv_pool",
    )(where, taps, w, b, left, head, tail, right, *after)


def side_kernel(grad_ref, slots_ref, labels_ref, out_ref):
    owned, width = grad_ref.shape
    entries = slots_ref.shape[1]
    out_ref[:owned] = grad_ref[...]
    lane = lax.broadcasted_iota(jnp.int32, (1, width), 1)
    labels = labels_ref[...]
    counts = jnp.zeros((1, width), F32)
    for e in range(entries):
        hit = jnp.where(labels == e, 1.0, 0.0)
        hit = jnp.sum(jnp.sum(hit, axis=0, keepdims=True), axis=1, keepdims=True)
        counts = jnp.where(lane == e, hit, counts)
    ids = jnp.concatenate(
        [slots_ref[...].astype(F32), jnp.zeros((1, width - entries), F32)], axis=1
    )
    row = lax.broadcasted_iota(jnp.int32, (SIDE, width), 0)
    out_ref[owned:] = jnp.where(row == 0, ids, jnp.where(row == 1, counts, 0.0))


def pack_side(grad, slots, labels):
    owned, width = grad.shape
    return pl.pallas_call(
        side_kernel,
        out_shape=jax.ShapeDtypeStruct((owned + SIDE, width), F32),
        in_specs=[VMEM] * 3,
        out_specs=VMEM,
        compiler_params=params(),
        name="pack_side",
    )(grad, slots.reshape(1, -1), labels)


def join_kernel(*refs):
    at = 0
    for ref in refs[:-1]:
        refs[-1][at : at + ref.shape[0]] = ref[...]
        at += ref.shape[0]


def join(parts):
    shape = (sum(p.shape[0] for p in parts),) + parts[0].shape[1:]
    return pl.pallas_call(
        join_kernel,
        out_shape=jax.ShapeDtypeStruct(shape, F32),
        in_specs=[VMEM] * len(parts),
        out_specs=VMEM,
        compiler_params=params(),
        name="join",
    )(*parts)


def scale_rows(block, note_rows, sums):
    def exponent(values):
        top = None
        for v in values:
            one = jnp.max(jnp.max(jnp.abs(v), axis=0, keepdims=True), axis=1, keepdims=True)
            top = one if top is None else jnp.maximum(top, one)
        return jnp.ceil(jnp.log2(jnp.maximum(top, 1e-30)))

    power = exponent([block, note_rows])
    power_sums = exponent([sums])
    return power, power_sums


def note_block(bias, power, power_sums, width):
    row = lax.broadcasted_iota(jnp.int32, (NOTE, width), 0)
    bias = jnp.broadcast_to(bias, (NOTE, width))
    power = jnp.broadcast_to(power, (NOTE, width))
    power_sums = jnp.broadcast_to(power_sums, (NOTE, width))
    return jnp.where(row == 0, bias, jnp.where(row == 1, power, power_sums))


def read_note(part, at):
    note = part[at : at + NOTE]
    down = jnp.exp2(note[1:2] - 12.0)
    return note[0:1] * down, down, jnp.exp2(note[2:3] - 12.0)


def deep_kernel(where_ref, edge_ref, w_ref, b_ref, lab_ref, *refs, block, n_maps, entries):
    map_refs = refs[: 2 * n_maps]
    taps, member, slope, sums_ref, wide = refs[2 * n_maps :]
    part, cols, chans = map_refs[0].shape
    rows = 2 * n_maps * part
    lanes = chans // 128
    width = w_ref.shape[-1]
    half = where_ref[0]
    taps[0] = jnp.zeros(taps.shape[1:], BF16)
    taps[rows + 1] = jnp.zeros(taps.shape[1:], BF16)

    def prepare(ref, base, i, slot):
        x = ref[i].astype(F32)
        r = base + i
        for t in range(lanes):
            s = slot * lanes + t
            at = t * 128
            wide[s, 8 : 8 + cols] = x[:, at : at + 128]
            for g, place in enumerate((7, 8, 7 + cols, 8 + cols)):
                wide[s, place : place + 1] = edge_ref[g, t, pl.ds(r, 1), :]
        for tap in range(3):
            for t in range(lanes):
                piece = wide[slot * lanes + t, 7 + tap : 7 + tap + cols, :]
                at = (tap * lanes + t) * 128
                taps[r + 1, :, at : at + 128] = piece.astype(BF16)

    def prepare_rows(k, carry):
        for q in range(n_maps):
            prepare(map_refs[q], (half * n_maps + q) * part, k, 2 * q)
            prepare(map_refs[n_maps + q], ((1 - half) * n_maps + q) * part, k, 2 * q + 1)
        return carry

    lax.fori_loop(0, part, prepare_rows, 0)
    lab = jnp.transpose(lab_ref[...].astype(F32))
    lane = lax.broadcasted_iota(jnp.int32, (cols, 128), 1)
    want = jnp.where(lane < 3 * entries, lane % entries, -1).astype(F32)
    for r in range(rows):
        member[r] = (lab[:, r : r + 1] == want).astype(BF16)
    bias = b_ref[...]
    size = block * cols

    def step(k, sums):
        r0 = k * block
        lhs = jnp.concatenate([taps[pl.ds(r0 + dr, block)] for dr in range(3)], axis=-1)
        v = jnp.dot(lhs.reshape(size, 9 * chans), w_ref[...], preferred_element_type=F32) + bias
        sig = jax.nn.sigmoid(v)
        features = (v * sig).astype(BF16)
        slope[pl.ds(k * size, size)] = sig * (1.0 + v * (1.0 - sig))
        mem = member[pl.ds(r0, block)].reshape(size, 128)
        return sums + lax.dot_general(
            mem, features, (((0,), (0,)), ((), ())), preferred_element_type=F32
        )[:entries]

    sums_ref[...] = lax.fori_loop(0, rows // block, step, jnp.zeros((entries, width), F32))


def deep_forward(where, own, other, edges, w, b, labels, entries):
    part, cols, chans = own[0].shape
    rows, width = 2 * len(own) * part, w.shape[-1]
    block = next(k for k in (8, 4, 2, 1) if rows % k == 0)
    return pl.pallas_call(
        functools.partial(deep_kernel, block=block, n_maps=len(own), entries=entries),
        out_shape=(
            jax.ShapeDtypeStruct((rows + 2, cols, 3 * chans), BF16),
            jax.ShapeDtypeStruct((rows, cols, 128), BF16),
            jax.ShapeDtypeStruct((rows * cols, width), F32),
            jax.ShapeDtypeStruct((entries, width), F32),
        ),
        in_specs=[SMEM] + [VMEM] * (4 + 2 * len(own)),
        out_specs=(VMEM,) * 4,
        scratch_shapes=[pltpu.VMEM((2 * len(own) * (chans // 128), cols + 16, 128), F32)],
        compiler_params=params(16),
        cost_estimate=pl.CostEstimate(
            flops=4 * rows * cols * 9 * chans * width, bytes_accessed=8 << 20, transcendentals=0
        ),
        name="deep_forward",
    )(where, edges, w, b, labels, *own, *other)


def grad_kernel(
    where_ref, taps, member, slope, sums_ref, slots_ref, *refs, n_parts, chunk, ways, with_sums
):
    part_refs = refs[:n_parts]
    out_refs = refs[n_parts : n_parts + ways]
    grad, weight = refs[n_parts + ways :]
    rows, cols, depth = member.shape[0], taps.shape[1], taps.shape[2]
    width = slope.shape[-1]
    me = where_ref[3]
    entries = slots_ref.shape[0]
    owned = part_refs[0].shape[1] - SIDE
    ids = slots_ref[...]
    total = jnp.zeros((entries, 1), F32)
    entry_grad = jnp.zeros((entries, width), F32)
    owner, inner = ids // owned, ids % owned
    spot = lax.broadcasted_iota(jnp.int32, (entries, owned), 1)
    for m, ref, k in relative(part_refs):
        there = ref[k, owned : owned + 1, :entries] == ids.astype(F32)
        counts = ref[k, owned + 1 : owned + 2, :entries]
        total += jnp.sum(jnp.where(there, counts, 0.0), axis=1, keepdims=True)
        hot = ((owner ^ me) == m) & (inner == spot)
        entry_grad += jnp.dot(
            hot.astype(F32), ref[k, :owned], precision=lax.Precision.HIGHEST, preferred_element_type=F32
        )
    entry_grad = entry_grad / jnp.maximum(total, 1.0)
    high = entry_grad.astype(BF16)
    rest = entry_grad - high.astype(F32)
    mid = rest.astype(BF16)
    low = (rest - mid.astype(F32)).astype(BF16)
    terms = jnp.concatenate([high, mid, low, jnp.zeros((128 - 3 * entries, width), BF16)], axis=0)
    pixel = jnp.dot(member[...].reshape(rows * cols, 128), terms, preferred_element_type=F32)
    dg = (pixel * slope[...]).astype(BF16)
    grad[...] = dg
    bias_sum = jnp.sum(dg.astype(F32), axis=0, keepdims=True)
    for dr in range(3):
        window = taps[dr : dr + rows].reshape(rows * cols, depth)
        out = lax.dot_general(grad[...], window, (((0,), (0,)), ((), ())), preferred_element_type=F32)
        weight[dr * depth : (dr + 1) * depth] = jnp.transpose(out)
    if weight.shape[0] > 3 * depth:
        weight[3 * depth :] = jnp.zeros((weight.shape[0] - 3 * depth, width), F32)
    sums = sums_ref[...]
    power, power_sums = scale_rows(weight[...], bias_sum, sums)
    up = jnp.exp2(12.0 - power)
    note = note_block(bias_sum * up, power, power_sums, width)
    digit = lax.rem(me, ways)
    heads = weight.shape[0] // chunk // ways
    for m in range(ways):
        for hi in range(heads):
            j = hi * ways + (digit ^ m)
            out_refs[m][hi * chunk : (hi + 1) * chunk] = (
                weight[pl.ds(pl.multiple_of(j * chunk, 8), chunk)] * up
            )
        out_refs[m][heads * chunk : heads * chunk + NOTE] = note
    out_refs[with_sums][heads * chunk + NOTE :] = sums * jnp.exp2(12.0 - power_sums)


def deep_backward(where, forward, slots, parts, chunk, count, ways, with_sums):
    taps, _, slope, sums = forward
    width, entries = slope.shape[-1], sums.shape[0]
    size = count // ways * chunk + NOTE
    return pl.pallas_call(
        functools.partial(
            grad_kernel, n_parts=len(parts), chunk=chunk, ways=ways, with_sums=with_sums
        ),
        out_shape=tuple(
            jax.ShapeDtypeStruct((size + (entries if m == with_sums else 0), width), F32)
            for m in range(ways)
        ),
        in_specs=[SMEM] + [VMEM] * (5 + len(parts)),
        out_specs=(VMEM,) * ways,
        scratch_shapes=[
            pltpu.VMEM(slope.shape, BF16),
            pltpu.VMEM((count * chunk, width), F32),
        ],
        compiler_params=params(16),
        cost_estimate=pl.CostEstimate(
            flops=4 * slope.shape[0] * 3 * taps.shape[2] * width, bytes_accessed=8 << 20, transcendentals=0
        ),
        name="deep_backward",
    )(where, *forward, slots, *parts)


def pair_kernel(own_ref, got_ref, own_sums_ref, got_sums_ref, *refs, size, entries):
    out_ref = refs[-1]
    own, got = own_ref[size : size + NOTE], got_ref[size : size + NOTE]
    power = jnp.maximum(own[1:2], got[1:2]) + 1.0
    power_sums = jnp.maximum(own[2:3], got[2:3])
    own_down, got_down = jnp.exp2(own[1:2] - power), jnp.exp2(got[1:2] - power)
    out_ref[:size] = own_ref[:size] * own_down + got_ref[:size] * got_down
    bias = own[0:1] * own_down + got[0:1] * got_down
    out_ref[size : size + NOTE] = note_block(bias, power, power_sums, own.shape[-1])
    at = size + NOTE
    sums = own_sums_ref[at : at + entries] * jnp.exp2(own[2:3] - power_sums)
    out_ref[at : at + entries] = sums
    sums = got_sums_ref[at : at + entries] * jnp.exp2(got[2:3] - power_sums)
    out_ref[at + entries : at + 2 * entries] = sums


def merge_pair(own, got, own_sums, got_sums, size, entries, after):
    width = own.shape[-1]
    return pl.pallas_call(
        functools.partial(pair_kernel, size=size, entries=entries),
        out_shape=jax.ShapeDtypeStruct((size + NOTE + 2 * entries, width), F32),
        in_specs=[VMEM] * 4 + [ANY] * len(after),
        out_specs=VMEM,
        compiler_params=params(),
        name="merge_pair",
    )(own, got, own_sums, got_sums, *after)


def merge_kernel(where_ref, *refs, chunk, heads, held, entries, shift, next_ways):
    n_parts = len(refs) - next_ways - 1
    part_refs, out_refs, sums_ref = refs[:n_parts], refs[n_parts:-1], refs[-1]
    width = part_refs[0].shape[-1]
    size = heads * chunk
    total, bias = jnp.zeros((size, width), F32), jnp.zeros((1, width), F32)
    sums_rows = held * entries
    for m, ref in enumerate(part_refs):
        more, down, down_sums = read_note(ref, size)
        total, bias = total + ref[:size] * down, bias + more
        sums_ref[m * sums_rows : (m + 1) * sums_rows] = ref[size + NOTE :] * down_sums
    sums = sums_ref[...]
    power, power_sums = scale_rows(total, bias, sums)
    up = jnp.exp2(12.0 - power)
    note = note_block(bias * up, power, power_sums, width)
    total = total * up
    if next_ways == 1:
        out_refs[0][:size] = total
        out_refs[0][size:] = note
        return
    sums = sums * jnp.exp2(12.0 - power_sums)
    digit = lax.rem(where_ref[3] >> shift, next_ways)
    for m in range(next_ways):
        for hi in range(heads // next_ways):
            piece = jnp.zeros((chunk, width), F32)
            for d in range(next_ways):
                at = (hi * next_ways + d) * chunk
                piece = jnp.where((digit ^ m) == d, total[at : at + chunk], piece)
            out_refs[m][hi * chunk : (hi + 1) * chunk] = piece
        at = heads // next_ways * chunk
        out_refs[m][at : at + NOTE] = note
        out_refs[m][at + NOTE :] = sums


def merge(where, parts, chunk, heads, held, entries, shift, next_ways):
    width = parts[0].shape[-1]
    sums_rows = len(parts) * held * entries
    if next_ways == 1:
        outs = (jax.ShapeDtypeStruct((heads * chunk + NOTE, width), F32),)
    else:
        rows = heads // next_ways * chunk + NOTE + sums_rows
        outs = (jax.ShapeDtypeStruct((rows, width), F32),) * next_ways
    outs = outs + (jax.ShapeDtypeStruct((sums_rows, width), F32),)
    out = pl.pallas_call(
        functools.partial(
            merge_kernel, chunk=chunk, heads=heads, held=held, entries=entries, shift=shift, next_ways=next_ways
        ),
        out_shape=outs,
        in_specs=[SMEM] + [VMEM] * len(parts),
        out_specs=(VMEM,) * len(outs),
        compiler_params=params(),
        name="merge",
    )(where, *parts)
    return out[:-1], out[-1]


def embed_kernel(where_ref, sums_ref, *refs, entries):
    part_refs, out_ref = refs[:-1], refs[-1]
    owned, width = out_ref.shape
    own = (where_ref[3] * owned + lax.broadcasted_iota(jnp.int32, (owned, entries), 0)).astype(F32)
    sums, counts = jnp.zeros((owned, width), F32), jnp.zeros((owned, 1), F32)
    for m, ref, k in relative(part_refs):
        there = ref[k, owned : owned + 1, :entries] == own
        count = ref[k, owned + 1 : owned + 2, :entries]
        counts += jnp.sum(jnp.where(there, count, 0.0), axis=1, keepdims=True)
        sums += jnp.dot(
            there.astype(F32),
            sums_ref[m * entries : (m + 1) * entries],
            precision=lax.Precision.HIGHEST,
            preferred_element_type=F32,
        )
    out_ref[...] = sums / jnp.maximum(counts, 1.0)


def spread_kernel(where_ref, *refs, chunk, rows):
    part_refs, weight_ref, bias_ref, place = refs[:-3], refs[-3], refs[-2], refs[-1]
    me = where_ref[3]
    for m, ref, k in relative(part_refs):
        bias, down, _ = read_note(ref[k], chunk)
        j = me ^ m
        place[pl.ds(pl.multiple_of(j * chunk, 8), chunk)] = ref[k, :chunk] * down

        @pl.when(j == 0)
        def _():
            bias_ref[...] = bias

    weight_ref[...] = place[:rows]


def spread(where, parts, chunk, count, rows):
    width = parts[0].shape[-1]
    return pl.pallas_call(
        functools.partial(spread_kernel, chunk=chunk, rows=rows),
        out_shape=(jax.ShapeDtypeStruct((rows, width), F32), jax.ShapeDtypeStruct((1, width), F32)),
        in_specs=[SMEM] + [VMEM] * len(parts),
        out_specs=(VMEM, VMEM),
        scratch_shapes=[pltpu.VMEM((count * chunk, width), F32)],
        compiler_params=params(),
        name="spread",
    )(where, *parts)


def body(
    section_input, conv_weight, conv_bias, deep_weight, deep_bias, labels, slot_ids, embed_grad
):
    chan_count = lax.axis_size("chan")
    strip_count = lax.axis_size("strip")
    chan_pos = lax.axis_index("chan")
    strip_pos = lax.axis_index("strip")
    half = chan_pos & 1
    channels = section_input.shape[-1]
    entries = slot_ids.shape[0]
    owned, width = embed_grad.shape
    where = jnp.stack(
        [half, (strip_pos == 0).astype(jnp.int32), (strip_pos == strip_count - 1).astype(jnp.int32), strip_pos]
    ).astype(jnp.int32)
    conv_w = conv_weight.reshape(9 * channels, -1)
    conv_b = conv_bias.reshape(1, -1)

    head, tail = section_input[:, :3], section_input[:, -3:]
    pairs = []
    for s in range(strip_count):
        for c in range(chan_count):
            to = s + 1 - 2 * (c & 1)
            if 0 <= to < strip_count:
                pairs.append((s * chan_count + c, to * chan_count + c))
    got = lax.ppermute(jnp.where(half == 0, tail, head), ("strip", "chan"), pairs)
    traded = swap(got, "chan", 1)
    left = jnp.where(half == 0, got, traded)
    right = jnp.where(half == 0, traded, got)

    shared = gather_groups(
        pack_side(embed_grad, slot_ids, labels)[None], "strip", high_groups(strip_count)
    )

    taps = windows(where, section_input)
    joined = join(shared)
    shared = [joined, swap(joined, "strip", 1)]
    pooled, edges = conv_pool(where, taps, conv_w, conv_b, left, head, tail, right, [joined])
    other = swap(pooled, "chan", 1)

    chunk = -(-9 * channels // strip_count // 8) * 8
    bits = min(2, strip_count.bit_length() - 2)
    pieces = 1 << bits
    order = list(range(pieces // 2, pieces)) + list(range(pieces // 2))[::-1]
    with_sums = 2 * order[0] + 1
    forward = deep_forward(
        where,
        [pooled],
        [other],
        edges,
        deep_weight.reshape(9 * channels, width),
        deep_bias.reshape(1, width),
        labels,
        entries,
    )
    send = deep_backward(
        where, forward, slot_ids.reshape(entries, 1), shared, chunk, strip_count, 2 * pieces, with_sums
    )
    heads, held = strip_count // (2 * pieces), 2
    got = {k: swap(send[2 * k + 1].astype(F16), "strip", 1).astype(F32) for k in order}
    pair, parts, before = {}, {}, []
    for k in order:
        pair[k] = merge_pair(
            send[2 * k], got[k], send[with_sums], got[order[0]], heads * chunk, entries, before
        )
        parts[k] = swap(pair[k].astype(F16), "strip", 2 * k).astype(F32) if k else pair[k]
        before = [pair[k]] if k < pieces // 2 or k + 1 < pieces else [pair[k], parts[order[0]]]
    parts = [parts[k] for k in range(pieces)]
    held *= pieces
    send, sums = parts, None
    shift = bits + 1
    while True:
        left_bits = strip_count.bit_length() - 1 - shift
        size = min(3, left_bits)
        send, sums = merge(
            where, parts, chunk, heads, held // len(parts), entries, shift, 1 << size
        )
        if size == 0:
            break
        ways = 1 << size
        heads //= ways
        parts = [send[0]] + [
            swap(send[m].astype(F16), "strip", m << shift).astype(F32) for m in range(1, ways)
        ]
        held *= ways
        shift += size
    embeddings = pl.pallas_call(
        functools.partial(embed_kernel, entries=entries),
        out_shape=jax.ShapeDtypeStruct((owned, width), F32),
        in_specs=[SMEM] + [VMEM] * (1 + len(shared)),
        out_specs=VMEM,
        compiler_params=params(),
        name="embed",
    )(where, sums, *shared)
    gathered = gather_groups(send[0].astype(F16)[None], "strip", high_groups(strip_count))
    gathered = gathered + [swap(g, "strip", 1) for g in gathered]
    weight_rows, bias_row = spread(
        where, [g.astype(F32) for g in gathered], chunk, strip_count, 9 * channels
    )
    return (embeddings, weight_rows.reshape(3, 3, channels, width), bias_row[0])


def solution(mesh):
    placed = (
        P(None, "strip", None),
        P(),
        P(),
        P(None, None, None, "chan"),
        P("chan"),
        P(None, "strip"),
        P("strip"),
        P("strip", "chan"),
    )
    return jax.shard_map(
        body,
        mesh=mesh,
        in_specs=placed,
        out_specs=(P("strip", "chan"), P(None, None, None, "chan"), P("chan")),
        check_vma=False,
    )
```

time: 77.7 us -> 68.1 us (0.88)
  starting transfers between devices: 39.3 us -> 25.9 us
  waiting for transfers between devices: 7.38 us -> 17.4 us
  local copies, waits for them, and re-layouts: 6.61 us -> 2.23 us
  other arithmetic: 3.2 us -> 1.62 us
    ppermute x21 -> x20, starting transfers between devices: 37.4 us -> 21 us  [swap(): return lax.ppermute(value, axis, [(i, i ^ mask) for i in range(count)])]
    ppermute x21 -> x20, waiting for transfers between devices: 7.38 us -> 17.4 us  [swap(): return lax.ppermute(value, axis, [(i, i ^ mask) for i in range(count)])]
    unnamed x20 -> x18, local copies, waits for them, and re-layouts: 5.75 us -> 2.15 us
    ppermute x1, starting transfers between devices: 1.91 us -> 4.85 us  [body(): lax.ppermute(jnp.where(half == 0, tail, head), ('strip', 'chan'), pairs)]
    another operation x4 -> x0, other arithmetic: 1.44 us -> none  [the longest x2 0.77 us: body(): jnp.stack([packed, near])]
    pallas_call x4 -> x10, Pallas kernels: 15.8 us -> 15.6 us  [the longest x1 5.5 us: conv_pool(): pl.pallas_call(functools.partial(conv_kernel, block=block), out_shape=(ja...]
  transfers between devices with their start and end apart: 22 -> 21, of which waited for: 7 -> 13; matrix products, arithmetic and copies ran while one was open for 2% -> 1% of each run, Pallas kernels for 14% -> 13%
where the time goes in v4:
time: 68.1 us; the launch traced here: 67.8 us
  starting transfers between devices  25.9 us (38%)
  Pallas kernels  19.6 us (29%)
  waiting for transfers between devices  17.4 us (26%)
  local copies, waits for them, and re-layouts  2.23 us (3%)
  other arithmetic  1.62 us (2%)
  between operations  0.98 us (1%)
    ppermute x20, starting transfers between devices, swap(): return lax.ppermute(value, axis, [(i, i ^ mask) for i in range(count)])  21 us
    ppermute x20, waiting for transfers between devices, swap(): return lax.ppermute(value, axis, [(i, i ^ mask) for i in range(count)])  17.4 us
    pallas_call x1, Pallas kernels, conv_pool(): pl.pallas_call(functools.partial(conv_kernel, block=block), out_shape=(ja...  5.5 us
    ppermute x1, starting transfers between devices, body(): lax.ppermute(jnp.where(half == 0, tail, head), ('strip', 'chan'), pairs)  4.85 us
    pallas_call x1, Pallas kernels, deep_forward(): pl.pallas_call(functools.partial(deep_kernel, block=block, n_maps=len(own...  4.38 us
    pallas_call x1, Pallas kernels, deep_backward(): pl.pallas_call(functools.partial(grad_kernel, n_parts=len(parts), chunk=c...  2.89 us
    pallas_call x1, Pallas kernels, windows(): pl.pallas_call(window_kernel, out_shape=jax.ShapeDtypeStruct((total, cols...  2.58 us
    unnamed x18, local copies, waits for them, and re-layouts  2.15 us
  transfers between devices with their start and end apart: 21, of which 13 were waited for; matrix products, arithmetic and copies ran while one was open for 1% of the time, Pallas kernels for 13%

profile of v4, /device:TPU:0, one launch (start us, length us, event | category | flops | bytes accessed | tf_op | source)
XLA Modules:
  0.0 67.8 jit_solution(13304103601805058586)
XLA Ops:
  0.6 1.1 %fusion.1 = (bf16[48,3,256]{2,1,0:T(4,128)(2,1)S(1)}, bf16[48,3,256]{2,1,0:T(4,128)(2,1)S(1)}, bf16[48,3,256]{2,1,0:T(4,128)(2,1)S(1)}) fusion(bf16[48,128,256]{2,1,0:T(8,128)(2,1)} %x_hbm.1, pred[]{:T(512)S(6)} %eq.13), kind=kLoop, calls=%fused_computation.6 | loop fusion | flops 36864 | bytes 368641 | tf_op jit(solution)/shard_map/slice | solution.py:632
  1.8 4.8 %collective-permute-start = (bf16[48,3,256]{2,1,0:T(4,128)(2,1)S(1)}, bf16[48,3,256]{2,1,0:T(4,128)(2,1)S(1)}, u32[]{:S(2)}, u32[]{:S(2)}) collective-permute-start(bf16[48,3,256]{2,1,0:T(4,128)(2,1)S(1)} %get-tuple-element.42), channel_id=1, source_target_pairs={{0,4},{2,6},{4,8},{5,1},{6,10},{7,3},{8,12},{9,5},{10,14},{11,7},{... | collective-permute-start | bytes 221192 | tf_op jit(solution)/shard_map/ppermute | solution.py:639
  6.7 0.7 %copy-done = f32[64,128]{1,0:T(8,128)S(1)} copy-done((f32[64,128]{1,0:T(8,128)S(1)}, f32[64,128]{1,0:T(8,128)}, u32[]{:S(2)}) %copy-start) | copy-done | bytes 32792
  8.9 3.7 %collective-permute-start.4 = (f32[1,72,128]{2,1,0:T(8,128)S(1)}, f32[1,72,128]{2,1,0:T(8,128)S(1)}, u32[]{:S(2)}, u32[]{:S(2)}) collective-permute-start(f32[1,72,128]{2,1,0:T(8,128)S(1)} %bitcast.16), channel_id=1, source_target_pairs={{0,24},{4,28},{8,16},{12,20},{16,8},{20,12},{24,0},{28,4},{1,25},{... | collective-permute-start | bytes 110600 | tf_op jit(solution)/shard_map/ppermute | solution.py:25
  12.6 0.8 %collective-permute-start.2 = (f32[1,72,128]{2,1,0:T(8,128)S(1)}, f32[1,72,128]{2,1,0:T(8,128)S(1)}, u32[]{:S(2)}, u32[]{:S(2)}) collective-permute-start(f32[1,72,128]{2,1,0:T(8,128)S(1)} %bitcast.18), channel_id=1, source_target_pairs={{0,8},{4,12},{8,0},{12,4},{16,24},{20,28},{24,16},{28,20},{1,9},{5... | collective-permute-start | bytes 110600 | tf_op jit(solution)/shard_map/ppermute | solution.py:25
  13.5 2.6 %windows.1.taps = bf16[26,64,1024]{2,1,0:T(8,128)(2,1)S(1)} custom-call(s32[4]{0:T(128)S(1)} %pad_add_fusion.where_ref, bf16[48,128,256]{2,1,0:T(8,128)(2,1)} %x_hbm.1), custom_call_target="tpu_custom_call" | custom-call | bytes 12582912 | tf_op jit(solution)/shard_map/windows/pallas_call | solution.py:113
  16.1 1.4 %collective-permute-done.3.refs_2_ = f32[1,72,128]{2,1,0:T(8,128)S(1)} collective-permute-done((f32[1,72,128]{2,1,0:T(8,128)S(1)}, f32[1,72,128]{2,1,0:T(8,128)S(1)}, u32[]{:S(2)}, u32[]{:S(2)}) %collective-permute-start.3) | collective-permute-done | bytes 36896 | tf_op jit(solution)/shard_map/ppermute | solution.py:25
  17.6 5.5 %conv_pool.1 = (bf16[12,64,256]{2,1,0:T(8,128)(2,1)S(1)}, f32[4,2,24,128]{3,2,1,0:T(8,128)S(1)}) custom-call(s32[4]{0:T(128)S(1)} %pad_add_fusion.where_ref, bf16[26,64,1024]{2,1,0:T(8,128)(2,1)S(1)} %windows.1.taps, bf16[2304,256]{1,0:T(8,128)(2,1)S(1)} %bitcast.22, f32[1,256]{1,0:T(1,128)S(1)} %bitcast.24, ...), custom_call_target="tpu_custom_call" | custom-call | flops 3623878656 | bytes 8388608 | tf_op jit(solution)/shard_map/conv_pool/pallas_call | solution.py:226
  24.0 0.9 %collective-permute-done.5.refs_1_ = bf16[12,64,256]{2,1,0:T(8,128)(2,1)S(1)} collective-permute-done((bf16[12,64,256]{2,1,0:T(8,128)(2,1)S(1)}, bf16[12,64,256]{2,1,0:T(8,128)(2,1)S(1)}, u32[]{:S(2)}, u32[]{:S(2)}) %collective-permute-start.5) | collective-permute-done | bytes 393248 | tf_op jit(solution)/shard_map/ppermute | solution.py:25
  24.9 4.4 %deep_forward.1 = (bf16[26,64,768]{2,1,0:T(8,128)(2,1)S(1)}, bf16[24,64,128]{2,1,0:T(8,128)(2,1)S(1)}, f32[1536,128]{1,0:T(8,128)S(1)}, f32[32,128]{1,0:T(8,128)S(1)}) custom-call(s32[4]{0:T(128)S(1)} %pad_add_fusion.where_ref, f32[4,2,24,128]{3,2,1,0:T(8,128)S(1)} %get-tuple-element.21.edge_ref, bf16[2304,128]{1,0:T(8,128)(2,1)S(1)} %bitcast.23, ...), custom_call_target="tpu_custom_call" | custom-call | flops 1811939328 | bytes 8388608 | tf_op jit(solution)/shard_map/deep_forward/pallas_call | solution.py:384
  29.6 2.9 %deep_backward.1 = (f32[304,128]{1,0:T(8,128)S(1)}, f32[304,128]{1,0:T(8,128)S(1)}, f32[304,128]{1,0:T(8,128)S(1)}, f32[304,128]{1,0:T(8,128)S(1)}, f32[304,128]...) custom-call(s32[4]{0:T(128)S(1)} %pad_add_fusion.where_ref, ...), custom_call_target="tpu_custom_call" | custom-call | flops 1811939328 | bytes 8388608 | tf_op jit(solution)/shard_map/deep_backward/pallas_call | solution.py:463
  32.8 4.2 %collective-permute-done.8 = f16[336,128]{1,0:T(8,128)(2,1)S(1)} collective-permute-done((f16[336,128]{1,0:T(8,128)(2,1)S(1)}, f16[336,128]{1,0:T(8,128)(2,1)S(1)}, u32[]{:S(2)}, u32[]{:S(2)}) %collective-permute-start.8) | collective-permute-done | bytes 86048 | tf_op jit(solution)/shard_map/ppermute | solution.py:25
  37.1 2.1 %collective-permute-start.11 = (f16[368,128]{1,0:T(8,128)(2,1)S(1)}, f16[368,128]{1,0:T(8,128)(2,1)S(1)}, u32[]{:S(2)}, u32[]{:S(2)}) collective-permute-start(f16[368,128]{1,0:T(8,128)(2,1)S(1)} %convert_element_type.81), channel_id=1, source_target_pairs={{0,16},{4,20},{8,24},{12,28},{16,0},{20,4},{24,8},{28,12},{1,17},{... | collective-permute-start | bytes 282632 | tf_op jit(solution)/shard_map/ppermute | solution.py:25
  39.7 1.7 %collective-permute-start.9 = (f16[304,128]{1,0:T(8,128)(2,1)S(1)}, f16[304,128]{1,0:T(8,128)(2,1)S(1)}, u32[]{:S(2)}, u32[]{:S(2)}) collective-permute-start(f16[304,128]{1,0:T(8,128)(2,1)S(1)} %convert_element_type.77), channel_id=1, source_target_pairs={{0,4},{4,0},{8,12},{12,8},{16,20},{20,16},{24,28},{28,24},{1,5},{5... | collective-permute-start | bytes 233480 | tf_op jit(solution)/shard_map/ppermute | solution.py:25
  41.4 2.3 %collective-permute-done.10 = f16[304,128]{1,0:T(8,128)(2,1)S(1)} collective-permute-done((f16[304,128]{1,0:T(8,128)(2,1)S(1)}, f16[304,128]{1,0:T(8,128)(2,1)S(1)}, u32[]{:S(2)}, u32[]{:S(2)}) %collective-permute-start.10) | collective-permute-done | bytes 77856 | tf_op jit(solution)/shard_map/ppermute | solution.py:25
  43.7 0.8 %collective-permute-done.9 = f16[304,128]{1,0:T(8,128)(2,1)S(1)} collective-permute-done((f16[304,128]{1,0:T(8,128)(2,1)S(1)}, f16[304,128]{1,0:T(8,128)(2,1)S(1)}, u32[]{:S(2)}, u32[]{:S(2)}) %collective-permute-start.9) | collective-permute-done | bytes 77856 | tf_op jit(solution)/shard_map/ppermute | solution.py:25
  44.6 1.1 %collective-permute-start.13 = (f16[368,128]{1,0:T(8,128)(2,1)S(1)}, f16[368,128]{1,0:T(8,128)(2,1)S(1)}, u32[]{:S(2)}, u32[]{:S(2)}) collective-permute-start(f16[368,128]{1,0:T(8,128)(2,1)S(1)} %convert_element_type.85), channel_id=1, source_target_pairs={{0,24},{4,28},{8,16},{12,20},{16,8},{20,12},{24,0},{28,4},{1,25},{... | collective-permute-start | bytes 282632 | tf_op jit(solution)/shard_map/ppermute | solution.py:25
  46.3 1.3 %collective-permute-start.7 = (f16[304,128]{1,0:T(8,128)(2,1)S(1)}, f16[304,128]{1,0:T(8,128)(2,1)S(1)}, u32[]{:S(2)}, u32[]{:S(2)}) collective-permute-start(f16[304,128]{1,0:T(8,128)(2,1)S(1)} %convert_element_type.73), channel_id=1, source_target_pairs={{0,4},{4,0},{8,12},{12,8},{16,20},{20,16},{24,28},{28,24},{1,5},{5... | collective-permute-start | bytes 233480 | tf_op jit(solution)/shard_map/ppermute | solution.py:25
  47.6 3.1 %collective-permute-done.7 = f16[304,128]{1,0:T(8,128)(2,1)S(1)} collective-permute-done((f16[304,128]{1,0:T(8,128)(2,1)S(1)}, f16[304,128]{1,0:T(8,128)(2,1)S(1)}, u32[]{:S(2)}, u32[]{:S(2)}) %collective-permute-start.7) | collective-permute-done | bytes 77856 | tf_op jit(solution)/shard_map/ppermute | solution.py:25
  51.4 0.7 %merge.1 = (f32[304,128]{1,0:T(8,128)S(1)}, f32[256,128]{1,0:T(8,128)S(1)}) custom-call(s32[4]{0:T(128)S(1)} %pad_add_fusion.where_ref, f32[368,128]{1,0:T(8,128)S(1)} %merge_pair.7.refs_0_, f32[368,128]{1,0:T(8,128)S(1)} %convert_element_type.84.refs_1_, f32[368,128]{1,0:T(8,128)S(1)} %convert_element_type.82.refs_1_.refs_2_, ...), custom_call_target="tpu_custom_call" | custom-call | tf_op jit(solution)/shard_map/merge/pallas_call | solution.py:556
  52.2 2.0 %collective-permute-start.16 = (f16[1,304,128]{2,1,0:T(8,128)(2,1)S(1)}, f16[1,304,128]{2,1,0:T(8,128)(2,1)S(1)}, u32[]{:S(2)}, u32[]{:S(2)}) collective-permute-start(f16[1,304,128]{2,1,0:T(8,128)(2,1)S(1)} %get-tuple-element.40), channel_id=1, source_target_pairs={{0,24},{4,28},{8,16},{12,20},{16,8},{20,12},{24,0},{28,4},{1,25},{... | collective-permute-start | bytes 233480 | tf_op jit(solution)/shard_map/ppermute | solution.py:25
  54.7 1.9 %collective-permute-start.14 = (f16[1,304,128]{2,1,0:T(8,128)(2,1)S(1)}, f16[1,304,128]{2,1,0:T(8,128)(2,1)S(1)}, u32[]{:S(2)}, u32[]{:S(2)}) collective-permute-start(f16[1,304,128]{2,1,0:T(8,128)(2,1)S(1)} %get-tuple-element.40), channel_id=1, source_target_pairs={{0,8},{4,12},{8,0},{12,4},{16,24},{20,28},{24,16},{28,20},{1,9},{5... | collective-permute-start | bytes 233480 | tf_op jit(solution)/shard_map/ppermute | solution.py:25
  56.6 0.9 %collective-permute-start.17 = (f16[1,304,128]{2,1,0:T(8,128)(2,1)S(1)}, f16[1,304,128]{2,1,0:T(8,128)(2,1)S(1)}, u32[]{:S(2)}, u32[]{:S(2)}) collective-permute-start(f16[1,304,128]{2,1,0:T(8,128)(2,1)S(1)} %get-tuple-element.40), channel_id=1, source_target_pairs={{0,4},{4,0},{8,12},{12,8},{16,20},{20,16},{24,28},{28,24},{1,5},{5... | collective-permute-start | bytes 233480 | tf_op jit(solution)/shard_map/ppermute | solution.py:25
  57.5 0.9 %collective-permute-done.16 = f16[1,304,128]{2,1,0:T(8,128)(2,1)S(1)} collective-permute-done((f16[1,304,128]{2,1,0:T(8,128)(2,1)S(1)}, f16[1,304,128]{2,1,0:T(8,128)(2,1)S(1)}, u32[]{:S(2)}, u32[]{:S(2)}) %collective-permute-start.16) | collective-permute-done | bytes 77856 | tf_op jit(solution)/shard_map/ppermute | solution.py:25
  58.4 0.9 %collective-permute-start.20 = (f16[1,304,128]{2,1,0:T(8,128)(2,1)S(1)}, f16[1,304,128]{2,1,0:T(8,128)(2,1)S(1)}, u32[]{:S(2)}, u32[]{:S(2)}) collective-permute-start(f16[1,304,128]{2,1,0:T(8,128)(2,1)S(1)} %collective-permute-done.16), channel_id=1, source_target_pairs={{0,4},{4,0},{8,12},{12,8},{16,20},{20,16},{24,28},{28,24},{1,5},{5... | collective-permute-start | bytes 233480 | tf_op jit(solution)/shard_map/ppermute | solution.py:25
  59.3 0.9 %collective-permute-done.15 = f16[1,304,128]{2,1,0:T(8,128)(2,1)S(1)} collective-permute-done((f16[1,304,128]{2,1,0:T(8,128)(2,1)S(1)}, f16[1,304,128]{2,1,0:T(8,128)(2,1)S(1)}, u32[]{:S(2)}, u32[]{:S(2)}) %collective-permute-start.15) | collective-permute-done | bytes 77856 | tf_op jit(solution)/shard_map/ppermute | solution.py:25
  60.3 1.3 %collective-permute-start.19 = (f16[1,304,128]{2,1,0:T(8,128)(2,1)S(1)}, f16[1,304,128]{2,1,0:T(8,128)(2,1)S(1)}, u32[]{:S(2)}, u32[]{:S(2)}) collective-permute-start(f16[1,304,128]{2,1,0:T(8,128)(2,1)S(1)} %collective-permute-done.15), channel_id=1, source_target_pairs={{0,4},{4,0},{8,12},{12,8},{16,20},{20,16},{24,28},{28,24},{1,5},{5... | collective-permute-start | bytes 233480 | tf_op jit(solution)/shard_map/ppermute | solution.py:25
  61.6 0.8 %collective-permute-start.18 = (f16[1,304,128]{2,1,0:T(8,128)(2,1)S(1)}, f16[1,304,128]{2,1,0:T(8,128)(2,1)S(1)}, u32[]{:S(2)}, u32[]{:S(2)}) collective-permute-start(f16[1,304,128]{2,1,0:T(8,128)(2,1)S(1)} %collective-permute-done.14), channel_id=1, source_target_pairs={{0,4},{4,0},{8,12},{12,8},{16,20},{20,16},{24,28},{28,24},{1,5},{5... | collective-permute-start | bytes 233480 | tf_op jit(solution)/shard_map/ppermute | solution.py:25
  62.3 1.5 %embed.1 = f32[64,128]{1,0:T(8,128)} custom-call(s32[4]{0:T(128)S(1)} %pad_add_fusion.where_ref, f32[256,128]{1,0:T(8,128)S(1)} %get-tuple-element.35.sums_ref, f32[4,72,128]{2,1,0:T(8,128)S(1)} %join.1.refs_0_, f32[4,72,128]{2,1,0:T(8,128)S(1)} %collective-permute-done.6.refs_1_), custom_call_target="tpu_custom_call" | custom-call | tf_op jit(solution)/shard_map/embed/pallas_call | solution.py:700
  64.0 0.7 %collective-permute-done.19 = f16[1,304,128]{2,1,0:T(8,128)(2,1)S(1)} collective-permute-done((f16[1,304,128]{2,1,0:T(8,128)(2,1)S(1)}, f16[1,304,128]{2,1,0:T(8,128)(2,1)S(1)}, u32[]{:S(2)}, u32[]{:S(2)}) %collective-permute-start.19) | collective-permute-done | bytes 77856 | tf_op jit(solution)/shard_map/ppermute | solution.py:25
  64.7 1.3 %collective-permute-done.18 = f16[1,304,128]{2,1,0:T(8,128)(2,1)S(1)} collective-permute-done((f16[1,304,128]{2,1,0:T(8,128)(2,1)S(1)}, f16[1,304,128]{2,1,0:T(8,128)(2,1)S(1)}, u32[]{:S(2)}, u32[]{:S(2)}) %collective-permute-start.18) | collective-permute-done | bytes 77856 | tf_op jit(solution)/shard_map/ppermute | solution.py:25
  66.0 1.8 %spread.1 = (f32[2304,128]{1,0:T(8,128)}, f32[1,128]{1,0:T(1,128)}) custom-call(s32[4]{0:T(128)S(1)} %pad_add_fusion.where_ref, f32[1,304,128]{2,1,0:T(8,128)S(1)} %get-tuple-element.39.refs_0_, f32[1,304,128]{2,1,0:T(8,128)S(1)} %convert_element_type.90.refs_1_, f32[1,304,128]{2,1,0:T(8,128)S(1)} %convert_element_type.91.refs_2_, ...), custom_call_target="tpu_custom_call" | custom-call | tf_op jit(solution)/shard_map/spread/pallas_call | solution.py:604
  (67 shorter events, 5.7 us)
Async XLA Ops:
  1.8 11.6 %collective-permute-start = (bf16[48,3,256]{2,1,0:T(4,128)(2,1)S(1)}, bf16[48,3,256]{2,1,0:T(4,128)(2,1)S(1)}, u32[]{:S(2)}, u32[]{:S(2)}) collective-permute-start(bf16[48,3,256]{2,1,0:T(4,128)(2,1)S(1)} %get-tuple-element.42), channel_id=1, source_target_pairs={{0,4},{2,6},{4,8},{5,1},{6,10},{7,3},{8,12},{9,5},{10,14},{11,7},{... | collective-permute-start | bytes 221192 | tf_op jit(solution)/shard_map/ppermute | solution.py:639
  6.6 0.8 %copy-start = (f32[64,128]{1,0:T(8,128)S(1)}, f32[64,128]{1,0:T(8,128)}, u32[]{:S(2)}) copy-start(f32[64,128]{1,0:T(8,128)} %grad_ref.1) | copy-start | bytes 98308
  7.4 0.7 %copy-start.1 = (s32[24,64]{1,0:T(8,128)S(1)}, s32[24,64]{1,0:T(8,128)}, u32[]{:S(2)}) copy-start(s32[24,64]{1,0:T(8,128)} %lab_ref.1) | copy-start | bytes 18436
  8.1 0.7 copy-start.3
  8.9 7.1 %collective-permute-start.4 = (f32[1,72,128]{2,1,0:T(8,128)S(1)}, f32[1,72,128]{2,1,0:T(8,128)S(1)}, u32[]{:S(2)}, u32[]{:S(2)}) collective-permute-start(f32[1,72,128]{2,1,0:T(8,128)S(1)} %bitcast.16), channel_id=1, source_target_pairs={{0,24},{4,28},{8,16},{12,20},{16,8},{20,12},{24,0},{28,4},{1,25},{... | collective-permute-start | bytes 110600 | tf_op jit(solution)/shard_map/ppermute | solution.py:25
  12.6 4.9 %collective-permute-start.3 = (f32[1,72,128]{2,1,0:T(8,128)S(1)}, f32[1,72,128]{2,1,0:T(8,128)S(1)}, u32[]{:S(2)}, u32[]{:S(2)}) collective-permute-start(f32[1,72,128]{2,1,0:T(8,128)S(1)} %bitcast.17), channel_id=1, source_target_pairs={{0,16},{4,20},{8,24},{12,28},{16,0},{20,4},{24,8},{28,12},{1,17},{... | collective-permute-start | bytes 110600 | tf_op jit(solution)/shard_map/ppermute | solution.py:25
  12.6 4.9 %collective-permute-start.2 = (f32[1,72,128]{2,1,0:T(8,128)S(1)}, f32[1,72,128]{2,1,0:T(8,128)S(1)}, u32[]{:S(2)}, u32[]{:S(2)}) collective-permute-start(f32[1,72,128]{2,1,0:T(8,128)S(1)} %bitcast.18), channel_id=1, source_target_pairs={{0,8},{4,12},{8,0},{12,4},{16,24},{20,28},{24,16},{28,20},{1,9},{5... | collective-permute-start | bytes 110600 | tf_op jit(solution)/shard_map/ppermute | solution.py:25
  13.4 4.1 %collective-permute-start.1 = (bf16[48,3,256]{2,1,0:T(4,128)(2,1)S(1)}, bf16[48,3,256]{2,1,0:T(4,128)(2,1)S(1)}, u32[]{:S(2)}, u32[]{:S(2)}) collective-permute-start(bf16[48,3,256]{2,1,0:T(4,128)(2,1)S(1)} %collective-permute-done), channel_id=1, source_target_pairs={{0,1},{1,0},{2,3},{3,2},{4,5},{5,4},{6,7},{7,6},{8,9},{9,8},{10,11... | collective-permute-start | bytes 221192 | tf_op jit(solution)/shard_map/ppermute | solution.py:25
  13.5 4.1 %copy-start.5 = (bf16[3,3,256,256]{3,2,1,0:T(8,128)(2,1)S(1)}, bf16[3,3,256,256]{3,2,1,0:T(8,128)(2,1)}, u32[]{:S(2)}) copy-start(bf16[3,3,256,256]{3,2,1,0:T(8,128)(2,1)} %param.9) | copy-start | bytes 3538948
  13.5 4.1 %copy-start.7 = (f32[256]{0:T(256)S(1)}, f32[256]{0:T(256)}, u32[]{:S(2)}) copy-start(f32[256]{0:T(256)} %param.10) | copy-start | bytes 3076
  17.6 5.6 %copy-start.4 = (s32[32]{0:T(128)S(1)}, s32[32]{0:T(128)}, u32[]{:S(2)}) copy-start(s32[32]{0:T(128)} %param.14) | copy-start | bytes 388
  17.6 7.3 %copy-start.2 = (s32[24,64]{1,0:T(8,128)S(1)}, s32[24,64]{1,0:T(8,128)}, u32[]{:S(2)}) copy-start(s32[24,64]{1,0:T(8,128)} %lab_ref.1) | copy-start | bytes 18436
  17.6 7.3 %copy-start.6 = (bf16[3,3,256,128]{3,2,1,0:T(8,128)(2,1)S(1)}, bf16[3,3,256,128]{3,2,1,0:T(8,128)(2,1)}, u32[]{:S(2)}) copy-start(bf16[3,3,256,128]{3,2,1,0:T(8,128)(2,1)} %param.11) | copy-start | bytes 1769476
  17.6 7.3 %copy-start.8 = (f32[128]{0:T(128)S(1)}, f32[128]{0:T(128)}, u32[]{:S(2)}) copy-start(f32[128]{0:T(128)} %param.12) | copy-start | bytes 1540
  23.1 1.8 %collective-permute-start.5 = (bf16[12,64,256]{2,1,0:T(8,128)(2,1)S(1)}, bf16[12,64,256]{2,1,0:T(8,128)(2,1)S(1)}, u32[]{:S(2)}, u32[]{:S(2)}) collective-permute-start(bf16[12,64,256]{2,1,0:T(8,128)(2,1)S(1)} %get-tuple-element.22.refs_0_), channel_id=1, source_target_pairs={{0,1},{1,0},{2,3},{3,2},{4,5},{5,4},{6,7},{7,6},{8,9},{9,8},{10,11... | collective-permute-start | bytes 1179656 | tf_op jit(solution)/shard_map/ppermute | solution.py:25
  23.3 6.2 %collective-permute-start.6 = (f32[4,72,128]{2,1,0:T(8,128)S(1)}, f32[4,72,128]{2,1,0:T(8,128)S(1)}, u32[]{:S(2)}, u32[]{:S(2)}) collective-permute-start(f32[4,72,128]{2,1,0:T(8,128)S(1)} %join.1.refs_0_), channel_id=1, source_target_pairs={{0,4},{4,0},{8,12},{12,8},{16,20},{20,16},{24,28},{28,24},{1,5},{5... | collective-permute-start | bytes 442376 | tf_op jit(solution)/shard_map/ppermute | solution.py:25
  32.5 4.6 %collective-permute-start.8 = (f16[336,128]{1,0:T(8,128)(2,1)S(1)}, f16[336,128]{1,0:T(8,128)(2,1)S(1)}, u32[]{:S(2)}, u32[]{:S(2)}) collective-permute-start(f16[336,128]{1,0:T(8,128)(2,1)S(1)} %convert_element_type.75), channel_id=1, source_target_pairs={{0,4},{4,0},{8,12},{12,8},{16,20},{20,16},{24,28},{28,24},{1,5},{5... | collective-permute-start | bytes 258056 | tf_op jit(solution)/shard_map/ppermute | solution.py:25
  37.1 8.6 %collective-permute-start.11 = (f16[368,128]{1,0:T(8,128)(2,1)S(1)}, f16[368,128]{1,0:T(8,128)(2,1)S(1)}, u32[]{:S(2)}, u32[]{:S(2)}) collective-permute-start(f16[368,128]{1,0:T(8,128)(2,1)S(1)} %convert_element_type.81), channel_id=1, source_target_pairs={{0,16},{4,20},{8,24},{12,28},{16,0},{20,4},{24,8},{28,12},{1,17},{... | collective-permute-start | bytes 282632 | tf_op jit(solution)/shard_map/ppermute | solution.py:25
  39.2 4.5 %collective-permute-start.10 = (f16[304,128]{1,0:T(8,128)(2,1)S(1)}, f16[304,128]{1,0:T(8,128)(2,1)S(1)}, u32[]{:S(2)}, u32[]{:S(2)}) collective-permute-start(f16[304,128]{1,0:T(8,128)(2,1)S(1)} %convert_element_type.79), channel_id=1, source_target_pairs={{0,4},{4,0},{8,12},{12,8},{16,20},{20,16},{24,28},{28,24},{1,5},{5... | collective-permute-start | bytes 233480 | tf_op jit(solution)/shard_map/ppermute | solution.py:25
  39.7 4.8 %collective-permute-start.9 = (f16[304,128]{1,0:T(8,128)(2,1)S(1)}, f16[304,128]{1,0:T(8,128)(2,1)S(1)}, u32[]{:S(2)}, u32[]{:S(2)}) collective-permute-start(f16[304,128]{1,0:T(8,128)(2,1)S(1)} %convert_element_type.77), channel_id=1, source_target_pairs={{0,4},{4,0},{8,12},{12,8},{16,20},{20,16},{24,28},{28,24},{1,5},{5... | collective-permute-start | bytes 233480 | tf_op jit(solution)/shard_map/ppermute | solution.py:25
  44.6 6.5 %collective-permute-start.13 = (f16[368,128]{1,0:T(8,128)(2,1)S(1)}, f16[368,128]{1,0:T(8,128)(2,1)S(1)}, u32[]{:S(2)}, u32[]{:S(2)}) collective-permute-start(f16[368,128]{1,0:T(8,128)(2,1)S(1)} %convert_element_type.85), channel_id=1, source_target_pairs={{0,24},{4,28},{8,16},{12,20},{16,8},{20,12},{24,0},{28,4},{1,25},{... | collective-permute-start | bytes 282632 | tf_op jit(solution)/shard_map/ppermute | solution.py:25
  45.7 5.6 %collective-permute-start.12 = (f16[368,128]{1,0:T(8,128)(2,1)S(1)}, f16[368,128]{1,0:T(8,128)(2,1)S(1)}, u32[]{:S(2)}, u32[]{:S(2)}) collective-permute-start(f16[368,128]{1,0:T(8,128)(2,1)S(1)} %convert_element_type.83), channel_id=1, source_target_pairs={{0,8},{4,12},{8,0},{12,4},{16,24},{20,28},{24,16},{28,20},{1,9},{5... | collective-permute-start | bytes 282632 | tf_op jit(solution)/shard_map/ppermute | solution.py:25
  46.3 4.5 %collective-permute-start.7 = (f16[304,128]{1,0:T(8,128)(2,1)S(1)}, f16[304,128]{1,0:T(8,128)(2,1)S(1)}, u32[]{:S(2)}, u32[]{:S(2)}) collective-permute-start(f16[304,128]{1,0:T(8,128)(2,1)S(1)} %convert_element_type.73), channel_id=1, source_target_pairs={{0,4},{4,0},{8,12},{12,8},{16,20},{20,16},{24,28},{28,24},{1,5},{5... | collective-permute-start | bytes 233480 | tf_op jit(solution)/shard_map/ppermute | solution.py:25
  52.2 6.3 %collective-permute-start.16 = (f16[1,304,128]{2,1,0:T(8,128)(2,1)S(1)}, f16[1,304,128]{2,1,0:T(8,128)(2,1)S(1)}, u32[]{:S(2)}, u32[]{:S(2)}) collective-permute-start(f16[1,304,128]{2,1,0:T(8,128)(2,1)S(1)} %get-tuple-element.40), channel_id=1, source_target_pairs={{0,24},{4,28},{8,16},{12,20},{16,8},{20,12},{24,0},{28,4},{1,25},{... | collective-permute-start | bytes 233480 | tf_op jit(solution)/shard_map/ppermute | solution.py:25
  54.2 6.1 %collective-permute-start.15 = (f16[1,304,128]{2,1,0:T(8,128)(2,1)S(1)}, f16[1,304,128]{2,1,0:T(8,128)(2,1)S(1)}, u32[]{:S(2)}, u32[]{:S(2)}) collective-permute-start(f16[1,304,128]{2,1,0:T(8,128)(2,1)S(1)} %get-tuple-element.40), channel_id=1, source_target_pairs={{0,16},{4,20},{8,24},{12,28},{16,0},{20,4},{24,8},{28,12},{1,17},{... | collective-permute-start | bytes 233480 | tf_op jit(solution)/shard_map/ppermute | solution.py:25
  54.7 6.9 %collective-permute-start.14 = (f16[1,304,128]{2,1,0:T(8,128)(2,1)S(1)}, f16[1,304,128]{2,1,0:T(8,128)(2,1)S(1)}, u32[]{:S(2)}, u32[]{:S(2)}) collective-permute-start(f16[1,304,128]{2,1,0:T(8,128)(2,1)S(1)} %get-tuple-element.40), channel_id=1, source_target_pairs={{0,8},{4,12},{8,0},{12,4},{16,24},{20,28},{24,16},{28,20},{1,9},{5... | collective-permute-start | bytes 233480 | tf_op jit(solution)/shard_map/ppermute | solution.py:25
  56.6 7.3 %collective-permute-start.17 = (f16[1,304,128]{2,1,0:T(8,128)(2,1)S(1)}, f16[1,304,128]{2,1,0:T(8,128)(2,1)S(1)}, u32[]{:S(2)}, u32[]{:S(2)}) collective-permute-start(f16[1,304,128]{2,1,0:T(8,128)(2,1)S(1)} %get-tuple-element.40), channel_id=1, source_target_pairs={{0,4},{4,0},{8,12},{12,8},{16,20},{20,16},{24,28},{28,24},{1,5},{5... | collective-permute-start | bytes 233480 | tf_op jit(solution)/shard_map/ppermute | solution.py:25
  58.4 5.5 %collective-permute-start.20 = (f16[1,304,128]{2,1,0:T(8,128)(2,1)S(1)}, f16[1,304,128]{2,1,0:T(8,128)(2,1)S(1)}, u32[]{:S(2)}, u32[]{:S(2)}) collective-permute-start(f16[1,304,128]{2,1,0:T(8,128)(2,1)S(1)} %collective-permute-done.16), channel_id=1, source_target_pairs={{0,4},{4,0},{8,12},{12,8},{16,20},{20,16},{24,28},{28,24},{1,5},{5... | collective-permute-start | bytes 233480 | tf_op jit(solution)/shard_map/ppermute | solution.py:25
  60.3 4.4 %collective-permute-start.19 = (f16[1,304,128]{2,1,0:T(8,128)(2,1)S(1)}, f16[1,304,128]{2,1,0:T(8,128)(2,1)S(1)}, u32[]{:S(2)}, u32[]{:S(2)}) collective-permute-start(f16[1,304,128]{2,1,0:T(8,128)(2,1)S(1)} %collective-permute-done.15), channel_id=1, source_target_pairs={{0,4},{4,0},{8,12},{12,8},{16,20},{20,16},{24,28},{28,24},{1,5},{5... | collective-permute-start | bytes 233480 | tf_op jit(solution)/shard_map/ppermute | solution.py:25
  61.6 4.4 %collective-permute-start.18 = (f16[1,304,128]{2,1,0:T(8,128)(2,1)S(1)}, f16[1,304,128]{2,1,0:T(8,128)(2,1)S(1)}, u32[]{:S(2)}, u32[]{:S(2)}) collective-permute-start(f16[1,304,128]{2,1,0:T(8,128)(2,1)S(1)} %collective-permute-done.14), channel_id=1, source_target_pairs={{0,4},{4,0},{8,12},{12,8},{16,20},{20,16},{24,28},{28,24},{1,5},{5... | collective-permute-start | bytes 233480 | tf_op jit(solution)/shard_map/ppermute | solution.py:25

commit v5 on v4

--- a/solution.py
+++ b/solution.py
@@ -1,4 +1,5 @@
 import functools
+import math
 
 import jax
 import jax.numpy as jnp
@@ -13,6 +14,9 @@
 HBM = pl.BlockSpec(memory_space=pltpu.HBM)
 ANY = pl.BlockSpec(memory_space=pl.ANY)
 SIDE = 8
+WIDTH = 3
+PIECE = 4
+STEP = 4
 NOTE = 16
 
 
@@ -57,104 +61,101 @@
     return [(at + 1, size) for at, size in bit_groups(count // 2, 2, 2)]
 
 
-def window_kernel(where_ref, x_hbm, taps, rows_ref, wide, sems):
+def shares(pooled_rows):
+    first = pooled_rows * 2 // 3 // STEP * STEP
+    return first, pooled_rows - first
+
+
+def pick(half, pair):
+    return jnp.where(half == 0, pair[0], pair[1])
+
+
+def window_kernel(where_ref, x_hbm, w_hbm, taps, w_ref, rows_ref, wide, sems):
     rows, cols, chans = x_hbm.shape
     half_cols = cols // 2
-    total = taps.shape[0]
-    first = where_ref[0] * (total - 2) - 1
-    start = jnp.clip(first, 0, rows - total)
-    offset = first - start
-    steps = sems.shape[0]
-    cuts = [k * total // steps for k in range(steps + 1)]
-    copies = []
-    for k in range(steps):
-        at, size = cuts[k], cuts[k + 1] - cuts[k]
-        copies.append(
-            pltpu.make_async_copy(
-                x_hbm.at[pl.ds(start + at, size)], rows_ref.at[pl.ds(at, size)], sems.at[k]
-            )
+    half = where_ref[0]
+    first, second = shares(rows // 2)
+    counts = [-(-(2 * n + 1) // PIECE) for n in (first, second)]
+    pieces = pick(half, counts)
+    start = pick(half, (0, rows - counts[1] * PIECE))
+    shift = pick(half, (PIECE + 1, PIECE - (2 * first - 1 - (rows - counts[1] * PIECE))))
+
+    def piece(k):
+        at = pl.ds(k * PIECE, PIECE)
+        return pltpu.make_async_copy(
+            x_hbm.at[pl.ds(start + k * PIECE, PIECE)], rows_ref.at[at], sems.at[k]
         )
-        copies[k].start()
+
+    def begin(k, carry):
+        piece(k).start()
+        return carry
+
+    lax.fori_loop(0, pieces, begin, 0)
+    weights = pltpu.make_async_copy(w_hbm, w_ref, sems.at[sems.shape[0] - 1])
+    weights.start()
     lanes = chans // 128
     border = jnp.zeros((8, 128), F32)
     for t in range(wide.shape[0]):
         wide[t, 0:8] = border
         wide[t, cols + 8 : cols + 16] = border
 
-    def prepare(i, slot):
-        r = i + offset
-        inside = (r >= 0) & (r < total)
-        x = rows_ref[jnp.clip(r, 0, total - 1)].astype(F32)
-        x = jnp.where(inside, x, 0.0)
-        for t in range(lanes):
-            wide[slot * lanes + t, 8 : 8 + cols] = x[:, t * 128 : (t + 1) * 128]
-        for tap in range(4):
+    def prepare(k, carry):
+        piece(k).wait()
+        for slot in range(PIECE):
+            r = k * PIECE + slot
+            x = rows_ref[r].astype(F32)
             for t in range(lanes):
-                piece = wide[slot * lanes + t, pl.ds(7 + tap, half_cols, stride=2), :]
-                at = (tap * lanes + t) * 128
-                taps[i, :, at : at + 128] = piece.astype(BF16)
-
-    def prepare_two(k, carry):
-        prepare(2 * k, 0)
-        prepare(2 * k + 1, 1)
+                wide[slot * lanes + t, 8 : 8 + cols] = x[:, t * 128 : (t + 1) * 128]
+            for tap in range(4):
+                for t in range(lanes):
+                    part = wide[slot * lanes + t, pl.ds(7 + tap, half_cols, stride=2), :]
+                    at = (tap * lanes + t) * 128
+                    taps[r + shift, :, at : at + 128] = part.astype(BF16)
         return carry
 
-    done = 0
-    for k in range(steps):
-        copies[k].wait()
-        ready = (cuts[k + 1] - 1) // 2 if k + 1 < steps else total // 2
-        lax.fori_loop(done, ready, prepare_two, 0)
-        done = ready
-
-
-def windows(where, x):
+    lax.fori_loop(0, pieces, prepare, 0)
+    outside = pick(half, (PIECE, PIECE + 2 * second + 1))
+    taps[outside] = jnp.zeros(taps.shape[1:], BF16)
+    weights.wait()
+
+
+def windows(where, x, w):
     rows, cols, chans = x.shape
-    total = rows // 2 + 2
+    first, _ = shares(rows // 2)
+    most = -(-(2 * first + 1) // PIECE)
     return pl.pallas_call(
         window_kernel,
-        out_shape=jax.ShapeDtypeStruct((total, cols // 2, 4 * chans), BF16),
-        in_specs=[SMEM, HBM],
-        out_specs=VMEM,
+        out_shape=(
+            jax.ShapeDtypeStruct(((most + 2) * PIECE, cols // 2, 4 * chans), BF16),
+            jax.ShapeDtypeStruct(w.shape, BF16),
+        ),
+        in_specs=[SMEM, HBM, HBM],
+        out_specs=(VMEM, VMEM),
         scratch_shapes=[
-            pltpu.VMEM((total, cols, chans), BF16),
-            pltpu.VMEM((2 * (chans // 128), cols + 16, 128), F32),
-            pltpu.SemaphoreType.DMA((4,)),
+            pltpu.VMEM((most * PIECE, cols, chans), BF16),
+            pltpu.VMEM((PIECE * (chans // 128), cols + 16, 128), F32),
+            pltpu.SemaphoreType.DMA((most + 1,)),
         ],
-        compiler_params=params(12),
+        compiler_params=params(16),
         cost_estimate=pl.CostEstimate(flops=0, bytes_accessed=12 << 20, transcendentals=0),
         name="windows",
-    )(where, pltpu.with_memory_space_constraint(x, pltpu.HBM))
-
-
-def edge_part(where_ref, pairs, w_ref, bias, edge_ref, wide, acc):
-    rows, width, chans = pairs[0][0].shape
+    )(where, *(pltpu.with_memory_space_constraint(a, pltpu.HBM) for a in (x, w)))
+
+
+def edge_part(where_ref, pairs, w_ref, bias, edge_ref, acc):
+    rows = pairs[0].shape[0]
+    chans = w_ref.shape[1]
     lanes = chans // 128
-    for s, pair in enumerate(pairs):
-        for k, ref in enumerate(pair):
-            x = ref[...].astype(F32)
-            for t in range(lanes):
-                for r in range(rows):
-                    at = r * 8 + k * width
-                    wide[s * lanes + t, at : at + width] = x[r, :, t * 128 : (t + 1) * 128]
-    column = [
-        [
-            jnp.concatenate(
-                [wide[s * lanes + t, pl.ds(c, rows, stride=8), :] for t in range(lanes)], axis=-1
-            ).astype(BF16)
-            for c in range(2 * width)
-        ]
-        for s in range(2)
-    ]
+    depth = 3 * chans
     lhs = jnp.concatenate(
         [
-            jnp.concatenate(column[s][2 * j + phase : 2 * j + phase + 3], axis=-1)
+            pairs[s][:, (2 * j + phase) * chans : (2 * j + phase + 3) * chans]
             for s in range(2)
             for j in range(2)
             for phase in range(2)
         ],
         axis=0,
     )
-    depth = 3 * chans
     pad = rows + 16
     for dr in range(3):
         part = jnp.dot(lhs, w_ref[dr * depth : (dr + 1) * depth], preferred_element_type=F32)
@@ -187,111 +188,153 @@
             edge_ref[g, t] = (total * keep).astype(BF16).astype(F32)
 
 
-def conv_kernel(
-    where_ref, taps, w_ref, b_ref, left_ref, head_ref, tail_ref, right_ref, *refs, block
-):
-    out_ref, edge_ref, wide, acc = refs[-4:]
+def conv_kernel(where_ref, taps, w_ref, b_ref, got_ref, traded_ref, head_ref, tail_ref, *refs):
+    out_ref, edge_ref, acc = refs[-3:]
     half_cols, chans = taps.shape[1], taps.shape[2] // 4
-    out_rows = out_ref.shape[0]
+    half = where_ref[0]
+    first, second = shares(head_ref.shape[0] // 2)
     bias = b_ref[...]
 
     def step(k, carry):
-        r0 = k * 2 * block
+        r0 = PIECE + k * 2 * STEP
         total = None
         for phase in range(2):
             lhs = jnp.concatenate(
                 [
-                    taps[pl.ds(r0 + dr, 2 * block), :, phase * chans : (phase + 3) * chans]
+                    taps[pl.ds(r0 + dr, 2 * STEP), :, phase * chans : (phase + 3) * chans]
                     for dr in range(3)
                 ],
                 axis=-1,
-            ).reshape(2 * block * half_cols, 9 * chans)
+            ).reshape(2 * STEP * half_cols, 9 * chans)
             v = jnp.dot(lhs, w_ref[...], preferred_element_type=F32) + bias
-            h = (v * jax.nn.sigmoid(v)).reshape(block, 2, half_cols, chans)
+            h = (v * jax.nn.sigmoid(v)).reshape(STEP, 2, half_cols, chans)
             h = h[:, 0] + h[:, 1]
             total = h if total is None else total + h
-        out_ref[pl.ds(k * block, block)] = (total * 0.25).astype(BF16)
+        out_ref[pl.ds(k * STEP, STEP)] = (total * 0.25).astype(BF16)
         return carry
 
-    lax.fori_loop(0, out_rows // block, step, 0)
-    pairs = ((left_ref, head_ref), (tail_ref, right_ref))
-    edge_part(where_ref, pairs, w_ref, bias, edge_ref, wide, acc)
-
-
-def conv_pool(where, taps, w, b, left, head, tail, right, after):
-    total, half_cols, width = taps.shape
+    lax.fori_loop(0, pick(half, (first // STEP, second // STEP)), step, 0)
+    got, traded = got_ref[...], traded_ref[...]
+    left = jnp.concatenate([jnp.where(half == 0, got, traded), head_ref[...]], axis=-1)
+    right = jnp.concatenate([tail_ref[...], jnp.where(half == 0, traded, got)], axis=-1)
+    edge_part(where_ref, (left, right), w_ref, bias, edge_ref, acc)
+
+
+def conv_pool(where, taps, w, b, got, traded, head, tail, after):
+    _, half_cols, width = taps.shape
     chans, rows = width // 4, head.shape[0]
-    out_rows, lanes = (total - 2) // 2, chans // 128
-    block = next(k for k in (6, 4, 3, 2, 1) if out_rows % k == 0)
+    first, lanes = shares(rows // 2)[0], chans // 128
     return pl.pallas_call(
-        functools.partial(conv_kernel, block=block),
+        conv_kernel,
         out_shape=(
-            jax.ShapeDtypeStruct((out_rows, half_cols, chans), BF16),
+            jax.ShapeDtypeStruct((first, half_cols, chans), BF16),
             jax.ShapeDtypeStruct((4, lanes, rows // 2, 128), F32),
         ),
         in_specs=[SMEM] + [VMEM] * 7 + [ANY] * len(after),
         out_specs=(VMEM, VMEM),
-        scratch_shapes=[
-            pltpu.VMEM((2 * lanes, 8 * rows, 128), F32),
-            pltpu.VMEM((8 * lanes, rows + 16, 128), F32),
-        ],
+        scratch_shapes=[pltpu.VMEM((8 * lanes, rows + 16, 128), F32)],
         compiler_params=params(24),
         cost_estimate=pl.CostEstimate(
-            flops=8 * out_rows * half_cols * 9 * chans * chans,
+            flops=8 * first * half_cols * 9 * chans * chans,
             bytes_accessed=8 << 20,
             transcendentals=0,
         ),
         name="conv_pool",
-    )(where, taps, w, b, left, head, tail, right, *after)
-
-
-def side_kernel(grad_ref, slots_ref, labels_ref, out_ref):
-    owned, width = grad_ref.shape
+    )(where, taps, w, b, got, traded, head, tail, *after)
+
+
+def start_kernel(
+    where_ref, x_hbm, grad_hbm, labels_hbm, slots_hbm, side_ref, head_ref, tail_ref, send_ref,
+    labels_ref, slots_ref, left, right, wide, sems,
+):
+    owned, width = grad_hbm.shape
+    rows, cols, chans = x_hbm.shape
     entries = slots_ref.shape[1]
-    out_ref[:owned] = grad_ref[...]
+    reach = left.shape[1]
+    half = where_ref[0]
+    copies = [
+        pltpu.make_async_copy(labels_hbm, labels_ref, sems.at[0]),
+        pltpu.make_async_copy(grad_hbm, side_ref.at[0, pl.ds(0, owned)], sems.at[1]),
+        pltpu.make_async_copy(x_hbm.at[:, pl.ds(0, reach)], left, sems.at[2]),
+        pltpu.make_async_copy(x_hbm.at[:, pl.ds(cols - reach, reach)], right, sems.at[3]),
+        pltpu.make_async_copy(slots_hbm, slots_ref, sems.at[4]),
+    ]
+    for copy in copies:
+        copy.start()
     lane = lax.broadcasted_iota(jnp.int32, (1, width), 1)
+    copies[0].wait()
+    copies[4].wait()
+    ids = jnp.concatenate(
+        [slots_ref[...].astype(F32), jnp.zeros((1, width - entries), F32)], axis=1
+    )
     labels = labels_ref[...]
     counts = jnp.zeros((1, width), F32)
     for e in range(entries):
         hit = jnp.where(labels == e, 1.0, 0.0)
         hit = jnp.sum(jnp.sum(hit, axis=0, keepdims=True), axis=1, keepdims=True)
         counts = jnp.where(lane == e, hit, counts)
-    ids = jnp.concatenate(
-        [slots_ref[...].astype(F32), jnp.zeros((1, width - entries), F32)], axis=1
-    )
     row = lax.broadcasted_iota(jnp.int32, (SIDE, width), 0)
-    out_ref[owned:] = jnp.where(row == 0, ids, jnp.where(row == 1, counts, 0.0))
-
-
-def pack_side(grad, slots, labels):
+    side_ref[0, owned:] = jnp.where(row == 0, ids, jnp.where(row == 1, counts, 0.0))
+    lanes = chans // 128
+    copies[2].wait()
+    copies[3].wait()
+    for ref, out_ref, at, sent in ((left, head_ref, 0, 1), (right, tail_ref, reach - WIDTH, 0)):
+        x = ref[...].astype(F32).reshape(rows * reach, chans)
+        for t in range(lanes):
+            wide[t] = x[:, t * 128 : (t + 1) * 128]
+        for c in range(WIDTH):
+            for t in range(lanes):
+                part = wide[t, pl.ds(at + c, rows, stride=reach), :].astype(BF16)
+                place = (c * lanes + t) * 128
+                out_ref[:, place : place + 128] = part
+    send_ref[...] = jnp.where(half == 0, tail_ref[...], head_ref[...])
+    copies[1].wait()
+
+
+def start(where, x, grad, slots, labels):
     owned, width = grad.shape
+    rows, _, chans = x.shape
+    reach = 16
+    columns = jax.ShapeDtypeStruct((rows, WIDTH * chans), BF16)
+    fixed = [
+        pltpu.with_memory_space_constraint(a, pltpu.HBM)
+        for a in (x, grad, labels, slots.reshape(1, -1))
+    ]
     return pl.pallas_call(
-        side_kernel,
-        out_shape=jax.ShapeDtypeStruct((owned + SIDE, width), F32),
-        in_specs=[VMEM] * 3,
-        out_specs=VMEM,
+        start_kernel,
+        out_shape=(jax.ShapeDtypeStruct((1, owned + SIDE, width), F32),) + (columns,) * 3,
+        in_specs=[SMEM, HBM, HBM, HBM, HBM],
+        out_specs=(VMEM,) * 4,
+        scratch_shapes=[
+            pltpu.VMEM(labels.shape, jnp.int32),
+            pltpu.VMEM((1, slots.shape[0]), jnp.int32),
+            pltpu.VMEM((rows, reach, chans), BF16),
+            pltpu.VMEM((rows, reach, chans), BF16),
+            pltpu.VMEM((chans // 128, rows * reach, 128), F32),
+            pltpu.SemaphoreType.DMA((5,)),
+        ],
         compiler_params=params(),
-        name="pack_side",
-    )(grad, slots.reshape(1, -1), labels)
-
-
-def join_kernel(*refs):
+        name="start",
+    )(where, *fixed)
+
+
+def join_kernel(*refs, count):
     at = 0
-    for ref in refs[:-1]:
+    for ref in refs[:count]:
         refs[-1][at : at + ref.shape[0]] = ref[...]
         at += ref.shape[0]
 
 
-def join(parts):
+def join(parts, after):
     shape = (sum(p.shape[0] for p in parts),) + parts[0].shape[1:]
     return pl.pallas_call(
-        join_kernel,
+        functools.partial(join_kernel, count=len(parts)),
         out_shape=jax.ShapeDtypeStruct(shape, F32),
-        in_specs=[VMEM] * len(parts),
+        in_specs=[VMEM] * len(parts) + [ANY] * len(after),
         out_specs=VMEM,
         compiler_params=params(),
         name="join",
-    )(*parts)
+    )(*parts, *after)
 
 
 def scale_rows(block, note_rows, sums):
@@ -321,11 +364,12 @@
     return note[0:1] * down, down, jnp.exp2(note[2:3] - 12.0)
 
 
-def deep_kernel(where_ref, edge_ref, w_ref, b_ref, lab_ref, *refs, block, n_maps, entries):
-    map_refs = refs[: 2 * n_maps]
-    taps, member, slope, sums_ref, wide = refs[2 * n_maps :]
-    part, cols, chans = map_refs[0].shape
-    rows = 2 * n_maps * part
+def deep_kernel(
+    where_ref, own_ref, other_ref, edge_ref, w_ref, b_ref, lab_ref, taps, member, slope, sums_ref, wide,
+    *, block, entries
+):
+    _, cols, chans = own_ref.shape
+    rows = lab_ref.shape[0]
     lanes = chans // 128
     width = w_ref.shape[-1]
     half = where_ref[0]
@@ -347,13 +391,26 @@
                 at = (tap * lanes + t) * 128
                 taps[r + 1, :, at : at + 128] = piece.astype(BF16)
 
-    def prepare_rows(k, carry):
-        for q in range(n_maps):
-            prepare(map_refs[q], (half * n_maps + q) * part, k, 2 * q)
-            prepare(map_refs[n_maps + q], ((1 - half) * n_maps + q) * part, k, 2 * q + 1)
-        return carry
-
-    lax.fori_loop(0, part, prepare_rows, 0)
+    first, second = shares(rows)
+    times = math.gcd(first, second)
+
+    def prepare_all(even_ref, odd_ref):
+        def prepare_rows(k, carry):
+            for q in range(rows // times):
+                ref, base = (even_ref, 0) if q < first // times else (odd_ref, first)
+                prepare(ref, base, q * times - base + k, q)
+            return carry
+
+        lax.fori_loop(0, times, prepare_rows, 0)
+
+    @pl.when(half == 0)
+    def _():
+        prepare_all(own_ref, other_ref)
+
+    @pl.when(half != 0)
+    def _():
+        prepare_all(other_ref, own_ref)
+
     lab = jnp.transpose(lab_ref[...].astype(F32))
     lane = lax.broadcasted_iota(jnp.int32, (cols, 128), 1)
     want = jnp.where(lane < 3 * entries, lane % entries, -1).astype(F32)
@@ -378,30 +435,32 @@
 
 
 def deep_forward(where, own, other, edges, w, b, labels, entries):
-    part, cols, chans = own[0].shape
-    rows, width = 2 * len(own) * part, w.shape[-1]
+    _, cols, chans = own.shape
+    rows, width = labels.shape[0], w.shape[-1]
     block = next(k for k in (8, 4, 2, 1) if rows % k == 0)
+    first, second = shares(rows)
+    slots = rows // math.gcd(first, second)
     return pl.pallas_call(
-        functools.partial(deep_kernel, block=block, n_maps=len(own), entries=entries),
+        functools.partial(deep_kernel, block=block, entries=entries),
         out_shape=(
             jax.ShapeDtypeStruct((rows + 2, cols, 3 * chans), BF16),
             jax.ShapeDtypeStruct((rows, cols, 128), BF16),
             jax.ShapeDtypeStruct((rows * cols, width), F32),
             jax.ShapeDtypeStruct((entries, width), F32),
         ),
-        in_specs=[SMEM] + [VMEM] * (4 + 2 * len(own)),
+        in_specs=[SMEM] + [VMEM] * 6,
         out_specs=(VMEM,) * 4,
-        scratch_shapes=[pltpu.VMEM((2 * len(own) * (chans // 128), cols + 16, 128), F32)],
+        scratch_shapes=[pltpu.VMEM((slots * (chans // 128), cols + 16, 128), F32)],
         compiler_params=params(16),
         cost_estimate=pl.CostEstimate(
             flops=4 * rows * cols * 9 * chans * width, bytes_accessed=8 << 20, transcendentals=0
         ),
         name="deep_forward",
-    )(where, edges, w, b, labels, *own, *other)
+    )(where, own, other, edges, w, b, labels)
 
 
 def grad_kernel(
-    where_ref, taps, member, slope, sums_ref, slots_ref, *refs, n_parts, chunk, ways, with_sums
+    where_ref, taps, member, slope, sums_ref, *refs, n_parts, chunk, ways, with_sums
 ):
     part_refs = refs[:n_parts]
     out_refs = refs[n_parts : n_parts + ways]
@@ -409,9 +468,12 @@
     rows, cols, depth = member.shape[0], taps.shape[1], taps.shape[2]
     width = slope.shape[-1]
     me = where_ref[3]
-    entries = slots_ref.shape[0]
+    entries = sums_ref.shape[0]
     owned = part_refs[0].shape[1] - SIDE
-    ids = slots_ref[...]
+    own_ids = jnp.broadcast_to(part_refs[0][0, owned : owned + 1, :entries], (entries, entries))
+    across = lax.broadcasted_iota(jnp.int32, (entries, entries), 1)
+    down = lax.broadcasted_iota(jnp.int32, (entries, entries), 0)
+    ids = jnp.sum(jnp.where(across == down, own_ids, 0.0), axis=1, keepdims=True).astype(jnp.int32)
     total = jnp.zeros((entries, 1), F32)
     entry_grad = jnp.zeros((entries, width), F32)
     owner, inner = ids // owned, ids % owned
@@ -456,7 +518,7 @@
     out_refs[with_sums][heads * chunk + NOTE :] = sums * jnp.exp2(12.0 - power_sums)
 
 
-def deep_backward(where, forward, slots, parts, chunk, count, ways, with_sums):
+def deep_backward(where, forward, parts, chunk, count, ways, with_sums):
     taps, _, slope, sums = forward
     width, entries = slope.shape[-1], sums.shape[0]
     size = count // ways * chunk + NOTE
@@ -468,7 +530,7 @@
             jax.ShapeDtypeStruct((size + (entries if m == with_sums else 0), width), F32)
             for m in range(ways)
         ),
-        in_specs=[SMEM] + [VMEM] * (5 + len(parts)),
+        in_specs=[SMEM] + [VMEM] * (4 + len(parts)),
         out_specs=(VMEM,) * ways,
         scratch_shapes=[
             pltpu.VMEM(slope.shape, BF16),
@@ -479,7 +541,7 @@
             flops=4 * slope.shape[0] * 3 * taps.shape[2] * width, bytes_accessed=8 << 20, transcendentals=0
         ),
         name="deep_backward",
-    )(where, *forward, slots, *parts)
+    )(where, *forward, *parts)
 
 
 def pair_kernel(own_ref, got_ref, own_sums_ref, got_sums_ref, *refs, size, entries):
@@ -585,18 +647,28 @@
 
 
 def spread_kernel(where_ref, *refs, chunk, rows):
-    part_refs, weight_ref, bias_ref, place = refs[:-3], refs[-3], refs[-2], refs[-1]
+    part_refs, weight_hbm, bias_ref, place, sems = refs[:-4], refs[-4], refs[-3], refs[-2], refs[-1]
     me = where_ref[3]
+    whole = rows == place.shape[0]
+    copies = []
     for m, ref, k in relative(part_refs):
         bias, down, _ = read_note(ref[k], chunk)
         j = me ^ m
-        place[pl.ds(pl.multiple_of(j * chunk, 8), chunk)] = ref[k, :chunk] * down
+        at = pl.ds(pl.multiple_of(j * chunk, 8), chunk)
+        place[at] = ref[k, :chunk] * down
+        if whole:
+            copies.append(pltpu.make_async_copy(place.at[at], weight_hbm.at[at], sems.at[m]))
+            copies[-1].start()
 
         @pl.when(j == 0)
         def _():
             bias_ref[...] = bias
 
-    weight_ref[...] = place[:rows]
+    if not whole:
+        copies.append(pltpu.make_async_copy(place.at[pl.ds(0, rows)], weight_hbm, sems.at[0]))
+        copies[-1].start()
+    for copy in copies:
+        copy.wait()
 
 
 def spread(where, parts, chunk, count, rows):
@@ -605,8 +677,11 @@
         functools.partial(spread_kernel, chunk=chunk, rows=rows),
         out_shape=(jax.ShapeDtypeStruct((rows, width), F32), jax.ShapeDtypeStruct((1, width), F32)),
         in_specs=[SMEM] + [VMEM] * len(parts),
-        out_specs=(VMEM, VMEM),
-        scratch_shapes=[pltpu.VMEM((count * chunk, width), F32)],
+        out_specs=(HBM, VMEM),
+        scratch_shapes=[
+            pltpu.VMEM((count * chunk, width), F32),
+            pltpu.SemaphoreType.DMA((count,)),
+        ],
         compiler_params=params(),
         name="spread",
     )(where, *parts)
@@ -629,26 +704,22 @@
     conv_w = conv_weight.reshape(9 * channels, -1)
     conv_b = conv_bias.reshape(1, -1)
 
-    head, tail = section_input[:, :3], section_input[:, -3:]
+    side, head, tail, sent = start(where, section_input, embed_grad, slot_ids, labels)
     pairs = []
     for s in range(strip_count):
         for c in range(chan_count):
             to = s + 1 - 2 * (c & 1)
             if 0 <= to < strip_count:
                 pairs.append((s * chan_count + c, to * chan_count + c))
-    got = lax.ppermute(jnp.where(half == 0, tail, head), ("strip", "chan"), pairs)
+    got = lax.ppermute(sent, ("strip", "chan"), pairs)
+
+    shared = gather_groups(side, "strip", high_groups(strip_count))
+
+    taps, near_w = windows(where, section_input, conv_w)
+    got, joined = lax.optimization_barrier((got, join(shared, [taps])))
     traded = swap(got, "chan", 1)
-    left = jnp.where(half == 0, got, traded)
-    right = jnp.where(half == 0, traded, got)
-
-    shared = gather_groups(
-        pack_side(embed_grad, slot_ids, labels)[None], "strip", high_groups(strip_count)
-    )
-
-    taps = windows(where, section_input)
-    joined = join(shared)
     shared = [joined, swap(joined, "strip", 1)]
-    pooled, edges = conv_pool(where, taps, conv_w, conv_b, left, head, tail, right, [joined])
+    pooled, edges = conv_pool(where, taps, near_w, conv_b, got, traded, head, tail, [joined])
     other = swap(pooled, "chan", 1)
 
     chunk = -(-9 * channels // strip_count // 8) * 8
@@ -658,8 +729,8 @@
     with_sums = 2 * order[0] + 1
     forward = deep_forward(
         where,
-        [pooled],
-        [other],
+        pooled,
+        other,
         edges,
         deep_weight.reshape(9 * channels, width),
         deep_bias.reshape(1, width),
@@ -667,7 +738,7 @@
         entries,
     )
     send = deep_backward(
-        where, forward, slot_ids.reshape(entries, 1), shared, chunk, strip_count, 2 * pieces, with_sums
+        where, forward, shared, chunk, strip_count, 2 * pieces, with_sums
     )
     heads, held = strip_count // (2 * pieces), 2
     got = {k: swap(send[2 * k + 1].astype(F16), "strip", 1).astype(F32) for k in order}

time: 68.1 us -> 69.7 us (1.023)
  Pallas kernels: 19.6 us -> 23.6 us
  local copies, waits for them, and re-layouts: 2.23 us -> 0.01 us
  waiting for transfers between devices: 17.4 us -> 18.8 us
  other arithmetic: 1.62 us -> 0.39 us
    pallas_call x5, Pallas kernels: 12.6 us -> 16.2 us  [the longest x1 7.07 us: conv_pool(): pl.pallas_call(conv_kernel, out_shape=(jax.ShapeDtypeStruct((first, half_...]
    unnamed x18 -> x8, local copies, waits for them, and re-layouts: 2.15 us -> 0.01 us
    ppermute x20, waiting for transfers between devices: 17.4 us -> 18.8 us  [swap(): return lax.ppermute(value, axis, [(i, i ^ mask) for i in range(count)])]
    slice x1 -> x0, other arithmetic: 1.15 us -> none  [body(): head, tail = (section_input[:, :3], section_input[:, -3:])]
  transfers between devices with their start and end apart: 21 -> 21, of which waited for: 13 -> 13; matrix products, arithmetic and copies ran while one was open for 1% -> 0% of each run, Pallas kernels for 13% -> 13%
where the time goes in v5:
time: 69.7 us; the launch traced here: 69.4 us
  starting transfers between devices  25.7 us (37%)
  Pallas kernels  23.6 us (34%)
  waiting for transfers between devices  18.8 us (27%)
  between operations  0.93 us (1%)
    ppermute x20, starting transfers between devices, swap(): return lax.ppermute(value, axis, [(i, i ^ mask) for i in range(count)])  20.9 us
    ppermute x20, waiting for transfers between devices, swap(): return lax.ppermute(value, axis, [(i, i ^ mask) for i in range(count)])  18.8 us
    pallas_call x1, Pallas kernels, conv_pool(): pl.pallas_call(conv_kernel, out_shape=(jax.ShapeDtypeStruct((first, half_...  7.07 us
    ppermute x1, starting transfers between devices, body(): got = lax.ppermute(sent, ('strip', 'chan'), pairs)  4.85 us
    pallas_call x1, Pallas kernels, deep_forward(): pl.pallas_call(functools.partial(deep_kernel, block=block, entries=entrie...  4.38 us
    pallas_call x1, Pallas kernels, deep_backward(): pl.pallas_call(functools.partial(grad_kernel, n_parts=len(parts), chunk=c...  2.91 us
    pallas_call x1, Pallas kernels, windows(): pl.pallas_call(window_kernel, out_shape=(jax.ShapeDtypeStruct(((most + 2)...  2.8 us
    pallas_call x1, Pallas kernels, spread(): pl.pallas_call(functools.partial(spread_kernel, chunk=chunk, rows=rows),...  2.14 us
  transfers between devices with their start and end apart: 21, of which 13 were waited for; matrix products, arithmetic and copies ran while one was open for 0% of the time, Pallas kernels for 13%

profile of v5, /device:TPU:0, one launch (start us, length us, event | category | flops | bytes accessed | tf_op | source)
XLA Modules:
  0.0 69.4 jit_solution(15236004758289668539)
XLA Ops:
  0.7 1.9 %start.1 = (f32[1,72,128]{2,1,0:T(8,128)S(1)}, bf16[48,768]{1,0:T(8,128)(2,1)S(1)}, bf16[48,768]{1,0:T(8,128)(2,1)S(1)}, bf16[48,768]{1,0:T(8,128)(2,1)S(1)}) custom-call(s32[4]{0:T(128)S(1)} %pad_add_fusion.where_ref, bf16[48,128,256]{2,1,0:T(8,128)(2,1)} %x_hbm.3, f32[64,128]{1,0:T(8,128)} %grad_hbm.1, s32[24,64]{1,0:T(8,128)} %lab_ref.1, s32[1,32]{1,0:T(1,128)} %bitcast.18), custom_call_target="tpu_custom_call" | custom-call | tf_op jit(solution)/shard_map/start/pallas_call | solution.py:303
  2.7 4.8 %collective-permute-start = (bf16[48,768]{1,0:T(8,128)(2,1)S(1)}, bf16[48,768]{1,0:T(8,128)(2,1)S(1)}, u32[]{:S(2)}, u32[]{:S(2)}) collective-permute-start(bf16[48,768]{1,0:T(8,128)(2,1)S(1)} %get-tuple-element.31), channel_id=1, source_target_pairs={{0,4},{2,6},{4,8},{5,1},{6,10},{7,3},{8,12},{9,5},{10,14},{11,7},{... | collective-permute-start | bytes 221192 | tf_op jit(solution)/shard_map/ppermute | solution.py:714
  7.5 3.7 %collective-permute-start.3 = (f32[1,72,128]{2,1,0:T(8,128)S(1)}, f32[1,72,128]{2,1,0:T(8,128)S(1)}, u32[]{:S(2)}, u32[]{:S(2)}) collective-permute-start(f32[1,72,128]{2,1,0:T(8,128)S(1)} %get-tuple-element.32.refs_0_), channel_id=1, source_target_pairs={{0,24},{4,28},{8,16},{12,20},{16,8},{20,12},{24,0},{28,4},{1,25},{... | collective-permute-start | bytes 110600 | tf_op jit(solution)/shard_map/ppermute | solution.py:29
  11.2 0.8 %collective-permute-start.1 = (f32[1,72,128]{2,1,0:T(8,128)S(1)}, f32[1,72,128]{2,1,0:T(8,128)S(1)}, u32[]{:S(2)}, u32[]{:S(2)}) collective-permute-start(f32[1,72,128]{2,1,0:T(8,128)S(1)} %get-tuple-element.32.refs_0_), channel_id=1, source_target_pairs={{0,8},{4,12},{8,0},{12,4},{16,24},{20,28},{24,16},{28,20},{1,9},{5... | collective-permute-start | bytes 110600 | tf_op jit(solution)/shard_map/ppermute | solution.py:29
  12.0 2.8 %windows.1 = (bf16[44,64,1024]{2,1,0:T(8,128)(2,1)S(1)}, bf16[2304,256]{1,0:T(8,128)(2,1)S(1)}) custom-call(s32[4]{0:T(128)S(1)} %pad_add_fusion.where_ref, bf16[48,128,256]{2,1,0:T(8,128)(2,1)} %x_hbm.3, bf16[2304,256]{1,0:T(8,128)(2,1)} %bitcast.17), custom_call_target="tpu_custom_call" | custom-call | bytes 12582912 | tf_op jit(solution)/shard_map/windows/pallas_call | solution.py:126
  14.8 1.3 %collective-permute-done.2.refs_2_ = f32[1,72,128]{2,1,0:T(8,128)S(1)} collective-permute-done((f32[1,72,128]{2,1,0:T(8,128)S(1)}, f32[1,72,128]{2,1,0:T(8,128)S(1)}, u32[]{:S(2)}, u32[]{:S(2)}) %collective-permute-start.2) | collective-permute-done | bytes 36896 | tf_op jit(solution)/shard_map/ppermute | solution.py:29
  16.1 1.3 %collective-permute-done.4.traded_ref = bf16[48,768]{1,0:T(8,128)(2,1)S(1)} collective-permute-done((bf16[48,768]{1,0:T(8,128)(2,1)S(1)}, bf16[48,768]{1,0:T(8,128)(2,1)S(1)}, u32[]{:S(2)}, u32[]{:S(2)}) %collective-permute-start.4) | collective-permute-done | bytes 73760 | tf_op jit(solution)/shard_map/ppermute | solution.py:29
  17.4 7.1 %conv_pool.1 = (bf16[16,64,256]{2,1,0:T(8,128)(2,1)S(1)}, f32[4,2,24,128]{3,2,1,0:T(8,128)S(1)}) custom-call(s32[4]{0:T(128)S(1)} %pad_add_fusion.where_ref, bf16[44,64,1024]{2,1,0:T(8,128)(2,1)S(1)} %get-tuple-element.29.refs_4_.taps, bf16[2304,256]{1,0:T(8,128)(2,1)S(1)} %get-tuple-element.30.w_ref, f32[1,256]{1,0:T(1,128)S(1)} %bitcast.15, ...), custom_call_target="tpu_custom_call" | custom-call | flops 4831838208 | bytes 8388608 | tf_op jit(solution)/shard_map/conv_pool/pallas_call | solution.py:227
  25.0 1.5 %collective-permute-done.5.other_ref = bf16[16,64,256]{2,1,0:T(8,128)(2,1)S(1)} collective-permute-done((bf16[16,64,256]{2,1,0:T(8,128)(2,1)S(1)}, bf16[16,64,256]{2,1,0:T(8,128)(2,1)S(1)}, u32[]{:S(2)}, u32[]{:S(2)}) %collective-permute-start.5) | collective-permute-done | bytes 524320 | tf_op jit(solution)/shard_map/ppermute | solution.py:29
  26.5 4.4 %deep_forward.1 = (bf16[26,64,768]{2,1,0:T(8,128)(2,1)S(1)}, bf16[24,64,128]{2,1,0:T(8,128)(2,1)S(1)}, f32[1536,128]{1,0:T(8,128)S(1)}, f32[32,128]{1,0:T(8,128)S(1)}) custom-call(s32[4]{0:T(128)S(1)} %pad_add_fusion.where_ref, bf16[16,64,256]{2,1,0:T(8,128)(2,1)S(1)} %get-tuple-element.37.own_ref, ...), custom_call_target="tpu_custom_call" | custom-call | flops 1811939328 | bytes 8388608 | tf_op jit(solution)/shard_map/deep_forward/pallas_call | solution.py:443
  30.9 2.9 %deep_backward.1 = (f32[304,128]{1,0:T(8,128)S(1)}, f32[304,128]{1,0:T(8,128)S(1)}, f32[304,128]{1,0:T(8,128)S(1)}, f32[304,128]{1,0:T(8,128)S(1)}, f32[304,128]...) custom-call(s32[4]{0:T(128)S(1)} %pad_add_fusion.where_ref, ...), custom_call_target="tpu_custom_call" | custom-call | flops 1811939328 | bytes 8388608 | tf_op jit(solution)/shard_map/deep_backward/pallas_call | solution.py:525
  34.2 4.2 %collective-permute-done.8 = f16[336,128]{1,0:T(8,128)(2,1)S(1)} collective-permute-done((f16[336,128]{1,0:T(8,128)(2,1)S(1)}, f16[336,128]{1,0:T(8,128)(2,1)S(1)}, u32[]{:S(2)}, u32[]{:S(2)}) %collective-permute-start.8) | collective-permute-done | bytes 86048 | tf_op jit(solution)/shard_map/ppermute | solution.py:29
  38.5 2.1 %collective-permute-start.11 = (f16[368,128]{1,0:T(8,128)(2,1)S(1)}, f16[368,128]{1,0:T(8,128)(2,1)S(1)}, u32[]{:S(2)}, u32[]{:S(2)}) collective-permute-start(f16[368,128]{1,0:T(8,128)(2,1)S(1)} %convert_element_type.81), channel_id=1, source_target_pairs={{0,16},{4,20},{8,24},{12,28},{16,0},{20,4},{24,8},{28,12},{1,17},{... | collective-permute-start | bytes 282632 | tf_op jit(solution)/shard_map/ppermute | solution.py:29
  41.0 1.8 %collective-permute-start.9 = (f16[304,128]{1,0:T(8,128)(2,1)S(1)}, f16[304,128]{1,0:T(8,128)(2,1)S(1)}, u32[]{:S(2)}, u32[]{:S(2)}) collective-permute-start(f16[304,128]{1,0:T(8,128)(2,1)S(1)} %convert_element_type.77), channel_id=1, source_target_pairs={{0,4},{4,0},{8,12},{12,8},{16,20},{20,16},{24,28},{28,24},{1,5},{5... | collective-permute-start | bytes 233480 | tf_op jit(solution)/shard_map/ppermute | solution.py:29
  42.8 2.3 %collective-permute-done.10 = f16[304,128]{1,0:T(8,128)(2,1)S(1)} collective-permute-done((f16[304,128]{1,0:T(8,128)(2,1)S(1)}, f16[304,128]{1,0:T(8,128)(2,1)S(1)}, u32[]{:S(2)}, u32[]{:S(2)}) %collective-permute-start.10) | collective-permute-done | bytes 77856 | tf_op jit(solution)/shard_map/ppermute | solution.py:29
  45.1 0.8 %collective-permute-done.9 = f16[304,128]{1,0:T(8,128)(2,1)S(1)} collective-permute-done((f16[304,128]{1,0:T(8,128)(2,1)S(1)}, f16[304,128]{1,0:T(8,128)(2,1)S(1)}, u32[]{:S(2)}, u32[]{:S(2)}) %collective-permute-start.9) | collective-permute-done | bytes 77856 | tf_op jit(solution)/shard_map/ppermute | solution.py:29
  46.0 1.1 %collective-permute-start.13 = (f16[368,128]{1,0:T(8,128)(2,1)S(1)}, f16[368,128]{1,0:T(8,128)(2,1)S(1)}, u32[]{:S(2)}, u32[]{:S(2)}) collective-permute-start(f16[368,128]{1,0:T(8,128)(2,1)S(1)} %convert_element_type.85), channel_id=1, source_target_pairs={{0,24},{4,28},{8,16},{12,20},{16,8},{20,12},{24,0},{28,4},{1,25},{... | collective-permute-start | bytes 282632 | tf_op jit(solution)/shard_map/ppermute | solution.py:29
  47.7 1.3 %collective-permute-start.7 = (f16[304,128]{1,0:T(8,128)(2,1)S(1)}, f16[304,128]{1,0:T(8,128)(2,1)S(1)}, u32[]{:S(2)}, u32[]{:S(2)}) collective-permute-start(f16[304,128]{1,0:T(8,128)(2,1)S(1)} %convert_element_type.73), channel_id=1, source_target_pairs={{0,4},{4,0},{8,12},{12,8},{16,20},{20,16},{24,28},{28,24},{1,5},{5... | collective-permute-start | bytes 233480 | tf_op jit(solution)/shard_map/ppermute | solution.py:29
  49.0 3.1 %collective-permute-done.7 = f16[304,128]{1,0:T(8,128)(2,1)S(1)} collective-permute-done((f16[304,128]{1,0:T(8,128)(2,1)S(1)}, f16[304,128]{1,0:T(8,128)(2,1)S(1)}, u32[]{:S(2)}, u32[]{:S(2)}) %collective-permute-start.7) | collective-permute-done | bytes 77856 | tf_op jit(solution)/shard_map/ppermute | solution.py:29
  52.8 0.7 %merge.1 = (f32[304,128]{1,0:T(8,128)S(1)}, f32[256,128]{1,0:T(8,128)S(1)}) custom-call(s32[4]{0:T(128)S(1)} %pad_add_fusion.where_ref, f32[368,128]{1,0:T(8,128)S(1)} %merge_pair.7.refs_0_, f32[368,128]{1,0:T(8,128)S(1)} %convert_element_type.84.refs_1_, f32[368,128]{1,0:T(8,128)S(1)} %convert_element_type.82.refs_1_.refs_2_, ...), custom_call_target="tpu_custom_call" | custom-call | tf_op jit(solution)/shard_map/merge/pallas_call | solution.py:618
  53.6 1.9 %collective-permute-start.16 = (f16[1,304,128]{2,1,0:T(8,128)(2,1)S(1)}, f16[1,304,128]{2,1,0:T(8,128)(2,1)S(1)}, u32[]{:S(2)}, u32[]{:S(2)}) collective-permute-start(f16[1,304,128]{2,1,0:T(8,128)(2,1)S(1)} %get-tuple-element.56), channel_id=1, source_target_pairs={{0,24},{4,28},{8,16},{12,20},{16,8},{20,12},{24,0},{28,4},{1,25},{... | collective-permute-start | bytes 233480 | tf_op jit(solution)/shard_map/ppermute | solution.py:29
  56.1 1.9 %collective-permute-start.14 = (f16[1,304,128]{2,1,0:T(8,128)(2,1)S(1)}, f16[1,304,128]{2,1,0:T(8,128)(2,1)S(1)}, u32[]{:S(2)}, u32[]{:S(2)}) collective-permute-start(f16[1,304,128]{2,1,0:T(8,128)(2,1)S(1)} %get-tuple-element.56), channel_id=1, source_target_pairs={{0,8},{4,12},{8,0},{12,4},{16,24},{20,28},{24,16},{28,20},{1,9},{5... | collective-permute-start | bytes 233480 | tf_op jit(solution)/shard_map/ppermute | solution.py:29
  58.0 0.9 %collective-permute-start.17 = (f16[1,304,128]{2,1,0:T(8,128)(2,1)S(1)}, f16[1,304,128]{2,1,0:T(8,128)(2,1)S(1)}, u32[]{:S(2)}, u32[]{:S(2)}) collective-permute-start(f16[1,304,128]{2,1,0:T(8,128)(2,1)S(1)} %get-tuple-element.56), channel_id=1, source_target_pairs={{0,4},{4,0},{8,12},{12,8},{16,20},{20,16},{24,28},{28,24},{1,5},{5... | collective-permute-start | bytes 233480 | tf_op jit(solution)/shard_map/ppermute | solution.py:29
  59.0 0.9 %collective-permute-done.16 = f16[1,304,128]{2,1,0:T(8,128)(2,1)S(1)} collective-permute-done((f16[1,304,128]{2,1,0:T(8,128)(2,1)S(1)}, f16[1,304,128]{2,1,0:T(8,128)(2,1)S(1)}, u32[]{:S(2)}, u32[]{:S(2)}) %collective-permute-start.16) | collective-permute-done | bytes 77856 | tf_op jit(solution)/shard_map/ppermute | solution.py:29
  59.9 0.9 %collective-permute-start.20 = (f16[1,304,128]{2,1,0:T(8,128)(2,1)S(1)}, f16[1,304,128]{2,1,0:T(8,128)(2,1)S(1)}, u32[]{:S(2)}, u32[]{:S(2)}) collective-permute-start(f16[1,304,128]{2,1,0:T(8,128)(2,1)S(1)} %collective-permute-done.16), channel_id=1, source_target_pairs={{0,4},{4,0},{8,12},{12,8},{16,20},{20,16},{24,28},{28,24},{1,5},{5... | collective-permute-start | bytes 233480 | tf_op jit(solution)/shard_map/ppermute | solution.py:29
  60.8 0.8 %collective-permute-done.15 = f16[1,304,128]{2,1,0:T(8,128)(2,1)S(1)} collective-permute-done((f16[1,304,128]{2,1,0:T(8,128)(2,1)S(1)}, f16[1,304,128]{2,1,0:T(8,128)(2,1)S(1)}, u32[]{:S(2)}, u32[]{:S(2)}) %collective-permute-start.15) | collective-permute-done | bytes 77856 | tf_op jit(solution)/shard_map/ppermute | solution.py:29
  61.6 1.3 %collective-permute-start.19 = (f16[1,304,128]{2,1,0:T(8,128)(2,1)S(1)}, f16[1,304,128]{2,1,0:T(8,128)(2,1)S(1)}, u32[]{:S(2)}, u32[]{:S(2)}) collective-permute-start(f16[1,304,128]{2,1,0:T(8,128)(2,1)S(1)} %collective-permute-done.15), channel_id=1, source_target_pairs={{0,4},{4,0},{8,12},{12,8},{16,20},{20,16},{24,28},{28,24},{1,5},{5... | collective-permute-start | bytes 233480 | tf_op jit(solution)/shard_map/ppermute | solution.py:29
  62.9 0.8 %collective-permute-start.18 = (f16[1,304,128]{2,1,0:T(8,128)(2,1)S(1)}, f16[1,304,128]{2,1,0:T(8,128)(2,1)S(1)}, u32[]{:S(2)}, u32[]{:S(2)}) collective-permute-start(f16[1,304,128]{2,1,0:T(8,128)(2,1)S(1)} %collective-permute-done.14), channel_id=1, source_target_pairs={{0,4},{4,0},{8,12},{12,8},{16,20},{20,16},{24,28},{28,24},{1,5},{5... | collective-permute-start | bytes 233480 | tf_op jit(solution)/shard_map/ppermute | solution.py:29
  63.6 1.5 %embed.1 = f32[64,128]{1,0:T(8,128)} custom-call(s32[4]{0:T(128)S(1)} %pad_add_fusion.where_ref, f32[256,128]{1,0:T(8,128)S(1)} %get-tuple-element.51.sums_ref, f32[4,72,128]{2,1,0:T(8,128)S(1)} %join.1.refs_0_, f32[4,72,128]{2,1,0:T(8,128)S(1)} %collective-permute-done.6.refs_1_), custom_call_target="tpu_custom_call" | custom-call | tf_op jit(solution)/shard_map/embed/pallas_call | solution.py:771
  65.3 0.7 %collective-permute-done.19 = f16[1,304,128]{2,1,0:T(8,128)(2,1)S(1)} collective-permute-done((f16[1,304,128]{2,1,0:T(8,128)(2,1)S(1)}, f16[1,304,128]{2,1,0:T(8,128)(2,1)S(1)}, u32[]{:S(2)}, u32[]{:S(2)}) %collective-permute-start.19) | collective-permute-done | bytes 77856 | tf_op jit(solution)/shard_map/ppermute | solution.py:29
  66.0 1.3 %collective-permute-done.18 = f16[1,304,128]{2,1,0:T(8,128)(2,1)S(1)} collective-permute-done((f16[1,304,128]{2,1,0:T(8,128)(2,1)S(1)}, f16[1,304,128]{2,1,0:T(8,128)(2,1)S(1)}, u32[]{:S(2)}, u32[]{:S(2)}) %collective-permute-start.18) | collective-permute-done | bytes 77856 | tf_op jit(solution)/shard_map/ppermute | solution.py:29
  67.3 2.1 %spread.1 = (f32[2304,128]{1,0:T(8,128)}, f32[1,128]{1,0:T(1,128)}) custom-call(s32[4]{0:T(128)S(1)} %pad_add_fusion.where_ref, f32[1,304,128]{2,1,0:T(8,128)S(1)} %get-tuple-element.55.refs_0_, f32[1,304,128]{2,1,0:T(8,128)S(1)} %convert_element_type.90.refs_1_, f32[1,304,128]{2,1,0:T(8,128)S(1)} %convert_element_type.91.refs_2_, ...), custom_call_target="tpu_custom_call" | custom-call | tf_op jit(solution)/shard_map/spread/pallas_call | solution.py:676
  (54 shorter events, 3.6 us)
Async XLA Ops:
  2.7 13.4 %collective-permute-start = (bf16[48,768]{1,0:T(8,128)(2,1)S(1)}, bf16[48,768]{1,0:T(8,128)(2,1)S(1)}, u32[]{:S(2)}, u32[]{:S(2)}) collective-permute-start(bf16[48,768]{1,0:T(8,128)(2,1)S(1)} %get-tuple-element.31), channel_id=1, source_target_pairs={{0,4},{2,6},{4,8},{5,1},{6,10},{7,3},{8,12},{9,5},{10,14},{11,7},{... | collective-permute-start | bytes 221192 | tf_op jit(solution)/shard_map/ppermute | solution.py:714
  7.5 7.3 %collective-permute-start.3 = (f32[1,72,128]{2,1,0:T(8,128)S(1)}, f32[1,72,128]{2,1,0:T(8,128)S(1)}, u32[]{:S(2)}, u32[]{:S(2)}) collective-permute-start(f32[1,72,128]{2,1,0:T(8,128)S(1)} %get-tuple-element.32.refs_0_), channel_id=1, source_target_pairs={{0,24},{4,28},{8,16},{12,20},{16,8},{20,12},{24,0},{28,4},{1,25},{... | collective-permute-start | bytes 110600 | tf_op jit(solution)/shard_map/ppermute | solution.py:29
  11.2 4.9 %collective-permute-start.2 = (f32[1,72,128]{2,1,0:T(8,128)S(1)}, f32[1,72,128]{2,1,0:T(8,128)S(1)}, u32[]{:S(2)}, u32[]{:S(2)}) collective-permute-start(f32[1,72,128]{2,1,0:T(8,128)S(1)} %get-tuple-element.32.refs_0_), channel_id=1, source_target_pairs={{0,16},{4,20},{8,24},{12,28},{16,0},{20,4},{24,8},{28,12},{1,17},{... | collective-permute-start | bytes 110600 | tf_op jit(solution)/shard_map/ppermute | solution.py:29
  11.2 4.9 %collective-permute-start.1 = (f32[1,72,128]{2,1,0:T(8,128)S(1)}, f32[1,72,128]{2,1,0:T(8,128)S(1)}, u32[]{:S(2)}, u32[]{:S(2)}) collective-permute-start(f32[1,72,128]{2,1,0:T(8,128)S(1)} %get-tuple-element.32.refs_0_), channel_id=1, source_target_pairs={{0,8},{4,12},{8,0},{12,4},{16,24},{20,28},{24,16},{28,20},{1,9},{5... | collective-permute-start | bytes 110600 | tf_op jit(solution)/shard_map/ppermute | solution.py:29
  16.0 1.4 %copy-start.2 = (f32[256]{0:T(256)S(1)}, f32[256]{0:T(256)}, u32[]{:S(2)}) copy-start(f32[256]{0:T(256)} %param.10) | copy-start | bytes 3076
  16.1 1.3 %collective-permute-start.4 = (bf16[48,768]{1,0:T(8,128)(2,1)S(1)}, bf16[48,768]{1,0:T(8,128)(2,1)S(1)}, u32[]{:S(2)}, u32[]{:S(2)}) collective-permute-start(bf16[48,768]{1,0:T(8,128)(2,1)S(1)} %collective-permute-done.got_ref), channel_id=1, source_target_pairs={{0,1},{1,0},{2,3},{3,2},{4,5},{5,4},{6,7},{7,6},{8,9},{9,8},{10,11... | collective-permute-start | bytes 221192 | tf_op jit(solution)/shard_map/ppermute | solution.py:29
  17.4 9.1 %copy-start = (s32[24,64]{1,0:T(8,128)S(1)}, s32[24,64]{1,0:T(8,128)}, u32[]{:S(2)}) copy-start(s32[24,64]{1,0:T(8,128)} %lab_ref.1) | copy-start | bytes 18436
  17.4 9.1 %copy-start.1 = (bf16[3,3,256,128]{3,2,1,0:T(8,128)(2,1)S(1)}, bf16[3,3,256,128]{3,2,1,0:T(8,128)(2,1)}, u32[]{:S(2)}) copy-start(bf16[3,3,256,128]{3,2,1,0:T(8,128)(2,1)} %param.11) | copy-start | bytes 1769476
  17.4 9.1 %copy-start.3 = (f32[128]{0:T(128)S(1)}, f32[128]{0:T(128)}, u32[]{:S(2)}) copy-start(f32[128]{0:T(128)} %param.12) | copy-start | bytes 1540
  24.5 2.0 %collective-permute-start.5 = (bf16[16,64,256]{2,1,0:T(8,128)(2,1)S(1)}, bf16[16,64,256]{2,1,0:T(8,128)(2,1)S(1)}, u32[]{:S(2)}, u32[]{:S(2)}) collective-permute-start(bf16[16,64,256]{2,1,0:T(8,128)(2,1)S(1)} %get-tuple-element.37.own_ref), channel_id=1, source_target_pairs={{0,1},{1,0},{2,3},{3,2},{4,5},{5,4},{6,7},{7,6},{8,9},{9,8},{10,11... | collective-permute-start | bytes 1572872 | tf_op jit(solution)/shard_map/ppermute | solution.py:29
  24.6 6.3 %collective-permute-start.6 = (f32[4,72,128]{2,1,0:T(8,128)S(1)}, f32[4,72,128]{2,1,0:T(8,128)S(1)}, u32[]{:S(2)}, u32[]{:S(2)}) collective-permute-start(f32[4,72,128]{2,1,0:T(8,128)S(1)} %join.1.refs_0_), channel_id=1, source_target_pairs={{0,4},{4,0},{8,12},{12,8},{16,20},{20,16},{24,28},{28,24},{1,5},{5... | collective-permute-start | bytes 442376 | tf_op jit(solution)/shard_map/ppermute | solution.py:29
  33.8 4.6 %collective-permute-start.8 = (f16[336,128]{1,0:T(8,128)(2,1)S(1)}, f16[336,128]{1,0:T(8,128)(2,1)S(1)}, u32[]{:S(2)}, u32[]{:S(2)}) collective-permute-start(f16[336,128]{1,0:T(8,128)(2,1)S(1)} %convert_element_type.75), channel_id=1, source_target_pairs={{0,4},{4,0},{8,12},{12,8},{16,20},{20,16},{24,28},{28,24},{1,5},{5... | collective-permute-start | bytes 258056 | tf_op jit(solution)/shard_map/ppermute | solution.py:29
  38.5 8.6 %collective-permute-start.11 = (f16[368,128]{1,0:T(8,128)(2,1)S(1)}, f16[368,128]{1,0:T(8,128)(2,1)S(1)}, u32[]{:S(2)}, u32[]{:S(2)}) collective-permute-start(f16[368,128]{1,0:T(8,128)(2,1)S(1)} %convert_element_type.81), channel_id=1, source_target_pairs={{0,16},{4,20},{8,24},{12,28},{16,0},{20,4},{24,8},{28,12},{1,17},{... | collective-permute-start | bytes 282632 | tf_op jit(solution)/shard_map/ppermute | solution.py:29
  40.6 4.5 %collective-permute-start.10 = (f16[304,128]{1,0:T(8,128)(2,1)S(1)}, f16[304,128]{1,0:T(8,128)(2,1)S(1)}, u32[]{:S(2)}, u32[]{:S(2)}) collective-permute-start(f16[304,128]{1,0:T(8,128)(2,1)S(1)} %convert_element_type.79), channel_id=1, source_target_pairs={{0,4},{4,0},{8,12},{12,8},{16,20},{20,16},{24,28},{28,24},{1,5},{5... | collective-permute-start | bytes 233480 | tf_op jit(solution)/shard_map/ppermute | solution.py:29
  41.0 4.9 %collective-permute-start.9 = (f16[304,128]{1,0:T(8,128)(2,1)S(1)}, f16[304,128]{1,0:T(8,128)(2,1)S(1)}, u32[]{:S(2)}, u32[]{:S(2)}) collective-permute-start(f16[304,128]{1,0:T(8,128)(2,1)S(1)} %convert_element_type.77), channel_id=1, source_target_pairs={{0,4},{4,0},{8,12},{12,8},{16,20},{20,16},{24,28},{28,24},{1,5},{5... | collective-permute-start | bytes 233480 | tf_op jit(solution)/shard_map/ppermute | solution.py:29
  46.0 6.5 %collective-permute-start.13 = (f16[368,128]{1,0:T(8,128)(2,1)S(1)}, f16[368,128]{1,0:T(8,128)(2,1)S(1)}, u32[]{:S(2)}, u32[]{:S(2)}) collective-permute-start(f16[368,128]{1,0:T(8,128)(2,1)S(1)} %convert_element_type.85), channel_id=1, source_target_pairs={{0,24},{4,28},{8,16},{12,20},{16,8},{20,12},{24,0},{28,4},{1,25},{... | collective-permute-start | bytes 282632 | tf_op jit(solution)/shard_map/ppermute | solution.py:29
  47.2 5.6 %collective-permute-start.12 = (f16[368,128]{1,0:T(8,128)(2,1)S(1)}, f16[368,128]{1,0:T(8,128)(2,1)S(1)}, u32[]{:S(2)}, u32[]{:S(2)}) collective-permute-start(f16[368,128]{1,0:T(8,128)(2,1)S(1)} %convert_element_type.83), channel_id=1, source_target_pairs={{0,8},{4,12},{8,0},{12,4},{16,24},{20,28},{24,16},{28,20},{1,9},{5... | collective-permute-start | bytes 282632 | tf_op jit(solution)/shard_map/ppermute | solution.py:29
  47.7 4.5 %collective-permute-start.7 = (f16[304,128]{1,0:T(8,128)(2,1)S(1)}, f16[304,128]{1,0:T(8,128)(2,1)S(1)}, u32[]{:S(2)}, u32[]{:S(2)}) collective-permute-start(f16[304,128]{1,0:T(8,128)(2,1)S(1)} %convert_element_type.73), channel_id=1, source_target_pairs={{0,4},{4,0},{8,12},{12,8},{16,20},{20,16},{24,28},{28,24},{1,5},{5... | collective-permute-start | bytes 233480 | tf_op jit(solution)/shard_map/ppermute | solution.py:29
  53.6 6.3 %collective-permute-start.16 = (f16[1,304,128]{2,1,0:T(8,128)(2,1)S(1)}, f16[1,304,128]{2,1,0:T(8,128)(2,1)S(1)}, u32[]{:S(2)}, u32[]{:S(2)}) collective-permute-start(f16[1,304,128]{2,1,0:T(8,128)(2,1)S(1)} %get-tuple-element.56), channel_id=1, source_target_pairs={{0,24},{4,28},{8,16},{12,20},{16,8},{20,12},{24,0},{28,4},{1,25},{... | collective-permute-start | bytes 233480 | tf_op jit(solution)/shard_map/ppermute | solution.py:29
  55.5 6.1 %collective-permute-start.15 = (f16[1,304,128]{2,1,0:T(8,128)(2,1)S(1)}, f16[1,304,128]{2,1,0:T(8,128)(2,1)S(1)}, u32[]{:S(2)}, u32[]{:S(2)}) collective-permute-start(f16[1,304,128]{2,1,0:T(8,128)(2,1)S(1)} %get-tuple-element.56), channel_id=1, source_target_pairs={{0,16},{4,20},{8,24},{12,28},{16,0},{20,4},{24,8},{28,12},{1,17},{... | collective-permute-start | bytes 233480 | tf_op jit(solution)/shard_map/ppermute | solution.py:29
  56.1 6.7 %collective-permute-start.14 = (f16[1,304,128]{2,1,0:T(8,128)(2,1)S(1)}, f16[1,304,128]{2,1,0:T(8,128)(2,1)S(1)}, u32[]{:S(2)}, u32[]{:S(2)}) collective-permute-start(f16[1,304,128]{2,1,0:T(8,128)(2,1)S(1)} %get-tuple-element.56), channel_id=1, source_target_pairs={{0,8},{4,12},{8,0},{12,4},{16,24},{20,28},{24,16},{28,20},{1,9},{5... | collective-permute-start | bytes 233480 | tf_op jit(solution)/shard_map/ppermute | solution.py:29
  58.0 7.2 %collective-permute-start.17 = (f16[1,304,128]{2,1,0:T(8,128)(2,1)S(1)}, f16[1,304,128]{2,1,0:T(8,128)(2,1)S(1)}, u32[]{:S(2)}, u32[]{:S(2)}) collective-permute-start(f16[1,304,128]{2,1,0:T(8,128)(2,1)S(1)} %get-tuple-element.56), channel_id=1, source_target_pairs={{0,4},{4,0},{8,12},{12,8},{16,20},{20,16},{24,28},{28,24},{1,5},{5... | collective-permute-start | bytes 233480 | tf_op jit(solution)/shard_map/ppermute | solution.py:29
  59.9 5.4 %collective-permute-start.20 = (f16[1,304,128]{2,1,0:T(8,128)(2,1)S(1)}, f16[1,304,128]{2,1,0:T(8,128)(2,1)S(1)}, u32[]{:S(2)}, u32[]{:S(2)}) collective-permute-start(f16[1,304,128]{2,1,0:T(8,128)(2,1)S(1)} %collective-permute-done.16), channel_id=1, source_target_pairs={{0,4},{4,0},{8,12},{12,8},{16,20},{20,16},{24,28},{28,24},{1,5},{5... | collective-permute-start | bytes 233480 | tf_op jit(solution)/shard_map/ppermute | solution.py:29
  61.6 4.4 %collective-permute-start.19 = (f16[1,304,128]{2,1,0:T(8,128)(2,1)S(1)}, f16[1,304,128]{2,1,0:T(8,128)(2,1)S(1)}, u32[]{:S(2)}, u32[]{:S(2)}) collective-permute-start(f16[1,304,128]{2,1,0:T(8,128)(2,1)S(1)} %collective-permute-done.15), channel_id=1, source_target_pairs={{0,4},{4,0},{8,12},{12,8},{16,20},{20,16},{24,28},{28,24},{1,5},{5... | collective-permute-start | bytes 233480 | tf_op jit(solution)/shard_map/ppermute | solution.py:29
  62.9 4.4 %collective-permute-start.18 = (f16[1,304,128]{2,1,0:T(8,128)(2,1)S(1)}, f16[1,304,128]{2,1,0:T(8,128)(2,1)S(1)}, u32[]{:S(2)}, u32[]{:S(2)}) collective-permute-start(f16[1,304,128]{2,1,0:T(8,128)(2,1)S(1)} %collective-permute-done.14), channel_id=1, source_target_pairs={{0,4},{4,0},{8,12},{12,8},{16,20},{20,16},{24,28},{28,24},{1,5},{5... | collective-permute-start | bytes 233480 | tf_op jit(solution)/shard_map/ppermute | solution.py:29

commit v6 on v5

--- a/solution.py
+++ b/solution.py
@@ -62,7 +62,7 @@
 
 
 def shares(pooled_rows):
-    first = pooled_rows * 2 // 3 // STEP * STEP
+    first = pooled_rows // 2
     return first, pooled_rows - first
 
 
@@ -188,11 +188,9 @@
             edge_ref[g, t] = (total * keep).astype(BF16).astype(F32)
 
 
-def conv_kernel(where_ref, taps, w_ref, b_ref, got_ref, traded_ref, head_ref, tail_ref, *refs):
-    out_ref, edge_ref, acc = refs[-3:]
+def conv_kernel(where_ref, taps, w_ref, b_ref, *refs):
+    out_ref = refs[-1]
     half_cols, chans = taps.shape[1], taps.shape[2] // 4
-    half = where_ref[0]
-    first, second = shares(head_ref.shape[0] // 2)
     bias = b_ref[...]
 
     def step(k, carry):
@@ -213,34 +211,48 @@
         out_ref[pl.ds(k * STEP, STEP)] = (total * 0.25).astype(BF16)
         return carry
 
-    lax.fori_loop(0, pick(half, (first // STEP, second // STEP)), step, 0)
-    got, traded = got_ref[...], traded_ref[...]
-    left = jnp.concatenate([jnp.where(half == 0, got, traded), head_ref[...]], axis=-1)
-    right = jnp.concatenate([tail_ref[...], jnp.where(half == 0, traded, got)], axis=-1)
-    edge_part(where_ref, (left, right), w_ref, bias, edge_ref, acc)
-
-
-def conv_pool(where, taps, w, b, got, traded, head, tail, after):
+    lax.fori_loop(0, out_ref.shape[0] // STEP, step, 0)
+
+
+def conv_pool(where, taps, w, b, pooled_rows, after):
     _, half_cols, width = taps.shape
-    chans, rows = width // 4, head.shape[0]
-    first, lanes = shares(rows // 2)[0], chans // 128
+    chans = width // 4
     return pl.pallas_call(
         conv_kernel,
-        out_shape=(
-            jax.ShapeDtypeStruct((first, half_cols, chans), BF16),
-            jax.ShapeDtypeStruct((4, lanes, rows // 2, 128), F32),
-        ),
-        in_specs=[SMEM] + [VMEM] * 7 + [ANY] * len(after),
-        out_specs=(VMEM, VMEM),
-        scratch_shapes=[pltpu.VMEM((8 * lanes, rows + 16, 128), F32)],
-        compiler_params=params(24),
+        out_shape=jax.ShapeDtypeStruct((pooled_rows, half_cols, chans), BF16),
+        in_specs=[SMEM] + [VMEM] * 3 + [ANY] * len(after),
+        out_specs=VMEM,
+        compiler_params=params(16),
         cost_estimate=pl.CostEstimate(
-            flops=8 * first * half_cols * 9 * chans * chans,
+            flops=8 * pooled_rows * half_cols * 9 * chans * chans,
             bytes_accessed=8 << 20,
             transcendentals=0,
         ),
         name="conv_pool",
-    )(where, taps, w, b, got, traded, head, tail, *after)
+    )(where, taps, w, b, *after)
+
+
+def edge_kernel(where_ref, w_ref, b_ref, got_ref, traded_ref, head_ref, tail_ref, *refs):
+    edge_ref, acc = refs[-2:]
+    half = where_ref[0]
+    got, traded = got_ref[...], traded_ref[...]
+    left = jnp.concatenate([jnp.where(half == 0, got, traded), head_ref[...]], axis=-1)
+    right = jnp.concatenate([tail_ref[...], jnp.where(half == 0, traded, got)], axis=-1)
+    edge_part(where_ref, (left, right), w_ref, b_ref[...], edge_ref, acc)
+
+
+def conv_edges(where, w, b, got, traded, head, tail, after):
+    rows, lanes = head.shape[0], w.shape[1] // 128
+    return pl.pallas_call(
+        edge_kernel,
+        out_shape=jax.ShapeDtypeStruct((4, lanes, rows // 2, 128), F32),
+        in_specs=[SMEM] + [VMEM] * 6 + [ANY] * len(after),
+        out_specs=VMEM,
+        scratch_shapes=[pltpu.VMEM((8 * lanes, rows + 16, 128), F32)],
+        compiler_params=params(),
+        cost_estimate=pl.CostEstimate(flops=0, bytes_accessed=4 << 20, transcendentals=0),
+        name="conv_edges",
+    )(where, w, b, got, traded, head, tail, *after)
 
 
 def start_kernel(
@@ -568,6 +580,7 @@
         in_specs=[VMEM] * 4 + [ANY] * len(after),
         out_specs=VMEM,
         compiler_params=params(),
+        cost_estimate=pl.CostEstimate(flops=0, bytes_accessed=32 << 20, transcendentals=0),
         name="merge_pair",
     )(own, got, own_sums, got_sums, *after)
 
@@ -647,28 +660,21 @@
 
 
 def spread_kernel(where_ref, *refs, chunk, rows):
-    part_refs, weight_hbm, bias_ref, place, sems = refs[:-4], refs[-4], refs[-3], refs[-2], refs[-1]
+    part_refs, weight_ref, bias_ref, place = refs[:-3], refs[-3], refs[-2], refs[-1]
     me = where_ref[3]
     whole = rows == place.shape[0]
-    copies = []
     for m, ref, k in relative(part_refs):
         bias, down, _ = read_note(ref[k], chunk)
         j = me ^ m
-        at = pl.ds(pl.multiple_of(j * chunk, 8), chunk)
-        place[at] = ref[k, :chunk] * down
-        if whole:
-            copies.append(pltpu.make_async_copy(place.at[at], weight_hbm.at[at], sems.at[m]))
-            copies[-1].start()
+        target = weight_ref if whole else place
+        target[pl.ds(pl.multiple_of(j * chunk, 8), chunk)] = ref[k, :chunk] * down
 
         @pl.when(j == 0)
         def _():
             bias_ref[...] = bias
 
     if not whole:
-        copies.append(pltpu.make_async_copy(place.at[pl.ds(0, rows)], weight_hbm, sems.at[0]))
-        copies[-1].start()
-    for copy in copies:
-        copy.wait()
+        weight_ref[...] = place[:rows]
 
 
 def spread(where, parts, chunk, count, rows):
@@ -677,11 +683,8 @@
         functools.partial(spread_kernel, chunk=chunk, rows=rows),
         out_shape=(jax.ShapeDtypeStruct((rows, width), F32), jax.ShapeDtypeStruct((1, width), F32)),
         in_specs=[SMEM] + [VMEM] * len(parts),
-        out_specs=(HBM, VMEM),
-        scratch_shapes=[
-            pltpu.VMEM((count * chunk, width), F32),
-            pltpu.SemaphoreType.DMA((count,)),
-        ],
+        out_specs=(VMEM, VMEM),
+        scratch_shapes=[pltpu.VMEM((count * chunk, width), F32)],
         compiler_params=params(),
         name="spread",
     )(where, *parts)
@@ -719,8 +722,9 @@
     got, joined = lax.optimization_barrier((got, join(shared, [taps])))
     traded = swap(got, "chan", 1)
     shared = [joined, swap(joined, "strip", 1)]
-    pooled, edges = conv_pool(where, taps, near_w, conv_b, got, traded, head, tail, [joined])
+    pooled = conv_pool(where, taps, near_w, conv_b, section_input.shape[0] // 4, [joined, got])
     other = swap(pooled, "chan", 1)
+    edges = conv_edges(where, near_w, conv_b, got, traded, head, tail, [pooled])
 
     chunk = -(-9 * channels // strip_count // 8) * 8
     bits = min(2, strip_count.bit_length() - 2)
@@ -741,7 +745,8 @@
         where, forward, shared, chunk, strip_count, 2 * pieces, with_sums
     )
     heads, held = strip_count // (2 * pieces), 2
-    got = {k: swap(send[2 * k + 1].astype(F16), "strip", 1).astype(F32) for k in order}
+    leaving = lax.optimization_barrier([send[2 * k + 1].astype(F16) for k in order])
+    got = {k: swap(part, "strip", 1).astype(F32) for k, part in zip(order, leaving)}
     pair, parts, before = {}, {}, []
     for k in order:
         pair[k] = merge_pair(

time: 69.7 us -> 67 us (0.961)
  waiting for transfers between devices: 18.8 us -> 16.9 us
  Pallas kernels: 23.6 us -> 21.9 us
  starting transfers between devices: 25.7 us -> 26.6 us
    ppermute x20, waiting for transfers between devices: 18.8 us -> 16.9 us  [swap(): return lax.ppermute(value, axis, [(i, i ^ mask) for i in range(count)])]
    pallas_call x1 -> x2, Pallas kernels: 7.07 us -> 6.16 us  [the longest x1 4.9 us: conv_pool(): pl.pallas_call(conv_kernel, out_shape=jax.ShapeDtypeStruct((pooled_rows,...]
    ppermute x20, starting transfers between devices: 20.9 us -> 21.8 us  [swap(): return lax.ppermute(value, axis, [(i, i ^ mask) for i in range(count)])]
  transfers between devices with their start and end apart: 21 -> 21, of which waited for: 13 -> 12; matrix products, arithmetic and copies ran while one was open for 0% -> 0% of each run, Pallas kernels for 13% -> 15%
where the time goes in v6:
time: 67 us; the launch traced here: 66.8 us
  starting transfers between devices  26.6 us (40%)
  Pallas kernels  21.9 us (33%)
  waiting for transfers between devices  16.9 us (25%)
  between operations  1 us (1%)
    ppermute x20, starting transfers between devices, swap(): return lax.ppermute(value, axis, [(i, i ^ mask) for i in range(count)])  21.8 us
    ppermute x20, waiting for transfers between devices, swap(): return lax.ppermute(value, axis, [(i, i ^ mask) for i in range(count)])  16.9 us
    pallas_call x1, Pallas kernels, conv_pool(): pl.pallas_call(conv_kernel, out_shape=jax.ShapeDtypeStruct((pooled_rows,...  4.9 us
    ppermute x1, starting transfers between devices, body(): got = lax.ppermute(sent, ('strip', 'chan'), pairs)  4.85 us
    pallas_call x1, Pallas kernels, deep_forward(): pl.pallas_call(functools.partial(deep_kernel, block=block, entries=entrie...  4.38 us
    pallas_call x1, Pallas kernels, deep_backward(): pl.pallas_call(functools.partial(grad_kernel, n_parts=len(parts), chunk=c...  2.86 us
    pallas_call x1, Pallas kernels, windows(): pl.pallas_call(window_kernel, out_shape=(jax.ShapeDtypeStruct(((most + 2)...  2.5 us
    pallas_call x1, Pallas kernels, start(): pl.pallas_call(start_kernel, out_shape=(jax.ShapeDtypeStruct((1, owned +...  1.93 us
  transfers between devices with their start and end apart: 21, of which 12 were waited for; matrix products, arithmetic and copies ran while one was open for 0% of the time, Pallas kernels for 15%

profile of v6, /device:TPU:0, one launch (start us, length us, event | category | flops | bytes accessed | tf_op | source)
XLA Modules:
  0.0 66.8 jit_solution(13412049924259971766)
XLA Ops:
  0.7 1.9 %start.1 = (f32[1,72,128]{2,1,0:T(8,128)S(1)}, bf16[48,768]{1,0:T(8,128)(2,1)S(1)}, bf16[48,768]{1,0:T(8,128)(2,1)S(1)}, bf16[48,768]{1,0:T(8,128)(2,1)S(1)}) custom-call(s32[4]{0:T(128)S(1)} %pad_add_fusion.where_ref, bf16[48,128,256]{2,1,0:T(8,128)(2,1)} %x_hbm.3, f32[64,128]{1,0:T(8,128)} %grad_hbm.1, s32[24,64]{1,0:T(8,128)} %lab_ref.1, s32[1,32]{1,0:T(1,128)} %bitcast.19), custom_call_target="tpu_custom_call" | custom-call | tf_op jit(solution)/shard_map/start/pallas_call | solution.py:315
  2.7 4.8 %collective-permute-start = (bf16[48,768]{1,0:T(8,128)(2,1)S(1)}, bf16[48,768]{1,0:T(8,128)(2,1)S(1)}, u32[]{:S(2)}, u32[]{:S(2)}) collective-permute-start(bf16[48,768]{1,0:T(8,128)(2,1)S(1)} %get-tuple-element.33), channel_id=1, source_target_pairs={{0,4},{2,6},{4,8},{5,1},{6,10},{7,3},{8,12},{9,5},{10,14},{11,7},{... | collective-permute-start | bytes 221192 | tf_op jit(solution)/shard_map/ppermute | solution.py:717
  7.5 3.7 %collective-permute-start.3 = (f32[1,72,128]{2,1,0:T(8,128)S(1)}, f32[1,72,128]{2,1,0:T(8,128)S(1)}, u32[]{:S(2)}, u32[]{:S(2)}) collective-permute-start(f32[1,72,128]{2,1,0:T(8,128)S(1)} %get-tuple-element.34.refs_0_), channel_id=1, source_target_pairs={{0,24},{4,28},{8,16},{12,20},{16,8},{20,12},{24,0},{28,4},{1,25},{... | collective-permute-start | bytes 110600 | tf_op jit(solution)/shard_map/ppermute | solution.py:29
  11.2 0.8 %collective-permute-start.1 = (f32[1,72,128]{2,1,0:T(8,128)S(1)}, f32[1,72,128]{2,1,0:T(8,128)S(1)}, u32[]{:S(2)}, u32[]{:S(2)}) collective-permute-start(f32[1,72,128]{2,1,0:T(8,128)S(1)} %get-tuple-element.34.refs_0_), channel_id=1, source_target_pairs={{0,8},{4,12},{8,0},{12,4},{16,24},{20,28},{24,16},{28,20},{1,9},{5... | collective-permute-start | bytes 110600 | tf_op jit(solution)/shard_map/ppermute | solution.py:29
  12.0 2.5 %windows.1 = (bf16[36,64,1024]{2,1,0:T(8,128)(2,1)S(1)}, bf16[2304,256]{1,0:T(8,128)(2,1)S(1)}) custom-call(s32[4]{0:T(128)S(1)} %pad_add_fusion.where_ref, bf16[48,128,256]{2,1,0:T(8,128)(2,1)} %x_hbm.3, bf16[2304,256]{1,0:T(8,128)(2,1)} %bitcast.18), custom_call_target="tpu_custom_call" | custom-call | bytes 12582912 | tf_op jit(solution)/shard_map/windows/pallas_call | solution.py:126
  14.5 1.5 %collective-permute-done.2.refs_2_ = f32[1,72,128]{2,1,0:T(8,128)S(1)} collective-permute-done((f32[1,72,128]{2,1,0:T(8,128)S(1)}, f32[1,72,128]{2,1,0:T(8,128)S(1)}, u32[]{:S(2)}, u32[]{:S(2)}) %collective-permute-start.2) | collective-permute-done | bytes 36896 | tf_op jit(solution)/shard_map/ppermute | solution.py:29
  16.1 4.9 %conv_pool.1.refs_0_.own_ref = bf16[12,64,256]{2,1,0:T(8,128)(2,1)S(1)} custom-call(s32[4]{0:T(128)S(1)} %pad_add_fusion.where_ref, bf16[36,64,1024]{2,1,0:T(8,128)(2,1)S(1)} %get-tuple-element.31.refs_4_.taps, bf16[2304,256]{1,0:T(8,128)(2,1)S(1)} %get-tuple-element.32.w_ref, f32[1,256]{1,0:T(1,128)S(1)} %bitcast.14, f32[4,72,128]{2,1,0:T(8,128)S(1)} %join.1.refs_0_, ...), custom_call_target="tpu_custom_call" | custom-call | flops 3623878656 | bytes 8388608 | tf_op jit(solution)/shard_map/conv_pool/pallas_call | solution.py:220
  22.2 0.7 %collective-permute-done.5.traded_ref = bf16[48,768]{1,0:T(8,128)(2,1)S(1)} collective-permute-done((bf16[48,768]{1,0:T(8,128)(2,1)S(1)}, bf16[48,768]{1,0:T(8,128)(2,1)S(1)}, u32[]{:S(2)}, u32[]{:S(2)}) %collective-permute-start.5) | collective-permute-done | bytes 73760 | tf_op jit(solution)/shard_map/ppermute | solution.py:29
  22.9 1.3 %conv_edges.1.edge_ref = f32[4,2,24,128]{3,2,1,0:T(8,128)S(1)} custom-call(s32[4]{0:T(128)S(1)} %pad_add_fusion.where_ref, bf16[2304,256]{1,0:T(8,128)(2,1)S(1)} %get-tuple-element.32.w_ref, f32[1,256]{1,0:T(1,128)S(1)} %bitcast.15, bf16[48,768]{1,0:T(8,128)(2,1)S(1)} %collective-permute-done.refs_1_.got_ref, ...), custom_call_target="tpu_custom_call" | custom-call | bytes 4194304 | tf_op jit(solution)/shard_map/conv_edges/pallas_call | solution.py:246
  24.2 4.4 %deep_forward.1 = (bf16[26,64,768]{2,1,0:T(8,128)(2,1)S(1)}, bf16[24,64,128]{2,1,0:T(8,128)(2,1)S(1)}, f32[1536,128]{1,0:T(8,128)S(1)}, f32[32,128]{1,0:T(8,128)S(1)}) custom-call(s32[4]{0:T(128)S(1)} %pad_add_fusion.where_ref, bf16[12,64,256]{2,1,0:T(8,128)(2,1)S(1)} %conv_pool.1.refs_0_.own_ref, bf16[12,64,256]{2,1,0:T(8,128)(2,1)S(1)} %collective-permute-done.4.other_ref, ...), custom_call_target="tpu_custom_call" | custom-call | flops 1811939328 | bytes 8388608 | tf_op jit(solution)/shard_map/deep_forward/pallas_call | solution.py:455
  28.6 2.9 %deep_backward.1 = (f32[304,128]{1,0:T(8,128)S(1)}, f32[304,128]{1,0:T(8,128)S(1)}, f32[304,128]{1,0:T(8,128)S(1)}, f32[304,128]{1,0:T(8,128)S(1)}, f32[304,128]...) custom-call(s32[4]{0:T(128)S(1)} %pad_add_fusion.where_ref, ...), custom_call_target="tpu_custom_call" | custom-call | flops 1811939328 | bytes 8388608 | tf_op jit(solution)/shard_map/deep_backward/pallas_call | solution.py:537
  31.6 0.8 %collective-permute-start.8 = (f16[336,128]{1,0:T(8,128)(2,1)S(1)}, f16[336,128]{1,0:T(8,128)(2,1)S(1)}, u32[]{:S(2)}, u32[]{:S(2)}) collective-permute-start(f16[336,128]{1,0:T(8,128)(2,1)S(1)} %convert_element_type.73), channel_id=1, source_target_pairs={{0,4},{4,0},{8,12},{12,8},{16,20},{20,16},{24,28},{28,24},{1,5},{5... | collective-permute-start | bytes 258056 | tf_op jit(solution)/shard_map/ppermute | solution.py:29
  32.4 3.9 %collective-permute-done.8 = f16[336,128]{1,0:T(8,128)(2,1)S(1)} collective-permute-done((f16[336,128]{1,0:T(8,128)(2,1)S(1)}, f16[336,128]{1,0:T(8,128)(2,1)S(1)}, u32[]{:S(2)}, u32[]{:S(2)}) %collective-permute-start.8) | collective-permute-done | bytes 86048 | tf_op jit(solution)/shard_map/ppermute | solution.py:29
  36.3 2.1 %collective-permute-start.11 = (f16[368,128]{1,0:T(8,128)(2,1)S(1)}, f16[368,128]{1,0:T(8,128)(2,1)S(1)}, u32[]{:S(2)}, u32[]{:S(2)}) collective-permute-start(f16[368,128]{1,0:T(8,128)(2,1)S(1)} %convert_element_type.81), channel_id=1, source_target_pairs={{0,16},{4,20},{8,24},{12,28},{16,0},{20,4},{24,8},{28,12},{1,17},{... | collective-permute-start | bytes 282632 | tf_op jit(solution)/shard_map/ppermute | solution.py:29
  39.0 1.4 %collective-permute-start.10 = (f16[304,128]{1,0:T(8,128)(2,1)S(1)}, f16[304,128]{1,0:T(8,128)(2,1)S(1)}, u32[]{:S(2)}, u32[]{:S(2)}) collective-permute-start(f16[304,128]{1,0:T(8,128)(2,1)S(1)} %convert_element_type.74), channel_id=1, source_target_pairs={{0,4},{4,0},{8,12},{12,8},{16,20},{20,16},{24,28},{28,24},{1,5},{5... | collective-permute-start | bytes 233480 | tf_op jit(solution)/shard_map/ppermute | solution.py:29
  40.4 2.4 %collective-permute-done.9 = f16[304,128]{1,0:T(8,128)(2,1)S(1)} collective-permute-done((f16[304,128]{1,0:T(8,128)(2,1)S(1)}, f16[304,128]{1,0:T(8,128)(2,1)S(1)}, u32[]{:S(2)}, u32[]{:S(2)}) %collective-permute-start.9) | collective-permute-done | bytes 77856 | tf_op jit(solution)/shard_map/ppermute | solution.py:29
  42.8 0.8 %collective-permute-done.10 = f16[304,128]{1,0:T(8,128)(2,1)S(1)} collective-permute-done((f16[304,128]{1,0:T(8,128)(2,1)S(1)}, f16[304,128]{1,0:T(8,128)(2,1)S(1)}, u32[]{:S(2)}, u32[]{:S(2)}) %collective-permute-start.10) | collective-permute-done | bytes 77856 | tf_op jit(solution)/shard_map/ppermute | solution.py:29
  43.7 1.0 %collective-permute-start.13 = (f16[368,128]{1,0:T(8,128)(2,1)S(1)}, f16[368,128]{1,0:T(8,128)(2,1)S(1)}, u32[]{:S(2)}, u32[]{:S(2)}) collective-permute-start(f16[368,128]{1,0:T(8,128)(2,1)S(1)} %convert_element_type.85), channel_id=1, source_target_pairs={{0,24},{4,28},{8,16},{12,20},{16,8},{20,12},{24,0},{28,4},{1,25},{... | collective-permute-start | bytes 282632 | tf_op jit(solution)/shard_map/ppermute | solution.py:29
  45.4 1.2 %collective-permute-start.7 = (f16[304,128]{1,0:T(8,128)(2,1)S(1)}, f16[304,128]{1,0:T(8,128)(2,1)S(1)}, u32[]{:S(2)}, u32[]{:S(2)}) collective-permute-start(f16[304,128]{1,0:T(8,128)(2,1)S(1)} %convert_element_type.76), channel_id=1, source_target_pairs={{0,4},{4,0},{8,12},{12,8},{16,20},{20,16},{24,28},{28,24},{1,5},{5... | collective-permute-start | bytes 233480 | tf_op jit(solution)/shard_map/ppermute | solution.py:29
  46.6 3.2 %collective-permute-done.7 = f16[304,128]{1,0:T(8,128)(2,1)S(1)} collective-permute-done((f16[304,128]{1,0:T(8,128)(2,1)S(1)}, f16[304,128]{1,0:T(8,128)(2,1)S(1)}, u32[]{:S(2)}, u32[]{:S(2)}) %collective-permute-start.7) | collective-permute-done | bytes 77856 | tf_op jit(solution)/shard_map/ppermute | solution.py:29
  51.2 2.2 %collective-permute-start.16 = (f16[1,304,128]{2,1,0:T(8,128)(2,1)S(1)}, f16[1,304,128]{2,1,0:T(8,128)(2,1)S(1)}, u32[]{:S(2)}, u32[]{:S(2)}) collective-permute-start(f16[1,304,128]{2,1,0:T(8,128)(2,1)S(1)} %get-tuple-element.60), channel_id=1, source_target_pairs={{0,24},{4,28},{8,16},{12,20},{16,8},{20,12},{24,0},{28,4},{1,25},{... | collective-permute-start | bytes 233480 | tf_op jit(solution)/shard_map/ppermute | solution.py:29
  53.7 1.9 %collective-permute-start.14 = (f16[1,304,128]{2,1,0:T(8,128)(2,1)S(1)}, f16[1,304,128]{2,1,0:T(8,128)(2,1)S(1)}, u32[]{:S(2)}, u32[]{:S(2)}) collective-permute-start(f16[1,304,128]{2,1,0:T(8,128)(2,1)S(1)} %get-tuple-element.60), channel_id=1, source_target_pairs={{0,8},{4,12},{8,0},{12,4},{16,24},{20,28},{24,16},{28,20},{1,9},{5... | collective-permute-start | bytes 233480 | tf_op jit(solution)/shard_map/ppermute | solution.py:29
  55.6 1.0 %collective-permute-start.17 = (f16[1,304,128]{2,1,0:T(8,128)(2,1)S(1)}, f16[1,304,128]{2,1,0:T(8,128)(2,1)S(1)}, u32[]{:S(2)}, u32[]{:S(2)}) collective-permute-start(f16[1,304,128]{2,1,0:T(8,128)(2,1)S(1)} %get-tuple-element.60), channel_id=1, source_target_pairs={{0,4},{4,0},{8,12},{12,8},{16,20},{20,16},{24,28},{28,24},{1,5},{5... | collective-permute-start | bytes 233480 | tf_op jit(solution)/shard_map/ppermute | solution.py:29
  56.6 0.8 %collective-permute-done.16 = f16[1,304,128]{2,1,0:T(8,128)(2,1)S(1)} collective-permute-done((f16[1,304,128]{2,1,0:T(8,128)(2,1)S(1)}, f16[1,304,128]{2,1,0:T(8,128)(2,1)S(1)}, u32[]{:S(2)}, u32[]{:S(2)}) %collective-permute-start.16) | collective-permute-done | bytes 77856 | tf_op jit(solution)/shard_map/ppermute | solution.py:29
  57.5 1.0 %collective-permute-start.20 = (f16[1,304,128]{2,1,0:T(8,128)(2,1)S(1)}, f16[1,304,128]{2,1,0:T(8,128)(2,1)S(1)}, u32[]{:S(2)}, u32[]{:S(2)}) collective-permute-start(f16[1,304,128]{2,1,0:T(8,128)(2,1)S(1)} %collective-permute-done.16), channel_id=1, source_target_pairs={{0,4},{4,0},{8,12},{12,8},{16,20},{20,16},{24,28},{28,24},{1,5},{5... | collective-permute-start | bytes 233480 | tf_op jit(solution)/shard_map/ppermute | solution.py:29
  58.4 1.0 %collective-permute-done.15 = f16[1,304,128]{2,1,0:T(8,128)(2,1)S(1)} collective-permute-done((f16[1,304,128]{2,1,0:T(8,128)(2,1)S(1)}, f16[1,304,128]{2,1,0:T(8,128)(2,1)S(1)}, u32[]{:S(2)}, u32[]{:S(2)}) %collective-permute-start.15) | collective-permute-done | bytes 77856 | tf_op jit(solution)/shard_map/ppermute | solution.py:29
  59.5 1.2 %collective-permute-start.19 = (f16[1,304,128]{2,1,0:T(8,128)(2,1)S(1)}, f16[1,304,128]{2,1,0:T(8,128)(2,1)S(1)}, u32[]{:S(2)}, u32[]{:S(2)}) collective-permute-start(f16[1,304,128]{2,1,0:T(8,128)(2,1)S(1)} %collective-permute-done.15), channel_id=1, source_target_pairs={{0,4},{4,0},{8,12},{12,8},{16,20},{20,16},{24,28},{28,24},{1,5},{5... | collective-permute-start | bytes 233480 | tf_op jit(solution)/shard_map/ppermute | solution.py:29
  60.7 0.8 %collective-permute-start.18 = (f16[1,304,128]{2,1,0:T(8,128)(2,1)S(1)}, f16[1,304,128]{2,1,0:T(8,128)(2,1)S(1)}, u32[]{:S(2)}, u32[]{:S(2)}) collective-permute-start(f16[1,304,128]{2,1,0:T(8,128)(2,1)S(1)} %collective-permute-done.14), channel_id=1, source_target_pairs={{0,4},{4,0},{8,12},{12,8},{16,20},{20,16},{24,28},{28,24},{1,5},{5... | collective-permute-start | bytes 233480 | tf_op jit(solution)/shard_map/ppermute | solution.py:29
  61.5 1.5 %embed.1 = f32[64,128]{1,0:T(8,128)} custom-call(s32[4]{0:T(128)S(1)} %pad_add_fusion.where_ref, f32[256,128]{1,0:T(8,128)S(1)} %get-tuple-element.55.sums_ref, f32[4,72,128]{2,1,0:T(8,128)S(1)} %join.1.refs_0_, f32[4,72,128]{2,1,0:T(8,128)S(1)} %collective-permute-done.6.refs_1_), custom_call_target="tpu_custom_call" | custom-call | tf_op jit(solution)/shard_map/embed/pallas_call | solution.py:776
  63.2 0.7 %collective-permute-done.19 = f16[1,304,128]{2,1,0:T(8,128)(2,1)S(1)} collective-permute-done((f16[1,304,128]{2,1,0:T(8,128)(2,1)S(1)}, f16[1,304,128]{2,1,0:T(8,128)(2,1)S(1)}, u32[]{:S(2)}, u32[]{:S(2)}) %collective-permute-start.19) | collective-permute-done | bytes 77856 | tf_op jit(solution)/shard_map/ppermute | solution.py:29
  63.9 1.2 %collective-permute-done.18 = f16[1,304,128]{2,1,0:T(8,128)(2,1)S(1)} collective-permute-done((f16[1,304,128]{2,1,0:T(8,128)(2,1)S(1)}, f16[1,304,128]{2,1,0:T(8,128)(2,1)S(1)}, u32[]{:S(2)}, u32[]{:S(2)}) %collective-permute-start.18) | collective-permute-done | bytes 77856 | tf_op jit(solution)/shard_map/ppermute | solution.py:29
  65.1 1.7 %spread.1 = (f32[2304,128]{1,0:T(8,128)}, f32[1,128]{1,0:T(1,128)}) custom-call(s32[4]{0:T(128)S(1)} %pad_add_fusion.where_ref, f32[1,304,128]{2,1,0:T(8,128)S(1)} %get-tuple-element.59.refs_0_, f32[1,304,128]{2,1,0:T(8,128)S(1)} %convert_element_type.90.refs_1_, f32[1,304,128]{2,1,0:T(8,128)S(1)} %convert_element_type.91.refs_2_, ...), custom_call_target="tpu_custom_call" | custom-call | tf_op jit(solution)/shard_map/spread/pallas_call | solution.py:682
  (55 shorter events, 4.6 us)
Async XLA Ops:
  2.7 13.4 %collective-permute-start = (bf16[48,768]{1,0:T(8,128)(2,1)S(1)}, bf16[48,768]{1,0:T(8,128)(2,1)S(1)}, u32[]{:S(2)}, u32[]{:S(2)}) collective-permute-start(bf16[48,768]{1,0:T(8,128)(2,1)S(1)} %get-tuple-element.33), channel_id=1, source_target_pairs={{0,4},{2,6},{4,8},{5,1},{6,10},{7,3},{8,12},{9,5},{10,14},{11,7},{... | collective-permute-start | bytes 221192 | tf_op jit(solution)/shard_map/ppermute | solution.py:717
  7.5 7.0 %collective-permute-start.3 = (f32[1,72,128]{2,1,0:T(8,128)S(1)}, f32[1,72,128]{2,1,0:T(8,128)S(1)}, u32[]{:S(2)}, u32[]{:S(2)}) collective-permute-start(f32[1,72,128]{2,1,0:T(8,128)S(1)} %get-tuple-element.34.refs_0_), channel_id=1, source_target_pairs={{0,24},{4,28},{8,16},{12,20},{16,8},{20,12},{24,0},{28,4},{1,25},{... | collective-permute-start | bytes 110600 | tf_op jit(solution)/shard_map/ppermute | solution.py:29
  11.2 4.9 %collective-permute-start.2 = (f32[1,72,128]{2,1,0:T(8,128)S(1)}, f32[1,72,128]{2,1,0:T(8,128)S(1)}, u32[]{:S(2)}, u32[]{:S(2)}) collective-permute-start(f32[1,72,128]{2,1,0:T(8,128)S(1)} %get-tuple-element.34.refs_0_), channel_id=1, source_target_pairs={{0,16},{4,20},{8,24},{12,28},{16,0},{20,4},{24,8},{28,12},{1,17},{... | collective-permute-start | bytes 110600 | tf_op jit(solution)/shard_map/ppermute | solution.py:29
  11.2 4.9 %collective-permute-start.1 = (f32[1,72,128]{2,1,0:T(8,128)S(1)}, f32[1,72,128]{2,1,0:T(8,128)S(1)}, u32[]{:S(2)}, u32[]{:S(2)}) collective-permute-start(f32[1,72,128]{2,1,0:T(8,128)S(1)} %get-tuple-element.34.refs_0_), channel_id=1, source_target_pairs={{0,8},{4,12},{8,0},{12,4},{16,24},{20,28},{24,16},{28,20},{1,9},{5... | collective-permute-start | bytes 110600 | tf_op jit(solution)/shard_map/ppermute | solution.py:29
  14.5 1.6 %copy-start.1 = (f32[256]{0:T(256)S(1)}, f32[256]{0:T(256)}, u32[]{:S(2)}) copy-start(f32[256]{0:T(256)} %param.10) | copy-start | bytes 3076
  16.1 8.1 %copy-start = (s32[24,64]{1,0:T(8,128)S(1)}, s32[24,64]{1,0:T(8,128)}, u32[]{:S(2)}) copy-start(s32[24,64]{1,0:T(8,128)} %lab_ref.1) | copy-start | bytes 18436
  16.1 8.1 %copy-start.2 = (bf16[3,3,256,128]{3,2,1,0:T(8,128)(2,1)S(1)}, bf16[3,3,256,128]{3,2,1,0:T(8,128)(2,1)}, u32[]{:S(2)}) copy-start(bf16[3,3,256,128]{3,2,1,0:T(8,128)(2,1)} %param.11) | copy-start | bytes 1769476
  16.1 8.1 %copy-start.3 = (f32[128]{0:T(128)S(1)}, f32[128]{0:T(128)}, u32[]{:S(2)}) copy-start(f32[128]{0:T(128)} %param.12) | copy-start | bytes 1540
  21.0 3.2 %collective-permute-start.4 = (bf16[12,64,256]{2,1,0:T(8,128)(2,1)S(1)}, bf16[12,64,256]{2,1,0:T(8,128)(2,1)S(1)}, u32[]{:S(2)}, u32[]{:S(2)}) collective-permute-start(bf16[12,64,256]{2,1,0:T(8,128)(2,1)S(1)} %conv_pool.1.refs_0_.own_ref), channel_id=1, source_target_pairs={{0,1},{1,0},{2,3},{3,2},{4,5},{5,4},{6,7},{7,6},{8,9},{9,8},{10,11... | collective-permute-start | bytes 1179656 | tf_op jit(solution)/shard_map/ppermute | solution.py:29
  21.1 1.8 %collective-permute-start.5 = (bf16[48,768]{1,0:T(8,128)(2,1)S(1)}, bf16[48,768]{1,0:T(8,128)(2,1)S(1)}, u32[]{:S(2)}, u32[]{:S(2)}) collective-permute-start(bf16[48,768]{1,0:T(8,128)(2,1)S(1)} %collective-permute-done.refs_1_.got_ref), channel_id=1, source_target_pairs={{0,1},{1,0},{2,3},{3,2},{4,5},{5,4},{6,7},{7,6},{8,9},{9,8},{10,11... | collective-permute-start | bytes 221192 | tf_op jit(solution)/shard_map/ppermute | solution.py:29
  21.6 7.0 %collective-permute-start.6 = (f32[4,72,128]{2,1,0:T(8,128)S(1)}, f32[4,72,128]{2,1,0:T(8,128)S(1)}, u32[]{:S(2)}, u32[]{:S(2)}) collective-permute-start(f32[4,72,128]{2,1,0:T(8,128)S(1)} %join.1.refs_0_), channel_id=1, source_target_pairs={{0,4},{4,0},{8,12},{12,8},{16,20},{20,16},{24,28},{28,24},{1,5},{5... | collective-permute-start | bytes 442376 | tf_op jit(solution)/shard_map/ppermute | solution.py:29
  31.6 4.6 %collective-permute-start.8 = (f16[336,128]{1,0:T(8,128)(2,1)S(1)}, f16[336,128]{1,0:T(8,128)(2,1)S(1)}, u32[]{:S(2)}, u32[]{:S(2)}) collective-permute-start(f16[336,128]{1,0:T(8,128)(2,1)S(1)} %convert_element_type.73), channel_id=1, source_target_pairs={{0,4},{4,0},{8,12},{12,8},{16,20},{20,16},{24,28},{28,24},{1,5},{5... | collective-permute-start | bytes 258056 | tf_op jit(solution)/shard_map/ppermute | solution.py:29
  36.3 8.4 %collective-permute-start.11 = (f16[368,128]{1,0:T(8,128)(2,1)S(1)}, f16[368,128]{1,0:T(8,128)(2,1)S(1)}, u32[]{:S(2)}, u32[]{:S(2)}) collective-permute-start(f16[368,128]{1,0:T(8,128)(2,1)S(1)} %convert_element_type.81), channel_id=1, source_target_pairs={{0,16},{4,20},{8,24},{12,28},{16,0},{20,4},{24,8},{28,12},{1,17},{... | collective-permute-start | bytes 282632 | tf_op jit(solution)/shard_map/ppermute | solution.py:29
  38.4 4.4 %collective-permute-start.9 = (f16[304,128]{1,0:T(8,128)(2,1)S(1)}, f16[304,128]{1,0:T(8,128)(2,1)S(1)}, u32[]{:S(2)}, u32[]{:S(2)}) collective-permute-start(f16[304,128]{1,0:T(8,128)(2,1)S(1)} %convert_element_type.75), channel_id=1, source_target_pairs={{0,4},{4,0},{8,12},{12,8},{16,20},{20,16},{24,28},{28,24},{1,5},{5... | collective-permute-start | bytes 233480 | tf_op jit(solution)/shard_map/ppermute | solution.py:29
  39.0 4.6 %collective-permute-start.10 = (f16[304,128]{1,0:T(8,128)(2,1)S(1)}, f16[304,128]{1,0:T(8,128)(2,1)S(1)}, u32[]{:S(2)}, u32[]{:S(2)}) collective-permute-start(f16[304,128]{1,0:T(8,128)(2,1)S(1)} %convert_element_type.74), channel_id=1, source_target_pairs={{0,4},{4,0},{8,12},{12,8},{16,20},{20,16},{24,28},{28,24},{1,5},{5... | collective-permute-start | bytes 233480 | tf_op jit(solution)/shard_map/ppermute | solution.py:29
  43.7 6.5 %collective-permute-start.13 = (f16[368,128]{1,0:T(8,128)(2,1)S(1)}, f16[368,128]{1,0:T(8,128)(2,1)S(1)}, u32[]{:S(2)}, u32[]{:S(2)}) collective-permute-start(f16[368,128]{1,0:T(8,128)(2,1)S(1)} %convert_element_type.85), channel_id=1, source_target_pairs={{0,24},{4,28},{8,16},{12,20},{16,8},{20,12},{24,0},{28,4},{1,25},{... | collective-permute-start | bytes 282632 | tf_op jit(solution)/shard_map/ppermute | solution.py:29
  44.8 5.6 %collective-permute-start.12 = (f16[368,128]{1,0:T(8,128)(2,1)S(1)}, f16[368,128]{1,0:T(8,128)(2,1)S(1)}, u32[]{:S(2)}, u32[]{:S(2)}) collective-permute-start(f16[368,128]{1,0:T(8,128)(2,1)S(1)} %convert_element_type.83), channel_id=1, source_target_pairs={{0,8},{4,12},{8,0},{12,4},{16,24},{20,28},{24,16},{28,20},{1,9},{5... | collective-permute-start | bytes 282632 | tf_op jit(solution)/shard_map/ppermute | solution.py:29
  45.4 4.4 %collective-permute-start.7 = (f16[304,128]{1,0:T(8,128)(2,1)S(1)}, f16[304,128]{1,0:T(8,128)(2,1)S(1)}, u32[]{:S(2)}, u32[]{:S(2)}) collective-permute-start(f16[304,128]{1,0:T(8,128)(2,1)S(1)} %convert_element_type.76), channel_id=1, source_target_pairs={{0,4},{4,0},{8,12},{12,8},{16,20},{20,16},{24,28},{28,24},{1,5},{5... | collective-permute-start | bytes 233480 | tf_op jit(solution)/shard_map/ppermute | solution.py:29
  51.2 6.3 %collective-permute-start.16 = (f16[1,304,128]{2,1,0:T(8,128)(2,1)S(1)}, f16[1,304,128]{2,1,0:T(8,128)(2,1)S(1)}, u32[]{:S(2)}, u32[]{:S(2)}) collective-permute-start(f16[1,304,128]{2,1,0:T(8,128)(2,1)S(1)} %get-tuple-element.60), channel_id=1, source_target_pairs={{0,24},{4,28},{8,16},{12,20},{16,8},{20,12},{24,0},{28,4},{1,25},{... | collective-permute-start | bytes 233480 | tf_op jit(solution)/shard_map/ppermute | solution.py:29
  53.4 6.1 %collective-permute-start.15 = (f16[1,304,128]{2,1,0:T(8,128)(2,1)S(1)}, f16[1,304,128]{2,1,0:T(8,128)(2,1)S(1)}, u32[]{:S(2)}, u32[]{:S(2)}) collective-permute-start(f16[1,304,128]{2,1,0:T(8,128)(2,1)S(1)} %get-tuple-element.60), channel_id=1, source_target_pairs={{0,16},{4,20},{8,24},{12,28},{16,0},{20,4},{24,8},{28,12},{1,17},{... | collective-permute-start | bytes 233480 | tf_op jit(solution)/shard_map/ppermute | solution.py:29
  53.7 7.0 %collective-permute-start.14 = (f16[1,304,128]{2,1,0:T(8,128)(2,1)S(1)}, f16[1,304,128]{2,1,0:T(8,128)(2,1)S(1)}, u32[]{:S(2)}, u32[]{:S(2)}) collective-permute-start(f16[1,304,128]{2,1,0:T(8,128)(2,1)S(1)} %get-tuple-element.60), channel_id=1, source_target_pairs={{0,8},{4,12},{8,0},{12,4},{16,24},{20,28},{24,16},{28,20},{1,9},{5... | collective-permute-start | bytes 233480 | tf_op jit(solution)/shard_map/ppermute | solution.py:29
  55.6 7.5 %collective-permute-start.17 = (f16[1,304,128]{2,1,0:T(8,128)(2,1)S(1)}, f16[1,304,128]{2,1,0:T(8,128)(2,1)S(1)}, u32[]{:S(2)}, u32[]{:S(2)}) collective-permute-start(f16[1,304,128]{2,1,0:T(8,128)(2,1)S(1)} %get-tuple-element.60), channel_id=1, source_target_pairs={{0,4},{4,0},{8,12},{12,8},{16,20},{20,16},{24,28},{28,24},{1,5},{5... | collective-permute-start | bytes 233480 | tf_op jit(solution)/shard_map/ppermute | solution.py:29
  57.5 5.7 %collective-permute-start.20 = (f16[1,304,128]{2,1,0:T(8,128)(2,1)S(1)}, f16[1,304,128]{2,1,0:T(8,128)(2,1)S(1)}, u32[]{:S(2)}, u32[]{:S(2)}) collective-permute-start(f16[1,304,128]{2,1,0:T(8,128)(2,1)S(1)} %collective-permute-done.16), channel_id=1, source_target_pairs={{0,4},{4,0},{8,12},{12,8},{16,20},{20,16},{24,28},{28,24},{1,5},{5... | collective-permute-start | bytes 233480 | tf_op jit(solution)/shard_map/ppermute | solution.py:29
  59.5 4.4 %collective-permute-start.19 = (f16[1,304,128]{2,1,0:T(8,128)(2,1)S(1)}, f16[1,304,128]{2,1,0:T(8,128)(2,1)S(1)}, u32[]{:S(2)}, u32[]{:S(2)}) collective-permute-start(f16[1,304,128]{2,1,0:T(8,128)(2,1)S(1)} %collective-permute-done.15), channel_id=1, source_target_pairs={{0,4},{4,0},{8,12},{12,8},{16,20},{20,16},{24,28},{28,24},{1,5},{5... | collective-permute-start | bytes 233480 | tf_op jit(solution)/shard_map/ppermute | solution.py:29
  60.7 4.4 %collective-permute-start.18 = (f16[1,304,128]{2,1,0:T(8,128)(2,1)S(1)}, f16[1,304,128]{2,1,0:T(8,128)(2,1)S(1)}, u32[]{:S(2)}, u32[]{:S(2)}) collective-permute-start(f16[1,304,128]{2,1,0:T(8,128)(2,1)S(1)} %collective-permute-done.14), channel_id=1, source_target_pairs={{0,4},{4,0},{8,12},{12,8},{16,20},{20,16},{24,28},{28,24},{1,5},{5... | collective-permute-start | bytes 233480 | tf_op jit(solution)/shard_map/ppermute | solution.py:29

commit v7 on v6

--- a/solution.py
+++ b/solution.py
@@ -1,4 +1,5 @@
 import functools
+import itertools
 import math
 
 import jax
@@ -16,7 +17,7 @@
 SIDE = 8
 WIDTH = 3
 PIECE = 4
-STEP = 4
+STEP = 6
 NOTE = 16
 
 
@@ -190,6 +191,7 @@
 
 def conv_kernel(where_ref, taps, w_ref, b_ref, *refs):
     out_ref = refs[-1]
+    assert out_ref.shape[0] % STEP == 0
     half_cols, chans = taps.shape[1], taps.shape[2] // 4
     bias = b_ref[...]
 
@@ -527,7 +529,9 @@
                 weight[pl.ds(pl.multiple_of(j * chunk, 8), chunk)] * up
             )
         out_refs[m][heads * chunk : heads * chunk + NOTE] = note
-    out_refs[with_sums][heads * chunk + NOTE :] = sums * jnp.exp2(12.0 - power_sums)
+    sums = sums * jnp.exp2(12.0 - power_sums)
+    for m in with_sums:
+        out_refs[m][heads * chunk + NOTE :] = sums
 
 
 def deep_backward(where, forward, parts, chunk, count, ways, with_sums):
@@ -539,7 +543,7 @@
             grad_kernel, n_parts=len(parts), chunk=chunk, ways=ways, with_sums=with_sums
         ),
         out_shape=tuple(
-            jax.ShapeDtypeStruct((size + (entries if m == with_sums else 0), width), F32)
+            jax.ShapeDtypeStruct((size + (entries if m in with_sums else 0), width), F32)
             for m in range(ways)
         ),
         in_specs=[SMEM] + [VMEM] * (4 + len(parts)),
@@ -585,17 +589,19 @@
     )(own, got, own_sums, got_sums, *after)
 
 
-def merge_kernel(where_ref, *refs, chunk, heads, held, entries, shift, next_ways):
-    n_parts = len(refs) - next_ways - 1
+def merge_kernel(where_ref, *refs, plan, chunk, heads, entries, shift, next_ways):
+    n_parts = len(plan)
     part_refs, out_refs, sums_ref = refs[:n_parts], refs[n_parts:-1], refs[-1]
     width = part_refs[0].shape[-1]
     size = heads * chunk
     total, bias = jnp.zeros((size, width), F32), jnp.zeros((1, width), F32)
-    sums_rows = held * entries
-    for m, ref in enumerate(part_refs):
+    for ref, (added, members) in zip(part_refs, plan):
         more, down, down_sums = read_note(ref, size)
-        total, bias = total + ref[:size] * down, bias + more
-        sums_ref[m * sums_rows : (m + 1) * sums_rows] = ref[size + NOTE :] * down_sums
+        if added:
+            total, bias = total + ref[:size] * down, bias + more
+        for k, m in enumerate(members):
+            at = size + NOTE + k * entries
+            sums_ref[m * entries : (m + 1) * entries] = ref[at : at + entries] * down_sums
     sums = sums_ref[...]
     power, power_sums = scale_rows(total, bias, sums)
     up = jnp.exp2(12.0 - power)
@@ -619,9 +625,9 @@
         out_refs[m][at + NOTE :] = sums
 
 
-def merge(where, parts, chunk, heads, held, entries, shift, next_ways):
-    width = parts[0].shape[-1]
-    sums_rows = len(parts) * held * entries
+def merge(where, parts, chunk, heads, entries, shift, next_ways):
+    width = parts[0][0].shape[-1]
+    sums_rows = sum(len(members) for _, _, members in parts) * entries
     if next_ways == 1:
         outs = (jax.ShapeDtypeStruct((heads * chunk + NOTE, width), F32),)
     else:
@@ -630,14 +636,20 @@
     outs = outs + (jax.ShapeDtypeStruct((sums_rows, width), F32),)
     out = pl.pallas_call(
         functools.partial(
-            merge_kernel, chunk=chunk, heads=heads, held=held, entries=entries, shift=shift, next_ways=next_ways
+            merge_kernel,
+            plan=tuple((added, tuple(members)) for _, added, members in parts),
+            chunk=chunk,
+            heads=heads,
+            entries=entries,
+            shift=shift,
+            next_ways=next_ways,
         ),
         out_shape=outs,
         in_specs=[SMEM] + [VMEM] * len(parts),
         out_specs=(VMEM,) * len(outs),
         compiler_params=params(),
         name="merge",
-    )(where, *parts)
+    )(where, *(part for part, _, _ in parts))
     return out[:-1], out[-1]
 
 
@@ -663,9 +675,11 @@
     part_refs, weight_ref, bias_ref, place = refs[:-3], refs[-3], refs[-2], refs[-1]
     me = where_ref[3]
     whole = rows == place.shape[0]
-    for m, ref, k in relative(part_refs):
+    count = len(part_refs)
+    for k, m in itertools.product(range(part_refs[0].shape[0]), range(count)):
+        ref = part_refs[m]
         bias, down, _ = read_note(ref[k], chunk)
-        j = me ^ m
+        j = me ^ (m + k * count)
         target = weight_ref if whole else place
         target[pl.ds(pl.multiple_of(j * chunk, 8), chunk)] = ref[k, :chunk] * down
 
@@ -727,10 +741,11 @@
     edges = conv_edges(where, near_w, conv_b, got, traded, head, tail, [pooled])
 
     chunk = -(-9 * channels // strip_count // 8) * 8
-    bits = min(2, strip_count.bit_length() - 2)
-    pieces = 1 << bits
-    order = list(range(pieces // 2, pieces)) + list(range(pieces // 2))[::-1]
-    with_sums = 2 * order[0] + 1
+    bits = strip_count.bit_length() - 1
+    pieces = 1 << min(2, bits - 1)
+    ways = 2 * pieces
+    far = list(range(2, pieces))
+    with_sums = {2, 3} | {2 * k + 1 for k in far[:1]}
     forward = deep_forward(
         where,
         pooled,
@@ -741,37 +756,37 @@
         labels,
         entries,
     )
-    send = deep_backward(
-        where, forward, shared, chunk, strip_count, 2 * pieces, with_sums
-    )
-    heads, held = strip_count // (2 * pieces), 2
-    leaving = lax.optimization_barrier([send[2 * k + 1].astype(F16) for k in order])
-    got = {k: swap(part, "strip", 1).astype(F32) for k, part in zip(order, leaving)}
-    pair, parts, before = {}, {}, []
-    for k in order:
-        pair[k] = merge_pair(
-            send[2 * k], got[k], send[with_sums], got[order[0]], heads * chunk, entries, before
-        )
-        parts[k] = swap(pair[k].astype(F16), "strip", 2 * k).astype(F32) if k else pair[k]
-        before = [pair[k]] if k < pieces // 2 or k + 1 < pieces else [pair[k], parts[order[0]]]
-    parts = [parts[k] for k in range(pieces)]
-    held *= pieces
-    send, sums = parts, None
-    shift = bits + 1
+    send = deep_backward(where, forward, shared, chunk, strip_count, ways, with_sums)
+    heads = strip_count // ways
+    got = {k: swap(send[2 * k + 1].astype(F16), "strip", 1).astype(F32) for k in far}
+    parts = [(send[0], True, [])]
+    for m in range(1, min(4, ways)):
+        sent = swap(send[m].astype(F16), "strip", m).astype(F32)
+        parts.append((sent, True, [m] if m in with_sums else []))
+    before = [part for part, _, members in parts if members == [2]]
+    for k in far:
+        own_sums, got_sums = send[2 * far[0] + 1], got[far[0]]
+        pair = merge_pair(send[2 * k], got[k], own_sums, got_sums, heads * chunk, entries, before)
+        before = [pair]
+        sent = swap(pair.astype(F16), "strip", 2 * k).astype(F32)
+        parts.append((sent, True, [2 * k, 2 * k + 1]))
+        if k == far[0]:
+            parts += [(own_sums, False, [0]), (got_sums, False, [1])]
+    held, shift = ways, ways.bit_length() - 1
     while True:
-        left_bits = strip_count.bit_length() - 1 - shift
-        size = min(3, left_bits)
-        send, sums = merge(
-            where, parts, chunk, heads, held // len(parts), entries, shift, 1 << size
-        )
+        size = min(3, bits - shift)
+        send, sums = merge(where, parts, chunk, heads, entries, shift, 1 << size)
         if size == 0:
             break
-        ways = 1 << size
-        heads //= ways
-        parts = [send[0]] + [
-            swap(send[m].astype(F16), "strip", m << shift).astype(F32) for m in range(1, ways)
+        more = 1 << size
+        heads //= more
+        arrived = [send[0]] + [
+            swap(send[m].astype(F16), "strip", m << shift).astype(F32) for m in range(1, more)
         ]
-        held *= ways
+        parts = [
+            (part, True, list(range(m * held, (m + 1) * held))) for m, part in enumerate(arrived)
+        ]
+        held *= more
         shift += size
     embeddings = pl.pallas_call(
         functools.partial(embed_kernel, entries=entries),
@@ -781,8 +796,13 @@
         compiler_params=params(),
         name="embed",
     )(where, sums, *shared)
-    gathered = gather_groups(send[0].astype(F16)[None], "strip", high_groups(strip_count))
-    gathered = gathered + [swap(g, "strip", 1) for g in gathered]
+    high = [(at, min(3, bits - at)) for at in range(ways.bit_length() - 1, bits, 3)]
+    own = gather_groups(send[0].astype(F16)[None], "strip", high)
+    own = own[0] if len(own) == 1 else jnp.concatenate(own, axis=0)
+    gathered = [own] + [swap(own, "strip", m) for m in range(1, min(4, ways))]
+    for k in far:
+        direct = swap(own, "strip", 2 * k)
+        gathered += [direct, swap(direct, "strip", 1)]
     weight_rows, bias_row = spread(
         where, [g.astype(F32) for g in gathered], chunk, strip_count, 9 * channels
     )

time: 67 us -> 64.7 us (0.966)
  waiting for transfers between devices: 16.9 us -> 13.9 us
  starting transfers between devices: 26.6 us -> 27.4 us
    ppermute x20, waiting for transfers between devices: 16.9 us -> 13.9 us  [swap(): return lax.ppermute(value, axis, [(i, i ^ mask) for i in range(count)])]
    ppermute x20, starting transfers between devices: 21.8 us -> 22.5 us  [swap(): return lax.ppermute(value, axis, [(i, i ^ mask) for i in range(count)])]
  transfers between devices with their start and end apart: 21 -> 21, of which waited for: 12 -> 8; matrix products, arithmetic and copies ran while one was open for 0% -> 0% of each run, Pallas kernels for 15% -> 15%
where the time goes in v7:
time: 64.7 us; the launch traced here: 64.4 us
  starting transfers between devices  27.4 us (42%)
  Pallas kernels  21.7 us (34%)
  waiting for transfers between devices  13.9 us (21%)
  between operations  1.03 us (2%)
    ppermute x20, starting transfers between devices, swap(): return lax.ppermute(value, axis, [(i, i ^ mask) for i in range(count)])  22.5 us
    ppermute x20, waiting for transfers between devices, swap(): return lax.ppermute(value, axis, [(i, i ^ mask) for i in range(count)])  13.9 us
    ppermute x1, starting transfers between devices, body(): got = lax.ppermute(sent, ('strip', 'chan'), pairs)  4.85 us
    pallas_call x1, Pallas kernels, conv_pool(): pl.pallas_call(conv_kernel, out_shape=jax.ShapeDtypeStruct((pooled_rows,...  4.7 us
    pallas_call x1, Pallas kernels, deep_forward(): pl.pallas_call(functools.partial(deep_kernel, block=block, entries=entrie...  4.38 us
    pallas_call x1, Pallas kernels, deep_backward(): pl.pallas_call(functools.partial(grad_kernel, n_parts=len(parts), chunk=c...  2.86 us
    pallas_call x1, Pallas kernels, windows(): pl.pallas_call(window_kernel, out_shape=(jax.ShapeDtypeStruct(((most + 2)...  2.5 us
    pallas_call x1, Pallas kernels, start(): pl.pallas_call(start_kernel, out_shape=(jax.ShapeDtypeStruct((1, owned +...  1.93 us
  transfers between devices with their start and end apart: 21, of which 8 were waited for; matrix products, arithmetic and copies ran while one was open for 0% of the time, Pallas kernels for 15%

profile of v7, /device:TPU:0, one launch (start us, length us, event | category | flops | bytes accessed | tf_op | source)
XLA Modules:
  0.0 64.4 jit_solution(3934902890150094026)
XLA Ops:
  0.7 1.9 %start.1 = (f32[1,72,128]{2,1,0:T(8,128)S(1)}, bf16[48,768]{1,0:T(8,128)(2,1)S(1)}, bf16[48,768]{1,0:T(8,128)(2,1)S(1)}, bf16[48,768]{1,0:T(8,128)(2,1)S(1)}) custom-call(s32[4]{0:T(128)S(1)} %pad_add_fusion.where_ref, bf16[48,128,256]{2,1,0:T(8,128)(2,1)} %x_hbm.3, f32[64,128]{1,0:T(8,128)} %grad_hbm.1, s32[24,64]{1,0:T(8,128)} %lab_ref.1, s32[1,32]{1,0:T(1,128)} %bitcast.19), custom_call_target="tpu_custom_call" | custom-call | tf_op jit(solution)/shard_map/start/pallas_call | solution.py:317
  2.7 4.8 %collective-permute-start = (bf16[48,768]{1,0:T(8,128)(2,1)S(1)}, bf16[48,768]{1,0:T(8,128)(2,1)S(1)}, u32[]{:S(2)}, u32[]{:S(2)}) collective-permute-start(bf16[48,768]{1,0:T(8,128)(2,1)S(1)} %get-tuple-element.29), channel_id=1, source_target_pairs={{0,4},{2,6},{4,8},{5,1},{6,10},{7,3},{8,12},{9,5},{10,14},{11,7},{... | collective-permute-start | bytes 221192 | tf_op jit(solution)/shard_map/ppermute | solution.py:731
  7.5 3.7 %collective-permute-start.3 = (f32[1,72,128]{2,1,0:T(8,128)S(1)}, f32[1,72,128]{2,1,0:T(8,128)S(1)}, u32[]{:S(2)}, u32[]{:S(2)}) collective-permute-start(f32[1,72,128]{2,1,0:T(8,128)S(1)} %get-tuple-element.30.refs_0_), channel_id=1, source_target_pairs={{0,24},{4,28},{8,16},{12,20},{16,8},{20,12},{24,0},{28,4},{1,25},{... | collective-permute-start | bytes 110600 | tf_op jit(solution)/shard_map/ppermute | solution.py:30
  11.2 0.8 %collective-permute-start.1 = (f32[1,72,128]{2,1,0:T(8,128)S(1)}, f32[1,72,128]{2,1,0:T(8,128)S(1)}, u32[]{:S(2)}, u32[]{:S(2)}) collective-permute-start(f32[1,72,128]{2,1,0:T(8,128)S(1)} %get-tuple-element.30.refs_0_), channel_id=1, source_target_pairs={{0,8},{4,12},{8,0},{12,4},{16,24},{20,28},{24,16},{28,20},{1,9},{5... | collective-permute-start | bytes 110600 | tf_op jit(solution)/shard_map/ppermute | solution.py:30
  12.0 2.5 %windows.1 = (bf16[36,64,1024]{2,1,0:T(8,128)(2,1)S(1)}, bf16[2304,256]{1,0:T(8,128)(2,1)S(1)}) custom-call(s32[4]{0:T(128)S(1)} %pad_add_fusion.where_ref, bf16[48,128,256]{2,1,0:T(8,128)(2,1)} %x_hbm.3, bf16[2304,256]{1,0:T(8,128)(2,1)} %bitcast.18), custom_call_target="tpu_custom_call" | custom-call | bytes 12582912 | tf_op jit(solution)/shard_map/windows/pallas_call | solution.py:127
  14.5 1.5 %collective-permute-done.2.refs_2_ = f32[1,72,128]{2,1,0:T(8,128)S(1)} collective-permute-done((f32[1,72,128]{2,1,0:T(8,128)S(1)}, f32[1,72,128]{2,1,0:T(8,128)S(1)}, u32[]{:S(2)}, u32[]{:S(2)}) %collective-permute-start.2) | collective-permute-done | bytes 36896 | tf_op jit(solution)/shard_map/ppermute | solution.py:30
  16.1 4.7 %conv_pool.1.refs_0_.own_ref = bf16[12,64,256]{2,1,0:T(8,128)(2,1)S(1)} custom-call(s32[4]{0:T(128)S(1)} %pad_add_fusion.where_ref, bf16[36,64,1024]{2,1,0:T(8,128)(2,1)S(1)} %get-tuple-element.27.refs_4_.taps, bf16[2304,256]{1,0:T(8,128)(2,1)S(1)} %get-tuple-element.28.w_ref, f32[1,256]{1,0:T(1,128)S(1)} %bitcast.14, f32[4,72,128]{2,1,0:T(8,128)S(1)} %join.1.refs_0_, ...), custom_call_target="tpu_custom_call" | custom-call | flops 3623878656 | bytes 8388608 | tf_op jit(solution)/shard_map/conv_pool/pallas_call | solution.py:222
  22.0 0.7 %collective-permute-done.5.traded_ref = bf16[48,768]{1,0:T(8,128)(2,1)S(1)} collective-permute-done((bf16[48,768]{1,0:T(8,128)(2,1)S(1)}, bf16[48,768]{1,0:T(8,128)(2,1)S(1)}, u32[]{:S(2)}, u32[]{:S(2)}) %collective-permute-start.5) | collective-permute-done | bytes 73760 | tf_op jit(solution)/shard_map/ppermute | solution.py:30
  22.7 1.3 %conv_edges.1.edge_ref = f32[4,2,24,128]{3,2,1,0:T(8,128)S(1)} custom-call(s32[4]{0:T(128)S(1)} %pad_add_fusion.where_ref, bf16[2304,256]{1,0:T(8,128)(2,1)S(1)} %get-tuple-element.28.w_ref, f32[1,256]{1,0:T(1,128)S(1)} %bitcast.15, bf16[48,768]{1,0:T(8,128)(2,1)S(1)} %collective-permute-done.refs_1_.got_ref, ...), custom_call_target="tpu_custom_call" | custom-call | bytes 4194304 | tf_op jit(solution)/shard_map/conv_edges/pallas_call | solution.py:248
  24.0 4.4 %deep_forward.1 = (bf16[26,64,768]{2,1,0:T(8,128)(2,1)S(1)}, bf16[24,64,128]{2,1,0:T(8,128)(2,1)S(1)}, f32[1536,128]{1,0:T(8,128)S(1)}, f32[32,128]{1,0:T(8,128)S(1)}) custom-call(s32[4]{0:T(128)S(1)} %pad_add_fusion.where_ref, bf16[12,64,256]{2,1,0:T(8,128)(2,1)S(1)} %conv_pool.1.refs_0_.own_ref, bf16[12,64,256]{2,1,0:T(8,128)(2,1)S(1)} %collective-permute-done.4.other_ref, ...), custom_call_target="tpu_custom_call" | custom-call | flops 1811939328 | bytes 8388608 | tf_op jit(solution)/shard_map/deep_forward/pallas_call | solution.py:457
  28.4 2.9 %deep_backward.1 = (f32[304,128]{1,0:T(8,128)S(1)}, f32[304,128]{1,0:T(8,128)S(1)}, f32[336,128]{1,0:T(8,128)S(1)}, f32[336,128]{1,0:T(8,128)S(1)}, f32[304,128]...) custom-call(s32[4]{0:T(128)S(1)} %pad_add_fusion.where_ref, ...), custom_call_target="tpu_custom_call" | custom-call | flops 1811939328 | bytes 8388608 | tf_op jit(solution)/shard_map/deep_backward/pallas_call | solution.py:541
  31.3 0.8 %collective-permute-start.10 = (f16[336,128]{1,0:T(8,128)(2,1)S(1)}, f16[336,128]{1,0:T(8,128)(2,1)S(1)}, u32[]{:S(2)}, u32[]{:S(2)}) collective-permute-start(f16[336,128]{1,0:T(8,128)(2,1)S(1)} %convert_element_type.79), channel_id=1, source_target_pairs={{0,4},{4,0},{8,12},{12,8},{16,20},{20,16},{24,28},{28,24},{1,5},{5... | collective-permute-start | bytes 258056 | tf_op jit(solution)/shard_map/ppermute | solution.py:30
  32.1 0.8 %collective-permute-start.8 = (f16[336,128]{1,0:T(8,128)(2,1)S(1)}, f16[336,128]{1,0:T(8,128)(2,1)S(1)}, u32[]{:S(2)}, u32[]{:S(2)}) collective-permute-start(f16[336,128]{1,0:T(8,128)(2,1)S(1)} %convert_element_type.75), channel_id=1, source_target_pairs={{0,8},{4,12},{8,0},{12,4},{16,24},{20,28},{24,16},{28,20},{1,9},{5... | collective-permute-start | bytes 258056 | tf_op jit(solution)/shard_map/ppermute | solution.py:30
  32.9 1.0 %collective-permute-start.12 = (f16[304,128]{1,0:T(8,128)(2,1)S(1)}, f16[304,128]{1,0:T(8,128)(2,1)S(1)}, u32[]{:S(2)}, u32[]{:S(2)}) collective-permute-start(f16[304,128]{1,0:T(8,128)(2,1)S(1)} %convert_element_type.83), channel_id=1, source_target_pairs={{0,4},{4,0},{8,12},{12,8},{16,20},{20,16},{24,28},{28,24},{1,5},{5... | collective-permute-start | bytes 233480 | tf_op jit(solution)/shard_map/ppermute | solution.py:30
  33.9 3.8 %collective-permute-done.12 = f16[304,128]{1,0:T(8,128)(2,1)S(1)} collective-permute-done((f16[304,128]{1,0:T(8,128)(2,1)S(1)}, f16[304,128]{1,0:T(8,128)(2,1)S(1)}, u32[]{:S(2)}, u32[]{:S(2)}) %collective-permute-start.12) | collective-permute-done | bytes 77856 | tf_op jit(solution)/shard_map/ppermute | solution.py:30
  37.8 2.7 %collective-permute-start.13 = (f16[368,128]{1,0:T(8,128)(2,1)S(1)}, f16[368,128]{1,0:T(8,128)(2,1)S(1)}, u32[]{:S(2)}, u32[]{:S(2)}) collective-permute-start(f16[368,128]{1,0:T(8,128)(2,1)S(1)} %convert_element_type.85), channel_id=1, source_target_pairs={{0,24},{4,28},{8,16},{12,20},{16,8},{20,12},{24,0},{28,4},{1,25},{... | collective-permute-start | bytes 282632 | tf_op jit(solution)/shard_map/ppermute | solution.py:30
  40.6 1.9 %collective-permute-start.9 = (f16[336,128]{1,0:T(8,128)(2,1)S(1)}, f16[336,128]{1,0:T(8,128)(2,1)S(1)}, u32[]{:S(2)}, u32[]{:S(2)}) collective-permute-start(f16[336,128]{1,0:T(8,128)(2,1)S(1)} %convert_element_type.77), channel_id=1, source_target_pairs={{0,12},{4,8},{8,4},{12,0},{16,28},{20,24},{24,20},{28,16},{1,13},{... | collective-permute-start | bytes 258056 | tf_op jit(solution)/shard_map/ppermute | solution.py:30
  42.5 1.4 %collective-permute-start.7 = (f16[304,128]{1,0:T(8,128)(2,1)S(1)}, f16[304,128]{1,0:T(8,128)(2,1)S(1)}, u32[]{:S(2)}, u32[]{:S(2)}) collective-permute-start(f16[304,128]{1,0:T(8,128)(2,1)S(1)} %convert_element_type.73), channel_id=1, source_target_pairs={{0,4},{4,0},{8,12},{12,8},{16,20},{20,16},{24,28},{28,24},{1,5},{5... | collective-permute-start | bytes 233480 | tf_op jit(solution)/shard_map/ppermute | solution.py:30
  44.0 3.3 %collective-permute-done.7 = f16[304,128]{1,0:T(8,128)(2,1)S(1)} collective-permute-done((f16[304,128]{1,0:T(8,128)(2,1)S(1)}, f16[304,128]{1,0:T(8,128)(2,1)S(1)}, u32[]{:S(2)}, u32[]{:S(2)}) %collective-permute-start.7) | collective-permute-done | bytes 77856 | tf_op jit(solution)/shard_map/ppermute | solution.py:30
  47.4 1.3 %collective-permute-done.11 = f16[368,128]{1,0:T(8,128)(2,1)S(1)} collective-permute-done((f16[368,128]{1,0:T(8,128)(2,1)S(1)}, f16[368,128]{1,0:T(8,128)(2,1)S(1)}, u32[]{:S(2)}, u32[]{:S(2)}) %collective-permute-start.11) | collective-permute-done | bytes 94240 | tf_op jit(solution)/shard_map/ppermute | solution.py:30
  48.6 0.7 %merge.1 = (f32[304,128]{1,0:T(8,128)S(1)}, f32[256,128]{1,0:T(8,128)S(1)}) custom-call(s32[4]{0:T(128)S(1)} %pad_add_fusion.where_ref, f32[304,128]{1,0:T(8,128)S(1)} %get-tuple-element.39.refs_0_, f32[304,128]{1,0:T(8,128)S(1)} %convert_element_type.74.refs_1_, f32[336,128]{1,0:T(8,128)S(1)} %convert_element_type.76.refs_0_.refs_2_, ...), custom_call_target="tpu_custom_call" | custom-call | tf_op jit(solution)/shard_map/merge/pallas_call | solution.py:637
  49.4 1.4 %collective-permute-start.17 = (f16[1,304,128]{2,1,0:T(8,128)(2,1)S(1)}, f16[1,304,128]{2,1,0:T(8,128)(2,1)S(1)}, u32[]{:S(2)}, u32[]{:S(2)}) collective-permute-start(f16[1,304,128]{2,1,0:T(8,128)(2,1)S(1)} %get-tuple-element.52), channel_id=1, source_target_pairs={{0,16},{4,20},{8,24},{12,28},{16,0},{20,4},{24,8},{28,12},{1,17},{... | collective-permute-start | bytes 233480 | tf_op jit(solution)/shard_map/ppermute | solution.py:30
  50.8 1.4 %collective-permute-start.19 = (f16[1,304,128]{2,1,0:T(8,128)(2,1)S(1)}, f16[1,304,128]{2,1,0:T(8,128)(2,1)S(1)}, u32[]{:S(2)}, u32[]{:S(2)}) collective-permute-start(f16[1,304,128]{2,1,0:T(8,128)(2,1)S(1)} %get-tuple-element.52), channel_id=1, source_target_pairs={{0,24},{4,28},{8,16},{12,20},{16,8},{20,12},{24,0},{28,4},{1,25},{... | collective-permute-start | bytes 233480 | tf_op jit(solution)/shard_map/ppermute | solution.py:30
  52.2 0.9 %collective-permute-start.16 = (f16[1,304,128]{2,1,0:T(8,128)(2,1)S(1)}, f16[1,304,128]{2,1,0:T(8,128)(2,1)S(1)}, u32[]{:S(2)}, u32[]{:S(2)}) collective-permute-start(f16[1,304,128]{2,1,0:T(8,128)(2,1)S(1)} %get-tuple-element.52), channel_id=1, source_target_pairs={{0,12},{4,8},{8,4},{12,0},{16,28},{20,24},{24,20},{28,16},{1,13},{... | collective-permute-start | bytes 233480 | tf_op jit(solution)/shard_map/ppermute | solution.py:30
  53.1 1.5 %collective-permute-start.15 = (f16[1,304,128]{2,1,0:T(8,128)(2,1)S(1)}, f16[1,304,128]{2,1,0:T(8,128)(2,1)S(1)}, u32[]{:S(2)}, u32[]{:S(2)}) collective-permute-start(f16[1,304,128]{2,1,0:T(8,128)(2,1)S(1)} %get-tuple-element.52), channel_id=1, source_target_pairs={{0,8},{4,12},{8,0},{12,4},{16,24},{20,28},{24,16},{28,20},{1,9},{5... | collective-permute-start | bytes 233480 | tf_op jit(solution)/shard_map/ppermute | solution.py:30
  54.5 1.2 %collective-permute-start.14 = (f16[1,304,128]{2,1,0:T(8,128)(2,1)S(1)}, f16[1,304,128]{2,1,0:T(8,128)(2,1)S(1)}, u32[]{:S(2)}, u32[]{:S(2)}) collective-permute-start(f16[1,304,128]{2,1,0:T(8,128)(2,1)S(1)} %get-tuple-element.52), channel_id=1, source_target_pairs={{0,4},{4,0},{8,12},{12,8},{16,20},{20,16},{24,28},{28,24},{1,5},{5... | collective-permute-start | bytes 233480 | tf_op jit(solution)/shard_map/ppermute | solution.py:30
  55.7 1.8 %collective-permute-done.17 = f16[1,304,128]{2,1,0:T(8,128)(2,1)S(1)} collective-permute-done((f16[1,304,128]{2,1,0:T(8,128)(2,1)S(1)}, f16[1,304,128]{2,1,0:T(8,128)(2,1)S(1)}, u32[]{:S(2)}, u32[]{:S(2)}) %collective-permute-start.17) | collective-permute-done | bytes 77856 | tf_op jit(solution)/shard_map/ppermute | solution.py:30
  57.7 1.8 %collective-permute-start.20 = (f16[1,304,128]{2,1,0:T(8,128)(2,1)S(1)}, f16[1,304,128]{2,1,0:T(8,128)(2,1)S(1)}, u32[]{:S(2)}, u32[]{:S(2)}) collective-permute-start(f16[1,304,128]{2,1,0:T(8,128)(2,1)S(1)} %collective-permute-done.19), channel_id=1, source_target_pairs={{0,4},{4,0},{8,12},{12,8},{16,20},{20,16},{24,28},{28,24},{1,5},{5... | collective-permute-start | bytes 233480 | tf_op jit(solution)/shard_map/ppermute | solution.py:30
  59.5 1.5 %embed.1 = f32[64,128]{1,0:T(8,128)} custom-call(s32[4]{0:T(128)S(1)} %pad_add_fusion.where_ref, f32[256,128]{1,0:T(8,128)S(1)} %get-tuple-element.47.sums_ref, f32[4,72,128]{2,1,0:T(8,128)S(1)} %join.1.refs_0_, f32[4,72,128]{2,1,0:T(8,128)S(1)} %collective-permute-done.6.refs_1_), custom_call_target="tpu_custom_call" | custom-call | tf_op jit(solution)/shard_map/embed/pallas_call | solution.py:791
  61.2 0.7 %collective-permute-done.18 = f16[1,304,128]{2,1,0:T(8,128)(2,1)S(1)} collective-permute-done((f16[1,304,128]{2,1,0:T(8,128)(2,1)S(1)}, f16[1,304,128]{2,1,0:T(8,128)(2,1)S(1)}, u32[]{:S(2)}, u32[]{:S(2)}) %collective-permute-start.18) | collective-permute-done | bytes 77856 | tf_op jit(solution)/shard_map/ppermute | solution.py:30
  61.9 0.8 %collective-permute-done.20 = f16[1,304,128]{2,1,0:T(8,128)(2,1)S(1)} collective-permute-done((f16[1,304,128]{2,1,0:T(8,128)(2,1)S(1)}, f16[1,304,128]{2,1,0:T(8,128)(2,1)S(1)}, u32[]{:S(2)}, u32[]{:S(2)}) %collective-permute-start.20) | collective-permute-done | bytes 77856 | tf_op jit(solution)/shard_map/ppermute | solution.py:30
  62.7 1.7 %spread.1 = (f32[2304,128]{1,0:T(8,128)}, f32[1,128]{1,0:T(1,128)}) custom-call(s32[4]{0:T(128)S(1)} %pad_add_fusion.where_ref, f32[1,304,128]{2,1,0:T(8,128)S(1)} %get-tuple-element.51.refs_0_, f32[1,304,128]{2,1,0:T(8,128)S(1)} %convert_element_type.90.refs_1_, f32[1,304,128]{2,1,0:T(8,128)S(1)} %convert_element_type.91.refs_2_, ...), custom_call_target="tpu_custom_call" | custom-call | tf_op jit(solution)/shard_map/spread/pallas_call | solution.py:696
  (53 shorter events, 2.0 us)
Async XLA Ops:
  2.7 13.4 %collective-permute-start = (bf16[48,768]{1,0:T(8,128)(2,1)S(1)}, bf16[48,768]{1,0:T(8,128)(2,1)S(1)}, u32[]{:S(2)}, u32[]{:S(2)}) collective-permute-start(bf16[48,768]{1,0:T(8,128)(2,1)S(1)} %get-tuple-element.29), channel_id=1, source_target_pairs={{0,4},{2,6},{4,8},{5,1},{6,10},{7,3},{8,12},{9,5},{10,14},{11,7},{... | collective-permute-start | bytes 221192 | tf_op jit(solution)/shard_map/ppermute | solution.py:731
  7.5 7.0 %collective-permute-start.3 = (f32[1,72,128]{2,1,0:T(8,128)S(1)}, f32[1,72,128]{2,1,0:T(8,128)S(1)}, u32[]{:S(2)}, u32[]{:S(2)}) collective-permute-start(f32[1,72,128]{2,1,0:T(8,128)S(1)} %get-tuple-element.30.refs_0_), channel_id=1, source_target_pairs={{0,24},{4,28},{8,16},{12,20},{16,8},{20,12},{24,0},{28,4},{1,25},{... | collective-permute-start | bytes 110600 | tf_op jit(solution)/shard_map/ppermute | solution.py:30
  11.2 4.9 %collective-permute-start.2 = (f32[1,72,128]{2,1,0:T(8,128)S(1)}, f32[1,72,128]{2,1,0:T(8,128)S(1)}, u32[]{:S(2)}, u32[]{:S(2)}) collective-permute-start(f32[1,72,128]{2,1,0:T(8,128)S(1)} %get-tuple-element.30.refs_0_), channel_id=1, source_target_pairs={{0,16},{4,20},{8,24},{12,28},{16,0},{20,4},{24,8},{28,12},{1,17},{... | collective-permute-start | bytes 110600 | tf_op jit(solution)/shard_map/ppermute | solution.py:30
  11.2 4.9 %collective-permute-start.1 = (f32[1,72,128]{2,1,0:T(8,128)S(1)}, f32[1,72,128]{2,1,0:T(8,128)S(1)}, u32[]{:S(2)}, u32[]{:S(2)}) collective-permute-start(f32[1,72,128]{2,1,0:T(8,128)S(1)} %get-tuple-element.30.refs_0_), channel_id=1, source_target_pairs={{0,8},{4,12},{8,0},{12,4},{16,24},{20,28},{24,16},{28,20},{1,9},{5... | collective-permute-start | bytes 110600 | tf_op jit(solution)/shard_map/ppermute | solution.py:30
  14.5 1.6 %copy-start.1 = (f32[256]{0:T(256)S(1)}, f32[256]{0:T(256)}, u32[]{:S(2)}) copy-start(f32[256]{0:T(256)} %param.10) | copy-start | bytes 3076
  16.1 7.9 %copy-start = (s32[24,64]{1,0:T(8,128)S(1)}, s32[24,64]{1,0:T(8,128)}, u32[]{:S(2)}) copy-start(s32[24,64]{1,0:T(8,128)} %lab_ref.1) | copy-start | bytes 18436
  16.1 7.9 %copy-start.2 = (bf16[3,3,256,128]{3,2,1,0:T(8,128)(2,1)S(1)}, bf16[3,3,256,128]{3,2,1,0:T(8,128)(2,1)}, u32[]{:S(2)}) copy-start(bf16[3,3,256,128]{3,2,1,0:T(8,128)(2,1)} %param.11) | copy-start | bytes 1769476
  16.1 7.9 %copy-start.3 = (f32[128]{0:T(128)S(1)}, f32[128]{0:T(128)}, u32[]{:S(2)}) copy-start(f32[128]{0:T(128)} %param.12) | copy-start | bytes 1540
  20.8 3.2 %collective-permute-start.4 = (bf16[12,64,256]{2,1,0:T(8,128)(2,1)S(1)}, bf16[12,64,256]{2,1,0:T(8,128)(2,1)S(1)}, u32[]{:S(2)}, u32[]{:S(2)}) collective-permute-start(bf16[12,64,256]{2,1,0:T(8,128)(2,1)S(1)} %conv_pool.1.refs_0_.own_ref), channel_id=1, source_target_pairs={{0,1},{1,0},{2,3},{3,2},{4,5},{5,4},{6,7},{7,6},{8,9},{9,8},{10,11... | collective-permute-start | bytes 1179656 | tf_op jit(solution)/shard_map/ppermute | solution.py:30
  20.9 1.8 %collective-permute-start.5 = (bf16[48,768]{1,0:T(8,128)(2,1)S(1)}, bf16[48,768]{1,0:T(8,128)(2,1)S(1)}, u32[]{:S(2)}, u32[]{:S(2)}) collective-permute-start(bf16[48,768]{1,0:T(8,128)(2,1)S(1)} %collective-permute-done.refs_1_.got_ref), channel_id=1, source_target_pairs={{0,1},{1,0},{2,3},{3,2},{4,5},{5,4},{6,7},{7,6},{8,9},{9,8},{10,11... | collective-permute-start | bytes 221192 | tf_op jit(solution)/shard_map/ppermute | solution.py:30
  21.4 7.0 %collective-permute-start.6 = (f32[4,72,128]{2,1,0:T(8,128)S(1)}, f32[4,72,128]{2,1,0:T(8,128)S(1)}, u32[]{:S(2)}, u32[]{:S(2)}) collective-permute-start(f32[4,72,128]{2,1,0:T(8,128)S(1)} %join.1.refs_0_), channel_id=1, source_target_pairs={{0,4},{4,0},{8,12},{12,8},{16,20},{20,16},{24,28},{28,24},{1,5},{5... | collective-permute-start | bytes 442376 | tf_op jit(solution)/shard_map/ppermute | solution.py:30
  31.3 6.3 %collective-permute-start.10 = (f16[336,128]{1,0:T(8,128)(2,1)S(1)}, f16[336,128]{1,0:T(8,128)(2,1)S(1)}, u32[]{:S(2)}, u32[]{:S(2)}) collective-permute-start(f16[336,128]{1,0:T(8,128)(2,1)S(1)} %convert_element_type.79), channel_id=1, source_target_pairs={{0,4},{4,0},{8,12},{12,8},{16,20},{20,16},{24,28},{28,24},{1,5},{5... | collective-permute-start | bytes 258056 | tf_op jit(solution)/shard_map/ppermute | solution.py:30
  32.1 5.6 %collective-permute-start.8 = (f16[336,128]{1,0:T(8,128)(2,1)S(1)}, f16[336,128]{1,0:T(8,128)(2,1)S(1)}, u32[]{:S(2)}, u32[]{:S(2)}) collective-permute-start(f16[336,128]{1,0:T(8,128)(2,1)S(1)} %convert_element_type.75), channel_id=1, source_target_pairs={{0,8},{4,12},{8,0},{12,4},{16,24},{20,28},{24,16},{28,20},{1,9},{5... | collective-permute-start | bytes 258056 | tf_op jit(solution)/shard_map/ppermute | solution.py:30
  32.9 4.7 %collective-permute-start.12 = (f16[304,128]{1,0:T(8,128)(2,1)S(1)}, f16[304,128]{1,0:T(8,128)(2,1)S(1)}, u32[]{:S(2)}, u32[]{:S(2)}) collective-permute-start(f16[304,128]{1,0:T(8,128)(2,1)S(1)} %convert_element_type.83), channel_id=1, source_target_pairs={{0,4},{4,0},{8,12},{12,8},{16,20},{20,16},{24,28},{28,24},{1,5},{5... | collective-permute-start | bytes 233480 | tf_op jit(solution)/shard_map/ppermute | solution.py:30
  37.8 9.5 %collective-permute-start.13 = (f16[368,128]{1,0:T(8,128)(2,1)S(1)}, f16[368,128]{1,0:T(8,128)(2,1)S(1)}, u32[]{:S(2)}, u32[]{:S(2)}) collective-permute-start(f16[368,128]{1,0:T(8,128)(2,1)S(1)} %convert_element_type.85), channel_id=1, source_target_pairs={{0,24},{4,28},{8,16},{12,20},{16,8},{20,12},{24,0},{28,4},{1,25},{... | collective-permute-start | bytes 282632 | tf_op jit(solution)/shard_map/ppermute | solution.py:30
  40.5 8.1 %collective-permute-start.11 = (f16[368,128]{1,0:T(8,128)(2,1)S(1)}, f16[368,128]{1,0:T(8,128)(2,1)S(1)}, u32[]{:S(2)}, u32[]{:S(2)}) collective-permute-start(f16[368,128]{1,0:T(8,128)(2,1)S(1)} %convert_element_type.81), channel_id=1, source_target_pairs={{0,16},{4,20},{8,24},{12,28},{16,0},{20,4},{24,8},{28,12},{1,17},{... | collective-permute-start | bytes 282632 | tf_op jit(solution)/shard_map/ppermute | solution.py:30
  40.6 6.7 %collective-permute-start.9 = (f16[336,128]{1,0:T(8,128)(2,1)S(1)}, f16[336,128]{1,0:T(8,128)(2,1)S(1)}, u32[]{:S(2)}, u32[]{:S(2)}) collective-permute-start(f16[336,128]{1,0:T(8,128)(2,1)S(1)} %convert_element_type.77), channel_id=1, source_target_pairs={{0,12},{4,8},{8,4},{12,0},{16,28},{20,24},{24,20},{28,16},{1,13},{... | collective-permute-start | bytes 258056 | tf_op jit(solution)/shard_map/ppermute | solution.py:30
  42.5 4.8 %collective-permute-start.7 = (f16[304,128]{1,0:T(8,128)(2,1)S(1)}, f16[304,128]{1,0:T(8,128)(2,1)S(1)}, u32[]{:S(2)}, u32[]{:S(2)}) collective-permute-start(f16[304,128]{1,0:T(8,128)(2,1)S(1)} %convert_element_type.73), channel_id=1, source_target_pairs={{0,4},{4,0},{8,12},{12,8},{16,20},{20,16},{24,28},{28,24},{1,5},{5... | collective-permute-start | bytes 233480 | tf_op jit(solution)/shard_map/ppermute | solution.py:30
  49.4 8.1 %collective-permute-start.17 = (f16[1,304,128]{2,1,0:T(8,128)(2,1)S(1)}, f16[1,304,128]{2,1,0:T(8,128)(2,1)S(1)}, u32[]{:S(2)}, u32[]{:S(2)}) collective-permute-start(f16[1,304,128]{2,1,0:T(8,128)(2,1)S(1)} %get-tuple-element.52), channel_id=1, source_target_pairs={{0,16},{4,20},{8,24},{12,28},{16,0},{20,4},{24,8},{28,12},{1,17},{... | collective-permute-start | bytes 233480 | tf_op jit(solution)/shard_map/ppermute | solution.py:30
  50.8 6.9 %collective-permute-start.19 = (f16[1,304,128]{2,1,0:T(8,128)(2,1)S(1)}, f16[1,304,128]{2,1,0:T(8,128)(2,1)S(1)}, u32[]{:S(2)}, u32[]{:S(2)}) collective-permute-start(f16[1,304,128]{2,1,0:T(8,128)(2,1)S(1)} %get-tuple-element.52), channel_id=1, source_target_pairs={{0,24},{4,28},{8,16},{12,20},{16,8},{20,12},{24,0},{28,4},{1,25},{... | collective-permute-start | bytes 233480 | tf_op jit(solution)/shard_map/ppermute | solution.py:30
  52.2 8.9 %collective-permute-start.16 = (f16[1,304,128]{2,1,0:T(8,128)(2,1)S(1)}, f16[1,304,128]{2,1,0:T(8,128)(2,1)S(1)}, u32[]{:S(2)}, u32[]{:S(2)}) collective-permute-start(f16[1,304,128]{2,1,0:T(8,128)(2,1)S(1)} %get-tuple-element.52), channel_id=1, source_target_pairs={{0,12},{4,8},{8,4},{12,0},{16,28},{20,24},{24,20},{28,16},{1,13},{... | collective-permute-start | bytes 233480 | tf_op jit(solution)/shard_map/ppermute | solution.py:30
  53.1 8.0 %collective-permute-start.15 = (f16[1,304,128]{2,1,0:T(8,128)(2,1)S(1)}, f16[1,304,128]{2,1,0:T(8,128)(2,1)S(1)}, u32[]{:S(2)}, u32[]{:S(2)}) collective-permute-start(f16[1,304,128]{2,1,0:T(8,128)(2,1)S(1)} %get-tuple-element.52), channel_id=1, source_target_pairs={{0,8},{4,12},{8,0},{12,4},{16,24},{20,28},{24,16},{28,20},{1,9},{5... | collective-permute-start | bytes 233480 | tf_op jit(solution)/shard_map/ppermute | solution.py:30
  54.5 6.6 %collective-permute-start.14 = (f16[1,304,128]{2,1,0:T(8,128)(2,1)S(1)}, f16[1,304,128]{2,1,0:T(8,128)(2,1)S(1)}, u32[]{:S(2)}, u32[]{:S(2)}) collective-permute-start(f16[1,304,128]{2,1,0:T(8,128)(2,1)S(1)} %get-tuple-element.52), channel_id=1, source_target_pairs={{0,4},{4,0},{8,12},{12,8},{16,20},{20,16},{24,28},{28,24},{1,5},{5... | collective-permute-start | bytes 233480 | tf_op jit(solution)/shard_map/ppermute | solution.py:30
  57.5 4.4 %collective-permute-start.18 = (f16[1,304,128]{2,1,0:T(8,128)(2,1)S(1)}, f16[1,304,128]{2,1,0:T(8,128)(2,1)S(1)}, u32[]{:S(2)}, u32[]{:S(2)}) collective-permute-start(f16[1,304,128]{2,1,0:T(8,128)(2,1)S(1)} %collective-permute-done.17), channel_id=1, source_target_pairs={{0,4},{4,0},{8,12},{12,8},{16,20},{20,16},{24,28},{28,24},{1,5},{5... | collective-permute-start | bytes 233480 | tf_op jit(solution)/shard_map/ppermute | solution.py:30
  57.7 5.0 %collective-permute-start.20 = (f16[1,304,128]{2,1,0:T(8,128)(2,1)S(1)}, f16[1,304,128]{2,1,0:T(8,128)(2,1)S(1)}, u32[]{:S(2)}, u32[]{:S(2)}) collective-permute-start(f16[1,304,128]{2,1,0:T(8,128)(2,1)S(1)} %collective-permute-done.19), channel_id=1, source_target_pairs={{0,4},{4,0},{8,12},{12,8},{16,20},{20,16},{24,28},{28,24},{1,5},{5... | collective-permute-start | bytes 233480 | tf_op jit(solution)/shard_map/ppermute | solution.py:30

commit v8 on v7

--- a/solution.py
+++ b/solution.py
@@ -30,22 +30,9 @@
     return lax.ppermute(value, axis, [(i, i ^ mask) for i in range(count)])
 
 
-def bit_groups(count, first, most):
-    bits = count.bit_length() - 1
-    groups, at = [], 0
-    while at < bits:
-        size = min(first if at == 0 else most, bits - at)
-        groups.append((at, size))
-        at += size
-    return groups
-
-
-def gather_groups(value, axis, groups):
-    parts = [value]
-    for shift, size in groups:
-        held = parts[0] if len(parts) == 1 else jnp.concatenate(parts, axis=0)
-        parts = [held] + [swap(held, axis, m << shift) for m in range(1, 1 << size)]
-    return parts
+def gather_step(held, axis, step):
+    shift, size = step
+    return [held] + [swap(held, axis, m << shift) for m in range(1, 1 << size)]
 
 
 def relative(refs):
@@ -56,10 +43,6 @@
             for k in range(ref.shape[0]):
                 yield m, ref, k
                 m += 2
-
-
-def high_groups(count):
-    return [(at + 1, size) for at, size in bit_groups(count // 2, 2, 2)]
 
 
 def shares(pooled_rows):
@@ -671,37 +654,81 @@
     out_ref[...] = sums / jnp.maximum(counts, 1.0)
 
 
-def spread_kernel(where_ref, *refs, chunk, rows):
-    part_refs, weight_ref, bias_ref, place = refs[:-3], refs[-3], refs[-2], refs[-1]
+def spread_kernel(where_ref, *refs, chunk, members):
+    count = len(members)
+    part_refs, before = refs[:count], refs[count:-4]
+    weight_hbm, bias_ref, place, sems = refs[-4:]
     me = where_ref[3]
-    whole = rows == place.shape[0]
-    count = len(part_refs)
-    for k, m in itertools.product(range(part_refs[0].shape[0]), range(count)):
-        ref = part_refs[m]
-        bias, down, _ = read_note(ref[k], chunk)
-        j = me ^ (m + k * count)
-        target = weight_ref if whole else place
-        target[pl.ds(pl.multiple_of(j * chunk, 8), chunk)] = ref[k, :chunk] * down
+    bias_ref[...] = before[1][...] if before else jnp.zeros_like(bias_ref)
+    copies = []
+    for p, m in enumerate(members):
+        bias, down, _ = read_note(part_refs[p][0], chunk)
+        place[p * chunk : (p + 1) * chunk] = part_refs[p][0, :chunk] * down
+        j = me ^ m
+        copies.append(
+            pltpu.make_async_copy(
+                place.at[pl.ds(p * chunk, chunk)],
+                weight_hbm.at[pl.ds(pl.multiple_of(j * chunk, 8), chunk)],
+                sems.at[p],
+            )
+        )
+        copies[p].start()
 
         @pl.when(j == 0)
         def _():
             bias_ref[...] = bias
 
-    if not whole:
-        weight_ref[...] = place[:rows]
-
-
-def spread(where, parts, chunk, count, rows):
+    for copy in copies:
+        copy.wait()
+
+
+def spread(where, parts, before, chunk, count, rows):
+    parts = {m: part.astype(F32) for m, part in parts.items()}
+    width = next(iter(parts.values())).shape[-1]
+    before = list(before)
+    return pl.pallas_call(
+        functools.partial(spread_kernel, chunk=chunk, members=tuple(parts)),
+        out_shape=(jax.ShapeDtypeStruct((rows, width), F32), jax.ShapeDtypeStruct((1, width), F32)),
+        in_specs=[SMEM] + [VMEM] * len(parts) + ([HBM, VMEM] if before else []),
+        out_specs=(HBM, VMEM),
+        scratch_shapes=[
+            pltpu.VMEM((len(parts) * chunk, width), F32),
+            pltpu.SemaphoreType.DMA((len(parts),)),
+        ],
+        input_output_aliases={1 + len(parts): 0} if before else {},
+        compiler_params=params(),
+        name="spread",
+    )(where, *parts.values(), *before)
+
+
+def spread_all_kernel(where_ref, *refs, chunk, rows, members):
+    part_refs, weight_ref, bias_ref, place = refs[:-3], refs[-3], refs[-2], refs[-1]
+    me = where_ref[3]
+    count = len(members)
+    for p, k in itertools.product(range(count), range(part_refs[0].shape[0])):
+        bias, down, _ = read_note(part_refs[p][k], chunk)
+        j = me ^ (members[p] + k * count)
+        place[pl.ds(pl.multiple_of(j * chunk, 8), chunk)] = part_refs[p][k, :chunk] * down
+
+        @pl.when(j == 0)
+        def _():
+            bias_ref[...] = bias
+
+    weight_ref[...] = place[:rows]
+
+
+def spread_all(where, parts, chunk, count, rows):
+    parts = {m: part.astype(F32) for m, part in parts.items()}
     width = parts[0].shape[-1]
     return pl.pallas_call(
-        functools.partial(spread_kernel, chunk=chunk, rows=rows),
+        functools.partial(spread_all_kernel, chunk=chunk, rows=rows, members=tuple(parts)),
         out_shape=(jax.ShapeDtypeStruct((rows, width), F32), jax.ShapeDtypeStruct((1, width), F32)),
         in_specs=[SMEM] + [VMEM] * len(parts),
         out_specs=(VMEM, VMEM),
         scratch_shapes=[pltpu.VMEM((count * chunk, width), F32)],
         compiler_params=params(),
-        name="spread",
-    )(where, *parts)
+        name="spread_all",
+    )(where, *parts.values())
 
 
 def body(
@@ -730,14 +757,20 @@
                 pairs.append((s * chan_count + c, to * chan_count + c))
     got = lax.ppermute(sent, ("strip", "chan"), pairs)
 
-    shared = gather_groups(side, "strip", high_groups(strip_count))
-
+    steps = [(at + 1, 1) for at in range(min(2, strip_count.bit_length() - 2))]
+    steps += [(at, min(3, strip_count.bit_length() - 1 - at)) for at in range(3, strip_count.bit_length() - 1, 3)]
+    ahead = gather_step(side, "strip", steps[0])
     taps, near_w = windows(where, section_input, conv_w)
-    got, joined = lax.optimization_barrier((got, join(shared, [taps])))
+    shared = join(ahead, [taps])
+    got, shared = lax.optimization_barrier((got, shared))
     traded = swap(got, "chan", 1)
-    shared = [joined, swap(joined, "strip", 1)]
-    pooled = conv_pool(where, taps, near_w, conv_b, section_input.shape[0] // 4, [joined, got])
+    ahead = gather_step(shared, "strip", steps[1])
+    pooled = conv_pool(where, taps, near_w, conv_b, section_input.shape[0] // 4, [shared, got])
+    pooled, shared = lax.optimization_barrier((pooled, join(ahead, [pooled])))
     other = swap(pooled, "chan", 1)
+    for step in steps[2:]:
+        shared = join(gather_step(shared, "strip", step), [])
+    shared = [shared, swap(shared, "strip", 1)]
     edges = conv_edges(where, near_w, conv_b, got, traded, head, tail, [pooled])
 
     chunk = -(-9 * channels // strip_count // 8) * 8
@@ -796,16 +829,19 @@
         compiler_params=params(),
         name="embed",
     )(where, sums, *shared)
-    high = [(at, min(3, bits - at)) for at in range(ways.bit_length() - 1, bits, 3)]
-    own = gather_groups(send[0].astype(F16)[None], "strip", high)
-    own = own[0] if len(own) == 1 else jnp.concatenate(own, axis=0)
-    gathered = [own] + [swap(own, "strip", m) for m in range(1, min(4, ways))]
+    own = send[0].astype(F16)[None]
+    for at in range(ways.bit_length() - 1, bits, 3):
+        own = jnp.concatenate(gather_step(own, "strip", (at, min(3, bits - at))), axis=0)
+    gathered = {m: swap(own, "strip", m) if m else own for m in range(min(4, ways))}
     for k in far:
-        direct = swap(own, "strip", 2 * k)
-        gathered += [direct, swap(direct, "strip", 1)]
-    weight_rows, bias_row = spread(
-        where, [g.astype(F32) for g in gathered], chunk, strip_count, 9 * channels
-    )
+        gathered[2 * k] = swap(own, "strip", 2 * k)
+    late = {2 * k + 1: swap(gathered[2 * k], "strip", 1) for k in far}
+    rows = 9 * channels
+    if strip_count * chunk == rows and late:
+        result = spread(where, gathered, [], chunk, strip_count, rows)
+        weight_rows, bias_row = spread(where, late, result, chunk, strip_count, rows)
+    else:
+        weight_rows, bias_row = spread_all(where, {**gathered, **late}, chunk, strip_count, rows)
     return (embeddings, weight_rows.reshape(3, 3, channels, width), bias_row[0])
 
 

time: 64.7 us -> 63.4 us (0.980)
  waiting for transfers between devices: 13.9 us -> 8.85 us
  starting transfers between devices: 27.4 us -> 29.5 us
  Pallas kernels: 21.7 us -> 23.3 us
    ppermute x20 -> x19, waiting for transfers between devices: 13.9 us -> 8.85 us  [swap(): return lax.ppermute(value, axis, [(i, i ^ mask) for i in range(count)])]
    ppermute x20 -> x19, starting transfers between devices: 22.5 us -> 24.7 us  [swap(): return lax.ppermute(value, axis, [(i, i ^ mask) for i in range(count)])]
    pallas_call x1 -> x2, Pallas kernels: 1.71 us -> 3.32 us  [spread(): pl.pallas_call(functools.partial(spread_kernel, chunk=chunk, members=tupl...]
  transfers between devices with their start and end apart: 21 -> 20, of which waited for: 8 -> 5; matrix products, arithmetic and copies ran while one was open for 0% -> 0% of each run, Pallas kernels for 15% -> 25%
where the time goes in v8:
time: 63.4 us; the launch traced here: 63.2 us
  starting transfers between devices  29.5 us (47%)
  Pallas kernels  23.3 us (37%)
  waiting for transfers between devices  8.85 us (14%)
  between operations  1.06 us (2%)
    ppermute x19, starting transfers between devices, swap(): return lax.ppermute(value, axis, [(i, i ^ mask) for i in range(count)])  24.7 us
    ppermute x19, waiting for transfers between devices, swap(): return lax.ppermute(value, axis, [(i, i ^ mask) for i in range(count)])  8.85 us
    ppermute x1, starting transfers between devices, body(): got = lax.ppermute(sent, ('strip', 'chan'), pairs)  4.85 us
    pallas_call x1, Pallas kernels, conv_pool(): pl.pallas_call(conv_kernel, out_shape=jax.ShapeDtypeStruct((pooled_rows,...  4.7 us
    pallas_call x1, Pallas kernels, deep_forward(): pl.pallas_call(functools.partial(deep_kernel, block=block, entries=entrie...  4.41 us
    pallas_call x2, Pallas kernels, spread(): pl.pallas_call(functools.partial(spread_kernel, chunk=chunk, members=tupl...  3.32 us
    pallas_call x1, Pallas kernels, deep_backward(): pl.pallas_call(functools.partial(grad_kernel, n_parts=len(parts), chunk=c...  2.86 us
    pallas_call x1, Pallas kernels, windows(): pl.pallas_call(window_kernel, out_shape=(jax.ShapeDtypeStruct(((most + 2)...  2.51 us
  transfers between devices with their start and end apart: 20, of which 5 were waited for; matrix products, arithmetic and copies ran while one was open for 0% of the time, Pallas kernels for 25%

profile of v8, /device:TPU:0, one launch (start us, length us, event | category | flops | bytes accessed | tf_op | source)
XLA Modules:
  0.0 63.2 jit_solution(18261425375237677892)
XLA Ops:
  0.7 1.9 %start.1 = (f32[1,72,128]{2,1,0:T(8,128)S(1)}, bf16[48,768]{1,0:T(8,128)(2,1)S(1)}, bf16[48,768]{1,0:T(8,128)(2,1)S(1)}, bf16[48,768]{1,0:T(8,128)(2,1)S(1)}) custom-call(s32[4]{0:T(128)S(1)} %pad_add_fusion.where_ref, bf16[48,128,256]{2,1,0:T(8,128)(2,1)} %x_hbm.3, f32[64,128]{1,0:T(8,128)} %grad_hbm.1, s32[24,64]{1,0:T(8,128)} %lab_ref.1, s32[1,32]{1,0:T(1,128)} %bitcast.20), custom_call_target="tpu_custom_call" | custom-call | tf_op jit(solution)/shard_map/start/pallas_call | solution.py:300
  2.7 4.8 %collective-permute-start = (bf16[48,768]{1,0:T(8,128)(2,1)S(1)}, bf16[48,768]{1,0:T(8,128)(2,1)S(1)}, u32[]{:S(2)}, u32[]{:S(2)}) collective-permute-start(bf16[48,768]{1,0:T(8,128)(2,1)S(1)} %get-tuple-element.33), channel_id=1, source_target_pairs={{0,4},{2,6},{4,8},{5,1},{6,10},{7,3},{8,12},{9,5},{10,14},{11,7},{... | collective-permute-start | bytes 221192 | tf_op jit(solution)/shard_map/ppermute | solution.py:758
  7.5 1.6 %collective-permute-start.1 = (f32[1,72,128]{2,1,0:T(8,128)S(1)}, f32[1,72,128]{2,1,0:T(8,128)S(1)}, u32[]{:S(2)}, u32[]{:S(2)}) collective-permute-start(f32[1,72,128]{2,1,0:T(8,128)S(1)} %get-tuple-element.34.refs_0_), channel_id=1, source_target_pairs={{0,8},{4,12},{8,0},{12,4},{16,24},{20,28},{24,16},{28,20},{1,9},{5... | collective-permute-start | bytes 110600 | tf_op jit(solution)/shard_map/ppermute | solution.py:30
  9.2 2.5 %windows.1 = (bf16[36,64,1024]{2,1,0:T(8,128)(2,1)S(1)}, bf16[2304,256]{1,0:T(8,128)(2,1)S(1)}) custom-call(s32[4]{0:T(128)S(1)} %pad_add_fusion.where_ref, bf16[48,128,256]{2,1,0:T(8,128)(2,1)} %x_hbm.3, bf16[2304,256]{1,0:T(8,128)(2,1)} %bitcast.18), custom_call_target="tpu_custom_call" | custom-call | bytes 12582912 | tf_op jit(solution)/shard_map/windows/pallas_call | solution.py:110
  11.7 2.7 %collective-permute-start.2 = (f32[2,72,128]{2,1,0:T(8,128)S(1)}, f32[2,72,128]{2,1,0:T(8,128)S(1)}, u32[]{:S(2)}, u32[]{:S(2)}) collective-permute-start(f32[2,72,128]{2,1,0:T(8,128)S(1)} %join.2.refs_0_), channel_id=1, source_target_pairs={{0,16},{4,20},{8,24},{12,28},{16,0},{20,4},{24,8},{28,12},{1,17},{... | collective-permute-start | bytes 221192 | tf_op jit(solution)/shard_map/ppermute | solution.py:30
  14.4 4.7 %conv_pool.1.refs_2_.refs_0_.own_ref = bf16[12,64,256]{2,1,0:T(8,128)(2,1)S(1)} custom-call(s32[4]{0:T(128)S(1)} %pad_add_fusion.where_ref, bf16[36,64,1024]{2,1,0:T(8,128)(2,1)S(1)} %get-tuple-element.31.refs_2_.taps, bf16[2304,256]{1,0:T(8,128)(2,1)S(1)} %get-tuple-element.32.w_ref, f32[1,256]{1,0:T(1,128)S(1)} %bitcast.14, ...), custom_call_target="tpu_custom_call" | custom-call | flops 3623878656 | bytes 8388608 | tf_op jit(solution)/shard_map/conv_pool/pallas_call | solution.py:205
  19.2 0.5 collective-permute-start.4
  19.7 1.4 %collective-permute-start.5 = (f32[4,72,128]{2,1,0:T(8,128)S(1)}, f32[4,72,128]{2,1,0:T(8,128)S(1)}, u32[]{:S(2)}, u32[]{:S(2)}) collective-permute-start(f32[4,72,128]{2,1,0:T(8,128)S(1)} %join.3.refs_0_), channel_id=1, source_target_pairs={{0,4},{4,0},{8,12},{12,8},{16,20},{20,16},{24,28},{28,24},{1,5},{5... | collective-permute-start | bytes 442376 | tf_op jit(solution)/shard_map/ppermute | solution.py:30
  21.1 1.3 %conv_edges.1.edge_ref = f32[4,2,24,128]{3,2,1,0:T(8,128)S(1)} custom-call(s32[4]{0:T(128)S(1)} %pad_add_fusion.where_ref, bf16[2304,256]{1,0:T(8,128)(2,1)S(1)} %get-tuple-element.32.w_ref, f32[1,256]{1,0:T(1,128)S(1)} %bitcast.15, bf16[48,768]{1,0:T(8,128)(2,1)S(1)} %collective-permute-done.refs_1_.got_ref, ...), custom_call_target="tpu_custom_call" | custom-call | bytes 4194304 | tf_op jit(solution)/shard_map/conv_edges/pallas_call | solution.py:231
  22.4 4.4 %deep_forward.1 = (bf16[26,64,768]{2,1,0:T(8,128)(2,1)S(1)}, bf16[24,64,128]{2,1,0:T(8,128)(2,1)S(1)}, f32[1536,128]{1,0:T(8,128)S(1)}, f32[32,128]{1,0:T(8,128)S(1)}) custom-call(s32[4]{0:T(128)S(1)} %pad_add_fusion.where_ref, bf16[12,64,256]{2,1,0:T(8,128)(2,1)S(1)} %conv_pool.1.refs_2_.refs_0_.own_ref, ...), custom_call_target="tpu_custom_call" | custom-call | flops 1811939328 | bytes 8388608 | tf_op jit(solution)/shard_map/deep_forward/pallas_call | solution.py:440
  26.9 2.9 %deep_backward.1 = (f32[304,128]{1,0:T(8,128)S(1)}, f32[304,128]{1,0:T(8,128)S(1)}, f32[336,128]{1,0:T(8,128)S(1)}, f32[336,128]{1,0:T(8,128)S(1)}, f32[304,128]...) custom-call(s32[4]{0:T(128)S(1)} %pad_add_fusion.where_ref, ...), custom_call_target="tpu_custom_call" | custom-call | flops 1811939328 | bytes 8388608 | tf_op jit(solution)/shard_map/deep_backward/pallas_call | solution.py:524
  29.8 1.4 %collective-permute-start.9 = (f16[336,128]{1,0:T(8,128)(2,1)S(1)}, f16[336,128]{1,0:T(8,128)(2,1)S(1)}, u32[]{:S(2)}, u32[]{:S(2)}) collective-permute-start(f16[336,128]{1,0:T(8,128)(2,1)S(1)} %convert_element_type.77), channel_id=1, source_target_pairs={{0,4},{4,0},{8,12},{12,8},{16,20},{20,16},{24,28},{28,24},{1,5},{5... | collective-permute-start | bytes 258056 | tf_op jit(solution)/shard_map/ppermute | solution.py:30
  31.2 0.8 %collective-permute-start.7 = (f16[336,128]{1,0:T(8,128)(2,1)S(1)}, f16[336,128]{1,0:T(8,128)(2,1)S(1)}, u32[]{:S(2)}, u32[]{:S(2)}) collective-permute-start(f16[336,128]{1,0:T(8,128)(2,1)S(1)} %convert_element_type.73), channel_id=1, source_target_pairs={{0,8},{4,12},{8,0},{12,4},{16,24},{20,28},{24,16},{28,20},{1,9},{5... | collective-permute-start | bytes 258056 | tf_op jit(solution)/shard_map/ppermute | solution.py:30
  32.0 1.4 %collective-permute-start.11 = (f16[304,128]{1,0:T(8,128)(2,1)S(1)}, f16[304,128]{1,0:T(8,128)(2,1)S(1)}, u32[]{:S(2)}, u32[]{:S(2)}) collective-permute-start(f16[304,128]{1,0:T(8,128)(2,1)S(1)} %convert_element_type.81), channel_id=1, source_target_pairs={{0,4},{4,0},{8,12},{12,8},{16,20},{20,16},{24,28},{28,24},{1,5},{5... | collective-permute-start | bytes 233480 | tf_op jit(solution)/shard_map/ppermute | solution.py:30
  33.3 3.1 %collective-permute-done.11 = f16[304,128]{1,0:T(8,128)(2,1)S(1)} collective-permute-done((f16[304,128]{1,0:T(8,128)(2,1)S(1)}, f16[304,128]{1,0:T(8,128)(2,1)S(1)}, u32[]{:S(2)}, u32[]{:S(2)}) %collective-permute-start.11) | collective-permute-done | bytes 77856 | tf_op jit(solution)/shard_map/ppermute | solution.py:30
  36.6 1.7 %collective-permute-start.12 = (f16[368,128]{1,0:T(8,128)(2,1)S(1)}, f16[368,128]{1,0:T(8,128)(2,1)S(1)}, u32[]{:S(2)}, u32[]{:S(2)}) collective-permute-start(f16[368,128]{1,0:T(8,128)(2,1)S(1)} %convert_element_type.83), channel_id=1, source_target_pairs={{0,24},{4,28},{8,16},{12,20},{16,8},{20,12},{24,0},{28,4},{1,25},{... | collective-permute-start | bytes 282632 | tf_op jit(solution)/shard_map/ppermute | solution.py:30
  38.4 1.1 %collective-permute-start.10 = (f16[368,128]{1,0:T(8,128)(2,1)S(1)}, f16[368,128]{1,0:T(8,128)(2,1)S(1)}, u32[]{:S(2)}, u32[]{:S(2)}) collective-permute-start(f16[368,128]{1,0:T(8,128)(2,1)S(1)} %convert_element_type.79), channel_id=1, source_target_pairs={{0,16},{4,20},{8,24},{12,28},{16,0},{20,4},{24,8},{28,12},{1,17},{... | collective-permute-start | bytes 282632 | tf_op jit(solution)/shard_map/ppermute | solution.py:30
  39.5 2.4 %collective-permute-start.8 = (f16[336,128]{1,0:T(8,128)(2,1)S(1)}, f16[336,128]{1,0:T(8,128)(2,1)S(1)}, u32[]{:S(2)}, u32[]{:S(2)}) collective-permute-start(f16[336,128]{1,0:T(8,128)(2,1)S(1)} %convert_element_type.75), channel_id=1, source_target_pairs={{0,12},{4,8},{8,4},{12,0},{16,28},{20,24},{24,20},{28,16},{1,13},{... | collective-permute-start | bytes 258056 | tf_op jit(solution)/shard_map/ppermute | solution.py:30
  42.0 0.8 %collective-permute-start.6 = (f16[304,128]{1,0:T(8,128)(2,1)S(1)}, f16[304,128]{1,0:T(8,128)(2,1)S(1)}, u32[]{:S(2)}, u32[]{:S(2)}) collective-permute-start(f16[304,128]{1,0:T(8,128)(2,1)S(1)} %convert_element_type.71), channel_id=1, source_target_pairs={{0,4},{4,0},{8,12},{12,8},{16,20},{20,16},{24,28},{28,24},{1,5},{5... | collective-permute-start | bytes 233480 | tf_op jit(solution)/shard_map/ppermute | solution.py:30
  42.8 3.7 %collective-permute-done.6 = f16[304,128]{1,0:T(8,128)(2,1)S(1)} collective-permute-done((f16[304,128]{1,0:T(8,128)(2,1)S(1)}, f16[304,128]{1,0:T(8,128)(2,1)S(1)}, u32[]{:S(2)}, u32[]{:S(2)}) %collective-permute-start.6) | collective-permute-done | bytes 77856 | tf_op jit(solution)/shard_map/ppermute | solution.py:30
  46.5 0.4 collective-permute-done.10
  47.0 0.7 %merge.1 = (f32[304,128]{1,0:T(8,128)S(1)}, f32[256,128]{1,0:T(8,128)S(1)}) custom-call(s32[4]{0:T(128)S(1)} %pad_add_fusion.where_ref, f32[304,128]{1,0:T(8,128)S(1)} %get-tuple-element.45.refs_0_, f32[304,128]{1,0:T(8,128)S(1)} %convert_element_type.72.refs_1_, f32[336,128]{1,0:T(8,128)S(1)} %convert_element_type.74.refs_0_.refs_2_, ...), custom_call_target="tpu_custom_call" | custom-call | tf_op jit(solution)/shard_map/merge/pallas_call | solution.py:620
  47.8 2.2 %collective-permute-start.15 = (f16[1,304,128]{2,1,0:T(8,128)(2,1)S(1)}, f16[1,304,128]{2,1,0:T(8,128)(2,1)S(1)}, u32[]{:S(2)}, u32[]{:S(2)}) collective-permute-start(f16[1,304,128]{2,1,0:T(8,128)(2,1)S(1)} %get-tuple-element.60), channel_id=1, source_target_pairs={{0,24},{4,28},{8,16},{12,20},{16,8},{20,12},{24,0},{28,4},{1,25},{... | collective-permute-start | bytes 233480 | tf_op jit(solution)/shard_map/ppermute | solution.py:30
  50.0 2.2 %collective-permute-start.18 = (f16[1,304,128]{2,1,0:T(8,128)(2,1)S(1)}, f16[1,304,128]{2,1,0:T(8,128)(2,1)S(1)}, u32[]{:S(2)}, u32[]{:S(2)}) collective-permute-start(f16[1,304,128]{2,1,0:T(8,128)(2,1)S(1)} %get-tuple-element.60), channel_id=1, source_target_pairs={{0,8},{4,12},{8,0},{12,4},{16,24},{20,28},{24,16},{28,20},{1,9},{5... | collective-permute-start | bytes 233480 | tf_op jit(solution)/shard_map/ppermute | solution.py:30
  52.2 1.3 %collective-permute-start.17 = (f16[1,304,128]{2,1,0:T(8,128)(2,1)S(1)}, f16[1,304,128]{2,1,0:T(8,128)(2,1)S(1)}, u32[]{:S(2)}, u32[]{:S(2)}) collective-permute-start(f16[1,304,128]{2,1,0:T(8,128)(2,1)S(1)} %get-tuple-element.60), channel_id=1, source_target_pairs={{0,4},{4,0},{8,12},{12,8},{16,20},{20,16},{24,28},{28,24},{1,5},{5... | collective-permute-start | bytes 233480 | tf_op jit(solution)/shard_map/ppermute | solution.py:30
  53.7 0.9 %collective-permute-done.15 = f16[1,304,128]{2,1,0:T(8,128)(2,1)S(1)} collective-permute-done((f16[1,304,128]{2,1,0:T(8,128)(2,1)S(1)}, f16[1,304,128]{2,1,0:T(8,128)(2,1)S(1)}, u32[]{:S(2)}, u32[]{:S(2)}) %collective-permute-start.15) | collective-permute-done | bytes 77856 | tf_op jit(solution)/shard_map/ppermute | solution.py:30
  54.6 1.6 %collective-permute-start.16 = (f16[1,304,128]{2,1,0:T(8,128)(2,1)S(1)}, f16[1,304,128]{2,1,0:T(8,128)(2,1)S(1)}, u32[]{:S(2)}, u32[]{:S(2)}) collective-permute-start(f16[1,304,128]{2,1,0:T(8,128)(2,1)S(1)} %collective-permute-done.15), channel_id=1, source_target_pairs={{0,4},{4,0},{8,12},{12,8},{16,20},{20,16},{24,28},{28,24},{1,5},{5... | collective-permute-start | bytes 233480 | tf_op jit(solution)/shard_map/ppermute | solution.py:30
  56.1 0.7 %collective-permute-done.13 = f16[1,304,128]{2,1,0:T(8,128)(2,1)S(1)} collective-permute-done((f16[1,304,128]{2,1,0:T(8,128)(2,1)S(1)}, f16[1,304,128]{2,1,0:T(8,128)(2,1)S(1)}, u32[]{:S(2)}, u32[]{:S(2)}) %collective-permute-start.13) | collective-permute-done | bytes 77856 | tf_op jit(solution)/shard_map/ppermute | solution.py:30
  56.9 1.3 %collective-permute-start.14 = (f16[1,304,128]{2,1,0:T(8,128)(2,1)S(1)}, f16[1,304,128]{2,1,0:T(8,128)(2,1)S(1)}, u32[]{:S(2)}, u32[]{:S(2)}) collective-permute-start(f16[1,304,128]{2,1,0:T(8,128)(2,1)S(1)} %collective-permute-done.13), channel_id=1, source_target_pairs={{0,4},{4,0},{8,12},{12,8},{16,20},{20,16},{24,28},{28,24},{1,5},{5... | collective-permute-start | bytes 233480 | tf_op jit(solution)/shard_map/ppermute | solution.py:30
  58.1 1.5 %embed.1 = f32[64,128]{1,0:T(8,128)} custom-call(s32[4]{0:T(128)S(1)} %pad_add_fusion.where_ref, f32[256,128]{1,0:T(8,128)S(1)} %get-tuple-element.53.sums_ref, f32[4,72,128]{2,1,0:T(8,128)S(1)} %join.3.refs_0_, f32[4,72,128]{2,1,0:T(8,128)S(1)} %collective-permute-done.5.refs_1_), custom_call_target="tpu_custom_call" | custom-call | tf_op jit(solution)/shard_map/embed/pallas_call | solution.py:824
  59.8 1.5 %spread.2 = (f32[2304,128]{1,0:T(8,128)}, f32[1,128]{1,0:T(1,128)S(1)}) custom-call(s32[4]{0:T(128)S(1)} %pad_add_fusion.where_ref, f32[1,304,128]{2,1,0:T(8,128)S(1)} %get-tuple-element.59.refs_0_, f32[1,304,128]{2,1,0:T(8,128)S(1)} %convert_element_type.89.refs_1_, f32[1,304,128]{2,1,0:T(8,128)S(1)} %convert_element_type.90.refs_2_, ...), custom_call_target="tpu_custom_call" | custom-call | tf_op jit(solution)/shard_map/spread/pallas_call | solution.py:689
  61.4 1.8 %spread.3 = (f32[2304,128]{1,0:T(8,128)}, f32[1,128]{1,0:T(1,128)}) custom-call(s32[4]{0:T(128)S(1)} %pad_add_fusion.where_ref, f32[1,304,128]{2,1,0:T(8,128)S(1)} %convert_element_type.86.refs_0_, f32[1,304,128]{2,1,0:T(8,128)S(1)} %convert_element_type.87.refs_1_, f32[2304,128]{1,0:T(8,128)} %get-tuple-element.55.refs_2_, ...), custom_call_target="tpu_custom_call", output_to_operand_aliasing={{0}: (3, {})} | custom-call | tf_op jit(solution)/shard_map/spread/pallas_call | solution.py:689
  (53 shorter events, 0.8 us)
Async XLA Ops:
  2.7 9.1 %collective-permute-start = (bf16[48,768]{1,0:T(8,128)(2,1)S(1)}, bf16[48,768]{1,0:T(8,128)(2,1)S(1)}, u32[]{:S(2)}, u32[]{:S(2)}) collective-permute-start(bf16[48,768]{1,0:T(8,128)(2,1)S(1)} %get-tuple-element.33), channel_id=1, source_target_pairs={{0,4},{2,6},{4,8},{5,1},{6,10},{7,3},{8,12},{9,5},{10,14},{11,7},{... | collective-permute-start | bytes 221192 | tf_op jit(solution)/shard_map/ppermute | solution.py:758
  7.5 4.2 %collective-permute-start.1 = (f32[1,72,128]{2,1,0:T(8,128)S(1)}, f32[1,72,128]{2,1,0:T(8,128)S(1)}, u32[]{:S(2)}, u32[]{:S(2)}) collective-permute-start(f32[1,72,128]{2,1,0:T(8,128)S(1)} %get-tuple-element.34.refs_0_), channel_id=1, source_target_pairs={{0,8},{4,12},{8,0},{12,4},{16,24},{20,28},{24,16},{28,20},{1,9},{5... | collective-permute-start | bytes 110600 | tf_op jit(solution)/shard_map/ppermute | solution.py:30
  11.7 2.7 %copy-start.1 = (f32[256]{0:T(256)S(1)}, f32[256]{0:T(256)}, u32[]{:S(2)}) copy-start(f32[256]{0:T(256)} %param.10) | copy-start | bytes 3076
  11.7 7.4 %collective-permute-start.2 = (f32[2,72,128]{2,1,0:T(8,128)S(1)}, f32[2,72,128]{2,1,0:T(8,128)S(1)}, u32[]{:S(2)}, u32[]{:S(2)}) collective-permute-start(f32[2,72,128]{2,1,0:T(8,128)S(1)} %join.2.refs_0_), channel_id=1, source_target_pairs={{0,16},{4,20},{8,24},{12,28},{16,0},{20,4},{24,8},{28,12},{1,17},{... | collective-permute-start | bytes 221192 | tf_op jit(solution)/shard_map/ppermute | solution.py:30
  19.1 3.3 %copy-start = (s32[24,64]{1,0:T(8,128)S(1)}, s32[24,64]{1,0:T(8,128)}, u32[]{:S(2)}) copy-start(s32[24,64]{1,0:T(8,128)} %lab_ref.1) | copy-start | bytes 18436
  19.1 3.3 %copy-start.2 = (bf16[3,3,256,128]{3,2,1,0:T(8,128)(2,1)S(1)}, bf16[3,3,256,128]{3,2,1,0:T(8,128)(2,1)}, u32[]{:S(2)}) copy-start(bf16[3,3,256,128]{3,2,1,0:T(8,128)(2,1)} %param.11) | copy-start | bytes 1769476
  19.1 3.3 %copy-start.3 = (f32[128]{0:T(128)S(1)}, f32[128]{0:T(128)}, u32[]{:S(2)}) copy-start(f32[128]{0:T(128)} %param.12) | copy-start | bytes 1540
  19.2 3.2 %collective-permute-start.3 = (bf16[12,64,256]{2,1,0:T(8,128)(2,1)S(1)}, bf16[12,64,256]{2,1,0:T(8,128)(2,1)S(1)}, u32[]{:S(2)}, u32[]{:S(2)}) collective-permute-start(bf16[12,64,256]{2,1,0:T(8,128)(2,1)S(1)} %conv_pool.1.refs_2_.refs_0_.own_ref), channel_id=1, source_target_pairs={{0,1},{1,0},{2,3},{3,2},{4,5},{5,4},{6,7},{7,6},{8,9},{9,8},{10,11... | collective-permute-start | bytes 1179656 | tf_op jit(solution)/shard_map/ppermute | solution.py:30
  19.2 1.9 %collective-permute-start.4 = (bf16[48,768]{1,0:T(8,128)(2,1)S(1)}, bf16[48,768]{1,0:T(8,128)(2,1)S(1)}, u32[]{:S(2)}, u32[]{:S(2)}) collective-permute-start(bf16[48,768]{1,0:T(8,128)(2,1)S(1)} %collective-permute-done.refs_1_.got_ref), channel_id=1, source_target_pairs={{0,1},{1,0},{2,3},{3,2},{4,5},{5,4},{6,7},{7,6},{8,9},{9,8},{10,11... | collective-permute-start | bytes 221192 | tf_op jit(solution)/shard_map/ppermute | solution.py:30
  19.7 7.1 %collective-permute-start.5 = (f32[4,72,128]{2,1,0:T(8,128)S(1)}, f32[4,72,128]{2,1,0:T(8,128)S(1)}, u32[]{:S(2)}, u32[]{:S(2)}) collective-permute-start(f32[4,72,128]{2,1,0:T(8,128)S(1)} %join.3.refs_0_), channel_id=1, source_target_pairs={{0,4},{4,0},{8,12},{12,8},{16,20},{20,16},{24,28},{28,24},{1,5},{5... | collective-permute-start | bytes 442376 | tf_op jit(solution)/shard_map/ppermute | solution.py:30
  29.8 6.7 %collective-permute-start.9 = (f16[336,128]{1,0:T(8,128)(2,1)S(1)}, f16[336,128]{1,0:T(8,128)(2,1)S(1)}, u32[]{:S(2)}, u32[]{:S(2)}) collective-permute-start(f16[336,128]{1,0:T(8,128)(2,1)S(1)} %convert_element_type.77), channel_id=1, source_target_pairs={{0,4},{4,0},{8,12},{12,8},{16,20},{20,16},{24,28},{28,24},{1,5},{5... | collective-permute-start | bytes 258056 | tf_op jit(solution)/shard_map/ppermute | solution.py:30
  31.2 5.3 %collective-permute-start.7 = (f16[336,128]{1,0:T(8,128)(2,1)S(1)}, f16[336,128]{1,0:T(8,128)(2,1)S(1)}, u32[]{:S(2)}, u32[]{:S(2)}) collective-permute-start(f16[336,128]{1,0:T(8,128)(2,1)S(1)} %convert_element_type.73), channel_id=1, source_target_pairs={{0,8},{4,12},{8,0},{12,4},{16,24},{20,28},{24,16},{28,20},{1,9},{5... | collective-permute-start | bytes 258056 | tf_op jit(solution)/shard_map/ppermute | solution.py:30
  32.0 4.5 %collective-permute-start.11 = (f16[304,128]{1,0:T(8,128)(2,1)S(1)}, f16[304,128]{1,0:T(8,128)(2,1)S(1)}, u32[]{:S(2)}, u32[]{:S(2)}) collective-permute-start(f16[304,128]{1,0:T(8,128)(2,1)S(1)} %convert_element_type.81), channel_id=1, source_target_pairs={{0,4},{4,0},{8,12},{12,8},{16,20},{20,16},{24,28},{28,24},{1,5},{5... | collective-permute-start | bytes 233480 | tf_op jit(solution)/shard_map/ppermute | solution.py:30
  36.6 9.9 %collective-permute-start.12 = (f16[368,128]{1,0:T(8,128)(2,1)S(1)}, f16[368,128]{1,0:T(8,128)(2,1)S(1)}, u32[]{:S(2)}, u32[]{:S(2)}) collective-permute-start(f16[368,128]{1,0:T(8,128)(2,1)S(1)} %convert_element_type.83), channel_id=1, source_target_pairs={{0,24},{4,28},{8,16},{12,20},{16,8},{20,12},{24,0},{28,4},{1,25},{... | collective-permute-start | bytes 282632 | tf_op jit(solution)/shard_map/ppermute | solution.py:30
  38.4 8.6 %collective-permute-start.10 = (f16[368,128]{1,0:T(8,128)(2,1)S(1)}, f16[368,128]{1,0:T(8,128)(2,1)S(1)}, u32[]{:S(2)}, u32[]{:S(2)}) collective-permute-start(f16[368,128]{1,0:T(8,128)(2,1)S(1)} %convert_element_type.79), channel_id=1, source_target_pairs={{0,16},{4,20},{8,24},{12,28},{16,0},{20,4},{24,8},{28,12},{1,17},{... | collective-permute-start | bytes 282632 | tf_op jit(solution)/shard_map/ppermute | solution.py:30
  39.5 6.9 %collective-permute-start.8 = (f16[336,128]{1,0:T(8,128)(2,1)S(1)}, f16[336,128]{1,0:T(8,128)(2,1)S(1)}, u32[]{:S(2)}, u32[]{:S(2)}) collective-permute-start(f16[336,128]{1,0:T(8,128)(2,1)S(1)} %convert_element_type.75), channel_id=1, source_target_pairs={{0,12},{4,8},{8,4},{12,0},{16,28},{20,24},{24,20},{28,16},{1,13},{... | collective-permute-start | bytes 258056 | tf_op jit(solution)/shard_map/ppermute | solution.py:30
  42.0 4.5 %collective-permute-start.6 = (f16[304,128]{1,0:T(8,128)(2,1)S(1)}, f16[304,128]{1,0:T(8,128)(2,1)S(1)}, u32[]{:S(2)}, u32[]{:S(2)}) collective-permute-start(f16[304,128]{1,0:T(8,128)(2,1)S(1)} %convert_element_type.71), channel_id=1, source_target_pairs={{0,4},{4,0},{8,12},{12,8},{16,20},{20,16},{24,28},{28,24},{1,5},{5... | collective-permute-start | bytes 233480 | tf_op jit(solution)/shard_map/ppermute | solution.py:30
  47.8 6.8 %collective-permute-start.15 = (f16[1,304,128]{2,1,0:T(8,128)(2,1)S(1)}, f16[1,304,128]{2,1,0:T(8,128)(2,1)S(1)}, u32[]{:S(2)}, u32[]{:S(2)}) collective-permute-start(f16[1,304,128]{2,1,0:T(8,128)(2,1)S(1)} %get-tuple-element.60), channel_id=1, source_target_pairs={{0,24},{4,28},{8,16},{12,20},{16,8},{20,12},{24,0},{28,4},{1,25},{... | collective-permute-start | bytes 233480 | tf_op jit(solution)/shard_map/ppermute | solution.py:30
  50.0 6.9 %collective-permute-start.13 = (f16[1,304,128]{2,1,0:T(8,128)(2,1)S(1)}, f16[1,304,128]{2,1,0:T(8,128)(2,1)S(1)}, u32[]{:S(2)}, u32[]{:S(2)}) collective-permute-start(f16[1,304,128]{2,1,0:T(8,128)(2,1)S(1)} %get-tuple-element.60), channel_id=1, source_target_pairs={{0,16},{4,20},{8,24},{12,28},{16,0},{20,4},{24,8},{28,12},{1,17},{... | collective-permute-start | bytes 233480 | tf_op jit(solution)/shard_map/ppermute | solution.py:30
  50.0 9.7 %collective-permute-start.18 = (f16[1,304,128]{2,1,0:T(8,128)(2,1)S(1)}, f16[1,304,128]{2,1,0:T(8,128)(2,1)S(1)}, u32[]{:S(2)}, u32[]{:S(2)}) collective-permute-start(f16[1,304,128]{2,1,0:T(8,128)(2,1)S(1)} %get-tuple-element.60), channel_id=1, source_target_pairs={{0,8},{4,12},{8,0},{12,4},{16,24},{20,28},{24,16},{28,20},{1,9},{5... | collective-permute-start | bytes 233480 | tf_op jit(solution)/shard_map/ppermute | solution.py:30
  52.2 7.5 %collective-permute-start.17 = (f16[1,304,128]{2,1,0:T(8,128)(2,1)S(1)}, f16[1,304,128]{2,1,0:T(8,128)(2,1)S(1)}, u32[]{:S(2)}, u32[]{:S(2)}) collective-permute-start(f16[1,304,128]{2,1,0:T(8,128)(2,1)S(1)} %get-tuple-element.60), channel_id=1, source_target_pairs={{0,4},{4,0},{8,12},{12,8},{16,20},{20,16},{24,28},{28,24},{1,5},{5... | collective-permute-start | bytes 233480 | tf_op jit(solution)/shard_map/ppermute | solution.py:30
  53.5 6.3 %collective-permute-start.19 = (f16[1,304,128]{2,1,0:T(8,128)(2,1)S(1)}, f16[1,304,128]{2,1,0:T(8,128)(2,1)S(1)}, u32[]{:S(2)}, u32[]{:S(2)}) collective-permute-start(f16[1,304,128]{2,1,0:T(8,128)(2,1)S(1)} %get-tuple-element.60), channel_id=1, source_target_pairs={{0,12},{4,8},{8,4},{12,0},{16,28},{20,24},{24,20},{28,16},{1,13},{... | collective-permute-start | bytes 233480 | tf_op jit(solution)/shard_map/ppermute | solution.py:30
  54.6 6.7 %collective-permute-start.16 = (f16[1,304,128]{2,1,0:T(8,128)(2,1)S(1)}, f16[1,304,128]{2,1,0:T(8,128)(2,1)S(1)}, u32[]{:S(2)}, u32[]{:S(2)}) collective-permute-start(f16[1,304,128]{2,1,0:T(8,128)(2,1)S(1)} %collective-permute-done.15), channel_id=1, source_target_pairs={{0,4},{4,0},{8,12},{12,8},{16,20},{20,16},{24,28},{28,24},{1,5},{5... | collective-permute-start | bytes 233480 | tf_op jit(solution)/shard_map/ppermute | solution.py:30
  56.9 4.5 %collective-permute-start.14 = (f16[1,304,128]{2,1,0:T(8,128)(2,1)S(1)}, f16[1,304,128]{2,1,0:T(8,128)(2,1)S(1)}, u32[]{:S(2)}, u32[]{:S(2)}) collective-permute-start(f16[1,304,128]{2,1,0:T(8,128)(2,1)S(1)} %collective-permute-done.13), channel_id=1, source_target_pairs={{0,4},{4,0},{8,12},{12,8},{16,20},{20,16},{24,28},{28,24},{1,5},{5... | collective-permute-start | bytes 233480 | tf_op jit(solution)/shard_map/ppermute | solution.py:30

commit v9 on v8

--- a/solution.py
+++ b/solution.py
@@ -45,6 +45,10 @@
                 m += 2
 
 
+def sigmoid(v):
+    return jax.nn.sigmoid(v)
+
+
 def shares(pooled_rows):
     first = pooled_rows // 2
     return first, pooled_rows - first
@@ -54,29 +58,18 @@
     return jnp.where(half == 0, pair[0], pair[1])
 
 
-def window_kernel(where_ref, x_hbm, w_hbm, taps, w_ref, rows_ref, wide, sems):
-    rows, cols, chans = x_hbm.shape
+def share_rows(half, rows):
+    first, second = shares(rows // 2)
+    most = -(-(2 * max(first, second) + 1) // PIECE) * PIECE
+    return most, pick(half, (0, rows - most)), pick(half, (-1, 2 * first - 1 - (rows - most)))
+
+
+def window_kernel(where_ref, rows_ref, taps, wide, *, rows):
+    most, cols, chans = rows_ref.shape
     half_cols = cols // 2
     half = where_ref[0]
-    first, second = shares(rows // 2)
-    counts = [-(-(2 * n + 1) // PIECE) for n in (first, second)]
-    pieces = pick(half, counts)
-    start = pick(half, (0, rows - counts[1] * PIECE))
-    shift = pick(half, (PIECE + 1, PIECE - (2 * first - 1 - (rows - counts[1] * PIECE))))
-
-    def piece(k):
-        at = pl.ds(k * PIECE, PIECE)
-        return pltpu.make_async_copy(
-            x_hbm.at[pl.ds(start + k * PIECE, PIECE)], rows_ref.at[at], sems.at[k]
-        )
-
-    def begin(k, carry):
-        piece(k).start()
-        return carry
-
-    lax.fori_loop(0, pieces, begin, 0)
-    weights = pltpu.make_async_copy(w_hbm, w_ref, sems.at[sems.shape[0] - 1])
-    weights.start()
+    _, _, before = share_rows(half, rows)
+    shift = PIECE - before
     lanes = chans // 128
     border = jnp.zeros((8, 128), F32)
     for t in range(wide.shape[0]):
@@ -84,7 +77,6 @@
         wide[t, cols + 8 : cols + 16] = border
 
     def prepare(k, carry):
-        piece(k).wait()
         for slot in range(PIECE):
             r = k * PIECE + slot
             x = rows_ref[r].astype(F32)
@@ -97,33 +89,24 @@
                     taps[r + shift, :, at : at + 128] = part.astype(BF16)
         return carry
 
-    lax.fori_loop(0, pieces, prepare, 0)
+    lax.fori_loop(0, most // PIECE, prepare, 0)
+    second = shares(rows // 2)[1]
     outside = pick(half, (PIECE, PIECE + 2 * second + 1))
     taps[outside] = jnp.zeros(taps.shape[1:], BF16)
-    weights.wait()
-
-
-def windows(where, x, w):
-    rows, cols, chans = x.shape
-    first, _ = shares(rows // 2)
-    most = -(-(2 * first + 1) // PIECE)
+
+
+def windows(where, near_rows, rows):
+    most, cols, chans = near_rows.shape
     return pl.pallas_call(
-        window_kernel,
-        out_shape=(
-            jax.ShapeDtypeStruct(((most + 2) * PIECE, cols // 2, 4 * chans), BF16),
-            jax.ShapeDtypeStruct(w.shape, BF16),
-        ),
-        in_specs=[SMEM, HBM, HBM],
-        out_specs=(VMEM, VMEM),
-        scratch_shapes=[
-            pltpu.VMEM((most * PIECE, cols, chans), BF16),
-            pltpu.VMEM((PIECE * (chans // 128), cols + 16, 128), F32),
-            pltpu.SemaphoreType.DMA((most + 1,)),
-        ],
+        functools.partial(window_kernel, rows=rows),
+        out_shape=jax.ShapeDtypeStruct((most + 2 * PIECE, cols // 2, 4 * chans), BF16),
+        in_specs=[SMEM, VMEM],
+        out_specs=VMEM,
+        scratch_shapes=[pltpu.VMEM((PIECE * (chans // 128), cols + 16, 128), F32)],
         compiler_params=params(16),
         cost_estimate=pl.CostEstimate(flops=0, bytes_accessed=12 << 20, transcendentals=0),
         name="windows",
-    )(where, *(pltpu.with_memory_space_constraint(a, pltpu.HBM) for a in (x, w)))
+    )(where, near_rows)
 
 
 def edge_part(where_ref, pairs, w_ref, bias, edge_ref, acc):
@@ -161,7 +144,7 @@
             for phase in range(2):
                 at = (2 * g + phase) * lanes + t
                 v = acc[at, 8 : 8 + rows] + bias[:, t * 128 : (t + 1) * 128]
-                acc[at, 8 : 8 + rows] = v * jax.nn.sigmoid(v)
+                acc[at, 8 : 8 + rows] = v * sigmoid(v)
                 both = (
                     acc[at, pl.ds(8, rows // 2, stride=2), :]
                     + acc[at, pl.ds(9, rows // 2, stride=2), :]
@@ -190,13 +173,14 @@
                 axis=-1,
             ).reshape(2 * STEP * half_cols, 9 * chans)
             v = jnp.dot(lhs, w_ref[...], preferred_element_type=F32) + bias
-            h = (v * jax.nn.sigmoid(v)).reshape(STEP, 2, half_cols, chans)
+            h = (v * sigmoid(v)).reshape(STEP, 2, half_cols, chans)
             h = h[:, 0] + h[:, 1]
             total = h if total is None else total + h
         out_ref[pl.ds(k * STEP, STEP)] = (total * 0.25).astype(BF16)
         return carry
 
-    lax.fori_loop(0, out_ref.shape[0] // STEP, step, 0)
+    for k in range(out_ref.shape[0] // STEP):
+        step(k, 0)
 
 
 def conv_pool(where, taps, w, b, pooled_rows, after):
@@ -241,7 +225,8 @@
 
 
 def start_kernel(
-    where_ref, x_hbm, grad_hbm, labels_hbm, slots_hbm, side_ref, head_ref, tail_ref, send_ref,
+    where_ref, x_hbm, w_hbm, grad_hbm, labels_hbm, slots_hbm,
+    side_ref, head_ref, tail_ref, send_ref, near_ref, w_ref,
     labels_ref, slots_ref, left, right, wide, sems,
 ):
     owned, width = grad_hbm.shape
@@ -256,6 +241,14 @@
         pltpu.make_async_copy(x_hbm.at[:, pl.ds(cols - reach, reach)], right, sems.at[3]),
         pltpu.make_async_copy(slots_hbm, slots_ref, sems.at[4]),
     ]
+    most, first, _ = share_rows(half, rows)
+    size = most // 4
+    for k in range(4):
+        source = x_hbm.at[pl.ds(first + k * size, size)]
+        copies.append(
+            pltpu.make_async_copy(source, near_ref.at[pl.ds(k * size, size)], sems.at[5 + k])
+        )
+    copies.append(pltpu.make_async_copy(w_hbm, w_ref, sems.at[9]))
     for copy in copies:
         copy.start()
     lane = lax.broadcasted_iota(jnp.int32, (1, width), 1)
@@ -286,31 +279,36 @@
                 out_ref[:, place : place + 128] = part
     send_ref[...] = jnp.where(half == 0, tail_ref[...], head_ref[...])
     copies[1].wait()
-
-
-def start(where, x, grad, slots, labels):
+    for copy in copies[5:]:
+        copy.wait()
+
+
+def start(where, x, w, grad, slots, labels):
     owned, width = grad.shape
-    rows, _, chans = x.shape
+    rows, cols, chans = x.shape
     reach = 16
+    most = share_rows(0, rows)[0]
     columns = jax.ShapeDtypeStruct((rows, WIDTH * chans), BF16)
     fixed = [
         pltpu.with_memory_space_constraint(a, pltpu.HBM)
-        for a in (x, grad, labels, slots.reshape(1, -1))
+        for a in (x, w, grad, labels, slots.reshape(1, -1))
     ]
     return pl.pallas_call(
         start_kernel,
-        out_shape=(jax.ShapeDtypeStruct((1, owned + SIDE, width), F32),) + (columns,) * 3,
-        in_specs=[SMEM, HBM, HBM, HBM, HBM],
-        out_specs=(VMEM,) * 4,
+        out_shape=(jax.ShapeDtypeStruct((1, owned + SIDE, width), F32),)
+        + (columns,) * 3
+        + (jax.ShapeDtypeStruct((most, cols, chans), BF16), jax.ShapeDtypeStruct(w.shape, BF16)),
+        in_specs=[SMEM] + [HBM] * 5,
+        out_specs=(VMEM,) * 6,
         scratch_shapes=[
             pltpu.VMEM(labels.shape, jnp.int32),
             pltpu.VMEM((1, slots.shape[0]), jnp.int32),
             pltpu.VMEM((rows, reach, chans), BF16),
             pltpu.VMEM((rows, reach, chans), BF16),
             pltpu.VMEM((chans // 128, rows * reach, 128), F32),
-            pltpu.SemaphoreType.DMA((5,)),
+            pltpu.SemaphoreType.DMA((10,)),
         ],
-        compiler_params=params(),
+        compiler_params=params(16),
         name="start",
     )(where, *fixed)
 
@@ -363,7 +361,7 @@
 
 def deep_kernel(
     where_ref, own_ref, other_ref, edge_ref, w_ref, b_ref, lab_ref, taps, member, slope, sums_ref, wide,
-    *, block, entries
+    inside, *, block, entries
 ):
     _, cols, chans = own_ref.shape
     rows = lab_ref.shape[0]
@@ -416,17 +414,19 @@
     bias = b_ref[...]
     size = block * cols
 
+    flat = jnp.concatenate([lab_ref[r : r + 1, :] for r in range(rows)], axis=1)
+    entry = lax.broadcasted_iota(jnp.int32, (entries, rows * cols), 0)
+    inside[...] = jnp.where(jnp.broadcast_to(flat, entry.shape) == entry, 1.0, 0.0).astype(BF16)
+
     def step(k, sums):
         r0 = k * block
         lhs = jnp.concatenate([taps[pl.ds(r0 + dr, block)] for dr in range(3)], axis=-1)
         v = jnp.dot(lhs.reshape(size, 9 * chans), w_ref[...], preferred_element_type=F32) + bias
-        sig = jax.nn.sigmoid(v)
+        sig = sigmoid(v)
         features = (v * sig).astype(BF16)
         slope[pl.ds(k * size, size)] = sig * (1.0 + v * (1.0 - sig))
-        mem = member[pl.ds(r0, block)].reshape(size, 128)
-        return sums + lax.dot_general(
-            mem, features, (((0,), (0,)), ((), ())), preferred_element_type=F32
-        )[:entries]
+        mine = inside[:, pl.ds(pl.multiple_of(k * size, 128), size)]
+        return sums + jnp.dot(mine, features, preferred_element_type=F32)
 
     sums_ref[...] = lax.fori_loop(0, rows // block, step, jnp.zeros((entries, width), F32))
 
@@ -447,7 +447,10 @@
         ),
         in_specs=[SMEM] + [VMEM] * 6,
         out_specs=(VMEM,) * 4,
-        scratch_shapes=[pltpu.VMEM((slots * (chans // 128), cols + 16, 128), F32)],
+        scratch_shapes=[
+            pltpu.VMEM((slots * (chans // 128), cols + 16, 128), F32),
+            pltpu.VMEM((entries, rows * cols), BF16),
+        ],
         compiler_params=params(16),
         cost_estimate=pl.CostEstimate(
             flops=4 * rows * cols * 9 * chans * width, bytes_accessed=8 << 20, transcendentals=0
@@ -461,7 +464,7 @@
 ):
     part_refs = refs[:n_parts]
     out_refs = refs[n_parts : n_parts + ways]
-    grad, weight = refs[n_parts + ways :]
+    (weight,) = refs[n_parts + ways :]
     rows, cols, depth = member.shape[0], taps.shape[1], taps.shape[2]
     width = slope.shape[-1]
     me = where_ref[3]
@@ -491,11 +494,11 @@
     terms = jnp.concatenate([high, mid, low, jnp.zeros((128 - 3 * entries, width), BF16)], axis=0)
     pixel = jnp.dot(member[...].reshape(rows * cols, 128), terms, preferred_element_type=F32)
     dg = (pixel * slope[...]).astype(BF16)
-    grad[...] = dg
+    turned = jnp.transpose(dg)
     bias_sum = jnp.sum(dg.astype(F32), axis=0, keepdims=True)
     for dr in range(3):
         window = taps[dr : dr + rows].reshape(rows * cols, depth)
-        out = lax.dot_general(grad[...], window, (((0,), (0,)), ((), ())), preferred_element_type=F32)
+        out = jnp.dot(turned, window, preferred_element_type=F32)
         weight[dr * depth : (dr + 1) * depth] = jnp.transpose(out)
     if weight.shape[0] > 3 * depth:
         weight[3 * depth :] = jnp.zeros((weight.shape[0] - 3 * depth, width), F32)
@@ -531,10 +534,7 @@
         ),
         in_specs=[SMEM] + [VMEM] * (4 + len(parts)),
         out_specs=(VMEM,) * ways,
-        scratch_shapes=[
-            pltpu.VMEM(slope.shape, BF16),
-            pltpu.VMEM((count * chunk, width), F32),
-        ],
+        scratch_shapes=[pltpu.VMEM((count * chunk, width), F32)],
         compiler_params=params(16),
         cost_estimate=pl.CostEstimate(
             flops=4 * slope.shape[0] * 3 * taps.shape[2] * width, bytes_accessed=8 << 20, transcendentals=0
@@ -654,80 +654,35 @@
     out_ref[...] = sums / jnp.maximum(counts, 1.0)
 
 
-def spread_kernel(where_ref, *refs, chunk, members):
-    count = len(members)
-    part_refs, before = refs[:count], refs[count:-4]
-    weight_hbm, bias_ref, place, sems = refs[-4:]
-    me = where_ref[3]
-    bias_ref[...] = before[1][...] if before else jnp.zeros_like(bias_ref)
-    copies = []
-    for p, m in enumerate(members):
-        bias, down, _ = read_note(part_refs[p][0], chunk)
-        place[p * chunk : (p + 1) * chunk] = part_refs[p][0, :chunk] * down
-        j = me ^ m
-        copies.append(
-            pltpu.make_async_copy(
-                place.at[pl.ds(p * chunk, chunk)],
-                weight_hbm.at[pl.ds(pl.multiple_of(j * chunk, 8), chunk)],
-                sems.at[p],
-            )
-        )
-        copies[p].start()
-
-        @pl.when(j == 0)
-        def _():
-            bias_ref[...] = bias
-
-    for copy in copies:
-        copy.wait()
-
-
-def spread(where, parts, before, chunk, count, rows):
-    parts = {m: part.astype(F32) for m, part in parts.items()}
-    width = next(iter(parts.values())).shape[-1]
-    before = list(before)
-    return pl.pallas_call(
-        functools.partial(spread_kernel, chunk=chunk, members=tuple(parts)),
-        out_shape=(jax.ShapeDtypeStruct((rows, width), F32), jax.ShapeDtypeStruct((1, width), F32)),
-        in_specs=[SMEM] + [VMEM] * len(parts) + ([HBM, VMEM] if before else []),
-        out_specs=(HBM, VMEM),
-        scratch_shapes=[
-            pltpu.VMEM((len(parts) * chunk, width), F32),
-            pltpu.SemaphoreType.DMA((len(parts),)),
-        ],
-        input_output_aliases={1 + len(parts): 0} if before else {},
-        compiler_params=params(),
-        name="spread",
-    )(where, *parts.values(), *before)
-
-
-def spread_all_kernel(where_ref, *refs, chunk, rows, members):
+def spread_kernel(where_ref, *refs, chunk, rows, members):
     part_refs, weight_ref, bias_ref, place = refs[:-3], refs[-3], refs[-2], refs[-1]
     me = where_ref[3]
     count = len(members)
     for p, k in itertools.product(range(count), range(part_refs[0].shape[0])):
         bias, down, _ = read_note(part_refs[p][k], chunk)
         j = me ^ (members[p] + k * count)
-        place[pl.ds(pl.multiple_of(j * chunk, 8), chunk)] = part_refs[p][k, :chunk] * down
+        target = weight_ref if rows == place.shape[0] else place
+        target[pl.ds(pl.multiple_of(j * chunk, 8), chunk)] = part_refs[p][k, :chunk] * down
 
         @pl.when(j == 0)
         def _():
             bias_ref[...] = bias
 
-    weight_ref[...] = place[:rows]
-
-
-def spread_all(where, parts, chunk, count, rows):
+    if rows != place.shape[0]:
+        weight_ref[...] = place[:rows]
+
+
+def spread(where, parts, chunk, count, rows):
     parts = {m: part.astype(F32) for m, part in parts.items()}
     width = parts[0].shape[-1]
     return pl.pallas_call(
-        functools.partial(spread_all_kernel, chunk=chunk, rows=rows, members=tuple(parts)),
+        functools.partial(spread_kernel, chunk=chunk, rows=rows, members=tuple(parts)),
         out_shape=(jax.ShapeDtypeStruct((rows, width), F32), jax.ShapeDtypeStruct((1, width), F32)),
         in_specs=[SMEM] + [VMEM] * len(parts),
         out_specs=(VMEM, VMEM),
         scratch_shapes=[pltpu.VMEM((count * chunk, width), F32)],
         compiler_params=params(),
-        name="spread_all",
+        name="spread",
     )(where, *parts.values())
 
 
@@ -748,7 +703,9 @@
     conv_w = conv_weight.reshape(9 * channels, -1)
     conv_b = conv_bias.reshape(1, -1)
 
-    side, head, tail, sent = start(where, section_input, embed_grad, slot_ids, labels)
+    side, head, tail, sent, near_rows, near_w = start(
+        where, section_input, conv_w, embed_grad, slot_ids, labels
+    )
     pairs = []
     for s in range(strip_count):
         for c in range(chan_count):
@@ -760,7 +717,7 @@
     steps = [(at + 1, 1) for at in range(min(2, strip_count.bit_length() - 2))]
     steps += [(at, min(3, strip_count.bit_length() - 1 - at)) for at in range(3, strip_count.bit_length() - 1, 3)]
     ahead = gather_step(side, "strip", steps[0])
-    taps, near_w = windows(where, section_input, conv_w)
+    taps = windows(where, near_rows, section_input.shape[0])
     shared = join(ahead, [taps])
     got, shared = lax.optimization_barrier((got, shared))
     traded = swap(got, "chan", 1)
@@ -836,12 +793,9 @@
     for k in far:
         gathered[2 * k] = swap(own, "strip", 2 * k)
     late = {2 * k + 1: swap(gathered[2 * k], "strip", 1) for k in far}
-    rows = 9 * channels
-    if strip_count * chunk == rows and late:
-        result = spread(where, gathered, [], chunk, strip_count, rows)
-        weight_rows, bias_row = spread(where, late, result, chunk, strip_count, rows)
-    else:
-        weight_rows, bias_row = spread_all(where, {**gathered, **late}, chunk, strip_count, rows)
+    weight_rows, bias_row = spread(
+        where, {**gathered, **late}, chunk, strip_count, 9 * channels
+    )
     return (embeddings, weight_rows.reshape(3, 3, channels, width), bias_row[0])
 
 

time: 63.4 us -> 63.9 us (level)
  waiting for transfers between devices: 8.85 us -> 12 us
  Pallas kernels: 23.3 us -> 21.3 us
    ppermute x19, waiting for transfers between devices: 8.85 us -> 12 us  [swap(): return lax.ppermute(value, axis, [(i, i ^ mask) for i in range(count)])]
    pallas_call x3 -> x2, Pallas kernels: 5.83 us -> 3.19 us  [the longest x1 1.71 us: spread(): pl.pallas_call(functools.partial(spread_kernel, chunk=chunk, rows=rows, m...]
    pallas_call x1, Pallas kernels: 1.93 us -> 2.75 us  [start(): pl.pallas_call(start_kernel, out_shape=(jax.ShapeDtypeStruct((1, owned +...]
  transfers between devices with their start and end apart: 20 -> 20, of which waited for: 5 -> 7; matrix products, arithmetic and copies ran while one was open for 0% -> 0% of each run, Pallas kernels for 25% -> 21%
where the time goes in v9:
time: 63.9 us; the launch traced here: 63.7 us
  starting transfers between devices  29 us (45%)
  Pallas kernels  21.3 us (33%)
  waiting for transfers between devices  12 us (19%)
  between operations  1 us (2%)
    ppermute x19, starting transfers between devices, swap(): return lax.ppermute(value, axis, [(i, i ^ mask) for i in range(count)])  24.2 us
    ppermute x19, waiting for transfers between devices, swap(): return lax.ppermute(value, axis, [(i, i ^ mask) for i in range(count)])  12 us
    ppermute x1, starting transfers between devices, body(): got = lax.ppermute(sent, ('strip', 'chan'), pairs)  4.85 us
    pallas_call x1, Pallas kernels, conv_pool(): pl.pallas_call(conv_kernel, out_shape=jax.ShapeDtypeStruct((pooled_rows,...  4.59 us
    pallas_call x1, Pallas kernels, deep_forward(): pl.pallas_call(functools.partial(deep_kernel, block=block, entries=entrie...  4.32 us
    pallas_call x1, Pallas kernels, deep_backward(): pl.pallas_call(functools.partial(grad_kernel, n_parts=len(parts), chunk=c...  2.83 us
    pallas_call x1, Pallas kernels, start(): pl.pallas_call(start_kernel, out_shape=(jax.ShapeDtypeStruct((1, owned +...  2.75 us
    pallas_call x1, Pallas kernels, spread(): pl.pallas_call(functools.partial(spread_kernel, chunk=chunk, rows=rows, m...  1.71 us
  transfers between devices with their start and end apart: 20, of which 7 were waited for; matrix products, arithmetic and copies ran while one was open for 0% of the time, Pallas kernels for 21%

profile of v9, /device:TPU:0, one launch (start us, length us, event | category | flops | bytes accessed | tf_op | source)
XLA Modules:
  0.0 63.7 jit_solution(9107366147335775923)
XLA Ops:
  0.7 2.8 %start.1 = (f32[1,72,128]{2,1,0:T(8,128)S(1)}, bf16[48,768]{1,0:T(8,128)(2,1)S(1)}, bf16[48,768]{1,0:T(8,128)(2,1)S(1)}, bf16[48,768]{1,0:T(8,128)(2,1)S(1)}, bf...) custom-call(s32[4]{0:T(128)S(1)} %pad_add_fusion.where_ref, bf16[48,128,256]{2,1,0:T(8,128)(2,1)} %x_hbm.1, ...), custom_call_target="tpu_custom_call" | custom-call | tf_op jit(solution)/shard_map/start/pallas_call | solution.py:296
  3.5 4.8 %collective-permute-start = (bf16[48,768]{1,0:T(8,128)(2,1)S(1)}, bf16[48,768]{1,0:T(8,128)(2,1)S(1)}, u32[]{:S(2)}, u32[]{:S(2)}) collective-permute-start(bf16[48,768]{1,0:T(8,128)(2,1)S(1)} %get-tuple-element.31), channel_id=1, source_target_pairs={{0,4},{2,6},{4,8},{5,1},{6,10},{7,3},{8,12},{9,5},{10,14},{11,7},{... | collective-permute-start | bytes 221192 | tf_op jit(solution)/shard_map/ppermute | solution.py:715
  8.3 1.6 %collective-permute-start.1 = (f32[1,72,128]{2,1,0:T(8,128)S(1)}, f32[1,72,128]{2,1,0:T(8,128)S(1)}, u32[]{:S(2)}, u32[]{:S(2)}) collective-permute-start(f32[1,72,128]{2,1,0:T(8,128)S(1)} %get-tuple-element.32.refs_0_), channel_id=1, source_target_pairs={{0,8},{4,12},{8,0},{12,4},{16,24},{20,28},{24,16},{28,20},{1,9},{5... | collective-permute-start | bytes 110600 | tf_op jit(solution)/shard_map/ppermute | solution.py:30
  10.0 1.5 %windows.1.refs_2_.taps = bf16[36,64,1024]{2,1,0:T(8,128)(2,1)S(1)} custom-call(s32[4]{0:T(128)S(1)} %pad_add_fusion.where_ref, bf16[28,128,256]{2,1,0:T(8,128)(2,1)S(1)} %get-tuple-element.29.rows_ref), custom_call_target="tpu_custom_call" | custom-call | bytes 12582912 | tf_op jit(solution)/shard_map/windows/pallas_call | solution.py:100
  11.5 0.9 %collective-permute-done.1.refs_1_ = f32[1,72,128]{2,1,0:T(8,128)S(1)} collective-permute-done((f32[1,72,128]{2,1,0:T(8,128)S(1)}, f32[1,72,128]{2,1,0:T(8,128)S(1)}, u32[]{:S(2)}, u32[]{:S(2)}) %collective-permute-start.1) | collective-permute-done | bytes 36896 | tf_op jit(solution)/shard_map/ppermute | solution.py:30
  12.4 2.7 %collective-permute-start.2 = (f32[2,72,128]{2,1,0:T(8,128)S(1)}, f32[2,72,128]{2,1,0:T(8,128)S(1)}, u32[]{:S(2)}, u32[]{:S(2)}) collective-permute-start(f32[2,72,128]{2,1,0:T(8,128)S(1)} %join.2.refs_0_), channel_id=1, source_target_pairs={{0,16},{4,20},{8,24},{12,28},{16,0},{20,4},{24,8},{28,12},{1,17},{... | collective-permute-start | bytes 221192 | tf_op jit(solution)/shard_map/ppermute | solution.py:30
  15.0 4.6 %conv_pool.1.refs_2_.refs_0_.own_ref = bf16[12,64,256]{2,1,0:T(8,128)(2,1)S(1)} custom-call(s32[4]{0:T(128)S(1)} %pad_add_fusion.where_ref, bf16[36,64,1024]{2,1,0:T(8,128)(2,1)S(1)} %windows.1.refs_2_.taps, bf16[2304,256]{1,0:T(8,128)(2,1)S(1)} %get-tuple-element.30.w_ref, f32[1,256]{1,0:T(1,128)S(1)} %bitcast.14, f32[2,72,128]{2,1,0:T(8,128)S(1)} %join.2.refs_0_, ...), custom_call_target="tpu_custom_call" | custom-call | flops 3623878656 | bytes 8388608 | tf_op jit(solution)/shard_map/conv_pool/pallas_call | solution.py:189
  20.3 1.5 %collective-permute-start.5 = (f32[4,72,128]{2,1,0:T(8,128)S(1)}, f32[4,72,128]{2,1,0:T(8,128)S(1)}, u32[]{:S(2)}, u32[]{:S(2)}) collective-permute-start(f32[4,72,128]{2,1,0:T(8,128)S(1)} %join.3.refs_0_), channel_id=1, source_target_pairs={{0,4},{4,0},{8,12},{12,8},{16,20},{20,16},{24,28},{28,24},{1,5},{5... | collective-permute-start | bytes 442376 | tf_op jit(solution)/shard_map/ppermute | solution.py:30
  21.8 1.3 %conv_edges.1.edge_ref = f32[4,2,24,128]{3,2,1,0:T(8,128)S(1)} custom-call(s32[4]{0:T(128)S(1)} %pad_add_fusion.where_ref, bf16[2304,256]{1,0:T(8,128)(2,1)S(1)} %get-tuple-element.30.w_ref, f32[1,256]{1,0:T(1,128)S(1)} %bitcast.15, bf16[48,768]{1,0:T(8,128)(2,1)S(1)} %collective-permute-done.refs_1_.got_ref, ...), custom_call_target="tpu_custom_call" | custom-call | bytes 4194304 | tf_op jit(solution)/shard_map/conv_edges/pallas_call | solution.py:215
  23.1 4.3 %deep_forward.1 = (bf16[26,64,768]{2,1,0:T(8,128)(2,1)S(1)}, bf16[24,64,128]{2,1,0:T(8,128)(2,1)S(1)}, f32[1536,128]{1,0:T(8,128)S(1)}, f32[32,128]{1,0:T(8,128)S(1)}) custom-call(s32[4]{0:T(128)S(1)} %pad_add_fusion.where_ref, bf16[12,64,256]{2,1,0:T(8,128)(2,1)S(1)} %conv_pool.1.refs_2_.refs_0_.own_ref, ...), custom_call_target="tpu_custom_call" | custom-call | flops 1811939328 | bytes 8388608 | tf_op jit(solution)/shard_map/deep_forward/pallas_call | solution.py:440
  27.5 2.8 %deep_backward.1 = (f32[304,128]{1,0:T(8,128)S(1)}, f32[304,128]{1,0:T(8,128)S(1)}, f32[336,128]{1,0:T(8,128)S(1)}, f32[336,128]{1,0:T(8,128)S(1)}, f32[304,128]...) custom-call(s32[4]{0:T(128)S(1)} %pad_add_fusion.where_ref, ...), custom_call_target="tpu_custom_call" | custom-call | flops 1811939328 | bytes 8388608 | tf_op jit(solution)/shard_map/deep_backward/pallas_call | solution.py:527
  30.3 1.4 %collective-permute-start.7 = (f16[336,128]{1,0:T(8,128)(2,1)S(1)}, f16[336,128]{1,0:T(8,128)(2,1)S(1)}, u32[]{:S(2)}, u32[]{:S(2)}) collective-permute-start(f16[336,128]{1,0:T(8,128)(2,1)S(1)} %convert_element_type.75), channel_id=1, source_target_pairs={{0,8},{4,12},{8,0},{12,4},{16,24},{20,28},{24,16},{28,20},{1,9},{5... | collective-permute-start | bytes 258056 | tf_op jit(solution)/shard_map/ppermute | solution.py:30
  31.7 0.8 %collective-permute-start.9 = (f16[336,128]{1,0:T(8,128)(2,1)S(1)}, f16[336,128]{1,0:T(8,128)(2,1)S(1)}, u32[]{:S(2)}, u32[]{:S(2)}) collective-permute-start(f16[336,128]{1,0:T(8,128)(2,1)S(1)} %convert_element_type.79), channel_id=1, source_target_pairs={{0,4},{4,0},{8,12},{12,8},{16,20},{20,16},{24,28},{28,24},{1,5},{5... | collective-permute-start | bytes 258056 | tf_op jit(solution)/shard_map/ppermute | solution.py:30
  32.5 1.4 %collective-permute-start.11 = (f16[304,128]{1,0:T(8,128)(2,1)S(1)}, f16[304,128]{1,0:T(8,128)(2,1)S(1)}, u32[]{:S(2)}, u32[]{:S(2)}) collective-permute-start(f16[304,128]{1,0:T(8,128)(2,1)S(1)} %convert_element_type.83), channel_id=1, source_target_pairs={{0,4},{4,0},{8,12},{12,8},{16,20},{20,16},{24,28},{28,24},{1,5},{5... | collective-permute-start | bytes 233480 | tf_op jit(solution)/shard_map/ppermute | solution.py:30
  33.9 3.9 %collective-permute-done.11 = f16[304,128]{1,0:T(8,128)(2,1)S(1)} collective-permute-done((f16[304,128]{1,0:T(8,128)(2,1)S(1)}, f16[304,128]{1,0:T(8,128)(2,1)S(1)}, u32[]{:S(2)}, u32[]{:S(2)}) %collective-permute-start.11) | collective-permute-done | bytes 77856 | tf_op jit(solution)/shard_map/ppermute | solution.py:30
  38.0 1.1 %collective-permute-start.12 = (f16[368,128]{1,0:T(8,128)(2,1)S(1)}, f16[368,128]{1,0:T(8,128)(2,1)S(1)}, u32[]{:S(2)}, u32[]{:S(2)}) collective-permute-start(f16[368,128]{1,0:T(8,128)(2,1)S(1)} %convert_element_type.85), channel_id=1, source_target_pairs={{0,24},{4,28},{8,16},{12,20},{16,8},{20,12},{24,0},{28,4},{1,25},{... | collective-permute-start | bytes 282632 | tf_op jit(solution)/shard_map/ppermute | solution.py:30
  39.0 1.4 %collective-permute-start.10 = (f16[368,128]{1,0:T(8,128)(2,1)S(1)}, f16[368,128]{1,0:T(8,128)(2,1)S(1)}, u32[]{:S(2)}, u32[]{:S(2)}) collective-permute-start(f16[368,128]{1,0:T(8,128)(2,1)S(1)} %convert_element_type.81), channel_id=1, source_target_pairs={{0,16},{4,20},{8,24},{12,28},{16,0},{20,4},{24,8},{28,12},{1,17},{... | collective-permute-start | bytes 282632 | tf_op jit(solution)/shard_map/ppermute | solution.py:30
  40.5 2.5 %collective-permute-start.8 = (f16[336,128]{1,0:T(8,128)(2,1)S(1)}, f16[336,128]{1,0:T(8,128)(2,1)S(1)}, u32[]{:S(2)}, u32[]{:S(2)}) collective-permute-start(f16[336,128]{1,0:T(8,128)(2,1)S(1)} %convert_element_type.77), channel_id=1, source_target_pairs={{0,12},{4,8},{8,4},{12,0},{16,28},{20,24},{24,20},{28,16},{1,13},{... | collective-permute-start | bytes 258056 | tf_op jit(solution)/shard_map/ppermute | solution.py:30
  42.9 1.2 %collective-permute-start.6 = (f16[304,128]{1,0:T(8,128)(2,1)S(1)}, f16[304,128]{1,0:T(8,128)(2,1)S(1)}, u32[]{:S(2)}, u32[]{:S(2)}) collective-permute-start(f16[304,128]{1,0:T(8,128)(2,1)S(1)} %convert_element_type.73), channel_id=1, source_target_pairs={{0,4},{4,0},{8,12},{12,8},{16,20},{20,16},{24,28},{28,24},{1,5},{5... | collective-permute-start | bytes 233480 | tf_op jit(solution)/shard_map/ppermute | solution.py:30
  44.1 3.3 %collective-permute-done.6 = f16[304,128]{1,0:T(8,128)(2,1)S(1)} collective-permute-done((f16[304,128]{1,0:T(8,128)(2,1)S(1)}, f16[304,128]{1,0:T(8,128)(2,1)S(1)}, u32[]{:S(2)}, u32[]{:S(2)}) %collective-permute-start.6) | collective-permute-done | bytes 77856 | tf_op jit(solution)/shard_map/ppermute | solution.py:30
  47.5 1.0 %collective-permute-done.10 = f16[368,128]{1,0:T(8,128)(2,1)S(1)} collective-permute-done((f16[368,128]{1,0:T(8,128)(2,1)S(1)}, f16[368,128]{1,0:T(8,128)(2,1)S(1)}, u32[]{:S(2)}, u32[]{:S(2)}) %collective-permute-start.10) | collective-permute-done | bytes 94240 | tf_op jit(solution)/shard_map/ppermute | solution.py:30
  48.5 0.7 %merge.1 = (f32[304,128]{1,0:T(8,128)S(1)}, f32[256,128]{1,0:T(8,128)S(1)}) custom-call(s32[4]{0:T(128)S(1)} %pad_add_fusion.where_ref, f32[304,128]{1,0:T(8,128)S(1)} %get-tuple-element.43.refs_0_, f32[304,128]{1,0:T(8,128)S(1)} %convert_element_type.74.refs_1_, f32[336,128]{1,0:T(8,128)S(1)} %convert_element_type.76.refs_0_.refs_2_, ...), custom_call_target="tpu_custom_call" | custom-call | tf_op jit(solution)/shard_map/merge/pallas_call | solution.py:620
  49.6 2.2 %collective-permute-start.17 = (f16[1,304,128]{2,1,0:T(8,128)(2,1)S(1)}, f16[1,304,128]{2,1,0:T(8,128)(2,1)S(1)}, u32[]{:S(2)}, u32[]{:S(2)}) collective-permute-start(f16[1,304,128]{2,1,0:T(8,128)(2,1)S(1)} %get-tuple-element.56), channel_id=1, source_target_pairs={{0,24},{4,28},{8,16},{12,20},{16,8},{20,12},{24,0},{28,4},{1,25},{... | collective-permute-start | bytes 233480 | tf_op jit(solution)/shard_map/ppermute | solution.py:30
  51.8 0.9 %collective-permute-start.13 = (f16[1,304,128]{2,1,0:T(8,128)(2,1)S(1)}, f16[1,304,128]{2,1,0:T(8,128)(2,1)S(1)}, u32[]{:S(2)}, u32[]{:S(2)}) collective-permute-start(f16[1,304,128]{2,1,0:T(8,128)(2,1)S(1)} %get-tuple-element.56), channel_id=1, source_target_pairs={{0,4},{4,0},{8,12},{12,8},{16,20},{20,16},{24,28},{28,24},{1,5},{5... | collective-permute-start | bytes 233480 | tf_op jit(solution)/shard_map/ppermute | solution.py:30
  52.7 1.0 %collective-permute-start.14 = (f16[1,304,128]{2,1,0:T(8,128)(2,1)S(1)}, f16[1,304,128]{2,1,0:T(8,128)(2,1)S(1)}, u32[]{:S(2)}, u32[]{:S(2)}) collective-permute-start(f16[1,304,128]{2,1,0:T(8,128)(2,1)S(1)} %get-tuple-element.56), channel_id=1, source_target_pairs={{0,8},{4,12},{8,0},{12,4},{16,24},{20,28},{24,16},{28,20},{1,9},{5... | collective-permute-start | bytes 233480 | tf_op jit(solution)/shard_map/ppermute | solution.py:30
  53.8 1.5 %collective-permute-start.15 = (f16[1,304,128]{2,1,0:T(8,128)(2,1)S(1)}, f16[1,304,128]{2,1,0:T(8,128)(2,1)S(1)}, u32[]{:S(2)}, u32[]{:S(2)}) collective-permute-start(f16[1,304,128]{2,1,0:T(8,128)(2,1)S(1)} %get-tuple-element.56), channel_id=1, source_target_pairs={{0,12},{4,8},{8,4},{12,0},{16,28},{20,24},{24,20},{28,16},{1,13},{... | collective-permute-start | bytes 233480 | tf_op jit(solution)/shard_map/ppermute | solution.py:30
  55.3 1.3 %collective-permute-done.16 = f16[1,304,128]{2,1,0:T(8,128)(2,1)S(1)} collective-permute-done((f16[1,304,128]{2,1,0:T(8,128)(2,1)S(1)}, f16[1,304,128]{2,1,0:T(8,128)(2,1)S(1)}, u32[]{:S(2)}, u32[]{:S(2)}) %collective-permute-start.16) | collective-permute-done | bytes 77856 | tf_op jit(solution)/shard_map/ppermute | solution.py:30
  56.6 1.0 %collective-permute-start.18 = (f16[1,304,128]{2,1,0:T(8,128)(2,1)S(1)}, f16[1,304,128]{2,1,0:T(8,128)(2,1)S(1)}, u32[]{:S(2)}, u32[]{:S(2)}) collective-permute-start(f16[1,304,128]{2,1,0:T(8,128)(2,1)S(1)} %collective-permute-done.16), channel_id=1, source_target_pairs={{0,4},{4,0},{8,12},{12,8},{16,20},{20,16},{24,28},{28,24},{1,5},{5... | collective-permute-start | bytes 233480 | tf_op jit(solution)/shard_map/ppermute | solution.py:30
  57.5 1.1 %collective-permute-start.19 = (f16[1,304,128]{2,1,0:T(8,128)(2,1)S(1)}, f16[1,304,128]{2,1,0:T(8,128)(2,1)S(1)}, u32[]{:S(2)}, u32[]{:S(2)}) collective-permute-start(f16[1,304,128]{2,1,0:T(8,128)(2,1)S(1)} %collective-permute-done.17), channel_id=1, source_target_pairs={{0,4},{4,0},{8,12},{12,8},{16,20},{20,16},{24,28},{28,24},{1,5},{5... | collective-permute-start | bytes 233480 | tf_op jit(solution)/shard_map/ppermute | solution.py:30
  58.6 1.5 %embed.1 = f32[64,128]{1,0:T(8,128)} custom-call(s32[4]{0:T(128)S(1)} %pad_add_fusion.where_ref, f32[256,128]{1,0:T(8,128)S(1)} %get-tuple-element.51.sums_ref, f32[4,72,128]{2,1,0:T(8,128)S(1)} %join.3.refs_0_, f32[4,72,128]{2,1,0:T(8,128)S(1)} %collective-permute-done.5.refs_1_), custom_call_target="tpu_custom_call" | custom-call | tf_op jit(solution)/shard_map/embed/pallas_call | solution.py:781
  61.0 0.9 %collective-permute-done.19 = f16[1,304,128]{2,1,0:T(8,128)(2,1)S(1)} collective-permute-done((f16[1,304,128]{2,1,0:T(8,128)(2,1)S(1)}, f16[1,304,128]{2,1,0:T(8,128)(2,1)S(1)}, u32[]{:S(2)}, u32[]{:S(2)}) %collective-permute-start.19) | collective-permute-done | bytes 77856 | tf_op jit(solution)/shard_map/ppermute | solution.py:30
  61.9 1.7 %spread.1 = (f32[2304,128]{1,0:T(8,128)}, f32[1,128]{1,0:T(1,128)}) custom-call(s32[4]{0:T(128)S(1)} %pad_add_fusion.where_ref, f32[1,304,128]{2,1,0:T(8,128)S(1)} %get-tuple-element.55.refs_0_, f32[1,304,128]{2,1,0:T(8,128)S(1)} %convert_element_type.90.refs_1_, f32[1,304,128]{2,1,0:T(8,128)S(1)} %convert_element_type.91.refs_2_, ...), custom_call_target="tpu_custom_call" | custom-call | tf_op jit(solution)/shard_map/spread/pallas_call | solution.py:678
  (52 shorter events, 2.2 us)
Async XLA Ops:
  3.5 8.9 %collective-permute-start = (bf16[48,768]{1,0:T(8,128)(2,1)S(1)}, bf16[48,768]{1,0:T(8,128)(2,1)S(1)}, u32[]{:S(2)}, u32[]{:S(2)}) collective-permute-start(bf16[48,768]{1,0:T(8,128)(2,1)S(1)} %get-tuple-element.31), channel_id=1, source_target_pairs={{0,4},{2,6},{4,8},{5,1},{6,10},{7,3},{8,12},{9,5},{10,14},{11,7},{... | collective-permute-start | bytes 221192 | tf_op jit(solution)/shard_map/ppermute | solution.py:715
  8.3 4.0 %collective-permute-start.1 = (f32[1,72,128]{2,1,0:T(8,128)S(1)}, f32[1,72,128]{2,1,0:T(8,128)S(1)}, u32[]{:S(2)}, u32[]{:S(2)}) collective-permute-start(f32[1,72,128]{2,1,0:T(8,128)S(1)} %get-tuple-element.32.refs_0_), channel_id=1, source_target_pairs={{0,8},{4,12},{8,0},{12,4},{16,24},{20,28},{24,16},{28,20},{1,9},{5... | collective-permute-start | bytes 110600 | tf_op jit(solution)/shard_map/ppermute | solution.py:30
  11.5 3.6 %copy-start.1 = (f32[256]{0:T(256)S(1)}, f32[256]{0:T(256)}, u32[]{:S(2)}) copy-start(f32[256]{0:T(256)} %param.10) | copy-start | bytes 3076
  12.4 7.3 %collective-permute-start.2 = (f32[2,72,128]{2,1,0:T(8,128)S(1)}, f32[2,72,128]{2,1,0:T(8,128)S(1)}, u32[]{:S(2)}, u32[]{:S(2)}) collective-permute-start(f32[2,72,128]{2,1,0:T(8,128)S(1)} %join.2.refs_0_), channel_id=1, source_target_pairs={{0,16},{4,20},{8,24},{12,28},{16,0},{20,4},{24,8},{28,12},{1,17},{... | collective-permute-start | bytes 221192 | tf_op jit(solution)/shard_map/ppermute | solution.py:30
  19.6 3.5 %copy-start = (s32[24,64]{1,0:T(8,128)S(1)}, s32[24,64]{1,0:T(8,128)}, u32[]{:S(2)}) copy-start(s32[24,64]{1,0:T(8,128)} %lab_ref.1) | copy-start | bytes 18436
  19.6 3.5 %copy-start.2 = (bf16[3,3,256,128]{3,2,1,0:T(8,128)(2,1)S(1)}, bf16[3,3,256,128]{3,2,1,0:T(8,128)(2,1)}, u32[]{:S(2)}) copy-start(bf16[3,3,256,128]{3,2,1,0:T(8,128)(2,1)} %param.11) | copy-start | bytes 1769476
  19.6 3.5 %copy-start.3 = (f32[128]{0:T(128)S(1)}, f32[128]{0:T(128)}, u32[]{:S(2)}) copy-start(f32[128]{0:T(128)} %param.12) | copy-start | bytes 1540
  19.7 3.4 %collective-permute-start.3 = (bf16[12,64,256]{2,1,0:T(8,128)(2,1)S(1)}, bf16[12,64,256]{2,1,0:T(8,128)(2,1)S(1)}, u32[]{:S(2)}, u32[]{:S(2)}) collective-permute-start(bf16[12,64,256]{2,1,0:T(8,128)(2,1)S(1)} %conv_pool.1.refs_2_.refs_0_.own_ref), channel_id=1, source_target_pairs={{0,1},{1,0},{2,3},{3,2},{4,5},{5,4},{6,7},{7,6},{8,9},{9,8},{10,11... | collective-permute-start | bytes 1179656 | tf_op jit(solution)/shard_map/ppermute | solution.py:30
  19.8 2.0 %collective-permute-start.4 = (bf16[48,768]{1,0:T(8,128)(2,1)S(1)}, bf16[48,768]{1,0:T(8,128)(2,1)S(1)}, u32[]{:S(2)}, u32[]{:S(2)}) collective-permute-start(bf16[48,768]{1,0:T(8,128)(2,1)S(1)} %collective-permute-done.refs_1_.got_ref), channel_id=1, source_target_pairs={{0,1},{1,0},{2,3},{3,2},{4,5},{5,4},{6,7},{7,6},{8,9},{9,8},{10,11... | collective-permute-start | bytes 221192 | tf_op jit(solution)/shard_map/ppermute | solution.py:30
  20.3 7.2 %collective-permute-start.5 = (f32[4,72,128]{2,1,0:T(8,128)S(1)}, f32[4,72,128]{2,1,0:T(8,128)S(1)}, u32[]{:S(2)}, u32[]{:S(2)}) collective-permute-start(f32[4,72,128]{2,1,0:T(8,128)S(1)} %join.3.refs_0_), channel_id=1, source_target_pairs={{0,4},{4,0},{8,12},{12,8},{16,20},{20,16},{24,28},{28,24},{1,5},{5... | collective-permute-start | bytes 442376 | tf_op jit(solution)/shard_map/ppermute | solution.py:30
  30.3 7.5 %collective-permute-start.7 = (f16[336,128]{1,0:T(8,128)(2,1)S(1)}, f16[336,128]{1,0:T(8,128)(2,1)S(1)}, u32[]{:S(2)}, u32[]{:S(2)}) collective-permute-start(f16[336,128]{1,0:T(8,128)(2,1)S(1)} %convert_element_type.75), channel_id=1, source_target_pairs={{0,8},{4,12},{8,0},{12,4},{16,24},{20,28},{24,16},{28,20},{1,9},{5... | collective-permute-start | bytes 258056 | tf_op jit(solution)/shard_map/ppermute | solution.py:30
  31.7 6.1 %collective-permute-start.9 = (f16[336,128]{1,0:T(8,128)(2,1)S(1)}, f16[336,128]{1,0:T(8,128)(2,1)S(1)}, u32[]{:S(2)}, u32[]{:S(2)}) collective-permute-start(f16[336,128]{1,0:T(8,128)(2,1)S(1)} %convert_element_type.79), channel_id=1, source_target_pairs={{0,4},{4,0},{8,12},{12,8},{16,20},{20,16},{24,28},{28,24},{1,5},{5... | collective-permute-start | bytes 258056 | tf_op jit(solution)/shard_map/ppermute | solution.py:30
  32.5 5.2 %collective-permute-start.11 = (f16[304,128]{1,0:T(8,128)(2,1)S(1)}, f16[304,128]{1,0:T(8,128)(2,1)S(1)}, u32[]{:S(2)}, u32[]{:S(2)}) collective-permute-start(f16[304,128]{1,0:T(8,128)(2,1)S(1)} %convert_element_type.83), channel_id=1, source_target_pairs={{0,4},{4,0},{8,12},{12,8},{16,20},{20,16},{24,28},{28,24},{1,5},{5... | collective-permute-start | bytes 233480 | tf_op jit(solution)/shard_map/ppermute | solution.py:30
  38.0 9.5 %collective-permute-start.12 = (f16[368,128]{1,0:T(8,128)(2,1)S(1)}, f16[368,128]{1,0:T(8,128)(2,1)S(1)}, u32[]{:S(2)}, u32[]{:S(2)}) collective-permute-start(f16[368,128]{1,0:T(8,128)(2,1)S(1)} %convert_element_type.85), channel_id=1, source_target_pairs={{0,24},{4,28},{8,16},{12,20},{16,8},{20,12},{24,0},{28,4},{1,25},{... | collective-permute-start | bytes 282632 | tf_op jit(solution)/shard_map/ppermute | solution.py:30
  39.0 9.4 %collective-permute-start.10 = (f16[368,128]{1,0:T(8,128)(2,1)S(1)}, f16[368,128]{1,0:T(8,128)(2,1)S(1)}, u32[]{:S(2)}, u32[]{:S(2)}) collective-permute-start(f16[368,128]{1,0:T(8,128)(2,1)S(1)} %convert_element_type.81), channel_id=1, source_target_pairs={{0,16},{4,20},{8,24},{12,28},{16,0},{20,4},{24,8},{28,12},{1,17},{... | collective-permute-start | bytes 282632 | tf_op jit(solution)/shard_map/ppermute | solution.py:30
  40.5 7.0 %collective-permute-start.8 = (f16[336,128]{1,0:T(8,128)(2,1)S(1)}, f16[336,128]{1,0:T(8,128)(2,1)S(1)}, u32[]{:S(2)}, u32[]{:S(2)}) collective-permute-start(f16[336,128]{1,0:T(8,128)(2,1)S(1)} %convert_element_type.77), channel_id=1, source_target_pairs={{0,12},{4,8},{8,4},{12,0},{16,28},{20,24},{24,20},{28,16},{1,13},{... | collective-permute-start | bytes 258056 | tf_op jit(solution)/shard_map/ppermute | solution.py:30
  42.9 4.5 %collective-permute-start.6 = (f16[304,128]{1,0:T(8,128)(2,1)S(1)}, f16[304,128]{1,0:T(8,128)(2,1)S(1)}, u32[]{:S(2)}, u32[]{:S(2)}) collective-permute-start(f16[304,128]{1,0:T(8,128)(2,1)S(1)} %convert_element_type.73), channel_id=1, source_target_pairs={{0,4},{4,0},{8,12},{12,8},{16,20},{20,16},{24,28},{28,24},{1,5},{5... | collective-permute-start | bytes 233480 | tf_op jit(solution)/shard_map/ppermute | solution.py:30
  49.3 7.3 %collective-permute-start.16 = (f16[1,304,128]{2,1,0:T(8,128)(2,1)S(1)}, f16[1,304,128]{2,1,0:T(8,128)(2,1)S(1)}, u32[]{:S(2)}, u32[]{:S(2)}) collective-permute-start(f16[1,304,128]{2,1,0:T(8,128)(2,1)S(1)} %get-tuple-element.56), channel_id=1, source_target_pairs={{0,16},{4,20},{8,24},{12,28},{16,0},{20,4},{24,8},{28,12},{1,17},{... | collective-permute-start | bytes 233480 | tf_op jit(solution)/shard_map/ppermute | solution.py:30
  49.6 7.9 %collective-permute-start.17 = (f16[1,304,128]{2,1,0:T(8,128)(2,1)S(1)}, f16[1,304,128]{2,1,0:T(8,128)(2,1)S(1)}, u32[]{:S(2)}, u32[]{:S(2)}) collective-permute-start(f16[1,304,128]{2,1,0:T(8,128)(2,1)S(1)} %get-tuple-element.56), channel_id=1, source_target_pairs={{0,24},{4,28},{8,16},{12,20},{16,8},{20,12},{24,0},{28,4},{1,25},{... | collective-permute-start | bytes 233480 | tf_op jit(solution)/shard_map/ppermute | solution.py:30
  51.8 8.3 %collective-permute-start.13 = (f16[1,304,128]{2,1,0:T(8,128)(2,1)S(1)}, f16[1,304,128]{2,1,0:T(8,128)(2,1)S(1)}, u32[]{:S(2)}, u32[]{:S(2)}) collective-permute-start(f16[1,304,128]{2,1,0:T(8,128)(2,1)S(1)} %get-tuple-element.56), channel_id=1, source_target_pairs={{0,4},{4,0},{8,12},{12,8},{16,20},{20,16},{24,28},{28,24},{1,5},{5... | collective-permute-start | bytes 233480 | tf_op jit(solution)/shard_map/ppermute | solution.py:30
  52.7 7.5 %collective-permute-start.14 = (f16[1,304,128]{2,1,0:T(8,128)(2,1)S(1)}, f16[1,304,128]{2,1,0:T(8,128)(2,1)S(1)}, u32[]{:S(2)}, u32[]{:S(2)}) collective-permute-start(f16[1,304,128]{2,1,0:T(8,128)(2,1)S(1)} %get-tuple-element.56), channel_id=1, source_target_pairs={{0,8},{4,12},{8,0},{12,4},{16,24},{20,28},{24,16},{28,20},{1,9},{5... | collective-permute-start | bytes 233480 | tf_op jit(solution)/shard_map/ppermute | solution.py:30
  53.8 6.4 %collective-permute-start.15 = (f16[1,304,128]{2,1,0:T(8,128)(2,1)S(1)}, f16[1,304,128]{2,1,0:T(8,128)(2,1)S(1)}, u32[]{:S(2)}, u32[]{:S(2)}) collective-permute-start(f16[1,304,128]{2,1,0:T(8,128)(2,1)S(1)} %get-tuple-element.56), channel_id=1, source_target_pairs={{0,12},{4,8},{8,4},{12,0},{16,28},{20,24},{24,20},{28,16},{1,13},{... | collective-permute-start | bytes 233480 | tf_op jit(solution)/shard_map/ppermute | solution.py:30
  56.6 4.4 %collective-permute-start.18 = (f16[1,304,128]{2,1,0:T(8,128)(2,1)S(1)}, f16[1,304,128]{2,1,0:T(8,128)(2,1)S(1)}, u32[]{:S(2)}, u32[]{:S(2)}) collective-permute-start(f16[1,304,128]{2,1,0:T(8,128)(2,1)S(1)} %collective-permute-done.16), channel_id=1, source_target_pairs={{0,4},{4,0},{8,12},{12,8},{16,20},{20,16},{24,28},{28,24},{1,5},{5... | collective-permute-start | bytes 233480 | tf_op jit(solution)/shard_map/ppermute | solution.py:30
  57.5 4.4 %collective-permute-start.19 = (f16[1,304,128]{2,1,0:T(8,128)(2,1)S(1)}, f16[1,304,128]{2,1,0:T(8,128)(2,1)S(1)}, u32[]{:S(2)}, u32[]{:S(2)}) collective-permute-start(f16[1,304,128]{2,1,0:T(8,128)(2,1)S(1)} %collective-permute-done.17), channel_id=1, source_target_pairs={{0,4},{4,0},{8,12},{12,8},{16,20},{20,16},{24,28},{28,24},{1,5},{5... | collective-permute-start | bytes 233480 | tf_op jit(solution)/shard_map/ppermute | solution.py:30

commit v10 on v9

--- a/solution.py
+++ b/solution.py
@@ -18,6 +18,7 @@
 WIDTH = 3
 PIECE = 4
 STEP = 6
+PAYLOADS = (((0,), 0), ((1,), 0), ((2,), 1), ((3,), 1), ((4,), 0), ((5,), 1), ((6, 7), 1))
 NOTE = 16
 
 
@@ -460,11 +461,10 @@
 
 
 def grad_kernel(
-    where_ref, taps, member, slope, sums_ref, *refs, n_parts, chunk, ways, with_sums
+    where_ref, taps, member, slope, sums_ref, *refs, n_parts, chunk
 ):
     part_refs = refs[:n_parts]
-    out_refs = refs[n_parts : n_parts + ways]
-    (weight,) = refs[n_parts + ways :]
+    out_refs, weight = refs[n_parts:-1], refs[-1]
     rows, cols, depth = member.shape[0], taps.shape[1], taps.shape[2]
     width = slope.shape[-1]
     me = where_ref[3]
@@ -506,34 +506,33 @@
     power, power_sums = scale_rows(weight[...], bias_sum, sums)
     up = jnp.exp2(12.0 - power)
     note = note_block(bias_sum * up, power, power_sums, width)
+    ways = 8
     digit = lax.rem(me, ways)
     heads = weight.shape[0] // chunk // ways
-    for m in range(ways):
-        for hi in range(heads):
+    sums = sums * jnp.exp2(12.0 - power_sums)
+    for out_ref, (members, with_sums) in zip(out_refs, PAYLOADS):
+        at = 0
+        for m, hi in itertools.product(members, range(heads)):
             j = hi * ways + (digit ^ m)
-            out_refs[m][hi * chunk : (hi + 1) * chunk] = (
-                weight[pl.ds(pl.multiple_of(j * chunk, 8), chunk)] * up
-            )
-        out_refs[m][heads * chunk : heads * chunk + NOTE] = note
-    sums = sums * jnp.exp2(12.0 - power_sums)
-    for m in with_sums:
-        out_refs[m][heads * chunk + NOTE :] = sums
-
-
-def deep_backward(where, forward, parts, chunk, count, ways, with_sums):
+            out_ref[at : at + chunk] = weight[pl.ds(pl.multiple_of(j * chunk, 8), chunk)] * up
+            at += chunk
+        out_ref[at : at + NOTE] = note
+        if with_sums:
+            out_ref[at + NOTE :] = sums
+
+
+def deep_backward(where, forward, parts, chunk, count):
     taps, _, slope, sums = forward
     width, entries = slope.shape[-1], sums.shape[0]
-    size = count // ways * chunk + NOTE
+    size = count // 8 * chunk
     return pl.pallas_call(
-        functools.partial(
-            grad_kernel, n_parts=len(parts), chunk=chunk, ways=ways, with_sums=with_sums
-        ),
+        functools.partial(grad_kernel, n_parts=len(parts), chunk=chunk),
         out_shape=tuple(
-            jax.ShapeDtypeStruct((size + (entries if m in with_sums else 0), width), F32)
-            for m in range(ways)
+            jax.ShapeDtypeStruct((len(members) * size + NOTE + with_sums * entries, width), F32)
+            for members, with_sums in PAYLOADS
         ),
         in_specs=[SMEM] + [VMEM] * (4 + len(parts)),
-        out_specs=(VMEM,) * ways,
+        out_specs=(VMEM,) * len(PAYLOADS),
         scratch_shapes=[pltpu.VMEM((count * chunk, width), F32)],
         compiler_params=params(16),
         cost_estimate=pl.CostEstimate(
@@ -543,33 +542,42 @@
     )(where, *forward, *parts)
 
 
-def pair_kernel(own_ref, got_ref, own_sums_ref, got_sums_ref, *refs, size, entries):
+def pair_kernel(own_ref, got_ref, *refs, size, entries, got_at, got_note, with_own):
     out_ref = refs[-1]
-    own, got = own_ref[size : size + NOTE], got_ref[size : size + NOTE]
+    own, got = own_ref[size : size + NOTE], got_ref[got_note : got_note + NOTE]
     power = jnp.maximum(own[1:2], got[1:2]) + 1.0
     power_sums = jnp.maximum(own[2:3], got[2:3])
     own_down, got_down = jnp.exp2(own[1:2] - power), jnp.exp2(got[1:2] - power)
-    out_ref[:size] = own_ref[:size] * own_down + got_ref[:size] * got_down
+    out_ref[:size] = own_ref[:size] * own_down + got_ref[got_at : got_at + size] * got_down
     bias = own[0:1] * own_down + got[0:1] * got_down
     out_ref[size : size + NOTE] = note_block(bias, power, power_sums, own.shape[-1])
     at = size + NOTE
-    sums = own_sums_ref[at : at + entries] * jnp.exp2(own[2:3] - power_sums)
+    if with_own:
+        sums = refs[0][at : at + entries] * jnp.exp2(own[2:3] - power_sums)
+        out_ref[at : at + entries] = sums
+        at += entries
+    sums = got_ref[got_note + NOTE : got_note + NOTE + entries] * jnp.exp2(got[2:3] - power_sums)
     out_ref[at : at + entries] = sums
-    sums = got_sums_ref[at : at + entries] * jnp.exp2(got[2:3] - power_sums)
-    out_ref[at + entries : at + 2 * entries] = sums
-
-
-def merge_pair(own, got, own_sums, got_sums, size, entries, after):
+
+
+def merge_pair(own, got, own_sums, size, entries, got_at, got_note, after):
     width = own.shape[-1]
+    rows = size + NOTE + (1 + len(own_sums)) * entries
     return pl.pallas_call(
-        functools.partial(pair_kernel, size=size, entries=entries),
-        out_shape=jax.ShapeDtypeStruct((size + NOTE + 2 * entries, width), F32),
-        in_specs=[VMEM] * 4 + [ANY] * len(after),
+        functools.partial(
+            pair_kernel,
+            size=size,
+            entries=entries,
+            got_at=got_at,
+            got_note=got_note,
+            with_own=bool(own_sums),
+        ),
+        out_shape=jax.ShapeDtypeStruct((rows, width), F32),
+        in_specs=[VMEM] * (2 + len(own_sums)) + [ANY] * len(after),
         out_specs=VMEM,
         compiler_params=params(),
-        cost_estimate=pl.CostEstimate(flops=0, bytes_accessed=32 << 20, transcendentals=0),
         name="merge_pair",
-    )(own, got, own_sums, got_sums, *after)
+    )(own, got, *own_sums, *after)
 
 
 def merge_kernel(where_ref, *refs, plan, chunk, heads, entries, shift, next_ways):
@@ -578,12 +586,12 @@
     width = part_refs[0].shape[-1]
     size = heads * chunk
     total, bias = jnp.zeros((size, width), F32), jnp.zeros((1, width), F32)
-    for ref, (added, members) in zip(part_refs, plan):
-        more, down, down_sums = read_note(ref, size)
+    for ref, (added, note_at, members) in zip(part_refs, plan):
+        more, down, down_sums = read_note(ref, note_at)
         if added:
             total, bias = total + ref[:size] * down, bias + more
         for k, m in enumerate(members):
-            at = size + NOTE + k * entries
+            at = note_at + NOTE + k * entries
             sums_ref[m * entries : (m + 1) * entries] = ref[at : at + entries] * down_sums
     sums = sums_ref[...]
     power, power_sums = scale_rows(total, bias, sums)
@@ -610,7 +618,7 @@
 
 def merge(where, parts, chunk, heads, entries, shift, next_ways):
     width = parts[0][0].shape[-1]
-    sums_rows = sum(len(members) for _, _, members in parts) * entries
+    sums_rows = sum(len(members) for _, _, _, members in parts) * entries
     if next_ways == 1:
         outs = (jax.ShapeDtypeStruct((heads * chunk + NOTE, width), F32),)
     else:
@@ -620,7 +628,7 @@
     out = pl.pallas_call(
         functools.partial(
             merge_kernel,
-            plan=tuple((added, tuple(members)) for _, added, members in parts),
+            plan=tuple((added, at, tuple(members)) for _, added, at, members in parts),
             chunk=chunk,
             heads=heads,
             entries=entries,
@@ -632,7 +640,7 @@
         out_specs=(VMEM,) * len(outs),
         compiler_params=params(),
         name="merge",
-    )(where, *(part for part, _, _ in parts))
+    )(where, *(part for part, _, _, _ in parts))
     return out[:-1], out[-1]
 
 
@@ -732,10 +740,7 @@
 
     chunk = -(-9 * channels // strip_count // 8) * 8
     bits = strip_count.bit_length() - 1
-    pieces = 1 << min(2, bits - 1)
-    ways = 2 * pieces
-    far = list(range(2, pieces))
-    with_sums = {2, 3} | {2 * k + 1 for k in far[:1]}
+    ways = 8
     forward = deep_forward(
         where,
         pooled,
@@ -746,38 +751,43 @@
         labels,
         entries,
     )
-    send = deep_backward(where, forward, shared, chunk, strip_count, ways, with_sums)
     heads = strip_count // ways
-    got = {k: swap(send[2 * k + 1].astype(F16), "strip", 1).astype(F32) for k in far}
-    parts = [(send[0], True, [])]
-    for m in range(1, min(4, ways)):
-        sent = swap(send[m].astype(F16), "strip", m).astype(F32)
-        parts.append((sent, True, [m] if m in with_sums else []))
-    before = [part for part, _, members in parts if members == [2]]
-    for k in far:
-        own_sums, got_sums = send[2 * far[0] + 1], got[far[0]]
-        pair = merge_pair(send[2 * k], got[k], own_sums, got_sums, heads * chunk, entries, before)
-        before = [pair]
-        sent = swap(pair.astype(F16), "strip", 2 * k).astype(F32)
-        parts.append((sent, True, [2 * k, 2 * k + 1]))
-        if k == far[0]:
-            parts += [(own_sums, False, [0]), (got_sums, False, [1])]
-    held, shift = ways, ways.bit_length() - 1
+    size = heads * chunk
+
+    def sent(part, mask):
+        return swap(part.astype(F16), "strip", mask).astype(F32)
+
+    kept, beside, near, across, paired, pair, far = deep_backward(
+        where, forward, shared, chunk, strip_count
+    )
+    got_far, got_pair = sent(far, 6), sent(pair, 1)
+    onward = merge_pair(paired, got_pair, [pair], size, entries, 0, size, [])
+    beside = merge_pair(beside, got_far, [], size, entries, size, 2 * size, [onward])
+    parts = [
+        (kept, True, size, []),
+        (sent(beside, 1), True, size, [7]),
+        (sent(near, 2), True, size, [2]),
+        (sent(across, 3), True, size, [3]),
+        (sent(onward, 4), True, size, [4, 5]),
+        (got_far, True, 2 * size, [6]),
+        (pair, False, size, [0]),
+        (got_pair, False, size, [1]),
+    ]
+    held, shift = ways, 3
     while True:
-        size = min(3, bits - shift)
-        send, sums = merge(where, parts, chunk, heads, entries, shift, 1 << size)
-        if size == 0:
+        step = min(3, bits - shift)
+        send, sums = merge(where, parts, chunk, heads, entries, shift, 1 << step)
+        if step == 0:
             break
-        more = 1 << size
+        more = 1 << step
         heads //= more
-        arrived = [send[0]] + [
-            swap(send[m].astype(F16), "strip", m << shift).astype(F32) for m in range(1, more)
-        ]
+        arrived = [send[0]] + [sent(send[m], m << shift) for m in range(1, more)]
         parts = [
-            (part, True, list(range(m * held, (m + 1) * held))) for m, part in enumerate(arrived)
+            (part, True, heads * chunk, list(range(m * held, (m + 1) * held)))
+            for m, part in enumerate(arrived)
         ]
         held *= more
-        shift += size
+        shift += step
     embeddings = pl.pallas_call(
         functools.partial(embed_kernel, entries=entries),
         out_shape=jax.ShapeDtypeStruct((owned, width), F32),
@@ -787,12 +797,12 @@
         name="embed",
     )(where, sums, *shared)
     own = send[0].astype(F16)[None]
-    for at in range(ways.bit_length() - 1, bits, 3):
+    for at in range(3, bits, 3):
         own = jnp.concatenate(gather_step(own, "strip", (at, min(3, bits - at))), axis=0)
-    gathered = {m: swap(own, "strip", m) if m else own for m in range(min(4, ways))}
-    for k in far:
+    gathered = {m: swap(own, "strip", m) if m else own for m in range(4)}
+    for k in (2, 3):
         gathered[2 * k] = swap(own, "strip", 2 * k)
-    late = {2 * k + 1: swap(gathered[2 * k], "strip", 1) for k in far}
+    late = {2 * k + 1: swap(gathered[2 * k], "strip", 1) for k in (2, 3)}
     weight_rows, bias_row = spread(
         where, {**gathered, **late}, chunk, strip_count, 9 * channels
     )

time: 63.9 us -> 62.7 us (0.981)
  waiting for transfers between devices: 12 us -> 10.4 us
    ppermute x19 -> x18, waiting for transfers between devices: 12 us -> 10.4 us  [swap(): return lax.ppermute(value, axis, [(i, i ^ mask) for i in range(count)])]
    ppermute x19 -> x18, starting transfers between devices: 24.2 us -> 24.5 us  [swap(): return lax.ppermute(value, axis, [(i, i ^ mask) for i in range(count)])]
  transfers between devices with their start and end apart: 20 -> 19, of which waited for: 7 -> 6; matrix products, arithmetic and copies ran while one was open for 0% -> 0% of each run, Pallas kernels for 21% -> 21%
where the time goes in v10:
time: 62.7 us; the launch traced here: 62.4 us
  starting transfers between devices  29.4 us (47%)
  Pallas kernels  21.3 us (34%)
  waiting for transfers between devices  10.4 us (17%)
  between operations  0.96 us (2%)
    ppermute x18, starting transfers between devices, swap(): return lax.ppermute(value, axis, [(i, i ^ mask) for i in range(count)])  24.5 us
    ppermute x18, waiting for transfers between devices, swap(): return lax.ppermute(value, axis, [(i, i ^ mask) for i in range(count)])  10.4 us
    ppermute x1, starting transfers between devices, body(): got = lax.ppermute(sent, ('strip', 'chan'), pairs)  4.85 us
    pallas_call x1, Pallas kernels, conv_pool(): pl.pallas_call(conv_kernel, out_shape=jax.ShapeDtypeStruct((pooled_rows,...  4.6 us
    pallas_call x1, Pallas kernels, deep_forward(): pl.pallas_call(functools.partial(deep_kernel, block=block, entries=entrie...  4.32 us
    pallas_call x1, Pallas kernels, deep_backward(): pl.pallas_call(functools.partial(grad_kernel, n_parts=len(parts), chunk=c...  2.83 us
    pallas_call x1, Pallas kernels, start(): pl.pallas_call(start_kernel, out_shape=(jax.ShapeDtypeStruct((1, owned +...  2.75 us
    pallas_call x1, Pallas kernels, spread(): pl.pallas_call(functools.partial(spread_kernel, chunk=chunk, rows=rows, m...  1.71 us
  transfers between devices with their start and end apart: 19, of which 6 were waited for; matrix products, arithmetic and copies ran while one was open for 0% of the time, Pallas kernels for 21%

profile of v10, /device:TPU:0, one launch (start us, length us, event | category | flops | bytes accessed | tf_op | source)
XLA Modules:
  0.0 62.4 jit_solution(14581184223109965187)
XLA Ops:
  0.7 2.8 %start.1 = (f32[1,72,128]{2,1,0:T(8,128)S(1)}, bf16[48,768]{1,0:T(8,128)(2,1)S(1)}, bf16[48,768]{1,0:T(8,128)(2,1)S(1)}, bf16[48,768]{1,0:T(8,128)(2,1)S(1)}, bf...) custom-call(s32[4]{0:T(128)S(1)} %pad_add_fusion.where_ref, bf16[48,128,256]{2,1,0:T(8,128)(2,1)} %x_hbm.1, ...), custom_call_target="tpu_custom_call" | custom-call | tf_op jit(solution)/shard_map/start/pallas_call | solution.py:297
  3.5 4.8 %collective-permute-start = (bf16[48,768]{1,0:T(8,128)(2,1)S(1)}, bf16[48,768]{1,0:T(8,128)(2,1)S(1)}, u32[]{:S(2)}, u32[]{:S(2)}) collective-permute-start(bf16[48,768]{1,0:T(8,128)(2,1)S(1)} %get-tuple-element.30), channel_id=1, source_target_pairs={{0,4},{2,6},{4,8},{5,1},{6,10},{7,3},{8,12},{9,5},{10,14},{11,7},{... | collective-permute-start | bytes 221192 | tf_op jit(solution)/shard_map/ppermute | solution.py:723
  8.3 1.6 %collective-permute-start.1 = (f32[1,72,128]{2,1,0:T(8,128)S(1)}, f32[1,72,128]{2,1,0:T(8,128)S(1)}, u32[]{:S(2)}, u32[]{:S(2)}) collective-permute-start(f32[1,72,128]{2,1,0:T(8,128)S(1)} %get-tuple-element.31.refs_0_), channel_id=1, source_target_pairs={{0,8},{4,12},{8,0},{12,4},{16,24},{20,28},{24,16},{28,20},{1,9},{5... | collective-permute-start | bytes 110600 | tf_op jit(solution)/shard_map/ppermute | solution.py:31
  10.0 1.5 %windows.1.refs_2_.taps = bf16[36,64,1024]{2,1,0:T(8,128)(2,1)S(1)} custom-call(s32[4]{0:T(128)S(1)} %pad_add_fusion.where_ref, bf16[28,128,256]{2,1,0:T(8,128)(2,1)S(1)} %get-tuple-element.28.rows_ref), custom_call_target="tpu_custom_call" | custom-call | bytes 12582912 | tf_op jit(solution)/shard_map/windows/pallas_call | solution.py:101
  11.5 0.9 %collective-permute-done.1.refs_1_ = f32[1,72,128]{2,1,0:T(8,128)S(1)} collective-permute-done((f32[1,72,128]{2,1,0:T(8,128)S(1)}, f32[1,72,128]{2,1,0:T(8,128)S(1)}, u32[]{:S(2)}, u32[]{:S(2)}) %collective-permute-start.1) | collective-permute-done | bytes 36896 | tf_op jit(solution)/shard_map/ppermute | solution.py:31
  12.4 2.7 %collective-permute-start.2 = (f32[2,72,128]{2,1,0:T(8,128)S(1)}, f32[2,72,128]{2,1,0:T(8,128)S(1)}, u32[]{:S(2)}, u32[]{:S(2)}) collective-permute-start(f32[2,72,128]{2,1,0:T(8,128)S(1)} %join.2.refs_0_), channel_id=1, source_target_pairs={{0,16},{4,20},{8,24},{12,28},{16,0},{20,4},{24,8},{28,12},{1,17},{... | collective-permute-start | bytes 221192 | tf_op jit(solution)/shard_map/ppermute | solution.py:31
  15.0 4.6 %conv_pool.1.refs_2_.refs_0_.own_ref = bf16[12,64,256]{2,1,0:T(8,128)(2,1)S(1)} custom-call(s32[4]{0:T(128)S(1)} %pad_add_fusion.where_ref, bf16[36,64,1024]{2,1,0:T(8,128)(2,1)S(1)} %windows.1.refs_2_.taps, bf16[2304,256]{1,0:T(8,128)(2,1)S(1)} %get-tuple-element.29.w_ref, f32[1,256]{1,0:T(1,128)S(1)} %bitcast.14, f32[2,72,128]{2,1,0:T(8,128)S(1)} %join.2.refs_0_, ...), custom_call_target="tpu_custom_call" | custom-call | flops 3623878656 | bytes 8388608 | tf_op jit(solution)/shard_map/conv_pool/pallas_call | solution.py:190
  19.8 0.5 collective-permute-start.4
  20.3 1.5 %collective-permute-start.5 = (f32[4,72,128]{2,1,0:T(8,128)S(1)}, f32[4,72,128]{2,1,0:T(8,128)S(1)}, u32[]{:S(2)}, u32[]{:S(2)}) collective-permute-start(f32[4,72,128]{2,1,0:T(8,128)S(1)} %join.3.refs_0_), channel_id=1, source_target_pairs={{0,4},{4,0},{8,12},{12,8},{16,20},{20,16},{24,28},{28,24},{1,5},{5... | collective-permute-start | bytes 442376 | tf_op jit(solution)/shard_map/ppermute | solution.py:31
  21.8 1.3 %conv_edges.1.edge_ref = f32[4,2,24,128]{3,2,1,0:T(8,128)S(1)} custom-call(s32[4]{0:T(128)S(1)} %pad_add_fusion.where_ref, bf16[2304,256]{1,0:T(8,128)(2,1)S(1)} %get-tuple-element.29.w_ref, f32[1,256]{1,0:T(1,128)S(1)} %bitcast.15, bf16[48,768]{1,0:T(8,128)(2,1)S(1)} %collective-permute-done.refs_1_.got_ref, ...), custom_call_target="tpu_custom_call" | custom-call | bytes 4194304 | tf_op jit(solution)/shard_map/conv_edges/pallas_call | solution.py:216
  23.1 4.3 %deep_forward.1 = (bf16[26,64,768]{2,1,0:T(8,128)(2,1)S(1)}, bf16[24,64,128]{2,1,0:T(8,128)(2,1)S(1)}, f32[1536,128]{1,0:T(8,128)S(1)}, f32[32,128]{1,0:T(8,128)S(1)}) custom-call(s32[4]{0:T(128)S(1)} %pad_add_fusion.where_ref, bf16[12,64,256]{2,1,0:T(8,128)(2,1)S(1)} %conv_pool.1.refs_2_.refs_0_.own_ref, ...), custom_call_target="tpu_custom_call" | custom-call | flops 1811939328 | bytes 8388608 | tf_op jit(solution)/shard_map/deep_forward/pallas_call | solution.py:441
  27.5 2.8 %deep_backward.1 = (f32[304,128]{1,0:T(8,128)S(1)}, f32[304,128]{1,0:T(8,128)S(1)}, f32[336,128]{1,0:T(8,128)S(1)}, f32[336,128]{1,0:T(8,128)S(1)}, f32[304,128]...) custom-call(s32[4]{0:T(128)S(1)} %pad_add_fusion.where_ref, ...), custom_call_target="tpu_custom_call" | custom-call | flops 1811939328 | bytes 8388608 | tf_op jit(solution)/shard_map/deep_backward/pallas_call | solution.py:528
  30.3 2.1 %collective-permute-start.6 = (f16[624,128]{1,0:T(8,128)(2,1)S(1)}, f16[624,128]{1,0:T(8,128)(2,1)S(1)}, u32[]{:S(2)}, u32[]{:S(2)}) collective-permute-start(f16[624,128]{1,0:T(8,128)(2,1)S(1)} %convert_element_type.67), channel_id=1, source_target_pairs={{0,24},{4,28},{8,16},{12,20},{16,8},{20,12},{24,0},{28,4},{1,25},{... | collective-permute-start | bytes 479240 | tf_op jit(solution)/shard_map/ppermute | solution.py:31
  32.5 0.8 %collective-permute-start.7 = (f16[336,128]{1,0:T(8,128)(2,1)S(1)}, f16[336,128]{1,0:T(8,128)(2,1)S(1)}, u32[]{:S(2)}, u32[]{:S(2)}) collective-permute-start(f16[336,128]{1,0:T(8,128)(2,1)S(1)} %convert_element_type.69), channel_id=1, source_target_pairs={{0,4},{4,0},{8,12},{12,8},{16,20},{20,16},{24,28},{28,24},{1,5},{5... | collective-permute-start | bytes 258056 | tf_op jit(solution)/shard_map/ppermute | solution.py:31
  33.2 3.8 %collective-permute-done.7 = f16[336,128]{1,0:T(8,128)(2,1)S(1)} collective-permute-done((f16[336,128]{1,0:T(8,128)(2,1)S(1)}, f16[336,128]{1,0:T(8,128)(2,1)S(1)}, u32[]{:S(2)}, u32[]{:S(2)}) %collective-permute-start.7) | collective-permute-done | bytes 86048 | tf_op jit(solution)/shard_map/ppermute | solution.py:31
  37.1 0.8 %collective-permute-start.11 = (f16[368,128]{1,0:T(8,128)(2,1)S(1)}, f16[368,128]{1,0:T(8,128)(2,1)S(1)}, u32[]{:S(2)}, u32[]{:S(2)}) collective-permute-start(f16[368,128]{1,0:T(8,128)(2,1)S(1)} %convert_element_type.77), channel_id=1, source_target_pairs={{0,16},{4,20},{8,24},{12,28},{16,0},{20,4},{24,8},{28,12},{1,17},{... | collective-permute-start | bytes 282632 | tf_op jit(solution)/shard_map/ppermute | solution.py:31
  37.9 1.6 %collective-permute-start.9 = (f16[336,128]{1,0:T(8,128)(2,1)S(1)}, f16[336,128]{1,0:T(8,128)(2,1)S(1)}, u32[]{:S(2)}, u32[]{:S(2)}) collective-permute-start(f16[336,128]{1,0:T(8,128)(2,1)S(1)} %convert_element_type.73), channel_id=1, source_target_pairs={{0,8},{4,12},{8,0},{12,4},{16,24},{20,28},{24,16},{28,20},{1,9},{5... | collective-permute-start | bytes 258056 | tf_op jit(solution)/shard_map/ppermute | solution.py:31
  39.6 0.8 %collective-permute-start.10 = (f16[336,128]{1,0:T(8,128)(2,1)S(1)}, f16[336,128]{1,0:T(8,128)(2,1)S(1)}, u32[]{:S(2)}, u32[]{:S(2)}) collective-permute-start(f16[336,128]{1,0:T(8,128)(2,1)S(1)} %convert_element_type.75), channel_id=1, source_target_pairs={{0,12},{4,8},{8,4},{12,0},{16,28},{20,24},{24,20},{28,16},{1,13},{... | collective-permute-start | bytes 258056 | tf_op jit(solution)/shard_map/ppermute | solution.py:31
  40.5 1.2 %collective-permute-start.8 = (f16[336,128]{1,0:T(8,128)(2,1)S(1)}, f16[336,128]{1,0:T(8,128)(2,1)S(1)}, u32[]{:S(2)}, u32[]{:S(2)}) collective-permute-start(f16[336,128]{1,0:T(8,128)(2,1)S(1)} %convert_element_type.71), channel_id=1, source_target_pairs={{0,4},{4,0},{8,12},{12,8},{16,20},{20,16},{24,28},{28,24},{1,5},{5... | collective-permute-start | bytes 258056 | tf_op jit(solution)/shard_map/ppermute | solution.py:31
  41.7 3.6 %collective-permute-done.9 = f16[336,128]{1,0:T(8,128)(2,1)S(1)} collective-permute-done((f16[336,128]{1,0:T(8,128)(2,1)S(1)}, f16[336,128]{1,0:T(8,128)(2,1)S(1)}, u32[]{:S(2)}, u32[]{:S(2)}) %collective-permute-start.9) | collective-permute-done | bytes 86048 | tf_op jit(solution)/shard_map/ppermute | solution.py:31
  45.3 0.6 collective-permute-done.10
  46.0 0.7 %merge.1 = (f32[304,128]{1,0:T(8,128)S(1)}, f32[256,128]{1,0:T(8,128)S(1)}) custom-call(s32[4]{0:T(128)S(1)} %pad_add_fusion.where_ref, f32[304,128]{1,0:T(8,128)S(1)} %get-tuple-element.42.refs_0_, f32[336,128]{1,0:T(8,128)S(1)} %convert_element_type.72.refs_1_, f32[336,128]{1,0:T(8,128)S(1)} %convert_element_type.74.refs_2_, ...), custom_call_target="tpu_custom_call" | custom-call | tf_op jit(solution)/shard_map/merge/pallas_call | solution.py:628
  46.8 1.8 %collective-permute-start.15 = (f16[1,304,128]{2,1,0:T(8,128)(2,1)S(1)}, f16[1,304,128]{2,1,0:T(8,128)(2,1)S(1)}, u32[]{:S(2)}, u32[]{:S(2)}) collective-permute-start(f16[1,304,128]{2,1,0:T(8,128)(2,1)S(1)} %get-tuple-element.54), channel_id=1, source_target_pairs={{0,16},{4,20},{8,24},{12,28},{16,0},{20,4},{24,8},{28,12},{1,17},{... | collective-permute-start | bytes 233480 | tf_op jit(solution)/shard_map/ppermute | solution.py:31
  48.6 3.4 %collective-permute-start.16 = (f16[1,304,128]{2,1,0:T(8,128)(2,1)S(1)}, f16[1,304,128]{2,1,0:T(8,128)(2,1)S(1)}, u32[]{:S(2)}, u32[]{:S(2)}) collective-permute-start(f16[1,304,128]{2,1,0:T(8,128)(2,1)S(1)} %get-tuple-element.54), channel_id=1, source_target_pairs={{0,24},{4,28},{8,16},{12,20},{16,8},{20,12},{24,0},{28,4},{1,25},{... | collective-permute-start | bytes 233480 | tf_op jit(solution)/shard_map/ppermute | solution.py:31
  52.0 0.7 %collective-permute-start.12 = (f16[1,304,128]{2,1,0:T(8,128)(2,1)S(1)}, f16[1,304,128]{2,1,0:T(8,128)(2,1)S(1)}, u32[]{:S(2)}, u32[]{:S(2)}) collective-permute-start(f16[1,304,128]{2,1,0:T(8,128)(2,1)S(1)} %get-tuple-element.54), channel_id=1, source_target_pairs={{0,4},{4,0},{8,12},{12,8},{16,20},{20,16},{24,28},{28,24},{1,5},{5... | collective-permute-start | bytes 233480 | tf_op jit(solution)/shard_map/ppermute | solution.py:31
  52.7 2.8 %collective-permute-start.14 = (f16[1,304,128]{2,1,0:T(8,128)(2,1)S(1)}, f16[1,304,128]{2,1,0:T(8,128)(2,1)S(1)}, u32[]{:S(2)}, u32[]{:S(2)}) collective-permute-start(f16[1,304,128]{2,1,0:T(8,128)(2,1)S(1)} %get-tuple-element.54), channel_id=1, source_target_pairs={{0,12},{4,8},{8,4},{12,0},{16,28},{20,24},{24,20},{28,16},{1,13},{... | collective-permute-start | bytes 233480 | tf_op jit(solution)/shard_map/ppermute | solution.py:31
  55.5 0.7 %collective-permute-start.17 = (f16[1,304,128]{2,1,0:T(8,128)(2,1)S(1)}, f16[1,304,128]{2,1,0:T(8,128)(2,1)S(1)}, u32[]{:S(2)}, u32[]{:S(2)}) collective-permute-start(f16[1,304,128]{2,1,0:T(8,128)(2,1)S(1)} %collective-permute-done.15), channel_id=1, source_target_pairs={{0,4},{4,0},{8,12},{12,8},{16,20},{20,16},{24,28},{28,24},{1,5},{5... | collective-permute-start | bytes 233480 | tf_op jit(solution)/shard_map/ppermute | solution.py:31
  56.2 1.3 %collective-permute-start.18 = (f16[1,304,128]{2,1,0:T(8,128)(2,1)S(1)}, f16[1,304,128]{2,1,0:T(8,128)(2,1)S(1)}, u32[]{:S(2)}, u32[]{:S(2)}) collective-permute-start(f16[1,304,128]{2,1,0:T(8,128)(2,1)S(1)} %collective-permute-done.16), channel_id=1, source_target_pairs={{0,4},{4,0},{8,12},{12,8},{16,20},{20,16},{24,28},{28,24},{1,5},{5... | collective-permute-start | bytes 233480 | tf_op jit(solution)/shard_map/ppermute | solution.py:31
  57.5 1.5 %embed.1 = f32[64,128]{1,0:T(8,128)} custom-call(s32[4]{0:T(128)S(1)} %pad_add_fusion.where_ref, f32[256,128]{1,0:T(8,128)S(1)} %get-tuple-element.49.sums_ref, f32[4,72,128]{2,1,0:T(8,128)S(1)} %join.3.refs_0_, f32[4,72,128]{2,1,0:T(8,128)S(1)} %collective-permute-done.5.refs_1_), custom_call_target="tpu_custom_call" | custom-call | tf_op jit(solution)/shard_map/embed/pallas_call | solution.py:791
  59.1 0.7 %collective-permute-done.17 = f16[1,304,128]{2,1,0:T(8,128)(2,1)S(1)} collective-permute-done((f16[1,304,128]{2,1,0:T(8,128)(2,1)S(1)}, f16[1,304,128]{2,1,0:T(8,128)(2,1)S(1)}, u32[]{:S(2)}, u32[]{:S(2)}) %collective-permute-start.17) | collective-permute-done | bytes 77856 | tf_op jit(solution)/shard_map/ppermute | solution.py:31
  59.9 0.8 %collective-permute-done.18 = f16[1,304,128]{2,1,0:T(8,128)(2,1)S(1)} collective-permute-done((f16[1,304,128]{2,1,0:T(8,128)(2,1)S(1)}, f16[1,304,128]{2,1,0:T(8,128)(2,1)S(1)}, u32[]{:S(2)}, u32[]{:S(2)}) %collective-permute-start.18) | collective-permute-done | bytes 77856 | tf_op jit(solution)/shard_map/ppermute | solution.py:31
  60.7 1.7 %spread.1 = (f32[2304,128]{1,0:T(8,128)}, f32[1,128]{1,0:T(1,128)}) custom-call(s32[4]{0:T(128)S(1)} %pad_add_fusion.where_ref, f32[1,304,128]{2,1,0:T(8,128)S(1)} %get-tuple-element.53.refs_0_, f32[1,304,128]{2,1,0:T(8,128)S(1)} %convert_element_type.82.refs_1_, f32[1,304,128]{2,1,0:T(8,128)S(1)} %convert_element_type.83.refs_2_, ...), custom_call_target="tpu_custom_call" | custom-call | tf_op jit(solution)/shard_map/spread/pallas_call | solution.py:686
  (48 shorter events, 0.6 us)
Async XLA Ops:
  3.5 8.9 %collective-permute-start = (bf16[48,768]{1,0:T(8,128)(2,1)S(1)}, bf16[48,768]{1,0:T(8,128)(2,1)S(1)}, u32[]{:S(2)}, u32[]{:S(2)}) collective-permute-start(bf16[48,768]{1,0:T(8,128)(2,1)S(1)} %get-tuple-element.30), channel_id=1, source_target_pairs={{0,4},{2,6},{4,8},{5,1},{6,10},{7,3},{8,12},{9,5},{10,14},{11,7},{... | collective-permute-start | bytes 221192 | tf_op jit(solution)/shard_map/ppermute | solution.py:723
  8.3 4.0 %collective-permute-start.1 = (f32[1,72,128]{2,1,0:T(8,128)S(1)}, f32[1,72,128]{2,1,0:T(8,128)S(1)}, u32[]{:S(2)}, u32[]{:S(2)}) collective-permute-start(f32[1,72,128]{2,1,0:T(8,128)S(1)} %get-tuple-element.31.refs_0_), channel_id=1, source_target_pairs={{0,8},{4,12},{8,0},{12,4},{16,24},{20,28},{24,16},{28,20},{1,9},{5... | collective-permute-start | bytes 110600 | tf_op jit(solution)/shard_map/ppermute | solution.py:31
  11.5 3.6 %copy-start.1 = (f32[256]{0:T(256)S(1)}, f32[256]{0:T(256)}, u32[]{:S(2)}) copy-start(f32[256]{0:T(256)} %param.10) | copy-start | bytes 3076
  12.4 7.3 %collective-permute-start.2 = (f32[2,72,128]{2,1,0:T(8,128)S(1)}, f32[2,72,128]{2,1,0:T(8,128)S(1)}, u32[]{:S(2)}, u32[]{:S(2)}) collective-permute-start(f32[2,72,128]{2,1,0:T(8,128)S(1)} %join.2.refs_0_), channel_id=1, source_target_pairs={{0,16},{4,20},{8,24},{12,28},{16,0},{20,4},{24,8},{28,12},{1,17},{... | collective-permute-start | bytes 221192 | tf_op jit(solution)/shard_map/ppermute | solution.py:31
  19.6 3.5 %copy-start = (s32[24,64]{1,0:T(8,128)S(1)}, s32[24,64]{1,0:T(8,128)}, u32[]{:S(2)}) copy-start(s32[24,64]{1,0:T(8,128)} %lab_ref.1) | copy-start | bytes 18436
  19.6 3.5 %copy-start.2 = (bf16[3,3,256,128]{3,2,1,0:T(8,128)(2,1)S(1)}, bf16[3,3,256,128]{3,2,1,0:T(8,128)(2,1)}, u32[]{:S(2)}) copy-start(bf16[3,3,256,128]{3,2,1,0:T(8,128)(2,1)} %param.11) | copy-start | bytes 1769476
  19.7 3.5 %copy-start.3 = (f32[128]{0:T(128)S(1)}, f32[128]{0:T(128)}, u32[]{:S(2)}) copy-start(f32[128]{0:T(128)} %param.12) | copy-start | bytes 1540
  19.7 3.4 %collective-permute-start.3 = (bf16[12,64,256]{2,1,0:T(8,128)(2,1)S(1)}, bf16[12,64,256]{2,1,0:T(8,128)(2,1)S(1)}, u32[]{:S(2)}, u32[]{:S(2)}) collective-permute-start(bf16[12,64,256]{2,1,0:T(8,128)(2,1)S(1)} %conv_pool.1.refs_2_.refs_0_.own_ref), channel_id=1, source_target_pairs={{0,1},{1,0},{2,3},{3,2},{4,5},{5,4},{6,7},{7,6},{8,9},{9,8},{10,11... | collective-permute-start | bytes 1179656 | tf_op jit(solution)/shard_map/ppermute | solution.py:31
  19.8 2.0 %collective-permute-start.4 = (bf16[48,768]{1,0:T(8,128)(2,1)S(1)}, bf16[48,768]{1,0:T(8,128)(2,1)S(1)}, u32[]{:S(2)}, u32[]{:S(2)}) collective-permute-start(bf16[48,768]{1,0:T(8,128)(2,1)S(1)} %collective-permute-done.refs_1_.got_ref), channel_id=1, source_target_pairs={{0,1},{1,0},{2,3},{3,2},{4,5},{5,4},{6,7},{7,6},{8,9},{9,8},{10,11... | collective-permute-start | bytes 221192 | tf_op jit(solution)/shard_map/ppermute | solution.py:31
  20.3 7.2 %collective-permute-start.5 = (f32[4,72,128]{2,1,0:T(8,128)S(1)}, f32[4,72,128]{2,1,0:T(8,128)S(1)}, u32[]{:S(2)}, u32[]{:S(2)}) collective-permute-start(f32[4,72,128]{2,1,0:T(8,128)S(1)} %join.3.refs_0_), channel_id=1, source_target_pairs={{0,4},{4,0},{8,12},{12,8},{16,20},{20,16},{24,28},{28,24},{1,5},{5... | collective-permute-start | bytes 442376 | tf_op jit(solution)/shard_map/ppermute | solution.py:31
  30.3 10.1 %collective-permute-start.6 = (f16[624,128]{1,0:T(8,128)(2,1)S(1)}, f16[624,128]{1,0:T(8,128)(2,1)S(1)}, u32[]{:S(2)}, u32[]{:S(2)}) collective-permute-start(f16[624,128]{1,0:T(8,128)(2,1)S(1)} %convert_element_type.67), channel_id=1, source_target_pairs={{0,24},{4,28},{8,16},{12,20},{16,8},{20,12},{24,0},{28,4},{1,25},{... | collective-permute-start | bytes 479240 | tf_op jit(solution)/shard_map/ppermute | solution.py:31
  32.5 4.6 %collective-permute-start.7 = (f16[336,128]{1,0:T(8,128)(2,1)S(1)}, f16[336,128]{1,0:T(8,128)(2,1)S(1)}, u32[]{:S(2)}, u32[]{:S(2)}) collective-permute-start(f16[336,128]{1,0:T(8,128)(2,1)S(1)} %convert_element_type.69), channel_id=1, source_target_pairs={{0,4},{4,0},{8,12},{12,8},{16,20},{20,16},{24,28},{28,24},{1,5},{5... | collective-permute-start | bytes 258056 | tf_op jit(solution)/shard_map/ppermute | solution.py:31
  37.1 8.9 %collective-permute-start.11 = (f16[368,128]{1,0:T(8,128)(2,1)S(1)}, f16[368,128]{1,0:T(8,128)(2,1)S(1)}, u32[]{:S(2)}, u32[]{:S(2)}) collective-permute-start(f16[368,128]{1,0:T(8,128)(2,1)S(1)} %convert_element_type.77), channel_id=1, source_target_pairs={{0,16},{4,20},{8,24},{12,28},{16,0},{20,4},{24,8},{28,12},{1,17},{... | collective-permute-start | bytes 282632 | tf_op jit(solution)/shard_map/ppermute | solution.py:31
  37.9 7.4 %collective-permute-start.9 = (f16[336,128]{1,0:T(8,128)(2,1)S(1)}, f16[336,128]{1,0:T(8,128)(2,1)S(1)}, u32[]{:S(2)}, u32[]{:S(2)}) collective-permute-start(f16[336,128]{1,0:T(8,128)(2,1)S(1)} %convert_element_type.73), channel_id=1, source_target_pairs={{0,8},{4,12},{8,0},{12,4},{16,24},{20,28},{24,16},{28,20},{1,9},{5... | collective-permute-start | bytes 258056 | tf_op jit(solution)/shard_map/ppermute | solution.py:31
  39.6 6.3 %collective-permute-start.10 = (f16[336,128]{1,0:T(8,128)(2,1)S(1)}, f16[336,128]{1,0:T(8,128)(2,1)S(1)}, u32[]{:S(2)}, u32[]{:S(2)}) collective-permute-start(f16[336,128]{1,0:T(8,128)(2,1)S(1)} %convert_element_type.75), channel_id=1, source_target_pairs={{0,12},{4,8},{8,4},{12,0},{16,28},{20,24},{24,20},{28,16},{1,13},{... | collective-permute-start | bytes 258056 | tf_op jit(solution)/shard_map/ppermute | solution.py:31
  40.5 5.5 %collective-permute-start.8 = (f16[336,128]{1,0:T(8,128)(2,1)S(1)}, f16[336,128]{1,0:T(8,128)(2,1)S(1)}, u32[]{:S(2)}, u32[]{:S(2)}) collective-permute-start(f16[336,128]{1,0:T(8,128)(2,1)S(1)} %convert_element_type.71), channel_id=1, source_target_pairs={{0,4},{4,0},{8,12},{12,8},{16,20},{20,16},{24,28},{28,24},{1,5},{5... | collective-permute-start | bytes 258056 | tf_op jit(solution)/shard_map/ppermute | solution.py:31
  46.8 8.7 %collective-permute-start.15 = (f16[1,304,128]{2,1,0:T(8,128)(2,1)S(1)}, f16[1,304,128]{2,1,0:T(8,128)(2,1)S(1)}, u32[]{:S(2)}, u32[]{:S(2)}) collective-permute-start(f16[1,304,128]{2,1,0:T(8,128)(2,1)S(1)} %get-tuple-element.54), channel_id=1, source_target_pairs={{0,16},{4,20},{8,24},{12,28},{16,0},{20,4},{24,8},{28,12},{1,17},{... | collective-permute-start | bytes 233480 | tf_op jit(solution)/shard_map/ppermute | solution.py:31
  48.6 7.6 %collective-permute-start.16 = (f16[1,304,128]{2,1,0:T(8,128)(2,1)S(1)}, f16[1,304,128]{2,1,0:T(8,128)(2,1)S(1)}, u32[]{:S(2)}, u32[]{:S(2)}) collective-permute-start(f16[1,304,128]{2,1,0:T(8,128)(2,1)S(1)} %get-tuple-element.54), channel_id=1, source_target_pairs={{0,24},{4,28},{8,16},{12,20},{16,8},{20,12},{24,0},{28,4},{1,25},{... | collective-permute-start | bytes 233480 | tf_op jit(solution)/shard_map/ppermute | solution.py:31
  52.0 7.1 %collective-permute-start.12 = (f16[1,304,128]{2,1,0:T(8,128)(2,1)S(1)}, f16[1,304,128]{2,1,0:T(8,128)(2,1)S(1)}, u32[]{:S(2)}, u32[]{:S(2)}) collective-permute-start(f16[1,304,128]{2,1,0:T(8,128)(2,1)S(1)} %get-tuple-element.54), channel_id=1, source_target_pairs={{0,4},{4,0},{8,12},{12,8},{16,20},{20,16},{24,28},{28,24},{1,5},{5... | collective-permute-start | bytes 233480 | tf_op jit(solution)/shard_map/ppermute | solution.py:31
  52.7 6.4 %collective-permute-start.13 = (f16[1,304,128]{2,1,0:T(8,128)(2,1)S(1)}, f16[1,304,128]{2,1,0:T(8,128)(2,1)S(1)}, u32[]{:S(2)}, u32[]{:S(2)}) collective-permute-start(f16[1,304,128]{2,1,0:T(8,128)(2,1)S(1)} %get-tuple-element.54), channel_id=1, source_target_pairs={{0,8},{4,12},{8,0},{12,4},{16,24},{20,28},{24,16},{28,20},{1,9},{5... | collective-permute-start | bytes 233480 | tf_op jit(solution)/shard_map/ppermute | solution.py:31
  52.7 6.4 %collective-permute-start.14 = (f16[1,304,128]{2,1,0:T(8,128)(2,1)S(1)}, f16[1,304,128]{2,1,0:T(8,128)(2,1)S(1)}, u32[]{:S(2)}, u32[]{:S(2)}) collective-permute-start(f16[1,304,128]{2,1,0:T(8,128)(2,1)S(1)} %get-tuple-element.54), channel_id=1, source_target_pairs={{0,12},{4,8},{8,4},{12,0},{16,28},{20,24},{24,20},{28,16},{1,13},{... | collective-permute-start | bytes 233480 | tf_op jit(solution)/shard_map/ppermute | solution.py:31
  55.5 4.4 %collective-permute-start.17 = (f16[1,304,128]{2,1,0:T(8,128)(2,1)S(1)}, f16[1,304,128]{2,1,0:T(8,128)(2,1)S(1)}, u32[]{:S(2)}, u32[]{:S(2)}) collective-permute-start(f16[1,304,128]{2,1,0:T(8,128)(2,1)S(1)} %collective-permute-done.15), channel_id=1, source_target_pairs={{0,4},{4,0},{8,12},{12,8},{16,20},{20,16},{24,28},{28,24},{1,5},{5... | collective-permute-start | bytes 233480 | tf_op jit(solution)/shard_map/ppermute | solution.py:31
  56.2 4.5 %collective-permute-start.18 = (f16[1,304,128]{2,1,0:T(8,128)(2,1)S(1)}, f16[1,304,128]{2,1,0:T(8,128)(2,1)S(1)}, u32[]{:S(2)}, u32[]{:S(2)}) collective-permute-start(f16[1,304,128]{2,1,0:T(8,128)(2,1)S(1)} %collective-permute-done.16), channel_id=1, source_target_pairs={{0,4},{4,0},{8,12},{12,8},{16,20},{20,16},{24,28},{28,24},{1,5},{5... | collective-permute-start | bytes 233480 | tf_op jit(solution)/shard_map/ppermute | solution.py:31

commit v11 on v10

--- a/solution.py
+++ b/solution.py
@@ -11,7 +11,6 @@
 
 F32, BF16, F16 = jnp.float32, jnp.bfloat16, jnp.float16
 VMEM = pl.BlockSpec(memory_space=pltpu.VMEM)
-SMEM = pl.BlockSpec(memory_space=pltpu.SMEM)
 HBM = pl.BlockSpec(memory_space=pltpu.HBM)
 ANY = pl.BlockSpec(memory_space=pl.ANY)
 SIDE = 8
@@ -26,6 +25,17 @@
     return pltpu.CompilerParams(vmem_limit_bytes=mib << 20)
 
 
+def position():
+    strip = lax.axis_index("strip")
+    last = lax.axis_size("strip") - 1
+    return (
+        lax.axis_index("chan") & 1,
+        (strip == 0).astype(jnp.int32),
+        (strip == last).astype(jnp.int32),
+        strip,
+    )
+
+
 def swap(value, axis, mask):
     count = lax.axis_size(axis)
     return lax.ppermute(value, axis, [(i, i ^ mask) for i in range(count)])
@@ -65,10 +75,10 @@
     return most, pick(half, (0, rows - most)), pick(half, (-1, 2 * first - 1 - (rows - most)))
 
 
-def window_kernel(where_ref, rows_ref, taps, wide, *, rows):
+def window_kernel(rows_ref, taps, wide, *, rows):
     most, cols, chans = rows_ref.shape
     half_cols = cols // 2
-    half = where_ref[0]
+    half = position()[0]
     _, _, before = share_rows(half, rows)
     shift = PIECE - before
     lanes = chans // 128
@@ -96,21 +106,21 @@
     taps[outside] = jnp.zeros(taps.shape[1:], BF16)
 
 
-def windows(where, near_rows, rows):
+def windows(near_rows, rows):
     most, cols, chans = near_rows.shape
     return pl.pallas_call(
         functools.partial(window_kernel, rows=rows),
         out_shape=jax.ShapeDtypeStruct((most + 2 * PIECE, cols // 2, 4 * chans), BF16),
-        in_specs=[SMEM, VMEM],
+        in_specs=[VMEM],
         out_specs=VMEM,
         scratch_shapes=[pltpu.VMEM((PIECE * (chans // 128), cols + 16, 128), F32)],
         compiler_params=params(16),
         cost_estimate=pl.CostEstimate(flops=0, bytes_accessed=12 << 20, transcendentals=0),
         name="windows",
-    )(where, near_rows)
-
-
-def edge_part(where_ref, pairs, w_ref, bias, edge_ref, acc):
+    )(near_rows)
+
+
+def edge_part(pairs, w_ref, bias, edge_ref, acc):
     rows = pairs[0].shape[0]
     chans = w_ref.shape[1]
     lanes = chans // 128
@@ -151,12 +161,12 @@
                     + acc[at, pl.ds(9, rows // 2, stride=2), :]
                 )
                 total = both if total is None else total + both
-            lost = jnp.where(g == 0, where_ref[1], jnp.where(g == 3, where_ref[2], 0))
+            lost = jnp.where(g == 0, position()[1], jnp.where(g == 3, position()[2], 0))
             keep = jnp.where(lost > 0, 0.0, 0.25)
             edge_ref[g, t] = (total * keep).astype(BF16).astype(F32)
 
 
-def conv_kernel(where_ref, taps, w_ref, b_ref, *refs):
+def conv_kernel(taps, w_ref, b_ref, *refs):
     out_ref = refs[-1]
     assert out_ref.shape[0] % STEP == 0
     half_cols, chans = taps.shape[1], taps.shape[2] // 4
@@ -184,13 +194,13 @@
         step(k, 0)
 
 
-def conv_pool(where, taps, w, b, pooled_rows, after):
+def conv_pool(taps, w, b, pooled_rows, after):
     _, half_cols, width = taps.shape
     chans = width // 4
     return pl.pallas_call(
         conv_kernel,
         out_shape=jax.ShapeDtypeStruct((pooled_rows, half_cols, chans), BF16),
-        in_specs=[SMEM] + [VMEM] * 3 + [ANY] * len(after),
+        in_specs=[VMEM] * 3 + [ANY] * len(after),
         out_specs=VMEM,
         compiler_params=params(16),
         cost_estimate=pl.CostEstimate(
@@ -199,34 +209,34 @@
             transcendentals=0,
         ),
         name="conv_pool",
-    )(where, taps, w, b, *after)
-
-
-def edge_kernel(where_ref, w_ref, b_ref, got_ref, traded_ref, head_ref, tail_ref, *refs):
+    )(taps, w, b, *after)
+
+
+def edge_kernel(w_ref, b_ref, got_ref, traded_ref, head_ref, tail_ref, *refs):
     edge_ref, acc = refs[-2:]
-    half = where_ref[0]
+    half = position()[0]
     got, traded = got_ref[...], traded_ref[...]
     left = jnp.concatenate([jnp.where(half == 0, got, traded), head_ref[...]], axis=-1)
     right = jnp.concatenate([tail_ref[...], jnp.where(half == 0, traded, got)], axis=-1)
-    edge_part(where_ref, (left, right), w_ref, b_ref[...], edge_ref, acc)
-
-
-def conv_edges(where, w, b, got, traded, head, tail, after):
+    edge_part((left, right), w_ref, b_ref[...], edge_ref, acc)
+
+
+def conv_edges(w, b, got, traded, head, tail, after):
     rows, lanes = head.shape[0], w.shape[1] // 128
     return pl.pallas_call(
         edge_kernel,
         out_shape=jax.ShapeDtypeStruct((4, lanes, rows // 2, 128), F32),
-        in_specs=[SMEM] + [VMEM] * 6 + [ANY] * len(after),
+        in_specs=[VMEM] * 6 + [ANY] * len(after),
         out_specs=VMEM,
         scratch_shapes=[pltpu.VMEM((8 * lanes, rows + 16, 128), F32)],
         compiler_params=params(),
         cost_estimate=pl.CostEstimate(flops=0, bytes_accessed=4 << 20, transcendentals=0),
         name="conv_edges",
-    )(where, w, b, got, traded, head, tail, *after)
+    )(w, b, got, traded, head, tail, *after)
 
 
 def start_kernel(
-    where_ref, x_hbm, w_hbm, grad_hbm, labels_hbm, slots_hbm,
+    x_hbm, w_hbm, grad_hbm, labels_hbm, slots_hbm,
     side_ref, head_ref, tail_ref, send_ref, near_ref, w_ref,
     labels_ref, slots_ref, left, right, wide, sems,
 ):
@@ -234,7 +244,7 @@
     rows, cols, chans = x_hbm.shape
     entries = slots_ref.shape[1]
     reach = left.shape[1]
-    half = where_ref[0]
+    half = position()[0]
     copies = [
         pltpu.make_async_copy(labels_hbm, labels_ref, sems.at[0]),
         pltpu.make_async_copy(grad_hbm, side_ref.at[0, pl.ds(0, owned)], sems.at[1]),
@@ -284,7 +294,7 @@
         copy.wait()
 
 
-def start(where, x, w, grad, slots, labels):
+def start(x, w, grad, slots, labels):
     owned, width = grad.shape
     rows, cols, chans = x.shape
     reach = 16
@@ -299,7 +309,7 @@
         out_shape=(jax.ShapeDtypeStruct((1, owned + SIDE, width), F32),)
         + (columns,) * 3
         + (jax.ShapeDtypeStruct((most, cols, chans), BF16), jax.ShapeDtypeStruct(w.shape, BF16)),
-        in_specs=[SMEM] + [HBM] * 5,
+        in_specs=[HBM] * 5,
         out_specs=(VMEM,) * 6,
         scratch_shapes=[
             pltpu.VMEM(labels.shape, jnp.int32),
@@ -311,7 +321,7 @@
         ],
         compiler_params=params(16),
         name="start",
-    )(where, *fixed)
+    )(*fixed)
 
 
 def join_kernel(*refs, count):
@@ -361,14 +371,14 @@
 
 
 def deep_kernel(
-    where_ref, own_ref, other_ref, edge_ref, w_ref, b_ref, lab_ref, taps, member, slope, sums_ref, wide,
+    own_ref, other_ref, edge_ref, w_ref, b_ref, lab_ref, taps, member, slope, sums_ref, wide,
     inside, *, block, entries
 ):
     _, cols, chans = own_ref.shape
     rows = lab_ref.shape[0]
     lanes = chans // 128
     width = w_ref.shape[-1]
-    half = where_ref[0]
+    half = position()[0]
     taps[0] = jnp.zeros(taps.shape[1:], BF16)
     taps[rows + 1] = jnp.zeros(taps.shape[1:], BF16)
 
@@ -432,7 +442,7 @@
     sums_ref[...] = lax.fori_loop(0, rows // block, step, jnp.zeros((entries, width), F32))
 
 
-def deep_forward(where, own, other, edges, w, b, labels, entries):
+def deep_forward(own, other, edges, w, b, labels, entries):
     _, cols, chans = own.shape
     rows, width = labels.shape[0], w.shape[-1]
     block = next(k for k in (8, 4, 2, 1) if rows % k == 0)
@@ -446,7 +456,7 @@
             jax.ShapeDtypeStruct((rows * cols, width), F32),
             jax.ShapeDtypeStruct((entries, width), F32),
         ),
-        in_specs=[SMEM] + [VMEM] * 6,
+        in_specs=[VMEM] * 6,
         out_specs=(VMEM,) * 4,
         scratch_shapes=[
             pltpu.VMEM((slots * (chans // 128), cols + 16, 128), F32),
@@ -457,17 +467,17 @@
             flops=4 * rows * cols * 9 * chans * width, bytes_accessed=8 << 20, transcendentals=0
         ),
         name="deep_forward",
-    )(where, own, other, edges, w, b, labels)
+    )(own, other, edges, w, b, labels)
 
 
 def grad_kernel(
-    where_ref, taps, member, slope, sums_ref, *refs, n_parts, chunk
+    taps, member, slope, sums_ref, *refs, n_parts, chunk
 ):
     part_refs = refs[:n_parts]
     out_refs, weight = refs[n_parts:-1], refs[-1]
     rows, cols, depth = member.shape[0], taps.shape[1], taps.shape[2]
     width = slope.shape[-1]
-    me = where_ref[3]
+    me = position()[3]
     entries = sums_ref.shape[0]
     owned = part_refs[0].shape[1] - SIDE
     own_ids = jnp.broadcast_to(part_refs[0][0, owned : owned + 1, :entries], (entries, entries))
@@ -521,7 +531,7 @@
             out_ref[at + NOTE :] = sums
 
 
-def deep_backward(where, forward, parts, chunk, count):
+def deep_backward(forward, parts, chunk, count):
     taps, _, slope, sums = forward
     width, entries = slope.shape[-1], sums.shape[0]
     size = count // 8 * chunk
@@ -531,7 +541,7 @@
             jax.ShapeDtypeStruct((len(members) * size + NOTE + with_sums * entries, width), F32)
             for members, with_sums in PAYLOADS
         ),
-        in_specs=[SMEM] + [VMEM] * (4 + len(parts)),
+        in_specs=[VMEM] * (4 + len(parts)),
         out_specs=(VMEM,) * len(PAYLOADS),
         scratch_shapes=[pltpu.VMEM((count * chunk, width), F32)],
         compiler_params=params(16),
@@ -539,7 +549,7 @@
             flops=4 * slope.shape[0] * 3 * taps.shape[2] * width, bytes_accessed=8 << 20, transcendentals=0
         ),
         name="deep_backward",
-    )(where, *forward, *parts)
+    )(*forward, *parts)
 
 
 def pair_kernel(own_ref, got_ref, *refs, size, entries, got_at, got_note, with_own):
@@ -580,7 +590,7 @@
     )(own, got, *own_sums, *after)
 
 
-def merge_kernel(where_ref, *refs, plan, chunk, heads, entries, shift, next_ways):
+def merge_kernel(*refs, plan, chunk, heads, entries, shift, next_ways):
     n_parts = len(plan)
     part_refs, out_refs, sums_ref = refs[:n_parts], refs[n_parts:-1], refs[-1]
     width = part_refs[0].shape[-1]
@@ -603,7 +613,7 @@
         out_refs[0][size:] = note
         return
     sums = sums * jnp.exp2(12.0 - power_sums)
-    digit = lax.rem(where_ref[3] >> shift, next_ways)
+    digit = lax.rem(position()[3] >> shift, next_ways)
     for m in range(next_ways):
         for hi in range(heads // next_ways):
             piece = jnp.zeros((chunk, width), F32)
@@ -616,7 +626,7 @@
         out_refs[m][at + NOTE :] = sums
 
 
-def merge(where, parts, chunk, heads, entries, shift, next_ways):
+def merge(parts, chunk, heads, entries, shift, next_ways):
     width = parts[0][0].shape[-1]
     sums_rows = sum(len(members) for _, _, _, members in parts) * entries
     if next_ways == 1:
@@ -636,18 +646,18 @@
             next_ways=next_ways,
         ),
         out_shape=outs,
-        in_specs=[SMEM] + [VMEM] * len(parts),
+        in_specs=[VMEM] * len(parts),
         out_specs=(VMEM,) * len(outs),
         compiler_params=params(),
         name="merge",
-    )(where, *(part for part, _, _, _ in parts))
+    )(*(part for part, _, _, _ in parts))
     return out[:-1], out[-1]
 
 
-def embed_kernel(where_ref, sums_ref, *refs, entries):
+def embed_kernel(sums_ref, *refs, entries):
     part_refs, out_ref = refs[:-1], refs[-1]
     owned, width = out_ref.shape
-    own = (where_ref[3] * owned + lax.broadcasted_iota(jnp.int32, (owned, entries), 0)).astype(F32)
+    own = (position()[3] * owned + lax.broadcasted_iota(jnp.int32, (owned, entries), 0)).astype(F32)
     sums, counts = jnp.zeros((owned, width), F32), jnp.zeros((owned, 1), F32)
     for m, ref, k in relative(part_refs):
         there = ref[k, owned : owned + 1, :entries] == own
@@ -662,9 +672,9 @@
     out_ref[...] = sums / jnp.maximum(counts, 1.0)
 
 
-def spread_kernel(where_ref, *refs, chunk, rows, members):
+def spread_kernel(*refs, chunk, rows, members):
     part_refs, weight_ref, bias_ref, place = refs[:-3], refs[-3], refs[-2], refs[-1]
-    me = where_ref[3]
+    me = position()[3]
     count = len(members)
     for p, k in itertools.product(range(count), range(part_refs[0].shape[0])):
         bias, down, _ = read_note(part_refs[p][k], chunk)
@@ -680,18 +690,18 @@
         weight_ref[...] = place[:rows]
 
 
-def spread(where, parts, chunk, count, rows):
+def spread(parts, chunk, count, rows):
     parts = {m: part.astype(F32) for m, part in parts.items()}
     width = parts[0].shape[-1]
     return pl.pallas_call(
         functools.partial(spread_kernel, chunk=chunk, rows=rows, members=tuple(parts)),
         out_shape=(jax.ShapeDtypeStruct((rows, width), F32), jax.ShapeDtypeStruct((1, width), F32)),
-        in_specs=[SMEM] + [VMEM] * len(parts),
+        in_specs=[VMEM] * len(parts),
         out_specs=(VMEM, VMEM),
         scratch_shapes=[pltpu.VMEM((count * chunk, width), F32)],
         compiler_params=params(),
         name="spread",
-    )(where, *parts.values())
+    )(*parts.values())
 
 
 def body(
@@ -699,20 +709,14 @@
 ):
     chan_count = lax.axis_size("chan")
     strip_count = lax.axis_size("strip")
-    chan_pos = lax.axis_index("chan")
-    strip_pos = lax.axis_index("strip")
-    half = chan_pos & 1
     channels = section_input.shape[-1]
     entries = slot_ids.shape[0]
     owned, width = embed_grad.shape
-    where = jnp.stack(
-        [half, (strip_pos == 0).astype(jnp.int32), (strip_pos == strip_count - 1).astype(jnp.int32), strip_pos]
-    ).astype(jnp.int32)
     conv_w = conv_weight.reshape(9 * channels, -1)
     conv_b = conv_bias.reshape(1, -1)
 
     side, head, tail, sent, near_rows, near_w = start(
-        where, section_input, conv_w, embed_grad, slot_ids, labels
+        section_input, conv_w, embed_grad, slot_ids, labels
     )
     pairs = []
     for s in range(strip_count):
@@ -725,25 +729,24 @@
     steps = [(at + 1, 1) for at in range(min(2, strip_count.bit_length() - 2))]
     steps += [(at, min(3, strip_count.bit_length() - 1 - at)) for at in range(3, strip_count.bit_length() - 1, 3)]
     ahead = gather_step(side, "strip", steps[0])
-    taps = windows(where, near_rows, section_input.shape[0])
+    taps = windows(near_rows, section_input.shape[0])
     shared = join(ahead, [taps])
     got, shared = lax.optimization_barrier((got, shared))
     traded = swap(got, "chan", 1)
     ahead = gather_step(shared, "strip", steps[1])
-    pooled = conv_pool(where, taps, near_w, conv_b, section_input.shape[0] // 4, [shared, got])
+    pooled = conv_pool(taps, near_w, conv_b, section_input.shape[0] // 4, [shared, got])
     pooled, shared = lax.optimization_barrier((pooled, join(ahead, [pooled])))
     other = swap(pooled, "chan", 1)
     for step in steps[2:]:
         shared = join(gather_step(shared, "strip", step), [])
     shared = [shared, swap(shared, "strip", 1)]
-    edges = conv_edges(where, near_w, conv_b, got, traded, head, tail, [pooled])
+    edges = conv_edges(near_w, conv_b, got, traded, head, tail, [pooled])
 
     chunk = -(-9 * channels // strip_count // 8) * 8
     bits = strip_count.bit_length() - 1
     ways = 8
     forward = deep_forward(
-        where,
-        pooled,
+                pooled,
         other,
         edges,
         deep_weight.reshape(9 * channels, width),
@@ -758,7 +761,7 @@
         return swap(part.astype(F16), "strip", mask).astype(F32)
 
     kept, beside, near, across, paired, pair, far = deep_backward(
-        where, forward, shared, chunk, strip_count
+        forward, shared, chunk, strip_count
     )
     got_far, got_pair = sent(far, 6), sent(pair, 1)
     onward = merge_pair(paired, got_pair, [pair], size, entries, 0, size, [])
@@ -776,7 +779,7 @@
     held, shift = ways, 3
     while True:
         step = min(3, bits - shift)
-        send, sums = merge(where, parts, chunk, heads, entries, shift, 1 << step)
+        send, sums = merge(parts, chunk, heads, entries, shift, 1 << step)
         if step == 0:
             break
         more = 1 << step
@@ -791,11 +794,11 @@
     embeddings = pl.pallas_call(
         functools.partial(embed_kernel, entries=entries),
         out_shape=jax.ShapeDtypeStruct((owned, width), F32),
-        in_specs=[SMEM] + [VMEM] * (1 + len(shared)),
+        in_specs=[VMEM] * (1 + len(shared)),
         out_specs=VMEM,
         compiler_params=params(),
         name="embed",
-    )(where, sums, *shared)
+    )(sums, *shared)
     own = send[0].astype(F16)[None]
     for at in range(3, bits, 3):
         own = jnp.concatenate(gather_step(own, "strip", (at, min(3, bits - at))), axis=0)
@@ -804,7 +807,7 @@
         gathered[2 * k] = swap(own, "strip", 2 * k)
     late = {2 * k + 1: swap(gathered[2 * k], "strip", 1) for k in (2, 3)}
     weight_rows, bias_row = spread(
-        where, {**gathered, **late}, chunk, strip_count, 9 * channels
+        {**gathered, **late}, chunk, strip_count, 9 * channels
     )
     return (embeddings, weight_rows.reshape(3, 3, channels, width), bias_row[0])
 

time: 62.7 us -> 58.8 us (0.938)
  Pallas kernels: 21.3 us -> 16.4 us
  waiting for transfers between devices: 10.4 us -> 11.5 us
    ppermute x18, waiting for transfers between devices: 10.4 us -> 11.5 us  [swap(): return lax.ppermute(value, axis, [(i, i ^ mask) for i in range(count)])]
  transfers between devices with their start and end apart: 19 -> 19, of which waited for: 6 -> 7; matrix products, arithmetic and copies ran while one was open for 0% -> 0% of each run, Pallas kernels for 21% -> 18%
where the time goes in v11:
time: 58.8 us; the launch traced here: 58.5 us
  starting transfers between devices  29.4 us (50%)
  Pallas kernels  16.4 us (28%)
  waiting for transfers between devices  11.5 us (20%)
  between operations  0.95 us (2%)
    ppermute x18, starting transfers between devices, swap(): return lax.ppermute(value, axis, [(i, i ^ mask) for i in range(count)])  24.5 us
    ppermute x18, waiting for transfers between devices, swap(): return lax.ppermute(value, axis, [(i, i ^ mask) for i in range(count)])  11.5 us
    ppermute x1, starting transfers between devices, body(): got = lax.ppermute(sent, ('strip', 'chan'), pairs)  4.85 us
    pallas_call x1, Pallas kernels, conv_pool(): pl.pallas_call(conv_kernel, out_shape=jax.ShapeDtypeStruct((pooled_rows,...  4.05 us
    pallas_call x1, Pallas kernels, deep_forward(): pl.pallas_call(functools.partial(deep_kernel, block=block, entries=entrie...  3.76 us
    pallas_call x1, Pallas kernels, deep_backward(): pl.pallas_call(functools.partial(grad_kernel, n_parts=len(parts), chunk=c...  2.28 us
    pallas_call x1, Pallas kernels, start(): pl.pallas_call(start_kernel, out_shape=(jax.ShapeDtypeStruct((1, owned +...  2.21 us
  transfers between devices with their start and end apart: 19, of which 7 were waited for; matrix products, arithmetic and copies ran while one was open for 0% of the time, Pallas kernels for 18%

profile of v11, /device:TPU:0, one launch (start us, length us, event | category | flops | bytes accessed | tf_op | source)
XLA Modules:
  0.0 58.5 jit_solution(12471800203810914765)
XLA Ops:
  0.6 2.2 %start.1 = (f32[1,72,128]{2,1,0:T(8,128)S(1)}, bf16[48,768]{1,0:T(8,128)(2,1)S(1)}, bf16[48,768]{1,0:T(8,128)(2,1)S(1)}, bf16[48,768]{1,0:T(8,128)(2,1)S(1)}, bf...) custom-call(bf16[48,128,256]{2,1,0:T(8,128)(2,1)} %x_hbm.1, bf16[2304,256]{1,0:T(8,128)(2,1)} %bitcast.14, ...), custom_call_target="tpu_custom_call" | custom-call | tf_op jit(solution)/shard_map/start/pallas_call | solution.py:307
  2.9 4.8 %collective-permute-start = (bf16[48,768]{1,0:T(8,128)(2,1)S(1)}, bf16[48,768]{1,0:T(8,128)(2,1)S(1)}, u32[]{:S(2)}, u32[]{:S(2)}) collective-permute-start(bf16[48,768]{1,0:T(8,128)(2,1)S(1)} %get-tuple-element.30), channel_id=1, source_target_pairs={{0,4},{2,6},{4,8},{5,1},{6,10},{7,3},{8,12},{9,5},{10,14},{11,7},{... | collective-permute-start | bytes 221192 | tf_op jit(solution)/shard_map/ppermute | solution.py:727
  7.7 1.6 %collective-permute-start.1 = (f32[1,72,128]{2,1,0:T(8,128)S(1)}, f32[1,72,128]{2,1,0:T(8,128)S(1)}, u32[]{:S(2)}, u32[]{:S(2)}) collective-permute-start(f32[1,72,128]{2,1,0:T(8,128)S(1)} %get-tuple-element.31.refs_0_), channel_id=1, source_target_pairs={{0,8},{4,12},{8,0},{12,4},{16,24},{20,28},{24,16},{28,20},{1,9},{5... | collective-permute-start | bytes 110600 | tf_op jit(solution)/shard_map/ppermute | solution.py:41
  9.3 0.9 %windows.1.refs_2_.taps = bf16[36,64,1024]{2,1,0:T(8,128)(2,1)S(1)} custom-call(bf16[28,128,256]{2,1,0:T(8,128)(2,1)S(1)} %get-tuple-element.28.rows_ref), custom_call_target="tpu_custom_call" | custom-call | bytes 12582912 | tf_op jit(solution)/shard_map/windows/pallas_call | solution.py:111
  10.3 1.4 %collective-permute-done.1.refs_1_ = f32[1,72,128]{2,1,0:T(8,128)S(1)} collective-permute-done((f32[1,72,128]{2,1,0:T(8,128)S(1)}, f32[1,72,128]{2,1,0:T(8,128)S(1)}, u32[]{:S(2)}, u32[]{:S(2)}) %collective-permute-start.1) | collective-permute-done | bytes 36896 | tf_op jit(solution)/shard_map/ppermute | solution.py:41
  11.7 2.7 %collective-permute-start.2 = (f32[2,72,128]{2,1,0:T(8,128)S(1)}, f32[2,72,128]{2,1,0:T(8,128)S(1)}, u32[]{:S(2)}, u32[]{:S(2)}) collective-permute-start(f32[2,72,128]{2,1,0:T(8,128)S(1)} %join.2.refs_0_), channel_id=1, source_target_pairs={{0,16},{4,20},{8,24},{12,28},{16,0},{20,4},{24,8},{28,12},{1,17},{... | collective-permute-start | bytes 221192 | tf_op jit(solution)/shard_map/ppermute | solution.py:41
  14.4 4.1 %conv_pool.1.refs_2_.refs_0_.own_ref = bf16[12,64,256]{2,1,0:T(8,128)(2,1)S(1)} custom-call(bf16[36,64,1024]{2,1,0:T(8,128)(2,1)S(1)} %windows.1.refs_2_.taps, bf16[2304,256]{1,0:T(8,128)(2,1)S(1)} %get-tuple-element.29.w_ref, f32[1,256]{1,0:T(1,128)S(1)} %bitcast.10, f32[2,72,128]{2,1,0:T(8,128)S(1)} %join.2.refs_0_, ...), custom_call_target="tpu_custom_call" | custom-call | flops 3623878656 | bytes 8388608 | tf_op jit(solution)/shard_map/conv_pool/pallas_call | solution.py:200
  18.6 0.5 collective-permute-start.4
  19.1 1.5 %collective-permute-start.5 = (f32[4,72,128]{2,1,0:T(8,128)S(1)}, f32[4,72,128]{2,1,0:T(8,128)S(1)}, u32[]{:S(2)}, u32[]{:S(2)}) collective-permute-start(f32[4,72,128]{2,1,0:T(8,128)S(1)} %join.3.refs_0_), channel_id=1, source_target_pairs={{0,4},{4,0},{8,12},{12,8},{16,20},{20,16},{24,28},{28,24},{1,5},{5... | collective-permute-start | bytes 442376 | tf_op jit(solution)/shard_map/ppermute | solution.py:41
  20.7 0.7 %conv_edges.1.edge_ref = f32[4,2,24,128]{3,2,1,0:T(8,128)S(1)} custom-call(bf16[2304,256]{1,0:T(8,128)(2,1)S(1)} %get-tuple-element.29.w_ref, f32[1,256]{1,0:T(1,128)S(1)} %bitcast.11, bf16[48,768]{1,0:T(8,128)(2,1)S(1)} %collective-permute-done.refs_1_.got_ref, bf16[48,768]{1,0:T(8,128)(2,1)S(1)} %collective-permute-done.4.traded_ref, ...), custom_call_target="tpu_custom_call" | custom-call | bytes 4194304 | tf_op jit(solution)/shard_map/conv_edges/pallas_call | solution.py:226
  21.4 3.8 %deep_forward.1 = (bf16[26,64,768]{2,1,0:T(8,128)(2,1)S(1)}, bf16[24,64,128]{2,1,0:T(8,128)(2,1)S(1)}, f32[1536,128]{1,0:T(8,128)S(1)}, f32[32,128]{1,0:T(8,128)S(1)}) custom-call(bf16[12,64,256]{2,1,0:T(8,128)(2,1)S(1)} %conv_pool.1.refs_2_.refs_0_.own_ref, bf16[12,64,256]{2,1,0:T(8,128)(2,1)S(1)} %collective-permute-done.3.other_ref, ...), custom_call_target="tpu_custom_call" | custom-call | flops 1811939328 | bytes 8388608 | tf_op jit(solution)/shard_map/deep_forward/pallas_call | solution.py:451
  25.2 2.3 %deep_backward.1 = (f32[304,128]{1,0:T(8,128)S(1)}, f32[304,128]{1,0:T(8,128)S(1)}, f32[336,128]{1,0:T(8,128)S(1)}, f32[336,128]{1,0:T(8,128)S(1)}, f32[304,128]...) custom-call(bf16[26,64,768]{2,1,0:T(8,128)(2,1)S(1)} %get-tuple-element.37.taps, ...), custom_call_target="tpu_custom_call" | custom-call | flops 1811939328 | bytes 8388608 | tf_op jit(solution)/shard_map/deep_backward/pallas_call | solution.py:538
  27.5 2.7 %collective-permute-start.6 = (f16[624,128]{1,0:T(8,128)(2,1)S(1)}, f16[624,128]{1,0:T(8,128)(2,1)S(1)}, u32[]{:S(2)}, u32[]{:S(2)}) collective-permute-start(f16[624,128]{1,0:T(8,128)(2,1)S(1)} %convert_element_type.65), channel_id=1, source_target_pairs={{0,24},{4,28},{8,16},{12,20},{16,8},{20,12},{24,0},{28,4},{1,25},{... | collective-permute-start | bytes 479240 | tf_op jit(solution)/shard_map/ppermute | solution.py:41
  30.2 0.8 %collective-permute-start.7 = (f16[336,128]{1,0:T(8,128)(2,1)S(1)}, f16[336,128]{1,0:T(8,128)(2,1)S(1)}, u32[]{:S(2)}, u32[]{:S(2)}) collective-permute-start(f16[336,128]{1,0:T(8,128)(2,1)S(1)} %convert_element_type.67), channel_id=1, source_target_pairs={{0,4},{4,0},{8,12},{12,8},{16,20},{20,16},{24,28},{28,24},{1,5},{5... | collective-permute-start | bytes 258056 | tf_op jit(solution)/shard_map/ppermute | solution.py:41
  31.0 3.8 %collective-permute-done.7 = f16[336,128]{1,0:T(8,128)(2,1)S(1)} collective-permute-done((f16[336,128]{1,0:T(8,128)(2,1)S(1)}, f16[336,128]{1,0:T(8,128)(2,1)S(1)}, u32[]{:S(2)}, u32[]{:S(2)}) %collective-permute-start.7) | collective-permute-done | bytes 86048 | tf_op jit(solution)/shard_map/ppermute | solution.py:41
  34.8 0.3 collective-permute-start.11
  35.1 1.6 %collective-permute-start.9 = (f16[336,128]{1,0:T(8,128)(2,1)S(1)}, f16[336,128]{1,0:T(8,128)(2,1)S(1)}, u32[]{:S(2)}, u32[]{:S(2)}) collective-permute-start(f16[336,128]{1,0:T(8,128)(2,1)S(1)} %convert_element_type.71), channel_id=1, source_target_pairs={{0,8},{4,12},{8,0},{12,4},{16,24},{20,28},{24,16},{28,20},{1,9},{5... | collective-permute-start | bytes 258056 | tf_op jit(solution)/shard_map/ppermute | solution.py:41
  36.8 0.8 %collective-permute-start.10 = (f16[336,128]{1,0:T(8,128)(2,1)S(1)}, f16[336,128]{1,0:T(8,128)(2,1)S(1)}, u32[]{:S(2)}, u32[]{:S(2)}) collective-permute-start(f16[336,128]{1,0:T(8,128)(2,1)S(1)} %convert_element_type.73), channel_id=1, source_target_pairs={{0,12},{4,8},{8,4},{12,0},{16,28},{20,24},{24,20},{28,16},{1,13},{... | collective-permute-start | bytes 258056 | tf_op jit(solution)/shard_map/ppermute | solution.py:41
  37.7 1.2 %collective-permute-start.8 = (f16[336,128]{1,0:T(8,128)(2,1)S(1)}, f16[336,128]{1,0:T(8,128)(2,1)S(1)}, u32[]{:S(2)}, u32[]{:S(2)}) collective-permute-start(f16[336,128]{1,0:T(8,128)(2,1)S(1)} %convert_element_type.69), channel_id=1, source_target_pairs={{0,4},{4,0},{8,12},{12,8},{16,20},{20,16},{24,28},{28,24},{1,5},{5... | collective-permute-start | bytes 258056 | tf_op jit(solution)/shard_map/ppermute | solution.py:41
  38.9 3.3 %collective-permute-done.9 = f16[336,128]{1,0:T(8,128)(2,1)S(1)} collective-permute-done((f16[336,128]{1,0:T(8,128)(2,1)S(1)}, f16[336,128]{1,0:T(8,128)(2,1)S(1)}, u32[]{:S(2)}, u32[]{:S(2)}) %collective-permute-start.9) | collective-permute-done | bytes 86048 | tf_op jit(solution)/shard_map/ppermute | solution.py:41
  42.2 0.9 %collective-permute-done.10 = f16[336,128]{1,0:T(8,128)(2,1)S(1)} collective-permute-done((f16[336,128]{1,0:T(8,128)(2,1)S(1)}, f16[336,128]{1,0:T(8,128)(2,1)S(1)}, u32[]{:S(2)}, u32[]{:S(2)}) %collective-permute-start.10) | collective-permute-done | bytes 86048 | tf_op jit(solution)/shard_map/ppermute | solution.py:41
  43.2 0.2 merge.1
  43.5 2.0 %collective-permute-start.15 = (f16[1,304,128]{2,1,0:T(8,128)(2,1)S(1)}, f16[1,304,128]{2,1,0:T(8,128)(2,1)S(1)}, u32[]{:S(2)}, u32[]{:S(2)}) collective-permute-start(f16[1,304,128]{2,1,0:T(8,128)(2,1)S(1)} %get-tuple-element.54), channel_id=1, source_target_pairs={{0,16},{4,20},{8,24},{12,28},{16,0},{20,4},{24,8},{28,12},{1,17},{... | collective-permute-start | bytes 233480 | tf_op jit(solution)/shard_map/ppermute | solution.py:41
  45.4 3.2 %collective-permute-start.16 = (f16[1,304,128]{2,1,0:T(8,128)(2,1)S(1)}, f16[1,304,128]{2,1,0:T(8,128)(2,1)S(1)}, u32[]{:S(2)}, u32[]{:S(2)}) collective-permute-start(f16[1,304,128]{2,1,0:T(8,128)(2,1)S(1)} %get-tuple-element.54), channel_id=1, source_target_pairs={{0,24},{4,28},{8,16},{12,20},{16,8},{20,12},{24,0},{28,4},{1,25},{... | collective-permute-start | bytes 233480 | tf_op jit(solution)/shard_map/ppermute | solution.py:41
  48.6 0.7 %collective-permute-start.12 = (f16[1,304,128]{2,1,0:T(8,128)(2,1)S(1)}, f16[1,304,128]{2,1,0:T(8,128)(2,1)S(1)}, u32[]{:S(2)}, u32[]{:S(2)}) collective-permute-start(f16[1,304,128]{2,1,0:T(8,128)(2,1)S(1)} %get-tuple-element.54), channel_id=1, source_target_pairs={{0,4},{4,0},{8,12},{12,8},{16,20},{20,16},{24,28},{28,24},{1,5},{5... | collective-permute-start | bytes 233480 | tf_op jit(solution)/shard_map/ppermute | solution.py:41
  49.4 2.8 %collective-permute-start.14 = (f16[1,304,128]{2,1,0:T(8,128)(2,1)S(1)}, f16[1,304,128]{2,1,0:T(8,128)(2,1)S(1)}, u32[]{:S(2)}, u32[]{:S(2)}) collective-permute-start(f16[1,304,128]{2,1,0:T(8,128)(2,1)S(1)} %get-tuple-element.54), channel_id=1, source_target_pairs={{0,12},{4,8},{8,4},{12,0},{16,28},{20,24},{24,20},{28,16},{1,13},{... | collective-permute-start | bytes 233480 | tf_op jit(solution)/shard_map/ppermute | solution.py:41
  52.1 0.7 %collective-permute-start.17 = (f16[1,304,128]{2,1,0:T(8,128)(2,1)S(1)}, f16[1,304,128]{2,1,0:T(8,128)(2,1)S(1)}, u32[]{:S(2)}, u32[]{:S(2)}) collective-permute-start(f16[1,304,128]{2,1,0:T(8,128)(2,1)S(1)} %collective-permute-done.15), channel_id=1, source_target_pairs={{0,4},{4,0},{8,12},{12,8},{16,20},{20,16},{24,28},{28,24},{1,5},{5... | collective-permute-start | bytes 233480 | tf_op jit(solution)/shard_map/ppermute | solution.py:41
  52.9 1.3 %collective-permute-start.18 = (f16[1,304,128]{2,1,0:T(8,128)(2,1)S(1)}, f16[1,304,128]{2,1,0:T(8,128)(2,1)S(1)}, u32[]{:S(2)}, u32[]{:S(2)}) collective-permute-start(f16[1,304,128]{2,1,0:T(8,128)(2,1)S(1)} %collective-permute-done.16), channel_id=1, source_target_pairs={{0,4},{4,0},{8,12},{12,8},{16,20},{20,16},{24,28},{28,24},{1,5},{5... | collective-permute-start | bytes 233480 | tf_op jit(solution)/shard_map/ppermute | solution.py:41
  54.2 1.0 %embed.1 = f32[64,128]{1,0:T(8,128)} custom-call(f32[256,128]{1,0:T(8,128)S(1)} %get-tuple-element.49.sums_ref, f32[4,72,128]{2,1,0:T(8,128)S(1)} %join.3.refs_0_, f32[4,72,128]{2,1,0:T(8,128)S(1)} %collective-permute-done.5.refs_1_), custom_call_target="tpu_custom_call" | custom-call | tf_op jit(solution)/shard_map/embed/pallas_call | solution.py:794
  55.3 1.2 %collective-permute-done.17 = f16[1,304,128]{2,1,0:T(8,128)(2,1)S(1)} collective-permute-done((f16[1,304,128]{2,1,0:T(8,128)(2,1)S(1)}, f16[1,304,128]{2,1,0:T(8,128)(2,1)S(1)}, u32[]{:S(2)}, u32[]{:S(2)}) %collective-permute-start.17) | collective-permute-done | bytes 77856 | tf_op jit(solution)/shard_map/ppermute | solution.py:41
  56.5 0.8 %collective-permute-done.18 = f16[1,304,128]{2,1,0:T(8,128)(2,1)S(1)} collective-permute-done((f16[1,304,128]{2,1,0:T(8,128)(2,1)S(1)}, f16[1,304,128]{2,1,0:T(8,128)(2,1)S(1)}, u32[]{:S(2)}, u32[]{:S(2)}) %collective-permute-start.18) | collective-permute-done | bytes 77856 | tf_op jit(solution)/shard_map/ppermute | solution.py:41
  57.4 1.2 %spread.1 = (f32[2304,128]{1,0:T(8,128)}, f32[1,128]{1,0:T(1,128)}) custom-call(f32[1,304,128]{2,1,0:T(8,128)S(1)} %get-tuple-element.53.refs_0_, f32[1,304,128]{2,1,0:T(8,128)S(1)} %convert_element_type.80.refs_1_, f32[1,304,128]{2,1,0:T(8,128)S(1)} %convert_element_type.81.refs_2_, f32[1,304,128]{2,1,0:T(8,128)S(1)} %convert_element_type.82.refs_3_, ...), custom_call_target="tpu_custom_call" | custom-call | tf_op jit(solution)/shard_map/spread/pallas_call | solution.py:696
  (47 shorter events, 0.6 us)
Async XLA Ops:
  2.9 8.9 %collective-permute-start = (bf16[48,768]{1,0:T(8,128)(2,1)S(1)}, bf16[48,768]{1,0:T(8,128)(2,1)S(1)}, u32[]{:S(2)}, u32[]{:S(2)}) collective-permute-start(bf16[48,768]{1,0:T(8,128)(2,1)S(1)} %get-tuple-element.30), channel_id=1, source_target_pairs={{0,4},{2,6},{4,8},{5,1},{6,10},{7,3},{8,12},{9,5},{10,14},{11,7},{... | collective-permute-start | bytes 221192 | tf_op jit(solution)/shard_map/ppermute | solution.py:727
  7.7 4.0 %collective-permute-start.1 = (f32[1,72,128]{2,1,0:T(8,128)S(1)}, f32[1,72,128]{2,1,0:T(8,128)S(1)}, u32[]{:S(2)}, u32[]{:S(2)}) collective-permute-start(f32[1,72,128]{2,1,0:T(8,128)S(1)} %get-tuple-element.31.refs_0_), channel_id=1, source_target_pairs={{0,8},{4,12},{8,0},{12,4},{16,24},{20,28},{24,16},{28,20},{1,9},{5... | collective-permute-start | bytes 110600 | tf_op jit(solution)/shard_map/ppermute | solution.py:41
  10.3 4.1 %copy-start.1 = (f32[256]{0:T(256)S(1)}, f32[256]{0:T(256)}, u32[]{:S(2)}) copy-start(f32[256]{0:T(256)} %param.10) | copy-start | bytes 3076
  11.7 6.8 %collective-permute-start.2 = (f32[2,72,128]{2,1,0:T(8,128)S(1)}, f32[2,72,128]{2,1,0:T(8,128)S(1)}, u32[]{:S(2)}, u32[]{:S(2)}) collective-permute-start(f32[2,72,128]{2,1,0:T(8,128)S(1)} %join.2.refs_0_), channel_id=1, source_target_pairs={{0,16},{4,20},{8,24},{12,28},{16,0},{20,4},{24,8},{28,12},{1,17},{... | collective-permute-start | bytes 221192 | tf_op jit(solution)/shard_map/ppermute | solution.py:41
  18.5 2.9 %copy-start = (s32[24,64]{1,0:T(8,128)S(1)}, s32[24,64]{1,0:T(8,128)}, u32[]{:S(2)}) copy-start(s32[24,64]{1,0:T(8,128)} %lab_ref.1) | copy-start | bytes 18436
  18.5 2.9 %copy-start.2 = (bf16[3,3,256,128]{3,2,1,0:T(8,128)(2,1)S(1)}, bf16[3,3,256,128]{3,2,1,0:T(8,128)(2,1)}, u32[]{:S(2)}) copy-start(bf16[3,3,256,128]{3,2,1,0:T(8,128)(2,1)} %param.11) | copy-start | bytes 1769476
  18.5 2.9 %copy-start.3 = (f32[128]{0:T(128)S(1)}, f32[128]{0:T(128)}, u32[]{:S(2)}) copy-start(f32[128]{0:T(128)} %param.12) | copy-start | bytes 1540
  18.5 2.9 %collective-permute-start.3 = (bf16[12,64,256]{2,1,0:T(8,128)(2,1)S(1)}, bf16[12,64,256]{2,1,0:T(8,128)(2,1)S(1)}, u32[]{:S(2)}, u32[]{:S(2)}) collective-permute-start(bf16[12,64,256]{2,1,0:T(8,128)(2,1)S(1)} %conv_pool.1.refs_2_.refs_0_.own_ref), channel_id=1, source_target_pairs={{0,1},{1,0},{2,3},{3,2},{4,5},{5,4},{6,7},{7,6},{8,9},{9,8},{10,11... | collective-permute-start | bytes 1179656 | tf_op jit(solution)/shard_map/ppermute | solution.py:41
  18.6 2.0 %collective-permute-start.4 = (bf16[48,768]{1,0:T(8,128)(2,1)S(1)}, bf16[48,768]{1,0:T(8,128)(2,1)S(1)}, u32[]{:S(2)}, u32[]{:S(2)}) collective-permute-start(bf16[48,768]{1,0:T(8,128)(2,1)S(1)} %collective-permute-done.refs_1_.got_ref), channel_id=1, source_target_pairs={{0,1},{1,0},{2,3},{3,2},{4,5},{5,4},{6,7},{7,6},{8,9},{9,8},{10,11... | collective-permute-start | bytes 221192 | tf_op jit(solution)/shard_map/ppermute | solution.py:41
  19.1 6.1 %collective-permute-start.5 = (f32[4,72,128]{2,1,0:T(8,128)S(1)}, f32[4,72,128]{2,1,0:T(8,128)S(1)}, u32[]{:S(2)}, u32[]{:S(2)}) collective-permute-start(f32[4,72,128]{2,1,0:T(8,128)S(1)} %join.3.refs_0_), channel_id=1, source_target_pairs={{0,4},{4,0},{8,12},{12,8},{16,20},{20,16},{24,28},{28,24},{1,5},{5... | collective-permute-start | bytes 442376 | tf_op jit(solution)/shard_map/ppermute | solution.py:41
  27.5 10.1 %collective-permute-start.6 = (f16[624,128]{1,0:T(8,128)(2,1)S(1)}, f16[624,128]{1,0:T(8,128)(2,1)S(1)}, u32[]{:S(2)}, u32[]{:S(2)}) collective-permute-start(f16[624,128]{1,0:T(8,128)(2,1)S(1)} %convert_element_type.65), channel_id=1, source_target_pairs={{0,24},{4,28},{8,16},{12,20},{16,8},{20,12},{24,0},{28,4},{1,25},{... | collective-permute-start | bytes 479240 | tf_op jit(solution)/shard_map/ppermute | solution.py:41
  30.2 4.6 %collective-permute-start.7 = (f16[336,128]{1,0:T(8,128)(2,1)S(1)}, f16[336,128]{1,0:T(8,128)(2,1)S(1)}, u32[]{:S(2)}, u32[]{:S(2)}) collective-permute-start(f16[336,128]{1,0:T(8,128)(2,1)S(1)} %convert_element_type.67), channel_id=1, source_target_pairs={{0,4},{4,0},{8,12},{12,8},{16,20},{20,16},{24,28},{28,24},{1,5},{5... | collective-permute-start | bytes 258056 | tf_op jit(solution)/shard_map/ppermute | solution.py:41
  34.8 8.3 %collective-permute-start.11 = (f16[368,128]{1,0:T(8,128)(2,1)S(1)}, f16[368,128]{1,0:T(8,128)(2,1)S(1)}, u32[]{:S(2)}, u32[]{:S(2)}) collective-permute-start(f16[368,128]{1,0:T(8,128)(2,1)S(1)} %convert_element_type.75), channel_id=1, source_target_pairs={{0,16},{4,20},{8,24},{12,28},{16,0},{20,4},{24,8},{28,12},{1,17},{... | collective-permute-start | bytes 282632 | tf_op jit(solution)/shard_map/ppermute | solution.py:41
  35.1 7.1 %collective-permute-start.9 = (f16[336,128]{1,0:T(8,128)(2,1)S(1)}, f16[336,128]{1,0:T(8,128)(2,1)S(1)}, u32[]{:S(2)}, u32[]{:S(2)}) collective-permute-start(f16[336,128]{1,0:T(8,128)(2,1)S(1)} %convert_element_type.71), channel_id=1, source_target_pairs={{0,8},{4,12},{8,0},{12,4},{16,24},{20,28},{24,16},{28,20},{1,9},{5... | collective-permute-start | bytes 258056 | tf_op jit(solution)/shard_map/ppermute | solution.py:41
  36.8 6.3 %collective-permute-start.10 = (f16[336,128]{1,0:T(8,128)(2,1)S(1)}, f16[336,128]{1,0:T(8,128)(2,1)S(1)}, u32[]{:S(2)}, u32[]{:S(2)}) collective-permute-start(f16[336,128]{1,0:T(8,128)(2,1)S(1)} %convert_element_type.73), channel_id=1, source_target_pairs={{0,12},{4,8},{8,4},{12,0},{16,28},{20,24},{24,20},{28,16},{1,13},{... | collective-permute-start | bytes 258056 | tf_op jit(solution)/shard_map/ppermute | solution.py:41
  37.7 5.5 %collective-permute-start.8 = (f16[336,128]{1,0:T(8,128)(2,1)S(1)}, f16[336,128]{1,0:T(8,128)(2,1)S(1)}, u32[]{:S(2)}, u32[]{:S(2)}) collective-permute-start(f16[336,128]{1,0:T(8,128)(2,1)S(1)} %convert_element_type.69), channel_id=1, source_target_pairs={{0,4},{4,0},{8,12},{12,8},{16,20},{20,16},{24,28},{28,24},{1,5},{5... | collective-permute-start | bytes 258056 | tf_op jit(solution)/shard_map/ppermute | solution.py:41
  43.5 8.7 %collective-permute-start.15 = (f16[1,304,128]{2,1,0:T(8,128)(2,1)S(1)}, f16[1,304,128]{2,1,0:T(8,128)(2,1)S(1)}, u32[]{:S(2)}, u32[]{:S(2)}) collective-permute-start(f16[1,304,128]{2,1,0:T(8,128)(2,1)S(1)} %get-tuple-element.54), channel_id=1, source_target_pairs={{0,16},{4,20},{8,24},{12,28},{16,0},{20,4},{24,8},{28,12},{1,17},{... | collective-permute-start | bytes 233480 | tf_op jit(solution)/shard_map/ppermute | solution.py:41
  45.4 7.4 %collective-permute-start.16 = (f16[1,304,128]{2,1,0:T(8,128)(2,1)S(1)}, f16[1,304,128]{2,1,0:T(8,128)(2,1)S(1)}, u32[]{:S(2)}, u32[]{:S(2)}) collective-permute-start(f16[1,304,128]{2,1,0:T(8,128)(2,1)S(1)} %get-tuple-element.54), channel_id=1, source_target_pairs={{0,24},{4,28},{8,16},{12,20},{16,8},{20,12},{24,0},{28,4},{1,25},{... | collective-permute-start | bytes 233480 | tf_op jit(solution)/shard_map/ppermute | solution.py:41
  48.6 6.5 %collective-permute-start.12 = (f16[1,304,128]{2,1,0:T(8,128)(2,1)S(1)}, f16[1,304,128]{2,1,0:T(8,128)(2,1)S(1)}, u32[]{:S(2)}, u32[]{:S(2)}) collective-permute-start(f16[1,304,128]{2,1,0:T(8,128)(2,1)S(1)} %get-tuple-element.54), channel_id=1, source_target_pairs={{0,4},{4,0},{8,12},{12,8},{16,20},{20,16},{24,28},{28,24},{1,5},{5... | collective-permute-start | bytes 233480 | tf_op jit(solution)/shard_map/ppermute | solution.py:41
  49.4 5.8 %collective-permute-start.13 = (f16[1,304,128]{2,1,0:T(8,128)(2,1)S(1)}, f16[1,304,128]{2,1,0:T(8,128)(2,1)S(1)}, u32[]{:S(2)}, u32[]{:S(2)}) collective-permute-start(f16[1,304,128]{2,1,0:T(8,128)(2,1)S(1)} %get-tuple-element.54), channel_id=1, source_target_pairs={{0,8},{4,12},{8,0},{12,4},{16,24},{20,28},{24,16},{28,20},{1,9},{5... | collective-permute-start | bytes 233480 | tf_op jit(solution)/shard_map/ppermute | solution.py:41
  49.4 6.0 %collective-permute-start.14 = (f16[1,304,128]{2,1,0:T(8,128)(2,1)S(1)}, f16[1,304,128]{2,1,0:T(8,128)(2,1)S(1)}, u32[]{:S(2)}, u32[]{:S(2)}) collective-permute-start(f16[1,304,128]{2,1,0:T(8,128)(2,1)S(1)} %get-tuple-element.54), channel_id=1, source_target_pairs={{0,12},{4,8},{8,4},{12,0},{16,28},{20,24},{24,20},{28,16},{1,13},{... | collective-permute-start | bytes 233480 | tf_op jit(solution)/shard_map/ppermute | solution.py:41
  52.1 4.4 %collective-permute-start.17 = (f16[1,304,128]{2,1,0:T(8,128)(2,1)S(1)}, f16[1,304,128]{2,1,0:T(8,128)(2,1)S(1)}, u32[]{:S(2)}, u32[]{:S(2)}) collective-permute-start(f16[1,304,128]{2,1,0:T(8,128)(2,1)S(1)} %collective-permute-done.15), channel_id=1, source_target_pairs={{0,4},{4,0},{8,12},{12,8},{16,20},{20,16},{24,28},{28,24},{1,5},{5... | collective-permute-start | bytes 233480 | tf_op jit(solution)/shard_map/ppermute | solution.py:41
  52.9 4.5 %collective-permute-start.18 = (f16[1,304,128]{2,1,0:T(8,128)(2,1)S(1)}, f16[1,304,128]{2,1,0:T(8,128)(2,1)S(1)}, u32[]{:S(2)}, u32[]{:S(2)}) collective-permute-start(f16[1,304,128]{2,1,0:T(8,128)(2,1)S(1)} %collective-permute-done.16), channel_id=1, source_target_pairs={{0,4},{4,0},{8,12},{12,8},{16,20},{20,16},{24,28},{28,24},{1,5},{5... | collective-permute-start | bytes 233480 | tf_op jit(solution)/shard_map/ppermute | solution.py:41

commit v12 on v11

--- a/solution.py
+++ b/solution.py
@@ -18,7 +18,7 @@
 PIECE = 4
 STEP = 6
 PAYLOADS = (((0,), 0), ((1,), 0), ((2,), 1), ((3,), 1), ((4,), 0), ((5,), 1), ((6, 7), 1))
-NOTE = 16
+NOTE = 8
 
 
 def params(mib=8):
@@ -75,7 +75,8 @@
     return most, pick(half, (0, rows - most)), pick(half, (-1, 2 * first - 1 - (rows - most)))
 
 
-def window_kernel(rows_ref, taps, wide, *, rows):
+def window_kernel(rows_ref, *refs, rows):
+    taps, wide = refs[-2:]
     most, cols, chans = rows_ref.shape
     half_cols = cols // 2
     half = position()[0]
@@ -106,18 +107,18 @@
     taps[outside] = jnp.zeros(taps.shape[1:], BF16)
 
 
-def windows(near_rows, rows):
+def windows(near_rows, rows, after):
     most, cols, chans = near_rows.shape
     return pl.pallas_call(
         functools.partial(window_kernel, rows=rows),
         out_shape=jax.ShapeDtypeStruct((most + 2 * PIECE, cols // 2, 4 * chans), BF16),
-        in_specs=[VMEM],
+        in_specs=[VMEM] + [ANY] * len(after),
         out_specs=VMEM,
         scratch_shapes=[pltpu.VMEM((PIECE * (chans // 128), cols + 16, 128), F32)],
         compiler_params=params(16),
         cost_estimate=pl.CostEstimate(flops=0, bytes_accessed=12 << 20, transcendentals=0),
         name="windows",
-    )(near_rows)
+    )(near_rows, *after)
 
 
 def edge_part(pairs, w_ref, bias, edge_ref, acc):
@@ -235,51 +236,76 @@
     )(w, b, got, traded, head, tail, *after)
 
 
-def start_kernel(
-    x_hbm, w_hbm, grad_hbm, labels_hbm, slots_hbm,
-    side_ref, head_ref, tail_ref, send_ref, near_ref, w_ref,
-    labels_ref, slots_ref, left, right, wide, sems,
-):
+def side_kernel(grad_hbm, labels_hbm, slots_hbm, side_ref, labels_ref, slots_ref, sems):
     owned, width = grad_hbm.shape
-    rows, cols, chans = x_hbm.shape
     entries = slots_ref.shape[1]
-    reach = left.shape[1]
-    half = position()[0]
     copies = [
         pltpu.make_async_copy(labels_hbm, labels_ref, sems.at[0]),
-        pltpu.make_async_copy(grad_hbm, side_ref.at[0, pl.ds(0, owned)], sems.at[1]),
-        pltpu.make_async_copy(x_hbm.at[:, pl.ds(0, reach)], left, sems.at[2]),
-        pltpu.make_async_copy(x_hbm.at[:, pl.ds(cols - reach, reach)], right, sems.at[3]),
-        pltpu.make_async_copy(slots_hbm, slots_ref, sems.at[4]),
+        pltpu.make_async_copy(slots_hbm, slots_ref, sems.at[1]),
+        pltpu.make_async_copy(grad_hbm, side_ref.at[0, pl.ds(0, owned)], sems.at[2]),
     ]
-    most, first, _ = share_rows(half, rows)
-    size = most // 4
-    for k in range(4):
-        source = x_hbm.at[pl.ds(first + k * size, size)]
-        copies.append(
-            pltpu.make_async_copy(source, near_ref.at[pl.ds(k * size, size)], sems.at[5 + k])
-        )
-    copies.append(pltpu.make_async_copy(w_hbm, w_ref, sems.at[9]))
     for copy in copies:
         copy.start()
     lane = lax.broadcasted_iota(jnp.int32, (1, width), 1)
     copies[0].wait()
-    copies[4].wait()
-    ids = jnp.concatenate(
-        [slots_ref[...].astype(F32), jnp.zeros((1, width - entries), F32)], axis=1
-    )
     labels = labels_ref[...]
     counts = jnp.zeros((1, width), F32)
     for e in range(entries):
         hit = jnp.where(labels == e, 1.0, 0.0)
         hit = jnp.sum(jnp.sum(hit, axis=0, keepdims=True), axis=1, keepdims=True)
         counts = jnp.where(lane == e, hit, counts)
+    copies[1].wait()
+    ids = jnp.concatenate(
+        [slots_ref[...].astype(F32), jnp.zeros((1, width - entries), F32)], axis=1
+    )
     row = lax.broadcasted_iota(jnp.int32, (SIDE, width), 0)
     side_ref[0, owned:] = jnp.where(row == 0, ids, jnp.where(row == 1, counts, 0.0))
+    copies[2].wait()
+
+
+def pack_side(grad, slots, labels):
+    owned, width = grad.shape
+    fixed = [
+        pltpu.with_memory_space_constraint(a, pltpu.HBM)
+        for a in (grad, labels, slots.reshape(1, -1))
+    ]
+    return pl.pallas_call(
+        side_kernel,
+        out_shape=jax.ShapeDtypeStruct((1, owned + SIDE, width), F32),
+        in_specs=[HBM] * 3,
+        out_specs=VMEM,
+        scratch_shapes=[
+            pltpu.VMEM(labels.shape, jnp.int32),
+            pltpu.VMEM((1, slots.shape[0]), jnp.int32),
+            pltpu.SemaphoreType.DMA((3,)),
+        ],
+        compiler_params=params(),
+        name="pack_side",
+    )(*fixed)
+
+
+def columns_kernel(x_hbm, w_hbm, head_ref, tail_ref, send_ref, near_ref, w_ref, left, right, wide, sems):
+    rows, cols, chans = x_hbm.shape
+    reach = left.shape[1]
+    half = position()[0]
+    most, first, _ = share_rows(half, rows)
+    size = most // 4
+    copies = [
+        pltpu.make_async_copy(x_hbm.at[:, pl.ds(0, reach)], left, sems.at[0]),
+        pltpu.make_async_copy(x_hbm.at[:, pl.ds(cols - reach, reach)], right, sems.at[1]),
+    ]
+    for k in range(4):
+        source = x_hbm.at[pl.ds(first + k * size, size)]
+        copies.append(
+            pltpu.make_async_copy(source, near_ref.at[pl.ds(k * size, size)], sems.at[2 + k])
+        )
+    copies.append(pltpu.make_async_copy(w_hbm, w_ref, sems.at[6]))
+    for copy in copies:
+        copy.start()
     lanes = chans // 128
-    copies[2].wait()
-    copies[3].wait()
-    for ref, out_ref, at, sent in ((left, head_ref, 0, 1), (right, tail_ref, reach - WIDTH, 0)):
+    sides = ((left, head_ref, 0), (right, tail_ref, reach - WIDTH))
+    for copy, (ref, out_ref, at) in zip(copies, sides):
+        copy.wait()
         x = ref[...].astype(F32).reshape(rows * reach, chans)
         for t in range(lanes):
             wide[t] = x[:, t * 128 : (t + 1) * 128]
@@ -289,39 +315,30 @@
                 place = (c * lanes + t) * 128
                 out_ref[:, place : place + 128] = part
     send_ref[...] = jnp.where(half == 0, tail_ref[...], head_ref[...])
-    copies[1].wait()
-    for copy in copies[5:]:
+    for copy in copies[2:]:
         copy.wait()
 
 
-def start(x, w, grad, slots, labels):
-    owned, width = grad.shape
+def columns(x, w):
     rows, cols, chans = x.shape
     reach = 16
     most = share_rows(0, rows)[0]
-    columns = jax.ShapeDtypeStruct((rows, WIDTH * chans), BF16)
-    fixed = [
-        pltpu.with_memory_space_constraint(a, pltpu.HBM)
-        for a in (x, w, grad, labels, slots.reshape(1, -1))
-    ]
-    return pl.pallas_call(
-        start_kernel,
-        out_shape=(jax.ShapeDtypeStruct((1, owned + SIDE, width), F32),)
-        + (columns,) * 3
+    border = jax.ShapeDtypeStruct((rows, WIDTH * chans), BF16)
+    return pl.pallas_call(
+        columns_kernel,
+        out_shape=(border,) * 3
         + (jax.ShapeDtypeStruct((most, cols, chans), BF16), jax.ShapeDtypeStruct(w.shape, BF16)),
-        in_specs=[HBM] * 5,
-        out_specs=(VMEM,) * 6,
+        in_specs=[HBM] * 2,
+        out_specs=(VMEM,) * 5,
         scratch_shapes=[
-            pltpu.VMEM(labels.shape, jnp.int32),
-            pltpu.VMEM((1, slots.shape[0]), jnp.int32),
             pltpu.VMEM((rows, reach, chans), BF16),
             pltpu.VMEM((rows, reach, chans), BF16),
             pltpu.VMEM((chans // 128, rows * reach, 128), F32),
-            pltpu.SemaphoreType.DMA((10,)),
+            pltpu.SemaphoreType.DMA((7,)),
         ],
         compiler_params=params(16),
-        name="start",
-    )(*fixed)
+        name="columns",
+    )(*(pltpu.with_memory_space_constraint(a, pltpu.HBM) for a in (x, w)))
 
 
 def join_kernel(*refs, count):
@@ -715,28 +732,26 @@
     conv_w = conv_weight.reshape(9 * channels, -1)
     conv_b = conv_bias.reshape(1, -1)
 
-    side, head, tail, sent, near_rows, near_w = start(
-        section_input, conv_w, embed_grad, slot_ids, labels
-    )
+    side = pack_side(embed_grad, slot_ids, labels)
+    head, tail, border, near_rows, near_w = columns(section_input, conv_w)
     pairs = []
     for s in range(strip_count):
         for c in range(chan_count):
             to = s + 1 - 2 * (c & 1)
             if 0 <= to < strip_count:
                 pairs.append((s * chan_count + c, to * chan_count + c))
-    got = lax.ppermute(sent, ("strip", "chan"), pairs)
+    got = lax.ppermute(border, ("strip", "chan"), pairs)
 
     steps = [(at + 1, 1) for at in range(min(2, strip_count.bit_length() - 2))]
     steps += [(at, min(3, strip_count.bit_length() - 1 - at)) for at in range(3, strip_count.bit_length() - 1, 3)]
     ahead = gather_step(side, "strip", steps[0])
-    taps = windows(near_rows, section_input.shape[0])
-    shared = join(ahead, [taps])
-    got, shared = lax.optimization_barrier((got, shared))
+    shared = join(ahead, [border])
+    taps = windows(near_rows, section_input.shape[0], [shared])
+    ahead = gather_step(shared, "strip", steps[1])
+    pooled = conv_pool(taps, near_w, conv_b, section_input.shape[0] // 4, [shared])
+    pooled, got, shared = lax.optimization_barrier((pooled, got, join(ahead, [pooled])))
+    other = swap(pooled, "chan", 1)
     traded = swap(got, "chan", 1)
-    ahead = gather_step(shared, "strip", steps[1])
-    pooled = conv_pool(taps, near_w, conv_b, section_input.shape[0] // 4, [shared, got])
-    pooled, shared = lax.optimization_barrier((pooled, join(ahead, [pooled])))
-    other = swap(pooled, "chan", 1)
     for step in steps[2:]:
         shared = join(gather_step(shared, "strip", step), [])
     shared = [shared, swap(shared, "strip", 1)]

time: 58.8 us -> 57 us (0.969)
  starting transfers between devices: 29.4 us -> 26.7 us
  Pallas kernels: 16.4 us -> 17.2 us
    ppermute x1, starting transfers between devices: 4.85 us -> 3.4 us  [body(): got = lax.ppermute(border, ('strip', 'chan'), pairs)]
    ppermute x18, starting transfers between devices: 24.5 us -> 23.3 us  [swap(): return lax.ppermute(value, axis, [(i, i ^ mask) for i in range(count)])]
    pallas_call x1 -> x2, Pallas kernels: 2.21 us -> 3.04 us  [the longest x1 2.14 us: columns(): pl.pallas_call(columns_kernel, out_shape=(border,) * 3 + (jax.ShapeDtypeS...]
  transfers between devices with their start and end apart: 19 -> 19, of which waited for: 7 -> 9; matrix products, arithmetic and copies ran while one was open for 0% -> 0% of each run, Pallas kernels for 18% -> 22%
where the time goes in v12:
time: 57 us; the launch traced here: 56.7 us
  starting transfers between devices  26.7 us (47%)
  Pallas kernels  17.2 us (30%)
  waiting for transfers between devices  11.6 us (20%)
  between operations  0.97 us (2%)
    ppermute x18, starting transfers between devices, swap(): return lax.ppermute(value, axis, [(i, i ^ mask) for i in range(count)])  23.3 us
    ppermute x18, waiting for transfers between devices, swap(): return lax.ppermute(value, axis, [(i, i ^ mask) for i in range(count)])  11.6 us
    pallas_call x1, Pallas kernels, conv_pool(): pl.pallas_call(conv_kernel, out_shape=jax.ShapeDtypeStruct((pooled_rows,...  4.05 us
    pallas_call x1, Pallas kernels, deep_forward(): pl.pallas_call(functools.partial(deep_kernel, block=block, entries=entrie...  3.71 us
    ppermute x1, starting transfers between devices, body(): got = lax.ppermute(border, ('strip', 'chan'), pairs)  3.4 us
    pallas_call x1, Pallas kernels, deep_backward(): pl.pallas_call(functools.partial(grad_kernel, n_parts=len(parts), chunk=c...  2.27 us
    pallas_call x1, Pallas kernels, columns(): pl.pallas_call(columns_kernel, out_shape=(border,) * 3 + (jax.ShapeDtypeS...  2.14 us
    pallas_call x1, Pallas kernels, spread(): pl.pallas_call(functools.partial(spread_kernel, chunk=chunk, rows=rows, m...  1.17 us
  transfers between devices with their start and end apart: 19, of which 9 were waited for; matrix products, arithmetic and copies ran while one was open for 0% of the time, Pallas kernels for 22%

profile of v12, /device:TPU:0, one launch (start us, length us, event | category | flops | bytes accessed | tf_op | source)
XLA Modules:
  0.0 56.7 jit_solution(11661609935152015296)
XLA Ops:
  0.6 0.9 %pack_side.1.refs_0_ = f32[1,72,128]{2,1,0:T(8,128)S(1)} custom-call(f32[64,128]{1,0:T(8,128)} %grad_hbm.1, s32[24,64]{1,0:T(8,128)} %lab_ref.1, s32[1,32]{1,0:T(1,128)} %bitcast.15), custom_call_target="tpu_custom_call" | custom-call | tf_op jit(solution)/shard_map/pack_side/pallas_call | solution.py:272
  1.5 3.1 %collective-permute-start = (f32[1,72,128]{2,1,0:T(8,128)S(1)}, f32[1,72,128]{2,1,0:T(8,128)S(1)}, u32[]{:S(2)}, u32[]{:S(2)}) collective-permute-start(f32[1,72,128]{2,1,0:T(8,128)S(1)} %pack_side.1.refs_0_), channel_id=1, source_target_pairs={{0,8},{4,12},{8,0},{12,4},{16,24},{20,28},{24,16},{28,20},{1,9},{5... | collective-permute-start | bytes 110600 | tf_op jit(solution)/shard_map/ppermute | solution.py:41
  4.6 2.1 %columns.1 = (bf16[48,768]{1,0:T(8,128)(2,1)S(1)}, bf16[48,768]{1,0:T(8,128)(2,1)S(1)}, bf16[48,768]{1,0:T(8,128)(2,1)S(1)}, bf16[28,128,256]{2,1,0:T(8,128)(2,1)S(1)}, bf16[2304,256]{1,0:T(8,128)(2,1)S(1)}) custom-call(bf16[48,128,256]{2,1,0:T(8,128)(2,1)} %x_hbm.1, bf16[2304,256]{1,0:T(8,128)(2,1)} %bitcast.14), custom_call_target="tpu_custom_call" | custom-call | tf_op jit(solution)/shard_map/columns/pallas_call | solution.py:327
  6.8 3.4 %collective-permute-start.1 = (bf16[48,768]{1,0:T(8,128)(2,1)S(1)}, bf16[48,768]{1,0:T(8,128)(2,1)S(1)}, u32[]{:S(2)}, u32[]{:S(2)}) collective-permute-start(bf16[48,768]{1,0:T(8,128)(2,1)S(1)} %get-tuple-element.27.refs_2_), channel_id=1, source_target_pairs={{0,4},{2,6},{4,8},{5,1},{6,10},{7,3},{8,12},{9,5},{10,14},{11,7},{... | collective-permute-start | bytes 221192 | tf_op jit(solution)/shard_map/ppermute | solution.py:743
  10.2 2.7 %collective-permute-start.2 = (f32[2,72,128]{2,1,0:T(8,128)S(1)}, f32[2,72,128]{2,1,0:T(8,128)S(1)}, u32[]{:S(2)}, u32[]{:S(2)}) collective-permute-start(f32[2,72,128]{2,1,0:T(8,128)S(1)} %join.2.refs_0_), channel_id=1, source_target_pairs={{0,16},{4,20},{8,24},{12,28},{16,0},{20,4},{24,8},{28,12},{1,17},{... | collective-permute-start | bytes 221192 | tf_op jit(solution)/shard_map/ppermute | solution.py:41
  12.9 1.0 %windows.1.taps = bf16[36,64,1024]{2,1,0:T(8,128)(2,1)S(1)} custom-call(bf16[28,128,256]{2,1,0:T(8,128)(2,1)S(1)} %get-tuple-element.26.rows_ref, f32[2,72,128]{2,1,0:T(8,128)S(1)} %join.2.refs_0_), custom_call_target="tpu_custom_call" | custom-call | bytes 12582912 | tf_op jit(solution)/shard_map/windows/pallas_call | solution.py:112
  13.9 4.0 %conv_pool.1.refs_2_.refs_0_.own_ref = bf16[12,64,256]{2,1,0:T(8,128)(2,1)S(1)} custom-call(bf16[36,64,1024]{2,1,0:T(8,128)(2,1)S(1)} %windows.1.taps, bf16[2304,256]{1,0:T(8,128)(2,1)S(1)} %get-tuple-element.28.w_ref, f32[1,256]{1,0:T(1,128)S(1)} %bitcast.10, f32[2,72,128]{2,1,0:T(8,128)S(1)} %join.2.refs_0_), custom_call_target="tpu_custom_call" | custom-call | flops 3623878656 | bytes 8388608 | tf_op jit(solution)/shard_map/conv_pool/pallas_call | solution.py:201
  18.1 0.5 collective-permute-start.4
  18.6 0.4 collective-permute-start.5
  19.0 0.9 %collective-permute-done.4.traded_ref = bf16[48,768]{1,0:T(8,128)(2,1)S(1)} collective-permute-done((bf16[48,768]{1,0:T(8,128)(2,1)S(1)}, bf16[48,768]{1,0:T(8,128)(2,1)S(1)}, u32[]{:S(2)}, u32[]{:S(2)}) %collective-permute-start.4) | collective-permute-done | bytes 73760 | tf_op jit(solution)/shard_map/ppermute | solution.py:41
  19.9 0.7 %conv_edges.1.edge_ref = f32[4,2,24,128]{3,2,1,0:T(8,128)S(1)} custom-call(bf16[2304,256]{1,0:T(8,128)(2,1)S(1)} %get-tuple-element.28.w_ref, f32[1,256]{1,0:T(1,128)S(1)} %bitcast.11, bf16[48,768]{1,0:T(8,128)(2,1)S(1)} %collective-permute-done.1.got_ref, bf16[48,768]{1,0:T(8,128)(2,1)S(1)} %collective-permute-done.4.traded_ref, ...), custom_call_target="tpu_custom_call" | custom-call | bytes 4194304 | tf_op jit(solution)/shard_map/conv_edges/pallas_call | solution.py:227
  20.7 3.7 %deep_forward.1 = (bf16[26,64,768]{2,1,0:T(8,128)(2,1)S(1)}, bf16[24,64,128]{2,1,0:T(8,128)(2,1)S(1)}, f32[1536,128]{1,0:T(8,128)S(1)}, f32[32,128]{1,0:T(8,128)S(1)}) custom-call(bf16[12,64,256]{2,1,0:T(8,128)(2,1)S(1)} %conv_pool.1.refs_2_.refs_0_.own_ref, bf16[12,64,256]{2,1,0:T(8,128)(2,1)S(1)} %collective-permute-done.3.other_ref, ...), custom_call_target="tpu_custom_call" | custom-call | flops 1811939328 | bytes 8388608 | tf_op jit(solution)/shard_map/deep_forward/pallas_call | solution.py:468
  24.4 2.3 %deep_backward.1 = (f32[296,128]{1,0:T(8,128)S(1)}, f32[296,128]{1,0:T(8,128)S(1)}, f32[328,128]{1,0:T(8,128)S(1)}, f32[328,128]{1,0:T(8,128)S(1)}, f32[296,128]...) custom-call(bf16[26,64,768]{2,1,0:T(8,128)(2,1)S(1)} %get-tuple-element.33.taps, ...), custom_call_target="tpu_custom_call" | custom-call | flops 1811939328 | bytes 8388608 | tf_op jit(solution)/shard_map/deep_backward/pallas_call | solution.py:555
  26.7 1.6 %collective-permute-start.6 = (f16[616,128]{1,0:T(8,128)(2,1)S(1)}, f16[616,128]{1,0:T(8,128)(2,1)S(1)}, u32[]{:S(2)}, u32[]{:S(2)}) collective-permute-start(f16[616,128]{1,0:T(8,128)(2,1)S(1)} %convert_element_type.65), channel_id=1, source_target_pairs={{0,24},{4,28},{8,16},{12,20},{16,8},{20,12},{24,0},{28,4},{1,25},{... | collective-permute-start | bytes 473096 | tf_op jit(solution)/shard_map/ppermute | solution.py:41
  28.4 1.4 %collective-permute-start.7 = (f16[328,128]{1,0:T(8,128)(2,1)S(1)}, f16[328,128]{1,0:T(8,128)(2,1)S(1)}, u32[]{:S(2)}, u32[]{:S(2)}) collective-permute-start(f16[328,128]{1,0:T(8,128)(2,1)S(1)} %convert_element_type.67), channel_id=1, source_target_pairs={{0,4},{4,0},{8,12},{12,8},{16,20},{20,16},{24,28},{28,24},{1,5},{5... | collective-permute-start | bytes 251912 | tf_op jit(solution)/shard_map/ppermute | solution.py:41
  29.8 3.1 %collective-permute-done.7 = f16[328,128]{1,0:T(8,128)(2,1)S(1)} collective-permute-done((f16[328,128]{1,0:T(8,128)(2,1)S(1)}, f16[328,128]{1,0:T(8,128)(2,1)S(1)}, u32[]{:S(2)}, u32[]{:S(2)}) %collective-permute-start.7) | collective-permute-done | bytes 84000 | tf_op jit(solution)/shard_map/ppermute | solution.py:41
  33.0 0.4 collective-permute-start.11
  33.4 2.5 %collective-permute-start.9 = (f16[328,128]{1,0:T(8,128)(2,1)S(1)}, f16[328,128]{1,0:T(8,128)(2,1)S(1)}, u32[]{:S(2)}, u32[]{:S(2)}) collective-permute-start(f16[328,128]{1,0:T(8,128)(2,1)S(1)} %convert_element_type.71), channel_id=1, source_target_pairs={{0,8},{4,12},{8,0},{12,4},{16,24},{20,28},{24,16},{28,20},{1,9},{5... | collective-permute-start | bytes 251912 | tf_op jit(solution)/shard_map/ppermute | solution.py:41
  36.0 0.2 collective-permute-start.10
  36.3 1.4 %collective-permute-start.8 = (f16[328,128]{1,0:T(8,128)(2,1)S(1)}, f16[328,128]{1,0:T(8,128)(2,1)S(1)}, u32[]{:S(2)}, u32[]{:S(2)}) collective-permute-start(f16[328,128]{1,0:T(8,128)(2,1)S(1)} %convert_element_type.69), channel_id=1, source_target_pairs={{0,4},{4,0},{8,12},{12,8},{16,20},{20,16},{24,28},{28,24},{1,5},{5... | collective-permute-start | bytes 251912 | tf_op jit(solution)/shard_map/ppermute | solution.py:41
  37.7 2.6 %collective-permute-done.9 = f16[328,128]{1,0:T(8,128)(2,1)S(1)} collective-permute-done((f16[328,128]{1,0:T(8,128)(2,1)S(1)}, f16[328,128]{1,0:T(8,128)(2,1)S(1)}, u32[]{:S(2)}, u32[]{:S(2)}) %collective-permute-start.9) | collective-permute-done | bytes 84000 | tf_op jit(solution)/shard_map/ppermute | solution.py:41
  40.2 1.8 %collective-permute-done.10 = f16[328,128]{1,0:T(8,128)(2,1)S(1)} collective-permute-done((f16[328,128]{1,0:T(8,128)(2,1)S(1)}, f16[328,128]{1,0:T(8,128)(2,1)S(1)}, u32[]{:S(2)}, u32[]{:S(2)}) %collective-permute-start.10) | collective-permute-done | bytes 84000 | tf_op jit(solution)/shard_map/ppermute | solution.py:41
  42.1 0.3 collective-permute-done.8
  42.6 1.3 %collective-permute-start.15 = (f16[1,296,128]{2,1,0:T(8,128)(2,1)S(1)}, f16[1,296,128]{2,1,0:T(8,128)(2,1)S(1)}, u32[]{:S(2)}, u32[]{:S(2)}) collective-permute-start(f16[1,296,128]{2,1,0:T(8,128)(2,1)S(1)} %get-tuple-element.50), channel_id=1, source_target_pairs={{0,16},{4,20},{8,24},{12,28},{16,0},{20,4},{24,8},{28,12},{1,17},{... | collective-permute-start | bytes 227336 | tf_op jit(solution)/shard_map/ppermute | solution.py:41
  43.9 2.9 %collective-permute-start.16 = (f16[1,296,128]{2,1,0:T(8,128)(2,1)S(1)}, f16[1,296,128]{2,1,0:T(8,128)(2,1)S(1)}, u32[]{:S(2)}, u32[]{:S(2)}) collective-permute-start(f16[1,296,128]{2,1,0:T(8,128)(2,1)S(1)} %get-tuple-element.50), channel_id=1, source_target_pairs={{0,24},{4,28},{8,16},{12,20},{16,8},{20,12},{24,0},{28,4},{1,25},{... | collective-permute-start | bytes 227336 | tf_op jit(solution)/shard_map/ppermute | solution.py:41
  46.9 3.3 %collective-permute-start.14 = (f16[1,296,128]{2,1,0:T(8,128)(2,1)S(1)}, f16[1,296,128]{2,1,0:T(8,128)(2,1)S(1)}, u32[]{:S(2)}, u32[]{:S(2)}) collective-permute-start(f16[1,296,128]{2,1,0:T(8,128)(2,1)S(1)} %get-tuple-element.50), channel_id=1, source_target_pairs={{0,12},{4,8},{8,4},{12,0},{16,28},{20,24},{24,20},{28,16},{1,13},{... | collective-permute-start | bytes 227336 | tf_op jit(solution)/shard_map/ppermute | solution.py:41
  50.4 0.7 %collective-permute-done.16 = f16[1,296,128]{2,1,0:T(8,128)(2,1)S(1)} collective-permute-done((f16[1,296,128]{2,1,0:T(8,128)(2,1)S(1)}, f16[1,296,128]{2,1,0:T(8,128)(2,1)S(1)}, u32[]{:S(2)}, u32[]{:S(2)}) %collective-permute-start.16) | collective-permute-done | bytes 75808 | tf_op jit(solution)/shard_map/ppermute | solution.py:41
  51.2 1.1 %collective-permute-start.18 = (f16[1,296,128]{2,1,0:T(8,128)(2,1)S(1)}, f16[1,296,128]{2,1,0:T(8,128)(2,1)S(1)}, u32[]{:S(2)}, u32[]{:S(2)}) collective-permute-start(f16[1,296,128]{2,1,0:T(8,128)(2,1)S(1)} %collective-permute-done.16), channel_id=1, source_target_pairs={{0,4},{4,0},{8,12},{12,8},{16,20},{20,16},{24,28},{28,24},{1,5},{5... | collective-permute-start | bytes 227336 | tf_op jit(solution)/shard_map/ppermute | solution.py:41
  52.3 1.0 %embed.1 = f32[64,128]{1,0:T(8,128)} custom-call(f32[256,128]{1,0:T(8,128)S(1)} %get-tuple-element.45.sums_ref, f32[4,72,128]{2,1,0:T(8,128)S(1)} %join.3.refs_0_, f32[4,72,128]{2,1,0:T(8,128)S(1)} %collective-permute-done.5.refs_1_), custom_call_target="tpu_custom_call" | custom-call | tf_op jit(solution)/shard_map/embed/pallas_call | solution.py:809
  53.5 1.2 %collective-permute-done.17 = f16[1,296,128]{2,1,0:T(8,128)(2,1)S(1)} collective-permute-done((f16[1,296,128]{2,1,0:T(8,128)(2,1)S(1)}, f16[1,296,128]{2,1,0:T(8,128)(2,1)S(1)}, u32[]{:S(2)}, u32[]{:S(2)}) %collective-permute-start.17) | collective-permute-done | bytes 75808 | tf_op jit(solution)/shard_map/ppermute | solution.py:41
  54.7 0.9 %collective-permute-done.18 = f16[1,296,128]{2,1,0:T(8,128)(2,1)S(1)} collective-permute-done((f16[1,296,128]{2,1,0:T(8,128)(2,1)S(1)}, f16[1,296,128]{2,1,0:T(8,128)(2,1)S(1)}, u32[]{:S(2)}, u32[]{:S(2)}) %collective-permute-start.18) | collective-permute-done | bytes 75808 | tf_op jit(solution)/shard_map/ppermute | solution.py:41
  55.6 1.2 %spread.1 = (f32[2304,128]{1,0:T(8,128)}, f32[1,128]{1,0:T(1,128)}) custom-call(f32[1,296,128]{2,1,0:T(8,128)S(1)} %get-tuple-element.49.refs_0_, f32[1,296,128]{2,1,0:T(8,128)S(1)} %convert_element_type.80.refs_1_, f32[1,296,128]{2,1,0:T(8,128)S(1)} %convert_element_type.81.refs_2_, f32[1,296,128]{2,1,0:T(8,128)S(1)} %convert_element_type.82.refs_3_, ...), custom_call_target="tpu_custom_call" | custom-call | tf_op jit(solution)/shard_map/spread/pallas_call | solution.py:713
  (48 shorter events, 1.1 us)
Async XLA Ops:
  1.5 8.6 %collective-permute-start = (f32[1,72,128]{2,1,0:T(8,128)S(1)}, f32[1,72,128]{2,1,0:T(8,128)S(1)}, u32[]{:S(2)}, u32[]{:S(2)}) collective-permute-start(f32[1,72,128]{2,1,0:T(8,128)S(1)} %pack_side.1.refs_0_), channel_id=1, source_target_pairs={{0,8},{4,12},{8,0},{12,4},{16,24},{20,28},{24,16},{28,20},{1,9},{5... | collective-permute-start | bytes 110600 | tf_op jit(solution)/shard_map/ppermute | solution.py:41
  6.8 11.2 %collective-permute-start.1 = (bf16[48,768]{1,0:T(8,128)(2,1)S(1)}, bf16[48,768]{1,0:T(8,128)(2,1)S(1)}, u32[]{:S(2)}, u32[]{:S(2)}) collective-permute-start(bf16[48,768]{1,0:T(8,128)(2,1)S(1)} %get-tuple-element.27.refs_2_), channel_id=1, source_target_pairs={{0,4},{2,6},{4,8},{5,1},{6,10},{7,3},{8,12},{9,5},{10,14},{11,7},{... | collective-permute-start | bytes 221192 | tf_op jit(solution)/shard_map/ppermute | solution.py:743
  10.2 7.8 %collective-permute-start.2 = (f32[2,72,128]{2,1,0:T(8,128)S(1)}, f32[2,72,128]{2,1,0:T(8,128)S(1)}, u32[]{:S(2)}, u32[]{:S(2)}) collective-permute-start(f32[2,72,128]{2,1,0:T(8,128)S(1)} %join.2.refs_0_), channel_id=1, source_target_pairs={{0,16},{4,20},{8,24},{12,28},{16,0},{20,4},{24,8},{28,12},{1,17},{... | collective-permute-start | bytes 221192 | tf_op jit(solution)/shard_map/ppermute | solution.py:41
  12.9 1.0 %copy-start.1 = (f32[256]{0:T(256)S(1)}, f32[256]{0:T(256)}, u32[]{:S(2)}) copy-start(f32[256]{0:T(256)} %param.10) | copy-start | bytes 3076
  17.9 2.7 %copy-start = (s32[24,64]{1,0:T(8,128)S(1)}, s32[24,64]{1,0:T(8,128)}, u32[]{:S(2)}) copy-start(s32[24,64]{1,0:T(8,128)} %lab_ref.1) | copy-start | bytes 18436
  17.9 2.7 %copy-start.2 = (bf16[3,3,256,128]{3,2,1,0:T(8,128)(2,1)S(1)}, bf16[3,3,256,128]{3,2,1,0:T(8,128)(2,1)}, u32[]{:S(2)}) copy-start(bf16[3,3,256,128]{3,2,1,0:T(8,128)(2,1)} %param.11) | copy-start | bytes 1769476
  17.9 2.7 %copy-start.3 = (f32[128]{0:T(128)S(1)}, f32[128]{0:T(128)}, u32[]{:S(2)}) copy-start(f32[128]{0:T(128)} %param.12) | copy-start | bytes 1540
  18.0 2.6 %collective-permute-start.3 = (bf16[12,64,256]{2,1,0:T(8,128)(2,1)S(1)}, bf16[12,64,256]{2,1,0:T(8,128)(2,1)S(1)}, u32[]{:S(2)}, u32[]{:S(2)}) collective-permute-start(bf16[12,64,256]{2,1,0:T(8,128)(2,1)S(1)} %conv_pool.1.refs_2_.refs_0_.own_ref), channel_id=1, source_target_pairs={{0,1},{1,0},{2,3},{3,2},{4,5},{5,4},{6,7},{7,6},{8,9},{9,8},{10,11... | collective-permute-start | bytes 1179656 | tf_op jit(solution)/shard_map/ppermute | solution.py:41
  18.1 1.8 %collective-permute-start.4 = (bf16[48,768]{1,0:T(8,128)(2,1)S(1)}, bf16[48,768]{1,0:T(8,128)(2,1)S(1)}, u32[]{:S(2)}, u32[]{:S(2)}) collective-permute-start(bf16[48,768]{1,0:T(8,128)(2,1)S(1)} %collective-permute-done.1.got_ref), channel_id=1, source_target_pairs={{0,1},{1,0},{2,3},{3,2},{4,5},{5,4},{6,7},{7,6},{8,9},{9,8},{10,11... | collective-permute-start | bytes 221192 | tf_op jit(solution)/shard_map/ppermute | solution.py:41
  18.6 5.8 %collective-permute-start.5 = (f32[4,72,128]{2,1,0:T(8,128)S(1)}, f32[4,72,128]{2,1,0:T(8,128)S(1)}, u32[]{:S(2)}, u32[]{:S(2)}) collective-permute-start(f32[4,72,128]{2,1,0:T(8,128)S(1)} %join.3.refs_0_), channel_id=1, source_target_pairs={{0,4},{4,0},{8,12},{12,8},{16,20},{20,16},{24,28},{28,24},{1,5},{5... | collective-permute-start | bytes 442376 | tf_op jit(solution)/shard_map/ppermute | solution.py:41
  26.7 9.5 %collective-permute-start.6 = (f16[616,128]{1,0:T(8,128)(2,1)S(1)}, f16[616,128]{1,0:T(8,128)(2,1)S(1)}, u32[]{:S(2)}, u32[]{:S(2)}) collective-permute-start(f16[616,128]{1,0:T(8,128)(2,1)S(1)} %convert_element_type.65), channel_id=1, source_target_pairs={{0,24},{4,28},{8,16},{12,20},{16,8},{20,12},{24,0},{28,4},{1,25},{... | collective-permute-start | bytes 473096 | tf_op jit(solution)/shard_map/ppermute | solution.py:41
  28.4 4.5 %collective-permute-start.7 = (f16[328,128]{1,0:T(8,128)(2,1)S(1)}, f16[328,128]{1,0:T(8,128)(2,1)S(1)}, u32[]{:S(2)}, u32[]{:S(2)}) collective-permute-start(f16[328,128]{1,0:T(8,128)(2,1)S(1)} %convert_element_type.67), channel_id=1, source_target_pairs={{0,4},{4,0},{8,12},{12,8},{16,20},{20,16},{24,28},{28,24},{1,5},{5... | collective-permute-start | bytes 251912 | tf_op jit(solution)/shard_map/ppermute | solution.py:41
  33.0 9.1 %collective-permute-start.11 = (f16[360,128]{1,0:T(8,128)(2,1)S(1)}, f16[360,128]{1,0:T(8,128)(2,1)S(1)}, u32[]{:S(2)}, u32[]{:S(2)}) collective-permute-start(f16[360,128]{1,0:T(8,128)(2,1)S(1)} %convert_element_type.75), channel_id=1, source_target_pairs={{0,16},{4,20},{8,24},{12,28},{16,0},{20,4},{24,8},{28,12},{1,17},{... | collective-permute-start | bytes 276488 | tf_op jit(solution)/shard_map/ppermute | solution.py:41
  33.4 6.8 %collective-permute-start.9 = (f16[328,128]{1,0:T(8,128)(2,1)S(1)}, f16[328,128]{1,0:T(8,128)(2,1)S(1)}, u32[]{:S(2)}, u32[]{:S(2)}) collective-permute-start(f16[328,128]{1,0:T(8,128)(2,1)S(1)} %convert_element_type.71), channel_id=1, source_target_pairs={{0,8},{4,12},{8,0},{12,4},{16,24},{20,28},{24,16},{28,20},{1,9},{5... | collective-permute-start | bytes 251912 | tf_op jit(solution)/shard_map/ppermute | solution.py:41
  36.0 6.1 %collective-permute-start.10 = (f16[328,128]{1,0:T(8,128)(2,1)S(1)}, f16[328,128]{1,0:T(8,128)(2,1)S(1)}, u32[]{:S(2)}, u32[]{:S(2)}) collective-permute-start(f16[328,128]{1,0:T(8,128)(2,1)S(1)} %convert_element_type.73), channel_id=1, source_target_pairs={{0,12},{4,8},{8,4},{12,0},{16,28},{20,24},{24,20},{28,16},{1,13},{... | collective-permute-start | bytes 251912 | tf_op jit(solution)/shard_map/ppermute | solution.py:41
  36.3 6.1 %collective-permute-start.8 = (f16[328,128]{1,0:T(8,128)(2,1)S(1)}, f16[328,128]{1,0:T(8,128)(2,1)S(1)}, u32[]{:S(2)}, u32[]{:S(2)}) collective-permute-start(f16[328,128]{1,0:T(8,128)(2,1)S(1)} %convert_element_type.69), channel_id=1, source_target_pairs={{0,4},{4,0},{8,12},{12,8},{16,20},{20,16},{24,28},{28,24},{1,5},{5... | collective-permute-start | bytes 251912 | tf_op jit(solution)/shard_map/ppermute | solution.py:41
  42.6 7.7 %collective-permute-start.15 = (f16[1,296,128]{2,1,0:T(8,128)(2,1)S(1)}, f16[1,296,128]{2,1,0:T(8,128)(2,1)S(1)}, u32[]{:S(2)}, u32[]{:S(2)}) collective-permute-start(f16[1,296,128]{2,1,0:T(8,128)(2,1)S(1)} %get-tuple-element.50), channel_id=1, source_target_pairs={{0,16},{4,20},{8,24},{12,28},{16,0},{20,4},{24,8},{28,12},{1,17},{... | collective-permute-start | bytes 227336 | tf_op jit(solution)/shard_map/ppermute | solution.py:41
  43.9 7.3 %collective-permute-start.16 = (f16[1,296,128]{2,1,0:T(8,128)(2,1)S(1)}, f16[1,296,128]{2,1,0:T(8,128)(2,1)S(1)}, u32[]{:S(2)}, u32[]{:S(2)}) collective-permute-start(f16[1,296,128]{2,1,0:T(8,128)(2,1)S(1)} %get-tuple-element.50), channel_id=1, source_target_pairs={{0,24},{4,28},{8,16},{12,20},{16,8},{20,12},{24,0},{28,4},{1,25},{... | collective-permute-start | bytes 227336 | tf_op jit(solution)/shard_map/ppermute | solution.py:41
  46.8 6.5 %collective-permute-start.12 = (f16[1,296,128]{2,1,0:T(8,128)(2,1)S(1)}, f16[1,296,128]{2,1,0:T(8,128)(2,1)S(1)}, u32[]{:S(2)}, u32[]{:S(2)}) collective-permute-start(f16[1,296,128]{2,1,0:T(8,128)(2,1)S(1)} %get-tuple-element.50), channel_id=1, source_target_pairs={{0,4},{4,0},{8,12},{12,8},{16,20},{20,16},{24,28},{28,24},{1,5},{5... | collective-permute-start | bytes 227336 | tf_op jit(solution)/shard_map/ppermute | solution.py:41
  46.9 6.4 %collective-permute-start.13 = (f16[1,296,128]{2,1,0:T(8,128)(2,1)S(1)}, f16[1,296,128]{2,1,0:T(8,128)(2,1)S(1)}, u32[]{:S(2)}, u32[]{:S(2)}) collective-permute-start(f16[1,296,128]{2,1,0:T(8,128)(2,1)S(1)} %get-tuple-element.50), channel_id=1, source_target_pairs={{0,8},{4,12},{8,0},{12,4},{16,24},{20,28},{24,16},{28,20},{1,9},{5... | collective-permute-start | bytes 227336 | tf_op jit(solution)/shard_map/ppermute | solution.py:41
  46.9 6.5 %collective-permute-start.14 = (f16[1,296,128]{2,1,0:T(8,128)(2,1)S(1)}, f16[1,296,128]{2,1,0:T(8,128)(2,1)S(1)}, u32[]{:S(2)}, u32[]{:S(2)}) collective-permute-start(f16[1,296,128]{2,1,0:T(8,128)(2,1)S(1)} %get-tuple-element.50), channel_id=1, source_target_pairs={{0,12},{4,8},{8,4},{12,0},{16,28},{20,24},{24,20},{28,16},{1,13},{... | collective-permute-start | bytes 227336 | tf_op jit(solution)/shard_map/ppermute | solution.py:41
  50.3 4.4 %collective-permute-start.17 = (f16[1,296,128]{2,1,0:T(8,128)(2,1)S(1)}, f16[1,296,128]{2,1,0:T(8,128)(2,1)S(1)}, u32[]{:S(2)}, u32[]{:S(2)}) collective-permute-start(f16[1,296,128]{2,1,0:T(8,128)(2,1)S(1)} %collective-permute-done.15), channel_id=1, source_target_pairs={{0,4},{4,0},{8,12},{12,8},{16,20},{20,16},{24,28},{28,24},{1,5},{5... | collective-permute-start | bytes 227336 | tf_op jit(solution)/shard_map/ppermute | solution.py:41
  51.2 4.4 %collective-permute-start.18 = (f16[1,296,128]{2,1,0:T(8,128)(2,1)S(1)}, f16[1,296,128]{2,1,0:T(8,128)(2,1)S(1)}, u32[]{:S(2)}, u32[]{:S(2)}) collective-permute-start(f16[1,296,128]{2,1,0:T(8,128)(2,1)S(1)} %collective-permute-done.16), channel_id=1, source_target_pairs={{0,4},{4,0},{8,12},{12,8},{16,20},{20,16},{24,28},{28,24},{1,5},{5... | collective-permute-start | bytes 227336 | tf_op jit(solution)/shard_map/ppermute | solution.py:41

commit v13 on v12

--- a/solution.py
+++ b/solution.py
@@ -17,7 +17,15 @@
 WIDTH = 3
 PIECE = 4
 STEP = 6
-PAYLOADS = (((0,), 0), ((1,), 0), ((2,), 1), ((3,), 1), ((4,), 0), ((5,), 1), ((6, 7), 1))
+PAYLOADS = (
+    ((0,), 0, 0),
+    ((1,), 0, 0),
+    ((2,), 1, 40),
+    ((3,), 1, 40),
+    ((4,), 0, 0),
+    ((5,), 1, 48),
+    ((6, 7), 1, 0),
+)
 NOTE = 8
 
 
@@ -537,15 +545,18 @@
     digit = lax.rem(me, ways)
     heads = weight.shape[0] // chunk // ways
     sums = sums * jnp.exp2(12.0 - power_sums)
-    for out_ref, (members, with_sums) in zip(out_refs, PAYLOADS):
+    for out_ref, (members, with_sums, spare) in zip(out_refs, PAYLOADS):
         at = 0
         for m, hi in itertools.product(members, range(heads)):
             j = hi * ways + (digit ^ m)
             out_ref[at : at + chunk] = weight[pl.ds(pl.multiple_of(j * chunk, 8), chunk)] * up
             at += chunk
         out_ref[at : at + NOTE] = note
+        at += NOTE
         if with_sums:
-            out_ref[at + NOTE :] = sums
+            out_ref[at : at + entries] = sums
+        if spare:
+            out_ref[at + entries :] = jnp.zeros((spare, width), F32)
 
 
 def deep_backward(forward, parts, chunk, count):
@@ -555,8 +566,10 @@
     return pl.pallas_call(
         functools.partial(grad_kernel, n_parts=len(parts), chunk=chunk),
         out_shape=tuple(
-            jax.ShapeDtypeStruct((len(members) * size + NOTE + with_sums * entries, width), F32)
-            for members, with_sums in PAYLOADS
+            jax.ShapeDtypeStruct(
+                (len(members) * size + NOTE + with_sums * entries + spare, width), F32
+            )
+            for members, with_sums, spare in PAYLOADS
         ),
         in_specs=[VMEM] * (4 + len(parts)),
         out_specs=(VMEM,) * len(PAYLOADS),

time: 57 us -> 57.6 us (1.011)
  waiting for transfers between devices: 11.6 us -> 13.2 us
  starting transfers between devices: 26.7 us -> 25.7 us
    ppermute x18, waiting for transfers between devices: 11.6 us -> 13.2 us  [swap(): return lax.ppermute(value, axis, [(i, i ^ mask) for i in range(count)])]
    ppermute x18, starting transfers between devices: 23.3 us -> 22.3 us  [swap(): return lax.ppermute(value, axis, [(i, i ^ mask) for i in range(count)])]
  transfers between devices with their start and end apart: 19 -> 19, of which waited for: 9 -> 10; matrix products, arithmetic and copies ran while one was open for 0% -> 0% of each run, Pallas kernels for 22% -> 22%
where the time goes in v13:
time: 57.6 us; the launch traced here: 57.4 us
  starting transfers between devices  25.7 us (45%)
  Pallas kernels  17.2 us (30%)
  waiting for transfers between devices  13.2 us (23%)
  between operations  0.98 us (2%)
    ppermute x18, starting transfers between devices, swap(): return lax.ppermute(value, axis, [(i, i ^ mask) for i in range(count)])  22.3 us
    ppermute x18, waiting for transfers between devices, swap(): return lax.ppermute(value, axis, [(i, i ^ mask) for i in range(count)])  13.2 us
    pallas_call x1, Pallas kernels, conv_pool(): pl.pallas_call(conv_kernel, out_shape=jax.ShapeDtypeStruct((pooled_rows,...  4.05 us
    pallas_call x1, Pallas kernels, deep_forward(): pl.pallas_call(functools.partial(deep_kernel, block=block, entries=entrie...  3.72 us
    ppermute x1, starting transfers between devices, body(): got = lax.ppermute(border, ('strip', 'chan'), pairs)  3.4 us
    pallas_call x1, Pallas kernels, deep_backward(): pl.pallas_call(functools.partial(grad_kernel, n_parts=len(parts), chunk=c...  2.27 us
    pallas_call x1, Pallas kernels, columns(): pl.pallas_call(columns_kernel, out_shape=(border,) * 3 + (jax.ShapeDtypeS...  2.14 us
    pallas_call x1, Pallas kernels, spread(): pl.pallas_call(functools.partial(spread_kernel, chunk=chunk, rows=rows, m...  1.17 us
  transfers between devices with their start and end apart: 19, of which 10 were waited for; matrix products, arithmetic and copies ran while one was open for 0% of the time, Pallas kernels for 22%

profile of v13, /device:TPU:0, one launch (start us, length us, event | category | flops | bytes accessed | tf_op | source)
XLA Modules:
  0.0 57.4 jit_solution(13400946511099589033)
XLA Ops:
  0.6 0.9 %pack_side.1.refs_0_ = f32[1,72,128]{2,1,0:T(8,128)S(1)} custom-call(f32[64,128]{1,0:T(8,128)} %grad_hbm.1, s32[24,64]{1,0:T(8,128)} %lab_ref.1, s32[1,32]{1,0:T(1,128)} %bitcast.15), custom_call_target="tpu_custom_call" | custom-call | tf_op jit(solution)/shard_map/pack_side/pallas_call | solution.py:280
  1.5 3.1 %collective-permute-start = (f32[1,72,128]{2,1,0:T(8,128)S(1)}, f32[1,72,128]{2,1,0:T(8,128)S(1)}, u32[]{:S(2)}, u32[]{:S(2)}) collective-permute-start(f32[1,72,128]{2,1,0:T(8,128)S(1)} %pack_side.1.refs_0_), channel_id=1, source_target_pairs={{0,8},{4,12},{8,0},{12,4},{16,24},{20,28},{24,16},{28,20},{1,9},{5... | collective-permute-start | bytes 110600 | tf_op jit(solution)/shard_map/ppermute | solution.py:49
  4.6 2.1 %columns.1 = (bf16[48,768]{1,0:T(8,128)(2,1)S(1)}, bf16[48,768]{1,0:T(8,128)(2,1)S(1)}, bf16[48,768]{1,0:T(8,128)(2,1)S(1)}, bf16[28,128,256]{2,1,0:T(8,128)(2,1)S(1)}, bf16[2304,256]{1,0:T(8,128)(2,1)S(1)}) custom-call(bf16[48,128,256]{2,1,0:T(8,128)(2,1)} %x_hbm.1, bf16[2304,256]{1,0:T(8,128)(2,1)} %bitcast.14), custom_call_target="tpu_custom_call" | custom-call | tf_op jit(solution)/shard_map/columns/pallas_call | solution.py:335
  6.8 3.4 %collective-permute-start.1 = (bf16[48,768]{1,0:T(8,128)(2,1)S(1)}, bf16[48,768]{1,0:T(8,128)(2,1)S(1)}, u32[]{:S(2)}, u32[]{:S(2)}) collective-permute-start(bf16[48,768]{1,0:T(8,128)(2,1)S(1)} %get-tuple-element.27.refs_2_), channel_id=1, source_target_pairs={{0,4},{2,6},{4,8},{5,1},{6,10},{7,3},{8,12},{9,5},{10,14},{11,7},{... | collective-permute-start | bytes 221192 | tf_op jit(solution)/shard_map/ppermute | solution.py:756
  10.2 2.7 %collective-permute-start.2 = (f32[2,72,128]{2,1,0:T(8,128)S(1)}, f32[2,72,128]{2,1,0:T(8,128)S(1)}, u32[]{:S(2)}, u32[]{:S(2)}) collective-permute-start(f32[2,72,128]{2,1,0:T(8,128)S(1)} %join.2.refs_0_), channel_id=1, source_target_pairs={{0,16},{4,20},{8,24},{12,28},{16,0},{20,4},{24,8},{28,12},{1,17},{... | collective-permute-start | bytes 221192 | tf_op jit(solution)/shard_map/ppermute | solution.py:49
  12.9 1.0 %windows.1.taps = bf16[36,64,1024]{2,1,0:T(8,128)(2,1)S(1)} custom-call(bf16[28,128,256]{2,1,0:T(8,128)(2,1)S(1)} %get-tuple-element.26.rows_ref, f32[2,72,128]{2,1,0:T(8,128)S(1)} %join.2.refs_0_), custom_call_target="tpu_custom_call" | custom-call | bytes 12582912 | tf_op jit(solution)/shard_map/windows/pallas_call | solution.py:120
  13.9 4.0 %conv_pool.1.refs_2_.refs_0_.own_ref = bf16[12,64,256]{2,1,0:T(8,128)(2,1)S(1)} custom-call(bf16[36,64,1024]{2,1,0:T(8,128)(2,1)S(1)} %windows.1.taps, bf16[2304,256]{1,0:T(8,128)(2,1)S(1)} %get-tuple-element.28.w_ref, f32[1,256]{1,0:T(1,128)S(1)} %bitcast.10, f32[2,72,128]{2,1,0:T(8,128)S(1)} %join.2.refs_0_), custom_call_target="tpu_custom_call" | custom-call | flops 3623878656 | bytes 8388608 | tf_op jit(solution)/shard_map/conv_pool/pallas_call | solution.py:209
  18.1 0.5 collective-permute-start.4
  19.0 0.9 %collective-permute-done.4.traded_ref = bf16[48,768]{1,0:T(8,128)(2,1)S(1)} collective-permute-done((bf16[48,768]{1,0:T(8,128)(2,1)S(1)}, bf16[48,768]{1,0:T(8,128)(2,1)S(1)}, u32[]{:S(2)}, u32[]{:S(2)}) %collective-permute-start.4) | collective-permute-done | bytes 73760 | tf_op jit(solution)/shard_map/ppermute | solution.py:49
  19.9 0.7 %conv_edges.1.edge_ref = f32[4,2,24,128]{3,2,1,0:T(8,128)S(1)} custom-call(bf16[2304,256]{1,0:T(8,128)(2,1)S(1)} %get-tuple-element.28.w_ref, f32[1,256]{1,0:T(1,128)S(1)} %bitcast.11, bf16[48,768]{1,0:T(8,128)(2,1)S(1)} %collective-permute-done.1.got_ref, bf16[48,768]{1,0:T(8,128)(2,1)S(1)} %collective-permute-done.4.traded_ref, ...), custom_call_target="tpu_custom_call" | custom-call | bytes 4194304 | tf_op jit(solution)/shard_map/conv_edges/pallas_call | solution.py:235
  20.7 3.7 %deep_forward.1 = (bf16[26,64,768]{2,1,0:T(8,128)(2,1)S(1)}, bf16[24,64,128]{2,1,0:T(8,128)(2,1)S(1)}, f32[1536,128]{1,0:T(8,128)S(1)}, f32[32,128]{1,0:T(8,128)S(1)}) custom-call(bf16[12,64,256]{2,1,0:T(8,128)(2,1)S(1)} %conv_pool.1.refs_2_.refs_0_.own_ref, bf16[12,64,256]{2,1,0:T(8,128)(2,1)S(1)} %collective-permute-done.3.other_ref, ...), custom_call_target="tpu_custom_call" | custom-call | flops 1811939328 | bytes 8388608 | tf_op jit(solution)/shard_map/deep_forward/pallas_call | solution.py:476
  24.4 2.3 %deep_backward.1 = (f32[296,128]{1,0:T(8,128)S(1)}, f32[296,128]{1,0:T(8,128)S(1)}, f32[368,128]{1,0:T(8,128)S(1)}, f32[368,128]{1,0:T(8,128)S(1)}, f32[296,128]...) custom-call(bf16[26,64,768]{2,1,0:T(8,128)(2,1)S(1)} %get-tuple-element.33.taps, ...), custom_call_target="tpu_custom_call" | custom-call | flops 1811939328 | bytes 8388608 | tf_op jit(solution)/shard_map/deep_backward/pallas_call | solution.py:566
  26.7 1.6 %collective-permute-start.6 = (f16[616,128]{1,0:T(8,128)(2,1)S(1)}, f16[616,128]{1,0:T(8,128)(2,1)S(1)}, u32[]{:S(2)}, u32[]{:S(2)}) collective-permute-start(f16[616,128]{1,0:T(8,128)(2,1)S(1)} %convert_element_type.65), channel_id=1, source_target_pairs={{0,24},{4,28},{8,16},{12,20},{16,8},{20,12},{24,0},{28,4},{1,25},{... | collective-permute-start | bytes 473096 | tf_op jit(solution)/shard_map/ppermute | solution.py:49
  28.4 1.4 %collective-permute-start.7 = (f16[376,128]{1,0:T(8,128)(2,1)S(1)}, f16[376,128]{1,0:T(8,128)(2,1)S(1)}, u32[]{:S(2)}, u32[]{:S(2)}) collective-permute-start(f16[376,128]{1,0:T(8,128)(2,1)S(1)} %convert_element_type.67), channel_id=1, source_target_pairs={{0,4},{4,0},{8,12},{12,8},{16,20},{20,16},{24,28},{28,24},{1,5},{5... | collective-permute-start | bytes 288776 | tf_op jit(solution)/shard_map/ppermute | solution.py:49
  29.9 2.2 %collective-permute-start.10 = (f16[368,128]{1,0:T(8,128)(2,1)S(1)}, f16[368,128]{1,0:T(8,128)(2,1)S(1)}, u32[]{:S(2)}, u32[]{:S(2)}) collective-permute-start(f16[368,128]{1,0:T(8,128)(2,1)S(1)} %convert_element_type.73), channel_id=1, source_target_pairs={{0,12},{4,8},{8,4},{12,0},{16,28},{20,24},{24,20},{28,16},{1,13},{... | collective-permute-start | bytes 282632 | tf_op jit(solution)/shard_map/ppermute | solution.py:49
  32.1 0.9 %collective-permute-done.7 = f16[376,128]{1,0:T(8,128)(2,1)S(1)} collective-permute-done((f16[376,128]{1,0:T(8,128)(2,1)S(1)}, f16[376,128]{1,0:T(8,128)(2,1)S(1)}, u32[]{:S(2)}, u32[]{:S(2)}) %collective-permute-start.7) | collective-permute-done | bytes 96288 | tf_op jit(solution)/shard_map/ppermute | solution.py:49
  33.5 2.0 %collective-permute-done.6 = f16[616,128]{1,0:T(8,128)(2,1)S(1)} collective-permute-done((f16[616,128]{1,0:T(8,128)(2,1)S(1)}, f16[616,128]{1,0:T(8,128)(2,1)S(1)}, u32[]{:S(2)}, u32[]{:S(2)}) %collective-permute-start.6) | collective-permute-done | bytes 157728 | tf_op jit(solution)/shard_map/ppermute | solution.py:49
  35.6 0.7 %collective-permute-start.8 = (f16[328,128]{1,0:T(8,128)(2,1)S(1)}, f16[328,128]{1,0:T(8,128)(2,1)S(1)}, u32[]{:S(2)}, u32[]{:S(2)}) collective-permute-start(f16[328,128]{1,0:T(8,128)(2,1)S(1)} %convert_element_type.69), channel_id=1, source_target_pairs={{0,4},{4,0},{8,12},{12,8},{16,20},{20,16},{24,28},{28,24},{1,5},{5... | collective-permute-start | bytes 251912 | tf_op jit(solution)/shard_map/ppermute | solution.py:49
  36.4 2.0 %collective-permute-done.9 = f16[368,128]{1,0:T(8,128)(2,1)S(1)} collective-permute-done((f16[368,128]{1,0:T(8,128)(2,1)S(1)}, f16[368,128]{1,0:T(8,128)(2,1)S(1)}, u32[]{:S(2)}, u32[]{:S(2)}) %collective-permute-start.9) | collective-permute-done | bytes 94240 | tf_op jit(solution)/shard_map/ppermute | solution.py:49
  38.4 2.1 %collective-permute-done.10 = f16[368,128]{1,0:T(8,128)(2,1)S(1)} collective-permute-done((f16[368,128]{1,0:T(8,128)(2,1)S(1)}, f16[368,128]{1,0:T(8,128)(2,1)S(1)}, u32[]{:S(2)}, u32[]{:S(2)}) %collective-permute-start.10) | collective-permute-done | bytes 94240 | tf_op jit(solution)/shard_map/ppermute | solution.py:49
  40.5 0.5 collective-permute-done.8
  41.5 3.3 %collective-permute-start.16 = (f16[1,296,128]{2,1,0:T(8,128)(2,1)S(1)}, f16[1,296,128]{2,1,0:T(8,128)(2,1)S(1)}, u32[]{:S(2)}, u32[]{:S(2)}) collective-permute-start(f16[1,296,128]{2,1,0:T(8,128)(2,1)S(1)} %get-tuple-element.50), channel_id=1, source_target_pairs={{0,24},{4,28},{8,16},{12,20},{16,8},{20,12},{24,0},{28,4},{1,25},{... | collective-permute-start | bytes 227336 | tf_op jit(solution)/shard_map/ppermute | solution.py:49
  44.8 1.7 %collective-permute-start.13 = (f16[1,296,128]{2,1,0:T(8,128)(2,1)S(1)}, f16[1,296,128]{2,1,0:T(8,128)(2,1)S(1)}, u32[]{:S(2)}, u32[]{:S(2)}) collective-permute-start(f16[1,296,128]{2,1,0:T(8,128)(2,1)S(1)} %get-tuple-element.50), channel_id=1, source_target_pairs={{0,8},{4,12},{8,0},{12,4},{16,24},{20,28},{24,16},{28,20},{1,9},{5... | collective-permute-start | bytes 227336 | tf_op jit(solution)/shard_map/ppermute | solution.py:49
  46.5 1.8 %collective-permute-start.14 = (f16[1,296,128]{2,1,0:T(8,128)(2,1)S(1)}, f16[1,296,128]{2,1,0:T(8,128)(2,1)S(1)}, u32[]{:S(2)}, u32[]{:S(2)}) collective-permute-start(f16[1,296,128]{2,1,0:T(8,128)(2,1)S(1)} %get-tuple-element.50), channel_id=1, source_target_pairs={{0,12},{4,8},{8,4},{12,0},{16,28},{20,24},{24,20},{28,16},{1,13},{... | collective-permute-start | bytes 227336 | tf_op jit(solution)/shard_map/ppermute | solution.py:49
  48.3 1.1 %collective-permute-done.15 = f16[1,296,128]{2,1,0:T(8,128)(2,1)S(1)} collective-permute-done((f16[1,296,128]{2,1,0:T(8,128)(2,1)S(1)}, f16[1,296,128]{2,1,0:T(8,128)(2,1)S(1)}, u32[]{:S(2)}, u32[]{:S(2)}) %collective-permute-start.15) | collective-permute-done | bytes 75808 | tf_op jit(solution)/shard_map/ppermute | solution.py:49
  49.4 1.2 %collective-permute-start.17 = (f16[1,296,128]{2,1,0:T(8,128)(2,1)S(1)}, f16[1,296,128]{2,1,0:T(8,128)(2,1)S(1)}, u32[]{:S(2)}, u32[]{:S(2)}) collective-permute-start(f16[1,296,128]{2,1,0:T(8,128)(2,1)S(1)} %collective-permute-done.15), channel_id=1, source_target_pairs={{0,4},{4,0},{8,12},{12,8},{16,20},{20,16},{24,28},{28,24},{1,5},{5... | collective-permute-start | bytes 227336 | tf_op jit(solution)/shard_map/ppermute | solution.py:49
  50.6 0.9 %collective-permute-start.18 = (f16[1,296,128]{2,1,0:T(8,128)(2,1)S(1)}, f16[1,296,128]{2,1,0:T(8,128)(2,1)S(1)}, u32[]{:S(2)}, u32[]{:S(2)}) collective-permute-start(f16[1,296,128]{2,1,0:T(8,128)(2,1)S(1)} %collective-permute-done.16), channel_id=1, source_target_pairs={{0,4},{4,0},{8,12},{12,8},{16,20},{20,16},{24,28},{28,24},{1,5},{5... | collective-permute-start | bytes 227336 | tf_op jit(solution)/shard_map/ppermute | solution.py:49
  51.4 1.0 %embed.1 = f32[64,128]{1,0:T(8,128)} custom-call(f32[256,128]{1,0:T(8,128)S(1)} %get-tuple-element.45.sums_ref, f32[4,72,128]{2,1,0:T(8,128)S(1)} %join.3.refs_0_, f32[4,72,128]{2,1,0:T(8,128)S(1)} %collective-permute-done.5.refs_1_), custom_call_target="tpu_custom_call" | custom-call | tf_op jit(solution)/shard_map/embed/pallas_call | solution.py:822
  52.5 0.5 collective-permute-done.14
  53.0 1.6 %collective-permute-done.17 = f16[1,296,128]{2,1,0:T(8,128)(2,1)S(1)} collective-permute-done((f16[1,296,128]{2,1,0:T(8,128)(2,1)S(1)}, f16[1,296,128]{2,1,0:T(8,128)(2,1)S(1)}, u32[]{:S(2)}, u32[]{:S(2)}) %collective-permute-start.17) | collective-permute-done | bytes 75808 | tf_op jit(solution)/shard_map/ppermute | solution.py:49
  54.7 1.5 %collective-permute-done.18 = f16[1,296,128]{2,1,0:T(8,128)(2,1)S(1)} collective-permute-done((f16[1,296,128]{2,1,0:T(8,128)(2,1)S(1)}, f16[1,296,128]{2,1,0:T(8,128)(2,1)S(1)}, u32[]{:S(2)}, u32[]{:S(2)}) %collective-permute-start.18) | collective-permute-done | bytes 75808 | tf_op jit(solution)/shard_map/ppermute | solution.py:49
  56.2 1.2 %spread.1 = (f32[2304,128]{1,0:T(8,128)}, f32[1,128]{1,0:T(1,128)}) custom-call(f32[1,296,128]{2,1,0:T(8,128)S(1)} %get-tuple-element.49.refs_0_, f32[1,296,128]{2,1,0:T(8,128)S(1)} %convert_element_type.80.refs_1_, f32[1,296,128]{2,1,0:T(8,128)S(1)} %convert_element_type.81.refs_2_, f32[1,296,128]{2,1,0:T(8,128)S(1)} %convert_element_type.82.refs_3_, ...), custom_call_target="tpu_custom_call" | custom-call | tf_op jit(solution)/shard_map/spread/pallas_call | solution.py:726
  (48 shorter events, 1.9 us)
Async XLA Ops:
  1.5 8.6 %collective-permute-start = (f32[1,72,128]{2,1,0:T(8,128)S(1)}, f32[1,72,128]{2,1,0:T(8,128)S(1)}, u32[]{:S(2)}, u32[]{:S(2)}) collective-permute-start(f32[1,72,128]{2,1,0:T(8,128)S(1)} %pack_side.1.refs_0_), channel_id=1, source_target_pairs={{0,8},{4,12},{8,0},{12,4},{16,24},{20,28},{24,16},{28,20},{1,9},{5... | collective-permute-start | bytes 110600 | tf_op jit(solution)/shard_map/ppermute | solution.py:49
  6.8 11.2 %collective-permute-start.1 = (bf16[48,768]{1,0:T(8,128)(2,1)S(1)}, bf16[48,768]{1,0:T(8,128)(2,1)S(1)}, u32[]{:S(2)}, u32[]{:S(2)}) collective-permute-start(bf16[48,768]{1,0:T(8,128)(2,1)S(1)} %get-tuple-element.27.refs_2_), channel_id=1, source_target_pairs={{0,4},{2,6},{4,8},{5,1},{6,10},{7,3},{8,12},{9,5},{10,14},{11,7},{... | collective-permute-start | bytes 221192 | tf_op jit(solution)/shard_map/ppermute | solution.py:756
  10.2 7.8 %collective-permute-start.2 = (f32[2,72,128]{2,1,0:T(8,128)S(1)}, f32[2,72,128]{2,1,0:T(8,128)S(1)}, u32[]{:S(2)}, u32[]{:S(2)}) collective-permute-start(f32[2,72,128]{2,1,0:T(8,128)S(1)} %join.2.refs_0_), channel_id=1, source_target_pairs={{0,16},{4,20},{8,24},{12,28},{16,0},{20,4},{24,8},{28,12},{1,17},{... | collective-permute-start | bytes 221192 | tf_op jit(solution)/shard_map/ppermute | solution.py:49
  12.9 1.0 %copy-start.1 = (f32[256]{0:T(256)S(1)}, f32[256]{0:T(256)}, u32[]{:S(2)}) copy-start(f32[256]{0:T(256)} %param.10) | copy-start | bytes 3076
  17.9 2.7 %copy-start = (s32[24,64]{1,0:T(8,128)S(1)}, s32[24,64]{1,0:T(8,128)}, u32[]{:S(2)}) copy-start(s32[24,64]{1,0:T(8,128)} %lab_ref.1) | copy-start | bytes 18436
  17.9 2.7 %copy-start.2 = (bf16[3,3,256,128]{3,2,1,0:T(8,128)(2,1)S(1)}, bf16[3,3,256,128]{3,2,1,0:T(8,128)(2,1)}, u32[]{:S(2)}) copy-start(bf16[3,3,256,128]{3,2,1,0:T(8,128)(2,1)} %param.11) | copy-start | bytes 1769476
  17.9 2.7 %copy-start.3 = (f32[128]{0:T(128)S(1)}, f32[128]{0:T(128)}, u32[]{:S(2)}) copy-start(f32[128]{0:T(128)} %param.12) | copy-start | bytes 1540
  18.0 2.6 %collective-permute-start.3 = (bf16[12,64,256]{2,1,0:T(8,128)(2,1)S(1)}, bf16[12,64,256]{2,1,0:T(8,128)(2,1)S(1)}, u32[]{:S(2)}, u32[]{:S(2)}) collective-permute-start(bf16[12,64,256]{2,1,0:T(8,128)(2,1)S(1)} %conv_pool.1.refs_2_.refs_0_.own_ref), channel_id=1, source_target_pairs={{0,1},{1,0},{2,3},{3,2},{4,5},{5,4},{6,7},{7,6},{8,9},{9,8},{10,11... | collective-permute-start | bytes 1179656 | tf_op jit(solution)/shard_map/ppermute | solution.py:49
  18.1 1.8 %collective-permute-start.4 = (bf16[48,768]{1,0:T(8,128)(2,1)S(1)}, bf16[48,768]{1,0:T(8,128)(2,1)S(1)}, u32[]{:S(2)}, u32[]{:S(2)}) collective-permute-start(bf16[48,768]{1,0:T(8,128)(2,1)S(1)} %collective-permute-done.1.got_ref), channel_id=1, source_target_pairs={{0,1},{1,0},{2,3},{3,2},{4,5},{5,4},{6,7},{7,6},{8,9},{9,8},{10,11... | collective-permute-start | bytes 221192 | tf_op jit(solution)/shard_map/ppermute | solution.py:49
  18.6 5.8 %collective-permute-start.5 = (f32[4,72,128]{2,1,0:T(8,128)S(1)}, f32[4,72,128]{2,1,0:T(8,128)S(1)}, u32[]{:S(2)}, u32[]{:S(2)}) collective-permute-start(f32[4,72,128]{2,1,0:T(8,128)S(1)} %join.3.refs_0_), channel_id=1, source_target_pairs={{0,4},{4,0},{8,12},{12,8},{16,20},{20,16},{24,28},{28,24},{1,5},{5... | collective-permute-start | bytes 442376 | tf_op jit(solution)/shard_map/ppermute | solution.py:49
  26.7 8.8 %collective-permute-start.6 = (f16[616,128]{1,0:T(8,128)(2,1)S(1)}, f16[616,128]{1,0:T(8,128)(2,1)S(1)}, u32[]{:S(2)}, u32[]{:S(2)}) collective-permute-start(f16[616,128]{1,0:T(8,128)(2,1)S(1)} %convert_element_type.65), channel_id=1, source_target_pairs={{0,24},{4,28},{8,16},{12,20},{16,8},{20,12},{24,0},{28,4},{1,25},{... | collective-permute-start | bytes 473096 | tf_op jit(solution)/shard_map/ppermute | solution.py:49
  28.4 4.7 %collective-permute-start.7 = (f16[376,128]{1,0:T(8,128)(2,1)S(1)}, f16[376,128]{1,0:T(8,128)(2,1)S(1)}, u32[]{:S(2)}, u32[]{:S(2)}) collective-permute-start(f16[376,128]{1,0:T(8,128)(2,1)S(1)} %convert_element_type.67), channel_id=1, source_target_pairs={{0,4},{4,0},{8,12},{12,8},{16,20},{20,16},{24,28},{28,24},{1,5},{5... | collective-permute-start | bytes 288776 | tf_op jit(solution)/shard_map/ppermute | solution.py:49
  29.8 8.6 %collective-permute-start.9 = (f16[368,128]{1,0:T(8,128)(2,1)S(1)}, f16[368,128]{1,0:T(8,128)(2,1)S(1)}, u32[]{:S(2)}, u32[]{:S(2)}) collective-permute-start(f16[368,128]{1,0:T(8,128)(2,1)S(1)} %convert_element_type.71), channel_id=1, source_target_pairs={{0,8},{4,12},{8,0},{12,4},{16,24},{20,28},{24,16},{28,20},{1,9},{5... | collective-permute-start | bytes 282632 | tf_op jit(solution)/shard_map/ppermute | solution.py:49
  29.9 10.6 %collective-permute-start.10 = (f16[368,128]{1,0:T(8,128)(2,1)S(1)}, f16[368,128]{1,0:T(8,128)(2,1)S(1)}, u32[]{:S(2)}, u32[]{:S(2)}) collective-permute-start(f16[368,128]{1,0:T(8,128)(2,1)S(1)} %convert_element_type.73), channel_id=1, source_target_pairs={{0,12},{4,8},{8,4},{12,0},{16,28},{20,24},{24,20},{28,16},{1,13},{... | collective-permute-start | bytes 282632 | tf_op jit(solution)/shard_map/ppermute | solution.py:49
  33.1 7.4 %collective-permute-start.11 = (f16[360,128]{1,0:T(8,128)(2,1)S(1)}, f16[360,128]{1,0:T(8,128)(2,1)S(1)}, u32[]{:S(2)}, u32[]{:S(2)}) collective-permute-start(f16[360,128]{1,0:T(8,128)(2,1)S(1)} %convert_element_type.75), channel_id=1, source_target_pairs={{0,16},{4,20},{8,24},{12,28},{16,0},{20,4},{24,8},{28,12},{1,17},{... | collective-permute-start | bytes 276488 | tf_op jit(solution)/shard_map/ppermute | solution.py:49
  35.6 5.4 %collective-permute-start.8 = (f16[328,128]{1,0:T(8,128)(2,1)S(1)}, f16[328,128]{1,0:T(8,128)(2,1)S(1)}, u32[]{:S(2)}, u32[]{:S(2)}) collective-permute-start(f16[328,128]{1,0:T(8,128)(2,1)S(1)} %convert_element_type.69), channel_id=1, source_target_pairs={{0,4},{4,0},{8,12},{12,8},{16,20},{20,16},{24,28},{28,24},{1,5},{5... | collective-permute-start | bytes 251912 | tf_op jit(solution)/shard_map/ppermute | solution.py:49
  41.2 8.1 %collective-permute-start.15 = (f16[1,296,128]{2,1,0:T(8,128)(2,1)S(1)}, f16[1,296,128]{2,1,0:T(8,128)(2,1)S(1)}, u32[]{:S(2)}, u32[]{:S(2)}) collective-permute-start(f16[1,296,128]{2,1,0:T(8,128)(2,1)S(1)} %get-tuple-element.50), channel_id=1, source_target_pairs={{0,16},{4,20},{8,24},{12,28},{16,0},{20,4},{24,8},{28,12},{1,17},{... | collective-permute-start | bytes 227336 | tf_op jit(solution)/shard_map/ppermute | solution.py:49
  41.5 9.0 %collective-permute-start.16 = (f16[1,296,128]{2,1,0:T(8,128)(2,1)S(1)}, f16[1,296,128]{2,1,0:T(8,128)(2,1)S(1)}, u32[]{:S(2)}, u32[]{:S(2)}) collective-permute-start(f16[1,296,128]{2,1,0:T(8,128)(2,1)S(1)} %get-tuple-element.50), channel_id=1, source_target_pairs={{0,24},{4,28},{8,16},{12,20},{16,8},{20,12},{24,0},{28,4},{1,25},{... | collective-permute-start | bytes 227336 | tf_op jit(solution)/shard_map/ppermute | solution.py:49
  44.8 7.6 %collective-permute-start.12 = (f16[1,296,128]{2,1,0:T(8,128)(2,1)S(1)}, f16[1,296,128]{2,1,0:T(8,128)(2,1)S(1)}, u32[]{:S(2)}, u32[]{:S(2)}) collective-permute-start(f16[1,296,128]{2,1,0:T(8,128)(2,1)S(1)} %get-tuple-element.50), channel_id=1, source_target_pairs={{0,4},{4,0},{8,12},{12,8},{16,20},{20,16},{24,28},{28,24},{1,5},{5... | collective-permute-start | bytes 227336 | tf_op jit(solution)/shard_map/ppermute | solution.py:49
  44.8 7.6 %collective-permute-start.13 = (f16[1,296,128]{2,1,0:T(8,128)(2,1)S(1)}, f16[1,296,128]{2,1,0:T(8,128)(2,1)S(1)}, u32[]{:S(2)}, u32[]{:S(2)}) collective-permute-start(f16[1,296,128]{2,1,0:T(8,128)(2,1)S(1)} %get-tuple-element.50), channel_id=1, source_target_pairs={{0,8},{4,12},{8,0},{12,4},{16,24},{20,28},{24,16},{28,20},{1,9},{5... | collective-permute-start | bytes 227336 | tf_op jit(solution)/shard_map/ppermute | solution.py:49
  46.5 6.5 %collective-permute-start.14 = (f16[1,296,128]{2,1,0:T(8,128)(2,1)S(1)}, f16[1,296,128]{2,1,0:T(8,128)(2,1)S(1)}, u32[]{:S(2)}, u32[]{:S(2)}) collective-permute-start(f16[1,296,128]{2,1,0:T(8,128)(2,1)S(1)} %get-tuple-element.50), channel_id=1, source_target_pairs={{0,12},{4,8},{8,4},{12,0},{16,28},{20,24},{24,20},{28,16},{1,13},{... | collective-permute-start | bytes 227336 | tf_op jit(solution)/shard_map/ppermute | solution.py:49
  49.4 5.3 %collective-permute-start.17 = (f16[1,296,128]{2,1,0:T(8,128)(2,1)S(1)}, f16[1,296,128]{2,1,0:T(8,128)(2,1)S(1)}, u32[]{:S(2)}, u32[]{:S(2)}) collective-permute-start(f16[1,296,128]{2,1,0:T(8,128)(2,1)S(1)} %collective-permute-done.15), channel_id=1, source_target_pairs={{0,4},{4,0},{8,12},{12,8},{16,20},{20,16},{24,28},{28,24},{1,5},{5... | collective-permute-start | bytes 227336 | tf_op jit(solution)/shard_map/ppermute | solution.py:49
  50.6 5.6 %collective-permute-start.18 = (f16[1,296,128]{2,1,0:T(8,128)(2,1)S(1)}, f16[1,296,128]{2,1,0:T(8,128)(2,1)S(1)}, u32[]{:S(2)}, u32[]{:S(2)}) collective-permute-start(f16[1,296,128]{2,1,0:T(8,128)(2,1)S(1)} %collective-permute-done.16), channel_id=1, source_target_pairs={{0,4},{4,0},{8,12},{12,8},{16,20},{20,16},{24,28},{28,24},{1,5},{5... | collective-permute-start | bytes 227336 | tf_op jit(solution)/shard_map/ppermute | solution.py:49

commit v14 on v13

--- a/solution.py
+++ b/solution.py
@@ -26,6 +26,7 @@
     ((5,), 1, 48),
     ((6, 7), 1, 0),
 )
+SPARE = (0, 16, 0)
 NOTE = 8
 
 
@@ -639,8 +640,11 @@
     note = note_block(bias * up, power, power_sums, width)
     total = total * up
     if next_ways == 1:
-        out_refs[0][:size] = total
-        out_refs[0][size:] = note
+        for out_ref, spare in zip(out_refs, SPARE):
+            out_ref[:size] = total
+            out_ref[size : size + NOTE] = note
+            if spare:
+                out_ref[size + NOTE :] = jnp.zeros((spare, width), F32)
         return
     sums = sums * jnp.exp2(12.0 - power_sums)
     digit = lax.rem(position()[3] >> shift, next_ways)
@@ -660,7 +664,9 @@
     width = parts[0][0].shape[-1]
     sums_rows = sum(len(members) for _, _, _, members in parts) * entries
     if next_ways == 1:
-        outs = (jax.ShapeDtypeStruct((heads * chunk + NOTE, width), F32),)
+        outs = tuple(
+            jax.ShapeDtypeStruct((heads * chunk + NOTE + spare, width), F32) for spare in SPARE
+        )
     else:
         rows = heads // next_ways * chunk + NOTE + sums_rows
         outs = (jax.ShapeDtypeStruct((rows, width), F32),) * next_ways
@@ -827,13 +833,14 @@
         compiler_params=params(),
         name="embed",
     )(sums, *shared)
-    own = send[0].astype(F16)[None]
+    own, middle, long = (part.astype(F16)[None] for part in send)
     for at in range(3, bits, 3):
         own = jnp.concatenate(gather_step(own, "strip", (at, min(3, bits - at))), axis=0)
-    gathered = {m: swap(own, "strip", m) if m else own for m in range(4)}
-    for k in (2, 3):
-        gathered[2 * k] = swap(own, "strip", 2 * k)
-    late = {2 * k + 1: swap(gathered[2 * k], "strip", 1) for k in (2, 3)}
+        middle = long = own
+    gathered = {0: own, 1: swap(middle, "strip", 1), 2: swap(own, "strip", 2)}
+    gathered[3] = swap(middle, "strip", 3)
+    gathered[4], gathered[6] = swap(long, "strip", 4), swap(own, "strip", 6)
+    late = {m + 1: swap(gathered[m], "strip", 1) for m in (4, 6)}
     weight_rows, bias_row = spread(
         {**gathered, **late}, chunk, strip_count, 9 * channels
     )

time: 57.6 us -> 56.8 us (0.986)
  waiting for transfers between devices: 13.2 us -> 12.5 us
    ppermute x18, waiting for transfers between devices: 13.2 us -> 12.5 us  [swap(): return lax.ppermute(value, axis, [(i, i ^ mask) for i in range(count)])]
  transfers between devices with their start and end apart: 19 -> 19, of which waited for: 10 -> 9; matrix products, arithmetic and copies ran while one was open for 0% -> 0% of each run, Pallas kernels for 22% -> 22%
where the time goes in v14:
time: 56.8 us; the launch traced here: 56.6 us
  starting transfers between devices  25.5 us (45%)
  Pallas kernels  17.2 us (30%)
  waiting for transfers between devices  12.5 us (22%)
  between operations  1.01 us (2%)
    ppermute x18, starting transfers between devices, swap(): return lax.ppermute(value, axis, [(i, i ^ mask) for i in range(count)])  22.1 us
    ppermute x18, waiting for transfers between devices, swap(): return lax.ppermute(value, axis, [(i, i ^ mask) for i in range(count)])  12.5 us
    pallas_call x1, Pallas kernels, conv_pool(): pl.pallas_call(conv_kernel, out_shape=jax.ShapeDtypeStruct((pooled_rows,...  4.05 us
    pallas_call x1, Pallas kernels, deep_forward(): pl.pallas_call(functools.partial(deep_kernel, block=block, entries=entrie...  3.72 us
    ppermute x1, starting transfers between devices, body(): got = lax.ppermute(border, ('strip', 'chan'), pairs)  3.4 us
    pallas_call x1, Pallas kernels, deep_backward(): pl.pallas_call(functools.partial(grad_kernel, n_parts=len(parts), chunk=c...  2.27 us
    pallas_call x1, Pallas kernels, columns(): pl.pallas_call(columns_kernel, out_shape=(border,) * 3 + (jax.ShapeDtypeS...  2.14 us
    pallas_call x1, Pallas kernels, spread(): pl.pallas_call(functools.partial(spread_kernel, chunk=chunk, rows=rows, m...  1.17 us
  transfers between devices with their start and end apart: 19, of which 9 were waited for; matrix products, arithmetic and copies ran while one was open for 0% of the time, Pallas kernels for 22%

profile of v14, /device:TPU:0, one launch (start us, length us, event | category | flops | bytes accessed | tf_op | source)
XLA Modules:
  0.0 56.6 jit_solution(15104211312439580439)
XLA Ops:
  0.6 0.9 %pack_side.1.refs_0_ = f32[1,72,128]{2,1,0:T(8,128)S(1)} custom-call(f32[64,128]{1,0:T(8,128)} %grad_hbm.1, s32[24,64]{1,0:T(8,128)} %lab_ref.1, s32[1,32]{1,0:T(1,128)} %bitcast.19), custom_call_target="tpu_custom_call" | custom-call | tf_op jit(solution)/shard_map/pack_side/pallas_call | solution.py:281
  1.5 3.1 %collective-permute-start = (f32[1,72,128]{2,1,0:T(8,128)S(1)}, f32[1,72,128]{2,1,0:T(8,128)S(1)}, u32[]{:S(2)}, u32[]{:S(2)}) collective-permute-start(f32[1,72,128]{2,1,0:T(8,128)S(1)} %pack_side.1.refs_0_), channel_id=1, source_target_pairs={{0,8},{4,12},{8,0},{12,4},{16,24},{20,28},{24,16},{28,20},{1,9},{5... | collective-permute-start | bytes 110600 | tf_op jit(solution)/shard_map/ppermute | solution.py:50
  4.6 2.1 %columns.1 = (bf16[48,768]{1,0:T(8,128)(2,1)S(1)}, bf16[48,768]{1,0:T(8,128)(2,1)S(1)}, bf16[48,768]{1,0:T(8,128)(2,1)S(1)}, bf16[28,128,256]{2,1,0:T(8,128)(2,1)S(1)}, bf16[2304,256]{1,0:T(8,128)(2,1)S(1)}) custom-call(bf16[48,128,256]{2,1,0:T(8,128)(2,1)} %x_hbm.1, bf16[2304,256]{1,0:T(8,128)(2,1)} %bitcast.18), custom_call_target="tpu_custom_call" | custom-call | tf_op jit(solution)/shard_map/columns/pallas_call | solution.py:336
  6.8 3.4 %collective-permute-start.1 = (bf16[48,768]{1,0:T(8,128)(2,1)S(1)}, bf16[48,768]{1,0:T(8,128)(2,1)S(1)}, u32[]{:S(2)}, u32[]{:S(2)}) collective-permute-start(bf16[48,768]{1,0:T(8,128)(2,1)S(1)} %get-tuple-element.29.refs_2_), channel_id=1, source_target_pairs={{0,4},{2,6},{4,8},{5,1},{6,10},{7,3},{8,12},{9,5},{10,14},{11,7},{... | collective-permute-start | bytes 221192 | tf_op jit(solution)/shard_map/ppermute | solution.py:762
  10.2 2.7 %collective-permute-start.2 = (f32[2,72,128]{2,1,0:T(8,128)S(1)}, f32[2,72,128]{2,1,0:T(8,128)S(1)}, u32[]{:S(2)}, u32[]{:S(2)}) collective-permute-start(f32[2,72,128]{2,1,0:T(8,128)S(1)} %join.2.refs_0_), channel_id=1, source_target_pairs={{0,16},{4,20},{8,24},{12,28},{16,0},{20,4},{24,8},{28,12},{1,17},{... | collective-permute-start | bytes 221192 | tf_op jit(solution)/shard_map/ppermute | solution.py:50
  12.9 1.0 %windows.1.taps = bf16[36,64,1024]{2,1,0:T(8,128)(2,1)S(1)} custom-call(bf16[28,128,256]{2,1,0:T(8,128)(2,1)S(1)} %get-tuple-element.28.rows_ref, f32[2,72,128]{2,1,0:T(8,128)S(1)} %join.2.refs_0_), custom_call_target="tpu_custom_call" | custom-call | bytes 12582912 | tf_op jit(solution)/shard_map/windows/pallas_call | solution.py:121
  13.9 4.0 %conv_pool.1.refs_2_.refs_0_.own_ref = bf16[12,64,256]{2,1,0:T(8,128)(2,1)S(1)} custom-call(bf16[36,64,1024]{2,1,0:T(8,128)(2,1)S(1)} %windows.1.taps, bf16[2304,256]{1,0:T(8,128)(2,1)S(1)} %get-tuple-element.30.w_ref, f32[1,256]{1,0:T(1,128)S(1)} %bitcast.14, f32[2,72,128]{2,1,0:T(8,128)S(1)} %join.2.refs_0_), custom_call_target="tpu_custom_call" | custom-call | flops 3623878656 | bytes 8388608 | tf_op jit(solution)/shard_map/conv_pool/pallas_call | solution.py:210
  18.1 0.5 collective-permute-start.4
  18.6 0.4 collective-permute-start.5
  19.0 0.9 %collective-permute-done.4.traded_ref = bf16[48,768]{1,0:T(8,128)(2,1)S(1)} collective-permute-done((bf16[48,768]{1,0:T(8,128)(2,1)S(1)}, bf16[48,768]{1,0:T(8,128)(2,1)S(1)}, u32[]{:S(2)}, u32[]{:S(2)}) %collective-permute-start.4) | collective-permute-done | bytes 73760 | tf_op jit(solution)/shard_map/ppermute | solution.py:50
  19.9 0.7 %conv_edges.1.edge_ref = f32[4,2,24,128]{3,2,1,0:T(8,128)S(1)} custom-call(bf16[2304,256]{1,0:T(8,128)(2,1)S(1)} %get-tuple-element.30.w_ref, f32[1,256]{1,0:T(1,128)S(1)} %bitcast.15, bf16[48,768]{1,0:T(8,128)(2,1)S(1)} %collective-permute-done.1.got_ref, bf16[48,768]{1,0:T(8,128)(2,1)S(1)} %collective-permute-done.4.traded_ref, ...), custom_call_target="tpu_custom_call" | custom-call | bytes 4194304 | tf_op jit(solution)/shard_map/conv_edges/pallas_call | solution.py:236
  20.7 3.7 %deep_forward.1 = (bf16[26,64,768]{2,1,0:T(8,128)(2,1)S(1)}, bf16[24,64,128]{2,1,0:T(8,128)(2,1)S(1)}, f32[1536,128]{1,0:T(8,128)S(1)}, f32[32,128]{1,0:T(8,128)S(1)}) custom-call(bf16[12,64,256]{2,1,0:T(8,128)(2,1)S(1)} %conv_pool.1.refs_2_.refs_0_.own_ref, bf16[12,64,256]{2,1,0:T(8,128)(2,1)S(1)} %collective-permute-done.3.other_ref, ...), custom_call_target="tpu_custom_call" | custom-call | flops 1811939328 | bytes 8388608 | tf_op jit(solution)/shard_map/deep_forward/pallas_call | solution.py:477
  24.4 2.3 %deep_backward.1 = (f32[296,128]{1,0:T(8,128)S(1)}, f32[296,128]{1,0:T(8,128)S(1)}, f32[368,128]{1,0:T(8,128)S(1)}, f32[368,128]{1,0:T(8,128)S(1)}, f32[296,128]...) custom-call(bf16[26,64,768]{2,1,0:T(8,128)(2,1)S(1)} %get-tuple-element.35.taps, ...), custom_call_target="tpu_custom_call" | custom-call | flops 1811939328 | bytes 8388608 | tf_op jit(solution)/shard_map/deep_backward/pallas_call | solution.py:567
  26.7 1.6 %collective-permute-start.6 = (f16[616,128]{1,0:T(8,128)(2,1)S(1)}, f16[616,128]{1,0:T(8,128)(2,1)S(1)}, u32[]{:S(2)}, u32[]{:S(2)}) collective-permute-start(f16[616,128]{1,0:T(8,128)(2,1)S(1)} %convert_element_type.71), channel_id=1, source_target_pairs={{0,24},{4,28},{8,16},{12,20},{16,8},{20,12},{24,0},{28,4},{1,25},{... | collective-permute-start | bytes 473096 | tf_op jit(solution)/shard_map/ppermute | solution.py:50
  28.4 1.4 %collective-permute-start.7 = (f16[376,128]{1,0:T(8,128)(2,1)S(1)}, f16[376,128]{1,0:T(8,128)(2,1)S(1)}, u32[]{:S(2)}, u32[]{:S(2)}) collective-permute-start(f16[376,128]{1,0:T(8,128)(2,1)S(1)} %convert_element_type.73), channel_id=1, source_target_pairs={{0,4},{4,0},{8,12},{12,8},{16,20},{20,16},{24,28},{28,24},{1,5},{5... | collective-permute-start | bytes 288776 | tf_op jit(solution)/shard_map/ppermute | solution.py:50
  29.9 2.2 %collective-permute-start.10 = (f16[368,128]{1,0:T(8,128)(2,1)S(1)}, f16[368,128]{1,0:T(8,128)(2,1)S(1)}, u32[]{:S(2)}, u32[]{:S(2)}) collective-permute-start(f16[368,128]{1,0:T(8,128)(2,1)S(1)} %convert_element_type.79), channel_id=1, source_target_pairs={{0,12},{4,8},{8,4},{12,0},{16,28},{20,24},{24,20},{28,16},{1,13},{... | collective-permute-start | bytes 282632 | tf_op jit(solution)/shard_map/ppermute | solution.py:50
  32.1 0.9 %collective-permute-done.7 = f16[376,128]{1,0:T(8,128)(2,1)S(1)} collective-permute-done((f16[376,128]{1,0:T(8,128)(2,1)S(1)}, f16[376,128]{1,0:T(8,128)(2,1)S(1)}, u32[]{:S(2)}, u32[]{:S(2)}) %collective-permute-start.7) | collective-permute-done | bytes 96288 | tf_op jit(solution)/shard_map/ppermute | solution.py:50
  33.1 0.4 collective-permute-start.11
  33.5 2.0 %collective-permute-done.6 = f16[616,128]{1,0:T(8,128)(2,1)S(1)} collective-permute-done((f16[616,128]{1,0:T(8,128)(2,1)S(1)}, f16[616,128]{1,0:T(8,128)(2,1)S(1)}, u32[]{:S(2)}, u32[]{:S(2)}) %collective-permute-start.6) | collective-permute-done | bytes 157728 | tf_op jit(solution)/shard_map/ppermute | solution.py:50
  35.6 0.7 %collective-permute-start.8 = (f16[328,128]{1,0:T(8,128)(2,1)S(1)}, f16[328,128]{1,0:T(8,128)(2,1)S(1)}, u32[]{:S(2)}, u32[]{:S(2)}) collective-permute-start(f16[328,128]{1,0:T(8,128)(2,1)S(1)} %convert_element_type.75), channel_id=1, source_target_pairs={{0,4},{4,0},{8,12},{12,8},{16,20},{20,16},{24,28},{28,24},{1,5},{5... | collective-permute-start | bytes 251912 | tf_op jit(solution)/shard_map/ppermute | solution.py:50
  36.4 2.0 %collective-permute-done.9 = f16[368,128]{1,0:T(8,128)(2,1)S(1)} collective-permute-done((f16[368,128]{1,0:T(8,128)(2,1)S(1)}, f16[368,128]{1,0:T(8,128)(2,1)S(1)}, u32[]{:S(2)}, u32[]{:S(2)}) %collective-permute-start.9) | collective-permute-done | bytes 94240 | tf_op jit(solution)/shard_map/ppermute | solution.py:50
  38.4 2.1 %collective-permute-done.10 = f16[368,128]{1,0:T(8,128)(2,1)S(1)} collective-permute-done((f16[368,128]{1,0:T(8,128)(2,1)S(1)}, f16[368,128]{1,0:T(8,128)(2,1)S(1)}, u32[]{:S(2)}, u32[]{:S(2)}) %collective-permute-start.10) | collective-permute-done | bytes 94240 | tf_op jit(solution)/shard_map/ppermute | solution.py:50
  40.5 0.5 collective-permute-done.8
  41.3 2.6 %collective-permute-start.16 = (f16[1,296,128]{2,1,0:T(8,128)(2,1)S(1)}, f16[1,296,128]{2,1,0:T(8,128)(2,1)S(1)}, u32[]{:S(2)}, u32[]{:S(2)}) collective-permute-start(f16[1,296,128]{2,1,0:T(8,128)(2,1)S(1)} %get-tuple-element.54), channel_id=1, source_target_pairs={{0,24},{4,28},{8,16},{12,20},{16,8},{20,12},{24,0},{28,4},{1,25},{... | collective-permute-start | bytes 227336 | tf_op jit(solution)/shard_map/ppermute | solution.py:50
  44.0 0.3 collective-permute-start.12
  44.3 3.0 %collective-permute-start.14 = (f16[1,312,128]{2,1,0:T(8,128)(2,1)S(1)}, f16[1,312,128]{2,1,0:T(8,128)(2,1)S(1)}, u32[]{:S(2)}, u32[]{:S(2)}) collective-permute-start(f16[1,312,128]{2,1,0:T(8,128)(2,1)S(1)} %convert_bitcast_fusion), channel_id=1, source_target_pairs={{0,12},{4,8},{8,4},{12,0},{16,28},{20,24},{24,20},{28,16},{1,13},{... | collective-permute-start | bytes 239624 | tf_op jit(solution)/shard_map/ppermute | solution.py:50
  47.8 1.9 %collective-permute-start.18 = (f16[1,296,128]{2,1,0:T(8,128)(2,1)S(1)}, f16[1,296,128]{2,1,0:T(8,128)(2,1)S(1)}, u32[]{:S(2)}, u32[]{:S(2)}) collective-permute-start(f16[1,296,128]{2,1,0:T(8,128)(2,1)S(1)} %collective-permute-done.16), channel_id=1, source_target_pairs={{0,4},{4,0},{8,12},{12,8},{16,20},{20,16},{24,28},{28,24},{1,5},{5... | collective-permute-start | bytes 227336 | tf_op jit(solution)/shard_map/ppermute | solution.py:50
  49.7 1.3 %collective-permute-done.15 = f16[1,296,128]{2,1,0:T(8,128)(2,1)S(1)} collective-permute-done((f16[1,296,128]{2,1,0:T(8,128)(2,1)S(1)}, f16[1,296,128]{2,1,0:T(8,128)(2,1)S(1)}, u32[]{:S(2)}, u32[]{:S(2)}) %collective-permute-start.15) | collective-permute-done | bytes 75808 | tf_op jit(solution)/shard_map/ppermute | solution.py:50
  51.0 0.7 %collective-permute-start.17 = (f16[1,296,128]{2,1,0:T(8,128)(2,1)S(1)}, f16[1,296,128]{2,1,0:T(8,128)(2,1)S(1)}, u32[]{:S(2)}, u32[]{:S(2)}) collective-permute-start(f16[1,296,128]{2,1,0:T(8,128)(2,1)S(1)} %collective-permute-done.15), channel_id=1, source_target_pairs={{0,4},{4,0},{8,12},{12,8},{16,20},{20,16},{24,28},{28,24},{1,5},{5... | collective-permute-start | bytes 227336 | tf_op jit(solution)/shard_map/ppermute | solution.py:50
  51.7 1.0 %embed.1 = f32[64,128]{1,0:T(8,128)} custom-call(f32[256,128]{1,0:T(8,128)S(1)} %get-tuple-element.47.sums_ref, f32[4,72,128]{2,1,0:T(8,128)S(1)} %join.3.refs_0_, f32[4,72,128]{2,1,0:T(8,128)S(1)} %collective-permute-done.5.refs_1_), custom_call_target="tpu_custom_call" | custom-call | tf_op jit(solution)/shard_map/embed/pallas_call | solution.py:828
  52.9 2.5 %collective-permute-done.17 = f16[1,296,128]{2,1,0:T(8,128)(2,1)S(1)} collective-permute-done((f16[1,296,128]{2,1,0:T(8,128)(2,1)S(1)}, f16[1,296,128]{2,1,0:T(8,128)(2,1)S(1)}, u32[]{:S(2)}, u32[]{:S(2)}) %collective-permute-start.17) | collective-permute-done | bytes 75808 | tf_op jit(solution)/shard_map/ppermute | solution.py:50
  55.4 1.2 %spread.1 = (f32[2304,128]{1,0:T(8,128)}, f32[1,128]{1,0:T(1,128)}) custom-call(f32[1,296,128]{2,1,0:T(8,128)S(1)} %get-tuple-element.53.refs_0_, f32[1,312,128]{2,1,0:T(8,128)S(1)} %convert_element_type.87.refs_1_, f32[1,296,128]{2,1,0:T(8,128)S(1)} %convert_element_type.88.refs_2_, f32[1,312,128]{2,1,0:T(8,128)S(1)} %convert_element_type.89.refs_3_, ...), custom_call_target="tpu_custom_call" | custom-call | tf_op jit(solution)/shard_map/spread/pallas_call | solution.py:732
  (50 shorter events, 1.4 us)
Async XLA Ops:
  1.5 8.6 %collective-permute-start = (f32[1,72,128]{2,1,0:T(8,128)S(1)}, f32[1,72,128]{2,1,0:T(8,128)S(1)}, u32[]{:S(2)}, u32[]{:S(2)}) collective-permute-start(f32[1,72,128]{2,1,0:T(8,128)S(1)} %pack_side.1.refs_0_), channel_id=1, source_target_pairs={{0,8},{4,12},{8,0},{12,4},{16,24},{20,28},{24,16},{28,20},{1,9},{5... | collective-permute-start | bytes 110600 | tf_op jit(solution)/shard_map/ppermute | solution.py:50
  6.8 11.2 %collective-permute-start.1 = (bf16[48,768]{1,0:T(8,128)(2,1)S(1)}, bf16[48,768]{1,0:T(8,128)(2,1)S(1)}, u32[]{:S(2)}, u32[]{:S(2)}) collective-permute-start(bf16[48,768]{1,0:T(8,128)(2,1)S(1)} %get-tuple-element.29.refs_2_), channel_id=1, source_target_pairs={{0,4},{2,6},{4,8},{5,1},{6,10},{7,3},{8,12},{9,5},{10,14},{11,7},{... | collective-permute-start | bytes 221192 | tf_op jit(solution)/shard_map/ppermute | solution.py:762
  10.2 7.8 %collective-permute-start.2 = (f32[2,72,128]{2,1,0:T(8,128)S(1)}, f32[2,72,128]{2,1,0:T(8,128)S(1)}, u32[]{:S(2)}, u32[]{:S(2)}) collective-permute-start(f32[2,72,128]{2,1,0:T(8,128)S(1)} %join.2.refs_0_), channel_id=1, source_target_pairs={{0,16},{4,20},{8,24},{12,28},{16,0},{20,4},{24,8},{28,12},{1,17},{... | collective-permute-start | bytes 221192 | tf_op jit(solution)/shard_map/ppermute | solution.py:50
  12.9 1.0 %copy-start.1 = (f32[256]{0:T(256)S(1)}, f32[256]{0:T(256)}, u32[]{:S(2)}) copy-start(f32[256]{0:T(256)} %param.10) | copy-start | bytes 3076
  17.9 2.7 %copy-start = (s32[24,64]{1,0:T(8,128)S(1)}, s32[24,64]{1,0:T(8,128)}, u32[]{:S(2)}) copy-start(s32[24,64]{1,0:T(8,128)} %lab_ref.1) | copy-start | bytes 18436
  17.9 2.7 %copy-start.2 = (bf16[3,3,256,128]{3,2,1,0:T(8,128)(2,1)S(1)}, bf16[3,3,256,128]{3,2,1,0:T(8,128)(2,1)}, u32[]{:S(2)}) copy-start(bf16[3,3,256,128]{3,2,1,0:T(8,128)(2,1)} %param.11) | copy-start | bytes 1769476
  17.9 2.7 %copy-start.3 = (f32[128]{0:T(128)S(1)}, f32[128]{0:T(128)}, u32[]{:S(2)}) copy-start(f32[128]{0:T(128)} %param.12) | copy-start | bytes 1540
  18.0 2.6 %collective-permute-start.3 = (bf16[12,64,256]{2,1,0:T(8,128)(2,1)S(1)}, bf16[12,64,256]{2,1,0:T(8,128)(2,1)S(1)}, u32[]{:S(2)}, u32[]{:S(2)}) collective-permute-start(bf16[12,64,256]{2,1,0:T(8,128)(2,1)S(1)} %conv_pool.1.refs_2_.refs_0_.own_ref), channel_id=1, source_target_pairs={{0,1},{1,0},{2,3},{3,2},{4,5},{5,4},{6,7},{7,6},{8,9},{9,8},{10,11... | collective-permute-start | bytes 1179656 | tf_op jit(solution)/shard_map/ppermute | solution.py:50
  18.1 1.8 %collective-permute-start.4 = (bf16[48,768]{1,0:T(8,128)(2,1)S(1)}, bf16[48,768]{1,0:T(8,128)(2,1)S(1)}, u32[]{:S(2)}, u32[]{:S(2)}) collective-permute-start(bf16[48,768]{1,0:T(8,128)(2,1)S(1)} %collective-permute-done.1.got_ref), channel_id=1, source_target_pairs={{0,1},{1,0},{2,3},{3,2},{4,5},{5,4},{6,7},{7,6},{8,9},{9,8},{10,11... | collective-permute-start | bytes 221192 | tf_op jit(solution)/shard_map/ppermute | solution.py:50
  18.6 5.8 %collective-permute-start.5 = (f32[4,72,128]{2,1,0:T(8,128)S(1)}, f32[4,72,128]{2,1,0:T(8,128)S(1)}, u32[]{:S(2)}, u32[]{:S(2)}) collective-permute-start(f32[4,72,128]{2,1,0:T(8,128)S(1)} %join.3.refs_0_), channel_id=1, source_target_pairs={{0,4},{4,0},{8,12},{12,8},{16,20},{20,16},{24,28},{28,24},{1,5},{5... | collective-permute-start | bytes 442376 | tf_op jit(solution)/shard_map/ppermute | solution.py:50
  26.7 8.8 %collective-permute-start.6 = (f16[616,128]{1,0:T(8,128)(2,1)S(1)}, f16[616,128]{1,0:T(8,128)(2,1)S(1)}, u32[]{:S(2)}, u32[]{:S(2)}) collective-permute-start(f16[616,128]{1,0:T(8,128)(2,1)S(1)} %convert_element_type.71), channel_id=1, source_target_pairs={{0,24},{4,28},{8,16},{12,20},{16,8},{20,12},{24,0},{28,4},{1,25},{... | collective-permute-start | bytes 473096 | tf_op jit(solution)/shard_map/ppermute | solution.py:50
  28.4 4.7 %collective-permute-start.7 = (f16[376,128]{1,0:T(8,128)(2,1)S(1)}, f16[376,128]{1,0:T(8,128)(2,1)S(1)}, u32[]{:S(2)}, u32[]{:S(2)}) collective-permute-start(f16[376,128]{1,0:T(8,128)(2,1)S(1)} %convert_element_type.73), channel_id=1, source_target_pairs={{0,4},{4,0},{8,12},{12,8},{16,20},{20,16},{24,28},{28,24},{1,5},{5... | collective-permute-start | bytes 288776 | tf_op jit(solution)/shard_map/ppermute | solution.py:50
  29.8 8.6 %collective-permute-start.9 = (f16[368,128]{1,0:T(8,128)(2,1)S(1)}, f16[368,128]{1,0:T(8,128)(2,1)S(1)}, u32[]{:S(2)}, u32[]{:S(2)}) collective-permute-start(f16[368,128]{1,0:T(8,128)(2,1)S(1)} %convert_element_type.77), channel_id=1, source_target_pairs={{0,8},{4,12},{8,0},{12,4},{16,24},{20,28},{24,16},{28,20},{1,9},{5... | collective-permute-start | bytes 282632 | tf_op jit(solution)/shard_map/ppermute | solution.py:50
  29.9 10.6 %collective-permute-start.10 = (f16[368,128]{1,0:T(8,128)(2,1)S(1)}, f16[368,128]{1,0:T(8,128)(2,1)S(1)}, u32[]{:S(2)}, u32[]{:S(2)}) collective-permute-start(f16[368,128]{1,0:T(8,128)(2,1)S(1)} %convert_element_type.79), channel_id=1, source_target_pairs={{0,12},{4,8},{8,4},{12,0},{16,28},{20,24},{24,20},{28,16},{1,13},{... | collective-permute-start | bytes 282632 | tf_op jit(solution)/shard_map/ppermute | solution.py:50
  33.1 7.4 %collective-permute-start.11 = (f16[360,128]{1,0:T(8,128)(2,1)S(1)}, f16[360,128]{1,0:T(8,128)(2,1)S(1)}, u32[]{:S(2)}, u32[]{:S(2)}) collective-permute-start(f16[360,128]{1,0:T(8,128)(2,1)S(1)} %convert_element_type.81), channel_id=1, source_target_pairs={{0,16},{4,20},{8,24},{12,28},{16,0},{20,4},{24,8},{28,12},{1,17},{... | collective-permute-start | bytes 276488 | tf_op jit(solution)/shard_map/ppermute | solution.py:50
  35.6 5.4 %collective-permute-start.8 = (f16[328,128]{1,0:T(8,128)(2,1)S(1)}, f16[328,128]{1,0:T(8,128)(2,1)S(1)}, u32[]{:S(2)}, u32[]{:S(2)}) collective-permute-start(f16[328,128]{1,0:T(8,128)(2,1)S(1)} %convert_element_type.75), channel_id=1, source_target_pairs={{0,4},{4,0},{8,12},{12,8},{16,20},{20,16},{24,28},{28,24},{1,5},{5... | collective-permute-start | bytes 251912 | tf_op jit(solution)/shard_map/ppermute | solution.py:50
  41.3 6.5 %collective-permute-start.16 = (f16[1,296,128]{2,1,0:T(8,128)(2,1)S(1)}, f16[1,296,128]{2,1,0:T(8,128)(2,1)S(1)}, u32[]{:S(2)}, u32[]{:S(2)}) collective-permute-start(f16[1,296,128]{2,1,0:T(8,128)(2,1)S(1)} %get-tuple-element.54), channel_id=1, source_target_pairs={{0,24},{4,28},{8,16},{12,20},{16,8},{20,12},{24,0},{28,4},{1,25},{... | collective-permute-start | bytes 227336 | tf_op jit(solution)/shard_map/ppermute | solution.py:50
  43.9 7.1 %collective-permute-start.15 = (f16[1,296,128]{2,1,0:T(8,128)(2,1)S(1)}, f16[1,296,128]{2,1,0:T(8,128)(2,1)S(1)}, u32[]{:S(2)}, u32[]{:S(2)}) collective-permute-start(f16[1,296,128]{2,1,0:T(8,128)(2,1)S(1)} %convert_bitcast_fusion.1), channel_id=1, source_target_pairs={{0,16},{4,20},{8,24},{12,28},{16,0},{20,4},{24,8},{28,12},{1,17},{... | collective-permute-start | bytes 227336 | tf_op jit(solution)/shard_map/ppermute | solution.py:50
  44.0 8.7 %collective-permute-start.12 = (f16[1,312,128]{2,1,0:T(8,128)(2,1)S(1)}, f16[1,312,128]{2,1,0:T(8,128)(2,1)S(1)}, u32[]{:S(2)}, u32[]{:S(2)}) collective-permute-start(f16[1,312,128]{2,1,0:T(8,128)(2,1)S(1)} %convert_bitcast_fusion), channel_id=1, source_target_pairs={{0,4},{4,0},{8,12},{12,8},{16,20},{20,16},{24,28},{28,24},{1,5},{5... | collective-permute-start | bytes 239624 | tf_op jit(solution)/shard_map/ppermute | solution.py:50
  44.3 8.5 %collective-permute-start.14 = (f16[1,312,128]{2,1,0:T(8,128)(2,1)S(1)}, f16[1,312,128]{2,1,0:T(8,128)(2,1)S(1)}, u32[]{:S(2)}, u32[]{:S(2)}) collective-permute-start(f16[1,312,128]{2,1,0:T(8,128)(2,1)S(1)} %convert_bitcast_fusion), channel_id=1, source_target_pairs={{0,12},{4,8},{8,4},{12,0},{16,28},{20,24},{24,20},{28,16},{1,13},{... | collective-permute-start | bytes 239624 | tf_op jit(solution)/shard_map/ppermute | solution.py:50
  47.3 5.4 %collective-permute-start.13 = (f16[1,296,128]{2,1,0:T(8,128)(2,1)S(1)}, f16[1,296,128]{2,1,0:T(8,128)(2,1)S(1)}, u32[]{:S(2)}, u32[]{:S(2)}) collective-permute-start(f16[1,296,128]{2,1,0:T(8,128)(2,1)S(1)} %get-tuple-element.54), channel_id=1, source_target_pairs={{0,8},{4,12},{8,0},{12,4},{16,24},{20,28},{24,16},{28,20},{1,9},{5... | collective-permute-start | bytes 227336 | tf_op jit(solution)/shard_map/ppermute | solution.py:50
  47.8 5.0 %collective-permute-start.18 = (f16[1,296,128]{2,1,0:T(8,128)(2,1)S(1)}, f16[1,296,128]{2,1,0:T(8,128)(2,1)S(1)}, u32[]{:S(2)}, u32[]{:S(2)}) collective-permute-start(f16[1,296,128]{2,1,0:T(8,128)(2,1)S(1)} %collective-permute-done.16), channel_id=1, source_target_pairs={{0,4},{4,0},{8,12},{12,8},{16,20},{20,16},{24,28},{28,24},{1,5},{5... | collective-permute-start | bytes 227336 | tf_op jit(solution)/shard_map/ppermute | solution.py:50
  51.0 4.4 %collective-permute-start.17 = (f16[1,296,128]{2,1,0:T(8,128)(2,1)S(1)}, f16[1,296,128]{2,1,0:T(8,128)(2,1)S(1)}, u32[]{:S(2)}, u32[]{:S(2)}) collective-permute-start(f16[1,296,128]{2,1,0:T(8,128)(2,1)S(1)} %collective-permute-done.15), channel_id=1, source_target_pairs={{0,4},{4,0},{8,12},{12,8},{16,20},{20,16},{24,28},{28,24},{1,5},{5... | collective-permute-start | bytes 227336 | tf_op jit(solution)/shard_map/ppermute | solution.py:50

commit v15 on v14

--- a/solution.py
+++ b/solution.py
@@ -17,15 +17,7 @@
 WIDTH = 3
 PIECE = 4
 STEP = 6
-PAYLOADS = (
-    ((0,), 0, 0),
-    ((1,), 0, 0),
-    ((2,), 1, 40),
-    ((3,), 1, 40),
-    ((4,), 0, 0),
-    ((5,), 1, 48),
-    ((6, 7), 1, 0),
-)
+PAYLOADS = (((0,), 0), ((1,), 0), ((2,), 0), ((3,), 0), ((4,), 0), ((5,), 1), ((6, 7), 1))
 SPARE = (0, 16, 0)
 NOTE = 8
 
@@ -546,18 +538,15 @@
     digit = lax.rem(me, ways)
     heads = weight.shape[0] // chunk // ways
     sums = sums * jnp.exp2(12.0 - power_sums)
-    for out_ref, (members, with_sums, spare) in zip(out_refs, PAYLOADS):
+    for out_ref, (members, with_sums) in zip(out_refs, PAYLOADS):
         at = 0
         for m, hi in itertools.product(members, range(heads)):
             j = hi * ways + (digit ^ m)
             out_ref[at : at + chunk] = weight[pl.ds(pl.multiple_of(j * chunk, 8), chunk)] * up
             at += chunk
         out_ref[at : at + NOTE] = note
-        at += NOTE
         if with_sums:
-            out_ref[at : at + entries] = sums
-        if spare:
-            out_ref[at + entries :] = jnp.zeros((spare, width), F32)
+            out_ref[at + NOTE :] = sums
 
 
 def deep_backward(forward, parts, chunk, count):
@@ -567,10 +556,8 @@
     return pl.pallas_call(
         functools.partial(grad_kernel, n_parts=len(parts), chunk=chunk),
         out_shape=tuple(
-            jax.ShapeDtypeStruct(
-                (len(members) * size + NOTE + with_sums * entries + spare, width), F32
-            )
-            for members, with_sums, spare in PAYLOADS
+            jax.ShapeDtypeStruct((len(members) * size + NOTE + with_sums * entries, width), F32)
+            for members, with_sums in PAYLOADS
         ),
         in_specs=[VMEM] * (4 + len(parts)),
         out_specs=(VMEM,) * len(PAYLOADS),
@@ -583,27 +570,27 @@
     )(*forward, *parts)
 
 
-def pair_kernel(own_ref, got_ref, *refs, size, entries, got_at, got_note, with_own):
+def pair_kernel(own_ref, got_ref, *refs, size, entries, got_at, got_note, sums_notes):
     out_ref = refs[-1]
     own, got = own_ref[size : size + NOTE], got_ref[got_note : got_note + NOTE]
     power = jnp.maximum(own[1:2], got[1:2]) + 1.0
-    power_sums = jnp.maximum(own[2:3], got[2:3])
     own_down, got_down = jnp.exp2(own[1:2] - power), jnp.exp2(got[1:2] - power)
     out_ref[:size] = own_ref[:size] * own_down + got_ref[got_at : got_at + size] * got_down
     bias = own[0:1] * own_down + got[0:1] * got_down
+    powers = [ref[at + 2 : at + 3] for ref, at in zip(refs, sums_notes)]
+    power_sums = functools.reduce(jnp.maximum, powers)
     out_ref[size : size + NOTE] = note_block(bias, power, power_sums, own.shape[-1])
-    at = size + NOTE
-    if with_own:
-        sums = refs[0][at : at + entries] * jnp.exp2(own[2:3] - power_sums)
-        out_ref[at : at + entries] = sums
-        at += entries
-    sums = got_ref[got_note + NOTE : got_note + NOTE + entries] * jnp.exp2(got[2:3] - power_sums)
-    out_ref[at : at + entries] = sums
-
-
-def merge_pair(own, got, own_sums, size, entries, got_at, got_note, after):
+    place = size + NOTE
+    for ref, at, one in zip(refs, sums_notes, powers):
+        sums = ref[at + NOTE : at + NOTE + entries] * jnp.exp2(one - power_sums)
+        out_ref[place : place + entries] = sums
+        place += entries
+    if place < out_ref.shape[0]:
+        out_ref[place:] = jnp.zeros((out_ref.shape[0] - place, own.shape[-1]), F32)
+
+
+def merge_pair(own, got, sums, size, entries, got_at, got_note, after, spare=0):
     width = own.shape[-1]
-    rows = size + NOTE + (1 + len(own_sums)) * entries
     return pl.pallas_call(
         functools.partial(
             pair_kernel,
@@ -611,14 +598,14 @@
             entries=entries,
             got_at=got_at,
             got_note=got_note,
-            with_own=bool(own_sums),
+            sums_notes=tuple(at for _, at in sums),
         ),
-        out_shape=jax.ShapeDtypeStruct((rows, width), F32),
-        in_specs=[VMEM] * (2 + len(own_sums)) + [ANY] * len(after),
+        out_shape=jax.ShapeDtypeStruct((size + NOTE + len(sums) * entries + spare, width), F32),
+        in_specs=[VMEM] * (2 + len(sums)) + [ANY] * len(after),
         out_specs=VMEM,
         compiler_params=params(),
         name="merge_pair",
-    )(own, got, *own_sums, *after)
+    )(own, got, *(part for part, _ in sums), *after)
 
 
 def merge_kernel(*refs, plan, chunk, heads, entries, shift, next_ways):
@@ -794,17 +781,19 @@
     def sent(part, mask):
         return swap(part.astype(F16), "strip", mask).astype(F32)
 
-    kept, beside, near, across, paired, pair, far = deep_backward(
+    kept, beside, near, near_pair, paired, pair, far = deep_backward(
         forward, shared, chunk, strip_count
     )
-    got_far, got_pair = sent(far, 6), sent(pair, 1)
-    onward = merge_pair(paired, got_pair, [pair], size, entries, 0, size, [])
-    beside = merge_pair(beside, got_far, [], size, entries, size, 2 * size, [onward])
+    got_far, got_pair, got_near = sent(far, 6), sent(pair, 1), sent(near_pair, 1)
+    both = [(pair, size), (got_pair, size)]
+    onward = merge_pair(paired, got_pair, both, size, entries, 0, size, [], spare=8)
+    near = merge_pair(near, got_near, both, size, entries, 0, size, [onward])
+    last = [(got_far, 2 * size)]
+    beside = merge_pair(beside, got_far, last, size, entries, size, 2 * size, [near])
     parts = [
         (kept, True, size, []),
         (sent(beside, 1), True, size, [7]),
-        (sent(near, 2), True, size, [2]),
-        (sent(across, 3), True, size, [3]),
+        (sent(near, 2), True, size, [2, 3]),
         (sent(onward, 4), True, size, [4, 5]),
         (got_far, True, 2 * size, [6]),
         (pair, False, size, [0]),

time: 56.8 us -> 56.2 us (0.989)
  waiting for transfers between devices: 12.5 us -> 10.9 us
  starting transfers between devices: 25.5 us -> 26.5 us
    ppermute x18, waiting for transfers between devices: 12.5 us -> 10.9 us  [swap(): return lax.ppermute(value, axis, [(i, i ^ mask) for i in range(count)])]
    ppermute x18, starting transfers between devices: 22.1 us -> 23.1 us  [swap(): return lax.ppermute(value, axis, [(i, i ^ mask) for i in range(count)])]
  transfers between devices with their start and end apart: 19 -> 19, of which waited for: 9 -> 9; matrix products, arithmetic and copies ran while one was open for 0% -> 0% of each run, Pallas kernels for 22% -> 23%
where the time goes in v15:
time: 56.2 us; the launch traced here: 56 us
  starting transfers between devices  26.5 us (47%)
  Pallas kernels  17.2 us (31%)
  waiting for transfers between devices  10.9 us (19%)
  between operations  0.99 us (2%)
    ppermute x18, starting transfers between devices, swap(): return lax.ppermute(value, axis, [(i, i ^ mask) for i in range(count)])  23.1 us
    ppermute x18, waiting for transfers between devices, swap(): return lax.ppermute(value, axis, [(i, i ^ mask) for i in range(count)])  10.9 us
    pallas_call x1, Pallas kernels, conv_pool(): pl.pallas_call(conv_kernel, out_shape=jax.ShapeDtypeStruct((pooled_rows,...  4.05 us
    pallas_call x1, Pallas kernels, deep_forward(): pl.pallas_call(functools.partial(deep_kernel, block=block, entries=entrie...  3.71 us
    ppermute x1, starting transfers between devices, body(): got = lax.ppermute(border, ('strip', 'chan'), pairs)  3.4 us
    pallas_call x1, Pallas kernels, deep_backward(): pl.pallas_call(functools.partial(grad_kernel, n_parts=len(parts), chunk=c...  2.27 us
    pallas_call x1, Pallas kernels, columns(): pl.pallas_call(columns_kernel, out_shape=(border,) * 3 + (jax.ShapeDtypeS...  2.14 us
    pallas_call x1, Pallas kernels, spread(): pl.pallas_call(functools.partial(spread_kernel, chunk=chunk, rows=rows, m...  1.17 us
  transfers between devices with their start and end apart: 19, of which 9 were waited for; matrix products, arithmetic and copies ran while one was open for 0% of the time, Pallas kernels for 23%

profile of v15, /device:TPU:0, one launch (start us, length us, event | category | flops | bytes accessed | tf_op | source)
XLA Modules:
  0.0 56.0 jit_solution(12199647280560598821)
XLA Ops:
  0.6 0.9 %pack_side.1.refs_0_ = f32[1,72,128]{2,1,0:T(8,128)S(1)} custom-call(f32[64,128]{1,0:T(8,128)} %grad_hbm.1, s32[24,64]{1,0:T(8,128)} %lab_ref.1, s32[1,32]{1,0:T(1,128)} %bitcast.19), custom_call_target="tpu_custom_call" | custom-call | tf_op jit(solution)/shard_map/pack_side/pallas_call | solution.py:273
  1.5 3.1 %collective-permute-start = (f32[1,72,128]{2,1,0:T(8,128)S(1)}, f32[1,72,128]{2,1,0:T(8,128)S(1)}, u32[]{:S(2)}, u32[]{:S(2)}) collective-permute-start(f32[1,72,128]{2,1,0:T(8,128)S(1)} %pack_side.1.refs_0_), channel_id=1, source_target_pairs={{0,8},{4,12},{8,0},{12,4},{16,24},{20,28},{24,16},{28,20},{1,9},{5... | collective-permute-start | bytes 110600 | tf_op jit(solution)/shard_map/ppermute | solution.py:42
  4.6 2.1 %columns.1 = (bf16[48,768]{1,0:T(8,128)(2,1)S(1)}, bf16[48,768]{1,0:T(8,128)(2,1)S(1)}, bf16[48,768]{1,0:T(8,128)(2,1)S(1)}, bf16[28,128,256]{2,1,0:T(8,128)(2,1)S(1)}, bf16[2304,256]{1,0:T(8,128)(2,1)S(1)}) custom-call(bf16[48,128,256]{2,1,0:T(8,128)(2,1)} %x_hbm.1, bf16[2304,256]{1,0:T(8,128)(2,1)} %bitcast.18), custom_call_target="tpu_custom_call" | custom-call | tf_op jit(solution)/shard_map/columns/pallas_call | solution.py:328
  6.8 3.4 %collective-permute-start.1 = (bf16[48,768]{1,0:T(8,128)(2,1)S(1)}, bf16[48,768]{1,0:T(8,128)(2,1)S(1)}, u32[]{:S(2)}, u32[]{:S(2)}) collective-permute-start(bf16[48,768]{1,0:T(8,128)(2,1)S(1)} %get-tuple-element.29.refs_2_), channel_id=1, source_target_pairs={{0,4},{2,6},{4,8},{5,1},{6,10},{7,3},{8,12},{9,5},{10,14},{11,7},{... | collective-permute-start | bytes 221192 | tf_op jit(solution)/shard_map/ppermute | solution.py:749
  10.2 2.7 %collective-permute-start.2 = (f32[2,72,128]{2,1,0:T(8,128)S(1)}, f32[2,72,128]{2,1,0:T(8,128)S(1)}, u32[]{:S(2)}, u32[]{:S(2)}) collective-permute-start(f32[2,72,128]{2,1,0:T(8,128)S(1)} %join.2.refs_0_), channel_id=1, source_target_pairs={{0,16},{4,20},{8,24},{12,28},{16,0},{20,4},{24,8},{28,12},{1,17},{... | collective-permute-start | bytes 221192 | tf_op jit(solution)/shard_map/ppermute | solution.py:42
  12.9 1.0 %windows.1.taps = bf16[36,64,1024]{2,1,0:T(8,128)(2,1)S(1)} custom-call(bf16[28,128,256]{2,1,0:T(8,128)(2,1)S(1)} %get-tuple-element.28.rows_ref, f32[2,72,128]{2,1,0:T(8,128)S(1)} %join.2.refs_0_), custom_call_target="tpu_custom_call" | custom-call | bytes 12582912 | tf_op jit(solution)/shard_map/windows/pallas_call | solution.py:113
  13.9 4.0 %conv_pool.1.refs_2_.refs_0_.own_ref = bf16[12,64,256]{2,1,0:T(8,128)(2,1)S(1)} custom-call(bf16[36,64,1024]{2,1,0:T(8,128)(2,1)S(1)} %windows.1.taps, bf16[2304,256]{1,0:T(8,128)(2,1)S(1)} %get-tuple-element.30.w_ref, f32[1,256]{1,0:T(1,128)S(1)} %bitcast.14, f32[2,72,128]{2,1,0:T(8,128)S(1)} %join.2.refs_0_), custom_call_target="tpu_custom_call" | custom-call | flops 3623878656 | bytes 8388608 | tf_op jit(solution)/shard_map/conv_pool/pallas_call | solution.py:202
  18.1 0.5 collective-permute-start.4
  18.6 0.4 collective-permute-start.5
  19.0 0.9 %collective-permute-done.4.traded_ref = bf16[48,768]{1,0:T(8,128)(2,1)S(1)} collective-permute-done((bf16[48,768]{1,0:T(8,128)(2,1)S(1)}, bf16[48,768]{1,0:T(8,128)(2,1)S(1)}, u32[]{:S(2)}, u32[]{:S(2)}) %collective-permute-start.4) | collective-permute-done | bytes 73760 | tf_op jit(solution)/shard_map/ppermute | solution.py:42
  19.9 0.7 %conv_edges.1.edge_ref = f32[4,2,24,128]{3,2,1,0:T(8,128)S(1)} custom-call(bf16[2304,256]{1,0:T(8,128)(2,1)S(1)} %get-tuple-element.30.w_ref, f32[1,256]{1,0:T(1,128)S(1)} %bitcast.15, bf16[48,768]{1,0:T(8,128)(2,1)S(1)} %collective-permute-done.1.got_ref, bf16[48,768]{1,0:T(8,128)(2,1)S(1)} %collective-permute-done.4.traded_ref, ...), custom_call_target="tpu_custom_call" | custom-call | bytes 4194304 | tf_op jit(solution)/shard_map/conv_edges/pallas_call | solution.py:228
  20.7 3.7 %deep_forward.1 = (bf16[26,64,768]{2,1,0:T(8,128)(2,1)S(1)}, bf16[24,64,128]{2,1,0:T(8,128)(2,1)S(1)}, f32[1536,128]{1,0:T(8,128)S(1)}, f32[32,128]{1,0:T(8,128)S(1)}) custom-call(bf16[12,64,256]{2,1,0:T(8,128)(2,1)S(1)} %conv_pool.1.refs_2_.refs_0_.own_ref, bf16[12,64,256]{2,1,0:T(8,128)(2,1)S(1)} %collective-permute-done.3.other_ref, ...), custom_call_target="tpu_custom_call" | custom-call | flops 1811939328 | bytes 8388608 | tf_op jit(solution)/shard_map/deep_forward/pallas_call | solution.py:469
  24.4 2.3 %deep_backward.1 = (f32[296,128]{1,0:T(8,128)S(1)}, f32[296,128]{1,0:T(8,128)S(1)}, f32[296,128]{1,0:T(8,128)S(1)}, f32[296,128]{1,0:T(8,128)S(1)}, f32[296,128]...) custom-call(bf16[26,64,768]{2,1,0:T(8,128)(2,1)S(1)} %get-tuple-element.35.taps, ...), custom_call_target="tpu_custom_call" | custom-call | flops 1811939328 | bytes 8388608 | tf_op jit(solution)/shard_map/deep_backward/pallas_call | solution.py:556
  26.7 1.6 %collective-permute-start.6 = (f16[616,128]{1,0:T(8,128)(2,1)S(1)}, f16[616,128]{1,0:T(8,128)(2,1)S(1)}, u32[]{:S(2)}, u32[]{:S(2)}) collective-permute-start(f16[616,128]{1,0:T(8,128)(2,1)S(1)} %convert_element_type.71), channel_id=1, source_target_pairs={{0,24},{4,28},{8,16},{12,20},{16,8},{20,12},{24,0},{28,4},{1,25},{... | collective-permute-start | bytes 473096 | tf_op jit(solution)/shard_map/ppermute | solution.py:42
  28.4 1.4 %collective-permute-start.8 = (f16[328,128]{1,0:T(8,128)(2,1)S(1)}, f16[328,128]{1,0:T(8,128)(2,1)S(1)}, u32[]{:S(2)}, u32[]{:S(2)}) collective-permute-start(f16[328,128]{1,0:T(8,128)(2,1)S(1)} %convert_element_type.75), channel_id=1, source_target_pairs={{0,4},{4,0},{8,12},{12,8},{16,20},{20,16},{24,28},{28,24},{1,5},{5... | collective-permute-start | bytes 251912 | tf_op jit(solution)/shard_map/ppermute | solution.py:42
  29.8 0.8 %collective-permute-start.7 = (f16[296,128]{1,0:T(8,128)(2,1)S(1)}, f16[296,128]{1,0:T(8,128)(2,1)S(1)}, u32[]{:S(2)}, u32[]{:S(2)}) collective-permute-start(f16[296,128]{1,0:T(8,128)(2,1)S(1)} %convert_element_type.73), channel_id=1, source_target_pairs={{0,4},{4,0},{8,12},{12,8},{16,20},{20,16},{24,28},{28,24},{1,5},{5... | collective-permute-start | bytes 227336 | tf_op jit(solution)/shard_map/ppermute | solution.py:42
  30.5 3.2 %collective-permute-done.8 = f16[328,128]{1,0:T(8,128)(2,1)S(1)} collective-permute-done((f16[328,128]{1,0:T(8,128)(2,1)S(1)}, f16[328,128]{1,0:T(8,128)(2,1)S(1)}, u32[]{:S(2)}, u32[]{:S(2)}) %collective-permute-start.8) | collective-permute-done | bytes 84000 | tf_op jit(solution)/shard_map/ppermute | solution.py:42
  34.0 0.5 collective-permute-done.7
  34.6 2.0 %collective-permute-start.10 = (f16[360,128]{1,0:T(8,128)(2,1)S(1)}, f16[360,128]{1,0:T(8,128)(2,1)S(1)}, u32[]{:S(2)}, u32[]{:S(2)}) collective-permute-start(f16[360,128]{1,0:T(8,128)(2,1)S(1)} %convert_element_type.79), channel_id=1, source_target_pairs={{0,8},{4,12},{8,0},{12,4},{16,24},{20,28},{24,16},{28,20},{1,9},{5... | collective-permute-start | bytes 276488 | tf_op jit(solution)/shard_map/ppermute | solution.py:42
  36.7 1.0 %collective-permute-start.9 = (f16[328,128]{1,0:T(8,128)(2,1)S(1)}, f16[328,128]{1,0:T(8,128)(2,1)S(1)}, u32[]{:S(2)}, u32[]{:S(2)}) collective-permute-start(f16[328,128]{1,0:T(8,128)(2,1)S(1)} %convert_element_type.77), channel_id=1, source_target_pairs={{0,4},{4,0},{8,12},{12,8},{16,20},{20,16},{24,28},{28,24},{1,5},{5... | collective-permute-start | bytes 251912 | tf_op jit(solution)/shard_map/ppermute | solution.py:42
  37.7 3.0 %collective-permute-done.10 = f16[360,128]{1,0:T(8,128)(2,1)S(1)} collective-permute-done((f16[360,128]{1,0:T(8,128)(2,1)S(1)}, f16[360,128]{1,0:T(8,128)(2,1)S(1)}, u32[]{:S(2)}, u32[]{:S(2)}) %collective-permute-start.10) | collective-permute-done | bytes 92192 | tf_op jit(solution)/shard_map/ppermute | solution.py:42
  40.7 0.5 collective-permute-done.9
  41.5 1.9 %collective-permute-start.16 = (f16[1,296,128]{2,1,0:T(8,128)(2,1)S(1)}, f16[1,296,128]{2,1,0:T(8,128)(2,1)S(1)}, u32[]{:S(2)}, u32[]{:S(2)}) collective-permute-start(f16[1,296,128]{2,1,0:T(8,128)(2,1)S(1)} %get-tuple-element.54), channel_id=1, source_target_pairs={{0,24},{4,28},{8,16},{12,20},{16,8},{20,12},{24,0},{28,4},{1,25},{... | collective-permute-start | bytes 227336 | tf_op jit(solution)/shard_map/ppermute | solution.py:42
  43.4 2.7 %collective-permute-start.15 = (f16[1,296,128]{2,1,0:T(8,128)(2,1)S(1)}, f16[1,296,128]{2,1,0:T(8,128)(2,1)S(1)}, u32[]{:S(2)}, u32[]{:S(2)}) collective-permute-start(f16[1,296,128]{2,1,0:T(8,128)(2,1)S(1)} %convert_bitcast_fusion.1), channel_id=1, source_target_pairs={{0,16},{4,20},{8,24},{12,28},{16,0},{20,4},{24,8},{28,12},{1,17},{... | collective-permute-start | bytes 227336 | tf_op jit(solution)/shard_map/ppermute | solution.py:42
  46.1 1.5 %collective-permute-start.14 = (f16[1,312,128]{2,1,0:T(8,128)(2,1)S(1)}, f16[1,312,128]{2,1,0:T(8,128)(2,1)S(1)}, u32[]{:S(2)}, u32[]{:S(2)}) collective-permute-start(f16[1,312,128]{2,1,0:T(8,128)(2,1)S(1)} %convert_bitcast_fusion), channel_id=1, source_target_pairs={{0,12},{4,8},{8,4},{12,0},{16,28},{20,24},{24,20},{28,16},{1,13},{... | collective-permute-start | bytes 239624 | tf_op jit(solution)/shard_map/ppermute | solution.py:42
  47.6 2.0 %collective-permute-start.13 = (f16[1,296,128]{2,1,0:T(8,128)(2,1)S(1)}, f16[1,296,128]{2,1,0:T(8,128)(2,1)S(1)}, u32[]{:S(2)}, u32[]{:S(2)}) collective-permute-start(f16[1,296,128]{2,1,0:T(8,128)(2,1)S(1)} %get-tuple-element.54), channel_id=1, source_target_pairs={{0,8},{4,12},{8,0},{12,4},{16,24},{20,28},{24,16},{28,20},{1,9},{5... | collective-permute-start | bytes 227336 | tf_op jit(solution)/shard_map/ppermute | solution.py:42
  49.7 0.7 %collective-permute-done.15 = f16[1,296,128]{2,1,0:T(8,128)(2,1)S(1)} collective-permute-done((f16[1,296,128]{2,1,0:T(8,128)(2,1)S(1)}, f16[1,296,128]{2,1,0:T(8,128)(2,1)S(1)}, u32[]{:S(2)}, u32[]{:S(2)}) %collective-permute-start.15) | collective-permute-done | bytes 75808 | tf_op jit(solution)/shard_map/ppermute | solution.py:42
  50.4 1.3 %collective-permute-start.17 = (f16[1,296,128]{2,1,0:T(8,128)(2,1)S(1)}, f16[1,296,128]{2,1,0:T(8,128)(2,1)S(1)}, u32[]{:S(2)}, u32[]{:S(2)}) collective-permute-start(f16[1,296,128]{2,1,0:T(8,128)(2,1)S(1)} %collective-permute-done.15), channel_id=1, source_target_pairs={{0,4},{4,0},{8,12},{12,8},{16,20},{20,16},{24,28},{28,24},{1,5},{5... | collective-permute-start | bytes 227336 | tf_op jit(solution)/shard_map/ppermute | solution.py:42
  51.6 1.0 %embed.1 = f32[64,128]{1,0:T(8,128)} custom-call(f32[256,128]{1,0:T(8,128)S(1)} %get-tuple-element.47.sums_ref, f32[4,72,128]{2,1,0:T(8,128)S(1)} %join.3.refs_0_, f32[4,72,128]{2,1,0:T(8,128)S(1)} %collective-permute-done.5.refs_1_), custom_call_target="tpu_custom_call" | custom-call | tf_op jit(solution)/shard_map/embed/pallas_call | solution.py:817
  52.9 1.1 %collective-permute-done.18 = f16[1,296,128]{2,1,0:T(8,128)(2,1)S(1)} collective-permute-done((f16[1,296,128]{2,1,0:T(8,128)(2,1)S(1)}, f16[1,296,128]{2,1,0:T(8,128)(2,1)S(1)}, u32[]{:S(2)}, u32[]{:S(2)}) %collective-permute-start.18) | collective-permute-done | bytes 75808 | tf_op jit(solution)/shard_map/ppermute | solution.py:42
  54.0 0.8 %collective-permute-done.17 = f16[1,296,128]{2,1,0:T(8,128)(2,1)S(1)} collective-permute-done((f16[1,296,128]{2,1,0:T(8,128)(2,1)S(1)}, f16[1,296,128]{2,1,0:T(8,128)(2,1)S(1)}, u32[]{:S(2)}, u32[]{:S(2)}) %collective-permute-start.17) | collective-permute-done | bytes 75808 | tf_op jit(solution)/shard_map/ppermute | solution.py:42
  54.8 1.2 %spread.1 = (f32[2304,128]{1,0:T(8,128)}, f32[1,128]{1,0:T(1,128)}) custom-call(f32[1,296,128]{2,1,0:T(8,128)S(1)} %get-tuple-element.53.refs_0_, f32[1,312,128]{2,1,0:T(8,128)S(1)} %convert_element_type.87.refs_1_, f32[1,296,128]{2,1,0:T(8,128)S(1)} %convert_element_type.88.refs_2_, f32[1,312,128]{2,1,0:T(8,128)S(1)} %convert_element_type.89.refs_3_, ...), custom_call_target="tpu_custom_call" | custom-call | tf_op jit(solution)/shard_map/spread/pallas_call | solution.py:719
  (51 shorter events, 1.3 us)
Async XLA Ops:
  1.5 8.6 %collective-permute-start = (f32[1,72,128]{2,1,0:T(8,128)S(1)}, f32[1,72,128]{2,1,0:T(8,128)S(1)}, u32[]{:S(2)}, u32[]{:S(2)}) collective-permute-start(f32[1,72,128]{2,1,0:T(8,128)S(1)} %pack_side.1.refs_0_), channel_id=1, source_target_pairs={{0,8},{4,12},{8,0},{12,4},{16,24},{20,28},{24,16},{28,20},{1,9},{5... | collective-permute-start | bytes 110600 | tf_op jit(solution)/shard_map/ppermute | solution.py:42
  6.8 11.2 %collective-permute-start.1 = (bf16[48,768]{1,0:T(8,128)(2,1)S(1)}, bf16[48,768]{1,0:T(8,128)(2,1)S(1)}, u32[]{:S(2)}, u32[]{:S(2)}) collective-permute-start(bf16[48,768]{1,0:T(8,128)(2,1)S(1)} %get-tuple-element.29.refs_2_), channel_id=1, source_target_pairs={{0,4},{2,6},{4,8},{5,1},{6,10},{7,3},{8,12},{9,5},{10,14},{11,7},{... | collective-permute-start | bytes 221192 | tf_op jit(solution)/shard_map/ppermute | solution.py:749
  10.2 7.8 %collective-permute-start.2 = (f32[2,72,128]{2,1,0:T(8,128)S(1)}, f32[2,72,128]{2,1,0:T(8,128)S(1)}, u32[]{:S(2)}, u32[]{:S(2)}) collective-permute-start(f32[2,72,128]{2,1,0:T(8,128)S(1)} %join.2.refs_0_), channel_id=1, source_target_pairs={{0,16},{4,20},{8,24},{12,28},{16,0},{20,4},{24,8},{28,12},{1,17},{... | collective-permute-start | bytes 221192 | tf_op jit(solution)/shard_map/ppermute | solution.py:42
  12.9 1.0 %copy-start.1 = (f32[256]{0:T(256)S(1)}, f32[256]{0:T(256)}, u32[]{:S(2)}) copy-start(f32[256]{0:T(256)} %param.10) | copy-start | bytes 3076
  17.9 2.7 %copy-start = (s32[24,64]{1,0:T(8,128)S(1)}, s32[24,64]{1,0:T(8,128)}, u32[]{:S(2)}) copy-start(s32[24,64]{1,0:T(8,128)} %lab_ref.1) | copy-start | bytes 18436
  17.9 2.7 %copy-start.2 = (bf16[3,3,256,128]{3,2,1,0:T(8,128)(2,1)S(1)}, bf16[3,3,256,128]{3,2,1,0:T(8,128)(2,1)}, u32[]{:S(2)}) copy-start(bf16[3,3,256,128]{3,2,1,0:T(8,128)(2,1)} %param.11) | copy-start | bytes 1769476
  17.9 2.7 %copy-start.3 = (f32[128]{0:T(128)S(1)}, f32[128]{0:T(128)}, u32[]{:S(2)}) copy-start(f32[128]{0:T(128)} %param.12) | copy-start | bytes 1540
  18.0 2.6 %collective-permute-start.3 = (bf16[12,64,256]{2,1,0:T(8,128)(2,1)S(1)}, bf16[12,64,256]{2,1,0:T(8,128)(2,1)S(1)}, u32[]{:S(2)}, u32[]{:S(2)}) collective-permute-start(bf16[12,64,256]{2,1,0:T(8,128)(2,1)S(1)} %conv_pool.1.refs_2_.refs_0_.own_ref), channel_id=1, source_target_pairs={{0,1},{1,0},{2,3},{3,2},{4,5},{5,4},{6,7},{7,6},{8,9},{9,8},{10,11... | collective-permute-start | bytes 1179656 | tf_op jit(solution)/shard_map/ppermute | solution.py:42
  18.1 1.8 %collective-permute-start.4 = (bf16[48,768]{1,0:T(8,128)(2,1)S(1)}, bf16[48,768]{1,0:T(8,128)(2,1)S(1)}, u32[]{:S(2)}, u32[]{:S(2)}) collective-permute-start(bf16[48,768]{1,0:T(8,128)(2,1)S(1)} %collective-permute-done.1.got_ref), channel_id=1, source_target_pairs={{0,1},{1,0},{2,3},{3,2},{4,5},{5,4},{6,7},{7,6},{8,9},{9,8},{10,11... | collective-permute-start | bytes 221192 | tf_op jit(solution)/shard_map/ppermute | solution.py:42
  18.6 5.8 %collective-permute-start.5 = (f32[4,72,128]{2,1,0:T(8,128)S(1)}, f32[4,72,128]{2,1,0:T(8,128)S(1)}, u32[]{:S(2)}, u32[]{:S(2)}) collective-permute-start(f32[4,72,128]{2,1,0:T(8,128)S(1)} %join.3.refs_0_), channel_id=1, source_target_pairs={{0,4},{4,0},{8,12},{12,8},{16,20},{20,16},{24,28},{28,24},{1,5},{5... | collective-permute-start | bytes 442376 | tf_op jit(solution)/shard_map/ppermute | solution.py:42
  26.7 9.9 %collective-permute-start.6 = (f16[616,128]{1,0:T(8,128)(2,1)S(1)}, f16[616,128]{1,0:T(8,128)(2,1)S(1)}, u32[]{:S(2)}, u32[]{:S(2)}) collective-permute-start(f16[616,128]{1,0:T(8,128)(2,1)S(1)} %convert_element_type.71), channel_id=1, source_target_pairs={{0,24},{4,28},{8,16},{12,20},{16,8},{20,12},{24,0},{28,4},{1,25},{... | collective-permute-start | bytes 473096 | tf_op jit(solution)/shard_map/ppermute | solution.py:42
  28.4 5.3 %collective-permute-start.8 = (f16[328,128]{1,0:T(8,128)(2,1)S(1)}, f16[328,128]{1,0:T(8,128)(2,1)S(1)}, u32[]{:S(2)}, u32[]{:S(2)}) collective-permute-start(f16[328,128]{1,0:T(8,128)(2,1)S(1)} %convert_element_type.75), channel_id=1, source_target_pairs={{0,4},{4,0},{8,12},{12,8},{16,20},{20,16},{24,28},{28,24},{1,5},{5... | collective-permute-start | bytes 251912 | tf_op jit(solution)/shard_map/ppermute | solution.py:42
  29.8 4.7 %collective-permute-start.7 = (f16[296,128]{1,0:T(8,128)(2,1)S(1)}, f16[296,128]{1,0:T(8,128)(2,1)S(1)}, u32[]{:S(2)}, u32[]{:S(2)}) collective-permute-start(f16[296,128]{1,0:T(8,128)(2,1)S(1)} %convert_element_type.73), channel_id=1, source_target_pairs={{0,4},{4,0},{8,12},{12,8},{16,20},{20,16},{24,28},{28,24},{1,5},{5... | collective-permute-start | bytes 227336 | tf_op jit(solution)/shard_map/ppermute | solution.py:42
  33.8 6.9 %collective-permute-start.11 = (f16[368,128]{1,0:T(8,128)(2,1)S(1)}, f16[368,128]{1,0:T(8,128)(2,1)S(1)}, u32[]{:S(2)}, u32[]{:S(2)}) collective-permute-start(f16[368,128]{1,0:T(8,128)(2,1)S(1)} %convert_element_type.81), channel_id=1, source_target_pairs={{0,16},{4,20},{8,24},{12,28},{16,0},{20,4},{24,8},{28,12},{1,17},{... | collective-permute-start | bytes 282632 | tf_op jit(solution)/shard_map/ppermute | solution.py:42
  34.6 6.0 %collective-permute-start.10 = (f16[360,128]{1,0:T(8,128)(2,1)S(1)}, f16[360,128]{1,0:T(8,128)(2,1)S(1)}, u32[]{:S(2)}, u32[]{:S(2)}) collective-permute-start(f16[360,128]{1,0:T(8,128)(2,1)S(1)} %convert_element_type.79), channel_id=1, source_target_pairs={{0,8},{4,12},{8,0},{12,4},{16,24},{20,28},{24,16},{28,20},{1,9},{5... | collective-permute-start | bytes 276488 | tf_op jit(solution)/shard_map/ppermute | solution.py:42
  36.7 4.5 %collective-permute-start.9 = (f16[328,128]{1,0:T(8,128)(2,1)S(1)}, f16[328,128]{1,0:T(8,128)(2,1)S(1)}, u32[]{:S(2)}, u32[]{:S(2)}) collective-permute-start(f16[328,128]{1,0:T(8,128)(2,1)S(1)} %convert_element_type.77), channel_id=1, source_target_pairs={{0,4},{4,0},{8,12},{12,8},{16,20},{20,16},{24,28},{28,24},{1,5},{5... | collective-permute-start | bytes 251912 | tf_op jit(solution)/shard_map/ppermute | solution.py:42
  41.5 8.1 %collective-permute-start.16 = (f16[1,296,128]{2,1,0:T(8,128)(2,1)S(1)}, f16[1,296,128]{2,1,0:T(8,128)(2,1)S(1)}, u32[]{:S(2)}, u32[]{:S(2)}) collective-permute-start(f16[1,296,128]{2,1,0:T(8,128)(2,1)S(1)} %get-tuple-element.54), channel_id=1, source_target_pairs={{0,24},{4,28},{8,16},{12,20},{16,8},{20,12},{24,0},{28,4},{1,25},{... | collective-permute-start | bytes 227336 | tf_op jit(solution)/shard_map/ppermute | solution.py:42
  43.4 7.0 %collective-permute-start.15 = (f16[1,296,128]{2,1,0:T(8,128)(2,1)S(1)}, f16[1,296,128]{2,1,0:T(8,128)(2,1)S(1)}, u32[]{:S(2)}, u32[]{:S(2)}) collective-permute-start(f16[1,296,128]{2,1,0:T(8,128)(2,1)S(1)} %convert_bitcast_fusion.1), channel_id=1, source_target_pairs={{0,16},{4,20},{8,24},{12,28},{16,0},{20,4},{24,8},{28,12},{1,17},{... | collective-permute-start | bytes 227336 | tf_op jit(solution)/shard_map/ppermute | solution.py:42
  46.0 6.8 %collective-permute-start.12 = (f16[1,312,128]{2,1,0:T(8,128)(2,1)S(1)}, f16[1,312,128]{2,1,0:T(8,128)(2,1)S(1)}, u32[]{:S(2)}, u32[]{:S(2)}) collective-permute-start(f16[1,312,128]{2,1,0:T(8,128)(2,1)S(1)} %convert_bitcast_fusion), channel_id=1, source_target_pairs={{0,4},{4,0},{8,12},{12,8},{16,20},{20,16},{24,28},{28,24},{1,5},{5... | collective-permute-start | bytes 239624 | tf_op jit(solution)/shard_map/ppermute | solution.py:42
  46.1 6.7 %collective-permute-start.14 = (f16[1,312,128]{2,1,0:T(8,128)(2,1)S(1)}, f16[1,312,128]{2,1,0:T(8,128)(2,1)S(1)}, u32[]{:S(2)}, u32[]{:S(2)}) collective-permute-start(f16[1,312,128]{2,1,0:T(8,128)(2,1)S(1)} %convert_bitcast_fusion), channel_id=1, source_target_pairs={{0,12},{4,8},{8,4},{12,0},{16,28},{20,24},{24,20},{28,16},{1,13},{... | collective-permute-start | bytes 239624 | tf_op jit(solution)/shard_map/ppermute | solution.py:42
  47.6 5.2 %collective-permute-start.13 = (f16[1,296,128]{2,1,0:T(8,128)(2,1)S(1)}, f16[1,296,128]{2,1,0:T(8,128)(2,1)S(1)}, u32[]{:S(2)}, u32[]{:S(2)}) collective-permute-start(f16[1,296,128]{2,1,0:T(8,128)(2,1)S(1)} %get-tuple-element.54), channel_id=1, source_target_pairs={{0,8},{4,12},{8,0},{12,4},{16,24},{20,28},{24,16},{28,20},{1,9},{5... | collective-permute-start | bytes 227336 | tf_op jit(solution)/shard_map/ppermute | solution.py:42
  49.6 4.4 %collective-permute-start.18 = (f16[1,296,128]{2,1,0:T(8,128)(2,1)S(1)}, f16[1,296,128]{2,1,0:T(8,128)(2,1)S(1)}, u32[]{:S(2)}, u32[]{:S(2)}) collective-permute-start(f16[1,296,128]{2,1,0:T(8,128)(2,1)S(1)} %collective-permute-done.16), channel_id=1, source_target_pairs={{0,4},{4,0},{8,12},{12,8},{16,20},{20,16},{24,28},{28,24},{1,5},{5... | collective-permute-start | bytes 227336 | tf_op jit(solution)/shard_map/ppermute | solution.py:42
  50.4 4.4 %collective-permute-start.17 = (f16[1,296,128]{2,1,0:T(8,128)(2,1)S(1)}, f16[1,296,128]{2,1,0:T(8,128)(2,1)S(1)}, u32[]{:S(2)}, u32[]{:S(2)}) collective-permute-start(f16[1,296,128]{2,1,0:T(8,128)(2,1)S(1)} %collective-permute-done.15), channel_id=1, source_target_pairs={{0,4},{4,0},{8,12},{12,8},{16,20},{20,16},{24,28},{28,24},{1,5},{5... | collective-permute-start | bytes 227336 | tf_op jit(solution)/shard_map/ppermute | solution.py:42

commit v16 on v15

--- a/solution.py
+++ b/solution.py
@@ -309,7 +309,7 @@
         copy.wait()
         x = ref[...].astype(F32).reshape(rows * reach, chans)
         for t in range(lanes):
-            wide[t] = x[:, t * 128 : (t + 1) * 128]
+            wide[t, : rows * reach] = x[:, t * 128 : (t + 1) * 128]
         for c in range(WIDTH):
             for t in range(lanes):
                 part = wide[t, pl.ds(at + c, rows, stride=reach), :].astype(BF16)
@@ -334,7 +334,7 @@
         scratch_shapes=[
             pltpu.VMEM((rows, reach, chans), BF16),
             pltpu.VMEM((rows, reach, chans), BF16),
-            pltpu.VMEM((chans // 128, rows * reach, 128), F32),
+            pltpu.VMEM((chans // 128, (rows + 1) * reach, 128), F32),
             pltpu.SemaphoreType.DMA((7,)),
         ],
         compiler_params=params(16),

time: 56.2 us -> 56.2 us (level)
  no operation moved by 1% of the time
where the time goes in v16:
time: 56.2 us; the launch traced here: 56 us
  starting transfers between devices  26.5 us (47%)
  Pallas kernels  17.2 us (31%)
  waiting for transfers between devices  10.9 us (19%)
  between operations  0.99 us (2%)
    ppermute x18, starting transfers between devices, swap(): return lax.ppermute(value, axis, [(i, i ^ mask) for i in range(count)])  23.1 us
    ppermute x18, waiting for transfers between devices, swap(): return lax.ppermute(value, axis, [(i, i ^ mask) for i in range(count)])  10.9 us
    pallas_call x1, Pallas kernels, conv_pool(): pl.pallas_call(conv_kernel, out_shape=jax.ShapeDtypeStruct((pooled_rows,...  4.05 us
    pallas_call x1, Pallas kernels, deep_forward(): pl.pallas_call(functools.partial(deep_kernel, block=block, entries=entrie...  3.71 us
    ppermute x1, starting transfers between devices, body(): got = lax.ppermute(border, ('strip', 'chan'), pairs)  3.4 us
    pallas_call x1, Pallas kernels, deep_backward(): pl.pallas_call(functools.partial(grad_kernel, n_parts=len(parts), chunk=c...  2.27 us
    pallas_call x1, Pallas kernels, columns(): pl.pallas_call(columns_kernel, out_shape=(border,) * 3 + (jax.ShapeDtypeS...  2.14 us
    pallas_call x1, Pallas kernels, spread(): pl.pallas_call(functools.partial(spread_kernel, chunk=chunk, rows=rows, m...  1.17 us
  transfers between devices with their start and end apart: 19, of which 9 were waited for; matrix products, arithmetic and copies ran while one was open for 0% of the time, Pallas kernels for 23%

profile of v16, /device:TPU:0, one launch (start us, length us, event | category | flops | bytes accessed | tf_op | source)
XLA Modules:
  0.0 56.0 jit_solution(12029800772973724013)
XLA Ops:
  0.6 0.9 %pack_side.1.refs_0_ = f32[1,72,128]{2,1,0:T(8,128)S(1)} custom-call(f32[64,128]{1,0:T(8,128)} %grad_hbm.1, s32[24,64]{1,0:T(8,128)} %lab_ref.1, s32[1,32]{1,0:T(1,128)} %bitcast.19), custom_call_target="tpu_custom_call" | custom-call | tf_op jit(solution)/shard_map/pack_side/pallas_call | solution.py:273
  1.5 3.1 %collective-permute-start = (f32[1,72,128]{2,1,0:T(8,128)S(1)}, f32[1,72,128]{2,1,0:T(8,128)S(1)}, u32[]{:S(2)}, u32[]{:S(2)}) collective-permute-start(f32[1,72,128]{2,1,0:T(8,128)S(1)} %pack_side.1.refs_0_), channel_id=1, source_target_pairs={{0,8},{4,12},{8,0},{12,4},{16,24},{20,28},{24,16},{28,20},{1,9},{5... | collective-permute-start | bytes 110600 | tf_op jit(solution)/shard_map/ppermute | solution.py:42
  4.6 2.1 %columns.1 = (bf16[48,768]{1,0:T(8,128)(2,1)S(1)}, bf16[48,768]{1,0:T(8,128)(2,1)S(1)}, bf16[48,768]{1,0:T(8,128)(2,1)S(1)}, bf16[28,128,256]{2,1,0:T(8,128)(2,1)S(1)}, bf16[2304,256]{1,0:T(8,128)(2,1)S(1)}) custom-call(bf16[48,128,256]{2,1,0:T(8,128)(2,1)} %x_hbm.1, bf16[2304,256]{1,0:T(8,128)(2,1)} %bitcast.18), custom_call_target="tpu_custom_call" | custom-call | tf_op jit(solution)/shard_map/columns/pallas_call | solution.py:328
  6.8 3.4 %collective-permute-start.1 = (bf16[48,768]{1,0:T(8,128)(2,1)S(1)}, bf16[48,768]{1,0:T(8,128)(2,1)S(1)}, u32[]{:S(2)}, u32[]{:S(2)}) collective-permute-start(bf16[48,768]{1,0:T(8,128)(2,1)S(1)} %get-tuple-element.29.refs_2_), channel_id=1, source_target_pairs={{0,4},{2,6},{4,8},{5,1},{6,10},{7,3},{8,12},{9,5},{10,14},{11,7},{... | collective-permute-start | bytes 221192 | tf_op jit(solution)/shard_map/ppermute | solution.py:749
  10.2 2.7 %collective-permute-start.2 = (f32[2,72,128]{2,1,0:T(8,128)S(1)}, f32[2,72,128]{2,1,0:T(8,128)S(1)}, u32[]{:S(2)}, u32[]{:S(2)}) collective-permute-start(f32[2,72,128]{2,1,0:T(8,128)S(1)} %join.2.refs_0_), channel_id=1, source_target_pairs={{0,16},{4,20},{8,24},{12,28},{16,0},{20,4},{24,8},{28,12},{1,17},{... | collective-permute-start | bytes 221192 | tf_op jit(solution)/shard_map/ppermute | solution.py:42
  12.9 1.0 %windows.1.taps = bf16[36,64,1024]{2,1,0:T(8,128)(2,1)S(1)} custom-call(bf16[28,128,256]{2,1,0:T(8,128)(2,1)S(1)} %get-tuple-element.28.rows_ref, f32[2,72,128]{2,1,0:T(8,128)S(1)} %join.2.refs_0_), custom_call_target="tpu_custom_call" | custom-call | bytes 12582912 | tf_op jit(solution)/shard_map/windows/pallas_call | solution.py:113
  13.9 4.0 %conv_pool.1.refs_2_.refs_0_.own_ref = bf16[12,64,256]{2,1,0:T(8,128)(2,1)S(1)} custom-call(bf16[36,64,1024]{2,1,0:T(8,128)(2,1)S(1)} %windows.1.taps, bf16[2304,256]{1,0:T(8,128)(2,1)S(1)} %get-tuple-element.30.w_ref, f32[1,256]{1,0:T(1,128)S(1)} %bitcast.14, f32[2,72,128]{2,1,0:T(8,128)S(1)} %join.2.refs_0_), custom_call_target="tpu_custom_call" | custom-call | flops 3623878656 | bytes 8388608 | tf_op jit(solution)/shard_map/conv_pool/pallas_call | solution.py:202
  18.1 0.5 collective-permute-start.4
  18.6 0.4 collective-permute-start.5
  19.0 0.9 %collective-permute-done.4.traded_ref = bf16[48,768]{1,0:T(8,128)(2,1)S(1)} collective-permute-done((bf16[48,768]{1,0:T(8,128)(2,1)S(1)}, bf16[48,768]{1,0:T(8,128)(2,1)S(1)}, u32[]{:S(2)}, u32[]{:S(2)}) %collective-permute-start.4) | collective-permute-done | bytes 73760 | tf_op jit(solution)/shard_map/ppermute | solution.py:42
  19.9 0.7 %conv_edges.1.edge_ref = f32[4,2,24,128]{3,2,1,0:T(8,128)S(1)} custom-call(bf16[2304,256]{1,0:T(8,128)(2,1)S(1)} %get-tuple-element.30.w_ref, f32[1,256]{1,0:T(1,128)S(1)} %bitcast.15, bf16[48,768]{1,0:T(8,128)(2,1)S(1)} %collective-permute-done.1.got_ref, bf16[48,768]{1,0:T(8,128)(2,1)S(1)} %collective-permute-done.4.traded_ref, ...), custom_call_target="tpu_custom_call" | custom-call | bytes 4194304 | tf_op jit(solution)/shard_map/conv_edges/pallas_call | solution.py:228
  20.7 3.7 %deep_forward.1 = (bf16[26,64,768]{2,1,0:T(8,128)(2,1)S(1)}, bf16[24,64,128]{2,1,0:T(8,128)(2,1)S(1)}, f32[1536,128]{1,0:T(8,128)S(1)}, f32[32,128]{1,0:T(8,128)S(1)}) custom-call(bf16[12,64,256]{2,1,0:T(8,128)(2,1)S(1)} %conv_pool.1.refs_2_.refs_0_.own_ref, bf16[12,64,256]{2,1,0:T(8,128)(2,1)S(1)} %collective-permute-done.3.other_ref, ...), custom_call_target="tpu_custom_call" | custom-call | flops 1811939328 | bytes 8388608 | tf_op jit(solution)/shard_map/deep_forward/pallas_call | solution.py:469
  24.4 2.3 %deep_backward.1 = (f32[296,128]{1,0:T(8,128)S(1)}, f32[296,128]{1,0:T(8,128)S(1)}, f32[296,128]{1,0:T(8,128)S(1)}, f32[296,128]{1,0:T(8,128)S(1)}, f32[296,128]...) custom-call(bf16[26,64,768]{2,1,0:T(8,128)(2,1)S(1)} %get-tuple-element.35.taps, ...), custom_call_target="tpu_custom_call" | custom-call | flops 1811939328 | bytes 8388608 | tf_op jit(solution)/shard_map/deep_backward/pallas_call | solution.py:556
  26.7 1.6 %collective-permute-start.6 = (f16[616,128]{1,0:T(8,128)(2,1)S(1)}, f16[616,128]{1,0:T(8,128)(2,1)S(1)}, u32[]{:S(2)}, u32[]{:S(2)}) collective-permute-start(f16[616,128]{1,0:T(8,128)(2,1)S(1)} %convert_element_type.71), channel_id=1, source_target_pairs={{0,24},{4,28},{8,16},{12,20},{16,8},{20,12},{24,0},{28,4},{1,25},{... | collective-permute-start | bytes 473096 | tf_op jit(solution)/shard_map/ppermute | solution.py:42
  28.4 1.4 %collective-permute-start.8 = (f16[328,128]{1,0:T(8,128)(2,1)S(1)}, f16[328,128]{1,0:T(8,128)(2,1)S(1)}, u32[]{:S(2)}, u32[]{:S(2)}) collective-permute-start(f16[328,128]{1,0:T(8,128)(2,1)S(1)} %convert_element_type.75), channel_id=1, source_target_pairs={{0,4},{4,0},{8,12},{12,8},{16,20},{20,16},{24,28},{28,24},{1,5},{5... | collective-permute-start | bytes 251912 | tf_op jit(solution)/shard_map/ppermute | solution.py:42
  29.8 0.8 %collective-permute-start.7 = (f16[296,128]{1,0:T(8,128)(2,1)S(1)}, f16[296,128]{1,0:T(8,128)(2,1)S(1)}, u32[]{:S(2)}, u32[]{:S(2)}) collective-permute-start(f16[296,128]{1,0:T(8,128)(2,1)S(1)} %convert_element_type.73), channel_id=1, source_target_pairs={{0,4},{4,0},{8,12},{12,8},{16,20},{20,16},{24,28},{28,24},{1,5},{5... | collective-permute-start | bytes 227336 | tf_op jit(solution)/shard_map/ppermute | solution.py:42
  30.5 3.2 %collective-permute-done.8 = f16[328,128]{1,0:T(8,128)(2,1)S(1)} collective-permute-done((f16[328,128]{1,0:T(8,128)(2,1)S(1)}, f16[328,128]{1,0:T(8,128)(2,1)S(1)}, u32[]{:S(2)}, u32[]{:S(2)}) %collective-permute-start.8) | collective-permute-done | bytes 84000 | tf_op jit(solution)/shard_map/ppermute | solution.py:42
  34.0 0.5 collective-permute-done.7
  34.6 2.0 %collective-permute-start.10 = (f16[360,128]{1,0:T(8,128)(2,1)S(1)}, f16[360,128]{1,0:T(8,128)(2,1)S(1)}, u32[]{:S(2)}, u32[]{:S(2)}) collective-permute-start(f16[360,128]{1,0:T(8,128)(2,1)S(1)} %convert_element_type.79), channel_id=1, source_target_pairs={{0,8},{4,12},{8,0},{12,4},{16,24},{20,28},{24,16},{28,20},{1,9},{5... | collective-permute-start | bytes 276488 | tf_op jit(solution)/shard_map/ppermute | solution.py:42
  36.7 1.0 %collective-permute-start.9 = (f16[328,128]{1,0:T(8,128)(2,1)S(1)}, f16[328,128]{1,0:T(8,128)(2,1)S(1)}, u32[]{:S(2)}, u32[]{:S(2)}) collective-permute-start(f16[328,128]{1,0:T(8,128)(2,1)S(1)} %convert_element_type.77), channel_id=1, source_target_pairs={{0,4},{4,0},{8,12},{12,8},{16,20},{20,16},{24,28},{28,24},{1,5},{5... | collective-permute-start | bytes 251912 | tf_op jit(solution)/shard_map/ppermute | solution.py:42
  37.7 3.0 %collective-permute-done.10 = f16[360,128]{1,0:T(8,128)(2,1)S(1)} collective-permute-done((f16[360,128]{1,0:T(8,128)(2,1)S(1)}, f16[360,128]{1,0:T(8,128)(2,1)S(1)}, u32[]{:S(2)}, u32[]{:S(2)}) %collective-permute-start.10) | collective-permute-done | bytes 92192 | tf_op jit(solution)/shard_map/ppermute | solution.py:42
  40.7 0.5 collective-permute-done.9
  41.5 1.9 %collective-permute-start.16 = (f16[1,296,128]{2,1,0:T(8,128)(2,1)S(1)}, f16[1,296,128]{2,1,0:T(8,128)(2,1)S(1)}, u32[]{:S(2)}, u32[]{:S(2)}) collective-permute-start(f16[1,296,128]{2,1,0:T(8,128)(2,1)S(1)} %get-tuple-element.54), channel_id=1, source_target_pairs={{0,24},{4,28},{8,16},{12,20},{16,8},{20,12},{24,0},{28,4},{1,25},{... | collective-permute-start | bytes 227336 | tf_op jit(solution)/shard_map/ppermute | solution.py:42
  43.4 2.7 %collective-permute-start.15 = (f16[1,296,128]{2,1,0:T(8,128)(2,1)S(1)}, f16[1,296,128]{2,1,0:T(8,128)(2,1)S(1)}, u32[]{:S(2)}, u32[]{:S(2)}) collective-permute-start(f16[1,296,128]{2,1,0:T(8,128)(2,1)S(1)} %convert_bitcast_fusion.1), channel_id=1, source_target_pairs={{0,16},{4,20},{8,24},{12,28},{16,0},{20,4},{24,8},{28,12},{1,17},{... | collective-permute-start | bytes 227336 | tf_op jit(solution)/shard_map/ppermute | solution.py:42
  46.1 1.5 %collective-permute-start.14 = (f16[1,312,128]{2,1,0:T(8,128)(2,1)S(1)}, f16[1,312,128]{2,1,0:T(8,128)(2,1)S(1)}, u32[]{:S(2)}, u32[]{:S(2)}) collective-permute-start(f16[1,312,128]{2,1,0:T(8,128)(2,1)S(1)} %convert_bitcast_fusion), channel_id=1, source_target_pairs={{0,12},{4,8},{8,4},{12,0},{16,28},{20,24},{24,20},{28,16},{1,13},{... | collective-permute-start | bytes 239624 | tf_op jit(solution)/shard_map/ppermute | solution.py:42
  47.6 2.0 %collective-permute-start.13 = (f16[1,296,128]{2,1,0:T(8,128)(2,1)S(1)}, f16[1,296,128]{2,1,0:T(8,128)(2,1)S(1)}, u32[]{:S(2)}, u32[]{:S(2)}) collective-permute-start(f16[1,296,128]{2,1,0:T(8,128)(2,1)S(1)} %get-tuple-element.54), channel_id=1, source_target_pairs={{0,8},{4,12},{8,0},{12,4},{16,24},{20,28},{24,16},{28,20},{1,9},{5... | collective-permute-start | bytes 227336 | tf_op jit(solution)/shard_map/ppermute | solution.py:42
  49.7 0.7 %collective-permute-done.15 = f16[1,296,128]{2,1,0:T(8,128)(2,1)S(1)} collective-permute-done((f16[1,296,128]{2,1,0:T(8,128)(2,1)S(1)}, f16[1,296,128]{2,1,0:T(8,128)(2,1)S(1)}, u32[]{:S(2)}, u32[]{:S(2)}) %collective-permute-start.15) | collective-permute-done | bytes 75808 | tf_op jit(solution)/shard_map/ppermute | solution.py:42
  50.4 1.3 %collective-permute-start.17 = (f16[1,296,128]{2,1,0:T(8,128)(2,1)S(1)}, f16[1,296,128]{2,1,0:T(8,128)(2,1)S(1)}, u32[]{:S(2)}, u32[]{:S(2)}) collective-permute-start(f16[1,296,128]{2,1,0:T(8,128)(2,1)S(1)} %collective-permute-done.15), channel_id=1, source_target_pairs={{0,4},{4,0},{8,12},{12,8},{16,20},{20,16},{24,28},{28,24},{1,5},{5... | collective-permute-start | bytes 227336 | tf_op jit(solution)/shard_map/ppermute | solution.py:42
  51.6 1.0 %embed.1 = f32[64,128]{1,0:T(8,128)} custom-call(f32[256,128]{1,0:T(8,128)S(1)} %get-tuple-element.47.sums_ref, f32[4,72,128]{2,1,0:T(8,128)S(1)} %join.3.refs_0_, f32[4,72,128]{2,1,0:T(8,128)S(1)} %collective-permute-done.5.refs_1_), custom_call_target="tpu_custom_call" | custom-call | tf_op jit(solution)/shard_map/embed/pallas_call | solution.py:817
  52.9 1.1 %collective-permute-done.18 = f16[1,296,128]{2,1,0:T(8,128)(2,1)S(1)} collective-permute-done((f16[1,296,128]{2,1,0:T(8,128)(2,1)S(1)}, f16[1,296,128]{2,1,0:T(8,128)(2,1)S(1)}, u32[]{:S(2)}, u32[]{:S(2)}) %collective-permute-start.18) | collective-permute-done | bytes 75808 | tf_op jit(solution)/shard_map/ppermute | solution.py:42
  54.0 0.8 %collective-permute-done.17 = f16[1,296,128]{2,1,0:T(8,128)(2,1)S(1)} collective-permute-done((f16[1,296,128]{2,1,0:T(8,128)(2,1)S(1)}, f16[1,296,128]{2,1,0:T(8,128)(2,1)S(1)}, u32[]{:S(2)}, u32[]{:S(2)}) %collective-permute-start.17) | collective-permute-done | bytes 75808 | tf_op jit(solution)/shard_map/ppermute | solution.py:42
  54.8 1.2 %spread.1 = (f32[2304,128]{1,0:T(8,128)}, f32[1,128]{1,0:T(1,128)}) custom-call(f32[1,296,128]{2,1,0:T(8,128)S(1)} %get-tuple-element.53.refs_0_, f32[1,312,128]{2,1,0:T(8,128)S(1)} %convert_element_type.87.refs_1_, f32[1,296,128]{2,1,0:T(8,128)S(1)} %convert_element_type.88.refs_2_, f32[1,312,128]{2,1,0:T(8,128)S(1)} %convert_element_type.89.refs_3_, ...), custom_call_target="tpu_custom_call" | custom-call | tf_op jit(solution)/shard_map/spread/pallas_call | solution.py:719
  (51 shorter events, 1.3 us)
Async XLA Ops:
  1.5 8.6 %collective-permute-start = (f32[1,72,128]{2,1,0:T(8,128)S(1)}, f32[1,72,128]{2,1,0:T(8,128)S(1)}, u32[]{:S(2)}, u32[]{:S(2)}) collective-permute-start(f32[1,72,128]{2,1,0:T(8,128)S(1)} %pack_side.1.refs_0_), channel_id=1, source_target_pairs={{0,8},{4,12},{8,0},{12,4},{16,24},{20,28},{24,16},{28,20},{1,9},{5... | collective-permute-start | bytes 110600 | tf_op jit(solution)/shard_map/ppermute | solution.py:42
  6.8 11.2 %collective-permute-start.1 = (bf16[48,768]{1,0:T(8,128)(2,1)S(1)}, bf16[48,768]{1,0:T(8,128)(2,1)S(1)}, u32[]{:S(2)}, u32[]{:S(2)}) collective-permute-start(bf16[48,768]{1,0:T(8,128)(2,1)S(1)} %get-tuple-element.29.refs_2_), channel_id=1, source_target_pairs={{0,4},{2,6},{4,8},{5,1},{6,10},{7,3},{8,12},{9,5},{10,14},{11,7},{... | collective-permute-start | bytes 221192 | tf_op jit(solution)/shard_map/ppermute | solution.py:749
  10.2 7.8 %collective-permute-start.2 = (f32[2,72,128]{2,1,0:T(8,128)S(1)}, f32[2,72,128]{2,1,0:T(8,128)S(1)}, u32[]{:S(2)}, u32[]{:S(2)}) collective-permute-start(f32[2,72,128]{2,1,0:T(8,128)S(1)} %join.2.refs_0_), channel_id=1, source_target_pairs={{0,16},{4,20},{8,24},{12,28},{16,0},{20,4},{24,8},{28,12},{1,17},{... | collective-permute-start | bytes 221192 | tf_op jit(solution)/shard_map/ppermute | solution.py:42
  12.9 1.0 %copy-start.1 = (f32[256]{0:T(256)S(1)}, f32[256]{0:T(256)}, u32[]{:S(2)}) copy-start(f32[256]{0:T(256)} %param.10) | copy-start | bytes 3076
  17.9 2.7 %copy-start = (s32[24,64]{1,0:T(8,128)S(1)}, s32[24,64]{1,0:T(8,128)}, u32[]{:S(2)}) copy-start(s32[24,64]{1,0:T(8,128)} %lab_ref.1) | copy-start | bytes 18436
  17.9 2.7 %copy-start.2 = (bf16[3,3,256,128]{3,2,1,0:T(8,128)(2,1)S(1)}, bf16[3,3,256,128]{3,2,1,0:T(8,128)(2,1)}, u32[]{:S(2)}) copy-start(bf16[3,3,256,128]{3,2,1,0:T(8,128)(2,1)} %param.11) | copy-start | bytes 1769476
  17.9 2.7 %copy-start.3 = (f32[128]{0:T(128)S(1)}, f32[128]{0:T(128)}, u32[]{:S(2)}) copy-start(f32[128]{0:T(128)} %param.12) | copy-start | bytes 1540
  18.0 2.6 %collective-permute-start.3 = (bf16[12,64,256]{2,1,0:T(8,128)(2,1)S(1)}, bf16[12,64,256]{2,1,0:T(8,128)(2,1)S(1)}, u32[]{:S(2)}, u32[]{:S(2)}) collective-permute-start(bf16[12,64,256]{2,1,0:T(8,128)(2,1)S(1)} %conv_pool.1.refs_2_.refs_0_.own_ref), channel_id=1, source_target_pairs={{0,1},{1,0},{2,3},{3,2},{4,5},{5,4},{6,7},{7,6},{8,9},{9,8},{10,11... | collective-permute-start | bytes 1179656 | tf_op jit(solution)/shard_map/ppermute | solution.py:42
  18.1 1.8 %collective-permute-start.4 = (bf16[48,768]{1,0:T(8,128)(2,1)S(1)}, bf16[48,768]{1,0:T(8,128)(2,1)S(1)}, u32[]{:S(2)}, u32[]{:S(2)}) collective-permute-start(bf16[48,768]{1,0:T(8,128)(2,1)S(1)} %collective-permute-done.1.got_ref), channel_id=1, source_target_pairs={{0,1},{1,0},{2,3},{3,2},{4,5},{5,4},{6,7},{7,6},{8,9},{9,8},{10,11... | collective-permute-start | bytes 221192 | tf_op jit(solution)/shard_map/ppermute | solution.py:42
  18.6 5.8 %collective-permute-start.5 = (f32[4,72,128]{2,1,0:T(8,128)S(1)}, f32[4,72,128]{2,1,0:T(8,128)S(1)}, u32[]{:S(2)}, u32[]{:S(2)}) collective-permute-start(f32[4,72,128]{2,1,0:T(8,128)S(1)} %join.3.refs_0_), channel_id=1, source_target_pairs={{0,4},{4,0},{8,12},{12,8},{16,20},{20,16},{24,28},{28,24},{1,5},{5... | collective-permute-start | bytes 442376 | tf_op jit(solution)/shard_map/ppermute | solution.py:42
  26.7 9.9 %collective-permute-start.6 = (f16[616,128]{1,0:T(8,128)(2,1)S(1)}, f16[616,128]{1,0:T(8,128)(2,1)S(1)}, u32[]{:S(2)}, u32[]{:S(2)}) collective-permute-start(f16[616,128]{1,0:T(8,128)(2,1)S(1)} %convert_element_type.71), channel_id=1, source_target_pairs={{0,24},{4,28},{8,16},{12,20},{16,8},{20,12},{24,0},{28,4},{1,25},{... | collective-permute-start | bytes 473096 | tf_op jit(solution)/shard_map/ppermute | solution.py:42
  28.4 5.3 %collective-permute-start.8 = (f16[328,128]{1,0:T(8,128)(2,1)S(1)}, f16[328,128]{1,0:T(8,128)(2,1)S(1)}, u32[]{:S(2)}, u32[]{:S(2)}) collective-permute-start(f16[328,128]{1,0:T(8,128)(2,1)S(1)} %convert_element_type.75), channel_id=1, source_target_pairs={{0,4},{4,0},{8,12},{12,8},{16,20},{20,16},{24,28},{28,24},{1,5},{5... | collective-permute-start | bytes 251912 | tf_op jit(solution)/shard_map/ppermute | solution.py:42
  29.8 4.7 %collective-permute-start.7 = (f16[296,128]{1,0:T(8,128)(2,1)S(1)}, f16[296,128]{1,0:T(8,128)(2,1)S(1)}, u32[]{:S(2)}, u32[]{:S(2)}) collective-permute-start(f16[296,128]{1,0:T(8,128)(2,1)S(1)} %convert_element_type.73), channel_id=1, source_target_pairs={{0,4},{4,0},{8,12},{12,8},{16,20},{20,16},{24,28},{28,24},{1,5},{5... | collective-permute-start | bytes 227336 | tf_op jit(solution)/shard_map/ppermute | solution.py:42
  33.8 6.9 %collective-permute-start.11 = (f16[368,128]{1,0:T(8,128)(2,1)S(1)}, f16[368,128]{1,0:T(8,128)(2,1)S(1)}, u32[]{:S(2)}, u32[]{:S(2)}) collective-permute-start(f16[368,128]{1,0:T(8,128)(2,1)S(1)} %convert_element_type.81), channel_id=1, source_target_pairs={{0,16},{4,20},{8,24},{12,28},{16,0},{20,4},{24,8},{28,12},{1,17},{... | collective-permute-start | bytes 282632 | tf_op jit(solution)/shard_map/ppermute | solution.py:42
  34.6 6.0 %collective-permute-start.10 = (f16[360,128]{1,0:T(8,128)(2,1)S(1)}, f16[360,128]{1,0:T(8,128)(2,1)S(1)}, u32[]{:S(2)}, u32[]{:S(2)}) collective-permute-start(f16[360,128]{1,0:T(8,128)(2,1)S(1)} %convert_element_type.79), channel_id=1, source_target_pairs={{0,8},{4,12},{8,0},{12,4},{16,24},{20,28},{24,16},{28,20},{1,9},{5... | collective-permute-start | bytes 276488 | tf_op jit(solution)/shard_map/ppermute | solution.py:42
  36.7 4.5 %collective-permute-start.9 = (f16[328,128]{1,0:T(8,128)(2,1)S(1)}, f16[328,128]{1,0:T(8,128)(2,1)S(1)}, u32[]{:S(2)}, u32[]{:S(2)}) collective-permute-start(f16[328,128]{1,0:T(8,128)(2,1)S(1)} %convert_element_type.77), channel_id=1, source_target_pairs={{0,4},{4,0},{8,12},{12,8},{16,20},{20,16},{24,28},{28,24},{1,5},{5... | collective-permute-start | bytes 251912 | tf_op jit(solution)/shard_map/ppermute | solution.py:42
  41.5 8.1 %collective-permute-start.16 = (f16[1,296,128]{2,1,0:T(8,128)(2,1)S(1)}, f16[1,296,128]{2,1,0:T(8,128)(2,1)S(1)}, u32[]{:S(2)}, u32[]{:S(2)}) collective-permute-start(f16[1,296,128]{2,1,0:T(8,128)(2,1)S(1)} %get-tuple-element.54), channel_id=1, source_target_pairs={{0,24},{4,28},{8,16},{12,20},{16,8},{20,12},{24,0},{28,4},{1,25},{... | collective-permute-start | bytes 227336 | tf_op jit(solution)/shard_map/ppermute | solution.py:42
  43.4 7.0 %collective-permute-start.15 = (f16[1,296,128]{2,1,0:T(8,128)(2,1)S(1)}, f16[1,296,128]{2,1,0:T(8,128)(2,1)S(1)}, u32[]{:S(2)}, u32[]{:S(2)}) collective-permute-start(f16[1,296,128]{2,1,0:T(8,128)(2,1)S(1)} %convert_bitcast_fusion.1), channel_id=1, source_target_pairs={{0,16},{4,20},{8,24},{12,28},{16,0},{20,4},{24,8},{28,12},{1,17},{... | collective-permute-start | bytes 227336 | tf_op jit(solution)/shard_map/ppermute | solution.py:42
  46.0 6.8 %collective-permute-start.12 = (f16[1,312,128]{2,1,0:T(8,128)(2,1)S(1)}, f16[1,312,128]{2,1,0:T(8,128)(2,1)S(1)}, u32[]{:S(2)}, u32[]{:S(2)}) collective-permute-start(f16[1,312,128]{2,1,0:T(8,128)(2,1)S(1)} %convert_bitcast_fusion), channel_id=1, source_target_pairs={{0,4},{4,0},{8,12},{12,8},{16,20},{20,16},{24,28},{28,24},{1,5},{5... | collective-permute-start | bytes 239624 | tf_op jit(solution)/shard_map/ppermute | solution.py:42
  46.1 6.7 %collective-permute-start.14 = (f16[1,312,128]{2,1,0:T(8,128)(2,1)S(1)}, f16[1,312,128]{2,1,0:T(8,128)(2,1)S(1)}, u32[]{:S(2)}, u32[]{:S(2)}) collective-permute-start(f16[1,312,128]{2,1,0:T(8,128)(2,1)S(1)} %convert_bitcast_fusion), channel_id=1, source_target_pairs={{0,12},{4,8},{8,4},{12,0},{16,28},{20,24},{24,20},{28,16},{1,13},{... | collective-permute-start | bytes 239624 | tf_op jit(solution)/shard_map/ppermute | solution.py:42
  47.6 5.2 %collective-permute-start.13 = (f16[1,296,128]{2,1,0:T(8,128)(2,1)S(1)}, f16[1,296,128]{2,1,0:T(8,128)(2,1)S(1)}, u32[]{:S(2)}, u32[]{:S(2)}) collective-permute-start(f16[1,296,128]{2,1,0:T(8,128)(2,1)S(1)} %get-tuple-element.54), channel_id=1, source_target_pairs={{0,8},{4,12},{8,0},{12,4},{16,24},{20,28},{24,16},{28,20},{1,9},{5... | collective-permute-start | bytes 227336 | tf_op jit(solution)/shard_map/ppermute | solution.py:42
  49.6 4.4 %collective-permute-start.18 = (f16[1,296,128]{2,1,0:T(8,128)(2,1)S(1)}, f16[1,296,128]{2,1,0:T(8,128)(2,1)S(1)}, u32[]{:S(2)}, u32[]{:S(2)}) collective-permute-start(f16[1,296,128]{2,1,0:T(8,128)(2,1)S(1)} %collective-permute-done.16), channel_id=1, source_target_pairs={{0,4},{4,0},{8,12},{12,8},{16,20},{20,16},{24,28},{28,24},{1,5},{5... | collective-permute-start | bytes 227336 | tf_op jit(solution)/shard_map/ppermute | solution.py:42
  50.4 4.4 %collective-permute-start.17 = (f16[1,296,128]{2,1,0:T(8,128)(2,1)S(1)}, f16[1,296,128]{2,1,0:T(8,128)(2,1)S(1)}, u32[]{:S(2)}, u32[]{:S(2)}) collective-permute-start(f16[1,296,128]{2,1,0:T(8,128)(2,1)S(1)} %collective-permute-done.15), channel_id=1, source_target_pairs={{0,4},{4,0},{8,12},{12,8},{16,20},{20,16},{24,28},{28,24},{1,5},{5... | collective-permute-start | bytes 227336 | tf_op jit(solution)/shard_map/ppermute | solution.py:42

commit v17 on v16

--- a/solution.py
+++ b/solution.py
@@ -488,6 +488,14 @@
     )(own, other, edges, w, b, labels)
 
 
+def three_terms(value, axis):
+    high = value.astype(BF16)
+    rest = value - high.astype(F32)
+    mid = rest.astype(BF16)
+    low = (rest - mid.astype(F32)).astype(BF16)
+    return jnp.concatenate([high, mid, low], axis=axis)
+
+
 def grad_kernel(
     taps, member, slope, sums_ref, *refs, n_parts, chunk
 ):
@@ -511,15 +519,13 @@
         counts = ref[k, owned + 1 : owned + 2, :entries]
         total += jnp.sum(jnp.where(there, counts, 0.0), axis=1, keepdims=True)
         hot = ((owner ^ me) == m) & (inner == spot)
-        entry_grad += jnp.dot(
-            hot.astype(F32), ref[k, :owned], precision=lax.Precision.HIGHEST, preferred_element_type=F32
+        picked = jnp.dot(
+            hot.astype(BF16), three_terms(ref[k, :owned], 1), preferred_element_type=F32
         )
+        entry_grad += picked[:, :width] + picked[:, width : 2 * width] + picked[:, 2 * width :]
     entry_grad = entry_grad / jnp.maximum(total, 1.0)
-    high = entry_grad.astype(BF16)
-    rest = entry_grad - high.astype(F32)
-    mid = rest.astype(BF16)
-    low = (rest - mid.astype(F32)).astype(BF16)
-    terms = jnp.concatenate([high, mid, low, jnp.zeros((128 - 3 * entries, width), BF16)], axis=0)
+    spare = jnp.zeros((128 - 3 * entries, width), BF16)
+    terms = jnp.concatenate([three_terms(entry_grad, 0), spare], axis=0)
     pixel = jnp.dot(member[...].reshape(rows * cols, 128), terms, preferred_element_type=F32)
     dg = (pixel * slope[...]).astype(BF16)
     turned = jnp.transpose(dg)

time: 56.2 us -> 55.9 us (level)
  no operation moved by 1% of the time
where the time goes in v17:
time: 55.9 us; the launch traced here: 55.6 us
  starting transfers between devices  26.5 us (47%)
  Pallas kernels  16.9 us (30%)
  waiting for transfers between devices  10.9 us (19%)
  between operations  0.99 us (2%)
    ppermute x18, starting transfers between devices, swap(): return lax.ppermute(value, axis, [(i, i ^ mask) for i in range(count)])  23.1 us
    ppermute x18, waiting for transfers between devices, swap(): return lax.ppermute(value, axis, [(i, i ^ mask) for i in range(count)])  10.9 us
    pallas_call x1, Pallas kernels, conv_pool(): pl.pallas_call(conv_kernel, out_shape=jax.ShapeDtypeStruct((pooled_rows,...  4.05 us
    pallas_call x1, Pallas kernels, deep_forward(): pl.pallas_call(functools.partial(deep_kernel, block=block, entries=entrie...  3.71 us
    ppermute x1, starting transfers between devices, body(): got = lax.ppermute(border, ('strip', 'chan'), pairs)  3.4 us
    pallas_call x1, Pallas kernels, columns(): pl.pallas_call(columns_kernel, out_shape=(border,) * 3 + (jax.ShapeDtypeS...  2.14 us
    pallas_call x1, Pallas kernels, deep_backward(): pl.pallas_call(functools.partial(grad_kernel, n_parts=len(parts), chunk=c...  1.92 us
    pallas_call x1, Pallas kernels, spread(): pl.pallas_call(functools.partial(spread_kernel, chunk=chunk, rows=rows, m...  1.17 us
  transfers between devices with their start and end apart: 19, of which 9 were waited for; matrix products, arithmetic and copies ran while one was open for 0% of the time, Pallas kernels for 23%

profile of v17, /device:TPU:0, one launch (start us, length us, event | category | flops | bytes accessed | tf_op | source)
XLA Modules:
  0.0 55.6 jit_solution(5107753345125892398)
XLA Ops:
  0.6 0.9 %pack_side.1.refs_0_ = f32[1,72,128]{2,1,0:T(8,128)S(1)} custom-call(f32[64,128]{1,0:T(8,128)} %grad_hbm.1, s32[24,64]{1,0:T(8,128)} %lab_ref.1, s32[1,32]{1,0:T(1,128)} %bitcast.19), custom_call_target="tpu_custom_call" | custom-call | tf_op jit(solution)/shard_map/pack_side/pallas_call | solution.py:273
  1.5 3.1 %collective-permute-start = (f32[1,72,128]{2,1,0:T(8,128)S(1)}, f32[1,72,128]{2,1,0:T(8,128)S(1)}, u32[]{:S(2)}, u32[]{:S(2)}) collective-permute-start(f32[1,72,128]{2,1,0:T(8,128)S(1)} %pack_side.1.refs_0_), channel_id=1, source_target_pairs={{0,8},{4,12},{8,0},{12,4},{16,24},{20,28},{24,16},{28,20},{1,9},{5... | collective-permute-start | bytes 110600 | tf_op jit(solution)/shard_map/ppermute | solution.py:42
  4.6 2.1 %columns.1 = (bf16[48,768]{1,0:T(8,128)(2,1)S(1)}, bf16[48,768]{1,0:T(8,128)(2,1)S(1)}, bf16[48,768]{1,0:T(8,128)(2,1)S(1)}, bf16[28,128,256]{2,1,0:T(8,128)(2,1)S(1)}, bf16[2304,256]{1,0:T(8,128)(2,1)S(1)}) custom-call(bf16[48,128,256]{2,1,0:T(8,128)(2,1)} %x_hbm.1, bf16[2304,256]{1,0:T(8,128)(2,1)} %bitcast.18), custom_call_target="tpu_custom_call" | custom-call | tf_op jit(solution)/shard_map/columns/pallas_call | solution.py:328
  6.8 3.4 %collective-permute-start.1 = (bf16[48,768]{1,0:T(8,128)(2,1)S(1)}, bf16[48,768]{1,0:T(8,128)(2,1)S(1)}, u32[]{:S(2)}, u32[]{:S(2)}) collective-permute-start(bf16[48,768]{1,0:T(8,128)(2,1)S(1)} %get-tuple-element.29.refs_2_), channel_id=1, source_target_pairs={{0,4},{2,6},{4,8},{5,1},{6,10},{7,3},{8,12},{9,5},{10,14},{11,7},{... | collective-permute-start | bytes 221192 | tf_op jit(solution)/shard_map/ppermute | solution.py:755
  10.2 2.7 %collective-permute-start.2 = (f32[2,72,128]{2,1,0:T(8,128)S(1)}, f32[2,72,128]{2,1,0:T(8,128)S(1)}, u32[]{:S(2)}, u32[]{:S(2)}) collective-permute-start(f32[2,72,128]{2,1,0:T(8,128)S(1)} %join.2.refs_0_), channel_id=1, source_target_pairs={{0,16},{4,20},{8,24},{12,28},{16,0},{20,4},{24,8},{28,12},{1,17},{... | collective-permute-start | bytes 221192 | tf_op jit(solution)/shard_map/ppermute | solution.py:42
  12.9 1.0 %windows.1.taps = bf16[36,64,1024]{2,1,0:T(8,128)(2,1)S(1)} custom-call(bf16[28,128,256]{2,1,0:T(8,128)(2,1)S(1)} %get-tuple-element.28.rows_ref, f32[2,72,128]{2,1,0:T(8,128)S(1)} %join.2.refs_0_), custom_call_target="tpu_custom_call" | custom-call | bytes 12582912 | tf_op jit(solution)/shard_map/windows/pallas_call | solution.py:113
  13.9 4.0 %conv_pool.1.refs_2_.refs_0_.own_ref = bf16[12,64,256]{2,1,0:T(8,128)(2,1)S(1)} custom-call(bf16[36,64,1024]{2,1,0:T(8,128)(2,1)S(1)} %windows.1.taps, bf16[2304,256]{1,0:T(8,128)(2,1)S(1)} %get-tuple-element.30.w_ref, f32[1,256]{1,0:T(1,128)S(1)} %bitcast.14, f32[2,72,128]{2,1,0:T(8,128)S(1)} %join.2.refs_0_), custom_call_target="tpu_custom_call" | custom-call | flops 3623878656 | bytes 8388608 | tf_op jit(solution)/shard_map/conv_pool/pallas_call | solution.py:202
  18.1 0.5 collective-permute-start.4
  18.6 0.4 collective-permute-start.5
  19.0 0.9 %collective-permute-done.4.traded_ref = bf16[48,768]{1,0:T(8,128)(2,1)S(1)} collective-permute-done((bf16[48,768]{1,0:T(8,128)(2,1)S(1)}, bf16[48,768]{1,0:T(8,128)(2,1)S(1)}, u32[]{:S(2)}, u32[]{:S(2)}) %collective-permute-start.4) | collective-permute-done | bytes 73760 | tf_op jit(solution)/shard_map/ppermute | solution.py:42
  19.9 0.7 %conv_edges.1.edge_ref = f32[4,2,24,128]{3,2,1,0:T(8,128)S(1)} custom-call(bf16[2304,256]{1,0:T(8,128)(2,1)S(1)} %get-tuple-element.30.w_ref, f32[1,256]{1,0:T(1,128)S(1)} %bitcast.15, bf16[48,768]{1,0:T(8,128)(2,1)S(1)} %collective-permute-done.1.got_ref, bf16[48,768]{1,0:T(8,128)(2,1)S(1)} %collective-permute-done.4.traded_ref, ...), custom_call_target="tpu_custom_call" | custom-call | bytes 4194304 | tf_op jit(solution)/shard_map/conv_edges/pallas_call | solution.py:228
  20.7 3.7 %deep_forward.1 = (bf16[26,64,768]{2,1,0:T(8,128)(2,1)S(1)}, bf16[24,64,128]{2,1,0:T(8,128)(2,1)S(1)}, f32[1536,128]{1,0:T(8,128)S(1)}, f32[32,128]{1,0:T(8,128)S(1)}) custom-call(bf16[12,64,256]{2,1,0:T(8,128)(2,1)S(1)} %conv_pool.1.refs_2_.refs_0_.own_ref, bf16[12,64,256]{2,1,0:T(8,128)(2,1)S(1)} %collective-permute-done.3.other_ref, ...), custom_call_target="tpu_custom_call" | custom-call | flops 1811939328 | bytes 8388608 | tf_op jit(solution)/shard_map/deep_forward/pallas_call | solution.py:469
  24.4 1.9 %deep_backward.1 = (f32[296,128]{1,0:T(8,128)S(1)}, f32[296,128]{1,0:T(8,128)S(1)}, f32[296,128]{1,0:T(8,128)S(1)}, f32[296,128]{1,0:T(8,128)S(1)}, f32[296,128]...) custom-call(bf16[26,64,768]{2,1,0:T(8,128)(2,1)S(1)} %get-tuple-element.35.taps, ...), custom_call_target="tpu_custom_call" | custom-call | flops 1811939328 | bytes 8388608 | tf_op jit(solution)/shard_map/deep_backward/pallas_call | solution.py:562
  26.4 1.6 %collective-permute-start.6 = (f16[616,128]{1,0:T(8,128)(2,1)S(1)}, f16[616,128]{1,0:T(8,128)(2,1)S(1)}, u32[]{:S(2)}, u32[]{:S(2)}) collective-permute-start(f16[616,128]{1,0:T(8,128)(2,1)S(1)} %convert_element_type.71), channel_id=1, source_target_pairs={{0,24},{4,28},{8,16},{12,20},{16,8},{20,12},{24,0},{28,4},{1,25},{... | collective-permute-start | bytes 473096 | tf_op jit(solution)/shard_map/ppermute | solution.py:42
  28.0 1.4 %collective-permute-start.8 = (f16[328,128]{1,0:T(8,128)(2,1)S(1)}, f16[328,128]{1,0:T(8,128)(2,1)S(1)}, u32[]{:S(2)}, u32[]{:S(2)}) collective-permute-start(f16[328,128]{1,0:T(8,128)(2,1)S(1)} %convert_element_type.75), channel_id=1, source_target_pairs={{0,4},{4,0},{8,12},{12,8},{16,20},{20,16},{24,28},{28,24},{1,5},{5... | collective-permute-start | bytes 251912 | tf_op jit(solution)/shard_map/ppermute | solution.py:42
  29.4 0.8 %collective-permute-start.7 = (f16[296,128]{1,0:T(8,128)(2,1)S(1)}, f16[296,128]{1,0:T(8,128)(2,1)S(1)}, u32[]{:S(2)}, u32[]{:S(2)}) collective-permute-start(f16[296,128]{1,0:T(8,128)(2,1)S(1)} %convert_element_type.73), channel_id=1, source_target_pairs={{0,4},{4,0},{8,12},{12,8},{16,20},{20,16},{24,28},{28,24},{1,5},{5... | collective-permute-start | bytes 227336 | tf_op jit(solution)/shard_map/ppermute | solution.py:42
  30.2 3.2 %collective-permute-done.8 = f16[328,128]{1,0:T(8,128)(2,1)S(1)} collective-permute-done((f16[328,128]{1,0:T(8,128)(2,1)S(1)}, f16[328,128]{1,0:T(8,128)(2,1)S(1)}, u32[]{:S(2)}, u32[]{:S(2)}) %collective-permute-start.8) | collective-permute-done | bytes 84000 | tf_op jit(solution)/shard_map/ppermute | solution.py:42
  33.6 0.5 collective-permute-done.7
  34.3 2.0 %collective-permute-start.10 = (f16[360,128]{1,0:T(8,128)(2,1)S(1)}, f16[360,128]{1,0:T(8,128)(2,1)S(1)}, u32[]{:S(2)}, u32[]{:S(2)}) collective-permute-start(f16[360,128]{1,0:T(8,128)(2,1)S(1)} %convert_element_type.79), channel_id=1, source_target_pairs={{0,8},{4,12},{8,0},{12,4},{16,24},{20,28},{24,16},{28,20},{1,9},{5... | collective-permute-start | bytes 276488 | tf_op jit(solution)/shard_map/ppermute | solution.py:42
  36.3 1.0 %collective-permute-start.9 = (f16[328,128]{1,0:T(8,128)(2,1)S(1)}, f16[328,128]{1,0:T(8,128)(2,1)S(1)}, u32[]{:S(2)}, u32[]{:S(2)}) collective-permute-start(f16[328,128]{1,0:T(8,128)(2,1)S(1)} %convert_element_type.77), channel_id=1, source_target_pairs={{0,4},{4,0},{8,12},{12,8},{16,20},{20,16},{24,28},{28,24},{1,5},{5... | collective-permute-start | bytes 251912 | tf_op jit(solution)/shard_map/ppermute | solution.py:42
  37.3 2.9 %collective-permute-done.10 = f16[360,128]{1,0:T(8,128)(2,1)S(1)} collective-permute-done((f16[360,128]{1,0:T(8,128)(2,1)S(1)}, f16[360,128]{1,0:T(8,128)(2,1)S(1)}, u32[]{:S(2)}, u32[]{:S(2)}) %collective-permute-start.10) | collective-permute-done | bytes 92192 | tf_op jit(solution)/shard_map/ppermute | solution.py:42
  40.3 0.5 collective-permute-done.9
  41.1 1.9 %collective-permute-start.16 = (f16[1,296,128]{2,1,0:T(8,128)(2,1)S(1)}, f16[1,296,128]{2,1,0:T(8,128)(2,1)S(1)}, u32[]{:S(2)}, u32[]{:S(2)}) collective-permute-start(f16[1,296,128]{2,1,0:T(8,128)(2,1)S(1)} %get-tuple-element.54), channel_id=1, source_target_pairs={{0,24},{4,28},{8,16},{12,20},{16,8},{20,12},{24,0},{28,4},{1,25},{... | collective-permute-start | bytes 227336 | tf_op jit(solution)/shard_map/ppermute | solution.py:42
  43.0 2.7 %collective-permute-start.15 = (f16[1,296,128]{2,1,0:T(8,128)(2,1)S(1)}, f16[1,296,128]{2,1,0:T(8,128)(2,1)S(1)}, u32[]{:S(2)}, u32[]{:S(2)}) collective-permute-start(f16[1,296,128]{2,1,0:T(8,128)(2,1)S(1)} %convert_bitcast_fusion.1), channel_id=1, source_target_pairs={{0,16},{4,20},{8,24},{12,28},{16,0},{20,4},{24,8},{28,12},{1,17},{... | collective-permute-start | bytes 227336 | tf_op jit(solution)/shard_map/ppermute | solution.py:42
  45.8 1.5 %collective-permute-start.14 = (f16[1,312,128]{2,1,0:T(8,128)(2,1)S(1)}, f16[1,312,128]{2,1,0:T(8,128)(2,1)S(1)}, u32[]{:S(2)}, u32[]{:S(2)}) collective-permute-start(f16[1,312,128]{2,1,0:T(8,128)(2,1)S(1)} %convert_bitcast_fusion), channel_id=1, source_target_pairs={{0,12},{4,8},{8,4},{12,0},{16,28},{20,24},{24,20},{28,16},{1,13},{... | collective-permute-start | bytes 239624 | tf_op jit(solution)/shard_map/ppermute | solution.py:42
  47.2 2.0 %collective-permute-start.13 = (f16[1,296,128]{2,1,0:T(8,128)(2,1)S(1)}, f16[1,296,128]{2,1,0:T(8,128)(2,1)S(1)}, u32[]{:S(2)}, u32[]{:S(2)}) collective-permute-start(f16[1,296,128]{2,1,0:T(8,128)(2,1)S(1)} %get-tuple-element.54), channel_id=1, source_target_pairs={{0,8},{4,12},{8,0},{12,4},{16,24},{20,28},{24,16},{28,20},{1,9},{5... | collective-permute-start | bytes 227336 | tf_op jit(solution)/shard_map/ppermute | solution.py:42
  49.3 0.7 %collective-permute-done.15 = f16[1,296,128]{2,1,0:T(8,128)(2,1)S(1)} collective-permute-done((f16[1,296,128]{2,1,0:T(8,128)(2,1)S(1)}, f16[1,296,128]{2,1,0:T(8,128)(2,1)S(1)}, u32[]{:S(2)}, u32[]{:S(2)}) %collective-permute-start.15) | collective-permute-done | bytes 75808 | tf_op jit(solution)/shard_map/ppermute | solution.py:42
  50.0 1.3 %collective-permute-start.17 = (f16[1,296,128]{2,1,0:T(8,128)(2,1)S(1)}, f16[1,296,128]{2,1,0:T(8,128)(2,1)S(1)}, u32[]{:S(2)}, u32[]{:S(2)}) collective-permute-start(f16[1,296,128]{2,1,0:T(8,128)(2,1)S(1)} %collective-permute-done.15), channel_id=1, source_target_pairs={{0,4},{4,0},{8,12},{12,8},{16,20},{20,16},{24,28},{28,24},{1,5},{5... | collective-permute-start | bytes 227336 | tf_op jit(solution)/shard_map/ppermute | solution.py:42
  51.3 1.0 %embed.1 = f32[64,128]{1,0:T(8,128)} custom-call(f32[256,128]{1,0:T(8,128)S(1)} %get-tuple-element.47.sums_ref, f32[4,72,128]{2,1,0:T(8,128)S(1)} %join.3.refs_0_, f32[4,72,128]{2,1,0:T(8,128)S(1)} %collective-permute-done.5.refs_1_), custom_call_target="tpu_custom_call" | custom-call | tf_op jit(solution)/shard_map/embed/pallas_call | solution.py:823
  52.5 1.1 %collective-permute-done.18 = f16[1,296,128]{2,1,0:T(8,128)(2,1)S(1)} collective-permute-done((f16[1,296,128]{2,1,0:T(8,128)(2,1)S(1)}, f16[1,296,128]{2,1,0:T(8,128)(2,1)S(1)}, u32[]{:S(2)}, u32[]{:S(2)}) %collective-permute-start.18) | collective-permute-done | bytes 75808 | tf_op jit(solution)/shard_map/ppermute | solution.py:42
  53.6 0.8 %collective-permute-done.17 = f16[1,296,128]{2,1,0:T(8,128)(2,1)S(1)} collective-permute-done((f16[1,296,128]{2,1,0:T(8,128)(2,1)S(1)}, f16[1,296,128]{2,1,0:T(8,128)(2,1)S(1)}, u32[]{:S(2)}, u32[]{:S(2)}) %collective-permute-start.17) | collective-permute-done | bytes 75808 | tf_op jit(solution)/shard_map/ppermute | solution.py:42
  54.5 1.2 %spread.1 = (f32[2304,128]{1,0:T(8,128)}, f32[1,128]{1,0:T(1,128)}) custom-call(f32[1,296,128]{2,1,0:T(8,128)S(1)} %get-tuple-element.53.refs_0_, f32[1,312,128]{2,1,0:T(8,128)S(1)} %convert_element_type.87.refs_1_, f32[1,296,128]{2,1,0:T(8,128)S(1)} %convert_element_type.88.refs_2_, f32[1,312,128]{2,1,0:T(8,128)S(1)} %convert_element_type.89.refs_3_, ...), custom_call_target="tpu_custom_call" | custom-call | tf_op jit(solution)/shard_map/spread/pallas_call | solution.py:725
  (51 shorter events, 1.3 us)
Async XLA Ops:
  1.5 8.6 %collective-permute-start = (f32[1,72,128]{2,1,0:T(8,128)S(1)}, f32[1,72,128]{2,1,0:T(8,128)S(1)}, u32[]{:S(2)}, u32[]{:S(2)}) collective-permute-start(f32[1,72,128]{2,1,0:T(8,128)S(1)} %pack_side.1.refs_0_), channel_id=1, source_target_pairs={{0,8},{4,12},{8,0},{12,4},{16,24},{20,28},{24,16},{28,20},{1,9},{5... | collective-permute-start | bytes 110600 | tf_op jit(solution)/shard_map/ppermute | solution.py:42
  6.8 11.2 %collective-permute-start.1 = (bf16[48,768]{1,0:T(8,128)(2,1)S(1)}, bf16[48,768]{1,0:T(8,128)(2,1)S(1)}, u32[]{:S(2)}, u32[]{:S(2)}) collective-permute-start(bf16[48,768]{1,0:T(8,128)(2,1)S(1)} %get-tuple-element.29.refs_2_), channel_id=1, source_target_pairs={{0,4},{2,6},{4,8},{5,1},{6,10},{7,3},{8,12},{9,5},{10,14},{11,7},{... | collective-permute-start | bytes 221192 | tf_op jit(solution)/shard_map/ppermute | solution.py:755
  10.2 7.8 %collective-permute-start.2 = (f32[2,72,128]{2,1,0:T(8,128)S(1)}, f32[2,72,128]{2,1,0:T(8,128)S(1)}, u32[]{:S(2)}, u32[]{:S(2)}) collective-permute-start(f32[2,72,128]{2,1,0:T(8,128)S(1)} %join.2.refs_0_), channel_id=1, source_target_pairs={{0,16},{4,20},{8,24},{12,28},{16,0},{20,4},{24,8},{28,12},{1,17},{... | collective-permute-start | bytes 221192 | tf_op jit(solution)/shard_map/ppermute | solution.py:42
  12.9 1.0 %copy-start.1 = (f32[256]{0:T(256)S(1)}, f32[256]{0:T(256)}, u32[]{:S(2)}) copy-start(f32[256]{0:T(256)} %param.10) | copy-start | bytes 3076
  17.9 2.7 %copy-start = (s32[24,64]{1,0:T(8,128)S(1)}, s32[24,64]{1,0:T(8,128)}, u32[]{:S(2)}) copy-start(s32[24,64]{1,0:T(8,128)} %lab_ref.1) | copy-start | bytes 18436
  17.9 2.7 %copy-start.2 = (bf16[3,3,256,128]{3,2,1,0:T(8,128)(2,1)S(1)}, bf16[3,3,256,128]{3,2,1,0:T(8,128)(2,1)}, u32[]{:S(2)}) copy-start(bf16[3,3,256,128]{3,2,1,0:T(8,128)(2,1)} %param.11) | copy-start | bytes 1769476
  17.9 2.7 %copy-start.3 = (f32[128]{0:T(128)S(1)}, f32[128]{0:T(128)}, u32[]{:S(2)}) copy-start(f32[128]{0:T(128)} %param.12) | copy-start | bytes 1540
  18.0 2.6 %collective-permute-start.3 = (bf16[12,64,256]{2,1,0:T(8,128)(2,1)S(1)}, bf16[12,64,256]{2,1,0:T(8,128)(2,1)S(1)}, u32[]{:S(2)}, u32[]{:S(2)}) collective-permute-start(bf16[12,64,256]{2,1,0:T(8,128)(2,1)S(1)} %conv_pool.1.refs_2_.refs_0_.own_ref), channel_id=1, source_target_pairs={{0,1},{1,0},{2,3},{3,2},{4,5},{5,4},{6,7},{7,6},{8,9},{9,8},{10,11... | collective-permute-start | bytes 1179656 | tf_op jit(solution)/shard_map/ppermute | solution.py:42
  18.1 1.8 %collective-permute-start.4 = (bf16[48,768]{1,0:T(8,128)(2,1)S(1)}, bf16[48,768]{1,0:T(8,128)(2,1)S(1)}, u32[]{:S(2)}, u32[]{:S(2)}) collective-permute-start(bf16[48,768]{1,0:T(8,128)(2,1)S(1)} %collective-permute-done.1.got_ref), channel_id=1, source_target_pairs={{0,1},{1,0},{2,3},{3,2},{4,5},{5,4},{6,7},{7,6},{8,9},{9,8},{10,11... | collective-permute-start | bytes 221192 | tf_op jit(solution)/shard_map/ppermute | solution.py:42
  18.6 5.8 %collective-permute-start.5 = (f32[4,72,128]{2,1,0:T(8,128)S(1)}, f32[4,72,128]{2,1,0:T(8,128)S(1)}, u32[]{:S(2)}, u32[]{:S(2)}) collective-permute-start(f32[4,72,128]{2,1,0:T(8,128)S(1)} %join.3.refs_0_), channel_id=1, source_target_pairs={{0,4},{4,0},{8,12},{12,8},{16,20},{20,16},{24,28},{28,24},{1,5},{5... | collective-permute-start | bytes 442376 | tf_op jit(solution)/shard_map/ppermute | solution.py:42
  26.4 9.9 %collective-permute-start.6 = (f16[616,128]{1,0:T(8,128)(2,1)S(1)}, f16[616,128]{1,0:T(8,128)(2,1)S(1)}, u32[]{:S(2)}, u32[]{:S(2)}) collective-permute-start(f16[616,128]{1,0:T(8,128)(2,1)S(1)} %convert_element_type.71), channel_id=1, source_target_pairs={{0,24},{4,28},{8,16},{12,20},{16,8},{20,12},{24,0},{28,4},{1,25},{... | collective-permute-start | bytes 473096 | tf_op jit(solution)/shard_map/ppermute | solution.py:42
  28.0 5.3 %collective-permute-start.8 = (f16[328,128]{1,0:T(8,128)(2,1)S(1)}, f16[328,128]{1,0:T(8,128)(2,1)S(1)}, u32[]{:S(2)}, u32[]{:S(2)}) collective-permute-start(f16[328,128]{1,0:T(8,128)(2,1)S(1)} %convert_element_type.75), channel_id=1, source_target_pairs={{0,4},{4,0},{8,12},{12,8},{16,20},{20,16},{24,28},{28,24},{1,5},{5... | collective-permute-start | bytes 251912 | tf_op jit(solution)/shard_map/ppermute | solution.py:42
  29.4 4.7 %collective-permute-start.7 = (f16[296,128]{1,0:T(8,128)(2,1)S(1)}, f16[296,128]{1,0:T(8,128)(2,1)S(1)}, u32[]{:S(2)}, u32[]{:S(2)}) collective-permute-start(f16[296,128]{1,0:T(8,128)(2,1)S(1)} %convert_element_type.73), channel_id=1, source_target_pairs={{0,4},{4,0},{8,12},{12,8},{16,20},{20,16},{24,28},{28,24},{1,5},{5... | collective-permute-start | bytes 227336 | tf_op jit(solution)/shard_map/ppermute | solution.py:42
  33.4 6.9 %collective-permute-start.11 = (f16[368,128]{1,0:T(8,128)(2,1)S(1)}, f16[368,128]{1,0:T(8,128)(2,1)S(1)}, u32[]{:S(2)}, u32[]{:S(2)}) collective-permute-start(f16[368,128]{1,0:T(8,128)(2,1)S(1)} %convert_element_type.81), channel_id=1, source_target_pairs={{0,16},{4,20},{8,24},{12,28},{16,0},{20,4},{24,8},{28,12},{1,17},{... | collective-permute-start | bytes 282632 | tf_op jit(solution)/shard_map/ppermute | solution.py:42
  34.3 6.0 %collective-permute-start.10 = (f16[360,128]{1,0:T(8,128)(2,1)S(1)}, f16[360,128]{1,0:T(8,128)(2,1)S(1)}, u32[]{:S(2)}, u32[]{:S(2)}) collective-permute-start(f16[360,128]{1,0:T(8,128)(2,1)S(1)} %convert_element_type.79), channel_id=1, source_target_pairs={{0,8},{4,12},{8,0},{12,4},{16,24},{20,28},{24,16},{28,20},{1,9},{5... | collective-permute-start | bytes 276488 | tf_op jit(solution)/shard_map/ppermute | solution.py:42
  36.3 4.5 %collective-permute-start.9 = (f16[328,128]{1,0:T(8,128)(2,1)S(1)}, f16[328,128]{1,0:T(8,128)(2,1)S(1)}, u32[]{:S(2)}, u32[]{:S(2)}) collective-permute-start(f16[328,128]{1,0:T(8,128)(2,1)S(1)} %convert_element_type.77), channel_id=1, source_target_pairs={{0,4},{4,0},{8,12},{12,8},{16,20},{20,16},{24,28},{28,24},{1,5},{5... | collective-permute-start | bytes 251912 | tf_op jit(solution)/shard_map/ppermute | solution.py:42
  41.1 8.1 %collective-permute-start.16 = (f16[1,296,128]{2,1,0:T(8,128)(2,1)S(1)}, f16[1,296,128]{2,1,0:T(8,128)(2,1)S(1)}, u32[]{:S(2)}, u32[]{:S(2)}) collective-permute-start(f16[1,296,128]{2,1,0:T(8,128)(2,1)S(1)} %get-tuple-element.54), channel_id=1, source_target_pairs={{0,24},{4,28},{8,16},{12,20},{16,8},{20,12},{24,0},{28,4},{1,25},{... | collective-permute-start | bytes 227336 | tf_op jit(solution)/shard_map/ppermute | solution.py:42
  43.0 7.0 %collective-permute-start.15 = (f16[1,296,128]{2,1,0:T(8,128)(2,1)S(1)}, f16[1,296,128]{2,1,0:T(8,128)(2,1)S(1)}, u32[]{:S(2)}, u32[]{:S(2)}) collective-permute-start(f16[1,296,128]{2,1,0:T(8,128)(2,1)S(1)} %convert_bitcast_fusion.1), channel_id=1, source_target_pairs={{0,16},{4,20},{8,24},{12,28},{16,0},{20,4},{24,8},{28,12},{1,17},{... | collective-permute-start | bytes 227336 | tf_op jit(solution)/shard_map/ppermute | solution.py:42
  45.7 6.8 %collective-permute-start.12 = (f16[1,312,128]{2,1,0:T(8,128)(2,1)S(1)}, f16[1,312,128]{2,1,0:T(8,128)(2,1)S(1)}, u32[]{:S(2)}, u32[]{:S(2)}) collective-permute-start(f16[1,312,128]{2,1,0:T(8,128)(2,1)S(1)} %convert_bitcast_fusion), channel_id=1, source_target_pairs={{0,4},{4,0},{8,12},{12,8},{16,20},{20,16},{24,28},{28,24},{1,5},{5... | collective-permute-start | bytes 239624 | tf_op jit(solution)/shard_map/ppermute | solution.py:42
  45.8 6.7 %collective-permute-start.14 = (f16[1,312,128]{2,1,0:T(8,128)(2,1)S(1)}, f16[1,312,128]{2,1,0:T(8,128)(2,1)S(1)}, u32[]{:S(2)}, u32[]{:S(2)}) collective-permute-start(f16[1,312,128]{2,1,0:T(8,128)(2,1)S(1)} %convert_bitcast_fusion), channel_id=1, source_target_pairs={{0,12},{4,8},{8,4},{12,0},{16,28},{20,24},{24,20},{28,16},{1,13},{... | collective-permute-start | bytes 239624 | tf_op jit(solution)/shard_map/ppermute | solution.py:42
  47.2 5.2 %collective-permute-start.13 = (f16[1,296,128]{2,1,0:T(8,128)(2,1)S(1)}, f16[1,296,128]{2,1,0:T(8,128)(2,1)S(1)}, u32[]{:S(2)}, u32[]{:S(2)}) collective-permute-start(f16[1,296,128]{2,1,0:T(8,128)(2,1)S(1)} %get-tuple-element.54), channel_id=1, source_target_pairs={{0,8},{4,12},{8,0},{12,4},{16,24},{20,28},{24,16},{28,20},{1,9},{5... | collective-permute-start | bytes 227336 | tf_op jit(solution)/shard_map/ppermute | solution.py:42
  49.3 4.4 %collective-permute-start.18 = (f16[1,296,128]{2,1,0:T(8,128)(2,1)S(1)}, f16[1,296,128]{2,1,0:T(8,128)(2,1)S(1)}, u32[]{:S(2)}, u32[]{:S(2)}) collective-permute-start(f16[1,296,128]{2,1,0:T(8,128)(2,1)S(1)} %collective-permute-done.16), channel_id=1, source_target_pairs={{0,4},{4,0},{8,12},{12,8},{16,20},{20,16},{24,28},{28,24},{1,5},{5... | collective-permute-start | bytes 227336 | tf_op jit(solution)/shard_map/ppermute | solution.py:42
  50.0 4.4 %collective-permute-start.17 = (f16[1,296,128]{2,1,0:T(8,128)(2,1)S(1)}, f16[1,296,128]{2,1,0:T(8,128)(2,1)S(1)}, u32[]{:S(2)}, u32[]{:S(2)}) collective-permute-start(f16[1,296,128]{2,1,0:T(8,128)(2,1)S(1)} %collective-permute-done.15), channel_id=1, source_target_pairs={{0,4},{4,0},{8,12},{12,8},{16,20},{20,16},{24,28},{28,24},{1,5},{5... | collective-permute-start | bytes 227336 | tf_op jit(solution)/shard_map/ppermute | solution.py:42
